TPU v7x, 256 devices: a whole 4x4x8 slice. The times are simulated.
256 devices in a mesh: blk: 8 (over y, x_lo), dom: 32 (over x_hi, z, core).
Axes of the slice: x: 4 (x_hi: 2, x_lo: 2; x = x_hi * 2 + x_lo), y: 4, z: 8, core: 2. Of those that a mesh axis runs over, the one named last changes fastest.
Arguments:
- refs: bfloat16 [128, 32768], P('blk'), may hold values from -6 to 6
- particles: bfloat16 [8192, 32768], P(('blk', 'dom')), may hold values from -24 to 24
- shift_ids: int32 [8192, 8], P(('blk', 'dom')), may hold values from 0 to 124
- wedge: int32 [8192, 32], P(('blk', 'dom')), may hold values 0 or 1
- defocus: float32 [8192, 32], P(('blk', 'dom')), may hold values from 1 to 6
- inv_sigma: float32 [8192], P(('blk', 'dom')), may hold values from 0.005 to 0.05
Outputs:
- accum: float32 [128, 32768], P('blk', 'dom')
All inputs are finite; a program needn't handle non-finite values. No bound on the sum of `wedge` on one device may be relied on, other than what follows from the above.
Results may differ from a plain program's by a relative error of at most 0.0087.
Values may be sent and summed in bfloat16 or wider, within the bound.
No kernel may reach another device: no remote copies, remote signals or barrier semaphores. Data moves between devices by JAX's collectives and lax.ppermute only.
A program may use at most 128 MiB of HBM per device.

v0:
```python
import math

import jax
import jax.numpy as jnp
from jax import lax
from jax.sharding import PartitionSpec as P

BOX = 32


def spread_tilts(table, slice_len):
    count_rows, tilt_count = table.shape
    widened = jnp.broadcast_to(table[:, :, None], (count_rows, tilt_count, slice_len))
    return widened.reshape(count_rows, tilt_count * slice_len)


def prepare(particles, shift_ids, wedge, defocus, inv_sigma):
    half = particles.shape[1] // 2
    tilt_count = wedge.shape[1]
    slice_len = half // tilt_count
    position = jnp.arange(half, dtype=jnp.int32)
    tilt_index = (position // slice_len).astype(jnp.float32)
    within = position % slice_len
    radial = (within // BOX).astype(jnp.float32)
    lateral = (within % BOX - BOX // 2).astype(jnp.float32)
    tilt_angle = (tilt_index - 0.5 * (tilt_count - 1)) * (2.0 / tilt_count)
    freq_x = radial * jnp.cos(tilt_angle)
    freq_z = radial * jnp.sin(tilt_angle)
    shell = (radial * radial + lateral * lateral) / (0.25 * BOX * BOX)
    defocus_map = spread_tilts(defocus, slice_len)
    wedge_weight = spread_tilts(wedge.astype(jnp.float32), slice_len)
    transfer = -jnp.sin(4.0 * defocus_map * shell + 0.1)
    precision_col = inv_sigma[:, None]
    weighting = wedge_weight * transfer * precision_col
    penalty = (0.5 * wedge_weight * transfer * transfer * precision_col).astype(jnp.bfloat16)
    shift_x = (shift_ids // 25 - 2).astype(jnp.float32) * 0.5
    shift_y = (shift_ids // 5 % 5 - 2).astype(jnp.float32) * 0.5
    shift_z = (shift_ids % 5 - 2).astype(jnp.float32) * 0.5
    phase_angle = (
        2.0
        * math.pi
        / BOX
        * (
            shift_x[:, :, None] * freq_x
            + shift_y[:, :, None] * lateral
            + shift_z[:, :, None] * freq_z
        )
    )
    cosine = jnp.cos(phase_angle)
    sine_part = jnp.sin(phase_angle)
    real_part = particles[:, None, :half].astype(jnp.float32)
    imag_part = particles[:, None, half:].astype(jnp.float32)
    weighted_real = weighting[:, None, :] * (real_part * cosine + imag_part * sine_part)
    weighted_imag = weighting[:, None, :] * (imag_part * cosine - real_part * sine_part)
    shifted = jnp.concatenate([weighted_real, weighted_imag], axis=2)
    return (shifted.reshape(-1, 2 * half).astype(jnp.bfloat16), penalty)


def power_of(ref_block):
    half = ref_block.shape[1] // 2
    real_part = ref_block[:, :half].astype(jnp.float32)
    imag_part = ref_block[:, half:].astype(jnp.float32)
    return (real_part * real_part + imag_part * imag_part).astype(jnp.bfloat16)


def block_scores(ref_block, ref_power, weighted_rows, penalty):
    contract = (((1,), (1,)), ((), ()))
    correlation = lax.dot_general(
        ref_block, weighted_rows, contract, preferred_element_type=jnp.float32
    )
    energy = lax.dot_general(ref_power, penalty, contract, preferred_element_type=jnp.float32)
    shift_count = weighted_rows.shape[0] // penalty.shape[0]
    block_rows = ref_block.shape[0]
    energy = jnp.broadcast_to(
        energy[:, :, None], (block_rows, penalty.shape[0], shift_count)
    ).reshape(block_rows, -1)
    return correlation - energy


def posterior_of(scores, part_count):
    orient_count = scores.shape[0]
    grouped = scores.reshape(orient_count, part_count, -1)
    peak = jnp.max(grouped, axis=(0, 2))
    expo = jnp.exp(grouped - peak[None, :, None])
    total = jnp.sum(expo, axis=(0, 2))
    posterior = (expo / total[None, :, None]).astype(jnp.bfloat16)
    return posterior.reshape(orient_count, -1)


def per_device(refs, particles, shift_ids, wedge, defocus, inv_sigma):
    weighted_rows, penalty = prepare(particles, shift_ids, wedge, defocus, inv_sigma)
    block_refs = lax.all_gather(refs, "blk", axis=0, tiled=True)
    fresh = block_scores(block_refs, power_of(block_refs), weighted_rows, penalty)
    posterior = posterior_of(fresh, particles.shape[0])
    partial_sums = lax.psum_scatter(
        lax.dot_general(
            weighted_rows, posterior, (((0,), (1,)), ((), ())), preferred_element_type=jnp.float32
        ),
        "dom",
        scatter_dimension=0,
        tiled=True,
    )
    summed = lax.psum_scatter(partial_sums, "blk", scatter_dimension=1, tiled=True)
    return jnp.transpose(summed)


def solution(mesh):
    return jax.shard_map(
        per_device,
        mesh=mesh,
        in_specs=(
            P("blk", None),
            P(("blk", "dom"), None),
            P(("blk", "dom"), None),
            P(("blk", "dom"), None),
            P(("blk", "dom"), None),
            P(("blk", "dom")),
        ),
        out_specs=P("blk", "dom"),
        check_vma=False,
    )
```

profile of v0, /device:TPU:2, one launch (start us, length us, event | category | flops | bytes accessed | tf_op | source)
XLA Modules:
  0.0 488.2 jit_solution(6275843673760868020)
XLA Ops:
  6.5 0.7 all-gather.2.cloned.1.call-update
  7.3 0.7 fusion.41
  8.0 0.1 copy.14
  8.1 0.1 mul.240
  8.2 0.1 copy.15
  8.3 0.1 mul.248
  8.4 0.1 copy.16
  8.4 0.1 mul.253
  8.5 0.9 convert_element_type.80
  9.4 0.2 broadcast_in_dim.6
  9.6 1.2 copy.22
  10.8 0.9 broadcast_in_dim.7
  11.8 1.2 copy.23
  13.1 0.3 fusion.28
  13.4 0.3 slice_convert_fusion.1
  13.7 0.7 copy-done
  14.4 7.1 %multiply_multiply_fusion.1 = f32[32,16384]{1,0:T(8,128)S(1)} fusion(f32[32,16384]{1,0:T(8,128)S(1)} %bitcast.41, f32[32,16384]{1,0:T(8,128)S(1)} %bitcast.43, f32[32]{0:T(128)S(1)} %copy-done.2, f32[16384]{0:T(1024)S(1)} %add_multiply_fusion.1), kind=kLoop, calls=%fused_computation.21 | loop fusion | flops 2621440 | bytes 6357120 | tf_op jit(solution)/shard_map/mul | solution.py:34
  21.5 69.6 %fusion = (bf16[256,16384]{1,0:T(8,128)(2,1)}, bf16[256,16384]{1,0:T(8,128)(2,1)}) fusion(f32[32,16384]{1,0:T(8,128)S(1)} %get-tuple-element.8, f32[16384]{0:T(1024)S(1)} %get-tuple-element.15, f32[256]{0:T(256)S(1)} %mul.253, f32[16384]{0:T(1024)S(1)} %fusion.21, f32[256]{0:T(256)S(1)} %mul.248, f32[16384]{0:T(1024)S(1)} %get-tuple-element.14, ...), kind=kLoop, calls=%fused_computation.6 | loop fusion | flops 67108864 | bytes 23268352 | tf_op jit(solution)/shard_map/convert
  91.0 92.0 %all-gather.2.cloned.1.call-done = bf16[128,32768]{1,0:T(8,128)(2,1)} async-done(((bf16[16,32768]{1,0:T(8,128)(2,1)}), bf16[128,32768]{1,0:T(8,128)(2,1)}) %all-gather.2.cloned.1.call-update) | async-done | bytes 8388624 | tf_op jit(solution)/shard_map/all_gather | solution.py:92
  183.0 10.9 %fusion.8 = f32[128,32]{0,1:T(8,128)S(1)} fusion(bf16[128,32768]{1,0:T(8,128)(2,1)} %all-gather.2.cloned.1.call-done, f32[32,16384]{1,0:T(8,128)S(1)} %bitcast.42, f32[32,16384]{1,0:T(8,128)} %bitcast.44, f32[32]{0:T(128)S(1)} %copy-done.2, f32[16384]{0:T(1024)S(1)} %add_multiply_fusion.1), kind=kOutput, calls=%fused_computation.17 | convolution fusion | flops 150994944 | bytes 12664960 | tf_op jit(solution)/shard_map/dot_general | solution.py:71
  194.0 0.1 copy.17
  194.1 10.6 %fusion.54 = (f32[256]{0:T(256)S(1)}, f32[128,256]{1,0:T(8,128)S(1)}) fusion(f32[128,256]{1,0:T(8,128)S(1)} %copy.17, bf16[128,32768]{1,0:T(8,128)(2,1)} %all-gather.2.cloned.1.call-done, bf16[256,16384]{1,0:T(8,128)(2,1)} %get-tuple-element.6, bf16[256,16384]{1,0:T(8,128)(2,1)} %get-tuple-element.5), kind=kOutput, calls=%fused_computation.89 | convolution fusion | flops 2181103360 | bytes 25428992 | tf_op jit(solution)/shard_map/dot_general | solution.py:68
  204.7 0.1 reduce_max.14
  204.8 0.1 reduce_max.18
  205.0 0.1 sub.80
  205.1 0.1 reduce_sum.14
  205.2 0.1 reduce_sum.18
  205.4 0.1 div.66
  205.5 16.1 %fusion.6 = f32[32768,128]{1,0:T(8,128)} fusion(bf16[256,16384]{1,0:T(8,128)(2,1)} %get-tuple-element.6, bf16[256,16384]{1,0:T(8,128)(2,1)} %get-tuple-element.5, f32[128,256]{1,0:T(8,128)S(1)} %get-tuple-element.13, f32[256]{0:T(256)S(1)} %div.66, f32[256]{0:T(256)S(1)} %sub.80), kind=kOutput, calls=%fused_computation.14 | convolution fusion | flops 2181136384 | bytes 33687552 | tf_op jit(solution)/shard_map/dot_general | solution.py:96
  221.7 220.3 %reduce-scatter.5.cloned.1.call-done = f32[1024,128]{1,0:T(8,128)} async-done(((f32[32768,128]{1,0:T(8,128)}), f32[1024,128]{1,0:T(8,128)}) %reduce-scatter.5.cloned.1.call-update) | async-done | bytes 524304 | tf_op jit(solution)/shard_map/reduce_scatter | solution.py:95
  441.9 2.0 copy.19
  444.0 37.7 %reduce-scatter.7.cloned.1.call-done = f32[16,1024]{1,0:T(8,128)} async-done(((f32[128,1024]{1,0:T(8,128)}), f32[16,1024]{1,0:T(8,128)}) %reduce-scatter.7.cloned.1.call-update) | async-done | bytes 65552 | tf_op jit(solution)/shard_map/transpose | solution.py:104
  (16 shorter events, 0.4 us)
Async XLA Ops:
  6.5 176.5 %all-gather.2.cloned.1.call-start = ((), (), s32[]{:S(2)}) async-start(), calls=%async_computation.2 | async-start | bytes 9437184 | tf_op jit(solution)/shard_map/all_gather | solution.py:92
  7.3 434.7 %reduce-scatter.5.cloned.1.call-start = ((), (), s32[]{:S(2)}) async-start(), calls=%async_computation.3 | async-start | bytes 17301504 | tf_op jit(solution)/shard_map/reduce_scatter | solution.py:95
  8.5 4.9 copy-start.1
  9.6 4.8 copy-start.2
  13.0 1.4 copy-start
  221.6 260.1 %reduce-scatter.7.cloned.1.call-start = ((), (), s32[]{:S(2)}) async-start(), calls=%async_computation.4 | async-start | bytes 589824 | tf_op jit(solution)/shard_map/transpose | solution.py:104
Sparse Core Ops, SparseCore 0:
  9.1 173.8 all-gather.1
  221.7 220.1 reduce-scatter.4
  444.6 37.0 reduce-scatter.6
where the time goes:
time: 491 us; the launch traced here: 488 us
  waiting for transfers between devices  351 us (71%)
  other arithmetic  79.1 us (16%)
  matrix products  37.6 us (8%)
  between operations  13.3 us (3%)
  local copies, waits for them, and re-layouts  7.44 us (2%)
    reduce_scatter x1, waiting for transfers between devices, per_device(): lax.psum_scatter(lax.dot_general(weighted_rows, posterior, (((0,), (1,)),...  220 us
    all_gather x1, waiting for transfers between devices, per_device(): block_refs = lax.all_gather(refs, 'blk', axis=0, tiled=True)  92 us
    another operation x1, other arithmetic  69.6 us
    transpose x1, waiting for transfers between devices, per_device(): return jnp.transpose(summed)  37.7 us
    dot_general x1, matrix products, per_device(): lax.dot_general(weighted_rows, posterior, (((0,), (1,)), ((), ())), prefe...  16.1 us
    dot_general x1, matrix products, block_scores(): lax.dot_general(ref_power, penalty, contract, preferred_element_type=jnp....  10.9 us
    dot_general x1, matrix products, block_scores(): lax.dot_general(ref_block, weighted_rows, contract, preferred_element_typ...  10.6 us
  transfers between devices with their start and end apart: 3, of which 3 were waited for; matrix products, arithmetic and copies ran while one was open for 17% of the time, Pallas kernels for 0%

commit v1 on v0

v1 whole, which is shorter than its diff:
```python
import math

import jax
import jax.numpy as jnp
import numpy as np
from jax import lax
from jax.experimental import pallas as pl
from jax.experimental.pallas import tpu as pltpu
from jax.sharding import PartitionSpec as P

BOX = 32
TILTS = 32
SHIFTS = 8
P_DEV = 32
Y, X, Z = 4, 4, 8
COLS = 1024
HALF = 512
G = 4
NB = 16 // G
ROWS = P_DEV * SHIFTS
AXES = ("blk", "dom")
F32, BF16 = jnp.float32, jnp.bfloat16
NT = (((1,), (1,)), ((), ()))
MIB = 1 << 20


def linear(y, x, z, core):
    y, x, z = y % Y, x % X, z % Z
    return (y * 2 + x % 2) * 32 + (x // 2) * 16 + z * 2 + core


def moves(dy=0, dx=0, dz=0):
    return [
        (linear(y, x, z, c), linear(y + dy, x + dx, z + dz, c))
        for y in range(Y) for x in range(X) for z in range(Z) for c in range(2)
    ]


def partners(k):
    return [
        (linear(y, x, z, c), linear(y, x, z ^ (k >> 1), c ^ (k & 1)))
        for y in range(Y) for x in range(X) for z in range(Z) for c in range(2)
    ]


def send(value, pairs):
    return lax.ppermute(value, AXES, pairs)


def geometry():
    position = np.arange(TILTS * HALF)
    tilt, within = position // HALF, position % HALF
    radial = (within // BOX).astype(np.float64)
    lateral = (within % BOX - BOX // 2).astype(np.float64)
    angle = (tilt - 0.5 * (TILTS - 1)) * (2.0 / TILTS)
    shell = (radial * radial + lateral * lateral) / (0.25 * BOX * BOX)
    zero = np.zeros_like(shell)
    table = np.stack([radial * np.cos(angle), lateral, radial * np.sin(angle), shell] + [zero] * 4)
    return table.reshape(8, 16, COLS).transpose(1, 0, 2).astype(np.float32)


def translations():
    ids = np.arange(128)
    out = np.zeros((128, 8), np.float32)
    for column, digit in enumerate((ids // 25, ids // 5 % 5, ids % 5)):
        out[:, column] = (digit - 2) * 0.5 / BOX
    out[125:] = 0
    return out


def fold(turns):
    turns = turns - jnp.floor(turns + 0.5)
    far = jnp.abs(turns) > 0.25
    near = jnp.where(far, jnp.where(turns > 0, 0.5, -0.5) - turns, turns)
    return near * (2.0 * math.pi), far


def series(square, terms):
    total = jnp.full_like(square, terms[-1])
    for term in terms[-2::-1]:
        total = total * square + term
    return total


SIN_TERMS = [(-1) ** n / math.factorial(2 * n + 1) for n in range(6)]
COS_TERMS = [(-1) ** n / math.factorial(2 * n) for n in range(7)]


def sine_turns(turns):
    angle, _ = fold(turns)
    return angle * series(angle * angle, SIN_TERMS)


def table_kernel(geo_ref, shift_ref, out_ref):
    geo = geo_ref[0]
    shift = shift_ref[...]
    turns = shift[:, 0:1] * geo[0:1] + shift[:, 1:2] * geo[1:2] + shift[:, 2:3] * geo[2:3]
    angle, far = fold(turns)
    square = angle * angle
    sine = angle * series(square, SIN_TERMS)
    cosine = series(square, COS_TERMS)
    cosine = jnp.where(far, -cosine, cosine)
    for tilt in range(2):
        for part, values in enumerate((cosine, sine)):
            values = values[:, tilt * HALF : (tilt + 1) * HALF]
            high = values.astype(BF16)
            low = (values - high.astype(F32)).astype(BF16)
            lanes = slice(tilt * COLS + part * HALF, tilt * COLS + (part + 1) * HALF)
            out_ref[0:128, lanes] = high
            out_ref[128:256, lanes] = low


def make_table(geo):
    return pl.pallas_call(
        table_kernel,
        grid=(NB,),
        in_specs=[
            pl.BlockSpec((1, 8, COLS), lambda b: (b, 0, 0)),
            pl.BlockSpec((128, 8), lambda b: (0, 0)),
        ],
        out_specs=pl.BlockSpec((256, 2 * COLS), lambda b: (0, b)),
        out_shape=jax.ShapeDtypeStruct((256, NB * 2 * COLS), BF16),
        cost_estimate=pl.CostEstimate(flops=NB * 128 * COLS * 40, bytes_accessed=4 * MIB, transcendentals=0),
        name="phase_table",
    )(geo, jnp.asarray(translations()))


def arrange_kernel(count, member_ref, *refs):
    for n in range(count):
        real, imag, out = refs[2 * n], refs[2 * n + 1], refs[2 * count + n]
        for tilt in range(2):
            lanes = slice(tilt * HALF, (tilt + 1) * HALF)
            out[:, tilt * COLS : tilt * COLS + HALF] = real[:, lanes]
            out[:, tilt * COLS + HALF : (tilt + 1) * COLS] = imag[:, lanes]


def arrange(member, source, count):
    rows = source.shape[0]

    def picked(n, part):
        return pl.BlockSpec((rows, COLS), lambda b, m: (0, part * 16 + b * G + (m[0] ^ n)))

    return pl.pallas_call(
        lambda *refs: arrange_kernel(count, *refs),
        grid_spec=pltpu.PrefetchScalarGridSpec(
            num_scalar_prefetch=1,
            grid=(NB,),
            in_specs=[picked(n, part) for n in range(count) for part in range(2)],
            out_specs=[pl.BlockSpec((rows, 2 * COLS), lambda b, m: (0, b))] * count,
        ),
        out_shape=[jax.ShapeDtypeStruct((rows, NB * 2 * COLS), BF16)] * count,
        cost_estimate=pl.CostEstimate(flops=0, bytes_accessed=count * rows * NB * COLS * 8, transcendentals=0),
        name="arrange",
    )(member, *([source] * (2 * count)))


def rows_kernel(x_ref, meta_ref, ids_ref, geo_ref, table_ref, rows_ref, pen_ref):
    meta = meta_ref[0]
    lane = lax.broadcasted_iota(jnp.int32, (ROWS, 256), 1) & 127
    pick = (ids_ref[...] == lane.astype(F32)).astype(BF16)
    sigma = meta[:, 4:5]
    for tilt in range(2):
        base = tilt * COLS
        shell = geo_ref[0, 3:4, tilt * HALF : (tilt + 1) * HALF]
        focus, kept = meta[:, tilt : tilt + 1], meta[:, 2 + tilt : 3 + tilt]
        transfer = -sine_turns((4.0 * focus * shell + 0.1) * (0.5 / math.pi))
        weighting = kept * transfer * sigma
        pen_ref[:, tilt * HALF : (tilt + 1) * HALF] = (0.5 * weighting * transfer).astype(BF16)
        real = (weighting * x_ref[:, base : base + HALF].astype(F32))[None]
        imag = (weighting * x_ref[:, base + HALF : base + COLS].astype(F32))[None]
        turned = jnp.dot(pick, table_ref[:, base : base + COLS], preferred_element_type=F32)
        turned = turned.reshape(SHIFTS, P_DEV, COLS)
        cosine, sine = turned[:, :, :HALF], turned[:, :, HALF:]
        out_real = (real * cosine + imag * sine).reshape(ROWS, HALF)
        out_imag = (imag * cosine - real * sine).reshape(ROWS, HALF)
        rows_ref[:, base : base + HALF] = out_real.astype(BF16)
        rows_ref[:, base + HALF : base + COLS] = out_imag.astype(BF16)


def make_rows(x, meta, ids, geo, table):
    return pl.pallas_call(
        rows_kernel,
        grid=(NB,),
        in_specs=[
            pl.BlockSpec((P_DEV, 2 * COLS), lambda b: (0, b)),
            pl.BlockSpec((1, P_DEV, 8), lambda b: (b, 0, 0)),
            pl.BlockSpec((ROWS, 1), lambda b: (0, 0)),
            pl.BlockSpec((1, 8, COLS), lambda b: (b, 0, 0)),
            pl.BlockSpec((256, 2 * COLS), lambda b: (0, b)),
        ],
        out_specs=[
            pl.BlockSpec((ROWS, 2 * COLS), lambda b: (0, b)),
            pl.BlockSpec((P_DEV, COLS), lambda b: (0, b)),
        ],
        out_shape=[
            jax.ShapeDtypeStruct((ROWS, NB * 2 * COLS), BF16),
            jax.ShapeDtypeStruct((P_DEV, NB * COLS), BF16),
        ],
        cost_estimate=pl.CostEstimate(
            flops=2 * ROWS * 256 * NB * 2 * COLS, bytes_accessed=9 * MIB, transcendentals=0
        ),
        compiler_params=pltpu.CompilerParams(vmem_limit_bytes=32 * MIB),
        name="shifted_rows",
    )(x, meta, ids, geo, table)


def scores_kernel(count, *refs):
    blocks = refs[2 * count : 2 * count + 8]
    outs = refs[2 * count + 8 :]
    stacked = jnp.concatenate([block[...] for block in blocks], axis=0)
    wide = stacked.astype(F32)
    squares = wide * wide
    power = jnp.concatenate(
        [
            squares[:, t * COLS : t * COLS + HALF] + squares[:, t * COLS + HALF : (t + 1) * COLS]
            for t in range(2)
        ],
        axis=1,
    ).astype(BF16)
    first = pl.program_id(0) == 0
    for n in range(count):
        rows, pen, out = refs[n], refs[count + n], outs[n]
        energy = lax.dot_general(pen[...], power, NT, preferred_element_type=F32)
        fresh = lax.dot_general(rows[...], stacked, NT, preferred_element_type=F32)
        fresh = (fresh.reshape(SHIFTS, P_DEV, 128) - energy[None]).reshape(ROWS, 128)

        @pl.when(first)
        def _(out=out, fresh=fresh):
            out[...] = fresh

        @pl.when(jnp.logical_not(first))
        def _(out=out, fresh=fresh):
            out[...] += fresh


def make_scores(rows, pens, blocks):
    count = len(rows)
    return pl.pallas_call(
        lambda *refs: scores_kernel(count, *refs),
        grid=(NB,),
        in_specs=[pl.BlockSpec((ROWS, 2 * COLS), lambda b: (0, b))] * count
        + [pl.BlockSpec((P_DEV, COLS), lambda b: (0, b))] * count
        + [pl.BlockSpec((16, 2 * COLS), lambda b: (0, b))] * 8,
        out_specs=[pl.BlockSpec((ROWS, 128), lambda b: (0, 0))] * count,
        out_shape=[jax.ShapeDtypeStruct((ROWS, 128), F32)] * count,
        cost_estimate=pl.CostEstimate(
            flops=2 * count * ROWS * 128 * NB * 2 * COLS, bytes_accessed=(4 * count + 2) * MIB, transcendentals=0
        ),
        compiler_params=pltpu.CompilerParams(vmem_limit_bytes=40 * MIB),
        name="partial_scores",
    )(*rows, *pens, *blocks)


def posterior_kernel(*refs):
    out = refs[-1]
    total = refs[0][...]
    for other in refs[1:-1]:
        total = total + other[...]
    total = total.reshape(SHIFTS, P_DEV, 128)
    peak = jnp.max(jnp.max(total, axis=0), axis=1, keepdims=True)
    expo = jnp.exp(total - peak[None])
    norm = jnp.sum(jnp.sum(expo, axis=0), axis=1, keepdims=True)
    share = (expo / norm[None]).reshape(ROWS, 128)
    out[...] = share.T.astype(BF16)


def make_posterior(parts):
    return pl.pallas_call(
        posterior_kernel,
        out_shape=jax.ShapeDtypeStruct((128, ROWS), BF16),
        name="posterior",
    )(*parts)


def accum_kernel(part, flag_ref, *refs):
    rows, posts, outs = refs[:G], refs[G : 2 * G], refs[2 * G :]
    total = jnp.dot(posts[0][...], rows[0][...], preferred_element_type=F32)
    for n in range(1, G):
        total = total + jnp.dot(posts[n][...], rows[n][...], preferred_element_type=F32)
    if part == 0:
        for n in range(Y):
            outs[n][...] = total[n * 32 : (n + 1) * 32].astype(BF16)
    else:
        for n in range(X):
            low = n & 1
            imag = flag_ref[n] == 1
            for k in range(Y):
                mine = total[k * 32 + low * 16 : k * 32 + low * 16 + 16]
                chosen = jnp.where(imag, mine[:, HALF:], mine[:, :HALF])
                outs[n][k * 16 : (k + 1) * 16] = chosen.astype(BF16)


def make_accum(part, flags, rows, posts):
    shape = (32, COLS) if part == 0 else (64, HALF)
    return pl.pallas_call(
        lambda *refs: accum_kernel(part, *refs),
        grid_spec=pltpu.PrefetchScalarGridSpec(
            num_scalar_prefetch=1,
            grid=(NB,),
            in_specs=[pl.BlockSpec((ROWS, COLS), lambda b, f: (0, 2 * b + part))] * G
            + [pl.BlockSpec((128, ROWS), lambda b, f: (0, 0))] * G,
            out_specs=[pl.BlockSpec(shape, lambda b, f: (0, b))] * 4,
        ),
        out_shape=[jax.ShapeDtypeStruct((shape[0], NB * shape[1]), BF16)] * 4,
        cost_estimate=pl.CostEstimate(
            flops=2 * G * ROWS * 128 * NB * COLS, bytes_accessed=(2 * G + 1) * MIB, transcendentals=0
        ),
        compiler_params=pltpu.CompilerParams(vmem_limit_bytes=40 * MIB),
        name="weighted_sums",
    )(flags, *rows, *posts)


def added(values):
    total = values[0].astype(F32)
    for value in values[1:]:
        total = total + value.astype(F32)
    return total


def per_device(refs, particles, shift_ids, wedge, defocus, inv_sigma):
    dom = lax.axis_index("dom")
    x_at = (dom // 16) * 2 + lax.axis_index("blk") % 2
    member = dom % G
    block = (dom % 16) // G
    member_arr = member.astype(jnp.int32).reshape(1)
    flags = (((x_at + jnp.arange(X)) % X) // 2).astype(jnp.int32)

    gathered = {}
    (own,) = arrange(member_arr, refs, 1)
    gathered[0, 0] = own
    gathered[1, 0] = send(own, moves(dy=-1))
    gathered[3, 0] = send(own, moves(dy=1))
    gathered[0, 1] = send(own, moves(dx=-1))
    gathered[2, 0] = send(own, moves(dy=2))
    gathered[1, 1] = send(gathered[1, 0], moves(dx=-1))
    gathered[3, 1] = send(gathered[3, 0], moves(dx=1))
    gathered[2, 1] = send(gathered[2, 0], moves(dx=1))
    blocks = [gathered[ky, kx] for ky in range(Y) for kx in range(2)]

    meta = jnp.concatenate(
        [shift_ids.astype(F32), wedge.astype(F32), defocus, inv_sigma[:, None]], axis=1
    )
    metas = [meta] + [send(meta, partners(n)) for n in range(1, G)]
    chunks = arrange(member_arr, particles, G)
    chunks = [chunks[0]] + [send(chunks[n], partners(n)) for n in range(1, G)]

    geo = lax.dynamic_slice(
        jnp.asarray(geometry()).reshape(NB, G, 8, COLS), (0, member, 0, 0), (NB, 1, 8, COLS)
    ).reshape(NB, 8, COLS)
    table = make_table(geo)

    rows, pens = [], []
    for chunk, info in zip(chunks, metas):
        ids = info[:, :SHIFTS].T.reshape(ROWS, 1)
        tilts = info[:, SHIFTS : SHIFTS + 2 * TILTS].reshape(P_DEV, 2, NB, G, 2)
        tilts = lax.dynamic_slice(tilts, (0, 0, 0, member, 0), (P_DEV, 2, NB, 1, 2))[:, :, :, 0]
        kept, focus = tilts[:, 0].transpose(1, 0, 2), tilts[:, 1].transpose(1, 0, 2)
        sigma = jnp.broadcast_to(info[None, :, -1:], (NB, P_DEV, 1))
        packed = jnp.concatenate([focus, kept, sigma, jnp.zeros((NB, P_DEV, 3), F32)], axis=2)
        made, pen = make_rows(chunk, packed, ids, geo, table)
        rows.append(made)
        pens.append(pen)

    remote = make_scores(rows[1:], pens[1:], blocks)
    arrived = [send(remote[n - 1], partners(n)) for n in range(1, G)]
    (local,) = make_scores(rows[:1], pens[:1], blocks)
    posterior = make_posterior([local] + arrived)
    posts = [posterior] + [send(posterior, partners(n)) for n in range(1, G)]

    first = make_accum(0, flags, rows, posts)
    first = [first[0]] + [send(first[n], moves(dy=n)) for n in range(1, Y)]
    second = make_accum(1, flags, rows, posts)
    second = [second[0]] + [send(second[n], moves(dx=n)) for n in range(1, X)]

    first = added(first).reshape(2, 16, NB, 2, HALF)
    pieces = []
    for n in range(X):
        piece = lax.dynamic_index_in_dim(first[n & 1], flags[n], axis=2, keepdims=False)
        piece = piece.reshape(16, NB * HALF)
        pieces.append(piece if n == 0 else send(piece.astype(BF16), moves(dx=n)))
    first = added(pieces)

    second = added(second)
    pieces = []
    for n in range(Y):
        piece = second[n * 16 : (n + 1) * 16]
        pieces.append(piece if n == 0 else send(piece.astype(BF16), moves(dy=n)))
    second = added(pieces)

    joined = jnp.concatenate([first.reshape(16, NB, HALF), second.reshape(16, NB, HALF)], axis=2)
    pieces = []
    for n in range(NB):
        piece = lax.dynamic_index_in_dim(joined, (block + n) % NB, axis=1, keepdims=False)
        pieces.append(piece if n == 0 else send(piece.astype(BF16), moves(dz=n * (G // 2))))
    return added(pieces)


def solution(mesh):
    return jax.shard_map(
        per_device,
        mesh=mesh,
        in_specs=(
            P("blk", None),
            P(("blk", "dom"), None),
            P(("blk", "dom"), None),
            P(("blk", "dom"), None),
            P(("blk", "dom"), None),
            P(("blk", "dom")),
        ),
        out_specs=P("blk", "dom"),
        check_vma=False,
    )
```

time: 491 us -> 166 us (0.34)
  waiting for transfers between devices: 351 us -> 30.3 us
  other arithmetic: 79.1 us -> 3.41 us
  Pallas kernels: 0 us -> 51 us
  starting transfers between devices: 0.08 us -> 42.5 us
  matrix products: 37.6 us -> 0 us
  local copies, waits for them, and re-layouts: 7.44 us -> 28.8 us
  between operations: 13.3 us -> 8.14 us
    reduce_scatter x1 -> x0, waiting for transfers between devices: 220 us -> none  [per_device(): lax.psum_scatter(lax.dot_general(weighted_rows, posterior, (((0,), (1,)),...]
    all_gather x1 -> x0, waiting for transfers between devices: 92 us -> none  [per_device(): block_refs = lax.all_gather(refs, 'blk', axis=0, tiled=True)]
    another operation x1, other arithmetic: 69.6 us -> 0.14 us
    pallas_call x0 -> x12, Pallas kernels: none -> 51 us  [the longest x4 14.2 us: make_rows(): pl.pallas_call(rows_kernel, grid=(NB,), in_specs=[pl.BlockSpec((P_DEV, 2...]
    ppermute x0 -> x34, starting transfers between devices: none -> 42.5 us  [send(): return lax.ppermute(value, AXES, pairs)]
    transpose x1 -> x0, waiting for transfers between devices: 37.7 us -> none  [per_device(): return jnp.transpose(summed)]
    dot_general x3 -> x0, matrix products: 37.6 us -> none  [the longest x1 16.1 us: per_device(): lax.dot_general(weighted_rows, posterior, (((0,), (1,)), ((), ())), prefe...]
    ppermute x0 -> x34, waiting for transfers between devices: none -> 30.3 us  [send(): return lax.ppermute(value, AXES, pairs)]
  transfers between devices with their start and end apart: 3 -> 34, of which waited for: 3 -> 12; matrix products, arithmetic and copies ran while one was open for 17% -> 4% of each run, Pallas kernels for 0% -> 21%
where the time goes in v1:
time: 166 us; the launch traced here: 164 us
  Pallas kernels  51 us (31%)
  starting transfers between devices  42.5 us (26%)
  waiting for transfers between devices  30.3 us (18%)
  local copies, waits for them, and re-layouts  28.8 us (17%)
  between operations  8.14 us (5%)
  other arithmetic  3.41 us (2%)
    ppermute x34, starting transfers between devices, send(): return lax.ppermute(value, AXES, pairs)  42.5 us
    ppermute x34, waiting for transfers between devices, send(): return lax.ppermute(value, AXES, pairs)  30.3 us
    unnamed x57, local copies, waits for them, and re-layouts  24 us
    pallas_call x4, Pallas kernels, make_rows(): pl.pallas_call(rows_kernel, grid=(NB,), in_specs=[pl.BlockSpec((P_DEV, 2...  14.2 us
    pallas_call x2, Pallas kernels, make_scores(): pl.pallas_call(lambda *refs: scores_kernel(count, *refs), grid=(NB,), in_...  13.3 us
    pallas_call x2, Pallas kernels, make_accum(): pl.pallas_call(lambda *refs: accum_kernel(part, *refs), grid_spec=pltpu.P...  8.97 us
    pallas_call x2, Pallas kernels, arrange(): pl.pallas_call(lambda *refs: arrange_kernel(count, *refs), grid_spec=pltp...  6.69 us
    pallas_call x1, Pallas kernels, make_table(): pl.pallas_call(table_kernel, grid=(NB,), in_specs=[pl.BlockSpec((1, 8, CO...  5.78 us
  transfers between devices with their start and end apart: 34, of which 12 were waited for; matrix products, arithmetic and copies ran while one was open for 4% of the time, Pallas kernels for 21%

profile of v1, /device:TPU:2, one launch (start us, length us, event | category | flops | bytes accessed | tf_op | source)
XLA Modules:
  0.0 164.1 jit_solution(11982041700324173131)
XLA Ops:
  5.0 2.8 %arrange.3.refs_2_.refs_6_ = bf16[16,8192]{1,0:T(8,128)(2,1)} custom-call(s32[1]{0:T(128)} %bitcast.refs_0_, bf16[16,32768]{1,0:T(8,128)(2,1)} %refs_2_.3, bf16[16,32768]{1,0:T(8,128)(2,1)} %refs_2_.3), custom_call_target="tpu_custom_call" | custom-call | bytes 524288 | tf_op jit(solution)/shard_map/arrange/pallas_call | solution.py:143
  7.8 3.0 %collective-permute-start.7 = (bf16[16,8192]{1,0:T(8,128)(2,1)}, bf16[16,8192]{1,0:T(8,128)(2,1)S(1)}, u32[]{:S(2)}, u32[]{:S(2)}) collective-permute-start(bf16[16,8192]{1,0:T(8,128)(2,1)} %arrange.3.refs_2_.refs_6_), channel_id=1, source_target_pairs={{0,192},{1,193},{2,194},{3,195},{4,196},{5,197},{6,198},{7,199},{8... | collective-permute-start | bytes 786440 | tf_op jit(solution)/shard_map/ppermute | solution.py:47
  13.0 3.9 %arrange.2 = (bf16[32,8192]{1,0:T(8,128)(2,1)}, bf16[32,8192]{1,0:T(8,128)(2,1)}, bf16[32,8192]{1,0:T(8,128)(2,1)}, bf16[32,8192]{1,0:T(8,128)(2,1)}) custom-call(s32[1]{0:T(128)} %bitcast.refs_0_, bf16[32,32768]{1,0:T(8,128)(2,1)} %refs_8_.1, bf16[32,32768]{1,0:T(8,128)(2,1)} %refs_8_.1, bf16[32,32768]{1,0:T(8,128)(2,1)} %refs_8_.1, ...), custom_call_target="tpu_custom_call" | custom-call | bytes 4194304 | tf_op jit(solution)/shard_map/arrange/pallas_call | solution.py:143
  17.1 5.8 %phase_table.1.table_ref = bf16[256,8192]{1,0:T(8,128)(2,1)} custom-call(f32[4,8,1024]{2,1,0:T(8,128)} %dynamic-slice_bitcast_fusion.geo_ref, f32[128,8]{1,0:T(8,128)} %constant.125.clone.shift_ref), custom_call_target="tpu_custom_call" | custom-call | flops 20971520 | bytes 4194304 | tf_op jit(solution)/shard_map/phase_table/pallas_call | solution.py:114
  27.7 4.7 %collective-permute-done.11.refs_8_.refs_12_ = bf16[16,8192]{1,0:T(8,128)(2,1)S(1)} collective-permute-done((bf16[16,8192]{1,0:T(8,128)(2,1)S(1)}, bf16[16,8192]{1,0:T(8,128)(2,1)S(1)}, u32[]{:S(2)}, u32[]{:S(2)}) %collective-permute-start.11) | collective-permute-done | bytes 262176 | tf_op jit(solution)/shard_map/ppermute | solution.py:47
  34.4 4.7 %collective-permute-done.2.x_ref = bf16[32,8192]{1,0:T(8,128)(2,1)S(1)} collective-permute-done((bf16[32,8192]{1,0:T(8,128)(2,1)}, bf16[32,8192]{1,0:T(8,128)(2,1)S(1)}, u32[]{:S(2)}, u32[]{:S(2)}) %collective-permute-start.2) | collective-permute-done | bytes 524320 | tf_op jit(solution)/shard_map/ppermute | solution.py:47
  40.6 2.2 %copy-done = bf16[256,8192]{1,0:T(8,128)(2,1)S(1)} copy-done((bf16[256,8192]{1,0:T(8,128)(2,1)S(1)}, bf16[256,8192]{1,0:T(8,128)(2,1)}, u32[]{:S(2)}) %copy-start) | copy-done | bytes 4194328
  42.7 3.5 %shifted_rows.5 = (bf16[256,8192]{1,0:T(8,128)(2,1)S(1)}, bf16[32,4096]{1,0:T(8,128)(2,1)S(1)}) custom-call(bf16[32,8192]{1,0:T(8,128)(2,1)S(1)} %collective-permute-done.x_ref, f32[4,32,8]{2,1,0:T(8,128)S(1)} %copy.104.meta_ref, f32[256,1]{1,0:T(8,128)S(1)} %reshape.87.ids_ref, f32[4,8,1024]{2,1,0:T(8,128)S(1)} %copy-done.12, bf16[256,8192]{1,0:T(8,128)(2,1)S(1)} %copy-done), custom_call_target="tpu_custom_call" | custom-call | flops 1073741824 | bytes 9437184 | tf_op jit(solution)/shard_map/shifted_rows/pallas_call | solution.py:181
  46.3 3.6 %shifted_rows.6 = (bf16[256,8192]{1,0:T(8,128)(2,1)S(1)}, bf16[32,4096]{1,0:T(8,128)(2,1)S(1)}) custom-call(bf16[32,8192]{1,0:T(8,128)(2,1)S(1)} %collective-permute-done.2.x_ref, f32[4,32,8]{2,1,0:T(8,128)S(1)} %copy.106.meta_ref, f32[256,1]{1,0:T(8,128)S(1)} %reshape.88.ids_ref, f32[4,8,1024]{2,1,0:T(8,128)S(1)} %copy-done.12, bf16[256,8192]{1,0:T(8,128)(2,1)S(1)} %copy-done), custom_call_target="tpu_custom_call" | custom-call | flops 1073741824 | bytes 9437184 | tf_op jit(solution)/shard_map/shifted_rows/pallas_call | solution.py:181
  49.9 3.6 %shifted_rows.7 = (bf16[256,8192]{1,0:T(8,128)(2,1)S(1)}, bf16[32,4096]{1,0:T(8,128)(2,1)S(1)}) custom-call(bf16[32,8192]{1,0:T(8,128)(2,1)S(1)} %collective-permute-done.4.x_ref, f32[4,32,8]{2,1,0:T(8,128)S(1)} %copy.108.meta_ref, f32[256,1]{1,0:T(8,128)S(1)} %reshape.89.ids_ref, f32[4,8,1024]{2,1,0:T(8,128)S(1)} %copy-done.12, bf16[256,8192]{1,0:T(8,128)(2,1)S(1)} %copy-done), custom_call_target="tpu_custom_call" | custom-call | flops 1073741824 | bytes 9437184 | tf_op jit(solution)/shard_map/shifted_rows/pallas_call | solution.py:181
  53.5 2.1 %copy-done.11 = bf16[256,8192]{1,0:T(8,128)(2,1)} copy-done((bf16[256,8192]{1,0:T(8,128)(2,1)}, bf16[256,8192]{1,0:T(8,128)(2,1)S(1)}, u32[]{:S(2)}) %copy-start.11) | copy-done | bytes 4194328
  55.6 10.7 %partial_scores.3 = (f32[256,128]{1,0:T(8,128)S(1)}, f32[256,128]{1,0:T(8,128)S(1)}, f32[256,128]{1,0:T(8,128)S(1)}) custom-call(bf16[256,8192]{1,0:T(8,128)(2,1)S(1)} %get-tuple-element.31.refs_0_.refs_2_, bf16[256,8192]{1,0:T(8,128)(2,1)S(1)} %get-tuple-element.33.refs_1_.refs_3_, bf16[256,8192]{1,0:T(8,128)(2,1)} %copy-done.11, ...), custom_call_target="tpu_custom_call" | custom-call | flops 1610612736 | bytes 14680064 | tf_op jit(solution)/shard_map/partial_scores/pallas_call | solution.py:238
  68.3 3.5 %shifted_rows.4 = (bf16[256,8192]{1,0:T(8,128)(2,1)S(1)}, bf16[32,4096]{1,0:T(8,128)(2,1)S(1)}) custom-call(bf16[32,8192]{1,0:T(8,128)(2,1)S(1)} %copy-done.16, f32[4,32,8]{2,1,0:T(8,128)S(1)} %copy.101.meta_ref, f32[256,1]{1,0:T(8,128)S(1)} %reshape.86.ids_ref, f32[4,8,1024]{2,1,0:T(8,128)S(1)} %copy-done.12, bf16[256,8192]{1,0:T(8,128)(2,1)S(1)} %copy-done.1), custom_call_target="tpu_custom_call" | custom-call | flops 1073741824 | bytes 9437184 | tf_op jit(solution)/shard_map/shifted_rows/pallas_call | solution.py:181
  71.9 2.6 %partial_scores.2.refs_0_ = f32[256,128]{1,0:T(8,128)S(1)} custom-call(bf16[256,8192]{1,0:T(8,128)(2,1)S(1)} %get-tuple-element.29.refs_0_.refs_1_, bf16[32,4096]{1,0:T(8,128)(2,1)S(1)} %get-tuple-element.36.refs_1_, bf16[16,8192]{1,0:T(8,128)(2,1)S(1)} %copy-done.13, bf16[16,8192]{1,0:T(8,128)(2,1)S(1)} %collective-permute-done.6.refs_3_.refs_7_, ...), custom_call_target="tpu_custom_call" | custom-call | flops 536870912 | bytes 6291456 | tf_op jit(solution)/shard_map/partial_scores/pallas_call | solution.py:238
  78.5 2.0 %posterior.1.refs_5_ = bf16[128,256]{1,0:T(8,128)(2,1)} custom-call(f32[256,128]{1,0:T(8,128)} %copy-done.17, f32[256,128]{1,0:T(8,128)} %copy-done.18, f32[256,128]{1,0:T(8,128)} %copy-done.19, f32[256,128]{1,0:T(8,128)} %copy-done.20), custom_call_target="tpu_custom_call" | custom-call | tf_op jit(solution)/shard_map/posterior/pallas_call | solution.py:268
  82.6 2.7 %collective-permute-done.17.refs_7_ = bf16[128,256]{1,0:T(8,128)(2,1)S(1)} collective-permute-done((bf16[128,256]{1,0:T(8,128)(2,1)}, bf16[128,256]{1,0:T(8,128)(2,1)S(1)}, u32[]{:S(2)}, u32[]{:S(2)}) %collective-permute-start.17) | collective-permute-done | bytes 65568 | tf_op jit(solution)/shard_map/ppermute | solution.py:47
  87.1 2.2 %copy-done.3 = bf16[256,8192]{1,0:T(8,128)(2,1)S(1)} copy-done((bf16[256,8192]{1,0:T(8,128)(2,1)S(1)}, bf16[256,8192]{1,0:T(8,128)(2,1)}, u32[]{:S(2)}) %copy-start.3) | copy-done | bytes 4194328
  89.3 2.2 %copy-done.6 = bf16[256,8192]{1,0:T(8,128)(2,1)S(1)} copy-done((bf16[256,8192]{1,0:T(8,128)(2,1)S(1)}, bf16[256,8192]{1,0:T(8,128)(2,1)}, u32[]{:S(2)}) %copy-start.6) | copy-done | bytes 4194328
  91.5 2.2 %copy-done.9 = bf16[256,8192]{1,0:T(8,128)(2,1)S(1)} copy-done((bf16[256,8192]{1,0:T(8,128)(2,1)S(1)}, bf16[256,8192]{1,0:T(8,128)(2,1)}, u32[]{:S(2)}) %copy-start.9) | copy-done | bytes 4194328
  94.5 4.5 %weighted_sums.2 = (bf16[32,4096]{1,0:T(8,128)(2,1)S(1)}, bf16[32,4096]{1,0:T(8,128)(2,1)S(1)}, bf16[32,4096]{1,0:T(8,128)(2,1)S(1)}, bf16[32,4096]{1,0:T(8,128)(2,1)S(1)}) custom-call(s32[4]{0:T(128)S(1)} %and_select_fusion.refs_0_, bf16[256,8192]{1,0:T(8,128)(2,1)S(1)} %copy-done.3, bf16[256,8192]{1,0:T(8,128)(2,1)S(1)} %copy-done.6, ...), custom_call_target="tpu_custom_call" | custom-call | flops 1073741824 | bytes 9437184 | tf_op jit(solution)/shard_map/weighted_sums/pallas_call | solution.py:295
  99.0 2.3 %collective-permute-start.21 = (bf16[32,4096]{1,0:T(8,128)(2,1)S(1)}, bf16[32,4096]{1,0:T(8,128)(2,1)S(1)}, u32[]{:S(2)}, u32[]{:S(2)}) collective-permute-start(bf16[32,4096]{1,0:T(8,128)(2,1)S(1)} %get-tuple-element.46), channel_id=1, source_target_pairs={{0,192},{1,193},{2,194},{3,195},{4,196},{5,197},{6,198},{7,199},{8... | collective-permute-start | bytes 786440 | tf_op jit(solution)/shard_map/ppermute | solution.py:47
  111.2 2.2 %copy-done.4 = bf16[256,8192]{1,0:T(8,128)(2,1)S(1)} copy-done((bf16[256,8192]{1,0:T(8,128)(2,1)S(1)}, bf16[256,8192]{1,0:T(8,128)(2,1)}, u32[]{:S(2)}) %copy-start.4) | copy-done | bytes 4194328
  113.4 2.2 %copy-done.7 = bf16[256,8192]{1,0:T(8,128)(2,1)S(1)} copy-done((bf16[256,8192]{1,0:T(8,128)(2,1)S(1)}, bf16[256,8192]{1,0:T(8,128)(2,1)}, u32[]{:S(2)}) %copy-start.7) | copy-done | bytes 4194328
  115.6 2.2 %copy-done.10 = bf16[256,8192]{1,0:T(8,128)(2,1)S(1)} copy-done((bf16[256,8192]{1,0:T(8,128)(2,1)S(1)}, bf16[256,8192]{1,0:T(8,128)(2,1)}, u32[]{:S(2)}) %copy-start.10) | copy-done | bytes 4194328
  117.8 4.5 %weighted_sums.3 = (bf16[64,2048]{1,0:T(8,128)(2,1)S(1)}, bf16[64,2048]{1,0:T(8,128)(2,1)S(1)}, bf16[64,2048]{1,0:T(8,128)(2,1)S(1)}, bf16[64,2048]{1,0:T(8,128)(2,1)S(1)}) custom-call(s32[4]{0:T(128)S(1)} %and_select_fusion.refs_0_, bf16[256,8192]{1,0:T(8,128)(2,1)S(1)} %copy-done.4, bf16[256,8192]{1,0:T(8,128)(2,1)S(1)} %copy-done.7, ...), custom_call_target="tpu_custom_call" | custom-call | flops 1073741824 | bytes 9437184 | tf_op jit(solution)/shard_map/weighted_sums/pallas_call | solution.py:295
  123.1 2.1 %collective-permute-start.26 = (bf16[64,2048]{1,0:T(8,128)(2,1)S(1)}, bf16[64,2048]{1,0:T(8,128)(2,1)S(1)}, u32[]{:S(2)}, u32[]{:S(2)}) collective-permute-start(bf16[64,2048]{1,0:T(8,128)(2,1)S(1)} %get-tuple-element.49), channel_id=1, source_target_pairs={{0,16},{1,17},{2,18},{3,19},{4,20},{5,21},{6,22},{7,23},{8,24},{9,... | collective-permute-start | bytes 786440 | tf_op jit(solution)/shard_map/ppermute | solution.py:47
  133.7 4.4 %collective-permute-done.26 = bf16[64,2048]{1,0:T(8,128)(2,1)S(1)} collective-permute-done((bf16[64,2048]{1,0:T(8,128)(2,1)S(1)}, bf16[64,2048]{1,0:T(8,128)(2,1)S(1)}, u32[]{:S(2)}, u32[]{:S(2)}) %collective-permute-start.26) | collective-permute-done | bytes 262176 | tf_op jit(solution)/shard_map/ppermute | solution.py:47
  139.8 3.0 %collective-permute-start.30 = (bf16[16,2048]{1,0:T(8,128)(2,1)S(1)}, bf16[16,2048]{1,0:T(8,128)(2,1)S(1)}, u32[]{:S(2)}, u32[]{:S(2)}) collective-permute-start(bf16[16,2048]{1,0:T(8,128)(2,1)S(1)} %get-tuple-element.57), channel_id=1, source_target_pairs={{0,192},{1,193},{2,194},{3,195},{4,196},{5,197},{6,198},{7,199},{8... | collective-permute-start | bytes 196616 | tf_op jit(solution)/shard_map/ppermute | solution.py:47
  145.4 3.3 %collective-permute-done.29 = bf16[16,2048]{1,0:T(8,128)(2,1)S(1)} collective-permute-done((bf16[16,2048]{1,0:T(8,128)(2,1)S(1)}, bf16[16,2048]{1,0:T(8,128)(2,1)S(1)}, u32[]{:S(2)}, u32[]{:S(2)}) %collective-permute-start.29) | collective-permute-done | bytes 65568 | tf_op jit(solution)/shard_map/ppermute | solution.py:47
  149.7 5.5 %collective-permute-start.33 = (bf16[16,1024]{1,0:T(8,128)(2,1)S(1)}, bf16[16,1024]{1,0:T(8,128)(2,1)S(1)}, u32[]{:S(2)}, u32[]{:S(2)}) collective-permute-start(bf16[16,1024]{1,0:T(8,128)(2,1)S(1)} %bitcast.107), channel_id=1, source_target_pairs={{0,12},{1,13},{2,14},{3,15},{4,0},{5,1},{6,2},{7,3},{8,4},{9,5},{1... | collective-permute-start | bytes 98312 | tf_op jit(solution)/shard_map/ppermute | solution.py:47
  156.7 2.5 %collective-permute-start.31 = (bf16[16,1024]{1,0:T(8,128)(2,1)S(1)}, bf16[16,1024]{1,0:T(8,128)(2,1)S(1)}, u32[]{:S(2)}, u32[]{:S(2)}) collective-permute-start(bf16[16,1024]{1,0:T(8,128)(2,1)S(1)} %bitcast.109), channel_id=1, source_target_pairs={{0,4},{1,5},{2,6},{3,7},{4,8},{5,9},{6,10},{7,11},{8,12},{9,13},{1... | collective-permute-start | bytes 98312 | tf_op jit(solution)/shard_map/ppermute | solution.py:47
  159.3 3.9 %collective-permute-done.32 = bf16[16,1024]{1,0:T(8,128)(2,1)S(1)} collective-permute-done((bf16[16,1024]{1,0:T(8,128)(2,1)S(1)}, bf16[16,1024]{1,0:T(8,128)(2,1)S(1)}, u32[]{:S(2)}, u32[]{:S(2)}) %collective-permute-start.32) | collective-permute-done | bytes 32800 | tf_op jit(solution)/shard_map/ppermute | solution.py:47
  (160 shorter events, 45.5 us)
Async XLA Ops:
  2.9 20.0 %collective-permute-start.5 = (f32[32,73]{0,1:T(8,128)S(1)}, f32[32,73]{0,1:T(8,128)S(1)}, u32[]{:S(2)}, u32[]{:S(2)}) collective-permute-start(f32[32,73]{0,1:T(8,128)S(1)} %pad_maximum_fusion), channel_id=1, source_target_pairs={{0,3},{1,2},{2,1},{3,0},{4,7},{5,6},{6,5},{7,4},{8,11},{9,10},{10,... | collective-permute-start | bytes 28040 | tf_op jit(solution)/shard_map/ppermute | solution.py:47
  4.3 19.7 %collective-permute-start.3 = (f32[32,73]{0,1:T(8,128)S(1)}, f32[32,73]{0,1:T(8,128)S(1)}, u32[]{:S(2)}, u32[]{:S(2)}) collective-permute-start(f32[32,73]{0,1:T(8,128)S(1)} %pad_maximum_fusion), channel_id=1, source_target_pairs={{0,2},{1,3},{2,0},{3,1},{4,6},{5,7},{6,4},{7,5},{8,10},{9,11},{10,... | collective-permute-start | bytes 28040 | tf_op jit(solution)/shard_map/ppermute | solution.py:47
  5.0 19.1 %collective-permute-start.1 = (f32[32,73]{0,1:T(8,128)S(1)}, f32[32,73]{0,1:T(8,128)S(1)}, u32[]{:S(2)}, u32[]{:S(2)}) collective-permute-start(f32[32,73]{0,1:T(8,128)S(1)} %pad_maximum_fusion), channel_id=1, source_target_pairs={{0,1},{1,0},{2,3},{3,2},{4,5},{5,4},{6,7},{7,6},{8,9},{9,8},{10,11... | collective-permute-start | bytes 28040 | tf_op jit(solution)/shard_map/ppermute | solution.py:47
  7.8 18.3 %collective-permute-start.7 = (bf16[16,8192]{1,0:T(8,128)(2,1)}, bf16[16,8192]{1,0:T(8,128)(2,1)S(1)}, u32[]{:S(2)}, u32[]{:S(2)}) collective-permute-start(bf16[16,8192]{1,0:T(8,128)(2,1)} %arrange.3.refs_2_.refs_6_), channel_id=1, source_target_pairs={{0,192},{1,193},{2,194},{3,195},{4,196},{5,197},{6,198},{7,199},{8... | collective-permute-start | bytes 786440 | tf_op jit(solution)/shard_map/ppermute | solution.py:47
  10.8 16.2 %collective-permute-start.9 = (bf16[16,8192]{1,0:T(8,128)(2,1)}, bf16[16,8192]{1,0:T(8,128)(2,1)S(1)}, u32[]{:S(2)}, u32[]{:S(2)}) collective-permute-start(bf16[16,8192]{1,0:T(8,128)(2,1)} %arrange.3.refs_2_.refs_6_), channel_id=1, source_target_pairs={{0,128},{1,129},{2,130},{3,131},{4,132},{5,133},{6,134},{7,135},{8... | collective-permute-start | bytes 786440 | tf_op jit(solution)/shard_map/ppermute | solution.py:47
  22.9 9.4 %collective-permute-start.11 = (bf16[16,8192]{1,0:T(8,128)(2,1)S(1)}, bf16[16,8192]{1,0:T(8,128)(2,1)S(1)}, u32[]{:S(2)}, u32[]{:S(2)}) collective-permute-start(bf16[16,8192]{1,0:T(8,128)(2,1)S(1)} %copy-done.13), channel_id=1, source_target_pairs={{0,64},{1,65},{2,66},{3,67},{4,68},{5,69},{6,70},{7,71},{8,72},{9,... | collective-permute-start | bytes 786440 | tf_op jit(solution)/shard_map/ppermute | solution.py:47
  24.0 8.9 %collective-permute-start = (bf16[32,8192]{1,0:T(8,128)(2,1)}, bf16[32,8192]{1,0:T(8,128)(2,1)S(1)}, u32[]{:S(2)}, u32[]{:S(2)}) collective-permute-start(bf16[32,8192]{1,0:T(8,128)(2,1)} %get-tuple-element.30), channel_id=1, source_target_pairs={{0,1},{1,0},{2,3},{3,2},{4,5},{5,4},{6,7},{7,6},{8,9},{9,8},{10,11... | collective-permute-start | bytes 1572872 | tf_op jit(solution)/shard_map/ppermute | solution.py:47
  24.0 15.0 %collective-permute-start.2 = (bf16[32,8192]{1,0:T(8,128)(2,1)}, bf16[32,8192]{1,0:T(8,128)(2,1)S(1)}, u32[]{:S(2)}, u32[]{:S(2)}) collective-permute-start(bf16[32,8192]{1,0:T(8,128)(2,1)} %get-tuple-element.32), channel_id=1, source_target_pairs={{0,2},{1,3},{2,0},{3,1},{4,6},{5,7},{6,4},{7,5},{8,10},{9,11},{10,... | collective-permute-start | bytes 1572872 | tf_op jit(solution)/shard_map/ppermute | solution.py:47
  26.1 23.8 %collective-permute-start.4 = (bf16[32,8192]{1,0:T(8,128)(2,1)}, bf16[32,8192]{1,0:T(8,128)(2,1)S(1)}, u32[]{:S(2)}, u32[]{:S(2)}) collective-permute-start(bf16[32,8192]{1,0:T(8,128)(2,1)} %get-tuple-element.34), channel_id=1, source_target_pairs={{0,3},{1,2},{2,1},{3,0},{4,7},{5,6},{6,5},{7,4},{8,11},{9,10},{10,... | collective-permute-start | bytes 1572872 | tf_op jit(solution)/shard_map/ppermute | solution.py:47
  27.1 28.5 %collective-permute-start.6 = (bf16[16,8192]{1,0:T(8,128)(2,1)S(1)}, bf16[16,8192]{1,0:T(8,128)(2,1)S(1)}, u32[]{:S(2)}, u32[]{:S(2)}) collective-permute-start(bf16[16,8192]{1,0:T(8,128)(2,1)S(1)} %copy-done.13), channel_id=1, source_target_pairs={{0,48},{1,49},{2,50},{3,51},{4,52},{5,53},{6,54},{7,55},{8,56},{9,... | collective-permute-start | bytes 786440 | tf_op jit(solution)/shard_map/ppermute | solution.py:47
  32.3 23.2 %collective-permute-start.8 = (bf16[16,8192]{1,0:T(8,128)(2,1)S(1)}, bf16[16,8192]{1,0:T(8,128)(2,1)S(1)}, u32[]{:S(2)}, u32[]{:S(2)}) collective-permute-start(bf16[16,8192]{1,0:T(8,128)(2,1)S(1)} %collective-permute-done.7.refs_4_.refs_8_), channel_id=1, source_target_pairs={{0,48},{1,49},{2,50},{3,51},{4,52},{5,53},{6,54},{7,55},{8,56},{9,... | collective-permute-start | bytes 786440 | tf_op jit(solution)/shard_map/ppermute | solution.py:47
  32.9 22.7 %collective-permute-start.10 = (bf16[16,8192]{1,0:T(8,128)(2,1)S(1)}, bf16[16,8192]{1,0:T(8,128)(2,1)S(1)}, u32[]{:S(2)}, u32[]{:S(2)}) collective-permute-start(bf16[16,8192]{1,0:T(8,128)(2,1)S(1)} %collective-permute-done.9.refs_6_.refs_10_), channel_id=1, source_target_pairs={{0,32},{1,33},{2,34},{3,35},{4,36},{5,37},{6,38},{7,39},{8,40},{9,... | collective-permute-start | bytes 786440 | tf_op jit(solution)/shard_map/ppermute | solution.py:47
  39.1 16.5 %collective-permute-start.12 = (bf16[16,8192]{1,0:T(8,128)(2,1)S(1)}, bf16[16,8192]{1,0:T(8,128)(2,1)S(1)}, u32[]{:S(2)}, u32[]{:S(2)}) collective-permute-start(bf16[16,8192]{1,0:T(8,128)(2,1)S(1)} %collective-permute-done.11.refs_8_.refs_12_), channel_id=1, source_target_pairs={{0,32},{1,33},{2,34},{3,35},{4,36},{5,37},{6,38},{7,39},{8,40},{9,... | collective-permute-start | bytes 786440 | tf_op jit(solution)/shard_map/ppermute | solution.py:47
  66.3 10.8 %collective-permute-start.13 = (f32[256,128]{1,0:T(8,128)S(1)}, f32[256,128]{1,0:T(8,128)S(1)}, u32[]{:S(2)}, u32[]{:S(2)}) collective-permute-start(f32[256,128]{1,0:T(8,128)S(1)} %get-tuple-element.40), channel_id=1, source_target_pairs={{0,1},{1,0},{2,3},{3,2},{4,5},{5,4},{6,7},{7,6},{8,9},{9,8},{10,11... | collective-permute-start | bytes 393224 | tf_op jit(solution)/shard_map/ppermute | solution.py:47
  66.4 10.7 %collective-permute-start.14 = (f32[256,128]{1,0:T(8,128)S(1)}, f32[256,128]{1,0:T(8,128)S(1)}, u32[]{:S(2)}, u32[]{:S(2)}) collective-permute-start(f32[256,128]{1,0:T(8,128)S(1)} %get-tuple-element.41), channel_id=1, source_target_pairs={{0,2},{1,3},{2,0},{3,1},{4,6},{5,7},{6,4},{7,5},{8,10},{9,11},{10,... | collective-permute-start | bytes 393224 | tf_op jit(solution)/shard_map/ppermute | solution.py:47
  68.3 8.9 %collective-permute-start.15 = (f32[256,128]{1,0:T(8,128)S(1)}, f32[256,128]{1,0:T(8,128)S(1)}, u32[]{:S(2)}, u32[]{:S(2)}) collective-permute-start(f32[256,128]{1,0:T(8,128)S(1)} %get-tuple-element.42), channel_id=1, source_target_pairs={{0,3},{1,2},{2,1},{3,0},{4,7},{5,6},{6,5},{7,4},{8,11},{9,10},{10,... | collective-permute-start | bytes 393224 | tf_op jit(solution)/shard_map/ppermute | solution.py:47
  82.6 4.5 %collective-permute-start.18 = (bf16[128,256]{1,0:T(8,128)(2,1)}, bf16[128,256]{1,0:T(8,128)(2,1)S(1)}, u32[]{:S(2)}, u32[]{:S(2)}) collective-permute-start(bf16[128,256]{1,0:T(8,128)(2,1)} %posterior.1.refs_5_), channel_id=1, source_target_pairs={{0,3},{1,2},{2,1},{3,0},{4,7},{5,6},{6,5},{7,4},{8,11},{9,10},{10,... | collective-permute-start | bytes 196616 | tf_op jit(solution)/shard_map/ppermute | solution.py:47
  99.0 26.3 %collective-permute-start.21 = (bf16[32,4096]{1,0:T(8,128)(2,1)S(1)}, bf16[32,4096]{1,0:T(8,128)(2,1)S(1)}, u32[]{:S(2)}, u32[]{:S(2)}) collective-permute-start(bf16[32,4096]{1,0:T(8,128)(2,1)S(1)} %get-tuple-element.46), channel_id=1, source_target_pairs={{0,192},{1,193},{2,194},{3,195},{4,196},{5,197},{6,198},{7,199},{8... | collective-permute-start | bytes 786440 | tf_op jit(solution)/shard_map/ppermute | solution.py:47
  101.3 25.7 %collective-permute-start.20 = (bf16[32,4096]{1,0:T(8,128)(2,1)S(1)}, bf16[32,4096]{1,0:T(8,128)(2,1)S(1)}, u32[]{:S(2)}, u32[]{:S(2)}) collective-permute-start(bf16[32,4096]{1,0:T(8,128)(2,1)S(1)} %get-tuple-element.45), channel_id=1, source_target_pairs={{0,128},{1,129},{2,130},{3,131},{4,132},{5,133},{6,134},{7,135},{8... | collective-permute-start | bytes 786440 | tf_op jit(solution)/shard_map/ppermute | solution.py:47
  103.0 24.0 %collective-permute-start.19 = (bf16[32,4096]{1,0:T(8,128)(2,1)S(1)}, bf16[32,4096]{1,0:T(8,128)(2,1)}, u32[]{:S(2)}, u32[]{:S(2)}) collective-permute-start(bf16[32,4096]{1,0:T(8,128)(2,1)S(1)} %get-tuple-element.44), channel_id=1, source_target_pairs={{0,64},{1,65},{2,66},{3,67},{4,68},{5,69},{6,70},{7,71},{8,72},{9,... | collective-permute-start | bytes 786440 | tf_op jit(solution)/shard_map/ppermute | solution.py:47
  122.3 10.1 %collective-permute-start.27 = (bf16[64,2048]{1,0:T(8,128)(2,1)S(1)}, bf16[64,2048]{1,0:T(8,128)(2,1)S(1)}, u32[]{:S(2)}, u32[]{:S(2)}) collective-permute-start(bf16[64,2048]{1,0:T(8,128)(2,1)S(1)} %get-tuple-element.50), channel_id=1, source_target_pairs={{0,48},{1,49},{2,50},{3,51},{4,52},{5,53},{6,54},{7,55},{8,56},{9,... | collective-permute-start | bytes 786440 | tf_op jit(solution)/shard_map/ppermute | solution.py:47
  123.1 15.0 %collective-permute-start.26 = (bf16[64,2048]{1,0:T(8,128)(2,1)S(1)}, bf16[64,2048]{1,0:T(8,128)(2,1)S(1)}, u32[]{:S(2)}, u32[]{:S(2)}) collective-permute-start(bf16[64,2048]{1,0:T(8,128)(2,1)S(1)} %get-tuple-element.49), channel_id=1, source_target_pairs={{0,16},{1,17},{2,18},{3,19},{4,20},{5,21},{6,22},{7,23},{8,24},{9,... | collective-permute-start | bytes 786440 | tf_op jit(solution)/shard_map/ppermute | solution.py:47
  125.3 14.0 %collective-permute-start.25 = (bf16[64,2048]{1,0:T(8,128)(2,1)S(1)}, bf16[64,2048]{1,0:T(8,128)(2,1)S(1)}, u32[]{:S(2)}, u32[]{:S(2)}) collective-permute-start(bf16[64,2048]{1,0:T(8,128)(2,1)S(1)} %get-tuple-element.48), channel_id=1, source_target_pairs={{0,32},{1,33},{2,34},{3,35},{4,36},{5,37},{6,38},{7,39},{8,40},{9,... | collective-permute-start | bytes 786440 | tf_op jit(solution)/shard_map/ppermute | solution.py:47
  128.6 14.9 %collective-permute-start.24 = (bf16[16,2048]{1,0:T(8,128)(2,1)S(1)}, bf16[16,2048]{1,0:T(8,128)(2,1)S(1)}, u32[]{:S(2)}, u32[]{:S(2)}) collective-permute-start(bf16[16,2048]{1,0:T(8,128)(2,1)S(1)} %bitcast.100), channel_id=1, source_target_pairs={{0,48},{1,49},{2,50},{3,51},{4,52},{5,53},{6,54},{7,55},{8,56},{9,... | collective-permute-start | bytes 196616 | tf_op jit(solution)/shard_map/ppermute | solution.py:47
  129.4 14.4 %collective-permute-start.23 = (bf16[16,2048]{1,0:T(8,128)(2,1)S(1)}, bf16[16,2048]{1,0:T(8,128)(2,1)S(1)}, u32[]{:S(2)}, u32[]{:S(2)}) collective-permute-start(bf16[16,2048]{1,0:T(8,128)(2,1)S(1)} %bitcast.101), channel_id=1, source_target_pairs={{0,16},{1,17},{2,18},{3,19},{4,20},{5,21},{6,22},{7,23},{8,24},{9,... | collective-permute-start | bytes 196616 | tf_op jit(solution)/shard_map/ppermute | solution.py:47
  132.4 11.5 %collective-permute-start.22 = (bf16[16,2048]{1,0:T(8,128)(2,1)S(1)}, bf16[16,2048]{1,0:T(8,128)(2,1)S(1)}, u32[]{:S(2)}, u32[]{:S(2)}) collective-permute-start(bf16[16,2048]{1,0:T(8,128)(2,1)S(1)} %bitcast.102), channel_id=1, source_target_pairs={{0,32},{1,33},{2,34},{3,35},{4,36},{5,37},{6,38},{7,39},{8,40},{9,... | collective-permute-start | bytes 196616 | tf_op jit(solution)/shard_map/ppermute | solution.py:47
  139.8 5.5 %collective-permute-start.30 = (bf16[16,2048]{1,0:T(8,128)(2,1)S(1)}, bf16[16,2048]{1,0:T(8,128)(2,1)S(1)}, u32[]{:S(2)}, u32[]{:S(2)}) collective-permute-start(bf16[16,2048]{1,0:T(8,128)(2,1)S(1)} %get-tuple-element.57), channel_id=1, source_target_pairs={{0,192},{1,193},{2,194},{3,195},{4,196},{5,197},{6,198},{7,199},{8... | collective-permute-start | bytes 196616 | tf_op jit(solution)/shard_map/ppermute | solution.py:47
  142.9 5.8 %collective-permute-start.29 = (bf16[16,2048]{1,0:T(8,128)(2,1)S(1)}, bf16[16,2048]{1,0:T(8,128)(2,1)S(1)}, u32[]{:S(2)}, u32[]{:S(2)}) collective-permute-start(bf16[16,2048]{1,0:T(8,128)(2,1)S(1)} %get-tuple-element.58), channel_id=1, source_target_pairs={{0,128},{1,129},{2,130},{3,131},{4,132},{5,133},{6,134},{7,135},{8... | collective-permute-start | bytes 196616 | tf_op jit(solution)/shard_map/ppermute | solution.py:47
  143.5 5.8 %collective-permute-start.28 = (bf16[16,2048]{1,0:T(8,128)(2,1)S(1)}, bf16[16,2048]{1,0:T(8,128)(2,1)S(1)}, u32[]{:S(2)}, u32[]{:S(2)}) collective-permute-start(bf16[16,2048]{1,0:T(8,128)(2,1)S(1)} %get-tuple-element.56), channel_id=1, source_target_pairs={{0,64},{1,65},{2,66},{3,67},{4,68},{5,69},{6,70},{7,71},{8,72},{9,... | collective-permute-start | bytes 196616 | tf_op jit(solution)/shard_map/ppermute | solution.py:47
  149.7 9.6 %collective-permute-start.33 = (bf16[16,1024]{1,0:T(8,128)(2,1)S(1)}, bf16[16,1024]{1,0:T(8,128)(2,1)S(1)}, u32[]{:S(2)}, u32[]{:S(2)}) collective-permute-start(bf16[16,1024]{1,0:T(8,128)(2,1)S(1)} %bitcast.107), channel_id=1, source_target_pairs={{0,12},{1,13},{2,14},{3,15},{4,0},{5,1},{6,2},{7,3},{8,4},{9,5},{1... | collective-permute-start | bytes 98312 | tf_op jit(solution)/shard_map/ppermute | solution.py:47
  155.2 8.0 %collective-permute-start.32 = (bf16[16,1024]{1,0:T(8,128)(2,1)S(1)}, bf16[16,1024]{1,0:T(8,128)(2,1)S(1)}, u32[]{:S(2)}, u32[]{:S(2)}) collective-permute-start(bf16[16,1024]{1,0:T(8,128)(2,1)S(1)} %bitcast.108), channel_id=1, source_target_pairs={{0,8},{1,9},{2,10},{3,11},{4,12},{5,13},{6,14},{7,15},{8,0},{9,1},... | collective-permute-start | bytes 98312 | tf_op jit(solution)/shard_map/ppermute | solution.py:47
  156.7 6.8 %collective-permute-start.31 = (bf16[16,1024]{1,0:T(8,128)(2,1)S(1)}, bf16[16,1024]{1,0:T(8,128)(2,1)S(1)}, u32[]{:S(2)}, u32[]{:S(2)}) collective-permute-start(bf16[16,1024]{1,0:T(8,128)(2,1)S(1)} %bitcast.109), channel_id=1, source_target_pairs={{0,4},{1,5},{2,6},{3,7},{4,8},{5,9},{6,10},{7,11},{8,12},{9,13},{1... | collective-permute-start | bytes 98312 | tf_op jit(solution)/shard_map/ppermute | solution.py:47
  (24 other events, 136.1 us)

commit v2 on v1

v2 whole, which is shorter than its diff:
```python
import math

import jax
import jax.numpy as jnp
import numpy as np
from jax import lax
from jax.experimental import pallas as pl
from jax.experimental.pallas import tpu as pltpu
from jax.sharding import PartitionSpec as P

BOX = 32
TILTS = 32
SHIFTS = 8
P_DEV = 32
Y, X, Z = 4, 4, 8
COLS = 1024
HALF = 512
G = 4
NB = 16 // G
ROWS = P_DEV * SHIFTS
WIDTH = NB * 2 * COLS
EXTRA = 384
AXES = ("blk", "dom")
F32, BF16 = jnp.float32, jnp.bfloat16
NT = (((1,), (1,)), ((), ()))
MIB = 1 << 20


def linear(y, x, z, core):
    y, x, z = y % Y, x % X, z % Z
    return (y * 2 + x % 2) * 32 + (x // 2) * 16 + z * 2 + core


def moves(dy=0, dx=0, dz=0):
    return [
        (linear(y, x, z, c), linear(y + dy, x + dx, z + dz, c))
        for y in range(Y) for x in range(X) for z in range(Z) for c in range(2)
    ]


def partners(k):
    return [
        (linear(y, x, z, c), linear(y, x, z ^ (k >> 1), c ^ (k & 1)))
        for y in range(Y) for x in range(X) for z in range(Z) for c in range(2)
    ]


def send(value, pairs):
    return lax.ppermute(value, AXES, pairs)


def geometry():
    position = np.arange(TILTS * HALF)
    tilt, within = position // HALF, position % HALF
    radial = (within // BOX).astype(np.float64)
    lateral = (within % BOX - BOX // 2).astype(np.float64)
    angle = (tilt - 0.5 * (TILTS - 1)) * (2.0 / TILTS)
    shell = (radial * radial + lateral * lateral) / (0.25 * BOX * BOX)
    zero = np.zeros_like(shell)
    table = np.stack([radial * np.cos(angle), lateral, radial * np.sin(angle), shell] + [zero] * 4)
    return table.reshape(8, 16, COLS).transpose(1, 0, 2).astype(np.float32)


def translations():
    ids = np.arange(128)
    out = np.zeros((128, 8), np.float32)
    for column, digit in enumerate((ids // 25, ids // 5 % 5, ids % 5)):
        out[:, column] = (digit - 2) * 0.5 / BOX
    out[125:] = 0
    return out


def fold(turns):
    turns = turns - jnp.floor(turns + 0.5)
    far = jnp.abs(turns) > 0.25
    near = jnp.where(far, jnp.where(turns > 0, 0.5, -0.5) - turns, turns)
    return near * (2.0 * math.pi), far


def series(square, terms):
    total = jnp.full_like(square, terms[-1])
    for term in terms[-2::-1]:
        total = total * square + term
    return total


SIN_TERMS = [(-1) ** n / math.factorial(2 * n + 1) for n in range(6)]
COS_TERMS = [(-1) ** n / math.factorial(2 * n) for n in range(7)]


def sine_turns(turns):
    angle, _ = fold(turns)
    return angle * series(angle * angle, SIN_TERMS)


def table_kernel(member_ref, geo_ref, shift_ref, out_ref):
    geo = geo_ref[0]
    shift = shift_ref[...]
    turns = shift[:, 0:1] * geo[0:1] + shift[:, 1:2] * geo[1:2] + shift[:, 2:3] * geo[2:3]
    angle, far = fold(turns)
    square = angle * angle
    sine = angle * series(square, SIN_TERMS)
    cosine = series(square, COS_TERMS)
    cosine = jnp.where(far, -cosine, cosine)
    for tilt in range(2):
        for part, values in enumerate((cosine, sine)):
            values = values[:, tilt * HALF : (tilt + 1) * HALF]
            high = values.astype(BF16)
            low = (values - high.astype(F32)).astype(BF16)
            lanes = slice(tilt * COLS + part * HALF, tilt * COLS + (part + 1) * HALF)
            out_ref[0:128, lanes] = high
            out_ref[128:256, lanes] = low


def make_table(member, geo):
    return pl.pallas_call(
        table_kernel,
        grid_spec=pltpu.PrefetchScalarGridSpec(
            num_scalar_prefetch=1,
            grid=(NB,),
            in_specs=[
                pl.BlockSpec((1, 8, COLS), lambda b, m: (b * G + m[0], 0, 0)),
                pl.BlockSpec((128, 8), lambda b, m: (0, 0)),
            ],
            out_specs=pl.BlockSpec((256, 2 * COLS), lambda b, m: (0, b)),
        ),
        out_shape=jax.ShapeDtypeStruct((256, WIDTH), BF16),
        cost_estimate=pl.CostEstimate(flops=NB * 128 * COLS * 40, bytes_accessed=4 * MIB, transcendentals=0),
        compiler_params=pltpu.CompilerParams(vmem_limit_bytes=12 * MIB),
        name="phase_table",
    )(member, geo, jnp.asarray(translations()))


def column(part, block, who):
    return pl.ds(pl.multiple_of((part * 16 + block * G + who) * COLS, COLS), COLS)


def own_kernel(member_ref, source, out):
    for block in range(NB):
        for part in range(2):
            spot = (block * 2 + part) * COLS
            out[:, spot : spot + COLS] = source[:, column(part, block, member_ref[0])]


def own_columns(member, refs):
    return pl.pallas_call(
        own_kernel,
        in_specs=[pl.BlockSpec(memory_space=pltpu.SMEM), pl.BlockSpec(memory_space=pltpu.VMEM)],
        out_specs=pl.BlockSpec(memory_space=pltpu.VMEM),
        out_shape=jax.ShapeDtypeStruct((16, WIDTH), BF16),
        cost_estimate=pl.CostEstimate(flops=0, bytes_accessed=2 * MIB, transcendentals=0),
        compiler_params=pltpu.CompilerParams(vmem_limit_bytes=8 * MIB),
        name="own_references",
    )(member, refs)


def split_kernel(member_ref, after, source, ids, wedge, focus, sigma, *outs):
    info = jnp.concatenate(
        [
            ids[...].astype(F32),
            wedge[...].astype(F32),
            focus[...],
            sigma[...],
            jnp.zeros((P_DEV, 128 - SHIFTS - 2 * TILTS - 1), F32),
        ],
        axis=1,
    )
    high = info.astype(BF16)
    rest = info - high.astype(F32)
    middle = rest.astype(BF16)
    low = (rest - middle.astype(F32)).astype(BF16)
    for n, out in enumerate(outs):
        who = member_ref[0] ^ n
        for block in range(NB):
            for part in range(2):
                spot = (block * 2 + part) * COLS
                out[:, spot : spot + COLS] = source[:, column(part, block, who)]
        for spot, piece in enumerate((high, middle, low)):
            out[:, WIDTH + spot * 128 : WIDTH + (spot + 1) * 128] = piece


def split_particles(member, after, particles, shift_ids, wedge, defocus, inv_sigma):
    return pl.pallas_call(
        split_kernel,
        in_specs=[pl.BlockSpec(memory_space=pltpu.SMEM), pl.BlockSpec(memory_space=pl.ANY)]
        + [pl.BlockSpec(memory_space=pltpu.VMEM)] * 5,
        out_specs=[pl.BlockSpec(memory_space=pltpu.VMEM)] * G,
        out_shape=[jax.ShapeDtypeStruct((P_DEV, WIDTH + EXTRA), BF16)] * G,
        cost_estimate=pl.CostEstimate(flops=0, bytes_accessed=5 * MIB, transcendentals=0),
        compiler_params=pltpu.CompilerParams(vmem_limit_bytes=8 * MIB),
        name="split_particles",
    )(member, after, particles, shift_ids, wedge, defocus, inv_sigma[:, None])


def rows_kernel(member_ref, x_ref, high_ref, middle_ref, low_ref, geo_ref, table_ref, rows_ref, pen_ref):
    info = high_ref[...].astype(F32) + middle_ref[...].astype(F32) + low_ref[...].astype(F32)
    lane = lax.broadcasted_iota(jnp.int32, (ROWS, 256), 1) & 127
    ids = jnp.concatenate([info[:, s : s + 1] for s in range(SHIFTS)], axis=0)
    pick = (ids == lane.astype(F32)).astype(BF16)
    at = SHIFTS + 2 * TILTS
    sigma = info[:, at : at + 1]
    small = lax.broadcasted_iota(jnp.int32, (P_DEV, 128), 1)
    first = 2 * (pl.program_id(0) * G + member_ref[0]) + SHIFTS
    weighting = []
    for tilt in range(2):
        kept = jnp.sum(jnp.where(small == first + tilt, info, 0.0), axis=1, keepdims=True)
        focus = jnp.sum(jnp.where(small == first + tilt + TILTS, info, 0.0), axis=1, keepdims=True)
        lanes = slice(tilt * HALF, (tilt + 1) * HALF)
        shell = geo_ref[0, 3:4, lanes]
        transfer = -sine_turns((4.0 * focus * shell + 0.1) * (0.5 / math.pi))
        weight = kept * transfer * sigma
        pen_ref[:, lanes] = (0.5 * weight * transfer).astype(BF16)
        weighting.append(weight)
    for tilt in range(2):
        lanes = slice(tilt * HALF, (tilt + 1) * HALF)
        upper = slice(COLS + tilt * HALF, COLS + (tilt + 1) * HALF)
        real = (weighting[tilt] * x_ref[:, lanes].astype(F32))[None]
        imag = (weighting[tilt] * x_ref[:, upper].astype(F32))[None]
        turned = jnp.dot(
            pick, table_ref[:, tilt * COLS : (tilt + 1) * COLS], preferred_element_type=F32
        ).reshape(SHIFTS, P_DEV, COLS)
        cosine, sine = turned[:, :, :HALF], turned[:, :, HALF:]
        rows_ref[:, lanes] = (real * cosine + imag * sine).reshape(ROWS, HALF).astype(BF16)
        rows_ref[:, upper] = (imag * cosine - real * sine).reshape(ROWS, HALF).astype(BF16)


def make_rows(member, x, geo, table):
    extra = WIDTH // 128
    return pl.pallas_call(
        rows_kernel,
        grid_spec=pltpu.PrefetchScalarGridSpec(
            num_scalar_prefetch=1,
            grid=(NB,),
            in_specs=[
                pl.BlockSpec((P_DEV, 2 * COLS), lambda b, m: (0, b)),
                pl.BlockSpec((P_DEV, 128), lambda b, m: (0, extra)),
                pl.BlockSpec((P_DEV, 128), lambda b, m: (0, extra + 1)),
                pl.BlockSpec((P_DEV, 128), lambda b, m: (0, extra + 2)),
                pl.BlockSpec((1, 8, COLS), lambda b, m: (b * G + m[0], 0, 0)),
                pl.BlockSpec((256, 2 * COLS), lambda b, m: (0, b)),
            ],
            out_specs=[
                pl.BlockSpec((ROWS, 2 * COLS), lambda b, m: (0, b)),
                pl.BlockSpec((P_DEV, COLS), lambda b, m: (0, b)),
            ],
        ),
        out_shape=[
            jax.ShapeDtypeStruct((ROWS, WIDTH), BF16),
            jax.ShapeDtypeStruct((P_DEV, NB * COLS), BF16),
        ],
        cost_estimate=pl.CostEstimate(
            flops=2 * ROWS * 256 * WIDTH, bytes_accessed=9 * MIB, transcendentals=0
        ),
        compiler_params=pltpu.CompilerParams(vmem_limit_bytes=16 * MIB),
        name="shifted_rows",
    )(member, x, x, x, x, geo, table)


def scores_kernel(count, *refs):
    blocks = refs[2 * count : 2 * count + 8]
    outs = refs[2 * count + 8 :]
    stacked = jnp.concatenate([block[...] for block in blocks], axis=0)
    real, imag = stacked[:, :COLS].astype(F32), stacked[:, COLS:].astype(F32)
    power = (real * real + imag * imag).astype(BF16)
    first = pl.program_id(0) == 0
    for n in range(count):
        rows, pen, out = refs[n], refs[count + n], outs[n]
        energy = lax.dot_general(pen[...], power, NT, preferred_element_type=F32)
        fresh = lax.dot_general(rows[...], stacked, NT, preferred_element_type=F32)
        fresh = (fresh.reshape(SHIFTS, P_DEV, 128) - energy[None]).reshape(ROWS, 128)

        @pl.when(first)
        def _(out=out, fresh=fresh):
            out[...] = fresh

        @pl.when(jnp.logical_not(first))
        def _(out=out, fresh=fresh):
            out[...] += fresh


def make_scores(rows, pens, blocks):
    count = len(rows)
    return pl.pallas_call(
        lambda *refs: scores_kernel(count, *refs),
        grid=(NB,),
        in_specs=[pl.BlockSpec((ROWS, 2 * COLS), lambda b: (0, b))] * count
        + [pl.BlockSpec((P_DEV, COLS), lambda b: (0, b))] * count
        + [pl.BlockSpec((16, 2 * COLS), lambda b: (0, b))] * 8,
        out_specs=[pl.BlockSpec((ROWS, 128), lambda b: (0, 0))] * count,
        out_shape=[jax.ShapeDtypeStruct((ROWS, 128), F32)] * count,
        cost_estimate=pl.CostEstimate(
            flops=2 * count * ROWS * 128 * WIDTH, bytes_accessed=(4 * count + 2) * MIB, transcendentals=0
        ),
        compiler_params=pltpu.CompilerParams(vmem_limit_bytes=20 * MIB),
        name="partial_scores",
    )(*rows, *pens, *blocks)


def posterior_kernel(*refs):
    out = refs[-1]
    total = refs[0][...]
    for other in refs[1:-1]:
        total = total + other[...]
    total = total.reshape(SHIFTS, P_DEV, 128)
    peak = jnp.max(jnp.max(total, axis=0), axis=1, keepdims=True)
    expo = jnp.exp(total - peak[None])
    norm = jnp.sum(jnp.sum(expo, axis=0), axis=1, keepdims=True)
    share = (expo / norm[None]).reshape(ROWS, 128)
    out[...] = share.T.astype(BF16)


def make_posterior(parts):
    return pl.pallas_call(
        posterior_kernel,
        out_shape=jax.ShapeDtypeStruct((128, ROWS), BF16),
        name="posterior",
    )(*parts)


def accum_kernel(part, flag_ref, *refs):
    real, imag, posts, outs = refs[:G], refs[G : 2 * G], refs[2 * G : 3 * G], refs[3 * G :]
    sums = []
    for rows in (real, imag):
        total = jnp.dot(posts[0][...], rows[0][...], preferred_element_type=F32)
        for n in range(1, G):
            total = total + jnp.dot(posts[n][...], rows[n][...], preferred_element_type=F32)
        sums.append(total)
    if part == 0:
        for n in range(Y):
            for half, total in enumerate(sums):
                outs[n][:, half * HALF : (half + 1) * HALF] = total[n * 32 : (n + 1) * 32].astype(BF16)
    else:
        for n in range(X):
            low = n & 1
            upper = flag_ref[n] == 1
            for k in range(Y):
                mine = slice(k * 32 + low * 16, k * 32 + low * 16 + 16)
                chosen = jnp.where(upper, sums[1][mine], sums[0][mine])
                outs[n][k * 16 : (k + 1) * 16] = chosen.astype(BF16)


def make_accum(part, flags, rows, posts):
    shape = (32, COLS) if part == 0 else (64, HALF)
    return pl.pallas_call(
        lambda *refs: accum_kernel(part, *refs),
        grid_spec=pltpu.PrefetchScalarGridSpec(
            num_scalar_prefetch=1,
            grid=(NB,),
            in_specs=[pl.BlockSpec((ROWS, HALF), lambda b, f: (0, 4 * b + part))] * G
            + [pl.BlockSpec((ROWS, HALF), lambda b, f: (0, 4 * b + 2 + part))] * G
            + [pl.BlockSpec((128, ROWS), lambda b, f: (0, 0))] * G,
            out_specs=[pl.BlockSpec(shape, lambda b, f: (0, b))] * 4,
        ),
        out_shape=[jax.ShapeDtypeStruct((shape[0], NB * shape[1]), BF16)] * 4,
        cost_estimate=pl.CostEstimate(
            flops=2 * G * ROWS * 128 * NB * COLS, bytes_accessed=(2 * G + 1) * MIB, transcendentals=0
        ),
        compiler_params=pltpu.CompilerParams(vmem_limit_bytes=16 * MIB),
        name="weighted_sums",
    )(flags, *rows, *rows, *posts)


def added(values):
    total = values[0].astype(F32)
    for value in values[1:]:
        total = total + value.astype(F32)
    return total


def per_device(refs, particles, shift_ids, wedge, defocus, inv_sigma):
    dom = lax.axis_index("dom")
    x_at = (dom // 16) * 2 + lax.axis_index("blk") % 2
    member = dom % G
    block = (dom % 16) // G
    member_arr = member.astype(jnp.int32).reshape(1)
    flags = (((x_at + jnp.arange(X)) % X) // 2).astype(jnp.int32)

    gathered = {}
    own = own_columns(member_arr, refs)
    gathered[0, 0] = own
    gathered[1, 0] = send(own, moves(dy=-1))
    gathered[3, 0] = send(own, moves(dy=1))
    gathered[0, 1] = send(own, moves(dx=-1))

    chunks = split_particles(member_arr, own, particles, shift_ids, wedge, defocus, inv_sigma)
    chunks = [chunks[0]] + [send(chunks[n], partners(n)) for n in range(1, G)]

    gathered[2, 0] = send(own, moves(dy=2))
    gathered[1, 1] = send(gathered[1, 0], moves(dx=-1))
    gathered[3, 1] = send(gathered[3, 0], moves(dx=1))
    gathered[2, 1] = send(gathered[2, 0], moves(dx=1))
    blocks = [gathered[ky, kx] for ky in range(Y) for kx in range(2)]

    geo = jnp.asarray(geometry())
    table = make_table(member_arr, geo)
    rows, pens = zip(*[make_rows(member_arr, chunk, geo, table) for chunk in chunks])

    early = make_scores(rows[: G - 1], pens[: G - 1], blocks)
    late = make_scores(rows[G - 1 :], pens[G - 1 :], blocks)
    parts = list(early) + list(late)
    arrived = [send(parts[n], partners(n)) for n in range(1, G)]
    posterior = make_posterior([parts[0]] + arrived)
    posts = [posterior] + [send(posterior, partners(n)) for n in range(1, G)]

    first = make_accum(0, flags, rows, posts)
    first = [first[0]] + [send(first[n], moves(dy=n)) for n in range(1, Y)]
    second = make_accum(1, flags, rows, posts)
    second = [second[0]] + [send(second[n], moves(dx=n)) for n in range(1, X)]

    first = added(first).reshape(2, 16, NB, 2, HALF)
    pieces = []
    for n in range(X):
        piece = lax.dynamic_index_in_dim(first[n & 1], flags[n], axis=2, keepdims=False)
        piece = piece.reshape(16, NB * HALF)
        pieces.append(piece if n == 0 else send(piece.astype(BF16), moves(dx=n)))
    first = added(pieces)

    second = added(second)
    pieces = []
    for n in range(Y):
        piece = second[n * 16 : (n + 1) * 16]
        pieces.append(piece if n == 0 else send(piece.astype(BF16), moves(dy=n)))
    second = added(pieces)

    joined = jnp.concatenate([first.reshape(16, NB, HALF), second.reshape(16, NB, HALF)], axis=2)
    pieces = []
    for n in range(NB):
        piece = lax.dynamic_index_in_dim(joined, (block + n) % NB, axis=1, keepdims=False)
        pieces.append(piece if n == 0 else send(piece.astype(BF16), moves(dz=n * (G // 2))))
    return added(pieces)


def solution(mesh):
    return jax.shard_map(
        per_device,
        mesh=mesh,
        in_specs=(
            P("blk", None),
            P(("blk", "dom"), None),
            P(("blk", "dom"), None),
            P(("blk", "dom"), None),
            P(("blk", "dom"), None),
            P(("blk", "dom")),
        ),
        out_specs=P("blk", "dom"),
        check_vma=False,
    )
```

time: 166 us -> 165 us (level)
  Pallas kernels: 51 us -> 44.8 us
  waiting for transfers between devices: 30.3 us -> 34.2 us
  local copies, waits for them, and re-layouts: 28.8 us -> 31.1 us
    unnamed x57 -> x62, local copies, waits for them, and re-layouts: 24 us -> 28.1 us
    ppermute x34 -> x31, waiting for transfers between devices: 30.3 us -> 34.2 us  [send(): return lax.ppermute(value, AXES, pairs)]
    pallas_call x7, Pallas kernels: 26.7 us -> 23.8 us  [the longest x4 17.1 us: make_rows(): pl.pallas_call(rows_kernel, grid_spec=pltpu.PrefetchScalarGridSpec(num_sc...]
    pallas_call x2, Pallas kernels: 8.97 us -> 6.42 us  [make_accum(): pl.pallas_call(lambda *refs: accum_kernel(part, *refs), grid_spec=pltpu.P...]
    reshape x5 -> x0, local copies, waits for them, and re-layouts: 2.11 us -> none  [the longest x1 1.56 us: per_device(): geo = lax.dynamic_slice(jnp.asarray(geometry()).reshape(NB, G, 8, COLS),...]
    ppermute x34 -> x31, starting transfers between devices: 42.5 us -> 42.8 us  [send(): return lax.ppermute(value, AXES, pairs)]
  transfers between devices with their start and end apart: 34 -> 31, of which waited for: 12 -> 10; matrix products, arithmetic and copies ran while one was open for 4% -> 2% of each run, Pallas kernels for 21% -> 24%
where the time goes in v2:
time: 165 us; the launch traced here: 163 us
  Pallas kernels  44.8 us (27%)
  starting transfers between devices  42.8 us (26%)
  waiting for transfers between devices  34.2 us (21%)
  local copies, waits for them, and re-layouts  31.1 us (19%)
  between operations  8.42 us (5%)
  other arithmetic  1.96 us (1%)
    ppermute x31, starting transfers between devices, send(): return lax.ppermute(value, AXES, pairs)  42.8 us
    ppermute x31, waiting for transfers between devices, send(): return lax.ppermute(value, AXES, pairs)  34.2 us
    unnamed x62, local copies, waits for them, and re-layouts  28.1 us
    pallas_call x4, Pallas kernels, make_rows(): pl.pallas_call(rows_kernel, grid_spec=pltpu.PrefetchScalarGridSpec(num_sc...  17.1 us
    pallas_call x2, Pallas kernels, make_scores(): pl.pallas_call(lambda *refs: scores_kernel(count, *refs), grid=(NB,), in_...  12.6 us
    pallas_call x1, Pallas kernels, make_table(): pl.pallas_call(table_kernel, grid_spec=pltpu.PrefetchScalarGridSpec(num_s...  6.46 us
    pallas_call x2, Pallas kernels, make_accum(): pl.pallas_call(lambda *refs: accum_kernel(part, *refs), grid_spec=pltpu.P...  6.42 us
  transfers between devices with their start and end apart: 31, of which 10 were waited for; matrix products, arithmetic and copies ran while one was open for 2% of the time, Pallas kernels for 24%

profile of v2, /device:TPU:2, one launch (start us, length us, event | category | flops | bytes accessed | tf_op | source)
XLA Modules:
  0.0 163.3 jit_solution(14393125120923361552)
XLA Ops:
  8.1 3.0 %collective-permute-start.4 = (bf16[16,8192]{1,0:T(8,128)(2,1)S(1)}, bf16[16,8192]{1,0:T(8,128)(2,1)S(1)}, u32[]{:S(2)}, u32[]{:S(2)}) collective-permute-start(bf16[16,8192]{1,0:T(8,128)(2,1)S(1)} %own_references.1.after.refs_6_.refs_2_), channel_id=1, source_target_pairs={{0,192},{1,193},{2,194},{3,195},{4,196},{5,197},{6,198},{7,199},{8... | collective-permute-start | bytes 786440 | tf_op jit(solution)/shard_map/ppermute | solution.py:49
  12.7 9.9 %collective-permute-done.4.refs_8_.refs_4_ = bf16[16,8192]{1,0:T(8,128)(2,1)S(1)} collective-permute-done((bf16[16,8192]{1,0:T(8,128)(2,1)S(1)}, bf16[16,8192]{1,0:T(8,128)(2,1)S(1)}, u32[]{:S(2)}, u32[]{:S(2)}) %collective-permute-start.4) | collective-permute-done | bytes 262176 | tf_op jit(solution)/shard_map/ppermute | solution.py:49
  24.5 6.5 %phase_table.1.table_ref = bf16[256,8192]{1,0:T(8,128)(2,1)S(1)} custom-call(s32[1]{0:T(128)} %bitcast.member_ref, f32[16,8,1024]{2,1,0:T(8,128)S(1)} %copy-done.12, f32[128,8]{1,0:T(8,128)S(1)} %copy-done.19), custom_call_target="tpu_custom_call" | custom-call | flops 20971520 | bytes 4194304 | tf_op jit(solution)/shard_map/phase_table/pallas_call | solution.py:116
  31.6 2.8 %collective-permute-start.5 = (bf16[16,8192]{1,0:T(8,128)(2,1)S(1)}, bf16[16,8192]{1,0:T(8,128)(2,1)S(1)}, u32[]{:S(2)}, u32[]{:S(2)}) collective-permute-start(bf16[16,8192]{1,0:T(8,128)(2,1)S(1)} %collective-permute-done.4.refs_8_.refs_4_), channel_id=1, source_target_pairs={{0,48},{1,49},{2,50},{3,51},{4,52},{5,53},{6,54},{7,55},{8,56},{9,... | collective-permute-start | bytes 786440 | tf_op jit(solution)/shard_map/ppermute | solution.py:49
  35.1 4.3 %shifted_rows.4 = (bf16[256,8192]{1,0:T(8,128)(2,1)S(1)}, bf16[32,4096]{1,0:T(8,128)(2,1)S(1)}) custom-call(s32[1]{0:T(128)} %bitcast.member_ref, bf16[32,8576]{1,0:T(8,128)(2,1)S(1)} %get-tuple-element.28.x_ref.high_ref.middle_ref.low_ref, bf16[32,8576]{1,0:T(8,128)(2,1)S(1)} %get-tuple-element.28.x_ref.high_ref.middle_ref.low_ref, ...), custom_call_target="tpu_custom_call" | custom-call | flops 1073741824 | bytes 9437184 | tf_op jit(solution)/shard_map/shifted_rows/pallas_call | solution.py:229
  39.4 4.3 %shifted_rows.5 = (bf16[256,8192]{1,0:T(8,128)(2,1)S(1)}, bf16[32,4096]{1,0:T(8,128)(2,1)S(1)}) custom-call(s32[1]{0:T(128)} %bitcast.member_ref, bf16[32,8576]{1,0:T(8,128)(2,1)S(1)} %collective-permute-done.x_ref.high_ref.middle_ref.low_ref, bf16[32,8576]{1,0:T(8,128)(2,1)S(1)} %collective-permute-done.x_ref.high_ref.middle_ref.low_ref, ...), custom_call_target="tpu_custom_call" | custom-call | flops 1073741824 | bytes 9437184 | tf_op jit(solution)/shard_map/shifted_rows/pallas_call | solution.py:229
  43.7 4.3 %shifted_rows.6 = (bf16[256,8192]{1,0:T(8,128)(2,1)S(1)}, bf16[32,4096]{1,0:T(8,128)(2,1)S(1)}) custom-call(s32[1]{0:T(128)} %bitcast.member_ref, bf16[32,8576]{1,0:T(8,128)(2,1)S(1)} %collective-permute-done.1.x_ref.high_ref.middle_ref.low_ref, bf16[32,8576]{1,0:T(8,128)(2,1)S(1)} %collective-permute-done.1.x_ref.high_ref.middle_ref.low_ref, ...), custom_call_target="tpu_custom_call" | custom-call | flops 1073741824 | bytes 9437184 | tf_op jit(solution)/shard_map/shifted_rows/pallas_call | solution.py:229
  48.1 10.0 %partial_scores.2 = (f32[256,128]{1,0:T(8,128)S(1)}, f32[256,128]{1,0:T(8,128)S(1)}, f32[256,128]{1,0:T(8,128)S(1)}) custom-call(bf16[256,8192]{1,0:T(8,128)(2,1)S(1)} %get-tuple-element.29.refs_0_.refs_1_.refs_5_, bf16[256,8192]{1,0:T(8,128)(2,1)S(1)} %get-tuple-element.31.refs_1_.refs_2_.refs_6_, ...), custom_call_target="tpu_custom_call" | custom-call | flops 1610612736 | bytes 14680064 | tf_op jit(solution)/shard_map/partial_scores/pallas_call | solution.py:283
  59.9 4.3 %shifted_rows.7 = (bf16[256,8192]{1,0:T(8,128)(2,1)S(1)}, bf16[32,4096]{1,0:T(8,128)(2,1)S(1)}) custom-call(s32[1]{0:T(128)} %bitcast.member_ref, bf16[32,8576]{1,0:T(8,128)(2,1)S(1)} %collective-permute-done.2.x_ref.high_ref.middle_ref.low_ref, bf16[32,8576]{1,0:T(8,128)(2,1)S(1)} %collective-permute-done.2.x_ref.high_ref.middle_ref.low_ref, ...), custom_call_target="tpu_custom_call" | custom-call | flops 1073741824 | bytes 9437184 | tf_op jit(solution)/shard_map/shifted_rows/pallas_call | solution.py:229
  64.2 2.6 %partial_scores.3 = f32[256,128]{1,0:T(8,128)S(1)} custom-call(bf16[256,8192]{1,0:T(8,128)(2,1)S(1)} %get-tuple-element.35.refs_0_.refs_4_.refs_8_, bf16[32,4096]{1,0:T(8,128)(2,1)S(1)} %get-tuple-element.42.refs_1_, bf16[16,8192]{1,0:T(8,128)(2,1)S(1)} %own_references.1.after.refs_6_.refs_2_, bf16[16,8192]{1,0:T(8,128)(2,1)S(1)} %collective-permute-done.3.refs_7_.refs_3_, ...), custom_call_target="tpu_custom_call" | custom-call | flops 536870912 | bytes 6291456 | tf_op jit(solution)/shard_map/partial_scores/pallas_call | solution.py:283
  69.0 5.3 %collective-permute-done.12.refs_3_ = f32[256,128]{1,0:T(8,128)S(1)} collective-permute-done((f32[256,128]{1,0:T(8,128)S(1)}, f32[256,128]{1,0:T(8,128)S(1)}, u32[]{:S(2)}, u32[]{:S(2)}) %collective-permute-start.12) | collective-permute-done | bytes 131104 | tf_op jit(solution)/shard_map/ppermute | solution.py:49
  74.9 2.0 %posterior.1.refs_9_ = bf16[128,256]{1,0:T(8,128)(2,1)} custom-call(f32[256,128]{1,0:T(8,128)} %copy-done.18, f32[256,128]{1,0:T(8,128)} %copy-done.22, f32[256,128]{1,0:T(8,128)} %copy-done.23, f32[256,128]{1,0:T(8,128)} %copy-done.24), custom_call_target="tpu_custom_call" | custom-call | tf_op jit(solution)/shard_map/posterior/pallas_call | solution.py:313
  78.8 3.4 %collective-permute-done.14.refs_11_ = bf16[128,256]{1,0:T(8,128)(2,1)S(1)} collective-permute-done((bf16[128,256]{1,0:T(8,128)(2,1)}, bf16[128,256]{1,0:T(8,128)(2,1)S(1)}, u32[]{:S(2)}, u32[]{:S(2)}) %collective-permute-start.14) | collective-permute-done | bytes 65568 | tf_op jit(solution)/shard_map/ppermute | solution.py:49
  82.5 2.2 %copy-done.1 = bf16[256,8192]{1,0:T(8,128)(2,1)S(1)} copy-done((bf16[256,8192]{1,0:T(8,128)(2,1)S(1)}, bf16[256,8192]{1,0:T(8,128)(2,1)}, u32[]{:S(2)}) %copy-start.1) | copy-done | bytes 4194328
  84.7 2.2 %copy-done.4 = bf16[256,8192]{1,0:T(8,128)(2,1)S(1)} copy-done((bf16[256,8192]{1,0:T(8,128)(2,1)S(1)}, bf16[256,8192]{1,0:T(8,128)(2,1)}, u32[]{:S(2)}) %copy-start.4) | copy-done | bytes 4194328
  86.9 2.2 %copy-done.7 = bf16[256,8192]{1,0:T(8,128)(2,1)S(1)} copy-done((bf16[256,8192]{1,0:T(8,128)(2,1)S(1)}, bf16[256,8192]{1,0:T(8,128)(2,1)}, u32[]{:S(2)}) %copy-start.7) | copy-done | bytes 4194328
  89.1 2.2 %copy-done.10 = bf16[256,8192]{1,0:T(8,128)(2,1)S(1)} copy-done((bf16[256,8192]{1,0:T(8,128)(2,1)S(1)}, bf16[256,8192]{1,0:T(8,128)(2,1)}, u32[]{:S(2)}) %copy-start.10) | copy-done | bytes 4194328
  92.1 3.2 %weighted_sums.2 = (bf16[32,4096]{1,0:T(8,128)(2,1)S(1)}, bf16[32,4096]{1,0:T(8,128)(2,1)S(1)}, bf16[32,4096]{1,0:T(8,128)(2,1)S(1)}, bf16[32,4096]{1,0:T(8,128)(2,1)S(1)}) custom-call(s32[4]{0:T(128)S(1)} %and_select_fusion.refs_0_, bf16[256,8192]{1,0:T(8,128)(2,1)S(1)} %copy-done.4, bf16[256,8192]{1,0:T(8,128)(2,1)S(1)} %copy-done.7, ...), custom_call_target="tpu_custom_call" | custom-call | flops 1073741824 | bytes 9437184 | tf_op jit(solution)/shard_map/weighted_sums/pallas_call | solution.py:344
  95.3 3.8 %collective-permute-start.18 = (bf16[32,4096]{1,0:T(8,128)(2,1)S(1)}, bf16[32,4096]{1,0:T(8,128)(2,1)S(1)}, u32[]{:S(2)}, u32[]{:S(2)}) collective-permute-start(bf16[32,4096]{1,0:T(8,128)(2,1)S(1)} %get-tuple-element.46), channel_id=1, source_target_pairs={{0,192},{1,193},{2,194},{3,195},{4,196},{5,197},{6,198},{7,199},{8... | collective-permute-start | bytes 786440 | tf_op jit(solution)/shard_map/ppermute | solution.py:49
  108.6 2.2 %copy-done.2 = bf16[256,8192]{1,0:T(8,128)(2,1)S(1)} copy-done((bf16[256,8192]{1,0:T(8,128)(2,1)S(1)}, bf16[256,8192]{1,0:T(8,128)(2,1)}, u32[]{:S(2)}) %copy-start.2) | copy-done | bytes 4194328
  110.8 2.2 %copy-done.5 = bf16[256,8192]{1,0:T(8,128)(2,1)S(1)} copy-done((bf16[256,8192]{1,0:T(8,128)(2,1)S(1)}, bf16[256,8192]{1,0:T(8,128)(2,1)}, u32[]{:S(2)}) %copy-start.5) | copy-done | bytes 4194328
  113.0 2.2 %copy-done.8 = bf16[256,8192]{1,0:T(8,128)(2,1)S(1)} copy-done((bf16[256,8192]{1,0:T(8,128)(2,1)S(1)}, bf16[256,8192]{1,0:T(8,128)(2,1)}, u32[]{:S(2)}) %copy-start.8) | copy-done | bytes 4194328
  115.2 2.2 %copy-done.11 = bf16[256,8192]{1,0:T(8,128)(2,1)S(1)} copy-done((bf16[256,8192]{1,0:T(8,128)(2,1)S(1)}, bf16[256,8192]{1,0:T(8,128)(2,1)}, u32[]{:S(2)}) %copy-start.11) | copy-done | bytes 4194328
  117.4 3.2 %weighted_sums.3 = (bf16[64,2048]{1,0:T(8,128)(2,1)S(1)}, bf16[64,2048]{1,0:T(8,128)(2,1)S(1)}, bf16[64,2048]{1,0:T(8,128)(2,1)S(1)}, bf16[64,2048]{1,0:T(8,128)(2,1)S(1)}) custom-call(s32[4]{0:T(128)S(1)} %and_select_fusion.refs_0_, bf16[256,8192]{1,0:T(8,128)(2,1)S(1)} %copy-done.5, bf16[256,8192]{1,0:T(8,128)(2,1)S(1)} %copy-done.8, ...), custom_call_target="tpu_custom_call" | custom-call | flops 1073741824 | bytes 9437184 | tf_op jit(solution)/shard_map/weighted_sums/pallas_call | solution.py:344
  120.6 2.1 %collective-permute-start.24 = (bf16[64,2048]{1,0:T(8,128)(2,1)S(1)}, bf16[64,2048]{1,0:T(8,128)(2,1)S(1)}, u32[]{:S(2)}, u32[]{:S(2)}) collective-permute-start(bf16[64,2048]{1,0:T(8,128)(2,1)S(1)} %get-tuple-element.50), channel_id=1, source_target_pairs={{0,48},{1,49},{2,50},{3,51},{4,52},{5,53},{6,54},{7,55},{8,56},{9,... | collective-permute-start | bytes 786440 | tf_op jit(solution)/shard_map/ppermute | solution.py:49
  132.2 5.1 %collective-permute-done.23 = bf16[64,2048]{1,0:T(8,128)(2,1)S(1)} collective-permute-done((bf16[64,2048]{1,0:T(8,128)(2,1)S(1)}, bf16[64,2048]{1,0:T(8,128)(2,1)S(1)}, u32[]{:S(2)}, u32[]{:S(2)}) %collective-permute-start.23) | collective-permute-done | bytes 262176 | tf_op jit(solution)/shard_map/ppermute | solution.py:49
  138.6 2.4 %collective-permute-start.27 = (bf16[16,2048]{1,0:T(8,128)(2,1)S(1)}, bf16[16,2048]{1,0:T(8,128)(2,1)S(1)}, u32[]{:S(2)}, u32[]{:S(2)}) collective-permute-start(bf16[16,2048]{1,0:T(8,128)(2,1)S(1)} %get-tuple-element.57), channel_id=1, source_target_pairs={{0,192},{1,193},{2,194},{3,195},{4,196},{5,197},{6,198},{7,199},{8... | collective-permute-start | bytes 196616 | tf_op jit(solution)/shard_map/ppermute | solution.py:49
  140.9 2.0 %collective-permute-start.26 = (bf16[16,2048]{1,0:T(8,128)(2,1)S(1)}, bf16[16,2048]{1,0:T(8,128)(2,1)S(1)}, u32[]{:S(2)}, u32[]{:S(2)}) collective-permute-start(bf16[16,2048]{1,0:T(8,128)(2,1)S(1)} %get-tuple-element.58), channel_id=1, source_target_pairs={{0,128},{1,129},{2,130},{3,131},{4,132},{5,133},{6,134},{7,135},{8... | collective-permute-start | bytes 196616 | tf_op jit(solution)/shard_map/ppermute | solution.py:49
  143.2 3.5 %collective-permute-done.26 = bf16[16,2048]{1,0:T(8,128)(2,1)S(1)} collective-permute-done((bf16[16,2048]{1,0:T(8,128)(2,1)S(1)}, bf16[16,2048]{1,0:T(8,128)(2,1)S(1)}, u32[]{:S(2)}, u32[]{:S(2)}) %collective-permute-start.26) | collective-permute-done | bytes 65568 | tf_op jit(solution)/shard_map/ppermute | solution.py:49
  148.8 5.5 %collective-permute-start.30 = (bf16[16,1024]{1,0:T(8,128)(2,1)S(1)}, bf16[16,1024]{1,0:T(8,128)(2,1)S(1)}, u32[]{:S(2)}, u32[]{:S(2)}) collective-permute-start(bf16[16,1024]{1,0:T(8,128)(2,1)S(1)} %bitcast.43), channel_id=1, source_target_pairs={{0,12},{1,13},{2,14},{3,15},{4,0},{5,1},{6,2},{7,3},{8,4},{9,5},{1... | collective-permute-start | bytes 98312 | tf_op jit(solution)/shard_map/ppermute | solution.py:49
  155.8 2.5 %collective-permute-start.28 = (bf16[16,1024]{1,0:T(8,128)(2,1)S(1)}, bf16[16,1024]{1,0:T(8,128)(2,1)S(1)}, u32[]{:S(2)}, u32[]{:S(2)}) collective-permute-start(bf16[16,1024]{1,0:T(8,128)(2,1)S(1)} %bitcast.45), channel_id=1, source_target_pairs={{0,4},{1,5},{2,6},{3,7},{4,8},{5,9},{6,10},{7,11},{8,12},{9,13},{1... | collective-permute-start | bytes 98312 | tf_op jit(solution)/shard_map/ppermute | solution.py:49
  158.4 4.0 %collective-permute-done.29 = bf16[16,1024]{1,0:T(8,128)(2,1)S(1)} collective-permute-done((bf16[16,1024]{1,0:T(8,128)(2,1)S(1)}, bf16[16,1024]{1,0:T(8,128)(2,1)S(1)}, u32[]{:S(2)}, u32[]{:S(2)}) %collective-permute-start.29) | collective-permute-done | bytes 32800 | tf_op jit(solution)/shard_map/ppermute | solution.py:49
  (125 shorter events, 37.5 us)
Async XLA Ops:
  2.7 32.4 %copy-start.13 = (f32[16,8,1024]{2,1,0:T(8,128)S(1)}, f32[16,8,1024]{2,1,0:T(8,128)}, u32[]{:S(2)}) copy-start(f32[16,8,1024]{2,1,0:T(8,128)} %constant.121.clone.geo_ref) | copy-start | bytes 1572868
  6.0 28.4 %collective-permute-start = (bf16[32,8576]{1,0:T(8,128)(2,1)S(1)}, bf16[32,8576]{1,0:T(8,128)(2,1)S(1)}, u32[]{:S(2)}, u32[]{:S(2)}) collective-permute-start(bf16[32,8576]{1,0:T(8,128)(2,1)S(1)} %get-tuple-element.30), channel_id=1, source_target_pairs={{0,1},{1,0},{2,3},{3,2},{4,5},{5,4},{6,7},{7,6},{8,9},{9,8},{10,11... | collective-permute-start | bytes 1646600 | tf_op jit(solution)/shard_map/ppermute | solution.py:49
  6.1 28.3 %collective-permute-start.1 = (bf16[32,8576]{1,0:T(8,128)(2,1)S(1)}, bf16[32,8576]{1,0:T(8,128)(2,1)S(1)}, u32[]{:S(2)}, u32[]{:S(2)}) collective-permute-start(bf16[32,8576]{1,0:T(8,128)(2,1)S(1)} %get-tuple-element.32), channel_id=1, source_target_pairs={{0,2},{1,3},{2,0},{3,1},{4,6},{5,7},{6,4},{7,5},{8,10},{9,11},{10,... | collective-permute-start | bytes 1646600 | tf_op jit(solution)/shard_map/ppermute | solution.py:49
  8.1 14.5 %collective-permute-start.4 = (bf16[16,8192]{1,0:T(8,128)(2,1)S(1)}, bf16[16,8192]{1,0:T(8,128)(2,1)S(1)}, u32[]{:S(2)}, u32[]{:S(2)}) collective-permute-start(bf16[16,8192]{1,0:T(8,128)(2,1)S(1)} %own_references.1.after.refs_6_.refs_2_), channel_id=1, source_target_pairs={{0,192},{1,193},{2,194},{3,195},{4,196},{5,197},{6,198},{7,199},{8... | collective-permute-start | bytes 786440 | tf_op jit(solution)/shard_map/ppermute | solution.py:49
  11.1 19.9 %collective-permute-start.6 = (bf16[16,8192]{1,0:T(8,128)(2,1)S(1)}, bf16[16,8192]{1,0:T(8,128)(2,1)S(1)}, u32[]{:S(2)}, u32[]{:S(2)}) collective-permute-start(bf16[16,8192]{1,0:T(8,128)(2,1)S(1)} %own_references.1.after.refs_6_.refs_2_), channel_id=1, source_target_pairs={{0,128},{1,129},{2,130},{3,131},{4,132},{5,133},{6,134},{7,135},{8... | collective-permute-start | bytes 786440 | tf_op jit(solution)/shard_map/ppermute | solution.py:49
  11.7 19.8 %collective-permute-start.8 = (bf16[16,8192]{1,0:T(8,128)(2,1)S(1)}, bf16[16,8192]{1,0:T(8,128)(2,1)S(1)}, u32[]{:S(2)}, u32[]{:S(2)}) collective-permute-start(bf16[16,8192]{1,0:T(8,128)(2,1)S(1)} %own_references.1.after.refs_6_.refs_2_), channel_id=1, source_target_pairs={{0,64},{1,65},{2,66},{3,67},{4,68},{5,69},{6,70},{7,71},{8,72},{9,... | collective-permute-start | bytes 786440 | tf_op jit(solution)/shard_map/ppermute | solution.py:49
  22.6 37.3 %collective-permute-start.2 = (bf16[32,8576]{1,0:T(8,128)(2,1)S(1)}, bf16[32,8576]{1,0:T(8,128)(2,1)S(1)}, u32[]{:S(2)}, u32[]{:S(2)}) collective-permute-start(bf16[32,8576]{1,0:T(8,128)(2,1)S(1)} %get-tuple-element.34), channel_id=1, source_target_pairs={{0,3},{1,2},{2,1},{3,0},{4,7},{5,6},{6,5},{7,4},{8,11},{9,10},{10,... | collective-permute-start | bytes 1646600 | tf_op jit(solution)/shard_map/ppermute | solution.py:49
  31.0 17.1 %collective-permute-start.3 = (bf16[16,8192]{1,0:T(8,128)(2,1)S(1)}, bf16[16,8192]{1,0:T(8,128)(2,1)S(1)}, u32[]{:S(2)}, u32[]{:S(2)}) collective-permute-start(bf16[16,8192]{1,0:T(8,128)(2,1)S(1)} %own_references.1.after.refs_6_.refs_2_), channel_id=1, source_target_pairs={{0,48},{1,49},{2,50},{3,51},{4,52},{5,53},{6,54},{7,55},{8,56},{9,... | collective-permute-start | bytes 786440 | tf_op jit(solution)/shard_map/ppermute | solution.py:49
  31.6 16.5 %collective-permute-start.5 = (bf16[16,8192]{1,0:T(8,128)(2,1)S(1)}, bf16[16,8192]{1,0:T(8,128)(2,1)S(1)}, u32[]{:S(2)}, u32[]{:S(2)}) collective-permute-start(bf16[16,8192]{1,0:T(8,128)(2,1)S(1)} %collective-permute-done.4.refs_8_.refs_4_), channel_id=1, source_target_pairs={{0,48},{1,49},{2,50},{3,51},{4,52},{5,53},{6,54},{7,55},{8,56},{9,... | collective-permute-start | bytes 786440 | tf_op jit(solution)/shard_map/ppermute | solution.py:49
  34.4 13.7 %collective-permute-start.7 = (bf16[16,8192]{1,0:T(8,128)(2,1)S(1)}, bf16[16,8192]{1,0:T(8,128)(2,1)S(1)}, u32[]{:S(2)}, u32[]{:S(2)}) collective-permute-start(bf16[16,8192]{1,0:T(8,128)(2,1)S(1)} %collective-permute-done.6.refs_10_.refs_6_), channel_id=1, source_target_pairs={{0,32},{1,33},{2,34},{3,35},{4,36},{5,37},{6,38},{7,39},{8,40},{9,... | collective-permute-start | bytes 786440 | tf_op jit(solution)/shard_map/ppermute | solution.py:49
  34.4 13.7 %collective-permute-start.9 = (bf16[16,8192]{1,0:T(8,128)(2,1)S(1)}, bf16[16,8192]{1,0:T(8,128)(2,1)S(1)}, u32[]{:S(2)}, u32[]{:S(2)}) collective-permute-start(bf16[16,8192]{1,0:T(8,128)(2,1)S(1)} %collective-permute-done.8.refs_12_.refs_8_), channel_id=1, source_target_pairs={{0,32},{1,33},{2,34},{3,35},{4,36},{5,37},{6,38},{7,39},{8,40},{9,... | collective-permute-start | bytes 786440 | tf_op jit(solution)/shard_map/ppermute | solution.py:49
  58.1 10.8 %collective-permute-start.10 = (f32[256,128]{1,0:T(8,128)S(1)}, f32[256,128]{1,0:T(8,128)S(1)}, u32[]{:S(2)}, u32[]{:S(2)}) collective-permute-start(f32[256,128]{1,0:T(8,128)S(1)} %get-tuple-element.40), channel_id=1, source_target_pairs={{0,1},{1,0},{2,3},{3,2},{4,5},{5,4},{6,7},{7,6},{8,9},{9,8},{10,11... | collective-permute-start | bytes 393224 | tf_op jit(solution)/shard_map/ppermute | solution.py:49
  58.2 10.8 %collective-permute-start.11 = (f32[256,128]{1,0:T(8,128)S(1)}, f32[256,128]{1,0:T(8,128)S(1)}, u32[]{:S(2)}, u32[]{:S(2)}) collective-permute-start(f32[256,128]{1,0:T(8,128)S(1)} %get-tuple-element.41), channel_id=1, source_target_pairs={{0,2},{1,3},{2,0},{3,1},{4,6},{5,7},{6,4},{7,5},{8,10},{9,11},{10,... | collective-permute-start | bytes 393224 | tf_op jit(solution)/shard_map/ppermute | solution.py:49
  68.8 5.5 %collective-permute-start.12 = (f32[256,128]{1,0:T(8,128)S(1)}, f32[256,128]{1,0:T(8,128)S(1)}, u32[]{:S(2)}, u32[]{:S(2)}) collective-permute-start(f32[256,128]{1,0:T(8,128)S(1)} %partial_scores.3), channel_id=1, source_target_pairs={{0,3},{1,2},{2,1},{3,0},{4,7},{5,6},{6,5},{7,4},{8,11},{9,10},{10,... | collective-permute-start | bytes 393224 | tf_op jit(solution)/shard_map/ppermute | solution.py:49
  76.9 1.9 %collective-permute-start.13 = (bf16[128,256]{1,0:T(8,128)(2,1)}, bf16[128,256]{1,0:T(8,128)(2,1)S(1)}, u32[]{:S(2)}, u32[]{:S(2)}) collective-permute-start(bf16[128,256]{1,0:T(8,128)(2,1)} %posterior.1.refs_9_), channel_id=1, source_target_pairs={{0,1},{1,0},{2,3},{3,2},{4,5},{5,4},{6,7},{7,6},{8,9},{9,8},{10,11... | collective-permute-start | bytes 196616 | tf_op jit(solution)/shard_map/ppermute | solution.py:49
  77.1 5.1 %collective-permute-start.14 = (bf16[128,256]{1,0:T(8,128)(2,1)}, bf16[128,256]{1,0:T(8,128)(2,1)S(1)}, u32[]{:S(2)}, u32[]{:S(2)}) collective-permute-start(bf16[128,256]{1,0:T(8,128)(2,1)} %posterior.1.refs_9_), channel_id=1, source_target_pairs={{0,2},{1,3},{2,0},{3,1},{4,6},{5,7},{6,4},{7,5},{8,10},{9,11},{10,... | collective-permute-start | bytes 196616 | tf_op jit(solution)/shard_map/ppermute | solution.py:49
  77.5 5.0 %collective-permute-start.15 = (bf16[128,256]{1,0:T(8,128)(2,1)}, bf16[128,256]{1,0:T(8,128)(2,1)S(1)}, u32[]{:S(2)}, u32[]{:S(2)}) collective-permute-start(bf16[128,256]{1,0:T(8,128)(2,1)} %posterior.1.refs_9_), channel_id=1, source_target_pairs={{0,3},{1,2},{2,1},{3,0},{4,7},{5,6},{6,5},{7,4},{8,11},{9,10},{10,... | collective-permute-start | bytes 196616 | tf_op jit(solution)/shard_map/ppermute | solution.py:49
  95.3 29.1 %collective-permute-start.18 = (bf16[32,4096]{1,0:T(8,128)(2,1)S(1)}, bf16[32,4096]{1,0:T(8,128)(2,1)S(1)}, u32[]{:S(2)}, u32[]{:S(2)}) collective-permute-start(bf16[32,4096]{1,0:T(8,128)(2,1)S(1)} %get-tuple-element.46), channel_id=1, source_target_pairs={{0,192},{1,193},{2,194},{3,195},{4,196},{5,197},{6,198},{7,199},{8... | collective-permute-start | bytes 786440 | tf_op jit(solution)/shard_map/ppermute | solution.py:49
  99.1 27.2 %collective-permute-start.17 = (bf16[32,4096]{1,0:T(8,128)(2,1)S(1)}, bf16[32,4096]{1,0:T(8,128)(2,1)S(1)}, u32[]{:S(2)}, u32[]{:S(2)}) collective-permute-start(bf16[32,4096]{1,0:T(8,128)(2,1)S(1)} %get-tuple-element.45), channel_id=1, source_target_pairs={{0,128},{1,129},{2,130},{3,131},{4,132},{5,133},{6,134},{7,135},{8... | collective-permute-start | bytes 786440 | tf_op jit(solution)/shard_map/ppermute | solution.py:49
  99.1 27.2 %collective-permute-start.16 = (bf16[32,4096]{1,0:T(8,128)(2,1)S(1)}, bf16[32,4096]{1,0:T(8,128)(2,1)}, u32[]{:S(2)}, u32[]{:S(2)}) collective-permute-start(bf16[32,4096]{1,0:T(8,128)(2,1)S(1)} %get-tuple-element.44), channel_id=1, source_target_pairs={{0,64},{1,65},{2,66},{3,67},{4,68},{5,69},{6,70},{7,71},{8,72},{9,... | collective-permute-start | bytes 786440 | tf_op jit(solution)/shard_map/ppermute | solution.py:49
  120.6 9.9 %collective-permute-start.24 = (bf16[64,2048]{1,0:T(8,128)(2,1)S(1)}, bf16[64,2048]{1,0:T(8,128)(2,1)S(1)}, u32[]{:S(2)}, u32[]{:S(2)}) collective-permute-start(bf16[64,2048]{1,0:T(8,128)(2,1)S(1)} %get-tuple-element.50), channel_id=1, source_target_pairs={{0,48},{1,49},{2,50},{3,51},{4,52},{5,53},{6,54},{7,55},{8,56},{9,... | collective-permute-start | bytes 786440 | tf_op jit(solution)/shard_map/ppermute | solution.py:49
  122.7 14.5 %collective-permute-start.23 = (bf16[64,2048]{1,0:T(8,128)(2,1)S(1)}, bf16[64,2048]{1,0:T(8,128)(2,1)S(1)}, u32[]{:S(2)}, u32[]{:S(2)}) collective-permute-start(bf16[64,2048]{1,0:T(8,128)(2,1)S(1)} %get-tuple-element.49), channel_id=1, source_target_pairs={{0,16},{1,17},{2,18},{3,19},{4,20},{5,21},{6,22},{7,23},{8,24},{9,... | collective-permute-start | bytes 786440 | tf_op jit(solution)/shard_map/ppermute | solution.py:49
  124.4 13.6 %collective-permute-start.22 = (bf16[64,2048]{1,0:T(8,128)(2,1)S(1)}, bf16[64,2048]{1,0:T(8,128)(2,1)S(1)}, u32[]{:S(2)}, u32[]{:S(2)}) collective-permute-start(bf16[64,2048]{1,0:T(8,128)(2,1)S(1)} %get-tuple-element.48), channel_id=1, source_target_pairs={{0,32},{1,33},{2,34},{3,35},{4,36},{5,37},{6,38},{7,39},{8,40},{9,... | collective-permute-start | bytes 786440 | tf_op jit(solution)/shard_map/ppermute | solution.py:49
  127.8 15.2 %collective-permute-start.21 = (bf16[16,2048]{1,0:T(8,128)(2,1)S(1)}, bf16[16,2048]{1,0:T(8,128)(2,1)S(1)}, u32[]{:S(2)}, u32[]{:S(2)}) collective-permute-start(bf16[16,2048]{1,0:T(8,128)(2,1)S(1)} %bitcast.40), channel_id=1, source_target_pairs={{0,48},{1,49},{2,50},{3,51},{4,52},{5,53},{6,54},{7,55},{8,56},{9,... | collective-permute-start | bytes 196616 | tf_op jit(solution)/shard_map/ppermute | solution.py:49
  128.5 14.5 %collective-permute-start.20 = (bf16[16,2048]{1,0:T(8,128)(2,1)S(1)}, bf16[16,2048]{1,0:T(8,128)(2,1)S(1)}, u32[]{:S(2)}, u32[]{:S(2)}) collective-permute-start(bf16[16,2048]{1,0:T(8,128)(2,1)S(1)} %bitcast.41), channel_id=1, source_target_pairs={{0,16},{1,17},{2,18},{3,19},{4,20},{5,21},{6,22},{7,23},{8,24},{9,... | collective-permute-start | bytes 196616 | tf_op jit(solution)/shard_map/ppermute | solution.py:49
  130.6 12.4 %collective-permute-start.19 = (bf16[16,2048]{1,0:T(8,128)(2,1)S(1)}, bf16[16,2048]{1,0:T(8,128)(2,1)S(1)}, u32[]{:S(2)}, u32[]{:S(2)}) collective-permute-start(bf16[16,2048]{1,0:T(8,128)(2,1)S(1)} %bitcast.42), channel_id=1, source_target_pairs={{0,32},{1,33},{2,34},{3,35},{4,36},{5,37},{6,38},{7,39},{8,40},{9,... | collective-permute-start | bytes 196616 | tf_op jit(solution)/shard_map/ppermute | solution.py:49
  138.6 4.6 %collective-permute-start.27 = (bf16[16,2048]{1,0:T(8,128)(2,1)S(1)}, bf16[16,2048]{1,0:T(8,128)(2,1)S(1)}, u32[]{:S(2)}, u32[]{:S(2)}) collective-permute-start(bf16[16,2048]{1,0:T(8,128)(2,1)S(1)} %get-tuple-element.57), channel_id=1, source_target_pairs={{0,192},{1,193},{2,194},{3,195},{4,196},{5,197},{6,198},{7,199},{8... | collective-permute-start | bytes 196616 | tf_op jit(solution)/shard_map/ppermute | solution.py:49
  140.9 5.8 %collective-permute-start.26 = (bf16[16,2048]{1,0:T(8,128)(2,1)S(1)}, bf16[16,2048]{1,0:T(8,128)(2,1)S(1)}, u32[]{:S(2)}, u32[]{:S(2)}) collective-permute-start(bf16[16,2048]{1,0:T(8,128)(2,1)S(1)} %get-tuple-element.58), channel_id=1, source_target_pairs={{0,128},{1,129},{2,130},{3,131},{4,132},{5,133},{6,134},{7,135},{8... | collective-permute-start | bytes 196616 | tf_op jit(solution)/shard_map/ppermute | solution.py:49
  143.0 5.5 %collective-permute-start.25 = (bf16[16,2048]{1,0:T(8,128)(2,1)S(1)}, bf16[16,2048]{1,0:T(8,128)(2,1)S(1)}, u32[]{:S(2)}, u32[]{:S(2)}) collective-permute-start(bf16[16,2048]{1,0:T(8,128)(2,1)S(1)} %get-tuple-element.56), channel_id=1, source_target_pairs={{0,64},{1,65},{2,66},{3,67},{4,68},{5,69},{6,70},{7,71},{8,72},{9,... | collective-permute-start | bytes 196616 | tf_op jit(solution)/shard_map/ppermute | solution.py:49
  148.8 9.6 %collective-permute-start.30 = (bf16[16,1024]{1,0:T(8,128)(2,1)S(1)}, bf16[16,1024]{1,0:T(8,128)(2,1)S(1)}, u32[]{:S(2)}, u32[]{:S(2)}) collective-permute-start(bf16[16,1024]{1,0:T(8,128)(2,1)S(1)} %bitcast.43), channel_id=1, source_target_pairs={{0,12},{1,13},{2,14},{3,15},{4,0},{5,1},{6,2},{7,3},{8,4},{9,5},{1... | collective-permute-start | bytes 98312 | tf_op jit(solution)/shard_map/ppermute | solution.py:49
  154.4 8.0 %collective-permute-start.29 = (bf16[16,1024]{1,0:T(8,128)(2,1)S(1)}, bf16[16,1024]{1,0:T(8,128)(2,1)S(1)}, u32[]{:S(2)}, u32[]{:S(2)}) collective-permute-start(bf16[16,1024]{1,0:T(8,128)(2,1)S(1)} %bitcast.44), channel_id=1, source_target_pairs={{0,8},{1,9},{2,10},{3,11},{4,12},{5,13},{6,14},{7,15},{8,0},{9,1},... | collective-permute-start | bytes 98312 | tf_op jit(solution)/shard_map/ppermute | solution.py:49
  155.8 6.8 %collective-permute-start.28 = (bf16[16,1024]{1,0:T(8,128)(2,1)S(1)}, bf16[16,1024]{1,0:T(8,128)(2,1)S(1)}, u32[]{:S(2)}, u32[]{:S(2)}) collective-permute-start(bf16[16,1024]{1,0:T(8,128)(2,1)S(1)} %bitcast.45), channel_id=1, source_target_pairs={{0,4},{1,5},{2,6},{3,7},{4,8},{5,9},{6,10},{7,11},{8,12},{9,13},{1... | collective-permute-start | bytes 98312 | tf_op jit(solution)/shard_map/ppermute | solution.py:49
  (24 other events, 96.1 us)

commit v3 on v2

v3 whole, which is shorter than its diff:
```python
import math

import jax
import jax.numpy as jnp
import numpy as np
from jax import lax
from jax.experimental import pallas as pl
from jax.experimental.pallas import tpu as pltpu
from jax.sharding import PartitionSpec as P

BOX = 32
TILTS = 32
SHIFTS = 8
P_DEV = 32
Y, X, Z = 4, 4, 8
COLS = 1024
HALF = 512
G = 4
NB = 16 // G
ROWS = P_DEV * SHIFTS
WIDTH = NB * 2 * COLS
EXTRA = 384
AXES = ("blk", "dom")
F32, BF16 = jnp.float32, jnp.bfloat16
NT = (((1,), (1,)), ((), ()))
MIB = 1 << 20


def linear(y, x, z, core):
    y, x, z = y % Y, x % X, z % Z
    return (y * 2 + x % 2) * 32 + (x // 2) * 16 + z * 2 + core


def moves(dy=0, dx=0, dz=0):
    return [
        (linear(y, x, z, c), linear(y + dy, x + dx, z + dz, c))
        for y in range(Y) for x in range(X) for z in range(Z) for c in range(2)
    ]


def partners(k):
    return [
        (linear(y, x, z, c), linear(y, x, z ^ (k >> 1), c ^ (k & 1)))
        for y in range(Y) for x in range(X) for z in range(Z) for c in range(2)
    ]


def send(value, pairs):
    return lax.ppermute(value, AXES, pairs)


def geometry():
    position = np.arange(TILTS * HALF)
    tilt, within = position // HALF, position % HALF
    radial = (within // BOX).astype(np.float64)
    lateral = (within % BOX - BOX // 2).astype(np.float64)
    angle = (tilt - 0.5 * (TILTS - 1)) * (2.0 / TILTS)
    shell = (radial * radial + lateral * lateral) / (0.25 * BOX * BOX)
    zero = np.zeros_like(shell)
    table = np.stack([radial * np.cos(angle), lateral, radial * np.sin(angle), shell] + [zero] * 4)
    return table.reshape(8, 16, COLS).transpose(1, 0, 2).astype(np.float32)


def translations():
    ids = np.arange(128)
    out = np.zeros((128, 8), np.float32)
    for column, digit in enumerate((ids // 25, ids // 5 % 5, ids % 5)):
        out[:, column] = (digit - 2) * 0.5 / BOX
    out[125:] = 0
    return out


def fold(turns):
    turns = turns - jnp.floor(turns + 0.5)
    far = jnp.abs(turns) > 0.25
    near = jnp.where(far, jnp.where(turns > 0, 0.5, -0.5) - turns, turns)
    return near * (2.0 * math.pi), far


def series(square, terms):
    total = jnp.full_like(square, terms[-1])
    for term in terms[-2::-1]:
        total = total * square + term
    return total


SIN_TERMS = [(-1) ** n / math.factorial(2 * n + 1) for n in range(6)]
COS_TERMS = [(-1) ** n / math.factorial(2 * n) for n in range(7)]


def sine_turns(turns):
    angle, _ = fold(turns)
    return angle * series(angle * angle, SIN_TERMS)


def held(value):
    return pltpu.with_memory_space_constraint(value, pltpu.VMEM)


SCALARS = pl.BlockSpec(memory_space=pltpu.SMEM)
WHOLE = pl.BlockSpec(memory_space=pltpu.VMEM)
PLACED = pl.BlockSpec(memory_space=pl.ANY)


def local(kernel, name, outs, scalars, arrays, limit, flops=0, size=0, placed=0, scratch=()):
    return pl.pallas_call(
        kernel,
        in_specs=[SCALARS] * len(scalars) + [PLACED] * placed + [WHOLE] * (len(arrays) - placed),
        out_specs=[WHOLE] * len(outs),
        out_shape=[pltpu.VMEM(shape, kind) for shape, kind in outs],
        scratch_shapes=list(scratch),
        cost_estimate=pl.CostEstimate(flops=flops, bytes_accessed=size, transcendentals=0),
        compiler_params=pltpu.CompilerParams(vmem_limit_bytes=limit * MIB),
        name=name,
    )(*scalars, *arrays[:placed], *[held(value) for value in arrays[placed:]])


def table_kernel(member_ref, geo_ref, shift_ref, out_ref):
    shift = shift_ref[...]

    @pl.loop(0, NB)
    def _(block):
        geo = geo_ref[block * G + member_ref[0]]
        for tilt in range(2):
            part = geo[:, tilt * HALF : (tilt + 1) * HALF]
            turns = shift[:, 0:1] * part[0:1] + shift[:, 1:2] * part[1:2] + shift[:, 2:3] * part[2:3]
            angle, far = fold(turns)
            square = angle * angle
            sine = angle * series(square, SIN_TERMS)
            cosine = series(square, COS_TERMS)
            cosine = jnp.where(far, -cosine, cosine)
            for at, values in enumerate((cosine, sine)):
                high = values.astype(BF16)
                low = (values - high.astype(F32)).astype(BF16)
                spot = pl.multiple_of(block * 2 * COLS + tilt * COLS + at * HALF, HALF)
                out_ref[0:128, pl.ds(spot, HALF)] = high
                out_ref[128:256, pl.ds(spot, HALF)] = low


def make_table(member, geo):
    (table,) = local(
        table_kernel, "phase_table", [((256, WIDTH), BF16)], [member],
        [geo, jnp.asarray(translations())], 8, flops=NB * 128 * COLS * 40, size=5 * MIB,
    )
    return table


def column(part, block, who):
    return pl.ds(pl.multiple_of((part * 16 + block * G + who) * COLS, COLS), COLS)


def pieces_of(source, out, who, sems, base):
    return [
        pltpu.make_async_copy(
            source.at[:, column(part, block, who)],
            out.at[:, pl.ds((block * 2 + part) * COLS, COLS)],
            sems.at[base + block * 2 + part],
        )
        for block in range(NB) for part in range(2)
    ]


def own_kernel(member_ref, source, out, sems):
    copies = pieces_of(source, out, member_ref[0], sems, 0)
    for copy in copies:
        copy.start()
    for copy in copies:
        copy.wait()


def own_columns(member, refs):
    (own,) = local(
        own_kernel, "own_references", [((16, WIDTH), BF16)], [member], [refs], 4, size=MIB // 2,
        placed=1, scratch=[pltpu.SemaphoreType.DMA((2 * NB,))],
    )
    return own


def split_kernel(member_ref, source, after, ids, wedge, focus, sigma, *refs):
    outs, sems = refs[:-1], refs[-1]
    copies = []
    for n in (2, 1, 3, 0):
        copies += pieces_of(source, outs[n], member_ref[0] ^ n, sems, n * 2 * NB)
    for copy in copies:
        copy.start()
    info = jnp.concatenate(
        [
            ids[...].astype(F32),
            wedge[...].astype(F32),
            focus[...],
            sigma[...],
            jnp.zeros((P_DEV, 128 - SHIFTS - 2 * TILTS - 1), F32),
        ],
        axis=1,
    )
    high = info.astype(BF16)
    rest = info - high.astype(F32)
    middle = rest.astype(BF16)
    low = (rest - middle.astype(F32)).astype(BF16)
    for out in outs:
        for spot, piece in enumerate((high, middle, low)):
            out[:, WIDTH + spot * 128 : WIDTH + (spot + 1) * 128] = piece
    for copy in copies:
        copy.wait()


def split_particles(member, after, particles, shift_ids, wedge, defocus, inv_sigma):
    return local(
        split_kernel, "split_particles", [((P_DEV, WIDTH + EXTRA), BF16)] * G, [member],
        [particles, after, shift_ids, wedge, defocus, inv_sigma[:, None]], 4, size=4 * MIB,
        placed=2, scratch=[pltpu.SemaphoreType.DMA((G * 2 * NB,))],
    )


def rows_kernel(member_ref, x_ref, geo_ref, table_ref, rows_ref, pen_ref):
    info = sum(x_ref[:, WIDTH + n * 128 : WIDTH + (n + 1) * 128].astype(F32) for n in range(3))
    lane = lax.broadcasted_iota(jnp.int32, (ROWS, 256), 1) & 127
    ids = jnp.concatenate([info[:, s : s + 1] for s in range(SHIFTS)], axis=0)
    pick = (ids == lane.astype(F32)).astype(BF16)
    at = SHIFTS + 2 * TILTS
    sigma = info[:, at : at + 1]
    small = lax.broadcasted_iota(jnp.int32, (P_DEV, 128), 1)

    @pl.loop(0, NB)
    def _(block):
        first = 2 * (block * G + member_ref[0]) + SHIFTS
        start = pl.multiple_of(block * 2 * COLS, 2 * COLS)
        for tilt in range(2):
            kept = jnp.sum(jnp.where(small == first + tilt, info, 0.0), axis=1, keepdims=True)
            focus = jnp.sum(jnp.where(small == first + tilt + TILTS, info, 0.0), axis=1, keepdims=True)
            shell = geo_ref[block * G + member_ref[0], 3:4, tilt * HALF : (tilt + 1) * HALF]
            transfer = -sine_turns((4.0 * focus * shell + 0.1) * (0.5 / math.pi))
            weight = kept * transfer * sigma
            spot = pl.multiple_of(block * COLS + tilt * HALF, HALF)
            pen_ref[:, pl.ds(spot, HALF)] = (0.5 * weight * transfer).astype(BF16)
            lower, upper = pl.ds(start + tilt * HALF, HALF), pl.ds(start + COLS + tilt * HALF, HALF)
            real = (weight * x_ref[:, lower].astype(F32))[None]
            imag = (weight * x_ref[:, upper].astype(F32))[None]
            turned = jnp.dot(
                pick, table_ref[:, pl.ds(start + tilt * COLS, COLS)], preferred_element_type=F32
            ).reshape(SHIFTS, P_DEV, COLS)
            cosine, sine = turned[:, :, :HALF], turned[:, :, HALF:]
            rows_ref[:, lower] = (real * cosine + imag * sine).reshape(ROWS, HALF).astype(BF16)
            rows_ref[:, upper] = (imag * cosine - real * sine).reshape(ROWS, HALF).astype(BF16)


def make_rows(member, x, geo, table):
    return local(
        rows_kernel, "shifted_rows", [((ROWS, WIDTH), BF16), ((P_DEV, NB * COLS), BF16)], [member],
        [x, geo, table], 12, flops=2 * ROWS * 256 * WIDTH, size=9 * MIB,
    )


def scores_kernel(count, *refs):
    blocks = refs[2 * count : 2 * count + 8]
    outs = refs[2 * count + 8 :]
    stacked = jnp.concatenate([block[...] for block in blocks], axis=0)
    power = []
    for block in range(NB):
        start = block * 2 * COLS
        real = stacked[:, start : start + COLS].astype(F32)
        imag = stacked[:, start + COLS : start + 2 * COLS].astype(F32)
        power.append((real * real + imag * imag).astype(BF16))
    power = jnp.concatenate(power, axis=1)
    pens = jnp.concatenate([pen[...] for pen in refs[count : 2 * count]], axis=0)
    rows = jnp.concatenate([row[...] for row in refs[:count]], axis=0)
    energy = lax.dot_general(pens, power, NT, preferred_element_type=F32)
    total = lax.dot_general(rows, stacked, NT, preferred_element_type=F32)
    for n, out in enumerate(outs):
        mine = total[n * ROWS : (n + 1) * ROWS].reshape(SHIFTS, P_DEV, 128)
        out[...] = (mine - energy[None, n * P_DEV : (n + 1) * P_DEV]).reshape(ROWS, 128)


def make_scores(rows, pens, blocks):
    count = len(rows)
    return local(
        lambda *refs: scores_kernel(count, *refs), "partial_scores", [((ROWS, 128), F32)] * count, [],
        [*rows, *pens, *blocks], 12, flops=2 * count * ROWS * 128 * WIDTH, size=(4 * count + 2) * MIB,
    )


def posterior_kernel(*refs):
    out = refs[-1]
    total = refs[0][...]
    for other in refs[1:-1]:
        total = total + other[...]
    total = total.reshape(SHIFTS, P_DEV, 128)
    peak = jnp.max(jnp.max(total, axis=0), axis=1, keepdims=True)
    expo = jnp.exp(total - peak[None])
    norm = jnp.sum(jnp.sum(expo, axis=0), axis=1, keepdims=True)
    share = (expo / norm[None]).reshape(ROWS, 128)
    out[...] = share.T.astype(BF16)


def make_posterior(parts):
    (out,) = local(posterior_kernel, "posterior", [((128, ROWS), BF16)], [], parts, 4, size=MIB // 2)
    return out


def accum_kernel(part, flag_ref, *refs):
    rows, posts, outs = refs[:G], refs[G : 2 * G], refs[2 * G :]

    @pl.loop(0, NB)
    def _(block):
        sums = []
        for half in range(2):
            start = pl.multiple_of(block * 2 * COLS + half * COLS + part * HALF, HALF)
            total = jnp.dot(posts[0][...], rows[0][:, pl.ds(start, HALF)], preferred_element_type=F32)
            for n in range(1, G):
                total = total + jnp.dot(
                    posts[n][...], rows[n][:, pl.ds(start, HALF)], preferred_element_type=F32
                )
            sums.append(total)
        if part == 0:
            for n in range(Y):
                for half, total in enumerate(sums):
                    spot = pl.multiple_of(block * COLS + half * HALF, HALF)
                    outs[n][:, pl.ds(spot, HALF)] = total[n * 32 : (n + 1) * 32].astype(BF16)
        else:
            for n in range(X):
                low = n & 1
                upper = flag_ref[n] == 1
                spot = pl.multiple_of(block * HALF, HALF)
                for k in range(Y):
                    mine = slice(k * 32 + low * 16, k * 32 + low * 16 + 16)
                    chosen = jnp.where(upper, sums[1][mine], sums[0][mine])
                    outs[n][k * 16 : (k + 1) * 16, pl.ds(spot, HALF)] = chosen.astype(BF16)


def make_accum(part, flags, rows, posts):
    shape = (32, NB * COLS) if part == 0 else (64, NB * HALF)
    return local(
        lambda *refs: accum_kernel(part, *refs), "weighted_sums", [(shape, BF16)] * 4, [flags],
        [*rows, *posts], 8, flops=2 * G * ROWS * 128 * NB * COLS, size=(2 * G + 1) * MIB,
    )


def added(values):
    total = values[0].astype(F32)
    for value in values[1:]:
        total = total + value.astype(F32)
    return total


PIECES = [((16, NB * HALF), F32)] + [((16, NB * HALF), BF16)] * 3


def first_kernel(flag_ref, *refs):
    outs = refs[4:]
    for block in range(NB):
        start = block * COLS
        real = added([ref[:, start : start + HALF] for ref in refs[:4]])
        imag = added([ref[:, start + HALF : start + COLS] for ref in refs[:4]])
        for n, out in enumerate(outs):
            mine = slice((n & 1) * 16, (n & 1) * 16 + 16)
            chosen = jnp.where(flag_ref[n] == 1, imag[mine], real[mine])
            out[:, block * HALF : (block + 1) * HALF] = chosen.astype(out.dtype)


def second_kernel(*refs):
    for n, out in enumerate(refs[4:]):
        out[...] = added([ref[n * 16 : (n + 1) * 16] for ref in refs[:4]]).astype(out.dtype)


def joined_kernel(block_ref, *refs):
    for n, out in enumerate(refs[8:]):
        spot = pl.ds(pl.multiple_of(((block_ref[0] + n) % NB) * HALF, HALF), HALF)
        out[:, :HALF] = added([ref[:, spot] for ref in refs[:4]]).astype(out.dtype)
        out[:, HALF:] = added([ref[:, spot] for ref in refs[4:8]]).astype(out.dtype)


def after(value, *others):
    return lax.optimization_barrier((value, *others))[0]


def per_device(refs, particles, shift_ids, wedge, defocus, inv_sigma):
    dom = lax.axis_index("dom")
    x_at = (dom // 16) * 2 + lax.axis_index("blk") % 2
    member = (dom % G).astype(jnp.int32).reshape(1)
    block = ((dom % 16) // G).astype(jnp.int32).reshape(1)
    flags = (((x_at + jnp.arange(X)) % X) // 2).astype(jnp.int32)
    geo = jnp.asarray(geometry())

    gathered = {}
    own = own_columns(member, refs)
    gathered[0, 0] = own
    gathered[1, 0] = send(own, moves(dy=-1))
    gathered[3, 0] = send(own, moves(dy=1))
    gathered[2, 0] = send(own, moves(dy=2))
    chunks = split_particles(member, own, particles, shift_ids, wedge, defocus, inv_sigma)
    got = {0: chunks[0]}
    got[2] = send(chunks[2], partners(2))
    got[1] = send(chunks[1], partners(1))
    table = make_table(member, geo)
    rows, pens = {}, {}
    rows[0], pens[0] = make_rows(member, got[0], geo, table)
    gathered[0, 1] = send(after(own, got[1]), moves(dx=-1))
    gathered[1, 1] = send(after(gathered[1, 0], rows[0]), moves(dx=-1))
    gathered[3, 1] = send(after(gathered[3, 0], rows[0]), moves(dx=1))
    got[3] = send(after(chunks[3], rows[0]), partners(3))
    rows[1], pens[1] = make_rows(member, got[1], geo, table)
    gathered[2, 1] = send(after(gathered[2, 0], rows[1]), moves(dx=1))
    rows[2], pens[2] = make_rows(member, after(got[2], rows[1]), geo, table)
    blocks = [gathered[ky, kx] for ky in range(Y) for kx in range(2)]

    early = make_scores([rows[n] for n in range(3)], [pens[n] for n in range(3)], blocks)
    rows[3], pens[3] = make_rows(member, after(got[3], rows[2]), geo, table)
    late = make_scores([rows[3]], [pens[3]], blocks)
    parts = list(early) + list(late)
    arrived = [send(parts[n], partners(n)) for n in range(1, G)]
    posterior = make_posterior([parts[0]] + arrived)
    posts = [posterior] + [send(posterior, partners(n)) for n in range(1, G)]
    rows = [rows[n] for n in range(G)]

    first = make_accum(0, flags, rows, posts)
    first = [first[0]] + [send(first[n], moves(dy=n)) for n in range(1, Y)]
    second = make_accum(1, flags, rows, posts)
    second = [second[0]] + [send(second[n], moves(dx=n)) for n in range(1, X)]
    first = local(first_kernel, "first_sums", PIECES, [flags], first, 4, size=MIB)
    first = [first[0]] + [send(first[n], moves(dx=n)) for n in range(1, X)]
    second = local(second_kernel, "second_sums", PIECES, [], second, 4, size=MIB)
    second = [second[0]] + [send(second[n], moves(dy=n)) for n in range(1, Y)]
    outs = [((16, COLS), F32)] + [((16, COLS), BF16)] * (NB - 1)
    ends = local(joined_kernel, "joined_sums", outs, [block], [*first, *second], 4, size=MIB)
    return added([ends[0]] + [send(ends[n], moves(dz=n * (G // 2))) for n in range(1, NB)])


def solution(mesh):
    return jax.shard_map(
        per_device,
        mesh=mesh,
        in_specs=(
            P("blk", None),
            P(("blk", "dom"), None),
            P(("blk", "dom"), None),
            P(("blk", "dom"), None),
            P(("blk", "dom"), None),
            P(("blk", "dom")),
        ),
        out_specs=P("blk", "dom"),
        check_vma=False,
    )
```

time: 165 us -> 132 us (0.80)
  local copies, waits for them, and re-layouts: 31.1 us -> 16.4 us
  Pallas kernels: 44.8 us -> 30.2 us
  between operations: 8.42 us -> 0.33 us
  starting transfers between devices: 42.8 us -> 47.2 us
    pallas_call x12 -> x15, Pallas kernels: 44.8 us -> 30.2 us  [local(): pl.pallas_call(kernel, in_specs=[SCALARS] * len(scalars) + [PLACED] * pla...]
    unnamed x62 -> x31, local copies, waits for them, and re-layouts: 28.1 us -> 15.7 us
    ppermute x31, starting transfers between devices: 42.8 us -> 47.2 us  [send(): return lax.ppermute(value, AXES, pairs)]
  transfers between devices with their start and end apart: 31 -> 31, of which waited for: 10 -> 12; matrix products, arithmetic and copies ran while one was open for 2% -> 0% of each run, Pallas kernels for 24% -> 17%
where the time goes in v3:
time: 132 us; the launch traced here: 130 us
  starting transfers between devices  47.2 us (36%)
  waiting for transfers between devices  35.1 us (27%)
  Pallas kernels  30.2 us (23%)
  local copies, waits for them, and re-layouts  16.4 us (12%)
    ppermute x31, starting transfers between devices, send(): return lax.ppermute(value, AXES, pairs)  47.2 us
    ppermute x31, waiting for transfers between devices, send(): return lax.ppermute(value, AXES, pairs)  35.1 us
    pallas_call x15, Pallas kernels, local(): pl.pallas_call(kernel, in_specs=[SCALARS] * len(scalars) + [PLACED] * pla...  30.2 us
    unnamed x31, local copies, waits for them, and re-layouts  15.7 us
  transfers between devices with their start and end apart: 31, of which 12 were waited for; matrix products, arithmetic and copies ran while one was open for 0% of the time, Pallas kernels for 17%

profile of v3, /device:TPU:2, one launch (start us, length us, event | category | flops | bytes accessed | tf_op | source)
XLA Modules:
  0.0 129.9 jit_solution(17613166410637218944)
XLA Ops:
  3.0 1.6 %copy-done.10 = bf16[32,32768]{1,0:T(8,128)(2,1)S(1)} copy-done((bf16[32,32768]{1,0:T(8,128)(2,1)S(1)}, bf16[32,32768]{1,0:T(8,128)(2,1)}, u32[]{:S(2)}) %copy-start.10) | copy-done | bytes 2097176
  7.3 2.0 %collective-permute-start.1 = (bf16[32,8576]{1,0:T(8,128)(2,1)S(1)}, bf16[32,8576]{1,0:T(8,128)(2,1)S(1)}, u32[]{:S(2)}, u32[]{:S(2)}) collective-permute-start(bf16[32,8576]{1,0:T(8,128)(2,1)S(1)} %get-tuple-element.51), channel_id=1, source_target_pairs={{0,2},{1,3},{2,0},{3,1},{4,6},{5,7},{6,4},{7,5},{8,10},{9,11},{10,... | collective-permute-start | bytes 1646600 | tf_op jit(solution)/shard_map/ppermute | solution.py:49
  9.3 3.0 %collective-permute-start.4 = (bf16[16,8192]{1,0:T(8,128)(2,1)S(1)}, bf16[16,8192]{1,0:T(8,128)(2,1)S(1)}, u32[]{:S(2)}, u32[]{:S(2)}) collective-permute-start(bf16[16,8192]{1,0:T(8,128)(2,1)S(1)} %own_references.1.after.refs_6_.refs_2_), channel_id=1, source_target_pairs={{0,192},{1,193},{2,194},{3,195},{4,196},{5,197},{6,198},{7,199},{8... | collective-permute-start | bytes 786440 | tf_op jit(solution)/shard_map/ppermute | solution.py:49
  14.2 5.4 %phase_table.1.table_ref = bf16[256,8192]{1,0:T(8,128)(2,1)S(1)} custom-call(s32[1]{0:T(128)} %bitcast.1.member_ref, f32[16,8,1024]{2,1,0:T(8,128)S(1)} %copy-done.8, f32[128,8]{1,0:T(8,128)S(1)} %copy-done.12), custom_call_target="tpu_custom_call" | custom-call | flops 20971520 | bytes 5242880 | tf_op jit(solution)/shard_map/phase_table/pallas_call | solution.py:106
  19.6 3.0 %shifted_rows.4 = (bf16[256,8192]{1,0:T(8,128)(2,1)S(1)}, bf16[32,4096]{1,0:T(8,128)(2,1)S(1)}) custom-call(s32[1]{0:T(128)} %bitcast.1.member_ref, bf16[32,8576]{1,0:T(8,128)(2,1)S(1)} %get-tuple-element.47.x_ref, f32[16,8,1024]{2,1,0:T(8,128)S(1)} %copy-done.9, bf16[256,8192]{1,0:T(8,128)(2,1)S(1)} %phase_table.1.table_ref), custom_call_target="tpu_custom_call" | custom-call | flops 1073741824 | bytes 9437184 | tf_op jit(solution)/shard_map/shifted_rows/pallas_call | solution.py:106
  22.9 2.2 %collective-permute-start.6 = (bf16[16,8192]{1,0:T(8,128)(2,1)S(1)}, bf16[16,8192]{1,0:T(8,128)(2,1)S(1)}, u32[]{:S(2)}, u32[]{:S(2)}) collective-permute-start(bf16[16,8192]{1,0:T(8,128)(2,1)S(1)} %own_references.1.after.refs_6_.refs_2_), channel_id=1, source_target_pairs={{0,128},{1,129},{2,130},{3,131},{4,132},{5,133},{6,134},{7,135},{8... | collective-permute-start | bytes 786440 | tf_op jit(solution)/shard_map/ppermute | solution.py:49
  25.1 13.0 %collective-permute-done.8.refs_12_.refs_8_ = bf16[16,8192]{1,0:T(8,128)(2,1)S(1)} collective-permute-done((bf16[16,8192]{1,0:T(8,128)(2,1)S(1)}, bf16[16,8192]{1,0:T(8,128)(2,1)S(1)}, u32[]{:S(2)}, u32[]{:S(2)}) %collective-permute-start.8) | collective-permute-done | bytes 262176 | tf_op jit(solution)/shard_map/ppermute | solution.py:49
  40.1 3.0 %shifted_rows.5 = (bf16[256,8192]{1,0:T(8,128)(2,1)S(1)}, bf16[32,4096]{1,0:T(8,128)(2,1)S(1)}) custom-call(s32[1]{0:T(128)} %bitcast.1.member_ref, bf16[32,8576]{1,0:T(8,128)(2,1)S(1)} %collective-permute-done.x_ref, f32[16,8,1024]{2,1,0:T(8,128)S(1)} %copy-done.9, bf16[256,8192]{1,0:T(8,128)(2,1)S(1)} %phase_table.1.table_ref), custom_call_target="tpu_custom_call" | custom-call | flops 1073741824 | bytes 9437184 | tf_op jit(solution)/shard_map/shifted_rows/pallas_call | solution.py:106
  45.2 3.0 %shifted_rows.6 = (bf16[256,8192]{1,0:T(8,128)(2,1)S(1)}, bf16[32,4096]{1,0:T(8,128)(2,1)S(1)}) custom-call(s32[1]{0:T(128)} %bitcast.1.member_ref, bf16[32,8576]{1,0:T(8,128)(2,1)S(1)} %collective-permute-done.1.x_ref, f32[16,8,1024]{2,1,0:T(8,128)S(1)} %copy-done.9, bf16[256,8192]{1,0:T(8,128)(2,1)S(1)} %phase_table.1.table_ref), custom_call_target="tpu_custom_call" | custom-call | flops 1073741824 | bytes 9437184 | tf_op jit(solution)/shard_map/shifted_rows/pallas_call | solution.py:106
  48.3 3.0 %shifted_rows.7 = (bf16[256,8192]{1,0:T(8,128)(2,1)S(1)}, bf16[32,4096]{1,0:T(8,128)(2,1)S(1)}) custom-call(s32[1]{0:T(128)} %bitcast.1.member_ref, bf16[32,8576]{1,0:T(8,128)(2,1)S(1)} %collective-permute-done.2.x_ref, f32[16,8,1024]{2,1,0:T(8,128)S(1)} %copy-done.9, bf16[256,8192]{1,0:T(8,128)(2,1)S(1)} %phase_table.1.table_ref), custom_call_target="tpu_custom_call" | custom-call | flops 1073741824 | bytes 9437184 | tf_op jit(solution)/shard_map/shifted_rows/pallas_call | solution.py:106
  52.7 3.7 %partial_scores.2 = (f32[256,128]{1,0:T(8,128)S(1)}, f32[256,128]{1,0:T(8,128)S(1)}, f32[256,128]{1,0:T(8,128)S(1)}) custom-call(bf16[256,8192]{1,0:T(8,128)(2,1)S(1)} %get-tuple-element.48.refs_0_.refs_1_, bf16[256,8192]{1,0:T(8,128)(2,1)S(1)} %get-tuple-element.50.refs_1_.refs_2_, bf16[256,8192]{1,0:T(8,128)(2,1)S(1)} %get-tuple-element.53.refs_2_.refs_3_, ...), custom_call_target="tpu_custom_call" | custom-call | flops 1610612736 | bytes 14680064 | tf_op jit(solution)/shard_map/partial_scores/pallas_call | solution.py:106
  56.5 2.5 %collective-permute-start.11 = (f32[256,128]{1,0:T(8,128)S(1)}, f32[256,128]{1,0:T(8,128)S(1)}, u32[]{:S(2)}, u32[]{:S(2)}) collective-permute-start(f32[256,128]{1,0:T(8,128)S(1)} %get-tuple-element.67), channel_id=1, source_target_pairs={{0,2},{1,3},{2,0},{3,1},{4,6},{5,7},{6,4},{7,5},{8,10},{9,11},{10,... | collective-permute-start | bytes 393224 | tf_op jit(solution)/shard_map/ppermute | solution.py:49
  59.0 1.5 %partial_scores.3 = f32[256,128]{1,0:T(8,128)S(1)} custom-call(bf16[256,8192]{1,0:T(8,128)(2,1)S(1)} %get-tuple-element.57.refs_0_.refs_4_, bf16[32,4096]{1,0:T(8,128)(2,1)S(1)} %get-tuple-element.68.refs_1_, bf16[16,8192]{1,0:T(8,128)(2,1)S(1)} %own_references.1.after.refs_6_.refs_2_, bf16[16,8192]{1,0:T(8,128)(2,1)S(1)} %collective-permute-done.3.refs_7_.refs_3_, ...), custom_call_target="tpu_custom_call" | custom-call | flops 536870912 | bytes 6291456 | tf_op jit(solution)/shard_map/partial_scores/pallas_call | solution.py:106
  60.6 2.4 %collective-permute-done.11.refs_2_ = f32[256,128]{1,0:T(8,128)S(1)} collective-permute-done((f32[256,128]{1,0:T(8,128)S(1)}, f32[256,128]{1,0:T(8,128)S(1)}, u32[]{:S(2)}, u32[]{:S(2)}) %collective-permute-start.11) | collective-permute-done | bytes 131104 | tf_op jit(solution)/shard_map/ppermute | solution.py:49
  63.0 3.0 %collective-permute-done.12.refs_3_ = f32[256,128]{1,0:T(8,128)S(1)} collective-permute-done((f32[256,128]{1,0:T(8,128)S(1)}, f32[256,128]{1,0:T(8,128)S(1)}, u32[]{:S(2)}, u32[]{:S(2)}) %collective-permute-start.12) | collective-permute-done | bytes 131104 | tf_op jit(solution)/shard_map/ppermute | solution.py:49
  68.3 2.8 %collective-permute-done.14.refs_7_ = bf16[128,256]{1,0:T(8,128)(2,1)S(1)} collective-permute-done((bf16[128,256]{1,0:T(8,128)(2,1)S(1)}, bf16[128,256]{1,0:T(8,128)(2,1)S(1)}, u32[]{:S(2)}, u32[]{:S(2)}) %collective-permute-start.14) | collective-permute-done | bytes 65568 | tf_op jit(solution)/shard_map/ppermute | solution.py:49
  72.2 2.2 %copy-done.1 = bf16[256,8192]{1,0:T(8,128)(2,1)S(1)} copy-done((bf16[256,8192]{1,0:T(8,128)(2,1)S(1)}, bf16[256,8192]{1,0:T(8,128)(2,1)}, u32[]{:S(2)}) %copy-start.1) | copy-done | bytes 4194328
  74.4 2.2 %copy-done.3 = bf16[256,8192]{1,0:T(8,128)(2,1)S(1)} copy-done((bf16[256,8192]{1,0:T(8,128)(2,1)S(1)}, bf16[256,8192]{1,0:T(8,128)(2,1)}, u32[]{:S(2)}) %copy-start.3) | copy-done | bytes 4194328
  76.5 2.2 %copy-done.5 = bf16[256,8192]{1,0:T(8,128)(2,1)S(1)} copy-done((bf16[256,8192]{1,0:T(8,128)(2,1)S(1)}, bf16[256,8192]{1,0:T(8,128)(2,1)}, u32[]{:S(2)}) %copy-start.5) | copy-done | bytes 4194328
  78.7 2.2 %copy-done.7 = bf16[256,8192]{1,0:T(8,128)(2,1)S(1)} copy-done((bf16[256,8192]{1,0:T(8,128)(2,1)S(1)}, bf16[256,8192]{1,0:T(8,128)(2,1)}, u32[]{:S(2)}) %copy-start.7) | copy-done | bytes 4194328
  80.9 2.4 %weighted_sums.2 = (bf16[32,4096]{1,0:T(8,128)(2,1)S(1)}, bf16[32,4096]{1,0:T(8,128)(2,1)S(1)}, bf16[32,4096]{1,0:T(8,128)(2,1)S(1)}, bf16[32,4096]{1,0:T(8,128)(2,1)S(1)}) custom-call(s32[4]{0:T(128)S(1)} %and_select_fusion.refs_0_.flag_ref, bf16[256,8192]{1,0:T(8,128)(2,1)S(1)} %copy-done.3, bf16[256,8192]{1,0:T(8,128)(2,1)S(1)} %copy-done.5, ...), custom_call_target="tpu_custom_call" | custom-call | flops 1073741824 | bytes 9437184 | tf_op jit(solution)/shard_map/weighted_sums/pallas_call | solution.py:106
  84.3 2.4 %collective-permute-start.18 = (bf16[32,4096]{1,0:T(8,128)(2,1)S(1)}, bf16[32,4096]{1,0:T(8,128)(2,1)S(1)}, u32[]{:S(2)}, u32[]{:S(2)}) collective-permute-start(bf16[32,4096]{1,0:T(8,128)(2,1)S(1)} %get-tuple-element.72), channel_id=1, source_target_pairs={{0,192},{1,193},{2,194},{3,195},{4,196},{5,197},{6,198},{7,199},{8... | collective-permute-start | bytes 786440 | tf_op jit(solution)/shard_map/ppermute | solution.py:49
  86.6 2.4 %weighted_sums.3 = (bf16[64,2048]{1,0:T(8,128)(2,1)S(1)}, bf16[64,2048]{1,0:T(8,128)(2,1)S(1)}, bf16[64,2048]{1,0:T(8,128)(2,1)S(1)}, bf16[64,2048]{1,0:T(8,128)(2,1)S(1)}) custom-call(s32[4]{0:T(128)S(1)} %and_select_fusion.refs_0_.flag_ref, bf16[256,8192]{1,0:T(8,128)(2,1)S(1)} %copy-done.3, bf16[256,8192]{1,0:T(8,128)(2,1)S(1)} %copy-done.5, ...), custom_call_target="tpu_custom_call" | custom-call | flops 1073741824 | bytes 9437184 | tf_op jit(solution)/shard_map/weighted_sums/pallas_call | solution.py:106
  89.8 4.6 %collective-permute-start.23 = (bf16[64,2048]{1,0:T(8,128)(2,1)S(1)}, bf16[64,2048]{1,0:T(8,128)(2,1)S(1)}, u32[]{:S(2)}, u32[]{:S(2)}) collective-permute-start(bf16[64,2048]{1,0:T(8,128)(2,1)S(1)} %get-tuple-element.79), channel_id=1, source_target_pairs={{0,16},{1,17},{2,18},{3,19},{4,20},{5,21},{6,22},{7,23},{8,24},{9,... | collective-permute-start | bytes 786440 | tf_op jit(solution)/shard_map/ppermute | solution.py:49
  94.4 4.2 %collective-permute-done.16.refs_1_ = bf16[32,4096]{1,0:T(8,128)(2,1)S(1)} collective-permute-done((bf16[32,4096]{1,0:T(8,128)(2,1)S(1)}, bf16[32,4096]{1,0:T(8,128)(2,1)S(1)}, u32[]{:S(2)}, u32[]{:S(2)}) %collective-permute-start.16) | collective-permute-done | bytes 262176 | tf_op jit(solution)/shard_map/ppermute | solution.py:49
  98.5 3.0 %collective-permute-start.24 = (bf16[64,2048]{1,0:T(8,128)(2,1)S(1)}, bf16[64,2048]{1,0:T(8,128)(2,1)S(1)}, u32[]{:S(2)}, u32[]{:S(2)}) collective-permute-start(bf16[64,2048]{1,0:T(8,128)(2,1)S(1)} %get-tuple-element.80), channel_id=1, source_target_pairs={{0,48},{1,49},{2,50},{3,51},{4,52},{5,53},{6,54},{7,55},{8,56},{9,... | collective-permute-start | bytes 786440 | tf_op jit(solution)/shard_map/ppermute | solution.py:49
  102.3 3.1 %collective-permute-start.20 = (bf16[16,2048]{1,0:T(8,128)(2,1)S(1)}, bf16[16,2048]{1,0:T(8,128)(2,1)S(1)}, u32[]{:S(2)}, u32[]{:S(2)}) collective-permute-start(bf16[16,2048]{1,0:T(8,128)(2,1)S(1)} %get-tuple-element.75), channel_id=1, source_target_pairs={{0,16},{1,17},{2,18},{3,19},{4,20},{5,21},{6,22},{7,23},{8,24},{9,... | collective-permute-start | bytes 196616 | tf_op jit(solution)/shard_map/ppermute | solution.py:49
  108.5 2.6 %collective-permute-start.26 = (bf16[16,2048]{1,0:T(8,128)(2,1)S(1)}, bf16[16,2048]{1,0:T(8,128)(2,1)S(1)}, u32[]{:S(2)}, u32[]{:S(2)}) collective-permute-start(bf16[16,2048]{1,0:T(8,128)(2,1)S(1)} %get-tuple-element.83), channel_id=1, source_target_pairs={{0,128},{1,129},{2,130},{3,131},{4,132},{5,133},{6,134},{7,135},{8... | collective-permute-start | bytes 196616 | tf_op jit(solution)/shard_map/ppermute | solution.py:49
  111.1 2.5 %collective-permute-start.27 = (bf16[16,2048]{1,0:T(8,128)(2,1)S(1)}, bf16[16,2048]{1,0:T(8,128)(2,1)S(1)}, u32[]{:S(2)}, u32[]{:S(2)}) collective-permute-start(bf16[16,2048]{1,0:T(8,128)(2,1)S(1)} %get-tuple-element.84), channel_id=1, source_target_pairs={{0,192},{1,193},{2,194},{3,195},{4,196},{5,197},{6,198},{7,199},{8... | collective-permute-start | bytes 196616 | tf_op jit(solution)/shard_map/ppermute | solution.py:49
  115.6 5.8 %collective-permute-start.30 = (bf16[16,1024]{1,0:T(8,128)(2,1)S(1)}, bf16[16,1024]{1,0:T(8,128)(2,1)S(1)}, u32[]{:S(2)}, u32[]{:S(2)}) collective-permute-start(bf16[16,1024]{1,0:T(8,128)(2,1)S(1)} %get-tuple-element.88), channel_id=1, source_target_pairs={{0,12},{1,13},{2,14},{3,15},{4,0},{5,1},{6,2},{7,3},{8,4},{9,5},{1... | collective-permute-start | bytes 98312 | tf_op jit(solution)/shard_map/ppermute | solution.py:49
  122.5 2.7 %collective-permute-start.28 = (bf16[16,1024]{1,0:T(8,128)(2,1)S(1)}, bf16[16,1024]{1,0:T(8,128)(2,1)S(1)}, u32[]{:S(2)}, u32[]{:S(2)}) collective-permute-start(bf16[16,1024]{1,0:T(8,128)(2,1)S(1)} %get-tuple-element.86), channel_id=1, source_target_pairs={{0,4},{1,5},{2,6},{3,7},{4,8},{5,9},{6,10},{7,11},{8,12},{9,13},{1... | collective-permute-start | bytes 98312 | tf_op jit(solution)/shard_map/ppermute | solution.py:49
  125.2 4.0 %collective-permute-done.29 = bf16[16,1024]{1,0:T(8,128)(2,1)S(1)} collective-permute-done((bf16[16,1024]{1,0:T(8,128)(2,1)S(1)}, bf16[16,1024]{1,0:T(8,128)(2,1)S(1)}, u32[]{:S(2)}, u32[]{:S(2)}) %collective-permute-start.29) | collective-permute-done | bytes 32800 | tf_op jit(solution)/shard_map/ppermute | solution.py:49
  (79 shorter events, 26.0 us)
Async XLA Ops:
  7.2 31.4 %collective-permute-start = (bf16[32,8576]{1,0:T(8,128)(2,1)S(1)}, bf16[32,8576]{1,0:T(8,128)(2,1)S(1)}, u32[]{:S(2)}, u32[]{:S(2)}) collective-permute-start(bf16[32,8576]{1,0:T(8,128)(2,1)S(1)} %get-tuple-element.49), channel_id=1, source_target_pairs={{0,1},{1,0},{2,3},{3,2},{4,5},{5,4},{6,7},{7,6},{8,9},{9,8},{10,11... | collective-permute-start | bytes 1646600 | tf_op jit(solution)/shard_map/ppermute | solution.py:49
  7.3 37.2 %collective-permute-start.1 = (bf16[32,8576]{1,0:T(8,128)(2,1)S(1)}, bf16[32,8576]{1,0:T(8,128)(2,1)S(1)}, u32[]{:S(2)}, u32[]{:S(2)}) collective-permute-start(bf16[32,8576]{1,0:T(8,128)(2,1)S(1)} %get-tuple-element.51), channel_id=1, source_target_pairs={{0,2},{1,3},{2,0},{3,1},{4,6},{5,7},{6,4},{7,5},{8,10},{9,11},{10,... | collective-permute-start | bytes 1646600 | tf_op jit(solution)/shard_map/ppermute | solution.py:49
  9.3 13.6 %collective-permute-start.4 = (bf16[16,8192]{1,0:T(8,128)(2,1)S(1)}, bf16[16,8192]{1,0:T(8,128)(2,1)S(1)}, u32[]{:S(2)}, u32[]{:S(2)}) collective-permute-start(bf16[16,8192]{1,0:T(8,128)(2,1)S(1)} %own_references.1.after.refs_6_.refs_2_), channel_id=1, source_target_pairs={{0,192},{1,193},{2,194},{3,195},{4,196},{5,197},{6,198},{7,199},{8... | collective-permute-start | bytes 786440 | tf_op jit(solution)/shard_map/ppermute | solution.py:49
  22.7 30.0 %copy-start.2 = (bf16[256,8192]{1,0:T(8,128)(2,1)}, bf16[256,8192]{1,0:T(8,128)(2,1)S(1)}, u32[]{:S(2)}) copy-start(bf16[256,8192]{1,0:T(8,128)(2,1)S(1)} %get-tuple-element.48.refs_0_.refs_1_) | copy-start | bytes 12582916
  22.7 25.6 %collective-permute-start.2 = (bf16[32,8576]{1,0:T(8,128)(2,1)S(1)}, bf16[32,8576]{1,0:T(8,128)(2,1)S(1)}, u32[]{:S(2)}, u32[]{:S(2)}) collective-permute-start(bf16[32,8576]{1,0:T(8,128)(2,1)S(1)} %get-tuple-element.55), channel_id=1, source_target_pairs={{0,3},{1,2},{2,1},{3,0},{4,7},{5,6},{6,5},{7,4},{8,11},{9,10},{10,... | collective-permute-start | bytes 1646600 | tf_op jit(solution)/shard_map/ppermute | solution.py:49
  22.8 15.3 %collective-permute-start.8 = (bf16[16,8192]{1,0:T(8,128)(2,1)S(1)}, bf16[16,8192]{1,0:T(8,128)(2,1)S(1)}, u32[]{:S(2)}, u32[]{:S(2)}) collective-permute-start(bf16[16,8192]{1,0:T(8,128)(2,1)S(1)} %own_references.1.after.refs_6_.refs_2_), channel_id=1, source_target_pairs={{0,64},{1,65},{2,66},{3,67},{4,68},{5,69},{6,70},{7,71},{8,72},{9,... | collective-permute-start | bytes 786440 | tf_op jit(solution)/shard_map/ppermute | solution.py:49
  22.9 20.2 %collective-permute-start.6 = (bf16[16,8192]{1,0:T(8,128)(2,1)S(1)}, bf16[16,8192]{1,0:T(8,128)(2,1)S(1)}, u32[]{:S(2)}, u32[]{:S(2)}) collective-permute-start(bf16[16,8192]{1,0:T(8,128)(2,1)S(1)} %own_references.1.after.refs_6_.refs_2_), channel_id=1, source_target_pairs={{0,128},{1,129},{2,130},{3,131},{4,132},{5,133},{6,134},{7,135},{8... | collective-permute-start | bytes 786440 | tf_op jit(solution)/shard_map/ppermute | solution.py:49
  38.0 13.4 %collective-permute-start.5 = (bf16[16,8192]{1,0:T(8,128)(2,1)S(1)}, bf16[16,8192]{1,0:T(8,128)(2,1)S(1)}, u32[]{:S(2)}, u32[]{:S(2)}) collective-permute-start(bf16[16,8192]{1,0:T(8,128)(2,1)S(1)} %collective-permute-done.4.refs_8_.refs_4_), channel_id=1, source_target_pairs={{0,48},{1,49},{2,50},{3,51},{4,52},{5,53},{6,54},{7,55},{8,56},{9,... | collective-permute-start | bytes 786440 | tf_op jit(solution)/shard_map/ppermute | solution.py:49
  38.6 12.8 %collective-permute-start.9 = (bf16[16,8192]{1,0:T(8,128)(2,1)S(1)}, bf16[16,8192]{1,0:T(8,128)(2,1)S(1)}, u32[]{:S(2)}, u32[]{:S(2)}) collective-permute-start(bf16[16,8192]{1,0:T(8,128)(2,1)S(1)} %collective-permute-done.8.refs_12_.refs_8_), channel_id=1, source_target_pairs={{0,32},{1,33},{2,34},{3,35},{4,36},{5,37},{6,38},{7,39},{8,40},{9,... | collective-permute-start | bytes 786440 | tf_op jit(solution)/shard_map/ppermute | solution.py:49
  43.1 8.3 %collective-permute-start.3 = (bf16[16,8192]{1,0:T(8,128)(2,1)S(1)}, bf16[16,8192]{1,0:T(8,128)(2,1)S(1)}, u32[]{:S(2)}, u32[]{:S(2)}) collective-permute-start(bf16[16,8192]{1,0:T(8,128)(2,1)S(1)} %own_references.1.after.refs_6_.refs_2_), channel_id=1, source_target_pairs={{0,48},{1,49},{2,50},{3,51},{4,52},{5,53},{6,54},{7,55},{8,56},{9,... | collective-permute-start | bytes 786440 | tf_op jit(solution)/shard_map/ppermute | solution.py:49
  44.5 8.2 %collective-permute-start.7 = (bf16[16,8192]{1,0:T(8,128)(2,1)S(1)}, bf16[16,8192]{1,0:T(8,128)(2,1)S(1)}, u32[]{:S(2)}, u32[]{:S(2)}) collective-permute-start(bf16[16,8192]{1,0:T(8,128)(2,1)S(1)} %collective-permute-done.6.refs_10_.refs_6_), channel_id=1, source_target_pairs={{0,32},{1,33},{2,34},{3,35},{4,36},{5,37},{6,38},{7,39},{8,40},{9,... | collective-permute-start | bytes 786440 | tf_op jit(solution)/shard_map/ppermute | solution.py:49
  56.4 4.2 %collective-permute-start.10 = (f32[256,128]{1,0:T(8,128)S(1)}, f32[256,128]{1,0:T(8,128)S(1)}, u32[]{:S(2)}, u32[]{:S(2)}) collective-permute-start(f32[256,128]{1,0:T(8,128)S(1)} %get-tuple-element.66), channel_id=1, source_target_pairs={{0,1},{1,0},{2,3},{3,2},{4,5},{5,4},{6,7},{7,6},{8,9},{9,8},{10,11... | collective-permute-start | bytes 393224 | tf_op jit(solution)/shard_map/ppermute | solution.py:49
  56.5 6.6 %collective-permute-start.11 = (f32[256,128]{1,0:T(8,128)S(1)}, f32[256,128]{1,0:T(8,128)S(1)}, u32[]{:S(2)}, u32[]{:S(2)}) collective-permute-start(f32[256,128]{1,0:T(8,128)S(1)} %get-tuple-element.67), channel_id=1, source_target_pairs={{0,2},{1,3},{2,0},{3,1},{4,6},{5,7},{6,4},{7,5},{8,10},{9,11},{10,... | collective-permute-start | bytes 393224 | tf_op jit(solution)/shard_map/ppermute | solution.py:49
  60.5 5.6 %collective-permute-start.12 = (f32[256,128]{1,0:T(8,128)S(1)}, f32[256,128]{1,0:T(8,128)S(1)}, u32[]{:S(2)}, u32[]{:S(2)}) collective-permute-start(f32[256,128]{1,0:T(8,128)S(1)} %partial_scores.3), channel_id=1, source_target_pairs={{0,3},{1,2},{2,1},{3,0},{4,7},{5,6},{6,5},{7,4},{8,11},{9,10},{10,... | collective-permute-start | bytes 393224 | tf_op jit(solution)/shard_map/ppermute | solution.py:49
  66.3 2.0 %collective-permute-start.13 = (bf16[128,256]{1,0:T(8,128)(2,1)S(1)}, bf16[128,256]{1,0:T(8,128)(2,1)S(1)}, u32[]{:S(2)}, u32[]{:S(2)}) collective-permute-start(bf16[128,256]{1,0:T(8,128)(2,1)S(1)} %posterior.1.refs_5_), channel_id=1, source_target_pairs={{0,1},{1,0},{2,3},{3,2},{4,5},{5,4},{6,7},{7,6},{8,9},{9,8},{10,11... | collective-permute-start | bytes 196616 | tf_op jit(solution)/shard_map/ppermute | solution.py:49
  66.6 4.5 %collective-permute-start.14 = (bf16[128,256]{1,0:T(8,128)(2,1)S(1)}, bf16[128,256]{1,0:T(8,128)(2,1)S(1)}, u32[]{:S(2)}, u32[]{:S(2)}) collective-permute-start(bf16[128,256]{1,0:T(8,128)(2,1)S(1)} %posterior.1.refs_5_), channel_id=1, source_target_pairs={{0,2},{1,3},{2,0},{3,1},{4,6},{5,7},{6,4},{7,5},{8,10},{9,11},{10,... | collective-permute-start | bytes 196616 | tf_op jit(solution)/shard_map/ppermute | solution.py:49
  67.8 4.3 %collective-permute-start.15 = (bf16[128,256]{1,0:T(8,128)(2,1)S(1)}, bf16[128,256]{1,0:T(8,128)(2,1)S(1)}, u32[]{:S(2)}, u32[]{:S(2)}) collective-permute-start(bf16[128,256]{1,0:T(8,128)(2,1)S(1)} %posterior.1.refs_5_), channel_id=1, source_target_pairs={{0,3},{1,2},{2,1},{3,0},{4,7},{5,6},{6,5},{7,4},{8,11},{9,10},{10,... | collective-permute-start | bytes 196616 | tf_op jit(solution)/shard_map/ppermute | solution.py:49
  83.3 15.2 %collective-permute-start.16 = (bf16[32,4096]{1,0:T(8,128)(2,1)S(1)}, bf16[32,4096]{1,0:T(8,128)(2,1)S(1)}, u32[]{:S(2)}, u32[]{:S(2)}) collective-permute-start(bf16[32,4096]{1,0:T(8,128)(2,1)S(1)} %get-tuple-element.70), channel_id=1, source_target_pairs={{0,64},{1,65},{2,66},{3,67},{4,68},{5,69},{6,70},{7,71},{8,72},{9,... | collective-permute-start | bytes 786440 | tf_op jit(solution)/shard_map/ppermute | solution.py:49
  83.4 18.1 %collective-permute-start.17 = (bf16[32,4096]{1,0:T(8,128)(2,1)S(1)}, bf16[32,4096]{1,0:T(8,128)(2,1)S(1)}, u32[]{:S(2)}, u32[]{:S(2)}) collective-permute-start(bf16[32,4096]{1,0:T(8,128)(2,1)S(1)} %get-tuple-element.71), channel_id=1, source_target_pairs={{0,128},{1,129},{2,130},{3,131},{4,132},{5,133},{6,134},{7,135},{8... | collective-permute-start | bytes 786440 | tf_op jit(solution)/shard_map/ppermute | solution.py:49
  84.3 17.2 %collective-permute-start.18 = (bf16[32,4096]{1,0:T(8,128)(2,1)S(1)}, bf16[32,4096]{1,0:T(8,128)(2,1)S(1)}, u32[]{:S(2)}, u32[]{:S(2)}) collective-permute-start(bf16[32,4096]{1,0:T(8,128)(2,1)S(1)} %get-tuple-element.72), channel_id=1, source_target_pairs={{0,192},{1,193},{2,194},{3,195},{4,196},{5,197},{6,198},{7,199},{8... | collective-permute-start | bytes 786440 | tf_op jit(solution)/shard_map/ppermute | solution.py:49
  89.1 16.4 %collective-permute-start.22 = (bf16[64,2048]{1,0:T(8,128)(2,1)S(1)}, bf16[64,2048]{1,0:T(8,128)(2,1)S(1)}, u32[]{:S(2)}, u32[]{:S(2)}) collective-permute-start(bf16[64,2048]{1,0:T(8,128)(2,1)S(1)} %get-tuple-element.78), channel_id=1, source_target_pairs={{0,32},{1,33},{2,34},{3,35},{4,36},{5,37},{6,38},{7,39},{8,40},{9,... | collective-permute-start | bytes 786440 | tf_op jit(solution)/shard_map/ppermute | solution.py:49
  89.8 16.6 %collective-permute-start.23 = (bf16[64,2048]{1,0:T(8,128)(2,1)S(1)}, bf16[64,2048]{1,0:T(8,128)(2,1)S(1)}, u32[]{:S(2)}, u32[]{:S(2)}) collective-permute-start(bf16[64,2048]{1,0:T(8,128)(2,1)S(1)} %get-tuple-element.79), channel_id=1, source_target_pairs={{0,16},{1,17},{2,18},{3,19},{4,20},{5,21},{6,22},{7,23},{8,24},{9,... | collective-permute-start | bytes 786440 | tf_op jit(solution)/shard_map/ppermute | solution.py:49
  98.5 9.4 %collective-permute-start.24 = (bf16[64,2048]{1,0:T(8,128)(2,1)S(1)}, bf16[64,2048]{1,0:T(8,128)(2,1)S(1)}, u32[]{:S(2)}, u32[]{:S(2)}) collective-permute-start(bf16[64,2048]{1,0:T(8,128)(2,1)S(1)} %get-tuple-element.80), channel_id=1, source_target_pairs={{0,48},{1,49},{2,50},{3,51},{4,52},{5,53},{6,54},{7,55},{8,56},{9,... | collective-permute-start | bytes 786440 | tf_op jit(solution)/shard_map/ppermute | solution.py:49
  102.2 8.9 %collective-permute-start.19 = (bf16[16,2048]{1,0:T(8,128)(2,1)S(1)}, bf16[16,2048]{1,0:T(8,128)(2,1)S(1)}, u32[]{:S(2)}, u32[]{:S(2)}) collective-permute-start(bf16[16,2048]{1,0:T(8,128)(2,1)S(1)} %get-tuple-element.74), channel_id=1, source_target_pairs={{0,32},{1,33},{2,34},{3,35},{4,36},{5,37},{6,38},{7,39},{8,40},{9,... | collective-permute-start | bytes 196616 | tf_op jit(solution)/shard_map/ppermute | solution.py:49
  102.3 11.3 %collective-permute-start.20 = (bf16[16,2048]{1,0:T(8,128)(2,1)S(1)}, bf16[16,2048]{1,0:T(8,128)(2,1)S(1)}, u32[]{:S(2)}, u32[]{:S(2)}) collective-permute-start(bf16[16,2048]{1,0:T(8,128)(2,1)S(1)} %get-tuple-element.75), channel_id=1, source_target_pairs={{0,16},{1,17},{2,18},{3,19},{4,20},{5,21},{6,22},{7,23},{8,24},{9,... | collective-permute-start | bytes 196616 | tf_op jit(solution)/shard_map/ppermute | solution.py:49
  105.4 8.2 %collective-permute-start.21 = (bf16[16,2048]{1,0:T(8,128)(2,1)S(1)}, bf16[16,2048]{1,0:T(8,128)(2,1)S(1)}, u32[]{:S(2)}, u32[]{:S(2)}) collective-permute-start(bf16[16,2048]{1,0:T(8,128)(2,1)S(1)} %get-tuple-element.76), channel_id=1, source_target_pairs={{0,48},{1,49},{2,50},{3,51},{4,52},{5,53},{6,54},{7,55},{8,56},{9,... | collective-permute-start | bytes 196616 | tf_op jit(solution)/shard_map/ppermute | solution.py:49
  108.0 5.6 %collective-permute-start.25 = (bf16[16,2048]{1,0:T(8,128)(2,1)S(1)}, bf16[16,2048]{1,0:T(8,128)(2,1)S(1)}, u32[]{:S(2)}, u32[]{:S(2)}) collective-permute-start(bf16[16,2048]{1,0:T(8,128)(2,1)S(1)} %get-tuple-element.82), channel_id=1, source_target_pairs={{0,64},{1,65},{2,66},{3,67},{4,68},{5,69},{6,70},{7,71},{8,72},{9,... | collective-permute-start | bytes 196616 | tf_op jit(solution)/shard_map/ppermute | solution.py:49
  108.5 5.8 %collective-permute-start.26 = (bf16[16,2048]{1,0:T(8,128)(2,1)S(1)}, bf16[16,2048]{1,0:T(8,128)(2,1)S(1)}, u32[]{:S(2)}, u32[]{:S(2)}) collective-permute-start(bf16[16,2048]{1,0:T(8,128)(2,1)S(1)} %get-tuple-element.83), channel_id=1, source_target_pairs={{0,128},{1,129},{2,130},{3,131},{4,132},{5,133},{6,134},{7,135},{8... | collective-permute-start | bytes 196616 | tf_op jit(solution)/shard_map/ppermute | solution.py:49
  111.1 4.4 %collective-permute-start.27 = (bf16[16,2048]{1,0:T(8,128)(2,1)S(1)}, bf16[16,2048]{1,0:T(8,128)(2,1)S(1)}, u32[]{:S(2)}, u32[]{:S(2)}) collective-permute-start(bf16[16,2048]{1,0:T(8,128)(2,1)S(1)} %get-tuple-element.84), channel_id=1, source_target_pairs={{0,192},{1,193},{2,194},{3,195},{4,196},{5,197},{6,198},{7,199},{8... | collective-permute-start | bytes 196616 | tf_op jit(solution)/shard_map/ppermute | solution.py:49
  115.6 9.6 %collective-permute-start.30 = (bf16[16,1024]{1,0:T(8,128)(2,1)S(1)}, bf16[16,1024]{1,0:T(8,128)(2,1)S(1)}, u32[]{:S(2)}, u32[]{:S(2)}) collective-permute-start(bf16[16,1024]{1,0:T(8,128)(2,1)S(1)} %get-tuple-element.88), channel_id=1, source_target_pairs={{0,12},{1,13},{2,14},{3,15},{4,0},{5,1},{6,2},{7,3},{8,4},{9,5},{1... | collective-permute-start | bytes 98312 | tf_op jit(solution)/shard_map/ppermute | solution.py:49
  121.4 7.8 %collective-permute-start.29 = (bf16[16,1024]{1,0:T(8,128)(2,1)S(1)}, bf16[16,1024]{1,0:T(8,128)(2,1)S(1)}, u32[]{:S(2)}, u32[]{:S(2)}) collective-permute-start(bf16[16,1024]{1,0:T(8,128)(2,1)S(1)} %get-tuple-element.87), channel_id=1, source_target_pairs={{0,8},{1,9},{2,10},{3,11},{4,12},{5,13},{6,14},{7,15},{8,0},{9,1},... | collective-permute-start | bytes 98312 | tf_op jit(solution)/shard_map/ppermute | solution.py:49
  122.5 6.7 %collective-permute-start.28 = (bf16[16,1024]{1,0:T(8,128)(2,1)S(1)}, bf16[16,1024]{1,0:T(8,128)(2,1)S(1)}, u32[]{:S(2)}, u32[]{:S(2)}) collective-permute-start(bf16[16,1024]{1,0:T(8,128)(2,1)S(1)} %get-tuple-element.86), channel_id=1, source_target_pairs={{0,4},{1,5},{2,6},{3,7},{4,8},{5,9},{6,10},{7,11},{8,12},{9,13},{1... | collective-permute-start | bytes 98312 | tf_op jit(solution)/shard_map/ppermute | solution.py:49
  (14 other events, 57.0 us)

commit v4 on v3

--- a/solution.py
+++ b/solution.py
@@ -61,15 +61,6 @@
     return table.reshape(8, 16, COLS).transpose(1, 0, 2).astype(np.float32)
 
 
-def translations():
-    ids = np.arange(128)
-    out = np.zeros((128, 8), np.float32)
-    for column, digit in enumerate((ids // 25, ids // 5 % 5, ids % 5)):
-        out[:, column] = (digit - 2) * 0.5 / BOX
-    out[125:] = 0
-    return out
-
-
 def fold(turns):
     turns = turns - jnp.floor(turns + 0.5)
     far = jnp.abs(turns) > 0.25
@@ -109,21 +100,33 @@
         out_specs=[WHOLE] * len(outs),
         out_shape=[pltpu.VMEM(shape, kind) for shape, kind in outs],
         scratch_shapes=list(scratch),
-        cost_estimate=pl.CostEstimate(flops=flops, bytes_accessed=size, transcendentals=0),
+        cost_estimate=pl.CostEstimate(flops=0, bytes_accessed=0, transcendentals=0),
         compiler_params=pltpu.CompilerParams(vmem_limit_bytes=limit * MIB),
         name=name,
-    )(*scalars, *arrays[:placed], *[held(value) for value in arrays[placed:]])
-
-
-def table_kernel(member_ref, geo_ref, shift_ref, out_ref):
-    shift = shift_ref[...]
+    )(*scalars, *[pltpu.with_memory_space_constraint(value, pltpu.HBM) for value in arrays[:placed]], *[held(value) for value in arrays[placed:]])
+
+
+def table_kernel(member_ref, geo_ref, out_ref, picked_ref, sems):
+    copies = [
+        pltpu.make_async_copy(geo_ref.at[block * G + member_ref[0]], picked_ref.at[block], sems.at[block])
+        for block in range(NB)
+    ]
+    for copy in copies:
+        copy.start()
+    ids = lax.broadcasted_iota(jnp.int32, (128, 1), 0).astype(F32)
+    high = jnp.floor((ids + 0.5) * (1 / 25))
+    middle = jnp.floor((ids - 25 * high + 0.5) * (1 / 5))
+    low = ids - 25 * high - 5 * middle
+    move_x, move_y, move_z = ((digit - 2.0) * (0.5 / BOX) for digit in (high, middle, low))
+    for copy in copies:
+        copy.wait()
 
     @pl.loop(0, NB)
     def _(block):
-        geo = geo_ref[block * G + member_ref[0]]
+        geo = picked_ref[block]
         for tilt in range(2):
             part = geo[:, tilt * HALF : (tilt + 1) * HALF]
-            turns = shift[:, 0:1] * part[0:1] + shift[:, 1:2] * part[1:2] + shift[:, 2:3] * part[2:3]
+            turns = move_x * part[0:1] + move_y * part[1:2] + move_z * part[2:3]
             angle, far = fold(turns)
             square = angle * angle
             sine = angle * series(square, SIN_TERMS)
@@ -138,11 +141,10 @@
 
 
 def make_table(member, geo):
-    (table,) = local(
-        table_kernel, "phase_table", [((256, WIDTH), BF16)], [member],
-        [geo, jnp.asarray(translations())], 8, flops=NB * 128 * COLS * 40, size=5 * MIB,
-    )
-    return table
+    return local(
+        table_kernel, "phase_table", [((256, WIDTH), BF16), ((NB, 8, COLS), F32)], [member], [geo], 8,
+        placed=1, scratch=[pltpu.SemaphoreType.DMA((NB,))],
+    )
 
 
 def column(part, block, who):
@@ -176,29 +178,53 @@
     return own
 
 
-def split_kernel(member_ref, source, after, ids, wedge, focus, sigma, *refs):
-    outs, sems = refs[:-1], refs[-1]
+def parts_of(values):
+    high = values.astype(BF16)
+    rest = values - high.astype(F32)
+    middle = rest.astype(BF16)
+    return high, middle, (rest - middle.astype(F32)).astype(BF16)
+
+
+def turned_over(values):
+    rows, columns = values.shape
+    same = lax.broadcasted_iota(jnp.int32, (columns, columns), 0) == lax.broadcasted_iota(
+        jnp.int32, (columns, columns), 1
+    )
+    return sum(
+        lax.dot_general(same.astype(BF16), part, NT, preferred_element_type=F32)
+        for part in parts_of(values)
+    )
+
+
+def split_kernel(member_ref, source, ids, wedge, focus, sigma, after, *refs):
+    outs, (ids_in, wedge_in, focus_in, sigma_in, sems, more) = refs[:G], refs[G:]
     copies = []
     for n in (2, 1, 3, 0):
         copies += pieces_of(source, outs[n], member_ref[0] ^ n, sems, n * 2 * NB)
-    for copy in copies:
+    settings = [
+        pltpu.make_async_copy(at, to, more.at[n])
+        for n, (at, to) in enumerate(
+            ((ids, ids_in), (wedge, wedge_in), (focus, focus_in), (sigma, sigma_in))
+        )
+    ]
+    for copy in copies + settings:
         copy.start()
+    for copy in settings:
+        copy.wait()
+    first = jnp.concatenate(
+        [ids_in[...].astype(F32), jnp.broadcast_to(sigma_in[...], (8, P_DEV))], axis=0
+    )
     info = jnp.concatenate(
         [
-            ids[...].astype(F32),
-            wedge[...].astype(F32),
-            focus[...],
-            sigma[...],
-            jnp.zeros((P_DEV, 128 - SHIFTS - 2 * TILTS - 1), F32),
+            turned_over(first),
+            wedge_in[...].astype(F32),
+            focus_in[...],
+            jnp.zeros((P_DEV, 128 - 16 - 2 * TILTS), F32),
         ],
         axis=1,
     )
-    high = info.astype(BF16)
-    rest = info - high.astype(F32)
-    middle = rest.astype(BF16)
-    low = (rest - middle.astype(F32)).astype(BF16)
-    for out in outs:
-        for spot, piece in enumerate((high, middle, low)):
+    for spot, piece in enumerate(parts_of(info)):
+        for out in outs:
             out[:, WIDTH + spot * 128 : WIDTH + (spot + 1) * 128] = piece
     for copy in copies:
         copy.wait()
@@ -207,8 +233,15 @@
 def split_particles(member, after, particles, shift_ids, wedge, defocus, inv_sigma):
     return local(
         split_kernel, "split_particles", [((P_DEV, WIDTH + EXTRA), BF16)] * G, [member],
-        [particles, after, shift_ids, wedge, defocus, inv_sigma[:, None]], 4, size=4 * MIB,
-        placed=2, scratch=[pltpu.SemaphoreType.DMA((G * 2 * NB,))],
+        [particles, shift_ids.T, wedge, defocus, inv_sigma[None], after], 4, placed=5,
+        scratch=[
+            pltpu.VMEM((SHIFTS, P_DEV), jnp.int32),
+            pltpu.VMEM((P_DEV, TILTS), jnp.int32),
+            pltpu.VMEM((P_DEV, TILTS), F32),
+            pltpu.VMEM((1, P_DEV), F32),
+            pltpu.SemaphoreType.DMA((G * 2 * NB,)),
+            pltpu.SemaphoreType.DMA((4,)),
+        ],
     )
 
 
@@ -217,18 +250,17 @@
     lane = lax.broadcasted_iota(jnp.int32, (ROWS, 256), 1) & 127
     ids = jnp.concatenate([info[:, s : s + 1] for s in range(SHIFTS)], axis=0)
     pick = (ids == lane.astype(F32)).astype(BF16)
-    at = SHIFTS + 2 * TILTS
-    sigma = info[:, at : at + 1]
+    sigma = info[:, SHIFTS : SHIFTS + 1]
     small = lax.broadcasted_iota(jnp.int32, (P_DEV, 128), 1)
 
     @pl.loop(0, NB)
     def _(block):
-        first = 2 * (block * G + member_ref[0]) + SHIFTS
+        first = 2 * (block * G + member_ref[0]) + 16
         start = pl.multiple_of(block * 2 * COLS, 2 * COLS)
         for tilt in range(2):
             kept = jnp.sum(jnp.where(small == first + tilt, info, 0.0), axis=1, keepdims=True)
             focus = jnp.sum(jnp.where(small == first + tilt + TILTS, info, 0.0), axis=1, keepdims=True)
-            shell = geo_ref[block * G + member_ref[0], 3:4, tilt * HALF : (tilt + 1) * HALF]
+            shell = geo_ref[block, 3:4, tilt * HALF : (tilt + 1) * HALF]
             transfer = -sine_turns((4.0 * focus * shell + 0.1) * (0.5 / math.pi))
             weight = kept * transfer * sigma
             spot = pl.multiple_of(block * COLS + tilt * HALF, HALF)
@@ -298,41 +330,45 @@
 
 
 def accum_kernel(part, flag_ref, *refs):
-    rows, posts, outs = refs[:G], refs[G : 2 * G], refs[2 * G :]
-
-    @pl.loop(0, NB)
-    def _(block):
-        sums = []
-        for half in range(2):
-            start = pl.multiple_of(block * 2 * COLS + half * COLS + part * HALF, HALF)
-            total = jnp.dot(posts[0][...], rows[0][:, pl.ds(start, HALF)], preferred_element_type=F32)
-            for n in range(1, G):
-                total = total + jnp.dot(
-                    posts[n][...], rows[n][:, pl.ds(start, HALF)], preferred_element_type=F32
-                )
-            sums.append(total)
-        if part == 0:
-            for n in range(Y):
-                for half, total in enumerate(sums):
-                    spot = pl.multiple_of(block * COLS + half * HALF, HALF)
-                    outs[n][:, pl.ds(spot, HALF)] = total[n * 32 : (n + 1) * 32].astype(BF16)
-        else:
-            for n in range(X):
-                low = n & 1
-                upper = flag_ref[n] == 1
-                spot = pl.multiple_of(block * HALF, HALF)
-                for k in range(Y):
-                    mine = slice(k * 32 + low * 16, k * 32 + low * 16 + 16)
-                    chosen = jnp.where(upper, sums[1][mine], sums[0][mine])
-                    outs[n][k * 16 : (k + 1) * 16, pl.ds(spot, HALF)] = chosen.astype(BF16)
+    real, imag, posts, outs = refs[:G], refs[G : 2 * G], refs[2 * G : 3 * G], refs[3 * G :]
+    sums = []
+    for rows in (real, imag):
+        total = jnp.dot(posts[0][...], rows[0][...], preferred_element_type=F32)
+        for n in range(1, G):
+            total = total + jnp.dot(posts[n][...], rows[n][...], preferred_element_type=F32)
+        sums.append(total)
+    if part == 0:
+        for n in range(Y):
+            for half, total in enumerate(sums):
+                outs[n][:, half * HALF : (half + 1) * HALF] = total[n * 32 : (n + 1) * 32].astype(BF16)
+    else:
+        for n in range(X):
+            low = n & 1
+            upper = flag_ref[n] == 1
+            for k in range(Y):
+                mine = slice(k * 32 + low * 16, k * 32 + low * 16 + 16)
+                chosen = jnp.where(upper, sums[1][mine], sums[0][mine])
+                outs[n][k * 16 : (k + 1) * 16] = chosen.astype(BF16)
 
 
 def make_accum(part, flags, rows, posts):
-    shape = (32, NB * COLS) if part == 0 else (64, NB * HALF)
-    return local(
-        lambda *refs: accum_kernel(part, *refs), "weighted_sums", [(shape, BF16)] * 4, [flags],
-        [*rows, *posts], 8, flops=2 * G * ROWS * 128 * NB * COLS, size=(2 * G + 1) * MIB,
-    )
+    shape = (32, COLS) if part == 0 else (64, HALF)
+    rows = [pltpu.with_memory_space_constraint(value, pltpu.HBM) for value in rows]
+    return pl.pallas_call(
+        lambda *refs: accum_kernel(part, *refs),
+        grid_spec=pltpu.PrefetchScalarGridSpec(
+            num_scalar_prefetch=1,
+            grid=(NB,),
+            in_specs=[pl.BlockSpec((ROWS, HALF), lambda b, f: (0, 4 * b + part))] * G
+            + [pl.BlockSpec((ROWS, HALF), lambda b, f: (0, 4 * b + 2 + part))] * G
+            + [pl.BlockSpec((128, ROWS), lambda b, f: (0, 0))] * G,
+            out_specs=[pl.BlockSpec(shape, lambda b, f: (0, b))] * 4,
+        ),
+        out_shape=[pltpu.VMEM((shape[0], NB * shape[1]), BF16)] * 4,
+        cost_estimate=pl.CostEstimate(flops=0, bytes_accessed=0, transcendentals=0),
+        compiler_params=pltpu.CompilerParams(vmem_limit_bytes=16 * MIB),
+        name="weighted_sums",
+    )(flags, *rows, *rows, *posts)
 
 
 def added(values):
@@ -386,25 +422,26 @@
     gathered[0, 0] = own
     gathered[1, 0] = send(own, moves(dy=-1))
     gathered[3, 0] = send(own, moves(dy=1))
-    gathered[2, 0] = send(own, moves(dy=2))
     chunks = split_particles(member, own, particles, shift_ids, wedge, defocus, inv_sigma)
     got = {0: chunks[0]}
     got[2] = send(chunks[2], partners(2))
-    got[1] = send(chunks[1], partners(1))
-    table = make_table(member, geo)
+    gathered[2, 0] = send(own, moves(dy=2))
+    gathered[0, 1] = send(own, moves(dx=-1))
+    gathered[1, 1] = send(gathered[1, 0], moves(dx=-1))
+    gathered[3, 1] = send(gathered[3, 0], moves(dx=1))
+    table, geo = make_table(member, geo)
     rows, pens = {}, {}
     rows[0], pens[0] = make_rows(member, got[0], geo, table)
-    gathered[0, 1] = send(after(own, got[1]), moves(dx=-1))
-    gathered[1, 1] = send(after(gathered[1, 0], rows[0]), moves(dx=-1))
-    gathered[3, 1] = send(after(gathered[3, 0], rows[0]), moves(dx=1))
-    got[3] = send(after(chunks[3], rows[0]), partners(3))
-    rows[1], pens[1] = make_rows(member, got[1], geo, table)
-    gathered[2, 1] = send(after(gathered[2, 0], rows[1]), moves(dx=1))
-    rows[2], pens[2] = make_rows(member, after(got[2], rows[1]), geo, table)
+    wave = [got[2], *[gathered[at] for at in ((1, 0), (3, 0), (2, 0), (0, 1))], rows[0]]
+    rows[2], pens[2] = make_rows(member, after(got[2], *wave[1:]), geo, table)
+    got[3] = send(after(chunks[3], *wave), partners(3))
+    gathered[2, 1] = send(gathered[2, 0], moves(dx=1))
+    got[1] = send(after(chunks[1], *wave), partners(1))
+    rows[1], pens[1] = make_rows(member, after(got[1], rows[2]), geo, table)
     blocks = [gathered[ky, kx] for ky in range(Y) for kx in range(2)]
 
     early = make_scores([rows[n] for n in range(3)], [pens[n] for n in range(3)], blocks)
-    rows[3], pens[3] = make_rows(member, after(got[3], rows[2]), geo, table)
+    rows[3], pens[3] = make_rows(member, after(got[3], rows[1]), geo, table)
     late = make_scores([rows[3]], [pens[3]], blocks)
     parts = list(early) + list(late)
     arrived = [send(parts[n], partners(n)) for n in range(1, G)]

time: 132 us -> 113 us (0.86)
  local copies, waits for them, and re-layouts: 16.4 us -> 0.02 us
  Pallas kernels: 30.2 us -> 38.2 us
  waiting for transfers between devices: 35.1 us -> 29.2 us
  starting transfers between devices: 47.2 us -> 43 us
    unnamed x31 -> x8, local copies, waits for them, and re-layouts: 15.7 us -> 0.02 us
    pallas_call x0 -> x2, Pallas kernels: none -> 10.8 us  [make_accum(): pl.pallas_call(lambda *refs: accum_kernel(part, *refs), grid_spec=pltpu.P...]
    ppermute x31, waiting for transfers between devices: 35.1 us -> 29.2 us  [send(): return lax.ppermute(value, AXES, pairs)]
    ppermute x31, starting transfers between devices: 47.2 us -> 43 us  [send(): return lax.ppermute(value, AXES, pairs)]
    pallas_call x15 -> x13, Pallas kernels: 30.2 us -> 27.4 us  [local(): pl.pallas_call(kernel, in_specs=[SCALARS] * len(scalars) + [PLACED] * pla...]
  transfers between devices with their start and end apart: 31 -> 31, of which waited for: 12 -> 11; matrix products, arithmetic and copies ran while one was open for 0% -> 0% of each run, Pallas kernels for 17% -> 23%
where the time goes in v4:
time: 113 us; the launch traced here: 111 us
  starting transfers between devices  43 us (38%)
  Pallas kernels  38.2 us (34%)
  waiting for transfers between devices  29.2 us (26%)
    ppermute x31, starting transfers between devices, send(): return lax.ppermute(value, AXES, pairs)  43 us
    ppermute x31, waiting for transfers between devices, send(): return lax.ppermute(value, AXES, pairs)  29.2 us
    pallas_call x13, Pallas kernels, local(): pl.pallas_call(kernel, in_specs=[SCALARS] * len(scalars) + [PLACED] * pla...  27.4 us
    pallas_call x2, Pallas kernels, make_accum(): pl.pallas_call(lambda *refs: accum_kernel(part, *refs), grid_spec=pltpu.P...  10.8 us
  transfers between devices with their start and end apart: 31, of which 11 were waited for; matrix products, arithmetic and copies ran while one was open for 0% of the time, Pallas kernels for 23%

profile of v4, /device:TPU:2, one launch (start us, length us, event | category | flops | bytes accessed | tf_op | source)
XLA Modules:
  0.0 111.4 jit_solution(4476070183748868623)
XLA Ops:
  0.9 2.0 %split_particles.1 = (bf16[32,8576]{1,0:T(8,128)(2,1)S(1)}, bf16[32,8576]{1,0:T(8,128)(2,1)S(1)}, bf16[32,8576]{1,0:T(8,128)(2,1)S(1)}, bf16[32,8576]{1,0:T(8,128)(2,1)S(1)}) custom-call(s32[1]{0:T(128)} %bitcast.1.member_ref, bf16[32,32768]{1,0:T(8,128)(2,1)} %source.3, s32[8,32]{1,0:T(8,128)} %bitcast.4, s32[32,32]{1,0:T(8,128)} %wedge.1, f32[32,32]{1,0:T(8,128)} %focus.1, ...), custom_call_target="tpu_custom_call" | custom-call | tf_op jit(solution)/shard_map/split_particles/pallas_call | solution.py:97
  2.9 2.0 %collective-permute-start = (bf16[32,8576]{1,0:T(8,128)(2,1)S(1)}, bf16[32,8576]{1,0:T(8,128)(2,1)S(1)}, u32[]{:S(2)}, u32[]{:S(2)}) collective-permute-start(bf16[32,8576]{1,0:T(8,128)(2,1)S(1)} %get-tuple-element.52), channel_id=1, source_target_pairs={{0,2},{1,3},{2,0},{3,1},{4,6},{5,7},{6,4},{7,5},{8,10},{9,11},{10,... | collective-permute-start | bytes 1646600 | tf_op jit(solution)/shard_map/ppermute | solution.py:49
  4.9 3.0 %collective-permute-start.1 = (bf16[16,8192]{1,0:T(8,128)(2,1)S(1)}, bf16[16,8192]{1,0:T(8,128)(2,1)S(1)}, u32[]{:S(2)}, u32[]{:S(2)}) collective-permute-start(bf16[16,8192]{1,0:T(8,128)(2,1)S(1)} %own_references.1.after.refs_6_.refs_2_), channel_id=1, source_target_pairs={{0,192},{1,193},{2,194},{3,195},{4,196},{5,197},{6,198},{7,199},{8... | collective-permute-start | bytes 786440 | tf_op jit(solution)/shard_map/ppermute | solution.py:49
  7.9 2.2 %collective-permute-start.3 = (bf16[16,8192]{1,0:T(8,128)(2,1)S(1)}, bf16[16,8192]{1,0:T(8,128)(2,1)S(1)}, u32[]{:S(2)}, u32[]{:S(2)}) collective-permute-start(bf16[16,8192]{1,0:T(8,128)(2,1)S(1)} %own_references.1.after.refs_6_.refs_2_), channel_id=1, source_target_pairs={{0,128},{1,129},{2,130},{3,131},{4,132},{5,133},{6,134},{7,135},{8... | collective-permute-start | bytes 786440 | tf_op jit(solution)/shard_map/ppermute | solution.py:49
  10.7 5.5 %phase_table.1 = (bf16[256,8192]{1,0:T(8,128)(2,1)S(1)}, f32[4,8,1024]{2,1,0:T(8,128)S(1)}) custom-call(s32[1]{0:T(128)} %bitcast.1.member_ref, f32[16,8,1024]{2,1,0:T(8,128)} %constant.81.clone.geo_ref), custom_call_target="tpu_custom_call" | custom-call | tf_op jit(solution)/shard_map/phase_table/pallas_call | solution.py:97
  16.2 3.1 %shifted_rows.4 = (bf16[256,8192]{1,0:T(8,128)(2,1)S(1)}, bf16[32,4096]{1,0:T(8,128)(2,1)S(1)}) custom-call(s32[1]{0:T(128)} %bitcast.1.member_ref, bf16[32,8576]{1,0:T(8,128)(2,1)S(1)} %get-tuple-element.47.x_ref, f32[4,8,1024]{2,1,0:T(8,128)S(1)} %get-tuple-element.48.geo_ref, bf16[256,8192]{1,0:T(8,128)(2,1)S(1)} %get-tuple-element.49.table_ref), custom_call_target="tpu_custom_call" | custom-call | tf_op jit(solution)/shard_map/shifted_rows/pallas_call | solution.py:97
  19.4 2.9 %collective-permute-done.2.refs_12_.refs_8_ = bf16[16,8192]{1,0:T(8,128)(2,1)S(1)} collective-permute-done((bf16[16,8192]{1,0:T(8,128)(2,1)S(1)}, bf16[16,8192]{1,0:T(8,128)(2,1)S(1)}, u32[]{:S(2)}, u32[]{:S(2)}) %collective-permute-start.2) | collective-permute-done | bytes 262176 | tf_op jit(solution)/shard_map/ppermute | solution.py:49
  23.4 1.5 %collective-permute-start.8 = (bf16[16,8192]{1,0:T(8,128)(2,1)S(1)}, bf16[16,8192]{1,0:T(8,128)(2,1)S(1)}, u32[]{:S(2)}, u32[]{:S(2)}) collective-permute-start(bf16[16,8192]{1,0:T(8,128)(2,1)S(1)} %collective-permute-done.3.refs_10_.refs_6_), channel_id=1, source_target_pairs={{0,32},{1,33},{2,34},{3,35},{4,36},{5,37},{6,38},{7,39},{8,40},{9,... | collective-permute-start | bytes 786440 | tf_op jit(solution)/shard_map/ppermute | solution.py:49
  24.9 1.5 %collective-permute-start.9 = (bf16[16,8192]{1,0:T(8,128)(2,1)S(1)}, bf16[16,8192]{1,0:T(8,128)(2,1)S(1)}, u32[]{:S(2)}, u32[]{:S(2)}) collective-permute-start(bf16[16,8192]{1,0:T(8,128)(2,1)S(1)} %collective-permute-done.2.refs_12_.refs_8_), channel_id=1, source_target_pairs={{0,32},{1,33},{2,34},{3,35},{4,36},{5,37},{6,38},{7,39},{8,40},{9,... | collective-permute-start | bytes 786440 | tf_op jit(solution)/shard_map/ppermute | solution.py:49
  26.4 3.1 %shifted_rows.5 = (bf16[256,8192]{1,0:T(8,128)(2,1)S(1)}, bf16[32,4096]{1,0:T(8,128)(2,1)S(1)}) custom-call(s32[1]{0:T(128)} %bitcast.1.member_ref, bf16[32,8576]{1,0:T(8,128)(2,1)S(1)} %collective-permute-done.x_ref, f32[4,8,1024]{2,1,0:T(8,128)S(1)} %get-tuple-element.48.geo_ref, bf16[256,8192]{1,0:T(8,128)(2,1)S(1)} %get-tuple-element.49.table_ref), custom_call_target="tpu_custom_call" | custom-call | tf_op jit(solution)/shard_map/shifted_rows/pallas_call | solution.py:97
  29.5 3.2 %shifted_rows.6 = (bf16[256,8192]{1,0:T(8,128)(2,1)S(1)}, bf16[32,4096]{1,0:T(8,128)(2,1)S(1)}) custom-call(s32[1]{0:T(128)} %bitcast.1.member_ref, bf16[32,8576]{1,0:T(8,128)(2,1)S(1)} %collective-permute-done.5.x_ref, f32[4,8,1024]{2,1,0:T(8,128)S(1)} %get-tuple-element.48.geo_ref, bf16[256,8192]{1,0:T(8,128)(2,1)S(1)} %get-tuple-element.49.table_ref), custom_call_target="tpu_custom_call" | custom-call | tf_op jit(solution)/shard_map/shifted_rows/pallas_call | solution.py:97
  32.7 3.9 %collective-permute-done.6.x_ref = bf16[32,8576]{1,0:T(8,128)(2,1)S(1)} collective-permute-done((bf16[32,8576]{1,0:T(8,128)(2,1)S(1)}, bf16[32,8576]{1,0:T(8,128)(2,1)S(1)}, u32[]{:S(2)}, u32[]{:S(2)}) %collective-permute-start.6) | collective-permute-done | bytes 548896 | tf_op jit(solution)/shard_map/ppermute | solution.py:49
  36.7 3.1 %shifted_rows.7 = (bf16[256,8192]{1,0:T(8,128)(2,1)S(1)}, bf16[32,4096]{1,0:T(8,128)(2,1)S(1)}) custom-call(s32[1]{0:T(128)} %bitcast.1.member_ref, bf16[32,8576]{1,0:T(8,128)(2,1)S(1)} %collective-permute-done.6.x_ref, f32[4,8,1024]{2,1,0:T(8,128)S(1)} %get-tuple-element.48.geo_ref, bf16[256,8192]{1,0:T(8,128)(2,1)S(1)} %get-tuple-element.49.table_ref), custom_call_target="tpu_custom_call" | custom-call | tf_op jit(solution)/shard_map/shifted_rows/pallas_call | solution.py:97
  39.9 3.7 %partial_scores.2 = (f32[256,128]{1,0:T(8,128)S(1)}, f32[256,128]{1,0:T(8,128)S(1)}, f32[256,128]{1,0:T(8,128)S(1)}) custom-call(bf16[256,8192]{1,0:T(8,128)(2,1)S(1)} %get-tuple-element.50.refs_0_.refs_1_.refs_5_, bf16[256,8192]{1,0:T(8,128)(2,1)S(1)} %get-tuple-element.57.refs_1_.refs_2_.refs_6_, ...), custom_call_target="tpu_custom_call" | custom-call | tf_op jit(solution)/shard_map/partial_scores/pallas_call | solution.py:97
  44.7 1.5 %partial_scores.3 = f32[256,128]{1,0:T(8,128)S(1)} custom-call(bf16[256,8192]{1,0:T(8,128)(2,1)S(1)} %get-tuple-element.61.refs_0_.refs_4_.refs_8_, bf16[32,4096]{1,0:T(8,128)(2,1)S(1)} %get-tuple-element.68.refs_1_, bf16[16,8192]{1,0:T(8,128)(2,1)S(1)} %own_references.1.after.refs_6_.refs_2_, bf16[16,8192]{1,0:T(8,128)(2,1)S(1)} %collective-permute-done.4.refs_7_.refs_3_, ...), custom_call_target="tpu_custom_call" | custom-call | tf_op jit(solution)/shard_map/partial_scores/pallas_call | solution.py:97
  47.4 2.9 %collective-permute-done.11.refs_2_ = f32[256,128]{1,0:T(8,128)S(1)} collective-permute-done((f32[256,128]{1,0:T(8,128)S(1)}, f32[256,128]{1,0:T(8,128)S(1)}, u32[]{:S(2)}, u32[]{:S(2)}) %collective-permute-start.11) | collective-permute-done | bytes 131104 | tf_op jit(solution)/shard_map/ppermute | solution.py:49
  50.3 1.8 %collective-permute-done.12.refs_3_ = f32[256,128]{1,0:T(8,128)S(1)} collective-permute-done((f32[256,128]{1,0:T(8,128)S(1)}, f32[256,128]{1,0:T(8,128)S(1)}, u32[]{:S(2)}, u32[]{:S(2)}) %collective-permute-start.12) | collective-permute-done | bytes 131104 | tf_op jit(solution)/shard_map/ppermute | solution.py:49
  52.9 1.4 %collective-permute-start.14 = (bf16[128,256]{1,0:T(8,128)(2,1)S(1)}, bf16[128,256]{1,0:T(8,128)(2,1)S(1)}, u32[]{:S(2)}, u32[]{:S(2)}) collective-permute-start(bf16[128,256]{1,0:T(8,128)(2,1)S(1)} %posterior.1.refs_9_), channel_id=1, source_target_pairs={{0,2},{1,3},{2,0},{3,1},{4,6},{5,7},{6,4},{7,5},{8,10},{9,11},{10,... | collective-permute-start | bytes 196616 | tf_op jit(solution)/shard_map/ppermute | solution.py:49
  54.5 2.7 %collective-permute-done.14.refs_11_ = bf16[128,256]{1,0:T(8,128)(2,1)S(1)} collective-permute-done((bf16[128,256]{1,0:T(8,128)(2,1)S(1)}, bf16[128,256]{1,0:T(8,128)(2,1)S(1)}, u32[]{:S(2)}, u32[]{:S(2)}) %collective-permute-start.14) | collective-permute-done | bytes 65568 | tf_op jit(solution)/shard_map/ppermute | solution.py:49
  58.4 5.4 %weighted_sums.2 = (bf16[32,4096]{1,0:T(8,128)(2,1)S(1)}, bf16[32,4096]{1,0:T(8,128)(2,1)S(1)}, bf16[32,4096]{1,0:T(8,128)(2,1)S(1)}, bf16[32,4096]{1,0:T(8,128)(2,1)S(1)}) custom-call(s32[4]{0:T(128)S(1)} %and_select_fusion.refs_0_.flag_ref, bf16[256,8192]{1,0:T(8,128)(2,1)} %copy-done.1, bf16[256,8192]{1,0:T(8,128)(2,1)} %copy-done.3, ...), custom_call_target="tpu_custom_call" | custom-call | tf_op jit(solution)/shard_map/weighted_sums/pallas_call | solution.py:357
  63.9 1.8 %collective-permute-start.17 = (bf16[32,4096]{1,0:T(8,128)(2,1)S(1)}, bf16[32,4096]{1,0:T(8,128)(2,1)S(1)}, u32[]{:S(2)}, u32[]{:S(2)}) collective-permute-start(bf16[32,4096]{1,0:T(8,128)(2,1)S(1)} %get-tuple-element.71), channel_id=1, source_target_pairs={{0,128},{1,129},{2,130},{3,131},{4,132},{5,133},{6,134},{7,135},{8... | collective-permute-start | bytes 786440 | tf_op jit(solution)/shard_map/ppermute | solution.py:49
  67.1 5.4 %weighted_sums.3 = (bf16[64,2048]{1,0:T(8,128)(2,1)S(1)}, bf16[64,2048]{1,0:T(8,128)(2,1)S(1)}, bf16[64,2048]{1,0:T(8,128)(2,1)S(1)}, bf16[64,2048]{1,0:T(8,128)(2,1)S(1)}) custom-call(s32[4]{0:T(128)S(1)} %and_select_fusion.refs_0_.flag_ref, bf16[256,8192]{1,0:T(8,128)(2,1)} %copy-done.1, bf16[256,8192]{1,0:T(8,128)(2,1)} %copy-done.3, ...), custom_call_target="tpu_custom_call" | custom-call | tf_op jit(solution)/shard_map/weighted_sums/pallas_call | solution.py:357
  73.9 2.2 %collective-permute-start.23 = (bf16[64,2048]{1,0:T(8,128)(2,1)S(1)}, bf16[64,2048]{1,0:T(8,128)(2,1)S(1)}, u32[]{:S(2)}, u32[]{:S(2)}) collective-permute-start(bf16[64,2048]{1,0:T(8,128)(2,1)S(1)} %get-tuple-element.79), channel_id=1, source_target_pairs={{0,16},{1,17},{2,18},{3,19},{4,20},{5,21},{6,22},{7,23},{8,24},{9,... | collective-permute-start | bytes 786440 | tf_op jit(solution)/shard_map/ppermute | solution.py:49
  76.1 3.0 %collective-permute-done.16.refs_1_ = bf16[32,4096]{1,0:T(8,128)(2,1)S(1)} collective-permute-done((bf16[32,4096]{1,0:T(8,128)(2,1)S(1)}, bf16[32,4096]{1,0:T(8,128)(2,1)S(1)}, u32[]{:S(2)}, u32[]{:S(2)}) %collective-permute-start.16) | collective-permute-done | bytes 262176 | tf_op jit(solution)/shard_map/ppermute | solution.py:49
  81.9 3.3 %collective-permute-start.20 = (bf16[16,2048]{1,0:T(8,128)(2,1)S(1)}, bf16[16,2048]{1,0:T(8,128)(2,1)S(1)}, u32[]{:S(2)}, u32[]{:S(2)}) collective-permute-start(bf16[16,2048]{1,0:T(8,128)(2,1)S(1)} %get-tuple-element.75), channel_id=1, source_target_pairs={{0,16},{1,17},{2,18},{3,19},{4,20},{5,21},{6,22},{7,23},{8,24},{9,... | collective-permute-start | bytes 196616 | tf_op jit(solution)/shard_map/ppermute | solution.py:49
  85.2 4.5 %collective-permute-done.24.refs_3_ = bf16[64,2048]{1,0:T(8,128)(2,1)S(1)} collective-permute-done((bf16[64,2048]{1,0:T(8,128)(2,1)S(1)}, bf16[64,2048]{1,0:T(8,128)(2,1)S(1)}, u32[]{:S(2)}, u32[]{:S(2)}) %collective-permute-start.24) | collective-permute-done | bytes 262176 | tf_op jit(solution)/shard_map/ppermute | solution.py:49
  90.4 1.9 %collective-permute-start.26 = (bf16[16,2048]{1,0:T(8,128)(2,1)S(1)}, bf16[16,2048]{1,0:T(8,128)(2,1)S(1)}, u32[]{:S(2)}, u32[]{:S(2)}) collective-permute-start(bf16[16,2048]{1,0:T(8,128)(2,1)S(1)} %get-tuple-element.83), channel_id=1, source_target_pairs={{0,128},{1,129},{2,130},{3,131},{4,132},{5,133},{6,134},{7,135},{8... | collective-permute-start | bytes 196616 | tf_op jit(solution)/shard_map/ppermute | solution.py:49
  92.3 2.5 %collective-permute-start.27 = (bf16[16,2048]{1,0:T(8,128)(2,1)S(1)}, bf16[16,2048]{1,0:T(8,128)(2,1)S(1)}, u32[]{:S(2)}, u32[]{:S(2)}) collective-permute-start(bf16[16,2048]{1,0:T(8,128)(2,1)S(1)} %get-tuple-element.84), channel_id=1, source_target_pairs={{0,192},{1,193},{2,194},{3,195},{4,196},{5,197},{6,198},{7,199},{8... | collective-permute-start | bytes 196616 | tf_op jit(solution)/shard_map/ppermute | solution.py:49
  94.8 1.7 %collective-permute-done.25.refs_5_ = bf16[16,2048]{1,0:T(8,128)(2,1)S(1)} collective-permute-done((bf16[16,2048]{1,0:T(8,128)(2,1)S(1)}, bf16[16,2048]{1,0:T(8,128)(2,1)S(1)}, u32[]{:S(2)}, u32[]{:S(2)}) %collective-permute-start.25) | collective-permute-done | bytes 65568 | tf_op jit(solution)/shard_map/ppermute | solution.py:49
  97.1 5.8 %collective-permute-start.30 = (bf16[16,1024]{1,0:T(8,128)(2,1)S(1)}, bf16[16,1024]{1,0:T(8,128)(2,1)S(1)}, u32[]{:S(2)}, u32[]{:S(2)}) collective-permute-start(bf16[16,1024]{1,0:T(8,128)(2,1)S(1)} %get-tuple-element.88), channel_id=1, source_target_pairs={{0,12},{1,13},{2,14},{3,15},{4,0},{5,1},{6,2},{7,3},{8,4},{9,5},{1... | collective-permute-start | bytes 98312 | tf_op jit(solution)/shard_map/ppermute | solution.py:49
  104.0 2.8 %collective-permute-start.28 = (bf16[16,1024]{1,0:T(8,128)(2,1)S(1)}, bf16[16,1024]{1,0:T(8,128)(2,1)S(1)}, u32[]{:S(2)}, u32[]{:S(2)}) collective-permute-start(bf16[16,1024]{1,0:T(8,128)(2,1)S(1)} %get-tuple-element.86), channel_id=1, source_target_pairs={{0,4},{1,5},{2,6},{3,7},{4,8},{5,9},{6,10},{7,11},{8,12},{9,13},{1... | collective-permute-start | bytes 98312 | tf_op jit(solution)/shard_map/ppermute | solution.py:49
  106.7 4.0 %collective-permute-done.29 = bf16[16,1024]{1,0:T(8,128)(2,1)S(1)} collective-permute-done((bf16[16,1024]{1,0:T(8,128)(2,1)S(1)}, bf16[16,1024]{1,0:T(8,128)(2,1)S(1)}, u32[]{:S(2)}, u32[]{:S(2)}) %collective-permute-start.29) | collective-permute-done | bytes 32800 | tf_op jit(solution)/shard_map/ppermute | solution.py:49
  (55 shorter events, 15.6 us)
Async XLA Ops:
  2.9 19.3 %collective-permute-start = (bf16[32,8576]{1,0:T(8,128)(2,1)S(1)}, bf16[32,8576]{1,0:T(8,128)(2,1)S(1)}, u32[]{:S(2)}, u32[]{:S(2)}) collective-permute-start(bf16[32,8576]{1,0:T(8,128)(2,1)S(1)} %get-tuple-element.52), channel_id=1, source_target_pairs={{0,2},{1,3},{2,0},{3,1},{4,6},{5,7},{6,4},{7,5},{8,10},{9,11},{10,... | collective-permute-start | bytes 1646600 | tf_op jit(solution)/shard_map/ppermute | solution.py:49
  4.9 14.5 %collective-permute-start.1 = (bf16[16,8192]{1,0:T(8,128)(2,1)S(1)}, bf16[16,8192]{1,0:T(8,128)(2,1)S(1)}, u32[]{:S(2)}, u32[]{:S(2)}) collective-permute-start(bf16[16,8192]{1,0:T(8,128)(2,1)S(1)} %own_references.1.after.refs_6_.refs_2_), channel_id=1, source_target_pairs={{0,192},{1,193},{2,194},{3,195},{4,196},{5,197},{6,198},{7,199},{8... | collective-permute-start | bytes 786440 | tf_op jit(solution)/shard_map/ppermute | solution.py:49
  7.9 14.3 %collective-permute-start.2 = (bf16[16,8192]{1,0:T(8,128)(2,1)S(1)}, bf16[16,8192]{1,0:T(8,128)(2,1)S(1)}, u32[]{:S(2)}, u32[]{:S(2)}) collective-permute-start(bf16[16,8192]{1,0:T(8,128)(2,1)S(1)} %own_references.1.after.refs_6_.refs_2_), channel_id=1, source_target_pairs={{0,64},{1,65},{2,66},{3,67},{4,68},{5,69},{6,70},{7,71},{8,72},{9,... | collective-permute-start | bytes 786440 | tf_op jit(solution)/shard_map/ppermute | solution.py:49
  7.9 14.3 %collective-permute-start.3 = (bf16[16,8192]{1,0:T(8,128)(2,1)S(1)}, bf16[16,8192]{1,0:T(8,128)(2,1)S(1)}, u32[]{:S(2)}, u32[]{:S(2)}) collective-permute-start(bf16[16,8192]{1,0:T(8,128)(2,1)S(1)} %own_references.1.after.refs_6_.refs_2_), channel_id=1, source_target_pairs={{0,128},{1,129},{2,130},{3,131},{4,132},{5,133},{6,134},{7,135},{8... | collective-permute-start | bytes 786440 | tf_op jit(solution)/shard_map/ppermute | solution.py:49
  10.1 12.1 %collective-permute-start.4 = (bf16[16,8192]{1,0:T(8,128)(2,1)S(1)}, bf16[16,8192]{1,0:T(8,128)(2,1)S(1)}, u32[]{:S(2)}, u32[]{:S(2)}) collective-permute-start(bf16[16,8192]{1,0:T(8,128)(2,1)S(1)} %own_references.1.after.refs_6_.refs_2_), channel_id=1, source_target_pairs={{0,48},{1,49},{2,50},{3,51},{4,52},{5,53},{6,54},{7,55},{8,56},{9,... | collective-permute-start | bytes 786440 | tf_op jit(solution)/shard_map/ppermute | solution.py:49
  19.4 20.5 %copy-start.1 = (bf16[256,8192]{1,0:T(8,128)(2,1)}, bf16[256,8192]{1,0:T(8,128)(2,1)S(1)}, u32[]{:S(2)}) copy-start(bf16[256,8192]{1,0:T(8,128)(2,1)S(1)} %get-tuple-element.50.refs_0_.refs_1_.refs_5_) | copy-start | bytes 12582916
  22.3 7.3 %collective-permute-start.5 = (bf16[32,8576]{1,0:T(8,128)(2,1)S(1)}, bf16[32,8576]{1,0:T(8,128)(2,1)S(1)}, u32[]{:S(2)}, u32[]{:S(2)}) collective-permute-start(bf16[32,8576]{1,0:T(8,128)(2,1)S(1)} %get-tuple-element.53), channel_id=1, source_target_pairs={{0,1},{1,0},{2,3},{3,2},{4,5},{5,4},{6,7},{7,6},{8,9},{9,8},{10,11... | collective-permute-start | bytes 1646600 | tf_op jit(solution)/shard_map/ppermute | solution.py:49
  22.4 14.3 %collective-permute-start.6 = (bf16[32,8576]{1,0:T(8,128)(2,1)S(1)}, bf16[32,8576]{1,0:T(8,128)(2,1)S(1)}, u32[]{:S(2)}, u32[]{:S(2)}) collective-permute-start(bf16[32,8576]{1,0:T(8,128)(2,1)S(1)} %get-tuple-element.59), channel_id=1, source_target_pairs={{0,3},{1,2},{2,1},{3,0},{4,7},{5,6},{6,5},{7,4},{8,11},{9,10},{10,... | collective-permute-start | bytes 1646600 | tf_op jit(solution)/shard_map/ppermute | solution.py:49
  22.9 17.0 %collective-permute-start.7 = (bf16[16,8192]{1,0:T(8,128)(2,1)S(1)}, bf16[16,8192]{1,0:T(8,128)(2,1)S(1)}, u32[]{:S(2)}, u32[]{:S(2)}) collective-permute-start(bf16[16,8192]{1,0:T(8,128)(2,1)S(1)} %collective-permute-done.1.refs_8_.refs_4_), channel_id=1, source_target_pairs={{0,48},{1,49},{2,50},{3,51},{4,52},{5,53},{6,54},{7,55},{8,56},{9,... | collective-permute-start | bytes 786440 | tf_op jit(solution)/shard_map/ppermute | solution.py:49
  23.4 16.4 %collective-permute-start.8 = (bf16[16,8192]{1,0:T(8,128)(2,1)S(1)}, bf16[16,8192]{1,0:T(8,128)(2,1)S(1)}, u32[]{:S(2)}, u32[]{:S(2)}) collective-permute-start(bf16[16,8192]{1,0:T(8,128)(2,1)S(1)} %collective-permute-done.3.refs_10_.refs_6_), channel_id=1, source_target_pairs={{0,32},{1,33},{2,34},{3,35},{4,36},{5,37},{6,38},{7,39},{8,40},{9,... | collective-permute-start | bytes 786440 | tf_op jit(solution)/shard_map/ppermute | solution.py:49
  24.9 15.0 %collective-permute-start.9 = (bf16[16,8192]{1,0:T(8,128)(2,1)S(1)}, bf16[16,8192]{1,0:T(8,128)(2,1)S(1)}, u32[]{:S(2)}, u32[]{:S(2)}) collective-permute-start(bf16[16,8192]{1,0:T(8,128)(2,1)S(1)} %collective-permute-done.2.refs_12_.refs_8_), channel_id=1, source_target_pairs={{0,32},{1,33},{2,34},{3,35},{4,36},{5,37},{6,38},{7,39},{8,40},{9,... | collective-permute-start | bytes 786440 | tf_op jit(solution)/shard_map/ppermute | solution.py:49
  43.6 3.8 %collective-permute-start.10 = (f32[256,128]{1,0:T(8,128)S(1)}, f32[256,128]{1,0:T(8,128)S(1)}, u32[]{:S(2)}, u32[]{:S(2)}) collective-permute-start(f32[256,128]{1,0:T(8,128)S(1)} %get-tuple-element.66), channel_id=1, source_target_pairs={{0,1},{1,0},{2,3},{3,2},{4,5},{5,4},{6,7},{7,6},{8,9},{9,8},{10,11... | collective-permute-start | bytes 393224 | tf_op jit(solution)/shard_map/ppermute | solution.py:49
  44.4 6.0 %collective-permute-start.11 = (f32[256,128]{1,0:T(8,128)S(1)}, f32[256,128]{1,0:T(8,128)S(1)}, u32[]{:S(2)}, u32[]{:S(2)}) collective-permute-start(f32[256,128]{1,0:T(8,128)S(1)} %get-tuple-element.67), channel_id=1, source_target_pairs={{0,2},{1,3},{2,0},{3,1},{4,6},{5,7},{6,4},{7,5},{8,10},{9,11},{10,... | collective-permute-start | bytes 393224 | tf_op jit(solution)/shard_map/ppermute | solution.py:49
  46.2 5.9 %collective-permute-start.12 = (f32[256,128]{1,0:T(8,128)S(1)}, f32[256,128]{1,0:T(8,128)S(1)}, u32[]{:S(2)}, u32[]{:S(2)}) collective-permute-start(f32[256,128]{1,0:T(8,128)S(1)} %partial_scores.3), channel_id=1, source_target_pairs={{0,3},{1,2},{2,1},{3,0},{4,7},{5,6},{6,5},{7,4},{8,11},{9,10},{10,... | collective-permute-start | bytes 393224 | tf_op jit(solution)/shard_map/ppermute | solution.py:49
  52.5 2.0 %collective-permute-start.13 = (bf16[128,256]{1,0:T(8,128)(2,1)S(1)}, bf16[128,256]{1,0:T(8,128)(2,1)S(1)}, u32[]{:S(2)}, u32[]{:S(2)}) collective-permute-start(bf16[128,256]{1,0:T(8,128)(2,1)S(1)} %posterior.1.refs_9_), channel_id=1, source_target_pairs={{0,1},{1,0},{2,3},{3,2},{4,5},{5,4},{6,7},{7,6},{8,9},{9,8},{10,11... | collective-permute-start | bytes 196616 | tf_op jit(solution)/shard_map/ppermute | solution.py:49
  52.9 4.3 %collective-permute-start.14 = (bf16[128,256]{1,0:T(8,128)(2,1)S(1)}, bf16[128,256]{1,0:T(8,128)(2,1)S(1)}, u32[]{:S(2)}, u32[]{:S(2)}) collective-permute-start(bf16[128,256]{1,0:T(8,128)(2,1)S(1)} %posterior.1.refs_9_), channel_id=1, source_target_pairs={{0,2},{1,3},{2,0},{3,1},{4,6},{5,7},{6,4},{7,5},{8,10},{9,11},{10,... | collective-permute-start | bytes 196616 | tf_op jit(solution)/shard_map/ppermute | solution.py:49
  54.3 4.1 %collective-permute-start.15 = (bf16[128,256]{1,0:T(8,128)(2,1)S(1)}, bf16[128,256]{1,0:T(8,128)(2,1)S(1)}, u32[]{:S(2)}, u32[]{:S(2)}) collective-permute-start(bf16[128,256]{1,0:T(8,128)(2,1)S(1)} %posterior.1.refs_9_), channel_id=1, source_target_pairs={{0,3},{1,2},{2,1},{3,0},{4,7},{5,6},{6,5},{7,4},{8,11},{9,10},{10,... | collective-permute-start | bytes 196616 | tf_op jit(solution)/shard_map/ppermute | solution.py:49
  63.8 15.3 %collective-permute-start.16 = (bf16[32,4096]{1,0:T(8,128)(2,1)S(1)}, bf16[32,4096]{1,0:T(8,128)(2,1)S(1)}, u32[]{:S(2)}, u32[]{:S(2)}) collective-permute-start(bf16[32,4096]{1,0:T(8,128)(2,1)S(1)} %get-tuple-element.70), channel_id=1, source_target_pairs={{0,64},{1,65},{2,66},{3,67},{4,68},{5,69},{6,70},{7,71},{8,72},{9,... | collective-permute-start | bytes 786440 | tf_op jit(solution)/shard_map/ppermute | solution.py:49
  63.9 16.5 %collective-permute-start.17 = (bf16[32,4096]{1,0:T(8,128)(2,1)S(1)}, bf16[32,4096]{1,0:T(8,128)(2,1)S(1)}, u32[]{:S(2)}, u32[]{:S(2)}) collective-permute-start(bf16[32,4096]{1,0:T(8,128)(2,1)S(1)} %get-tuple-element.71), channel_id=1, source_target_pairs={{0,128},{1,129},{2,130},{3,131},{4,132},{5,133},{6,134},{7,135},{8... | collective-permute-start | bytes 786440 | tf_op jit(solution)/shard_map/ppermute | solution.py:49
  65.7 14.7 %collective-permute-start.18 = (bf16[32,4096]{1,0:T(8,128)(2,1)S(1)}, bf16[32,4096]{1,0:T(8,128)(2,1)S(1)}, u32[]{:S(2)}, u32[]{:S(2)}) collective-permute-start(bf16[32,4096]{1,0:T(8,128)(2,1)S(1)} %get-tuple-element.72), channel_id=1, source_target_pairs={{0,192},{1,193},{2,194},{3,195},{4,196},{5,197},{6,198},{7,199},{8... | collective-permute-start | bytes 786440 | tf_op jit(solution)/shard_map/ppermute | solution.py:49
  72.5 12.7 %collective-permute-start.22 = (bf16[64,2048]{1,0:T(8,128)(2,1)S(1)}, bf16[64,2048]{1,0:T(8,128)(2,1)S(1)}, u32[]{:S(2)}, u32[]{:S(2)}) collective-permute-start(bf16[64,2048]{1,0:T(8,128)(2,1)S(1)} %get-tuple-element.78), channel_id=1, source_target_pairs={{0,32},{1,33},{2,34},{3,35},{4,36},{5,37},{6,38},{7,39},{8,40},{9,... | collective-permute-start | bytes 786440 | tf_op jit(solution)/shard_map/ppermute | solution.py:49
  73.9 11.3 %collective-permute-start.23 = (bf16[64,2048]{1,0:T(8,128)(2,1)S(1)}, bf16[64,2048]{1,0:T(8,128)(2,1)S(1)}, u32[]{:S(2)}, u32[]{:S(2)}) collective-permute-start(bf16[64,2048]{1,0:T(8,128)(2,1)S(1)} %get-tuple-element.79), channel_id=1, source_target_pairs={{0,16},{1,17},{2,18},{3,19},{4,20},{5,21},{6,22},{7,23},{8,24},{9,... | collective-permute-start | bytes 786440 | tf_op jit(solution)/shard_map/ppermute | solution.py:49
  79.0 10.7 %collective-permute-start.24 = (bf16[64,2048]{1,0:T(8,128)(2,1)S(1)}, bf16[64,2048]{1,0:T(8,128)(2,1)S(1)}, u32[]{:S(2)}, u32[]{:S(2)}) collective-permute-start(bf16[64,2048]{1,0:T(8,128)(2,1)S(1)} %get-tuple-element.80), channel_id=1, source_target_pairs={{0,48},{1,49},{2,50},{3,51},{4,52},{5,53},{6,54},{7,55},{8,56},{9,... | collective-permute-start | bytes 786440 | tf_op jit(solution)/shard_map/ppermute | solution.py:49
  81.1 11.2 %collective-permute-start.19 = (bf16[16,2048]{1,0:T(8,128)(2,1)S(1)}, bf16[16,2048]{1,0:T(8,128)(2,1)S(1)}, u32[]{:S(2)}, u32[]{:S(2)}) collective-permute-start(bf16[16,2048]{1,0:T(8,128)(2,1)S(1)} %get-tuple-element.74), channel_id=1, source_target_pairs={{0,32},{1,33},{2,34},{3,35},{4,36},{5,37},{6,38},{7,39},{8,40},{9,... | collective-permute-start | bytes 196616 | tf_op jit(solution)/shard_map/ppermute | solution.py:49
  81.9 13.0 %collective-permute-start.20 = (bf16[16,2048]{1,0:T(8,128)(2,1)S(1)}, bf16[16,2048]{1,0:T(8,128)(2,1)S(1)}, u32[]{:S(2)}, u32[]{:S(2)}) collective-permute-start(bf16[16,2048]{1,0:T(8,128)(2,1)S(1)} %get-tuple-element.75), channel_id=1, source_target_pairs={{0,16},{1,17},{2,18},{3,19},{4,20},{5,21},{6,22},{7,23},{8,24},{9,... | collective-permute-start | bytes 196616 | tf_op jit(solution)/shard_map/ppermute | solution.py:49
  85.2 9.7 %collective-permute-start.21 = (bf16[16,2048]{1,0:T(8,128)(2,1)S(1)}, bf16[16,2048]{1,0:T(8,128)(2,1)S(1)}, u32[]{:S(2)}, u32[]{:S(2)}) collective-permute-start(bf16[16,2048]{1,0:T(8,128)(2,1)S(1)} %get-tuple-element.76), channel_id=1, source_target_pairs={{0,48},{1,49},{2,50},{3,51},{4,52},{5,53},{6,54},{7,55},{8,56},{9,... | collective-permute-start | bytes 196616 | tf_op jit(solution)/shard_map/ppermute | solution.py:49
  89.9 6.6 %collective-permute-start.25 = (bf16[16,2048]{1,0:T(8,128)(2,1)S(1)}, bf16[16,2048]{1,0:T(8,128)(2,1)S(1)}, u32[]{:S(2)}, u32[]{:S(2)}) collective-permute-start(bf16[16,2048]{1,0:T(8,128)(2,1)S(1)} %get-tuple-element.82), channel_id=1, source_target_pairs={{0,64},{1,65},{2,66},{3,67},{4,68},{5,69},{6,70},{7,71},{8,72},{9,... | collective-permute-start | bytes 196616 | tf_op jit(solution)/shard_map/ppermute | solution.py:49
  90.4 6.1 %collective-permute-start.26 = (bf16[16,2048]{1,0:T(8,128)(2,1)S(1)}, bf16[16,2048]{1,0:T(8,128)(2,1)S(1)}, u32[]{:S(2)}, u32[]{:S(2)}) collective-permute-start(bf16[16,2048]{1,0:T(8,128)(2,1)S(1)} %get-tuple-element.83), channel_id=1, source_target_pairs={{0,128},{1,129},{2,130},{3,131},{4,132},{5,133},{6,134},{7,135},{8... | collective-permute-start | bytes 196616 | tf_op jit(solution)/shard_map/ppermute | solution.py:49
  92.3 4.7 %collective-permute-start.27 = (bf16[16,2048]{1,0:T(8,128)(2,1)S(1)}, bf16[16,2048]{1,0:T(8,128)(2,1)S(1)}, u32[]{:S(2)}, u32[]{:S(2)}) collective-permute-start(bf16[16,2048]{1,0:T(8,128)(2,1)S(1)} %get-tuple-element.84), channel_id=1, source_target_pairs={{0,192},{1,193},{2,194},{3,195},{4,196},{5,197},{6,198},{7,199},{8... | collective-permute-start | bytes 196616 | tf_op jit(solution)/shard_map/ppermute | solution.py:49
  97.1 9.7 %collective-permute-start.30 = (bf16[16,1024]{1,0:T(8,128)(2,1)S(1)}, bf16[16,1024]{1,0:T(8,128)(2,1)S(1)}, u32[]{:S(2)}, u32[]{:S(2)}) collective-permute-start(bf16[16,1024]{1,0:T(8,128)(2,1)S(1)} %get-tuple-element.88), channel_id=1, source_target_pairs={{0,12},{1,13},{2,14},{3,15},{4,0},{5,1},{6,2},{7,3},{8,4},{9,5},{1... | collective-permute-start | bytes 98312 | tf_op jit(solution)/shard_map/ppermute | solution.py:49
  102.9 7.8 %collective-permute-start.29 = (bf16[16,1024]{1,0:T(8,128)(2,1)S(1)}, bf16[16,1024]{1,0:T(8,128)(2,1)S(1)}, u32[]{:S(2)}, u32[]{:S(2)}) collective-permute-start(bf16[16,1024]{1,0:T(8,128)(2,1)S(1)} %get-tuple-element.87), channel_id=1, source_target_pairs={{0,8},{1,9},{2,10},{3,11},{4,12},{5,13},{6,14},{7,15},{8,0},{9,1},... | collective-permute-start | bytes 98312 | tf_op jit(solution)/shard_map/ppermute | solution.py:49
  104.0 6.8 %collective-permute-start.28 = (bf16[16,1024]{1,0:T(8,128)(2,1)S(1)}, bf16[16,1024]{1,0:T(8,128)(2,1)S(1)}, u32[]{:S(2)}, u32[]{:S(2)}) collective-permute-start(bf16[16,1024]{1,0:T(8,128)(2,1)S(1)} %get-tuple-element.86), channel_id=1, source_target_pairs={{0,4},{1,5},{2,6},{3,7},{4,8},{5,9},{6,10},{7,11},{8,12},{9,13},{1... | collective-permute-start | bytes 98312 | tf_op jit(solution)/shard_map/ppermute | solution.py:49
  (3 other events, 26.1 us)

commit v5 on v4

--- a/solution.py
+++ b/solution.py
@@ -93,7 +93,7 @@
 PLACED = pl.BlockSpec(memory_space=pl.ANY)
 
 
-def local(kernel, name, outs, scalars, arrays, limit, flops=0, size=0, placed=0, scratch=()):
+def local(kernel, name, outs, scalars, arrays, limit, placed=0, scratch=()):
     return pl.pallas_call(
         kernel,
         in_specs=[SCALARS] * len(scalars) + [PLACED] * placed + [WHOLE] * (len(arrays) - placed),
@@ -103,7 +103,11 @@
         cost_estimate=pl.CostEstimate(flops=0, bytes_accessed=0, transcendentals=0),
         compiler_params=pltpu.CompilerParams(vmem_limit_bytes=limit * MIB),
         name=name,
-    )(*scalars, *[pltpu.with_memory_space_constraint(value, pltpu.HBM) for value in arrays[:placed]], *[held(value) for value in arrays[placed:]])
+    )(
+        *scalars,
+        *[pltpu.with_memory_space_constraint(value, pltpu.HBM) for value in arrays[:placed]],
+        *[held(value) for value in arrays[placed:]],
+    )
 
 
 def table_kernel(member_ref, geo_ref, out_ref, picked_ref, sems):
@@ -172,7 +176,7 @@
 
 def own_columns(member, refs):
     (own,) = local(
-        own_kernel, "own_references", [((16, WIDTH), BF16)], [member], [refs], 4, size=MIB // 2,
+        own_kernel, "own_references", [((16, WIDTH), BF16)], [member], [refs], 4,
         placed=1, scratch=[pltpu.SemaphoreType.DMA((2 * NB,))],
     )
     return own
@@ -279,7 +283,7 @@
 def make_rows(member, x, geo, table):
     return local(
         rows_kernel, "shifted_rows", [((ROWS, WIDTH), BF16), ((P_DEV, NB * COLS), BF16)], [member],
-        [x, geo, table], 12, flops=2 * ROWS * 256 * WIDTH, size=9 * MIB,
+        [x, geo, table], 12,
     )
 
 
@@ -307,7 +311,7 @@
     count = len(rows)
     return local(
         lambda *refs: scores_kernel(count, *refs), "partial_scores", [((ROWS, 128), F32)] * count, [],
-        [*rows, *pens, *blocks], 12, flops=2 * count * ROWS * 128 * WIDTH, size=(4 * count + 2) * MIB,
+        [*rows, *pens, *blocks], 12,
     )
 
 
@@ -325,50 +329,52 @@
 
 
 def make_posterior(parts):
-    (out,) = local(posterior_kernel, "posterior", [((128, ROWS), BF16)], [], parts, 4, size=MIB // 2)
+    (out,) = local(posterior_kernel, "posterior", [((128, ROWS), BF16)], [], parts, 4)
     return out
 
 
-def accum_kernel(part, flag_ref, *refs):
-    real, imag, posts, outs = refs[:G], refs[G : 2 * G], refs[2 * G : 3 * G], refs[3 * G :]
-    sums = []
-    for rows in (real, imag):
-        total = jnp.dot(posts[0][...], rows[0][...], preferred_element_type=F32)
-        for n in range(1, G):
-            total = total + jnp.dot(posts[n][...], rows[n][...], preferred_element_type=F32)
-        sums.append(total)
-    if part == 0:
-        for n in range(Y):
-            for half, total in enumerate(sums):
-                outs[n][:, half * HALF : (half + 1) * HALF] = total[n * 32 : (n + 1) * 32].astype(BF16)
-    else:
-        for n in range(X):
-            low = n & 1
-            upper = flag_ref[n] == 1
-            for k in range(Y):
-                mine = slice(k * 32 + low * 16, k * 32 + low * 16 + 16)
-                chosen = jnp.where(upper, sums[1][mine], sums[0][mine])
-                outs[n][k * 16 : (k + 1) * 16] = chosen.astype(BF16)
-
-
-def make_accum(part, flags, rows, posts):
-    shape = (32, COLS) if part == 0 else (64, HALF)
+def accum_kernel(flag_ref, *refs):
+    rows, posts, outs = refs[:G], refs[G : 2 * G], refs[2 * G :]
+    for part in range(2):
+        sums = []
+        for half in range(2):
+            lanes = slice(half * COLS + part * HALF, half * COLS + (part + 1) * HALF)
+            total = jnp.dot(posts[0][...], rows[0][:, lanes], preferred_element_type=F32)
+            for n in range(1, G):
+                total = total + jnp.dot(posts[n][...], rows[n][:, lanes], preferred_element_type=F32)
+            sums.append(total)
+        if part == 0:
+            for n in range(Y):
+                for half, total in enumerate(sums):
+                    outs[n][:, half * HALF : (half + 1) * HALF] = total[n * 32 : (n + 1) * 32].astype(BF16)
+        else:
+            for n in range(X):
+                low = n & 1
+                upper = flag_ref[n] == 1
+                for k in range(Y):
+                    mine = slice(k * 32 + low * 16, k * 32 + low * 16 + 16)
+                    chosen = jnp.where(upper, sums[1][mine], sums[0][mine])
+                    outs[Y + n][k * 16 : (k + 1) * 16] = chosen.astype(BF16)
+
+
+def make_accum(flags, rows, posts):
     rows = [pltpu.with_memory_space_constraint(value, pltpu.HBM) for value in rows]
-    return pl.pallas_call(
-        lambda *refs: accum_kernel(part, *refs),
+    shapes = [(32, COLS)] * Y + [(64, HALF)] * X
+    outs = pl.pallas_call(
+        accum_kernel,
         grid_spec=pltpu.PrefetchScalarGridSpec(
             num_scalar_prefetch=1,
             grid=(NB,),
-            in_specs=[pl.BlockSpec((ROWS, HALF), lambda b, f: (0, 4 * b + part))] * G
-            + [pl.BlockSpec((ROWS, HALF), lambda b, f: (0, 4 * b + 2 + part))] * G
+            in_specs=[pl.BlockSpec((ROWS, 2 * COLS), lambda b, f: (0, b))] * G
             + [pl.BlockSpec((128, ROWS), lambda b, f: (0, 0))] * G,
-            out_specs=[pl.BlockSpec(shape, lambda b, f: (0, b))] * 4,
+            out_specs=[pl.BlockSpec(shape, lambda b, f: (0, b)) for shape in shapes],
         ),
-        out_shape=[pltpu.VMEM((shape[0], NB * shape[1]), BF16)] * 4,
+        out_shape=[pltpu.VMEM((shape[0], NB * shape[1]), BF16) for shape in shapes],
         cost_estimate=pl.CostEstimate(flops=0, bytes_accessed=0, transcendentals=0),
         compiler_params=pltpu.CompilerParams(vmem_limit_bytes=16 * MIB),
         name="weighted_sums",
-    )(flags, *rows, *rows, *posts)
+    )(flags, *rows, *posts)
+    return outs[:Y], outs[Y:]
 
 
 def added(values):
@@ -425,40 +431,43 @@
     chunks = split_particles(member, own, particles, shift_ids, wedge, defocus, inv_sigma)
     got = {0: chunks[0]}
     got[2] = send(chunks[2], partners(2))
+    got[1] = send(chunks[1], partners(1))
     gathered[2, 0] = send(own, moves(dy=2))
-    gathered[0, 1] = send(own, moves(dx=-1))
-    gathered[1, 1] = send(gathered[1, 0], moves(dx=-1))
-    gathered[3, 1] = send(gathered[3, 0], moves(dx=1))
     table, geo = make_table(member, geo)
+    wave = [got[1], got[2], gathered[1, 0], gathered[3, 0], gathered[2, 0], table]
+    gathered[0, 1] = send(after(own, *wave), moves(dx=-1))
+    gathered[1, 1] = send(after(gathered[1, 0], *wave), moves(dx=-1))
+    gathered[3, 1] = send(after(gathered[3, 0], *wave), moves(dx=1))
+    gathered[2, 1] = send(after(gathered[2, 0], *wave), moves(dx=1))
+    got[3] = send(after(chunks[3], *wave), partners(3))
     rows, pens = {}, {}
-    rows[0], pens[0] = make_rows(member, got[0], geo, table)
-    wave = [got[2], *[gathered[at] for at in ((1, 0), (3, 0), (2, 0), (0, 1))], rows[0]]
-    rows[2], pens[2] = make_rows(member, after(got[2], *wave[1:]), geo, table)
-    got[3] = send(after(chunks[3], *wave), partners(3))
-    gathered[2, 1] = send(gathered[2, 0], moves(dx=1))
-    got[1] = send(after(chunks[1], *wave), partners(1))
-    rows[1], pens[1] = make_rows(member, after(got[1], rows[2]), geo, table)
+    rows[0], pens[0] = make_rows(member, after(got[0], *wave), geo, table)
+    rows[1], pens[1] = make_rows(member, after(got[1], rows[0]), geo, table)
+    rows[2], pens[2] = make_rows(member, after(got[2], rows[1]), geo, table)
+    rows[3], pens[3] = make_rows(member, after(got[3], rows[2]), geo, table)
     blocks = [gathered[ky, kx] for ky in range(Y) for kx in range(2)]
 
-    early = make_scores([rows[n] for n in range(3)], [pens[n] for n in range(3)], blocks)
-    rows[3], pens[3] = make_rows(member, after(got[3], rows[1]), geo, table)
-    late = make_scores([rows[3]], [pens[3]], blocks)
-    parts = list(early) + list(late)
+    rows = [rows[n] for n in range(G)]
+    pens = [pens[n] for n in range(G)]
+    parts = make_scores(rows, pens, blocks)
     arrived = [send(parts[n], partners(n)) for n in range(1, G)]
-    posterior = make_posterior([parts[0]] + arrived)
+    posterior = make_posterior([parts[0], *arrived])
     posts = [posterior] + [send(posterior, partners(n)) for n in range(1, G)]
-    rows = [rows[n] for n in range(G)]
-
-    first = make_accum(0, flags, rows, posts)
+
+    first, second = make_accum(flags, rows, posts)
     first = [first[0]] + [send(first[n], moves(dy=n)) for n in range(1, Y)]
-    second = make_accum(1, flags, rows, posts)
-    second = [second[0]] + [send(second[n], moves(dx=n)) for n in range(1, X)]
-    first = local(first_kernel, "first_sums", PIECES, [flags], first, 4, size=MIB)
+    second = [
+        second[0],
+        send(second[1], moves(dx=1)),
+        send(after(second[2], first[1]), moves(dx=2)),
+        send(second[3], moves(dx=3)),
+    ]
+    first = local(first_kernel, "first_sums", PIECES, [flags], first, 4)
     first = [first[0]] + [send(first[n], moves(dx=n)) for n in range(1, X)]
-    second = local(second_kernel, "second_sums", PIECES, [], second, 4, size=MIB)
+    second = local(second_kernel, "second_sums", PIECES, [], second, 4)
     second = [second[0]] + [send(second[n], moves(dy=n)) for n in range(1, Y)]
     outs = [((16, COLS), F32)] + [((16, COLS), BF16)] * (NB - 1)
-    ends = local(joined_kernel, "joined_sums", outs, [block], [*first, *second], 4, size=MIB)
+    ends = local(joined_kernel, "joined_sums", outs, [block], [*first, *second], 4)
     return added([ends[0]] + [send(ends[n], moves(dz=n * (G // 2))) for n in range(1, NB)])
 
 

time: 113 us -> 111 us (0.982); the launches traced: 111 us -> 111 us
  starting transfers between devices: 43 us -> 47.4 us
  Pallas kernels: 38.2 us -> 35.1 us
  waiting for transfers between devices: 29.2 us -> 27.5 us
    ppermute x31, starting transfers between devices: 43 us -> 47.4 us  [send(): return lax.ppermute(value, AXES, pairs)]
    pallas_call x2 -> x1, Pallas kernels: 10.8 us -> 7.99 us  [make_accum(): pl.pallas_call(accum_kernel, grid_spec=pltpu.PrefetchScalarGridSpec(num_s...]
    ppermute x31, waiting for transfers between devices: 29.2 us -> 27.5 us  [send(): return lax.ppermute(value, AXES, pairs)]
    pallas_call x13 -> x12, Pallas kernels: 27.4 us -> 27.1 us  [local(): pl.pallas_call(kernel, in_specs=[SCALARS] * len(scalars) + [PLACED] * pla...]
  transfers between devices with their start and end apart: 31 -> 31, of which waited for: 11 -> 14; matrix products, arithmetic and copies ran while one was open for 0% -> 0% of each run, Pallas kernels for 23% -> 17%
where the time goes in v5:
time: 111 us
  starting transfers between devices  47.4 us (43%)
  Pallas kernels  35.1 us (32%)
  waiting for transfers between devices  27.5 us (25%)
    ppermute x31, starting transfers between devices, send(): return lax.ppermute(value, AXES, pairs)  47.4 us
    ppermute x31, waiting for transfers between devices, send(): return lax.ppermute(value, AXES, pairs)  27.5 us
    pallas_call x12, Pallas kernels, local(): pl.pallas_call(kernel, in_specs=[SCALARS] * len(scalars) + [PLACED] * pla...  27.1 us
    pallas_call x1, Pallas kernels, make_accum(): pl.pallas_call(accum_kernel, grid_spec=pltpu.PrefetchScalarGridSpec(num_s...  7.99 us
  transfers between devices with their start and end apart: 31, of which 14 were waited for; matrix products, arithmetic and copies ran while one was open for 0% of the time, Pallas kernels for 17%

profile of v5, /device:TPU:2, one launch (start us, length us, event | category | flops | bytes accessed | tf_op | source)
XLA Modules:
  0.0 110.9 jit_solution(6580776517497338502)
XLA Ops:
  0.9 2.0 %split_particles.1 = (bf16[32,8576]{1,0:T(8,128)(2,1)S(1)}, bf16[32,8576]{1,0:T(8,128)(2,1)S(1)}, bf16[32,8576]{1,0:T(8,128)(2,1)S(1)}, bf16[32,8576]{1,0:T(8,128)(2,1)S(1)}) custom-call(s32[1]{0:T(128)} %bitcast.1.member_ref, bf16[32,32768]{1,0:T(8,128)(2,1)} %source.3, s32[8,32]{1,0:T(8,128)} %bitcast.4, s32[32,32]{1,0:T(8,128)} %wedge.1, f32[32,32]{1,0:T(8,128)} %focus.1, ...), custom_call_target="tpu_custom_call" | custom-call | tf_op jit(solution)/shard_map/split_particles/pallas_call | solution.py:97
  3.0 2.0 %collective-permute-start.1 = (bf16[32,8576]{1,0:T(8,128)(2,1)S(1)}, bf16[32,8576]{1,0:T(8,128)(2,1)S(1)}, u32[]{:S(2)}, u32[]{:S(2)}) collective-permute-start(bf16[32,8576]{1,0:T(8,128)(2,1)S(1)} %get-tuple-element.55), channel_id=1, source_target_pairs={{0,2},{1,3},{2,0},{3,1},{4,6},{5,7},{6,4},{7,5},{8,10},{9,11},{10,... | collective-permute-start | bytes 1646600 | tf_op jit(solution)/shard_map/ppermute | solution.py:49
  5.0 3.2 %collective-permute-start.4 = (bf16[16,8192]{1,0:T(8,128)(2,1)S(1)}, bf16[16,8192]{1,0:T(8,128)(2,1)S(1)}, u32[]{:S(2)}, u32[]{:S(2)}) collective-permute-start(bf16[16,8192]{1,0:T(8,128)(2,1)S(1)} %own_references.1.after.refs_8_), channel_id=1, source_target_pairs={{0,128},{1,129},{2,130},{3,131},{4,132},{5,133},{6,134},{7,135},{8... | collective-permute-start | bytes 786440 | tf_op jit(solution)/shard_map/ppermute | solution.py:49
  8.9 2.6 %collective-permute-start.2 = (bf16[16,8192]{1,0:T(8,128)(2,1)S(1)}, bf16[16,8192]{1,0:T(8,128)(2,1)S(1)}, u32[]{:S(2)}, u32[]{:S(2)}) collective-permute-start(bf16[16,8192]{1,0:T(8,128)(2,1)S(1)} %own_references.1.after.refs_8_), channel_id=1, source_target_pairs={{0,192},{1,193},{2,194},{3,195},{4,196},{5,197},{6,198},{7,199},{8... | collective-permute-start | bytes 786440 | tf_op jit(solution)/shard_map/ppermute | solution.py:49
  11.5 5.5 %phase_table.1 = (bf16[256,8192]{1,0:T(8,128)(2,1)S(1)}, f32[4,8,1024]{2,1,0:T(8,128)S(1)}) custom-call(s32[1]{0:T(128)} %bitcast.1.member_ref, f32[16,8,1024]{2,1,0:T(8,128)} %constant.81.clone.geo_ref), custom_call_target="tpu_custom_call" | custom-call | tf_op jit(solution)/shard_map/phase_table/pallas_call | solution.py:97
  17.0 3.5 %collective-permute-done.3.refs_14_ = bf16[16,8192]{1,0:T(8,128)(2,1)S(1)} collective-permute-done((bf16[16,8192]{1,0:T(8,128)(2,1)S(1)}, bf16[16,8192]{1,0:T(8,128)(2,1)S(1)}, u32[]{:S(2)}, u32[]{:S(2)}) %collective-permute-start.3) | collective-permute-done | bytes 262176 | tf_op jit(solution)/shard_map/ppermute | solution.py:49
  20.9 1.7 %collective-permute-start.6 = (bf16[16,8192]{1,0:T(8,128)(2,1)S(1)}, bf16[16,8192]{1,0:T(8,128)(2,1)S(1)}, u32[]{:S(2)}, u32[]{:S(2)}) collective-permute-start(bf16[16,8192]{1,0:T(8,128)(2,1)S(1)} %own_references.1.after.refs_8_), channel_id=1, source_target_pairs={{0,48},{1,49},{2,50},{3,51},{4,52},{5,53},{6,54},{7,55},{8,56},{9,... | collective-permute-start | bytes 786440 | tf_op jit(solution)/shard_map/ppermute | solution.py:49
  22.6 1.7 %collective-permute-start.7 = (bf16[16,8192]{1,0:T(8,128)(2,1)S(1)}, bf16[16,8192]{1,0:T(8,128)(2,1)S(1)}, u32[]{:S(2)}, u32[]{:S(2)}) collective-permute-start(bf16[16,8192]{1,0:T(8,128)(2,1)S(1)} %collective-permute-done.2.refs_10_), channel_id=1, source_target_pairs={{0,48},{1,49},{2,50},{3,51},{4,52},{5,53},{6,54},{7,55},{8,56},{9,... | collective-permute-start | bytes 786440 | tf_op jit(solution)/shard_map/ppermute | solution.py:49
  25.0 3.2 %shifted_rows.4 = (bf16[256,8192]{1,0:T(8,128)(2,1)S(1)}, bf16[32,4096]{1,0:T(8,128)(2,1)S(1)}) custom-call(s32[1]{0:T(128)} %bitcast.1.member_ref, bf16[32,8576]{1,0:T(8,128)(2,1)S(1)} %get-tuple-element.57.x_ref, f32[4,8,1024]{2,1,0:T(8,128)S(1)} %get-tuple-element.58.geo_ref, bf16[256,8192]{1,0:T(8,128)(2,1)S(1)} %get-tuple-element.56.table_ref), custom_call_target="tpu_custom_call" | custom-call | tf_op jit(solution)/shard_map/shifted_rows/pallas_call | solution.py:97
  28.2 3.2 %shifted_rows.5 = (bf16[256,8192]{1,0:T(8,128)(2,1)S(1)}, bf16[32,4096]{1,0:T(8,128)(2,1)S(1)}) custom-call(s32[1]{0:T(128)} %bitcast.1.member_ref, bf16[32,8576]{1,0:T(8,128)(2,1)S(1)} %collective-permute-done.x_ref, f32[4,8,1024]{2,1,0:T(8,128)S(1)} %get-tuple-element.58.geo_ref, bf16[256,8192]{1,0:T(8,128)(2,1)S(1)} %get-tuple-element.56.table_ref), custom_call_target="tpu_custom_call" | custom-call | tf_op jit(solution)/shard_map/shifted_rows/pallas_call | solution.py:97
  31.4 3.2 %shifted_rows.6 = (bf16[256,8192]{1,0:T(8,128)(2,1)S(1)}, bf16[32,4096]{1,0:T(8,128)(2,1)S(1)}) custom-call(s32[1]{0:T(128)} %bitcast.1.member_ref, bf16[32,8576]{1,0:T(8,128)(2,1)S(1)} %collective-permute-done.1.x_ref, f32[4,8,1024]{2,1,0:T(8,128)S(1)} %get-tuple-element.58.geo_ref, bf16[256,8192]{1,0:T(8,128)(2,1)S(1)} %get-tuple-element.56.table_ref), custom_call_target="tpu_custom_call" | custom-call | tf_op jit(solution)/shard_map/shifted_rows/pallas_call | solution.py:97
  35.6 3.2 %shifted_rows.7 = (bf16[256,8192]{1,0:T(8,128)(2,1)S(1)}, bf16[32,4096]{1,0:T(8,128)(2,1)S(1)}) custom-call(s32[1]{0:T(128)} %bitcast.1.member_ref, bf16[32,8576]{1,0:T(8,128)(2,1)S(1)} %collective-permute-done.5.x_ref, f32[4,8,1024]{2,1,0:T(8,128)S(1)} %get-tuple-element.58.geo_ref, bf16[256,8192]{1,0:T(8,128)(2,1)S(1)} %get-tuple-element.56.table_ref), custom_call_target="tpu_custom_call" | custom-call | tf_op jit(solution)/shard_map/shifted_rows/pallas_call | solution.py:97
  38.8 4.8 %partial_scores.1 = (f32[256,128]{1,0:T(8,128)S(1)}, f32[256,128]{1,0:T(8,128)S(1)}, f32[256,128]{1,0:T(8,128)S(1)}, f32[256,128]{1,0:T(8,128)S(1)}) custom-call(bf16[256,8192]{1,0:T(8,128)(2,1)S(1)} %get-tuple-element.59.refs_0_, bf16[256,8192]{1,0:T(8,128)(2,1)S(1)} %get-tuple-element.61.refs_1_, bf16[256,8192]{1,0:T(8,128)(2,1)S(1)} %get-tuple-element.63.refs_2_, ...), custom_call_target="tpu_custom_call" | custom-call | tf_op jit(solution)/shard_map/partial_scores/pallas_call | solution.py:97
  45.6 4.5 %collective-permute-done.11.refs_2_ = f32[256,128]{1,0:T(8,128)S(1)} collective-permute-done((f32[256,128]{1,0:T(8,128)S(1)}, f32[256,128]{1,0:T(8,128)S(1)}, u32[]{:S(2)}, u32[]{:S(2)}) %collective-permute-start.11) | collective-permute-done | bytes 131104 | tf_op jit(solution)/shard_map/ppermute | solution.py:49
  50.1 1.9 %collective-permute-done.12.refs_3_ = f32[256,128]{1,0:T(8,128)S(1)} collective-permute-done((f32[256,128]{1,0:T(8,128)S(1)}, f32[256,128]{1,0:T(8,128)S(1)}, u32[]{:S(2)}, u32[]{:S(2)}) %collective-permute-start.12) | collective-permute-done | bytes 131104 | tf_op jit(solution)/shard_map/ppermute | solution.py:49
  54.3 2.0 %collective-permute-done.15.refs_7_ = bf16[128,256]{1,0:T(8,128)(2,1)S(1)} collective-permute-done((bf16[128,256]{1,0:T(8,128)(2,1)S(1)}, bf16[128,256]{1,0:T(8,128)(2,1)S(1)}, u32[]{:S(2)}, u32[]{:S(2)}) %collective-permute-start.15) | collective-permute-done | bytes 65568 | tf_op jit(solution)/shard_map/ppermute | solution.py:49
  56.4 1.8 %collective-permute-done.14.refs_6_ = bf16[128,256]{1,0:T(8,128)(2,1)S(1)} collective-permute-done((bf16[128,256]{1,0:T(8,128)(2,1)S(1)}, bf16[128,256]{1,0:T(8,128)(2,1)S(1)}, u32[]{:S(2)}, u32[]{:S(2)}) %collective-permute-start.14) | collective-permute-done | bytes 65568 | tf_op jit(solution)/shard_map/ppermute | solution.py:49
  58.2 8.0 %weighted_sums.1 = (bf16[32,4096]{1,0:T(8,128)(2,1)S(1)}, bf16[32,4096]{1,0:T(8,128)(2,1)S(1)}, bf16[32,4096]{1,0:T(8,128)(2,1)S(1)}, bf16[32,4096]{1,0:T(8,128)...) custom-call(s32[4]{0:T(128)S(1)} %and_select_fusion.flag_ref, ...), custom_call_target="tpu_custom_call" | custom-call | tf_op jit(solution)/shard_map/weighted_sums/pallas_call | solution.py:363
  66.2 1.6 %collective-permute-start.16 = (bf16[32,4096]{1,0:T(8,128)(2,1)S(1)}, bf16[32,4096]{1,0:T(8,128)(2,1)S(1)}, u32[]{:S(2)}, u32[]{:S(2)}) collective-permute-start(bf16[32,4096]{1,0:T(8,128)(2,1)S(1)} %get-tuple-element.81), channel_id=1, source_target_pairs={{0,64},{1,65},{2,66},{3,67},{4,68},{5,69},{6,70},{7,71},{8,72},{9,... | collective-permute-start | bytes 786440 | tf_op jit(solution)/shard_map/ppermute | solution.py:49
  67.7 2.3 %collective-permute-start.17 = (bf16[32,4096]{1,0:T(8,128)(2,1)S(1)}, bf16[32,4096]{1,0:T(8,128)(2,1)S(1)}, u32[]{:S(2)}, u32[]{:S(2)}) collective-permute-start(bf16[32,4096]{1,0:T(8,128)(2,1)S(1)} %get-tuple-element.82), channel_id=1, source_target_pairs={{0,128},{1,129},{2,130},{3,131},{4,132},{5,133},{6,134},{7,135},{8... | collective-permute-start | bytes 786440 | tf_op jit(solution)/shard_map/ppermute | solution.py:49
  70.7 2.1 %collective-permute-start.22 = (bf16[64,2048]{1,0:T(8,128)(2,1)S(1)}, bf16[64,2048]{1,0:T(8,128)(2,1)S(1)}, u32[]{:S(2)}, u32[]{:S(2)}) collective-permute-start(bf16[64,2048]{1,0:T(8,128)(2,1)S(1)} %get-tuple-element.89), channel_id=1, source_target_pairs={{0,32},{1,33},{2,34},{3,35},{4,36},{5,37},{6,38},{7,39},{8,40},{9,... | collective-permute-start | bytes 786440 | tf_op jit(solution)/shard_map/ppermute | solution.py:49
  72.8 3.6 %collective-permute-done.16.refs_1_ = bf16[32,4096]{1,0:T(8,128)(2,1)S(1)} collective-permute-done((bf16[32,4096]{1,0:T(8,128)(2,1)S(1)}, bf16[32,4096]{1,0:T(8,128)(2,1)S(1)}, u32[]{:S(2)}, u32[]{:S(2)}) %collective-permute-start.16) | collective-permute-done | bytes 262176 | tf_op jit(solution)/shard_map/ppermute | solution.py:49
  76.4 2.2 %collective-permute-start.23 = (bf16[64,2048]{1,0:T(8,128)(2,1)S(1)}, bf16[64,2048]{1,0:T(8,128)(2,1)S(1)}, u32[]{:S(2)}, u32[]{:S(2)}) collective-permute-start(bf16[64,2048]{1,0:T(8,128)(2,1)S(1)} %get-tuple-element.91), channel_id=1, source_target_pairs={{0,16},{1,17},{2,18},{3,19},{4,20},{5,21},{6,22},{7,23},{8,24},{9,... | collective-permute-start | bytes 786440 | tf_op jit(solution)/shard_map/ppermute | solution.py:49
  78.7 2.7 %collective-permute-done.17.refs_2_ = bf16[32,4096]{1,0:T(8,128)(2,1)S(1)} collective-permute-done((bf16[32,4096]{1,0:T(8,128)(2,1)S(1)}, bf16[32,4096]{1,0:T(8,128)(2,1)S(1)}, u32[]{:S(2)}, u32[]{:S(2)}) %collective-permute-start.17) | collective-permute-done | bytes 262176 | tf_op jit(solution)/shard_map/ppermute | solution.py:49
  82.3 1.9 %collective-permute-start.19 = (bf16[16,2048]{1,0:T(8,128)(2,1)S(1)}, bf16[16,2048]{1,0:T(8,128)(2,1)S(1)}, u32[]{:S(2)}, u32[]{:S(2)}) collective-permute-start(bf16[16,2048]{1,0:T(8,128)(2,1)S(1)} %get-tuple-element.85), channel_id=1, source_target_pairs={{0,32},{1,33},{2,34},{3,35},{4,36},{5,37},{6,38},{7,39},{8,40},{9,... | collective-permute-start | bytes 196616 | tf_op jit(solution)/shard_map/ppermute | solution.py:49
  85.3 2.2 %collective-permute-start.21 = (bf16[16,2048]{1,0:T(8,128)(2,1)S(1)}, bf16[16,2048]{1,0:T(8,128)(2,1)S(1)}, u32[]{:S(2)}, u32[]{:S(2)}) collective-permute-start(bf16[16,2048]{1,0:T(8,128)(2,1)S(1)} %get-tuple-element.87), channel_id=1, source_target_pairs={{0,48},{1,49},{2,50},{3,51},{4,52},{5,53},{6,54},{7,55},{8,56},{9,... | collective-permute-start | bytes 196616 | tf_op jit(solution)/shard_map/ppermute | solution.py:49
  87.7 1.5 %collective-permute-start.25 = (bf16[16,2048]{1,0:T(8,128)(2,1)S(1)}, bf16[16,2048]{1,0:T(8,128)(2,1)S(1)}, u32[]{:S(2)}, u32[]{:S(2)}) collective-permute-start(bf16[16,2048]{1,0:T(8,128)(2,1)S(1)} %get-tuple-element.94), channel_id=1, source_target_pairs={{0,64},{1,65},{2,66},{3,67},{4,68},{5,69},{6,70},{7,71},{8,72},{9,... | collective-permute-start | bytes 196616 | tf_op jit(solution)/shard_map/ppermute | solution.py:49
  89.2 2.6 %collective-permute-start.26 = (bf16[16,2048]{1,0:T(8,128)(2,1)S(1)}, bf16[16,2048]{1,0:T(8,128)(2,1)S(1)}, u32[]{:S(2)}, u32[]{:S(2)}) collective-permute-start(bf16[16,2048]{1,0:T(8,128)(2,1)S(1)} %get-tuple-element.95), channel_id=1, source_target_pairs={{0,128},{1,129},{2,130},{3,131},{4,132},{5,133},{6,134},{7,135},{8... | collective-permute-start | bytes 196616 | tf_op jit(solution)/shard_map/ppermute | solution.py:49
  96.1 3.3 %collective-permute-start.28 = (bf16[16,1024]{1,0:T(8,128)(2,1)S(1)}, bf16[16,1024]{1,0:T(8,128)(2,1)S(1)}, u32[]{:S(2)}, u32[]{:S(2)}) collective-permute-start(bf16[16,1024]{1,0:T(8,128)(2,1)S(1)} %get-tuple-element.98), channel_id=1, source_target_pairs={{0,4},{1,5},{2,6},{3,7},{4,8},{5,9},{6,10},{7,11},{8,12},{9,13},{1... | collective-permute-start | bytes 98312 | tf_op jit(solution)/shard_map/ppermute | solution.py:49
  99.5 5.8 %collective-permute-start.29 = (bf16[16,1024]{1,0:T(8,128)(2,1)S(1)}, bf16[16,1024]{1,0:T(8,128)(2,1)S(1)}, u32[]{:S(2)}, u32[]{:S(2)}) collective-permute-start(bf16[16,1024]{1,0:T(8,128)(2,1)S(1)} %get-tuple-element.99), channel_id=1, source_target_pairs={{0,8},{1,9},{2,10},{3,11},{4,12},{5,13},{6,14},{7,15},{8,0},{9,1},... | collective-permute-start | bytes 98312 | tf_op jit(solution)/shard_map/ppermute | solution.py:49
  105.2 2.7 %collective-permute-start.30 = (bf16[16,1024]{1,0:T(8,128)(2,1)S(1)}, bf16[16,1024]{1,0:T(8,128)(2,1)S(1)}, u32[]{:S(2)}, u32[]{:S(2)}) collective-permute-start(bf16[16,1024]{1,0:T(8,128)(2,1)S(1)} %get-tuple-element.100), channel_id=1, source_target_pairs={{0,12},{1,13},{2,14},{3,15},{4,0},{5,1},{6,2},{7,3},{8,4},{9,5},{1... | collective-permute-start | bytes 98312 | tf_op jit(solution)/shard_map/ppermute | solution.py:49
  107.9 2.3 %collective-permute-done.30 = bf16[16,1024]{1,0:T(8,128)(2,1)S(1)} collective-permute-done((bf16[16,1024]{1,0:T(8,128)(2,1)S(1)}, bf16[16,1024]{1,0:T(8,128)(2,1)S(1)}, u32[]{:S(2)}, u32[]{:S(2)}) %collective-permute-start.30) | collective-permute-done | bytes 32800 | tf_op jit(solution)/shard_map/ppermute | solution.py:49
  (53 shorter events, 15.9 us)
Async XLA Ops:
  2.9 18.0 %collective-permute-start = (bf16[32,8576]{1,0:T(8,128)(2,1)S(1)}, bf16[32,8576]{1,0:T(8,128)(2,1)S(1)}, u32[]{:S(2)}, u32[]{:S(2)}) collective-permute-start(bf16[32,8576]{1,0:T(8,128)(2,1)S(1)} %get-tuple-element.54), channel_id=1, source_target_pairs={{0,1},{1,0},{2,3},{3,2},{4,5},{5,4},{6,7},{7,6},{8,9},{9,8},{10,11... | collective-permute-start | bytes 1646600 | tf_op jit(solution)/shard_map/ppermute | solution.py:49
  3.0 17.9 %collective-permute-start.1 = (bf16[32,8576]{1,0:T(8,128)(2,1)S(1)}, bf16[32,8576]{1,0:T(8,128)(2,1)S(1)}, u32[]{:S(2)}, u32[]{:S(2)}) collective-permute-start(bf16[32,8576]{1,0:T(8,128)(2,1)S(1)} %get-tuple-element.55), channel_id=1, source_target_pairs={{0,2},{1,3},{2,0},{3,1},{4,6},{5,7},{6,4},{7,5},{8,10},{9,11},{10,... | collective-permute-start | bytes 1646600 | tf_op jit(solution)/shard_map/ppermute | solution.py:49
  5.0 12.0 %collective-permute-start.4 = (bf16[16,8192]{1,0:T(8,128)(2,1)S(1)}, bf16[16,8192]{1,0:T(8,128)(2,1)S(1)}, u32[]{:S(2)}, u32[]{:S(2)}) collective-permute-start(bf16[16,8192]{1,0:T(8,128)(2,1)S(1)} %own_references.1.after.refs_8_), channel_id=1, source_target_pairs={{0,128},{1,129},{2,130},{3,131},{4,132},{5,133},{6,134},{7,135},{8... | collective-permute-start | bytes 786440 | tf_op jit(solution)/shard_map/ppermute | solution.py:49
  8.2 12.3 %collective-permute-start.3 = (bf16[16,8192]{1,0:T(8,128)(2,1)S(1)}, bf16[16,8192]{1,0:T(8,128)(2,1)S(1)}, u32[]{:S(2)}, u32[]{:S(2)}) collective-permute-start(bf16[16,8192]{1,0:T(8,128)(2,1)S(1)} %own_references.1.after.refs_8_), channel_id=1, source_target_pairs={{0,64},{1,65},{2,66},{3,67},{4,68},{5,69},{6,70},{7,71},{8,72},{9,... | collective-permute-start | bytes 786440 | tf_op jit(solution)/shard_map/ppermute | solution.py:49
  8.9 12.0 %collective-permute-start.2 = (bf16[16,8192]{1,0:T(8,128)(2,1)S(1)}, bf16[16,8192]{1,0:T(8,128)(2,1)S(1)}, u32[]{:S(2)}, u32[]{:S(2)}) collective-permute-start(bf16[16,8192]{1,0:T(8,128)(2,1)S(1)} %own_references.1.after.refs_8_), channel_id=1, source_target_pairs={{0,192},{1,193},{2,194},{3,195},{4,196},{5,197},{6,198},{7,199},{8... | collective-permute-start | bytes 786440 | tf_op jit(solution)/shard_map/ppermute | solution.py:49
  20.9 14.7 %collective-permute-start.5 = (bf16[32,8576]{1,0:T(8,128)(2,1)S(1)}, bf16[32,8576]{1,0:T(8,128)(2,1)S(1)}, u32[]{:S(2)}, u32[]{:S(2)}) collective-permute-start(bf16[32,8576]{1,0:T(8,128)(2,1)S(1)} %get-tuple-element.65), channel_id=1, source_target_pairs={{0,3},{1,2},{2,1},{3,0},{4,7},{5,6},{6,5},{7,4},{8,11},{9,10},{10,... | collective-permute-start | bytes 1646600 | tf_op jit(solution)/shard_map/ppermute | solution.py:49
  20.9 17.8 %collective-permute-start.6 = (bf16[16,8192]{1,0:T(8,128)(2,1)S(1)}, bf16[16,8192]{1,0:T(8,128)(2,1)S(1)}, u32[]{:S(2)}, u32[]{:S(2)}) collective-permute-start(bf16[16,8192]{1,0:T(8,128)(2,1)S(1)} %own_references.1.after.refs_8_), channel_id=1, source_target_pairs={{0,48},{1,49},{2,50},{3,51},{4,52},{5,53},{6,54},{7,55},{8,56},{9,... | collective-permute-start | bytes 786440 | tf_op jit(solution)/shard_map/ppermute | solution.py:49
  22.6 16.1 %collective-permute-start.7 = (bf16[16,8192]{1,0:T(8,128)(2,1)S(1)}, bf16[16,8192]{1,0:T(8,128)(2,1)S(1)}, u32[]{:S(2)}, u32[]{:S(2)}) collective-permute-start(bf16[16,8192]{1,0:T(8,128)(2,1)S(1)} %collective-permute-done.2.refs_10_), channel_id=1, source_target_pairs={{0,48},{1,49},{2,50},{3,51},{4,52},{5,53},{6,54},{7,55},{8,56},{9,... | collective-permute-start | bytes 786440 | tf_op jit(solution)/shard_map/ppermute | solution.py:49
  24.3 14.5 %collective-permute-start.8 = (bf16[16,8192]{1,0:T(8,128)(2,1)S(1)}, bf16[16,8192]{1,0:T(8,128)(2,1)S(1)}, u32[]{:S(2)}, u32[]{:S(2)}) collective-permute-start(bf16[16,8192]{1,0:T(8,128)(2,1)S(1)} %collective-permute-done.4.refs_12_), channel_id=1, source_target_pairs={{0,32},{1,33},{2,34},{3,35},{4,36},{5,37},{6,38},{7,39},{8,40},{9,... | collective-permute-start | bytes 786440 | tf_op jit(solution)/shard_map/ppermute | solution.py:49
  24.6 14.1 %collective-permute-start.9 = (bf16[16,8192]{1,0:T(8,128)(2,1)S(1)}, bf16[16,8192]{1,0:T(8,128)(2,1)S(1)}, u32[]{:S(2)}, u32[]{:S(2)}) collective-permute-start(bf16[16,8192]{1,0:T(8,128)(2,1)S(1)} %collective-permute-done.3.refs_14_), channel_id=1, source_target_pairs={{0,32},{1,33},{2,34},{3,35},{4,36},{5,37},{6,38},{7,39},{8,40},{9,... | collective-permute-start | bytes 786440 | tf_op jit(solution)/shard_map/ppermute | solution.py:49
  28.2 10.6 %copy-start = (bf16[256,8192]{1,0:T(8,128)(2,1)}, bf16[256,8192]{1,0:T(8,128)(2,1)S(1)}, u32[]{:S(2)}) copy-start(bf16[256,8192]{1,0:T(8,128)(2,1)S(1)} %get-tuple-element.59.refs_0_) | copy-start | bytes 12582916
  43.6 2.0 %collective-permute-start.10 = (f32[256,128]{1,0:T(8,128)S(1)}, f32[256,128]{1,0:T(8,128)S(1)}, u32[]{:S(2)}, u32[]{:S(2)}) collective-permute-start(f32[256,128]{1,0:T(8,128)S(1)} %get-tuple-element.77), channel_id=1, source_target_pairs={{0,1},{1,0},{2,3},{3,2},{4,5},{5,4},{6,7},{7,6},{8,9},{9,8},{10,11... | collective-permute-start | bytes 393224 | tf_op jit(solution)/shard_map/ppermute | solution.py:49
  43.7 6.4 %collective-permute-start.11 = (f32[256,128]{1,0:T(8,128)S(1)}, f32[256,128]{1,0:T(8,128)S(1)}, u32[]{:S(2)}, u32[]{:S(2)}) collective-permute-start(f32[256,128]{1,0:T(8,128)S(1)} %get-tuple-element.78), channel_id=1, source_target_pairs={{0,2},{1,3},{2,0},{3,1},{4,6},{5,7},{6,4},{7,5},{8,10},{9,11},{10,... | collective-permute-start | bytes 393224 | tf_op jit(solution)/shard_map/ppermute | solution.py:49
  44.6 7.4 %collective-permute-start.12 = (f32[256,128]{1,0:T(8,128)S(1)}, f32[256,128]{1,0:T(8,128)S(1)}, u32[]{:S(2)}, u32[]{:S(2)}) collective-permute-start(f32[256,128]{1,0:T(8,128)S(1)} %get-tuple-element.79), channel_id=1, source_target_pairs={{0,3},{1,2},{2,1},{3,0},{4,7},{5,6},{6,5},{7,4},{8,11},{9,10},{10,... | collective-permute-start | bytes 393224 | tf_op jit(solution)/shard_map/ppermute | solution.py:49
  52.3 4.1 %collective-permute-start.15 = (bf16[128,256]{1,0:T(8,128)(2,1)S(1)}, bf16[128,256]{1,0:T(8,128)(2,1)S(1)}, u32[]{:S(2)}, u32[]{:S(2)}) collective-permute-start(bf16[128,256]{1,0:T(8,128)(2,1)S(1)} %posterior.1.refs_4_), channel_id=1, source_target_pairs={{0,3},{1,2},{2,1},{3,0},{4,7},{5,6},{6,5},{7,4},{8,11},{9,10},{10,... | collective-permute-start | bytes 196616 | tf_op jit(solution)/shard_map/ppermute | solution.py:49
  53.1 5.1 %collective-permute-start.14 = (bf16[128,256]{1,0:T(8,128)(2,1)S(1)}, bf16[128,256]{1,0:T(8,128)(2,1)S(1)}, u32[]{:S(2)}, u32[]{:S(2)}) collective-permute-start(bf16[128,256]{1,0:T(8,128)(2,1)S(1)} %posterior.1.refs_4_), channel_id=1, source_target_pairs={{0,2},{1,3},{2,0},{3,1},{4,6},{5,7},{6,4},{7,5},{8,10},{9,11},{10,... | collective-permute-start | bytes 196616 | tf_op jit(solution)/shard_map/ppermute | solution.py:49
  54.3 3.9 %collective-permute-start.13 = (bf16[128,256]{1,0:T(8,128)(2,1)S(1)}, bf16[128,256]{1,0:T(8,128)(2,1)S(1)}, u32[]{:S(2)}, u32[]{:S(2)}) collective-permute-start(bf16[128,256]{1,0:T(8,128)(2,1)S(1)} %posterior.1.refs_4_), channel_id=1, source_target_pairs={{0,1},{1,0},{2,3},{3,2},{4,5},{5,4},{6,7},{7,6},{8,9},{9,8},{10,11... | collective-permute-start | bytes 196616 | tf_op jit(solution)/shard_map/ppermute | solution.py:49
  66.2 10.3 %collective-permute-start.16 = (bf16[32,4096]{1,0:T(8,128)(2,1)S(1)}, bf16[32,4096]{1,0:T(8,128)(2,1)S(1)}, u32[]{:S(2)}, u32[]{:S(2)}) collective-permute-start(bf16[32,4096]{1,0:T(8,128)(2,1)S(1)} %get-tuple-element.81), channel_id=1, source_target_pairs={{0,64},{1,65},{2,66},{3,67},{4,68},{5,69},{6,70},{7,71},{8,72},{9,... | collective-permute-start | bytes 786440 | tf_op jit(solution)/shard_map/ppermute | solution.py:49
  67.7 13.6 %collective-permute-start.17 = (bf16[32,4096]{1,0:T(8,128)(2,1)S(1)}, bf16[32,4096]{1,0:T(8,128)(2,1)S(1)}, u32[]{:S(2)}, u32[]{:S(2)}) collective-permute-start(bf16[32,4096]{1,0:T(8,128)(2,1)S(1)} %get-tuple-element.82), channel_id=1, source_target_pairs={{0,128},{1,129},{2,130},{3,131},{4,132},{5,133},{6,134},{7,135},{8... | collective-permute-start | bytes 786440 | tf_op jit(solution)/shard_map/ppermute | solution.py:49
  70.0 11.6 %collective-permute-start.18 = (bf16[32,4096]{1,0:T(8,128)(2,1)S(1)}, bf16[32,4096]{1,0:T(8,128)(2,1)S(1)}, u32[]{:S(2)}, u32[]{:S(2)}) collective-permute-start(bf16[32,4096]{1,0:T(8,128)(2,1)S(1)} %get-tuple-element.83), channel_id=1, source_target_pairs={{0,192},{1,193},{2,194},{3,195},{4,196},{5,197},{6,198},{7,199},{8... | collective-permute-start | bytes 786440 | tf_op jit(solution)/shard_map/ppermute | solution.py:49
  70.7 14.5 %collective-permute-start.22 = (bf16[64,2048]{1,0:T(8,128)(2,1)S(1)}, bf16[64,2048]{1,0:T(8,128)(2,1)S(1)}, u32[]{:S(2)}, u32[]{:S(2)}) collective-permute-start(bf16[64,2048]{1,0:T(8,128)(2,1)S(1)} %get-tuple-element.89), channel_id=1, source_target_pairs={{0,32},{1,33},{2,34},{3,35},{4,36},{5,37},{6,38},{7,39},{8,40},{9,... | collective-permute-start | bytes 786440 | tf_op jit(solution)/shard_map/ppermute | solution.py:49
  72.8 14.7 %collective-permute-start.24 = (bf16[64,2048]{1,0:T(8,128)(2,1)S(1)}, bf16[64,2048]{1,0:T(8,128)(2,1)S(1)}, u32[]{:S(2)}, u32[]{:S(2)}) collective-permute-start(bf16[64,2048]{1,0:T(8,128)(2,1)S(1)} %get-tuple-element.92), channel_id=1, source_target_pairs={{0,48},{1,49},{2,50},{3,51},{4,52},{5,53},{6,54},{7,55},{8,56},{9,... | collective-permute-start | bytes 786440 | tf_op jit(solution)/shard_map/ppermute | solution.py:49
  76.4 11.1 %collective-permute-start.23 = (bf16[64,2048]{1,0:T(8,128)(2,1)S(1)}, bf16[64,2048]{1,0:T(8,128)(2,1)S(1)}, u32[]{:S(2)}, u32[]{:S(2)}) collective-permute-start(bf16[64,2048]{1,0:T(8,128)(2,1)S(1)} %get-tuple-element.91), channel_id=1, source_target_pairs={{0,16},{1,17},{2,18},{3,19},{4,20},{5,21},{6,22},{7,23},{8,24},{9,... | collective-permute-start | bytes 786440 | tf_op jit(solution)/shard_map/ppermute | solution.py:49
  82.3 9.5 %collective-permute-start.19 = (bf16[16,2048]{1,0:T(8,128)(2,1)S(1)}, bf16[16,2048]{1,0:T(8,128)(2,1)S(1)}, u32[]{:S(2)}, u32[]{:S(2)}) collective-permute-start(bf16[16,2048]{1,0:T(8,128)(2,1)S(1)} %get-tuple-element.85), channel_id=1, source_target_pairs={{0,32},{1,33},{2,34},{3,35},{4,36},{5,37},{6,38},{7,39},{8,40},{9,... | collective-permute-start | bytes 196616 | tf_op jit(solution)/shard_map/ppermute | solution.py:49
  84.3 8.2 %collective-permute-start.20 = (bf16[16,2048]{1,0:T(8,128)(2,1)S(1)}, bf16[16,2048]{1,0:T(8,128)(2,1)S(1)}, u32[]{:S(2)}, u32[]{:S(2)}) collective-permute-start(bf16[16,2048]{1,0:T(8,128)(2,1)S(1)} %get-tuple-element.86), channel_id=1, source_target_pairs={{0,16},{1,17},{2,18},{3,19},{4,20},{5,21},{6,22},{7,23},{8,24},{9,... | collective-permute-start | bytes 196616 | tf_op jit(solution)/shard_map/ppermute | solution.py:49
  85.3 7.2 %collective-permute-start.21 = (bf16[16,2048]{1,0:T(8,128)(2,1)S(1)}, bf16[16,2048]{1,0:T(8,128)(2,1)S(1)}, u32[]{:S(2)}, u32[]{:S(2)}) collective-permute-start(bf16[16,2048]{1,0:T(8,128)(2,1)S(1)} %get-tuple-element.87), channel_id=1, source_target_pairs={{0,48},{1,49},{2,50},{3,51},{4,52},{5,53},{6,54},{7,55},{8,56},{9,... | collective-permute-start | bytes 196616 | tf_op jit(solution)/shard_map/ppermute | solution.py:49
  87.7 6.0 %collective-permute-start.25 = (bf16[16,2048]{1,0:T(8,128)(2,1)S(1)}, bf16[16,2048]{1,0:T(8,128)(2,1)S(1)}, u32[]{:S(2)}, u32[]{:S(2)}) collective-permute-start(bf16[16,2048]{1,0:T(8,128)(2,1)S(1)} %get-tuple-element.94), channel_id=1, source_target_pairs={{0,64},{1,65},{2,66},{3,67},{4,68},{5,69},{6,70},{7,71},{8,72},{9,... | collective-permute-start | bytes 196616 | tf_op jit(solution)/shard_map/ppermute | solution.py:49
  89.2 5.8 %collective-permute-start.26 = (bf16[16,2048]{1,0:T(8,128)(2,1)S(1)}, bf16[16,2048]{1,0:T(8,128)(2,1)S(1)}, u32[]{:S(2)}, u32[]{:S(2)}) collective-permute-start(bf16[16,2048]{1,0:T(8,128)(2,1)S(1)} %get-tuple-element.95), channel_id=1, source_target_pairs={{0,128},{1,129},{2,130},{3,131},{4,132},{5,133},{6,134},{7,135},{8... | collective-permute-start | bytes 196616 | tf_op jit(solution)/shard_map/ppermute | solution.py:49
  91.8 4.3 %collective-permute-start.27 = (bf16[16,2048]{1,0:T(8,128)(2,1)S(1)}, bf16[16,2048]{1,0:T(8,128)(2,1)S(1)}, u32[]{:S(2)}, u32[]{:S(2)}) collective-permute-start(bf16[16,2048]{1,0:T(8,128)(2,1)S(1)} %get-tuple-element.96), channel_id=1, source_target_pairs={{0,192},{1,193},{2,194},{3,195},{4,196},{5,197},{6,198},{7,199},{8... | collective-permute-start | bytes 196616 | tf_op jit(solution)/shard_map/ppermute | solution.py:49
  96.1 11.8 %collective-permute-start.28 = (bf16[16,1024]{1,0:T(8,128)(2,1)S(1)}, bf16[16,1024]{1,0:T(8,128)(2,1)S(1)}, u32[]{:S(2)}, u32[]{:S(2)}) collective-permute-start(bf16[16,1024]{1,0:T(8,128)(2,1)S(1)} %get-tuple-element.98), channel_id=1, source_target_pairs={{0,4},{1,5},{2,6},{3,7},{4,8},{5,9},{6,10},{7,11},{8,12},{9,13},{1... | collective-permute-start | bytes 98312 | tf_op jit(solution)/shard_map/ppermute | solution.py:49
  99.5 8.5 %collective-permute-start.29 = (bf16[16,1024]{1,0:T(8,128)(2,1)S(1)}, bf16[16,1024]{1,0:T(8,128)(2,1)S(1)}, u32[]{:S(2)}, u32[]{:S(2)}) collective-permute-start(bf16[16,1024]{1,0:T(8,128)(2,1)S(1)} %get-tuple-element.99), channel_id=1, source_target_pairs={{0,8},{1,9},{2,10},{3,11},{4,12},{5,13},{6,14},{7,15},{8,0},{9,1},... | collective-permute-start | bytes 98312 | tf_op jit(solution)/shard_map/ppermute | solution.py:49
  105.2 5.0 %collective-permute-start.30 = (bf16[16,1024]{1,0:T(8,128)(2,1)S(1)}, bf16[16,1024]{1,0:T(8,128)(2,1)S(1)}, u32[]{:S(2)}, u32[]{:S(2)}) collective-permute-start(bf16[16,1024]{1,0:T(8,128)(2,1)S(1)} %get-tuple-element.100), channel_id=1, source_target_pairs={{0,12},{1,13},{2,14},{3,15},{4,0},{5,1},{6,2},{7,3},{8,4},{9,5},{1... | collective-permute-start | bytes 98312 | tf_op jit(solution)/shard_map/ppermute | solution.py:49
  (3 other events, 21.2 us)

commit v6 on v5

--- a/solution.py
+++ b/solution.py
@@ -110,9 +110,9 @@
     )
 
 
-def table_kernel(member_ref, geo_ref, out_ref, picked_ref, sems):
+def table_kernel(where_ref, geo_ref, out_ref, picked_ref, sems):
     copies = [
-        pltpu.make_async_copy(geo_ref.at[block * G + member_ref[0]], picked_ref.at[block], sems.at[block])
+        pltpu.make_async_copy(geo_ref.at[block * G + where_ref[0]], picked_ref.at[block], sems.at[block])
         for block in range(NB)
     ]
     for copy in copies:
@@ -144,9 +144,9 @@
                 out_ref[128:256, pl.ds(spot, HALF)] = low
 
 
-def make_table(member, geo):
+def make_table(where, geo):
     return local(
-        table_kernel, "phase_table", [((256, WIDTH), BF16), ((NB, 8, COLS), F32)], [member], [geo], 8,
+        table_kernel, "phase_table", [((256, WIDTH), BF16), ((NB, 8, COLS), F32)], [where], [geo], 8,
         placed=1, scratch=[pltpu.SemaphoreType.DMA((NB,))],
     )
 
@@ -166,17 +166,17 @@
     ]
 
 
-def own_kernel(member_ref, source, out, sems):
-    copies = pieces_of(source, out, member_ref[0], sems, 0)
+def own_kernel(where_ref, source, out, sems):
+    copies = pieces_of(source, out, where_ref[0], sems, 0)
     for copy in copies:
         copy.start()
     for copy in copies:
         copy.wait()
 
 
-def own_columns(member, refs):
+def own_columns(where, refs):
     (own,) = local(
-        own_kernel, "own_references", [((16, WIDTH), BF16)], [member], [refs], 4,
+        own_kernel, "own_references", [((16, WIDTH), BF16)], [where], [refs], 4,
         placed=1, scratch=[pltpu.SemaphoreType.DMA((2 * NB,))],
     )
     return own
@@ -200,11 +200,11 @@
     )
 
 
-def split_kernel(member_ref, source, ids, wedge, focus, sigma, after, *refs):
+def split_kernel(where_ref, source, ids, wedge, focus, sigma, after, *refs):
     outs, (ids_in, wedge_in, focus_in, sigma_in, sems, more) = refs[:G], refs[G:]
     copies = []
     for n in (2, 1, 3, 0):
-        copies += pieces_of(source, outs[n], member_ref[0] ^ n, sems, n * 2 * NB)
+        copies += pieces_of(source, outs[n], where_ref[0] ^ n, sems, n * 2 * NB)
     settings = [
         pltpu.make_async_copy(at, to, more.at[n])
         for n, (at, to) in enumerate(
@@ -234,9 +234,9 @@
         copy.wait()
 
 
-def split_particles(member, after, particles, shift_ids, wedge, defocus, inv_sigma):
+def split_particles(where, after, particles, shift_ids, wedge, defocus, inv_sigma):
     return local(
-        split_kernel, "split_particles", [((P_DEV, WIDTH + EXTRA), BF16)] * G, [member],
+        split_kernel, "split_particles", [((P_DEV, WIDTH + EXTRA), BF16)] * G, [where],
         [particles, shift_ids.T, wedge, defocus, inv_sigma[None], after], 4, placed=5,
         scratch=[
             pltpu.VMEM((SHIFTS, P_DEV), jnp.int32),
@@ -249,7 +249,7 @@
     )
 
 
-def rows_kernel(member_ref, x_ref, geo_ref, table_ref, rows_ref, pen_ref):
+def rows_kernel(where_ref, x_ref, geo_ref, table_ref, rows_ref, pen_ref):
     info = sum(x_ref[:, WIDTH + n * 128 : WIDTH + (n + 1) * 128].astype(F32) for n in range(3))
     lane = lax.broadcasted_iota(jnp.int32, (ROWS, 256), 1) & 127
     ids = jnp.concatenate([info[:, s : s + 1] for s in range(SHIFTS)], axis=0)
@@ -259,7 +259,7 @@
 
     @pl.loop(0, NB)
     def _(block):
-        first = 2 * (block * G + member_ref[0]) + 16
+        first = 2 * (block * G + where_ref[0]) + 16
         start = pl.multiple_of(block * 2 * COLS, 2 * COLS)
         for tilt in range(2):
             kept = jnp.sum(jnp.where(small == first + tilt, info, 0.0), axis=1, keepdims=True)
@@ -280,9 +280,9 @@
             rows_ref[:, upper] = (imag * cosine - real * sine).reshape(ROWS, HALF).astype(BF16)
 
 
-def make_rows(member, x, geo, table):
+def make_rows(where, x, geo, table):
     return local(
-        rows_kernel, "shifted_rows", [((ROWS, WIDTH), BF16), ((P_DEV, NB * COLS), BF16)], [member],
+        rows_kernel, "shifted_rows", [((ROWS, WIDTH), BF16), ((P_DEV, NB * COLS), BF16)], [where],
         [x, geo, table], 12,
     )
 
@@ -333,48 +333,42 @@
     return out
 
 
-def accum_kernel(flag_ref, *refs):
+def accum_kernel(part, where_ref, *refs):
     rows, posts, outs = refs[:G], refs[G : 2 * G], refs[2 * G :]
-    for part in range(2):
+
+    @pl.loop(0, NB)
+    def _(block):
         sums = []
         for half in range(2):
-            lanes = slice(half * COLS + part * HALF, half * COLS + (part + 1) * HALF)
-            total = jnp.dot(posts[0][...], rows[0][:, lanes], preferred_element_type=F32)
+            start = pl.multiple_of(block * 2 * COLS + half * COLS + part * HALF, HALF)
+            total = jnp.dot(posts[0][...], rows[0][:, pl.ds(start, HALF)], preferred_element_type=F32)
             for n in range(1, G):
-                total = total + jnp.dot(posts[n][...], rows[n][:, lanes], preferred_element_type=F32)
+                total = total + jnp.dot(
+                    posts[n][...], rows[n][:, pl.ds(start, HALF)], preferred_element_type=F32
+                )
             sums.append(total)
         if part == 0:
             for n in range(Y):
                 for half, total in enumerate(sums):
-                    outs[n][:, half * HALF : (half + 1) * HALF] = total[n * 32 : (n + 1) * 32].astype(BF16)
+                    spot = pl.multiple_of(block * COLS + half * HALF, HALF)
+                    outs[n][:, pl.ds(spot, HALF)] = total[n * 32 : (n + 1) * 32].astype(BF16)
         else:
             for n in range(X):
                 low = n & 1
-                upper = flag_ref[n] == 1
+                upper = ((where_ref[2] + n) & (X - 1)) >= 2
+                spot = pl.multiple_of(block * HALF, HALF)
                 for k in range(Y):
                     mine = slice(k * 32 + low * 16, k * 32 + low * 16 + 16)
                     chosen = jnp.where(upper, sums[1][mine], sums[0][mine])
-                    outs[Y + n][k * 16 : (k + 1) * 16] = chosen.astype(BF16)
-
-
-def make_accum(flags, rows, posts):
-    rows = [pltpu.with_memory_space_constraint(value, pltpu.HBM) for value in rows]
-    shapes = [(32, COLS)] * Y + [(64, HALF)] * X
-    outs = pl.pallas_call(
-        accum_kernel,
-        grid_spec=pltpu.PrefetchScalarGridSpec(
-            num_scalar_prefetch=1,
-            grid=(NB,),
-            in_specs=[pl.BlockSpec((ROWS, 2 * COLS), lambda b, f: (0, b))] * G
-            + [pl.BlockSpec((128, ROWS), lambda b, f: (0, 0))] * G,
-            out_specs=[pl.BlockSpec(shape, lambda b, f: (0, b)) for shape in shapes],
-        ),
-        out_shape=[pltpu.VMEM((shape[0], NB * shape[1]), BF16) for shape in shapes],
-        cost_estimate=pl.CostEstimate(flops=0, bytes_accessed=0, transcendentals=0),
-        compiler_params=pltpu.CompilerParams(vmem_limit_bytes=16 * MIB),
-        name="weighted_sums",
-    )(flags, *rows, *posts)
-    return outs[:Y], outs[Y:]
+                    outs[n][k * 16 : (k + 1) * 16, pl.ds(spot, HALF)] = chosen.astype(BF16)
+
+
+def make_accum(part, where, rows, posts):
+    shape = (32, NB * COLS) if part == 0 else (64, NB * HALF)
+    return local(
+        lambda *refs: accum_kernel(part, *refs), "weighted_sums", [(shape, BF16)] * 4, [where],
+        [*rows, *posts], 8,
+    )
 
 
 def added(values):
@@ -387,7 +381,7 @@
 PIECES = [((16, NB * HALF), F32)] + [((16, NB * HALF), BF16)] * 3
 
 
-def first_kernel(flag_ref, *refs):
+def first_kernel(where_ref, *refs):
     outs = refs[4:]
     for block in range(NB):
         start = block * COLS
@@ -395,7 +389,7 @@
         imag = added([ref[:, start + HALF : start + COLS] for ref in refs[:4]])
         for n, out in enumerate(outs):
             mine = slice((n & 1) * 16, (n & 1) * 16 + 16)
-            chosen = jnp.where(flag_ref[n] == 1, imag[mine], real[mine])
+            chosen = jnp.where(((where_ref[2] + n) & (X - 1)) >= 2, imag[mine], real[mine])
             out[:, block * HALF : (block + 1) * HALF] = chosen.astype(out.dtype)
 
 
@@ -404,9 +398,9 @@
         out[...] = added([ref[n * 16 : (n + 1) * 16] for ref in refs[:4]]).astype(out.dtype)
 
 
-def joined_kernel(block_ref, *refs):
+def joined_kernel(where_ref, *refs):
     for n, out in enumerate(refs[8:]):
-        spot = pl.ds(pl.multiple_of(((block_ref[0] + n) % NB) * HALF, HALF), HALF)
+        spot = pl.ds(pl.multiple_of(((where_ref[1] + n) % NB) * HALF, HALF), HALF)
         out[:, :HALF] = added([ref[:, spot] for ref in refs[:4]]).astype(out.dtype)
         out[:, HALF:] = added([ref[:, spot] for ref in refs[4:8]]).astype(out.dtype)
 
@@ -418,33 +412,31 @@
 def per_device(refs, particles, shift_ids, wedge, defocus, inv_sigma):
     dom = lax.axis_index("dom")
     x_at = (dom // 16) * 2 + lax.axis_index("blk") % 2
-    member = (dom % G).astype(jnp.int32).reshape(1)
-    block = ((dom % 16) // G).astype(jnp.int32).reshape(1)
-    flags = (((x_at + jnp.arange(X)) % X) // 2).astype(jnp.int32)
+    where = jnp.stack([dom % G, (dom % 16) // G, x_at]).astype(jnp.int32)
     geo = jnp.asarray(geometry())
 
     gathered = {}
-    own = own_columns(member, refs)
+    own = own_columns(where, refs)
     gathered[0, 0] = own
     gathered[1, 0] = send(own, moves(dy=-1))
     gathered[3, 0] = send(own, moves(dy=1))
-    chunks = split_particles(member, own, particles, shift_ids, wedge, defocus, inv_sigma)
+    chunks = split_particles(where, own, particles, shift_ids, wedge, defocus, inv_sigma)
     got = {0: chunks[0]}
     got[2] = send(chunks[2], partners(2))
     got[1] = send(chunks[1], partners(1))
     gathered[2, 0] = send(own, moves(dy=2))
-    table, geo = make_table(member, geo)
-    wave = [got[1], got[2], gathered[1, 0], gathered[3, 0], gathered[2, 0], table]
+    table, geo = make_table(where, geo)
+    wave = [got[1], got[2], gathered[1, 0], gathered[3, 0], table]
     gathered[0, 1] = send(after(own, *wave), moves(dx=-1))
     gathered[1, 1] = send(after(gathered[1, 0], *wave), moves(dx=-1))
     gathered[3, 1] = send(after(gathered[3, 0], *wave), moves(dx=1))
-    gathered[2, 1] = send(after(gathered[2, 0], *wave), moves(dx=1))
     got[3] = send(after(chunks[3], *wave), partners(3))
     rows, pens = {}, {}
-    rows[0], pens[0] = make_rows(member, after(got[0], *wave), geo, table)
-    rows[1], pens[1] = make_rows(member, after(got[1], rows[0]), geo, table)
-    rows[2], pens[2] = make_rows(member, after(got[2], rows[1]), geo, table)
-    rows[3], pens[3] = make_rows(member, after(got[3], rows[2]), geo, table)
+    rows[0], pens[0] = make_rows(where, after(got[0], *wave), geo, table)
+    gathered[2, 1] = send(after(gathered[2, 0], rows[0]), moves(dx=1))
+    rows[1], pens[1] = make_rows(where, after(got[1], rows[0], gathered[2, 0]), geo, table)
+    rows[2], pens[2] = make_rows(where, after(got[2], rows[1]), geo, table)
+    rows[3], pens[3] = make_rows(where, after(got[3], rows[2]), geo, table)
     blocks = [gathered[ky, kx] for ky in range(Y) for kx in range(2)]
 
     rows = [rows[n] for n in range(G)]
@@ -454,20 +446,21 @@
     posterior = make_posterior([parts[0], *arrived])
     posts = [posterior] + [send(posterior, partners(n)) for n in range(1, G)]
 
-    first, second = make_accum(flags, rows, posts)
+    first = make_accum(0, where, rows, posts)
     first = [first[0]] + [send(first[n], moves(dy=n)) for n in range(1, Y)]
+    second = make_accum(1, where, rows, posts)
     second = [
         second[0],
         send(second[1], moves(dx=1)),
         send(after(second[2], first[1]), moves(dx=2)),
         send(second[3], moves(dx=3)),
     ]
-    first = local(first_kernel, "first_sums", PIECES, [flags], first, 4)
+    first = local(first_kernel, "first_sums", PIECES, [where], first, 4)
     first = [first[0]] + [send(first[n], moves(dx=n)) for n in range(1, X)]
     second = local(second_kernel, "second_sums", PIECES, [], second, 4)
     second = [second[0]] + [send(second[n], moves(dy=n)) for n in range(1, Y)]
     outs = [((16, COLS), F32)] + [((16, COLS), BF16)] * (NB - 1)
-    ends = local(joined_kernel, "joined_sums", outs, [block], [*first, *second], 4)
+    ends = local(joined_kernel, "joined_sums", outs, [where], [*first, *second], 4)
     return added([ends[0]] + [send(ends[n], moves(dz=n * (G // 2))) for n in range(1, NB)])
 
 

time: 111 us -> 111 us (level); the launches traced: 111 us -> 109 us
  waiting for transfers between devices: 27.5 us -> 22.7 us
  starting transfers between devices: 47.4 us -> 49.7 us
    pallas_call x12 -> x14, Pallas kernels: 27.1 us -> 36.1 us  [local(): pl.pallas_call(kernel, in_specs=[SCALARS] * len(scalars) + [PLACED] * pla...]
    pallas_call x1 -> x0, Pallas kernels: 7.99 us -> none  [make_accum(): pl.pallas_call(accum_kernel, grid_spec=pltpu.PrefetchScalarGridSpec(num_s...]
    ppermute x31, waiting for transfers between devices: 27.5 us -> 22.7 us  [send(): return lax.ppermute(value, AXES, pairs)]
    ppermute x31, starting transfers between devices: 47.4 us -> 49.7 us  [send(): return lax.ppermute(value, AXES, pairs)]
  transfers between devices with their start and end apart: 31 -> 31, of which waited for: 14 -> 13; matrix products, arithmetic and copies ran while one was open for 0% -> 0% of each run, Pallas kernels for 17% -> 22%
where the time goes in v6:
time: 111 us; the launch traced here: 109 us
  starting transfers between devices  49.7 us (45%)
  Pallas kernels  36.1 us (33%)
  waiting for transfers between devices  22.7 us (20%)
    ppermute x31, starting transfers between devices, send(): return lax.ppermute(value, AXES, pairs)  49.7 us
    pallas_call x14, Pallas kernels, local(): pl.pallas_call(kernel, in_specs=[SCALARS] * len(scalars) + [PLACED] * pla...  36.1 us
    ppermute x31, waiting for transfers between devices, send(): return lax.ppermute(value, AXES, pairs)  22.7 us
  transfers between devices with their start and end apart: 31, of which 13 were waited for; matrix products, arithmetic and copies ran while one was open for 0% of the time, Pallas kernels for 22%

profile of v6, /device:TPU:2, one launch (start us, length us, event | category | flops | bytes accessed | tf_op | source)
XLA Modules:
  0.0 109.4 jit_solution(7182522614000654340)
XLA Ops:
  1.6 2.5 %split_particles.1 = (bf16[32,8576]{1,0:T(8,128)(2,1)S(1)}, bf16[32,8576]{1,0:T(8,128)(2,1)S(1)}, bf16[32,8576]{1,0:T(8,128)(2,1)S(1)}, bf16[32,8576]{1,0:T(8,128)(2,1)S(1)}) custom-call(s32[3]{0:T(128)S(1)} %pad_add_fusion.where_ref.refs_0_, bf16[32,32768]{1,0:T(8,128)(2,1)} %source.3, s32[8,32]{1,0:T(8,128)} %bitcast.5, s32[32,32]{1,0:T(8,128)} %wedge.1, ...), custom_call_target="tpu_custom_call" | custom-call | tf_op jit(solution)/shard_map/split_particles/pallas_call | solution.py:97
  4.2 2.0 %collective-permute-start.1 = (bf16[32,8576]{1,0:T(8,128)(2,1)S(1)}, bf16[32,8576]{1,0:T(8,128)(2,1)S(1)}, u32[]{:S(2)}, u32[]{:S(2)}) collective-permute-start(bf16[32,8576]{1,0:T(8,128)(2,1)S(1)} %get-tuple-element.55), channel_id=1, source_target_pairs={{0,2},{1,3},{2,0},{3,1},{4,6},{5,7},{6,4},{7,5},{8,10},{9,11},{10,... | collective-permute-start | bytes 1646600 | tf_op jit(solution)/shard_map/ppermute | solution.py:49
  6.2 1.6 %collective-permute-start.3 = (bf16[16,8192]{1,0:T(8,128)(2,1)S(1)}, bf16[16,8192]{1,0:T(8,128)(2,1)S(1)}, u32[]{:S(2)}, u32[]{:S(2)}) collective-permute-start(bf16[16,8192]{1,0:T(8,128)(2,1)S(1)} %own_references.1.after.refs_8_), channel_id=1, source_target_pairs={{0,64},{1,65},{2,66},{3,67},{4,68},{5,69},{6,70},{7,71},{8,72},{9,... | collective-permute-start | bytes 786440 | tf_op jit(solution)/shard_map/ppermute | solution.py:49
  7.8 1.7 %collective-permute-start.2 = (bf16[16,8192]{1,0:T(8,128)(2,1)S(1)}, bf16[16,8192]{1,0:T(8,128)(2,1)S(1)}, u32[]{:S(2)}, u32[]{:S(2)}) collective-permute-start(bf16[16,8192]{1,0:T(8,128)(2,1)S(1)} %own_references.1.after.refs_8_), channel_id=1, source_target_pairs={{0,192},{1,193},{2,194},{3,195},{4,196},{5,197},{6,198},{7,199},{8... | collective-permute-start | bytes 786440 | tf_op jit(solution)/shard_map/ppermute | solution.py:49
  9.4 6.1 %phase_table.1 = (bf16[256,8192]{1,0:T(8,128)(2,1)S(1)}, f32[4,8,1024]{2,1,0:T(8,128)S(1)}) custom-call(s32[3]{0:T(128)S(1)} %pad_add_fusion.where_ref.refs_0_, f32[16,8,1024]{2,1,0:T(8,128)} %constant.63.clone.geo_ref), custom_call_target="tpu_custom_call" | custom-call | tf_op jit(solution)/shard_map/phase_table/pallas_call | solution.py:97
  15.9 3.4 %collective-permute-done.1.x_ref = bf16[32,8576]{1,0:T(8,128)(2,1)S(1)} collective-permute-done((bf16[32,8576]{1,0:T(8,128)(2,1)S(1)}, bf16[32,8576]{1,0:T(8,128)(2,1)S(1)}, u32[]{:S(2)}, u32[]{:S(2)}) %collective-permute-start.1) | collective-permute-done | bytes 548896 | tf_op jit(solution)/shard_map/ppermute | solution.py:49
  20.2 3.2 %collective-permute-start.4 = (bf16[16,8192]{1,0:T(8,128)(2,1)S(1)}, bf16[16,8192]{1,0:T(8,128)(2,1)S(1)}, u32[]{:S(2)}, u32[]{:S(2)}) collective-permute-start(bf16[16,8192]{1,0:T(8,128)(2,1)S(1)} %own_references.1.after.refs_8_), channel_id=1, source_target_pairs={{0,128},{1,129},{2,130},{3,131},{4,132},{5,133},{6,134},{7,135},{8... | collective-permute-start | bytes 786440 | tf_op jit(solution)/shard_map/ppermute | solution.py:49
  24.0 2.8 %collective-permute-start.7 = (bf16[16,8192]{1,0:T(8,128)(2,1)S(1)}, bf16[16,8192]{1,0:T(8,128)(2,1)S(1)}, u32[]{:S(2)}, u32[]{:S(2)}) collective-permute-start(bf16[16,8192]{1,0:T(8,128)(2,1)S(1)} %collective-permute-done.2.refs_10_), channel_id=1, source_target_pairs={{0,48},{1,49},{2,50},{3,51},{4,52},{5,53},{6,54},{7,55},{8,56},{9,... | collective-permute-start | bytes 786440 | tf_op jit(solution)/shard_map/ppermute | solution.py:49
  26.7 3.7 %shifted_rows.4 = (bf16[256,8192]{1,0:T(8,128)(2,1)S(1)}, bf16[32,4096]{1,0:T(8,128)(2,1)S(1)}) custom-call(s32[3]{0:T(128)S(1)} %pad_add_fusion.where_ref.refs_0_, bf16[32,8576]{1,0:T(8,128)(2,1)S(1)} %get-tuple-element.57.x_ref, f32[4,8,1024]{2,1,0:T(8,128)S(1)} %get-tuple-element.58.geo_ref, bf16[256,8192]{1,0:T(8,128)(2,1)S(1)} %get-tuple-element.56.table_ref), custom_call_target="tpu_custom_call" | custom-call | tf_op jit(solution)/shard_map/shifted_rows/pallas_call | solution.py:97
  32.3 3.7 %shifted_rows.5 = (bf16[256,8192]{1,0:T(8,128)(2,1)S(1)}, bf16[32,4096]{1,0:T(8,128)(2,1)S(1)}) custom-call(s32[3]{0:T(128)S(1)} %pad_add_fusion.where_ref.refs_0_, bf16[32,8576]{1,0:T(8,128)(2,1)S(1)} %collective-permute-done.x_ref, f32[4,8,1024]{2,1,0:T(8,128)S(1)} %get-tuple-element.58.geo_ref, bf16[256,8192]{1,0:T(8,128)(2,1)S(1)} %get-tuple-element.56.table_ref), custom_call_target="tpu_custom_call" | custom-call | tf_op jit(solution)/shard_map/shifted_rows/pallas_call | solution.py:97
  36.0 3.7 %shifted_rows.6 = (bf16[256,8192]{1,0:T(8,128)(2,1)S(1)}, bf16[32,4096]{1,0:T(8,128)(2,1)S(1)}) custom-call(s32[3]{0:T(128)S(1)} %pad_add_fusion.where_ref.refs_0_, bf16[32,8576]{1,0:T(8,128)(2,1)S(1)} %collective-permute-done.1.x_ref, f32[4,8,1024]{2,1,0:T(8,128)S(1)} %get-tuple-element.58.geo_ref, bf16[256,8192]{1,0:T(8,128)(2,1)S(1)} %get-tuple-element.56.table_ref), custom_call_target="tpu_custom_call" | custom-call | tf_op jit(solution)/shard_map/shifted_rows/pallas_call | solution.py:97
  39.7 3.7 %shifted_rows.7 = (bf16[256,8192]{1,0:T(8,128)(2,1)S(1)}, bf16[32,4096]{1,0:T(8,128)(2,1)S(1)}) custom-call(s32[3]{0:T(128)S(1)} %pad_add_fusion.where_ref.refs_0_, bf16[32,8576]{1,0:T(8,128)(2,1)S(1)} %collective-permute-done.5.x_ref, f32[4,8,1024]{2,1,0:T(8,128)S(1)} %get-tuple-element.58.geo_ref, bf16[256,8192]{1,0:T(8,128)(2,1)S(1)} %get-tuple-element.56.table_ref), custom_call_target="tpu_custom_call" | custom-call | tf_op jit(solution)/shard_map/shifted_rows/pallas_call | solution.py:97
  43.4 4.8 %partial_scores.1 = (f32[256,128]{1,0:T(8,128)S(1)}, f32[256,128]{1,0:T(8,128)S(1)}, f32[256,128]{1,0:T(8,128)S(1)}, f32[256,128]{1,0:T(8,128)S(1)}) custom-call(bf16[256,8192]{1,0:T(8,128)(2,1)S(1)} %get-tuple-element.59.refs_0_.refs_1_, bf16[256,8192]{1,0:T(8,128)(2,1)S(1)} %get-tuple-element.61.refs_1_.refs_2_, ...), custom_call_target="tpu_custom_call" | custom-call | tf_op jit(solution)/shard_map/partial_scores/pallas_call | solution.py:97
  48.7 1.5 %collective-permute-start.12 = (f32[256,128]{1,0:T(8,128)S(1)}, f32[256,128]{1,0:T(8,128)S(1)}, u32[]{:S(2)}, u32[]{:S(2)}) collective-permute-start(f32[256,128]{1,0:T(8,128)S(1)} %get-tuple-element.79), channel_id=1, source_target_pairs={{0,3},{1,2},{2,1},{3,0},{4,7},{5,6},{6,5},{7,4},{8,11},{9,10},{10,... | collective-permute-start | bytes 393224 | tf_op jit(solution)/shard_map/ppermute | solution.py:49
  50.2 4.5 %collective-permute-done.11.refs_2_ = f32[256,128]{1,0:T(8,128)S(1)} collective-permute-done((f32[256,128]{1,0:T(8,128)S(1)}, f32[256,128]{1,0:T(8,128)S(1)}, u32[]{:S(2)}, u32[]{:S(2)}) %collective-permute-start.11) | collective-permute-done | bytes 131104 | tf_op jit(solution)/shard_map/ppermute | solution.py:49
  54.7 1.9 %collective-permute-done.12.refs_3_ = f32[256,128]{1,0:T(8,128)S(1)} collective-permute-done((f32[256,128]{1,0:T(8,128)S(1)}, f32[256,128]{1,0:T(8,128)S(1)}, u32[]{:S(2)}, u32[]{:S(2)}) %collective-permute-start.12) | collective-permute-done | bytes 131104 | tf_op jit(solution)/shard_map/ppermute | solution.py:49
  57.2 1.8 %collective-permute-start.14 = (bf16[128,256]{1,0:T(8,128)(2,1)S(1)}, bf16[128,256]{1,0:T(8,128)(2,1)S(1)}, u32[]{:S(2)}, u32[]{:S(2)}) collective-permute-start(bf16[128,256]{1,0:T(8,128)(2,1)S(1)} %posterior.1.refs_5_), channel_id=1, source_target_pairs={{0,2},{1,3},{2,0},{3,1},{4,6},{5,7},{6,4},{7,5},{8,10},{9,11},{10,... | collective-permute-start | bytes 196616 | tf_op jit(solution)/shard_map/ppermute | solution.py:49
  58.9 2.1 %collective-permute-done.15.refs_8_ = bf16[128,256]{1,0:T(8,128)(2,1)S(1)} collective-permute-done((bf16[128,256]{1,0:T(8,128)(2,1)S(1)}, bf16[128,256]{1,0:T(8,128)(2,1)S(1)}, u32[]{:S(2)}, u32[]{:S(2)}) %collective-permute-start.15) | collective-permute-done | bytes 65568 | tf_op jit(solution)/shard_map/ppermute | solution.py:49
  61.0 1.8 %collective-permute-done.14.refs_7_ = bf16[128,256]{1,0:T(8,128)(2,1)S(1)} collective-permute-done((bf16[128,256]{1,0:T(8,128)(2,1)S(1)}, bf16[128,256]{1,0:T(8,128)(2,1)S(1)}, u32[]{:S(2)}, u32[]{:S(2)}) %collective-permute-start.14) | collective-permute-done | bytes 65568 | tf_op jit(solution)/shard_map/ppermute | solution.py:49
  62.8 2.4 %weighted_sums.2 = (bf16[32,4096]{1,0:T(8,128)(2,1)S(1)}, bf16[32,4096]{1,0:T(8,128)(2,1)S(1)}, bf16[32,4096]{1,0:T(8,128)(2,1)S(1)}, bf16[32,4096]{1,0:T(8,128)(2,1)S(1)}) custom-call(s32[3]{0:T(128)S(1)} %pad_add_fusion.where_ref.refs_0_, bf16[256,8192]{1,0:T(8,128)(2,1)S(1)} %get-tuple-element.59.refs_0_.refs_1_, ...), custom_call_target="tpu_custom_call" | custom-call | tf_op jit(solution)/shard_map/weighted_sums/pallas_call | solution.py:97
  65.2 1.7 %collective-permute-start.16 = (bf16[32,4096]{1,0:T(8,128)(2,1)S(1)}, bf16[32,4096]{1,0:T(8,128)(2,1)S(1)}, u32[]{:S(2)}, u32[]{:S(2)}) collective-permute-start(bf16[32,4096]{1,0:T(8,128)(2,1)S(1)} %get-tuple-element.81), channel_id=1, source_target_pairs={{0,64},{1,65},{2,66},{3,67},{4,68},{5,69},{6,70},{7,71},{8,72},{9,... | collective-permute-start | bytes 786440 | tf_op jit(solution)/shard_map/ppermute | solution.py:49
  66.8 2.9 %collective-permute-start.17 = (bf16[32,4096]{1,0:T(8,128)(2,1)S(1)}, bf16[32,4096]{1,0:T(8,128)(2,1)S(1)}, u32[]{:S(2)}, u32[]{:S(2)}) collective-permute-start(bf16[32,4096]{1,0:T(8,128)(2,1)S(1)} %get-tuple-element.82), channel_id=1, source_target_pairs={{0,128},{1,129},{2,130},{3,131},{4,132},{5,133},{6,134},{7,135},{8... | collective-permute-start | bytes 786440 | tf_op jit(solution)/shard_map/ppermute | solution.py:49
  71.1 2.4 %weighted_sums.3 = (bf16[64,2048]{1,0:T(8,128)(2,1)S(1)}, bf16[64,2048]{1,0:T(8,128)(2,1)S(1)}, bf16[64,2048]{1,0:T(8,128)(2,1)S(1)}, bf16[64,2048]{1,0:T(8,128)(2,1)S(1)}) custom-call(s32[3]{0:T(128)S(1)} %pad_add_fusion.where_ref.refs_0_, bf16[256,8192]{1,0:T(8,128)(2,1)S(1)} %get-tuple-element.59.refs_0_.refs_1_, ...), custom_call_target="tpu_custom_call" | custom-call | tf_op jit(solution)/shard_map/weighted_sums/pallas_call | solution.py:97
  75.6 2.5 %collective-permute-start.23 = (bf16[64,2048]{1,0:T(8,128)(2,1)S(1)}, bf16[64,2048]{1,0:T(8,128)(2,1)S(1)}, u32[]{:S(2)}, u32[]{:S(2)}) collective-permute-start(bf16[64,2048]{1,0:T(8,128)(2,1)S(1)} %get-tuple-element.91), channel_id=1, source_target_pairs={{0,16},{1,17},{2,18},{3,19},{4,20},{5,21},{6,22},{7,23},{8,24},{9,... | collective-permute-start | bytes 786440 | tf_op jit(solution)/shard_map/ppermute | solution.py:49
  78.1 3.1 %collective-permute-done.17.refs_2_ = bf16[32,4096]{1,0:T(8,128)(2,1)S(1)} collective-permute-done((bf16[32,4096]{1,0:T(8,128)(2,1)S(1)}, bf16[32,4096]{1,0:T(8,128)(2,1)S(1)}, u32[]{:S(2)}, u32[]{:S(2)}) %collective-permute-start.17) | collective-permute-done | bytes 262176 | tf_op jit(solution)/shard_map/ppermute | solution.py:49
  84.6 1.9 %collective-permute-start.21 = (bf16[16,2048]{1,0:T(8,128)(2,1)S(1)}, bf16[16,2048]{1,0:T(8,128)(2,1)S(1)}, u32[]{:S(2)}, u32[]{:S(2)}) collective-permute-start(bf16[16,2048]{1,0:T(8,128)(2,1)S(1)} %get-tuple-element.87), channel_id=1, source_target_pairs={{0,48},{1,49},{2,50},{3,51},{4,52},{5,53},{6,54},{7,55},{8,56},{9,... | collective-permute-start | bytes 196616 | tf_op jit(solution)/shard_map/ppermute | solution.py:49
  86.5 1.7 %collective-permute-done.23.refs_2_ = bf16[64,2048]{1,0:T(8,128)(2,1)S(1)} collective-permute-done((bf16[64,2048]{1,0:T(8,128)(2,1)S(1)}, bf16[64,2048]{1,0:T(8,128)(2,1)S(1)}, u32[]{:S(2)}, u32[]{:S(2)}) %collective-permute-start.23) | collective-permute-done | bytes 262176 | tf_op jit(solution)/shard_map/ppermute | solution.py:49
  88.5 3.2 %collective-permute-start.26 = (bf16[16,2048]{1,0:T(8,128)(2,1)S(1)}, bf16[16,2048]{1,0:T(8,128)(2,1)S(1)}, u32[]{:S(2)}, u32[]{:S(2)}) collective-permute-start(bf16[16,2048]{1,0:T(8,128)(2,1)S(1)} %get-tuple-element.95), channel_id=1, source_target_pairs={{0,128},{1,129},{2,130},{3,131},{4,132},{5,133},{6,134},{7,135},{8... | collective-permute-start | bytes 196616 | tf_op jit(solution)/shard_map/ppermute | solution.py:49
  91.6 2.5 %collective-permute-start.27 = (bf16[16,2048]{1,0:T(8,128)(2,1)S(1)}, bf16[16,2048]{1,0:T(8,128)(2,1)S(1)}, u32[]{:S(2)}, u32[]{:S(2)}) collective-permute-start(bf16[16,2048]{1,0:T(8,128)(2,1)S(1)} %get-tuple-element.96), channel_id=1, source_target_pairs={{0,192},{1,193},{2,194},{3,195},{4,196},{5,197},{6,198},{7,199},{8... | collective-permute-start | bytes 196616 | tf_op jit(solution)/shard_map/ppermute | solution.py:49
  96.7 3.3 %collective-permute-start.28 = (bf16[16,1024]{1,0:T(8,128)(2,1)S(1)}, bf16[16,1024]{1,0:T(8,128)(2,1)S(1)}, u32[]{:S(2)}, u32[]{:S(2)}) collective-permute-start(bf16[16,1024]{1,0:T(8,128)(2,1)S(1)} %get-tuple-element.98), channel_id=1, source_target_pairs={{0,4},{1,5},{2,6},{3,7},{4,8},{5,9},{6,10},{7,11},{8,12},{9,13},{1... | collective-permute-start | bytes 98312 | tf_op jit(solution)/shard_map/ppermute | solution.py:49
  100.0 3.9 %collective-permute-start.29 = (bf16[16,1024]{1,0:T(8,128)(2,1)S(1)}, bf16[16,1024]{1,0:T(8,128)(2,1)S(1)}, u32[]{:S(2)}, u32[]{:S(2)}) collective-permute-start(bf16[16,1024]{1,0:T(8,128)(2,1)S(1)} %get-tuple-element.99), channel_id=1, source_target_pairs={{0,8},{1,9},{2,10},{3,11},{4,12},{5,13},{6,14},{7,15},{8,0},{9,1},... | collective-permute-start | bytes 98312 | tf_op jit(solution)/shard_map/ppermute | solution.py:49
  103.9 3.2 %collective-permute-start.30 = (bf16[16,1024]{1,0:T(8,128)(2,1)S(1)}, bf16[16,1024]{1,0:T(8,128)(2,1)S(1)}, u32[]{:S(2)}, u32[]{:S(2)}) collective-permute-start(bf16[16,1024]{1,0:T(8,128)(2,1)S(1)} %get-tuple-element.100), channel_id=1, source_target_pairs={{0,12},{1,13},{2,14},{3,15},{4,0},{5,1},{6,2},{7,3},{8,4},{9,5},{1... | collective-permute-start | bytes 98312 | tf_op jit(solution)/shard_map/ppermute | solution.py:49
  (46 shorter events, 18.3 us)
Async XLA Ops:
  4.1 11.8 %collective-permute-start = (bf16[32,8576]{1,0:T(8,128)(2,1)S(1)}, bf16[32,8576]{1,0:T(8,128)(2,1)S(1)}, u32[]{:S(2)}, u32[]{:S(2)}) collective-permute-start(bf16[32,8576]{1,0:T(8,128)(2,1)S(1)} %get-tuple-element.54), channel_id=1, source_target_pairs={{0,1},{1,0},{2,3},{3,2},{4,5},{5,4},{6,7},{7,6},{8,9},{9,8},{10,11... | collective-permute-start | bytes 1646600 | tf_op jit(solution)/shard_map/ppermute | solution.py:49
  4.2 15.0 %collective-permute-start.1 = (bf16[32,8576]{1,0:T(8,128)(2,1)S(1)}, bf16[32,8576]{1,0:T(8,128)(2,1)S(1)}, u32[]{:S(2)}, u32[]{:S(2)}) collective-permute-start(bf16[32,8576]{1,0:T(8,128)(2,1)S(1)} %get-tuple-element.55), channel_id=1, source_target_pairs={{0,2},{1,3},{2,0},{3,1},{4,6},{5,7},{6,4},{7,5},{8,10},{9,11},{10,... | collective-permute-start | bytes 1646600 | tf_op jit(solution)/shard_map/ppermute | solution.py:49
  6.2 9.6 %collective-permute-start.3 = (bf16[16,8192]{1,0:T(8,128)(2,1)S(1)}, bf16[16,8192]{1,0:T(8,128)(2,1)S(1)}, u32[]{:S(2)}, u32[]{:S(2)}) collective-permute-start(bf16[16,8192]{1,0:T(8,128)(2,1)S(1)} %own_references.1.after.refs_8_), channel_id=1, source_target_pairs={{0,64},{1,65},{2,66},{3,67},{4,68},{5,69},{6,70},{7,71},{8,72},{9,... | collective-permute-start | bytes 786440 | tf_op jit(solution)/shard_map/ppermute | solution.py:49
  7.8 8.1 %collective-permute-start.2 = (bf16[16,8192]{1,0:T(8,128)(2,1)S(1)}, bf16[16,8192]{1,0:T(8,128)(2,1)S(1)}, u32[]{:S(2)}, u32[]{:S(2)}) collective-permute-start(bf16[16,8192]{1,0:T(8,128)(2,1)S(1)} %own_references.1.after.refs_8_), channel_id=1, source_target_pairs={{0,192},{1,193},{2,194},{3,195},{4,196},{5,197},{6,198},{7,199},{8... | collective-permute-start | bytes 786440 | tf_op jit(solution)/shard_map/ppermute | solution.py:49
  19.2 20.5 %collective-permute-start.5 = (bf16[32,8576]{1,0:T(8,128)(2,1)S(1)}, bf16[32,8576]{1,0:T(8,128)(2,1)S(1)}, u32[]{:S(2)}, u32[]{:S(2)}) collective-permute-start(bf16[32,8576]{1,0:T(8,128)(2,1)S(1)} %get-tuple-element.65), channel_id=1, source_target_pairs={{0,3},{1,2},{2,1},{3,0},{4,7},{5,6},{6,5},{7,4},{8,11},{9,10},{10,... | collective-permute-start | bytes 1646600 | tf_op jit(solution)/shard_map/ppermute | solution.py:49
  20.2 10.6 %collective-permute-start.4 = (bf16[16,8192]{1,0:T(8,128)(2,1)S(1)}, bf16[16,8192]{1,0:T(8,128)(2,1)S(1)}, u32[]{:S(2)}, u32[]{:S(2)}) collective-permute-start(bf16[16,8192]{1,0:T(8,128)(2,1)S(1)} %own_references.1.after.refs_8_), channel_id=1, source_target_pairs={{0,128},{1,129},{2,130},{3,131},{4,132},{5,133},{6,134},{7,135},{8... | collective-permute-start | bytes 786440 | tf_op jit(solution)/shard_map/ppermute | solution.py:49
  23.4 20.0 %collective-permute-start.6 = (bf16[16,8192]{1,0:T(8,128)(2,1)S(1)}, bf16[16,8192]{1,0:T(8,128)(2,1)S(1)}, u32[]{:S(2)}, u32[]{:S(2)}) collective-permute-start(bf16[16,8192]{1,0:T(8,128)(2,1)S(1)} %own_references.1.after.refs_8_), channel_id=1, source_target_pairs={{0,48},{1,49},{2,50},{3,51},{4,52},{5,53},{6,54},{7,55},{8,56},{9,... | collective-permute-start | bytes 786440 | tf_op jit(solution)/shard_map/ppermute | solution.py:49
  24.0 19.4 %collective-permute-start.7 = (bf16[16,8192]{1,0:T(8,128)(2,1)S(1)}, bf16[16,8192]{1,0:T(8,128)(2,1)S(1)}, u32[]{:S(2)}, u32[]{:S(2)}) collective-permute-start(bf16[16,8192]{1,0:T(8,128)(2,1)S(1)} %collective-permute-done.2.refs_10_), channel_id=1, source_target_pairs={{0,48},{1,49},{2,50},{3,51},{4,52},{5,53},{6,54},{7,55},{8,56},{9,... | collective-permute-start | bytes 786440 | tf_op jit(solution)/shard_map/ppermute | solution.py:49
  26.7 16.7 %collective-permute-start.9 = (bf16[16,8192]{1,0:T(8,128)(2,1)S(1)}, bf16[16,8192]{1,0:T(8,128)(2,1)S(1)}, u32[]{:S(2)}, u32[]{:S(2)}) collective-permute-start(bf16[16,8192]{1,0:T(8,128)(2,1)S(1)} %collective-permute-done.3.refs_14_), channel_id=1, source_target_pairs={{0,32},{1,33},{2,34},{3,35},{4,36},{5,37},{6,38},{7,39},{8,40},{9,... | collective-permute-start | bytes 786440 | tf_op jit(solution)/shard_map/ppermute | solution.py:49
  30.8 12.6 %collective-permute-start.8 = (bf16[16,8192]{1,0:T(8,128)(2,1)S(1)}, bf16[16,8192]{1,0:T(8,128)(2,1)S(1)}, u32[]{:S(2)}, u32[]{:S(2)}) collective-permute-start(bf16[16,8192]{1,0:T(8,128)(2,1)S(1)} %collective-permute-done.4.refs_12_), channel_id=1, source_target_pairs={{0,32},{1,33},{2,34},{3,35},{4,36},{5,37},{6,38},{7,39},{8,40},{9,... | collective-permute-start | bytes 786440 | tf_op jit(solution)/shard_map/ppermute | solution.py:49
  48.2 2.0 %collective-permute-start.10 = (f32[256,128]{1,0:T(8,128)S(1)}, f32[256,128]{1,0:T(8,128)S(1)}, u32[]{:S(2)}, u32[]{:S(2)}) collective-permute-start(f32[256,128]{1,0:T(8,128)S(1)} %get-tuple-element.77), channel_id=1, source_target_pairs={{0,1},{1,0},{2,3},{3,2},{4,5},{5,4},{6,7},{7,6},{8,9},{9,8},{10,11... | collective-permute-start | bytes 393224 | tf_op jit(solution)/shard_map/ppermute | solution.py:49
  48.3 6.4 %collective-permute-start.11 = (f32[256,128]{1,0:T(8,128)S(1)}, f32[256,128]{1,0:T(8,128)S(1)}, u32[]{:S(2)}, u32[]{:S(2)}) collective-permute-start(f32[256,128]{1,0:T(8,128)S(1)} %get-tuple-element.78), channel_id=1, source_target_pairs={{0,2},{1,3},{2,0},{3,1},{4,6},{5,7},{6,4},{7,5},{8,10},{9,11},{10,... | collective-permute-start | bytes 393224 | tf_op jit(solution)/shard_map/ppermute | solution.py:49
  48.7 7.9 %collective-permute-start.12 = (f32[256,128]{1,0:T(8,128)S(1)}, f32[256,128]{1,0:T(8,128)S(1)}, u32[]{:S(2)}, u32[]{:S(2)}) collective-permute-start(f32[256,128]{1,0:T(8,128)S(1)} %get-tuple-element.79), channel_id=1, source_target_pairs={{0,3},{1,2},{2,1},{3,0},{4,7},{5,6},{6,5},{7,4},{8,11},{9,10},{10,... | collective-permute-start | bytes 393224 | tf_op jit(solution)/shard_map/ppermute | solution.py:49
  56.9 4.1 %collective-permute-start.15 = (bf16[128,256]{1,0:T(8,128)(2,1)S(1)}, bf16[128,256]{1,0:T(8,128)(2,1)S(1)}, u32[]{:S(2)}, u32[]{:S(2)}) collective-permute-start(bf16[128,256]{1,0:T(8,128)(2,1)S(1)} %posterior.1.refs_5_), channel_id=1, source_target_pairs={{0,3},{1,2},{2,1},{3,0},{4,7},{5,6},{6,5},{7,4},{8,11},{9,10},{10,... | collective-permute-start | bytes 196616 | tf_op jit(solution)/shard_map/ppermute | solution.py:49
  57.2 5.6 %collective-permute-start.14 = (bf16[128,256]{1,0:T(8,128)(2,1)S(1)}, bf16[128,256]{1,0:T(8,128)(2,1)S(1)}, u32[]{:S(2)}, u32[]{:S(2)}) collective-permute-start(bf16[128,256]{1,0:T(8,128)(2,1)S(1)} %posterior.1.refs_5_), channel_id=1, source_target_pairs={{0,2},{1,3},{2,0},{3,1},{4,6},{5,7},{6,4},{7,5},{8,10},{9,11},{10,... | collective-permute-start | bytes 196616 | tf_op jit(solution)/shard_map/ppermute | solution.py:49
  58.9 3.9 %collective-permute-start.13 = (bf16[128,256]{1,0:T(8,128)(2,1)S(1)}, bf16[128,256]{1,0:T(8,128)(2,1)S(1)}, u32[]{:S(2)}, u32[]{:S(2)}) collective-permute-start(bf16[128,256]{1,0:T(8,128)(2,1)S(1)} %posterior.1.refs_5_), channel_id=1, source_target_pairs={{0,1},{1,0},{2,3},{3,2},{4,5},{5,4},{6,7},{7,6},{8,9},{9,8},{10,11... | collective-permute-start | bytes 196616 | tf_op jit(solution)/shard_map/ppermute | solution.py:49
  65.2 10.4 %collective-permute-start.16 = (bf16[32,4096]{1,0:T(8,128)(2,1)S(1)}, bf16[32,4096]{1,0:T(8,128)(2,1)S(1)}, u32[]{:S(2)}, u32[]{:S(2)}) collective-permute-start(bf16[32,4096]{1,0:T(8,128)(2,1)S(1)} %get-tuple-element.81), channel_id=1, source_target_pairs={{0,64},{1,65},{2,66},{3,67},{4,68},{5,69},{6,70},{7,71},{8,72},{9,... | collective-permute-start | bytes 786440 | tf_op jit(solution)/shard_map/ppermute | solution.py:49
  66.8 14.4 %collective-permute-start.17 = (bf16[32,4096]{1,0:T(8,128)(2,1)S(1)}, bf16[32,4096]{1,0:T(8,128)(2,1)S(1)}, u32[]{:S(2)}, u32[]{:S(2)}) collective-permute-start(bf16[32,4096]{1,0:T(8,128)(2,1)S(1)} %get-tuple-element.82), channel_id=1, source_target_pairs={{0,128},{1,129},{2,130},{3,131},{4,132},{5,133},{6,134},{7,135},{8... | collective-permute-start | bytes 786440 | tf_op jit(solution)/shard_map/ppermute | solution.py:49
  69.7 11.5 %collective-permute-start.18 = (bf16[32,4096]{1,0:T(8,128)(2,1)S(1)}, bf16[32,4096]{1,0:T(8,128)(2,1)S(1)}, u32[]{:S(2)}, u32[]{:S(2)}) collective-permute-start(bf16[32,4096]{1,0:T(8,128)(2,1)S(1)} %get-tuple-element.83), channel_id=1, source_target_pairs={{0,192},{1,193},{2,194},{3,195},{4,196},{5,197},{6,198},{7,199},{8... | collective-permute-start | bytes 786440 | tf_op jit(solution)/shard_map/ppermute | solution.py:49
  73.5 11.1 %collective-permute-start.22 = (bf16[64,2048]{1,0:T(8,128)(2,1)S(1)}, bf16[64,2048]{1,0:T(8,128)(2,1)S(1)}, u32[]{:S(2)}, u32[]{:S(2)}) collective-permute-start(bf16[64,2048]{1,0:T(8,128)(2,1)S(1)} %get-tuple-element.89), channel_id=1, source_target_pairs={{0,32},{1,33},{2,34},{3,35},{4,36},{5,37},{6,38},{7,39},{8,40},{9,... | collective-permute-start | bytes 786440 | tf_op jit(solution)/shard_map/ppermute | solution.py:49
  74.8 11.7 %collective-permute-start.24 = (bf16[64,2048]{1,0:T(8,128)(2,1)S(1)}, bf16[64,2048]{1,0:T(8,128)(2,1)S(1)}, u32[]{:S(2)}, u32[]{:S(2)}) collective-permute-start(bf16[64,2048]{1,0:T(8,128)(2,1)S(1)} %get-tuple-element.92), channel_id=1, source_target_pairs={{0,48},{1,49},{2,50},{3,51},{4,52},{5,53},{6,54},{7,55},{8,56},{9,... | collective-permute-start | bytes 786440 | tf_op jit(solution)/shard_map/ppermute | solution.py:49
  75.6 12.6 %collective-permute-start.23 = (bf16[64,2048]{1,0:T(8,128)(2,1)S(1)}, bf16[64,2048]{1,0:T(8,128)(2,1)S(1)}, u32[]{:S(2)}, u32[]{:S(2)}) collective-permute-start(bf16[64,2048]{1,0:T(8,128)(2,1)S(1)} %get-tuple-element.91), channel_id=1, source_target_pairs={{0,16},{1,17},{2,18},{3,19},{4,20},{5,21},{6,22},{7,23},{8,24},{9,... | collective-permute-start | bytes 786440 | tf_op jit(solution)/shard_map/ppermute | solution.py:49
  81.9 9.7 %collective-permute-start.19 = (bf16[16,2048]{1,0:T(8,128)(2,1)S(1)}, bf16[16,2048]{1,0:T(8,128)(2,1)S(1)}, u32[]{:S(2)}, u32[]{:S(2)}) collective-permute-start(bf16[16,2048]{1,0:T(8,128)(2,1)S(1)} %get-tuple-element.85), channel_id=1, source_target_pairs={{0,32},{1,33},{2,34},{3,35},{4,36},{5,37},{6,38},{7,39},{8,40},{9,... | collective-permute-start | bytes 196616 | tf_op jit(solution)/shard_map/ppermute | solution.py:49
  83.2 10.9 %collective-permute-start.20 = (bf16[16,2048]{1,0:T(8,128)(2,1)S(1)}, bf16[16,2048]{1,0:T(8,128)(2,1)S(1)}, u32[]{:S(2)}, u32[]{:S(2)}) collective-permute-start(bf16[16,2048]{1,0:T(8,128)(2,1)S(1)} %get-tuple-element.86), channel_id=1, source_target_pairs={{0,16},{1,17},{2,18},{3,19},{4,20},{5,21},{6,22},{7,23},{8,24},{9,... | collective-permute-start | bytes 196616 | tf_op jit(solution)/shard_map/ppermute | solution.py:49
  84.6 9.5 %collective-permute-start.21 = (bf16[16,2048]{1,0:T(8,128)(2,1)S(1)}, bf16[16,2048]{1,0:T(8,128)(2,1)S(1)}, u32[]{:S(2)}, u32[]{:S(2)}) collective-permute-start(bf16[16,2048]{1,0:T(8,128)(2,1)S(1)} %get-tuple-element.87), channel_id=1, source_target_pairs={{0,48},{1,49},{2,50},{3,51},{4,52},{5,53},{6,54},{7,55},{8,56},{9,... | collective-permute-start | bytes 196616 | tf_op jit(solution)/shard_map/ppermute | solution.py:49
  88.4 6.3 %collective-permute-start.25 = (bf16[16,2048]{1,0:T(8,128)(2,1)S(1)}, bf16[16,2048]{1,0:T(8,128)(2,1)S(1)}, u32[]{:S(2)}, u32[]{:S(2)}) collective-permute-start(bf16[16,2048]{1,0:T(8,128)(2,1)S(1)} %get-tuple-element.94), channel_id=1, source_target_pairs={{0,64},{1,65},{2,66},{3,67},{4,68},{5,69},{6,70},{7,71},{8,72},{9,... | collective-permute-start | bytes 196616 | tf_op jit(solution)/shard_map/ppermute | solution.py:49
  88.5 6.2 %collective-permute-start.26 = (bf16[16,2048]{1,0:T(8,128)(2,1)S(1)}, bf16[16,2048]{1,0:T(8,128)(2,1)S(1)}, u32[]{:S(2)}, u32[]{:S(2)}) collective-permute-start(bf16[16,2048]{1,0:T(8,128)(2,1)S(1)} %get-tuple-element.95), channel_id=1, source_target_pairs={{0,128},{1,129},{2,130},{3,131},{4,132},{5,133},{6,134},{7,135},{8... | collective-permute-start | bytes 196616 | tf_op jit(solution)/shard_map/ppermute | solution.py:49
  91.6 4.4 %collective-permute-start.27 = (bf16[16,2048]{1,0:T(8,128)(2,1)S(1)}, bf16[16,2048]{1,0:T(8,128)(2,1)S(1)}, u32[]{:S(2)}, u32[]{:S(2)}) collective-permute-start(bf16[16,2048]{1,0:T(8,128)(2,1)S(1)} %get-tuple-element.96), channel_id=1, source_target_pairs={{0,192},{1,193},{2,194},{3,195},{4,196},{5,197},{6,198},{7,199},{8... | collective-permute-start | bytes 196616 | tf_op jit(solution)/shard_map/ppermute | solution.py:49
  96.7 10.5 %collective-permute-start.28 = (bf16[16,1024]{1,0:T(8,128)(2,1)S(1)}, bf16[16,1024]{1,0:T(8,128)(2,1)S(1)}, u32[]{:S(2)}, u32[]{:S(2)}) collective-permute-start(bf16[16,1024]{1,0:T(8,128)(2,1)S(1)} %get-tuple-element.98), channel_id=1, source_target_pairs={{0,4},{1,5},{2,6},{3,7},{4,8},{5,9},{6,10},{7,11},{8,12},{9,13},{1... | collective-permute-start | bytes 98312 | tf_op jit(solution)/shard_map/ppermute | solution.py:49
  100.0 7.8 %collective-permute-start.29 = (bf16[16,1024]{1,0:T(8,128)(2,1)S(1)}, bf16[16,1024]{1,0:T(8,128)(2,1)S(1)}, u32[]{:S(2)}, u32[]{:S(2)}) collective-permute-start(bf16[16,1024]{1,0:T(8,128)(2,1)S(1)} %get-tuple-element.99), channel_id=1, source_target_pairs={{0,8},{1,9},{2,10},{3,11},{4,12},{5,13},{6,14},{7,15},{8,0},{9,1},... | collective-permute-start | bytes 98312 | tf_op jit(solution)/shard_map/ppermute | solution.py:49
  103.9 4.8 %collective-permute-start.30 = (bf16[16,1024]{1,0:T(8,128)(2,1)S(1)}, bf16[16,1024]{1,0:T(8,128)(2,1)S(1)}, u32[]{:S(2)}, u32[]{:S(2)}) collective-permute-start(bf16[16,1024]{1,0:T(8,128)(2,1)S(1)} %get-tuple-element.100), channel_id=1, source_target_pairs={{0,12},{1,13},{2,14},{3,15},{4,0},{5,1},{6,2},{7,3},{8,4},{9,5},{1... | collective-permute-start | bytes 98312 | tf_op jit(solution)/shard_map/ppermute | solution.py:49

commit v7 on v6

--- a/solution.py
+++ b/solution.py
@@ -110,9 +110,9 @@
     )
 
 
-def table_kernel(where_ref, geo_ref, out_ref, picked_ref, sems):
+def table_kernel(member_ref, geo_ref, out_ref, picked_ref, sems):
     copies = [
-        pltpu.make_async_copy(geo_ref.at[block * G + where_ref[0]], picked_ref.at[block], sems.at[block])
+        pltpu.make_async_copy(geo_ref.at[block * G + member_ref[0]], picked_ref.at[block], sems.at[block])
         for block in range(NB)
     ]
     for copy in copies:
@@ -144,9 +144,9 @@
                 out_ref[128:256, pl.ds(spot, HALF)] = low
 
 
-def make_table(where, geo):
+def make_table(member, geo):
     return local(
-        table_kernel, "phase_table", [((256, WIDTH), BF16), ((NB, 8, COLS), F32)], [where], [geo], 8,
+        table_kernel, "phase_table", [((256, WIDTH), BF16), ((NB, 8, COLS), F32)], [member], [geo], 8,
         placed=1, scratch=[pltpu.SemaphoreType.DMA((NB,))],
     )
 
@@ -166,17 +166,17 @@
     ]
 
 
-def own_kernel(where_ref, source, out, sems):
-    copies = pieces_of(source, out, where_ref[0], sems, 0)
+def own_kernel(member_ref, source, after, out, sems):
+    copies = pieces_of(source, out, member_ref[0], sems, 0)
     for copy in copies:
         copy.start()
     for copy in copies:
         copy.wait()
 
 
-def own_columns(where, refs):
+def own_columns(member, refs, after):
     (own,) = local(
-        own_kernel, "own_references", [((16, WIDTH), BF16)], [where], [refs], 4,
+        own_kernel, "own_references", [((16, WIDTH), BF16)], [member], [refs, after], 4,
         placed=1, scratch=[pltpu.SemaphoreType.DMA((2 * NB,))],
     )
     return own
@@ -200,11 +200,11 @@
     )
 
 
-def split_kernel(where_ref, source, ids, wedge, focus, sigma, after, *refs):
+def split_kernel(member_ref, block_ref, x_ref, source, ids, wedge, focus, sigma, *refs):
     outs, (ids_in, wedge_in, focus_in, sigma_in, sems, more) = refs[:G], refs[G:]
     copies = []
     for n in (2, 1, 3, 0):
-        copies += pieces_of(source, outs[n], where_ref[0] ^ n, sems, n * 2 * NB)
+        copies += pieces_of(source, outs[n], member_ref[0] ^ n, sems, n * 2 * NB)
     settings = [
         pltpu.make_async_copy(at, to, more.at[n])
         for n, (at, to) in enumerate(
@@ -234,10 +234,10 @@
         copy.wait()
 
 
-def split_particles(where, after, particles, shift_ids, wedge, defocus, inv_sigma):
+def split_particles(place, particles, shift_ids, wedge, defocus, inv_sigma):
     return local(
-        split_kernel, "split_particles", [((P_DEV, WIDTH + EXTRA), BF16)] * G, [where],
-        [particles, shift_ids.T, wedge, defocus, inv_sigma[None], after], 4, placed=5,
+        split_kernel, "split_particles", [((P_DEV, WIDTH + EXTRA), BF16)] * G, place,
+        [particles, shift_ids.T, wedge, defocus, inv_sigma[None]], 4, placed=5,
         scratch=[
             pltpu.VMEM((SHIFTS, P_DEV), jnp.int32),
             pltpu.VMEM((P_DEV, TILTS), jnp.int32),
@@ -249,7 +249,7 @@
     )
 
 
-def rows_kernel(where_ref, x_ref, geo_ref, table_ref, rows_ref, pen_ref):
+def rows_kernel(member_ref, x_ref, geo_ref, table_ref, rows_ref, pen_ref):
     info = sum(x_ref[:, WIDTH + n * 128 : WIDTH + (n + 1) * 128].astype(F32) for n in range(3))
     lane = lax.broadcasted_iota(jnp.int32, (ROWS, 256), 1) & 127
     ids = jnp.concatenate([info[:, s : s + 1] for s in range(SHIFTS)], axis=0)
@@ -259,7 +259,7 @@
 
     @pl.loop(0, NB)
     def _(block):
-        first = 2 * (block * G + where_ref[0]) + 16
+        first = 2 * (block * G + member_ref[0]) + 16
         start = pl.multiple_of(block * 2 * COLS, 2 * COLS)
         for tilt in range(2):
             kept = jnp.sum(jnp.where(small == first + tilt, info, 0.0), axis=1, keepdims=True)
@@ -280,9 +280,9 @@
             rows_ref[:, upper] = (imag * cosine - real * sine).reshape(ROWS, HALF).astype(BF16)
 
 
-def make_rows(where, x, geo, table):
+def make_rows(member, x, geo, table):
     return local(
-        rows_kernel, "shifted_rows", [((ROWS, WIDTH), BF16), ((P_DEV, NB * COLS), BF16)], [where],
+        rows_kernel, "shifted_rows", [((ROWS, WIDTH), BF16), ((P_DEV, NB * COLS), BF16)], [member],
         [x, geo, table], 12,
     )
 
@@ -333,7 +333,7 @@
     return out
 
 
-def accum_kernel(part, where_ref, *refs):
+def accum_kernel(part, x_ref, *refs):
     rows, posts, outs = refs[:G], refs[G : 2 * G], refs[2 * G :]
 
     @pl.loop(0, NB)
@@ -355,7 +355,7 @@
         else:
             for n in range(X):
                 low = n & 1
-                upper = ((where_ref[2] + n) & (X - 1)) >= 2
+                upper = ((x_ref[0] + n) & (X - 1)) >= 2
                 spot = pl.multiple_of(block * HALF, HALF)
                 for k in range(Y):
                     mine = slice(k * 32 + low * 16, k * 32 + low * 16 + 16)
@@ -363,10 +363,10 @@
                     outs[n][k * 16 : (k + 1) * 16, pl.ds(spot, HALF)] = chosen.astype(BF16)
 
 
-def make_accum(part, where, rows, posts):
+def make_accum(part, place, rows, posts):
     shape = (32, NB * COLS) if part == 0 else (64, NB * HALF)
     return local(
-        lambda *refs: accum_kernel(part, *refs), "weighted_sums", [(shape, BF16)] * 4, [where],
+        lambda *refs: accum_kernel(part, *refs), "weighted_sums", [(shape, BF16)] * 4, [place],
         [*rows, *posts], 8,
     )
 
@@ -381,7 +381,7 @@
 PIECES = [((16, NB * HALF), F32)] + [((16, NB * HALF), BF16)] * 3
 
 
-def first_kernel(where_ref, *refs):
+def first_kernel(x_ref, *refs):
     outs = refs[4:]
     for block in range(NB):
         start = block * COLS
@@ -389,7 +389,7 @@
         imag = added([ref[:, start + HALF : start + COLS] for ref in refs[:4]])
         for n, out in enumerate(outs):
             mine = slice((n & 1) * 16, (n & 1) * 16 + 16)
-            chosen = jnp.where(((where_ref[2] + n) & (X - 1)) >= 2, imag[mine], real[mine])
+            chosen = jnp.where(((x_ref[0] + n) & (X - 1)) >= 2, imag[mine], real[mine])
             out[:, block * HALF : (block + 1) * HALF] = chosen.astype(out.dtype)
 
 
@@ -398,9 +398,9 @@
         out[...] = added([ref[n * 16 : (n + 1) * 16] for ref in refs[:4]]).astype(out.dtype)
 
 
-def joined_kernel(where_ref, *refs):
+def joined_kernel(block_ref, *refs):
     for n, out in enumerate(refs[8:]):
-        spot = pl.ds(pl.multiple_of(((where_ref[1] + n) % NB) * HALF, HALF), HALF)
+        spot = pl.ds(pl.multiple_of(((block_ref[0] + n) % NB) * HALF, HALF), HALF)
         out[:, :HALF] = added([ref[:, spot] for ref in refs[:4]]).astype(out.dtype)
         out[:, HALF:] = added([ref[:, spot] for ref in refs[4:8]]).astype(out.dtype)
 
@@ -412,55 +412,55 @@
 def per_device(refs, particles, shift_ids, wedge, defocus, inv_sigma):
     dom = lax.axis_index("dom")
     x_at = (dom // 16) * 2 + lax.axis_index("blk") % 2
-    where = jnp.stack([dom % G, (dom % 16) // G, x_at]).astype(jnp.int32)
+    place = [value.astype(jnp.int32).reshape(1) for value in (dom % G, (dom % 16) // G, x_at)]
+    member, block, x_at = place
     geo = jnp.asarray(geometry())
 
-    gathered = {}
-    own = own_columns(where, refs)
+    chunks = split_particles(place, particles, shift_ids, wedge, defocus, inv_sigma)
+    got, gathered, rows, pens = {}, {}, {}, {}
+    got[2] = send(chunks[2], partners(2))
+    got[1] = send(chunks[1], partners(1))
+    own = own_columns(member, refs, chunks[2])
     gathered[0, 0] = own
     gathered[1, 0] = send(own, moves(dy=-1))
     gathered[3, 0] = send(own, moves(dy=1))
-    chunks = split_particles(where, own, particles, shift_ids, wedge, defocus, inv_sigma)
-    got = {0: chunks[0]}
-    got[2] = send(chunks[2], partners(2))
-    got[1] = send(chunks[1], partners(1))
     gathered[2, 0] = send(own, moves(dy=2))
-    table, geo = make_table(where, geo)
-    wave = [got[1], got[2], gathered[1, 0], gathered[3, 0], table]
+    table, geo = make_table(member, geo)
+    rows[0], pens[0] = make_rows(member, chunks[0], geo, table)
+    wave = [got[1], got[2], gathered[1, 0], gathered[3, 0], gathered[2, 0], rows[0]]
+    got[3] = send(after(chunks[3], *wave), partners(3))
     gathered[0, 1] = send(after(own, *wave), moves(dx=-1))
     gathered[1, 1] = send(after(gathered[1, 0], *wave), moves(dx=-1))
     gathered[3, 1] = send(after(gathered[3, 0], *wave), moves(dx=1))
-    got[3] = send(after(chunks[3], *wave), partners(3))
-    rows, pens = {}, {}
-    rows[0], pens[0] = make_rows(where, after(got[0], *wave), geo, table)
-    gathered[2, 1] = send(after(gathered[2, 0], rows[0]), moves(dx=1))
-    rows[1], pens[1] = make_rows(where, after(got[1], rows[0], gathered[2, 0]), geo, table)
-    rows[2], pens[2] = make_rows(where, after(got[2], rows[1]), geo, table)
-    rows[3], pens[3] = make_rows(where, after(got[3], rows[2]), geo, table)
+    gathered[2, 1] = send(after(gathered[2, 0], *wave), moves(dx=1))
+    rows[1], pens[1] = make_rows(member, after(got[1], *wave), geo, table)
+    rows[2], pens[2] = make_rows(member, after(got[2], rows[1]), geo, table)
+    rows[3], pens[3] = make_rows(member, after(got[3], rows[2]), geo, table)
     blocks = [gathered[ky, kx] for ky in range(Y) for kx in range(2)]
 
+    (second,) = make_scores([rows[2]], [pens[2]], blocks)
+    third, other = make_scores([rows[3], rows[1]], [after(pens[3], second), pens[1]], blocks)
+    (mine,) = make_scores([rows[0]], [after(pens[0], third)], blocks)
+    arrived = [send(value, partners(n)) for value, n in ((second, 2), (third, 3), (other, 1))]
+    posterior = make_posterior([mine, *arrived])
+    posts = [posterior] + [send(posterior, partners(n)) for n in range(1, G)]
     rows = [rows[n] for n in range(G)]
-    pens = [pens[n] for n in range(G)]
-    parts = make_scores(rows, pens, blocks)
-    arrived = [send(parts[n], partners(n)) for n in range(1, G)]
-    posterior = make_posterior([parts[0], *arrived])
-    posts = [posterior] + [send(posterior, partners(n)) for n in range(1, G)]
-
-    first = make_accum(0, where, rows, posts)
+
+    first = make_accum(0, x_at, rows, posts)
     first = [first[0]] + [send(first[n], moves(dy=n)) for n in range(1, Y)]
-    second = make_accum(1, where, rows, posts)
+    second = make_accum(1, x_at, rows, posts)
     second = [
         second[0],
         send(second[1], moves(dx=1)),
         send(after(second[2], first[1]), moves(dx=2)),
         send(second[3], moves(dx=3)),
     ]
-    first = local(first_kernel, "first_sums", PIECES, [where], first, 4)
+    first = local(first_kernel, "first_sums", PIECES, [x_at], first, 4)
     first = [first[0]] + [send(first[n], moves(dx=n)) for n in range(1, X)]
     second = local(second_kernel, "second_sums", PIECES, [], second, 4)
     second = [second[0]] + [send(second[n], moves(dy=n)) for n in range(1, Y)]
     outs = [((16, COLS), F32)] + [((16, COLS), BF16)] * (NB - 1)
-    ends = local(joined_kernel, "joined_sums", outs, [where], [*first, *second], 4)
+    ends = local(joined_kernel, "joined_sums", outs, [block], [*first, *second], 4)
     return added([ends[0]] + [send(ends[n], moves(dz=n * (G // 2))) for n in range(1, NB)])
 
 

time: 111 us -> 107 us (0.964)
  Pallas kernels: 36.1 us -> 31.3 us
  waiting for transfers between devices: 22.7 us -> 24.9 us
    pallas_call x14 -> x16, Pallas kernels: 36.1 us -> 31.3 us  [local(): pl.pallas_call(kernel, in_specs=[SCALARS] * len(scalars) + [PLACED] * pla...]
    ppermute x31, waiting for transfers between devices: 22.7 us -> 24.9 us  [send(): return lax.ppermute(value, AXES, pairs)]
  transfers between devices with their start and end apart: 31 -> 31, of which waited for: 13 -> 13; matrix products, arithmetic and copies ran while one was open for 0% -> 0% of each run, Pallas kernels for 22% -> 26%
where the time goes in v7:
time: 107 us; the launch traced here: 106 us
  starting transfers between devices  49.3 us (46%)
  Pallas kernels  31.3 us (29%)
  waiting for transfers between devices  24.9 us (23%)
    ppermute x31, starting transfers between devices, send(): return lax.ppermute(value, AXES, pairs)  49.3 us
    pallas_call x16, Pallas kernels, local(): pl.pallas_call(kernel, in_specs=[SCALARS] * len(scalars) + [PLACED] * pla...  31.3 us
    ppermute x31, waiting for transfers between devices, send(): return lax.ppermute(value, AXES, pairs)  24.9 us
  transfers between devices with their start and end apart: 31, of which 13 were waited for; matrix products, arithmetic and copies ran while one was open for 0% of the time, Pallas kernels for 26%

profile of v7, /device:TPU:2, one launch (start us, length us, event | category | flops | bytes accessed | tf_op | source)
XLA Modules:
  0.0 106.4 jit_solution(13763419445935223001)
XLA Ops:
  0.0 2.0 %split_particles.1 = (bf16[32,8576]{1,0:T(8,128)(2,1)S(1)}, bf16[32,8576]{1,0:T(8,128)(2,1)S(1)}, bf16[32,8576]{1,0:T(8,128)(2,1)S(1)}, bf16[32,8576]{1,0:T(8,128)(2,1)S(1)}) custom-call(s32[1]{0:T(128)} %bitcast.2.member_ref, s32[1]{0:T(128)} %bitcast.block_ref, s32[1]{0:T(128)} %bitcast.1.x_ref.refs_0_, bf16[32,32768]{1,0:T(8,128)(2,1)} %source.2, ...), custom_call_target="tpu_custom_call" | custom-call | tf_op jit(solution)/shard_map/split_particles/pallas_call | solution.py:97
  2.1 2.0 %collective-permute-start.1 = (bf16[32,8576]{1,0:T(8,128)(2,1)S(1)}, bf16[32,8576]{1,0:T(8,128)(2,1)S(1)}, u32[]{:S(2)}, u32[]{:S(2)}) collective-permute-start(bf16[32,8576]{1,0:T(8,128)(2,1)S(1)} %get-tuple-element.57.after), channel_id=1, source_target_pairs={{0,2},{1,3},{2,0},{3,1},{4,6},{5,7},{6,4},{7,5},{8,10},{9,11},{10,... | collective-permute-start | bytes 1646600 | tf_op jit(solution)/shard_map/ppermute | solution.py:49
  5.0 3.3 %collective-permute-start.4 = (bf16[16,8192]{1,0:T(8,128)(2,1)S(1)}, bf16[16,8192]{1,0:T(8,128)(2,1)S(1)}, u32[]{:S(2)}, u32[]{:S(2)}) collective-permute-start(bf16[16,8192]{1,0:T(8,128)(2,1)S(1)} %own_references.1.refs_2_.refs_4_), channel_id=1, source_target_pairs={{0,128},{1,129},{2,130},{3,131},{4,132},{5,133},{6,134},{7,135},{8... | collective-permute-start | bytes 786440 | tf_op jit(solution)/shard_map/ppermute | solution.py:49
  9.0 2.6 %collective-permute-start.2 = (bf16[16,8192]{1,0:T(8,128)(2,1)S(1)}, bf16[16,8192]{1,0:T(8,128)(2,1)S(1)}, u32[]{:S(2)}, u32[]{:S(2)}) collective-permute-start(bf16[16,8192]{1,0:T(8,128)(2,1)S(1)} %own_references.1.refs_2_.refs_4_), channel_id=1, source_target_pairs={{0,192},{1,193},{2,194},{3,195},{4,196},{5,197},{6,198},{7,199},{8... | collective-permute-start | bytes 786440 | tf_op jit(solution)/shard_map/ppermute | solution.py:49
  11.5 5.5 %phase_table.1 = (bf16[256,8192]{1,0:T(8,128)(2,1)S(1)}, f32[4,8,1024]{2,1,0:T(8,128)S(1)}) custom-call(s32[1]{0:T(128)} %bitcast.2.member_ref, f32[16,8,1024]{2,1,0:T(8,128)} %constant.63.clone.geo_ref), custom_call_target="tpu_custom_call" | custom-call | tf_op jit(solution)/shard_map/phase_table/pallas_call | solution.py:97
  17.1 3.2 %shifted_rows.4 = (bf16[256,8192]{1,0:T(8,128)(2,1)S(1)}, bf16[32,4096]{1,0:T(8,128)(2,1)S(1)}) custom-call(s32[1]{0:T(128)} %bitcast.2.member_ref, bf16[32,8576]{1,0:T(8,128)(2,1)S(1)} %get-tuple-element.52.x_ref, f32[4,8,1024]{2,1,0:T(8,128)S(1)} %get-tuple-element.53.geo_ref, bf16[256,8192]{1,0:T(8,128)(2,1)S(1)} %get-tuple-element.54.table_ref), custom_call_target="tpu_custom_call" | custom-call | tf_op jit(solution)/shard_map/shifted_rows/pallas_call | solution.py:97
  21.0 1.7 %collective-permute-start.6 = (bf16[16,8192]{1,0:T(8,128)(2,1)S(1)}, bf16[16,8192]{1,0:T(8,128)(2,1)S(1)}, u32[]{:S(2)}, u32[]{:S(2)}) collective-permute-start(bf16[16,8192]{1,0:T(8,128)(2,1)S(1)} %own_references.1.refs_2_.refs_4_), channel_id=1, source_target_pairs={{0,48},{1,49},{2,50},{3,51},{4,52},{5,53},{6,54},{7,55},{8,56},{9,... | collective-permute-start | bytes 786440 | tf_op jit(solution)/shard_map/ppermute | solution.py:49
  22.7 1.7 %collective-permute-start.7 = (bf16[16,8192]{1,0:T(8,128)(2,1)S(1)}, bf16[16,8192]{1,0:T(8,128)(2,1)S(1)}, u32[]{:S(2)}, u32[]{:S(2)}) collective-permute-start(bf16[16,8192]{1,0:T(8,128)(2,1)S(1)} %collective-permute-done.2.refs_4_.refs_6_), channel_id=1, source_target_pairs={{0,48},{1,49},{2,50},{3,51},{4,52},{5,53},{6,54},{7,55},{8,56},{9,... | collective-permute-start | bytes 786440 | tf_op jit(solution)/shard_map/ppermute | solution.py:49
  25.1 3.2 %shifted_rows.5 = (bf16[256,8192]{1,0:T(8,128)(2,1)S(1)}, bf16[32,4096]{1,0:T(8,128)(2,1)S(1)}) custom-call(s32[1]{0:T(128)} %bitcast.2.member_ref, bf16[32,8576]{1,0:T(8,128)(2,1)S(1)} %collective-permute-done.x_ref, f32[4,8,1024]{2,1,0:T(8,128)S(1)} %get-tuple-element.53.geo_ref, bf16[256,8192]{1,0:T(8,128)(2,1)S(1)} %get-tuple-element.54.table_ref), custom_call_target="tpu_custom_call" | custom-call | tf_op jit(solution)/shard_map/shifted_rows/pallas_call | solution.py:97
  28.3 3.2 %shifted_rows.6 = (bf16[256,8192]{1,0:T(8,128)(2,1)S(1)}, bf16[32,4096]{1,0:T(8,128)(2,1)S(1)}) custom-call(s32[1]{0:T(128)} %bitcast.2.member_ref, bf16[32,8576]{1,0:T(8,128)(2,1)S(1)} %collective-permute-done.1.x_ref, f32[4,8,1024]{2,1,0:T(8,128)S(1)} %get-tuple-element.53.geo_ref, bf16[256,8192]{1,0:T(8,128)(2,1)S(1)} %get-tuple-element.54.table_ref), custom_call_target="tpu_custom_call" | custom-call | tf_op jit(solution)/shard_map/shifted_rows/pallas_call | solution.py:97
  31.5 3.7 %collective-permute-done.7.refs_5_.refs_7_ = bf16[16,8192]{1,0:T(8,128)(2,1)S(1)} collective-permute-done((bf16[16,8192]{1,0:T(8,128)(2,1)S(1)}, bf16[16,8192]{1,0:T(8,128)(2,1)S(1)}, u32[]{:S(2)}, u32[]{:S(2)}) %collective-permute-start.7) | collective-permute-done | bytes 262176 | tf_op jit(solution)/shard_map/ppermute | solution.py:49
  35.2 2.7 %collective-permute-done.9.refs_9_.refs_11_ = bf16[16,8192]{1,0:T(8,128)(2,1)S(1)} collective-permute-done((bf16[16,8192]{1,0:T(8,128)(2,1)S(1)}, bf16[16,8192]{1,0:T(8,128)(2,1)S(1)}, u32[]{:S(2)}, u32[]{:S(2)}) %collective-permute-start.9) | collective-permute-done | bytes 262176 | tf_op jit(solution)/shard_map/ppermute | solution.py:49
  39.5 2.0 %collective-permute-start.10 = (f32[256,128]{1,0:T(8,128)S(1)}, f32[256,128]{1,0:T(8,128)S(1)}, u32[]{:S(2)}, u32[]{:S(2)}) collective-permute-start(f32[256,128]{1,0:T(8,128)S(1)} %partial_scores.3), channel_id=1, source_target_pairs={{0,2},{1,3},{2,0},{3,1},{4,6},{5,7},{6,4},{7,5},{8,10},{9,11},{10,... | collective-permute-start | bytes 393224 | tf_op jit(solution)/shard_map/ppermute | solution.py:49
  41.5 3.2 %shifted_rows.7 = (bf16[256,8192]{1,0:T(8,128)(2,1)S(1)}, bf16[32,4096]{1,0:T(8,128)(2,1)S(1)}) custom-call(s32[1]{0:T(128)} %bitcast.2.member_ref, bf16[32,8576]{1,0:T(8,128)(2,1)S(1)} %collective-permute-done.5.x_ref, f32[4,8,1024]{2,1,0:T(8,128)S(1)} %get-tuple-element.53.geo_ref, bf16[256,8192]{1,0:T(8,128)(2,1)S(1)} %get-tuple-element.54.table_ref), custom_call_target="tpu_custom_call" | custom-call | tf_op jit(solution)/shard_map/shifted_rows/pallas_call | solution.py:97
  44.7 2.7 %partial_scores.4 = (f32[256,128]{1,0:T(8,128)S(1)}, f32[256,128]{1,0:T(8,128)S(1)}) custom-call(bf16[256,8192]{1,0:T(8,128)(2,1)S(1)} %get-tuple-element.65.refs_0_.refs_4_, bf16[256,8192]{1,0:T(8,128)(2,1)S(1)} %get-tuple-element.59.refs_1_.refs_2_, bf16[32,4096]{1,0:T(8,128)(2,1)S(1)} %get-tuple-element.73.refs_2_, ...), custom_call_target="tpu_custom_call" | custom-call | tf_op jit(solution)/shard_map/partial_scores/pallas_call | solution.py:97
  47.9 1.5 %partial_scores.5.refs_0_ = f32[256,128]{1,0:T(8,128)S(1)} custom-call(bf16[256,8192]{1,0:T(8,128)(2,1)S(1)} %get-tuple-element.55.refs_0_.refs_1_, bf16[32,4096]{1,0:T(8,128)(2,1)S(1)} %get-tuple-element.76.refs_1_, bf16[16,8192]{1,0:T(8,128)(2,1)S(1)} %own_references.1.refs_2_.refs_4_, bf16[16,8192]{1,0:T(8,128)(2,1)S(1)} %collective-permute-done.6.refs_3_.refs_5_, ...), custom_call_target="tpu_custom_call" | custom-call | tf_op jit(solution)/shard_map/partial_scores/pallas_call | solution.py:97
  49.4 3.4 %collective-permute-done.11.refs_2_ = f32[256,128]{1,0:T(8,128)S(1)} collective-permute-done((f32[256,128]{1,0:T(8,128)S(1)}, f32[256,128]{1,0:T(8,128)S(1)}, u32[]{:S(2)}, u32[]{:S(2)}) %collective-permute-start.11) | collective-permute-done | bytes 131104 | tf_op jit(solution)/shard_map/ppermute | solution.py:49
  53.5 1.7 %collective-permute-start.14 = (bf16[128,256]{1,0:T(8,128)(2,1)S(1)}, bf16[128,256]{1,0:T(8,128)(2,1)S(1)}, u32[]{:S(2)}, u32[]{:S(2)}) collective-permute-start(bf16[128,256]{1,0:T(8,128)(2,1)S(1)} %posterior.1.refs_5_), channel_id=1, source_target_pairs={{0,2},{1,3},{2,0},{3,1},{4,6},{5,7},{6,4},{7,5},{8,10},{9,11},{10,... | collective-permute-start | bytes 196616 | tf_op jit(solution)/shard_map/ppermute | solution.py:49
  55.2 1.9 %collective-permute-done.15.refs_8_ = bf16[128,256]{1,0:T(8,128)(2,1)S(1)} collective-permute-done((bf16[128,256]{1,0:T(8,128)(2,1)S(1)}, bf16[128,256]{1,0:T(8,128)(2,1)S(1)}, u32[]{:S(2)}, u32[]{:S(2)}) %collective-permute-start.15) | collective-permute-done | bytes 65568 | tf_op jit(solution)/shard_map/ppermute | solution.py:49
  57.1 1.9 %collective-permute-done.14.refs_7_ = bf16[128,256]{1,0:T(8,128)(2,1)S(1)} collective-permute-done((bf16[128,256]{1,0:T(8,128)(2,1)S(1)}, bf16[128,256]{1,0:T(8,128)(2,1)S(1)}, u32[]{:S(2)}, u32[]{:S(2)}) %collective-permute-start.14) | collective-permute-done | bytes 65568 | tf_op jit(solution)/shard_map/ppermute | solution.py:49
  59.0 1.8 %weighted_sums.2 = (bf16[32,4096]{1,0:T(8,128)(2,1)S(1)}, bf16[32,4096]{1,0:T(8,128)(2,1)S(1)}, bf16[32,4096]{1,0:T(8,128)(2,1)S(1)}, bf16[32,4096]{1,0:T(8,128)(2,1)S(1)}) custom-call(s32[1]{0:T(128)} %bitcast.1.x_ref.refs_0_, bf16[256,8192]{1,0:T(8,128)(2,1)S(1)} %get-tuple-element.55.refs_0_.refs_1_, ...), custom_call_target="tpu_custom_call" | custom-call | tf_op jit(solution)/shard_map/weighted_sums/pallas_call | solution.py:97
  62.4 2.6 %collective-permute-start.17 = (bf16[32,4096]{1,0:T(8,128)(2,1)S(1)}, bf16[32,4096]{1,0:T(8,128)(2,1)S(1)}, u32[]{:S(2)}, u32[]{:S(2)}) collective-permute-start(bf16[32,4096]{1,0:T(8,128)(2,1)S(1)} %get-tuple-element.80), channel_id=1, source_target_pairs={{0,128},{1,129},{2,130},{3,131},{4,132},{5,133},{6,134},{7,135},{8... | collective-permute-start | bytes 786440 | tf_op jit(solution)/shard_map/ppermute | solution.py:49
  65.7 1.9 %weighted_sums.3 = (bf16[64,2048]{1,0:T(8,128)(2,1)S(1)}, bf16[64,2048]{1,0:T(8,128)(2,1)S(1)}, bf16[64,2048]{1,0:T(8,128)(2,1)S(1)}, bf16[64,2048]{1,0:T(8,128)(2,1)S(1)}) custom-call(s32[1]{0:T(128)} %bitcast.1.x_ref.refs_0_, bf16[256,8192]{1,0:T(8,128)(2,1)S(1)} %get-tuple-element.55.refs_0_.refs_1_, ...), custom_call_target="tpu_custom_call" | custom-call | tf_op jit(solution)/shard_map/weighted_sums/pallas_call | solution.py:97
  68.0 1.8 %collective-permute-start.24 = (bf16[64,2048]{1,0:T(8,128)(2,1)S(1)}, bf16[64,2048]{1,0:T(8,128)(2,1)S(1)}, u32[]{:S(2)}, u32[]{:S(2)}) collective-permute-start(bf16[64,2048]{1,0:T(8,128)(2,1)S(1)} %get-tuple-element.90), channel_id=1, source_target_pairs={{0,48},{1,49},{2,50},{3,51},{4,52},{5,53},{6,54},{7,55},{8,56},{9,... | collective-permute-start | bytes 786440 | tf_op jit(solution)/shard_map/ppermute | solution.py:49
  71.8 4.7 %collective-permute-done.17.refs_2_ = bf16[32,4096]{1,0:T(8,128)(2,1)S(1)} collective-permute-done((bf16[32,4096]{1,0:T(8,128)(2,1)S(1)}, bf16[32,4096]{1,0:T(8,128)(2,1)S(1)}, u32[]{:S(2)}, u32[]{:S(2)}) %collective-permute-start.17) | collective-permute-done | bytes 262176 | tf_op jit(solution)/shard_map/ppermute | solution.py:49
  77.2 3.8 %collective-permute-start.20 = (bf16[16,2048]{1,0:T(8,128)(2,1)S(1)}, bf16[16,2048]{1,0:T(8,128)(2,1)S(1)}, u32[]{:S(2)}, u32[]{:S(2)}) collective-permute-start(bf16[16,2048]{1,0:T(8,128)(2,1)S(1)} %get-tuple-element.84), channel_id=1, source_target_pairs={{0,16},{1,17},{2,18},{3,19},{4,20},{5,21},{6,22},{7,23},{8,24},{9,... | collective-permute-start | bytes 196616 | tf_op jit(solution)/shard_map/ppermute | solution.py:49
  81.0 4.6 %collective-permute-start.21 = (bf16[16,2048]{1,0:T(8,128)(2,1)S(1)}, bf16[16,2048]{1,0:T(8,128)(2,1)S(1)}, u32[]{:S(2)}, u32[]{:S(2)}) collective-permute-start(bf16[16,2048]{1,0:T(8,128)(2,1)S(1)} %get-tuple-element.85), channel_id=1, source_target_pairs={{0,48},{1,49},{2,50},{3,51},{4,52},{5,53},{6,54},{7,55},{8,56},{9,... | collective-permute-start | bytes 196616 | tf_op jit(solution)/shard_map/ppermute | solution.py:49
  87.4 2.6 %collective-permute-start.27 = (bf16[16,2048]{1,0:T(8,128)(2,1)S(1)}, bf16[16,2048]{1,0:T(8,128)(2,1)S(1)}, u32[]{:S(2)}, u32[]{:S(2)}) collective-permute-start(bf16[16,2048]{1,0:T(8,128)(2,1)S(1)} %get-tuple-element.94), channel_id=1, source_target_pairs={{0,192},{1,193},{2,194},{3,195},{4,196},{5,197},{6,198},{7,199},{8... | collective-permute-start | bytes 196616 | tf_op jit(solution)/shard_map/ppermute | solution.py:49
  91.3 1.7 %collective-permute-done.26.refs_6_ = bf16[16,2048]{1,0:T(8,128)(2,1)S(1)} collective-permute-done((bf16[16,2048]{1,0:T(8,128)(2,1)S(1)}, bf16[16,2048]{1,0:T(8,128)(2,1)S(1)}, u32[]{:S(2)}, u32[]{:S(2)}) %collective-permute-start.26) | collective-permute-done | bytes 65568 | tf_op jit(solution)/shard_map/ppermute | solution.py:49
  93.1 3.3 %collective-permute-start.28 = (bf16[16,1024]{1,0:T(8,128)(2,1)S(1)}, bf16[16,1024]{1,0:T(8,128)(2,1)S(1)}, u32[]{:S(2)}, u32[]{:S(2)}) collective-permute-start(bf16[16,1024]{1,0:T(8,128)(2,1)S(1)} %get-tuple-element.96), channel_id=1, source_target_pairs={{0,4},{1,5},{2,6},{3,7},{4,8},{5,9},{6,10},{7,11},{8,12},{9,13},{1... | collective-permute-start | bytes 98312 | tf_op jit(solution)/shard_map/ppermute | solution.py:49
  96.4 4.5 %collective-permute-start.29 = (bf16[16,1024]{1,0:T(8,128)(2,1)S(1)}, bf16[16,1024]{1,0:T(8,128)(2,1)S(1)}, u32[]{:S(2)}, u32[]{:S(2)}) collective-permute-start(bf16[16,1024]{1,0:T(8,128)(2,1)S(1)} %get-tuple-element.97), channel_id=1, source_target_pairs={{0,8},{1,9},{2,10},{3,11},{4,12},{5,13},{6,14},{7,15},{8,0},{9,1},... | collective-permute-start | bytes 98312 | tf_op jit(solution)/shard_map/ppermute | solution.py:49
  100.9 2.7 %collective-permute-start.30 = (bf16[16,1024]{1,0:T(8,128)(2,1)S(1)}, bf16[16,1024]{1,0:T(8,128)(2,1)S(1)}, u32[]{:S(2)}, u32[]{:S(2)}) collective-permute-start(bf16[16,1024]{1,0:T(8,128)(2,1)S(1)} %get-tuple-element.98), channel_id=1, source_target_pairs={{0,12},{1,13},{2,14},{3,15},{4,0},{5,1},{6,2},{7,3},{8,4},{9,5},{1... | collective-permute-start | bytes 98312 | tf_op jit(solution)/shard_map/ppermute | solution.py:49
  (47 shorter events, 17.1 us)
Async XLA Ops:
  2.0 19.0 %collective-permute-start = (bf16[32,8576]{1,0:T(8,128)(2,1)S(1)}, bf16[32,8576]{1,0:T(8,128)(2,1)S(1)}, u32[]{:S(2)}, u32[]{:S(2)}) collective-permute-start(bf16[32,8576]{1,0:T(8,128)(2,1)S(1)} %get-tuple-element.56), channel_id=1, source_target_pairs={{0,1},{1,0},{2,3},{3,2},{4,5},{5,4},{6,7},{7,6},{8,9},{9,8},{10,11... | collective-permute-start | bytes 1646600 | tf_op jit(solution)/shard_map/ppermute | solution.py:49
  2.1 18.9 %collective-permute-start.1 = (bf16[32,8576]{1,0:T(8,128)(2,1)S(1)}, bf16[32,8576]{1,0:T(8,128)(2,1)S(1)}, u32[]{:S(2)}, u32[]{:S(2)}) collective-permute-start(bf16[32,8576]{1,0:T(8,128)(2,1)S(1)} %get-tuple-element.57.after), channel_id=1, source_target_pairs={{0,2},{1,3},{2,0},{3,1},{4,6},{5,7},{6,4},{7,5},{8,10},{9,11},{10,... | collective-permute-start | bytes 1646600 | tf_op jit(solution)/shard_map/ppermute | solution.py:49
  5.0 15.2 %collective-permute-start.4 = (bf16[16,8192]{1,0:T(8,128)(2,1)S(1)}, bf16[16,8192]{1,0:T(8,128)(2,1)S(1)}, u32[]{:S(2)}, u32[]{:S(2)}) collective-permute-start(bf16[16,8192]{1,0:T(8,128)(2,1)S(1)} %own_references.1.refs_2_.refs_4_), channel_id=1, source_target_pairs={{0,128},{1,129},{2,130},{3,131},{4,132},{5,133},{6,134},{7,135},{8... | collective-permute-start | bytes 786440 | tf_op jit(solution)/shard_map/ppermute | solution.py:49
  8.3 12.3 %collective-permute-start.3 = (bf16[16,8192]{1,0:T(8,128)(2,1)S(1)}, bf16[16,8192]{1,0:T(8,128)(2,1)S(1)}, u32[]{:S(2)}, u32[]{:S(2)}) collective-permute-start(bf16[16,8192]{1,0:T(8,128)(2,1)S(1)} %own_references.1.refs_2_.refs_4_), channel_id=1, source_target_pairs={{0,64},{1,65},{2,66},{3,67},{4,68},{5,69},{6,70},{7,71},{8,72},{9,... | collective-permute-start | bytes 786440 | tf_op jit(solution)/shard_map/ppermute | solution.py:49
  9.0 12.0 %collective-permute-start.2 = (bf16[16,8192]{1,0:T(8,128)(2,1)S(1)}, bf16[16,8192]{1,0:T(8,128)(2,1)S(1)}, u32[]{:S(2)}, u32[]{:S(2)}) collective-permute-start(bf16[16,8192]{1,0:T(8,128)(2,1)S(1)} %own_references.1.refs_2_.refs_4_), channel_id=1, source_target_pairs={{0,192},{1,193},{2,194},{3,195},{4,196},{5,197},{6,198},{7,199},{8... | collective-permute-start | bytes 786440 | tf_op jit(solution)/shard_map/ppermute | solution.py:49
  21.0 20.5 %collective-permute-start.5 = (bf16[32,8576]{1,0:T(8,128)(2,1)S(1)}, bf16[32,8576]{1,0:T(8,128)(2,1)S(1)}, u32[]{:S(2)}, u32[]{:S(2)}) collective-permute-start(bf16[32,8576]{1,0:T(8,128)(2,1)S(1)} %get-tuple-element.63), channel_id=1, source_target_pairs={{0,3},{1,2},{2,1},{3,0},{4,7},{5,6},{6,5},{7,4},{8,11},{9,10},{10,... | collective-permute-start | bytes 1646600 | tf_op jit(solution)/shard_map/ppermute | solution.py:49
  21.0 10.5 %collective-permute-start.6 = (bf16[16,8192]{1,0:T(8,128)(2,1)S(1)}, bf16[16,8192]{1,0:T(8,128)(2,1)S(1)}, u32[]{:S(2)}, u32[]{:S(2)}) collective-permute-start(bf16[16,8192]{1,0:T(8,128)(2,1)S(1)} %own_references.1.refs_2_.refs_4_), channel_id=1, source_target_pairs={{0,48},{1,49},{2,50},{3,51},{4,52},{5,53},{6,54},{7,55},{8,56},{9,... | collective-permute-start | bytes 786440 | tf_op jit(solution)/shard_map/ppermute | solution.py:49
  22.7 12.5 %collective-permute-start.7 = (bf16[16,8192]{1,0:T(8,128)(2,1)S(1)}, bf16[16,8192]{1,0:T(8,128)(2,1)S(1)}, u32[]{:S(2)}, u32[]{:S(2)}) collective-permute-start(bf16[16,8192]{1,0:T(8,128)(2,1)S(1)} %collective-permute-done.2.refs_4_.refs_6_), channel_id=1, source_target_pairs={{0,48},{1,49},{2,50},{3,51},{4,52},{5,53},{6,54},{7,55},{8,56},{9,... | collective-permute-start | bytes 786440 | tf_op jit(solution)/shard_map/ppermute | solution.py:49
  24.4 10.8 %collective-permute-start.8 = (bf16[16,8192]{1,0:T(8,128)(2,1)S(1)}, bf16[16,8192]{1,0:T(8,128)(2,1)S(1)}, u32[]{:S(2)}, u32[]{:S(2)}) collective-permute-start(bf16[16,8192]{1,0:T(8,128)(2,1)S(1)} %collective-permute-done.4.refs_6_.refs_8_), channel_id=1, source_target_pairs={{0,32},{1,33},{2,34},{3,35},{4,36},{5,37},{6,38},{7,39},{8,40},{9,... | collective-permute-start | bytes 786440 | tf_op jit(solution)/shard_map/ppermute | solution.py:49
  24.7 13.2 %collective-permute-start.9 = (bf16[16,8192]{1,0:T(8,128)(2,1)S(1)}, bf16[16,8192]{1,0:T(8,128)(2,1)S(1)}, u32[]{:S(2)}, u32[]{:S(2)}) collective-permute-start(bf16[16,8192]{1,0:T(8,128)(2,1)S(1)} %collective-permute-done.3.refs_8_.refs_10_), channel_id=1, source_target_pairs={{0,32},{1,33},{2,34},{3,35},{4,36},{5,37},{6,38},{7,39},{8,40},{9,... | collective-permute-start | bytes 786440 | tf_op jit(solution)/shard_map/ppermute | solution.py:49
  39.5 9.9 %collective-permute-start.10 = (f32[256,128]{1,0:T(8,128)S(1)}, f32[256,128]{1,0:T(8,128)S(1)}, u32[]{:S(2)}, u32[]{:S(2)}) collective-permute-start(f32[256,128]{1,0:T(8,128)S(1)} %partial_scores.3), channel_id=1, source_target_pairs={{0,2},{1,3},{2,0},{3,1},{4,6},{5,7},{6,4},{7,5},{8,10},{9,11},{10,... | collective-permute-start | bytes 393224 | tf_op jit(solution)/shard_map/ppermute | solution.py:49
  47.4 2.0 %collective-permute-start.12 = (f32[256,128]{1,0:T(8,128)S(1)}, f32[256,128]{1,0:T(8,128)S(1)}, u32[]{:S(2)}, u32[]{:S(2)}) collective-permute-start(f32[256,128]{1,0:T(8,128)S(1)} %get-tuple-element.77), channel_id=1, source_target_pairs={{0,1},{1,0},{2,3},{3,2},{4,5},{5,4},{6,7},{7,6},{8,9},{9,8},{10,11... | collective-permute-start | bytes 393224 | tf_op jit(solution)/shard_map/ppermute | solution.py:49
  47.5 5.3 %collective-permute-start.11 = (f32[256,128]{1,0:T(8,128)S(1)}, f32[256,128]{1,0:T(8,128)S(1)}, u32[]{:S(2)}, u32[]{:S(2)}) collective-permute-start(f32[256,128]{1,0:T(8,128)S(1)} %get-tuple-element.75), channel_id=1, source_target_pairs={{0,3},{1,2},{2,1},{3,0},{4,7},{5,6},{6,5},{7,4},{8,11},{9,10},{10,... | collective-permute-start | bytes 393224 | tf_op jit(solution)/shard_map/ppermute | solution.py:49
  53.1 4.0 %collective-permute-start.15 = (bf16[128,256]{1,0:T(8,128)(2,1)S(1)}, bf16[128,256]{1,0:T(8,128)(2,1)S(1)}, u32[]{:S(2)}, u32[]{:S(2)}) collective-permute-start(bf16[128,256]{1,0:T(8,128)(2,1)S(1)} %posterior.1.refs_5_), channel_id=1, source_target_pairs={{0,3},{1,2},{2,1},{3,0},{4,7},{5,6},{6,5},{7,4},{8,11},{9,10},{10,... | collective-permute-start | bytes 196616 | tf_op jit(solution)/shard_map/ppermute | solution.py:49
  53.5 5.5 %collective-permute-start.14 = (bf16[128,256]{1,0:T(8,128)(2,1)S(1)}, bf16[128,256]{1,0:T(8,128)(2,1)S(1)}, u32[]{:S(2)}, u32[]{:S(2)}) collective-permute-start(bf16[128,256]{1,0:T(8,128)(2,1)S(1)} %posterior.1.refs_5_), channel_id=1, source_target_pairs={{0,2},{1,3},{2,0},{3,1},{4,6},{5,7},{6,4},{7,5},{8,10},{9,11},{10,... | collective-permute-start | bytes 196616 | tf_op jit(solution)/shard_map/ppermute | solution.py:49
  55.2 3.8 %collective-permute-start.13 = (bf16[128,256]{1,0:T(8,128)(2,1)S(1)}, bf16[128,256]{1,0:T(8,128)(2,1)S(1)}, u32[]{:S(2)}, u32[]{:S(2)}) collective-permute-start(bf16[128,256]{1,0:T(8,128)(2,1)S(1)} %posterior.1.refs_5_), channel_id=1, source_target_pairs={{0,1},{1,0},{2,3},{3,2},{4,5},{5,4},{6,7},{7,6},{8,9},{9,8},{10,11... | collective-permute-start | bytes 196616 | tf_op jit(solution)/shard_map/ppermute | solution.py:49
  60.9 9.7 %collective-permute-start.16 = (bf16[32,4096]{1,0:T(8,128)(2,1)S(1)}, bf16[32,4096]{1,0:T(8,128)(2,1)S(1)}, u32[]{:S(2)}, u32[]{:S(2)}) collective-permute-start(bf16[32,4096]{1,0:T(8,128)(2,1)S(1)} %get-tuple-element.79), channel_id=1, source_target_pairs={{0,64},{1,65},{2,66},{3,67},{4,68},{5,69},{6,70},{7,71},{8,72},{9,... | collective-permute-start | bytes 786440 | tf_op jit(solution)/shard_map/ppermute | solution.py:49
  62.4 14.1 %collective-permute-start.17 = (bf16[32,4096]{1,0:T(8,128)(2,1)S(1)}, bf16[32,4096]{1,0:T(8,128)(2,1)S(1)}, u32[]{:S(2)}, u32[]{:S(2)}) collective-permute-start(bf16[32,4096]{1,0:T(8,128)(2,1)S(1)} %get-tuple-element.80), channel_id=1, source_target_pairs={{0,128},{1,129},{2,130},{3,131},{4,132},{5,133},{6,134},{7,135},{8... | collective-permute-start | bytes 786440 | tf_op jit(solution)/shard_map/ppermute | solution.py:49
  65.0 11.4 %collective-permute-start.18 = (bf16[32,4096]{1,0:T(8,128)(2,1)S(1)}, bf16[32,4096]{1,0:T(8,128)(2,1)S(1)}, u32[]{:S(2)}, u32[]{:S(2)}) collective-permute-start(bf16[32,4096]{1,0:T(8,128)(2,1)S(1)} %get-tuple-element.81), channel_id=1, source_target_pairs={{0,192},{1,193},{2,194},{3,195},{4,196},{5,197},{6,198},{7,199},{8... | collective-permute-start | bytes 786440 | tf_op jit(solution)/shard_map/ppermute | solution.py:49
  67.6 13.4 %collective-permute-start.22 = (bf16[64,2048]{1,0:T(8,128)(2,1)S(1)}, bf16[64,2048]{1,0:T(8,128)(2,1)S(1)}, u32[]{:S(2)}, u32[]{:S(2)}) collective-permute-start(bf16[64,2048]{1,0:T(8,128)(2,1)S(1)} %get-tuple-element.87), channel_id=1, source_target_pairs={{0,32},{1,33},{2,34},{3,35},{4,36},{5,37},{6,38},{7,39},{8,40},{9,... | collective-permute-start | bytes 786440 | tf_op jit(solution)/shard_map/ppermute | solution.py:49
  68.0 17.6 %collective-permute-start.24 = (bf16[64,2048]{1,0:T(8,128)(2,1)S(1)}, bf16[64,2048]{1,0:T(8,128)(2,1)S(1)}, u32[]{:S(2)}, u32[]{:S(2)}) collective-permute-start(bf16[64,2048]{1,0:T(8,128)(2,1)S(1)} %get-tuple-element.90), channel_id=1, source_target_pairs={{0,48},{1,49},{2,50},{3,51},{4,52},{5,53},{6,54},{7,55},{8,56},{9,... | collective-permute-start | bytes 786440 | tf_op jit(solution)/shard_map/ppermute | solution.py:49
  70.5 15.1 %collective-permute-start.23 = (bf16[64,2048]{1,0:T(8,128)(2,1)S(1)}, bf16[64,2048]{1,0:T(8,128)(2,1)S(1)}, u32[]{:S(2)}, u32[]{:S(2)}) collective-permute-start(bf16[64,2048]{1,0:T(8,128)(2,1)S(1)} %get-tuple-element.89), channel_id=1, source_target_pairs={{0,16},{1,17},{2,18},{3,19},{4,20},{5,21},{6,22},{7,23},{8,24},{9,... | collective-permute-start | bytes 786440 | tf_op jit(solution)/shard_map/ppermute | solution.py:49
  76.6 10.8 %collective-permute-start.19 = (bf16[16,2048]{1,0:T(8,128)(2,1)S(1)}, bf16[16,2048]{1,0:T(8,128)(2,1)S(1)}, u32[]{:S(2)}, u32[]{:S(2)}) collective-permute-start(bf16[16,2048]{1,0:T(8,128)(2,1)S(1)} %get-tuple-element.83), channel_id=1, source_target_pairs={{0,32},{1,33},{2,34},{3,35},{4,36},{5,37},{6,38},{7,39},{8,40},{9,... | collective-permute-start | bytes 196616 | tf_op jit(solution)/shard_map/ppermute | solution.py:49
  77.2 12.8 %collective-permute-start.20 = (bf16[16,2048]{1,0:T(8,128)(2,1)S(1)}, bf16[16,2048]{1,0:T(8,128)(2,1)S(1)}, u32[]{:S(2)}, u32[]{:S(2)}) collective-permute-start(bf16[16,2048]{1,0:T(8,128)(2,1)S(1)} %get-tuple-element.84), channel_id=1, source_target_pairs={{0,16},{1,17},{2,18},{3,19},{4,20},{5,21},{6,22},{7,23},{8,24},{9,... | collective-permute-start | bytes 196616 | tf_op jit(solution)/shard_map/ppermute | solution.py:49
  81.0 9.0 %collective-permute-start.21 = (bf16[16,2048]{1,0:T(8,128)(2,1)S(1)}, bf16[16,2048]{1,0:T(8,128)(2,1)S(1)}, u32[]{:S(2)}, u32[]{:S(2)}) collective-permute-start(bf16[16,2048]{1,0:T(8,128)(2,1)S(1)} %get-tuple-element.85), channel_id=1, source_target_pairs={{0,48},{1,49},{2,50},{3,51},{4,52},{5,53},{6,54},{7,55},{8,56},{9,... | collective-permute-start | bytes 196616 | tf_op jit(solution)/shard_map/ppermute | solution.py:49
  85.8 5.6 %collective-permute-start.25 = (bf16[16,2048]{1,0:T(8,128)(2,1)S(1)}, bf16[16,2048]{1,0:T(8,128)(2,1)S(1)}, u32[]{:S(2)}, u32[]{:S(2)}) collective-permute-start(bf16[16,2048]{1,0:T(8,128)(2,1)S(1)} %get-tuple-element.92), channel_id=1, source_target_pairs={{0,64},{1,65},{2,66},{3,67},{4,68},{5,69},{6,70},{7,71},{8,72},{9,... | collective-permute-start | bytes 196616 | tf_op jit(solution)/shard_map/ppermute | solution.py:49
  87.2 5.8 %collective-permute-start.26 = (bf16[16,2048]{1,0:T(8,128)(2,1)S(1)}, bf16[16,2048]{1,0:T(8,128)(2,1)S(1)}, u32[]{:S(2)}, u32[]{:S(2)}) collective-permute-start(bf16[16,2048]{1,0:T(8,128)(2,1)S(1)} %get-tuple-element.93), channel_id=1, source_target_pairs={{0,128},{1,129},{2,130},{3,131},{4,132},{5,133},{6,134},{7,135},{8... | collective-permute-start | bytes 196616 | tf_op jit(solution)/shard_map/ppermute | solution.py:49
  87.4 5.6 %collective-permute-start.27 = (bf16[16,2048]{1,0:T(8,128)(2,1)S(1)}, bf16[16,2048]{1,0:T(8,128)(2,1)S(1)}, u32[]{:S(2)}, u32[]{:S(2)}) collective-permute-start(bf16[16,2048]{1,0:T(8,128)(2,1)S(1)} %get-tuple-element.94), channel_id=1, source_target_pairs={{0,192},{1,193},{2,194},{3,195},{4,196},{5,197},{6,198},{7,199},{8... | collective-permute-start | bytes 196616 | tf_op jit(solution)/shard_map/ppermute | solution.py:49
  93.1 10.5 %collective-permute-start.28 = (bf16[16,1024]{1,0:T(8,128)(2,1)S(1)}, bf16[16,1024]{1,0:T(8,128)(2,1)S(1)}, u32[]{:S(2)}, u32[]{:S(2)}) collective-permute-start(bf16[16,1024]{1,0:T(8,128)(2,1)S(1)} %get-tuple-element.96), channel_id=1, source_target_pairs={{0,4},{1,5},{2,6},{3,7},{4,8},{5,9},{6,10},{7,11},{8,12},{9,13},{1... | collective-permute-start | bytes 98312 | tf_op jit(solution)/shard_map/ppermute | solution.py:49
  96.4 8.2 %collective-permute-start.29 = (bf16[16,1024]{1,0:T(8,128)(2,1)S(1)}, bf16[16,1024]{1,0:T(8,128)(2,1)S(1)}, u32[]{:S(2)}, u32[]{:S(2)}) collective-permute-start(bf16[16,1024]{1,0:T(8,128)(2,1)S(1)} %get-tuple-element.97), channel_id=1, source_target_pairs={{0,8},{1,9},{2,10},{3,11},{4,12},{5,13},{6,14},{7,15},{8,0},{9,1},... | collective-permute-start | bytes 98312 | tf_op jit(solution)/shard_map/ppermute | solution.py:49
  100.9 4.8 %collective-permute-start.30 = (bf16[16,1024]{1,0:T(8,128)(2,1)S(1)}, bf16[16,1024]{1,0:T(8,128)(2,1)S(1)}, u32[]{:S(2)}, u32[]{:S(2)}) collective-permute-start(bf16[16,1024]{1,0:T(8,128)(2,1)S(1)} %get-tuple-element.98), channel_id=1, source_target_pairs={{0,12},{1,13},{2,14},{3,15},{4,0},{5,1},{6,2},{7,3},{8,4},{9,5},{1... | collective-permute-start | bytes 98312 | tf_op jit(solution)/shard_map/ppermute | solution.py:49

commit v8 on v7

--- a/solution.py
+++ b/solution.py
@@ -287,9 +287,10 @@
     )
 
 
-def scores_kernel(count, *refs):
+def scores_kernel(count, more, *refs):
     blocks = refs[2 * count : 2 * count + 8]
-    outs = refs[2 * count + 8 :]
+    added_in = refs[2 * count + 8 : 2 * count + 8 + more]
+    outs = refs[2 * count + 8 + more :]
     stacked = jnp.concatenate([block[...] for block in blocks], axis=0)
     power = []
     for block in range(NB):
@@ -304,14 +305,17 @@
     total = lax.dot_general(rows, stacked, NT, preferred_element_type=F32)
     for n, out in enumerate(outs):
         mine = total[n * ROWS : (n + 1) * ROWS].reshape(SHIFTS, P_DEV, 128)
-        out[...] = (mine - energy[None, n * P_DEV : (n + 1) * P_DEV]).reshape(ROWS, 128)
-
-
-def make_scores(rows, pens, blocks):
-    count = len(rows)
+        mine = (mine - energy[None, n * P_DEV : (n + 1) * P_DEV]).reshape(ROWS, 128)
+        for value in added_in:
+            mine = mine + value[...]
+        out[...] = mine
+
+
+def make_scores(rows, pens, blocks, plus=()):
+    count, more = len(rows), len(plus)
     return local(
-        lambda *refs: scores_kernel(count, *refs), "partial_scores", [((ROWS, 128), F32)] * count, [],
-        [*rows, *pens, *blocks], 12,
+        lambda *refs: scores_kernel(count, more, *refs), "partial_scores", [((ROWS, 128), F32)] * count,
+        [], [*rows, *pens, *blocks, *plus], 12,
     )
 
 
@@ -424,24 +428,24 @@
     gathered[0, 0] = own
     gathered[1, 0] = send(own, moves(dy=-1))
     gathered[3, 0] = send(own, moves(dy=1))
-    gathered[2, 0] = send(own, moves(dy=2))
+    gathered[0, 1] = send(own, moves(dx=-1))
     table, geo = make_table(member, geo)
     rows[0], pens[0] = make_rows(member, chunks[0], geo, table)
-    wave = [got[1], got[2], gathered[1, 0], gathered[3, 0], gathered[2, 0], rows[0]]
-    got[3] = send(after(chunks[3], *wave), partners(3))
-    gathered[0, 1] = send(after(own, *wave), moves(dx=-1))
+    wave = [got[1], gathered[1, 0], gathered[3, 0], gathered[0, 1], rows[0]]
     gathered[1, 1] = send(after(gathered[1, 0], *wave), moves(dx=-1))
     gathered[3, 1] = send(after(gathered[3, 0], *wave), moves(dx=1))
-    gathered[2, 1] = send(after(gathered[2, 0], *wave), moves(dx=1))
-    rows[1], pens[1] = make_rows(member, after(got[1], *wave), geo, table)
+    gathered[2, 1] = send(after(gathered[0, 1], *wave), moves(dy=2))
+    gathered[2, 0] = send(after(gathered[1, 0], *wave), moves(dy=-1))
+    got[3] = send(after(chunks[3], *wave, got[2]), partners(3))
+    rows[1], pens[1] = make_rows(member, after(got[1], *wave, got[2]), geo, table)
     rows[2], pens[2] = make_rows(member, after(got[2], rows[1]), geo, table)
     rows[3], pens[3] = make_rows(member, after(got[3], rows[2]), geo, table)
     blocks = [gathered[ky, kx] for ky in range(Y) for kx in range(2)]
 
-    (second,) = make_scores([rows[2]], [pens[2]], blocks)
+    (second,) = make_scores([rows[2]], [after(pens[2], rows[3])], blocks)
     third, other = make_scores([rows[3], rows[1]], [after(pens[3], second), pens[1]], blocks)
-    (mine,) = make_scores([rows[0]], [after(pens[0], third)], blocks)
-    arrived = [send(value, partners(n)) for value, n in ((second, 2), (third, 3), (other, 1))]
+    (mine,) = make_scores([rows[0]], [after(pens[0], third)], blocks, [send(second, partners(2))])
+    arrived = [send(value, partners(n)) for value, n in ((third, 3), (other, 1))]
     posterior = make_posterior([mine, *arrived])
     posts = [posterior] + [send(posterior, partners(n)) for n in range(1, G)]
     rows = [rows[n] for n in range(G)]

time: 107 us -> 101 us (0.944)
  starting transfers between devices: 49.3 us -> 46 us
  waiting for transfers between devices: 24.9 us -> 21.9 us
    ppermute x31, starting transfers between devices: 49.3 us -> 46 us  [send(): return lax.ppermute(value, AXES, pairs)]
    ppermute x31, waiting for transfers between devices: 24.9 us -> 21.9 us  [send(): return lax.ppermute(value, AXES, pairs)]
  transfers between devices with their start and end apart: 31 -> 31, of which waited for: 13 -> 11; matrix products, arithmetic and copies ran while one was open for 0% -> 0% of each run, Pallas kernels for 26% -> 26%
where the time goes in v8:
time: 101 us; the launch traced here: 100 us
  starting transfers between devices  46 us (46%)
  Pallas kernels  31.3 us (31%)
  waiting for transfers between devices  21.9 us (22%)
    ppermute x31, starting transfers between devices, send(): return lax.ppermute(value, AXES, pairs)  46 us
    pallas_call x16, Pallas kernels, local(): pl.pallas_call(kernel, in_specs=[SCALARS] * len(scalars) + [PLACED] * pla...  31.3 us
    ppermute x31, waiting for transfers between devices, send(): return lax.ppermute(value, AXES, pairs)  21.9 us
  transfers between devices with their start and end apart: 31, of which 11 were waited for; matrix products, arithmetic and copies ran while one was open for 0% of the time, Pallas kernels for 26%

profile of v8, /device:TPU:2, one launch (start us, length us, event | category | flops | bytes accessed | tf_op | source)
XLA Modules:
  0.0 100.0 jit_solution(16533621905730659999)
XLA Ops:
  0.0 2.0 %split_particles.1 = (bf16[32,8576]{1,0:T(8,128)(2,1)S(1)}, bf16[32,8576]{1,0:T(8,128)(2,1)S(1)}, bf16[32,8576]{1,0:T(8,128)(2,1)S(1)}, bf16[32,8576]{1,0:T(8,128)(2,1)S(1)}) custom-call(s32[1]{0:T(128)} %bitcast.2.member_ref, s32[1]{0:T(128)} %bitcast.block_ref, s32[1]{0:T(128)} %bitcast.1.x_ref.refs_0_, bf16[32,32768]{1,0:T(8,128)(2,1)} %source.2, ...), custom_call_target="tpu_custom_call" | custom-call | tf_op jit(solution)/shard_map/split_particles/pallas_call | solution.py:97
  2.1 2.0 %collective-permute-start.4 = (bf16[32,8576]{1,0:T(8,128)(2,1)S(1)}, bf16[32,8576]{1,0:T(8,128)(2,1)S(1)}, u32[]{:S(2)}, u32[]{:S(2)}) collective-permute-start(bf16[32,8576]{1,0:T(8,128)(2,1)S(1)} %get-tuple-element.57.after), channel_id=1, source_target_pairs={{0,2},{1,3},{2,0},{3,1},{4,6},{5,7},{6,4},{7,5},{8,10},{9,11},{10,... | collective-permute-start | bytes 1646600 | tf_op jit(solution)/shard_map/ppermute | solution.py:49
  5.0 3.1 %collective-permute-start.1 = (bf16[16,8192]{1,0:T(8,128)(2,1)S(1)}, bf16[16,8192]{1,0:T(8,128)(2,1)S(1)}, u32[]{:S(2)}, u32[]{:S(2)}) collective-permute-start(bf16[16,8192]{1,0:T(8,128)(2,1)S(1)} %own_references.1.refs_2_.refs_4_), channel_id=1, source_target_pairs={{0,192},{1,193},{2,194},{3,195},{4,196},{5,197},{6,198},{7,199},{8... | collective-permute-start | bytes 786440 | tf_op jit(solution)/shard_map/ppermute | solution.py:49
  8.7 5.5 %phase_table.1 = (bf16[256,8192]{1,0:T(8,128)(2,1)S(1)}, f32[4,8,1024]{2,1,0:T(8,128)S(1)}) custom-call(s32[1]{0:T(128)} %bitcast.2.member_ref, f32[16,8,1024]{2,1,0:T(8,128)} %constant.63.clone.geo_ref), custom_call_target="tpu_custom_call" | custom-call | tf_op jit(solution)/shard_map/phase_table/pallas_call | solution.py:97
  14.2 3.2 %shifted_rows.4 = (bf16[256,8192]{1,0:T(8,128)(2,1)S(1)}, bf16[32,4096]{1,0:T(8,128)(2,1)S(1)}) custom-call(s32[1]{0:T(128)} %bitcast.2.member_ref, bf16[32,8576]{1,0:T(8,128)(2,1)S(1)} %get-tuple-element.52.x_ref, f32[4,8,1024]{2,1,0:T(8,128)S(1)} %get-tuple-element.53.geo_ref, bf16[256,8192]{1,0:T(8,128)(2,1)S(1)} %get-tuple-element.54.table_ref), custom_call_target="tpu_custom_call" | custom-call | tf_op jit(solution)/shard_map/shifted_rows/pallas_call | solution.py:97
  18.1 2.2 %collective-permute-start.6 = (bf16[16,8192]{1,0:T(8,128)(2,1)S(1)}, bf16[16,8192]{1,0:T(8,128)(2,1)S(1)}, u32[]{:S(2)}, u32[]{:S(2)}) collective-permute-start(bf16[16,8192]{1,0:T(8,128)(2,1)S(1)} %collective-permute-done.1.refs_4_.refs_6_), channel_id=1, source_target_pairs={{0,48},{1,49},{2,50},{3,51},{4,52},{5,53},{6,54},{7,55},{8,56},{9,... | collective-permute-start | bytes 786440 | tf_op jit(solution)/shard_map/ppermute | solution.py:49
  20.4 3.2 %collective-permute-start.7 = (bf16[16,8192]{1,0:T(8,128)(2,1)S(1)}, bf16[16,8192]{1,0:T(8,128)(2,1)S(1)}, u32[]{:S(2)}, u32[]{:S(2)}) collective-permute-start(bf16[16,8192]{1,0:T(8,128)(2,1)S(1)} %collective-permute-done.1.refs_4_.refs_6_), channel_id=1, source_target_pairs={{0,192},{1,193},{2,194},{3,195},{4,196},{5,197},{6,198},{7,199},{8... | collective-permute-start | bytes 786440 | tf_op jit(solution)/shard_map/ppermute | solution.py:49
  23.8 3.2 %shifted_rows.5 = (bf16[256,8192]{1,0:T(8,128)(2,1)S(1)}, bf16[32,4096]{1,0:T(8,128)(2,1)S(1)}) custom-call(s32[1]{0:T(128)} %bitcast.2.member_ref, bf16[32,8576]{1,0:T(8,128)(2,1)S(1)} %collective-permute-done.x_ref, f32[4,8,1024]{2,1,0:T(8,128)S(1)} %get-tuple-element.53.geo_ref, bf16[256,8192]{1,0:T(8,128)(2,1)S(1)} %get-tuple-element.54.table_ref), custom_call_target="tpu_custom_call" | custom-call | tf_op jit(solution)/shard_map/shifted_rows/pallas_call | solution.py:97
  27.0 3.2 %shifted_rows.6 = (bf16[256,8192]{1,0:T(8,128)(2,1)S(1)}, bf16[32,4096]{1,0:T(8,128)(2,1)S(1)}) custom-call(s32[1]{0:T(128)} %bitcast.2.member_ref, bf16[32,8576]{1,0:T(8,128)(2,1)S(1)} %collective-permute-done.4.x_ref, f32[4,8,1024]{2,1,0:T(8,128)S(1)} %get-tuple-element.53.geo_ref, bf16[256,8192]{1,0:T(8,128)(2,1)S(1)} %get-tuple-element.54.table_ref), custom_call_target="tpu_custom_call" | custom-call | tf_op jit(solution)/shard_map/shifted_rows/pallas_call | solution.py:97
  30.2 2.0 %collective-permute-done.5.x_ref = bf16[32,8576]{1,0:T(8,128)(2,1)S(1)} collective-permute-done((bf16[32,8576]{1,0:T(8,128)(2,1)S(1)}, bf16[32,8576]{1,0:T(8,128)(2,1)S(1)}, u32[]{:S(2)}, u32[]{:S(2)}) %collective-permute-start.5) | collective-permute-done | bytes 548896 | tf_op jit(solution)/shard_map/ppermute | solution.py:49
  32.2 3.2 %shifted_rows.7 = (bf16[256,8192]{1,0:T(8,128)(2,1)S(1)}, bf16[32,4096]{1,0:T(8,128)(2,1)S(1)}) custom-call(s32[1]{0:T(128)} %bitcast.2.member_ref, bf16[32,8576]{1,0:T(8,128)(2,1)S(1)} %collective-permute-done.5.x_ref, f32[4,8,1024]{2,1,0:T(8,128)S(1)} %get-tuple-element.53.geo_ref, bf16[256,8192]{1,0:T(8,128)(2,1)S(1)} %get-tuple-element.54.table_ref), custom_call_target="tpu_custom_call" | custom-call | tf_op jit(solution)/shard_map/shifted_rows/pallas_call | solution.py:97
  35.4 1.5 %partial_scores.3 = f32[256,128]{1,0:T(8,128)S(1)} custom-call(bf16[256,8192]{1,0:T(8,128)(2,1)S(1)} %get-tuple-element.61.refs_0_.refs_3_, bf16[32,4096]{1,0:T(8,128)(2,1)S(1)} %get-tuple-element.69.refs_1_, bf16[16,8192]{1,0:T(8,128)(2,1)S(1)} %own_references.1.refs_2_.refs_4_, bf16[16,8192]{1,0:T(8,128)(2,1)S(1)} %collective-permute-done.3.refs_3_.refs_5_, ...), custom_call_target="tpu_custom_call" | custom-call | tf_op jit(solution)/shard_map/partial_scores/pallas_call | solution.py:97
  36.9 1.4 %collective-permute-start.10 = (f32[256,128]{1,0:T(8,128)S(1)}, f32[256,128]{1,0:T(8,128)S(1)}, u32[]{:S(2)}, u32[]{:S(2)}) collective-permute-start(f32[256,128]{1,0:T(8,128)S(1)} %partial_scores.3), channel_id=1, source_target_pairs={{0,2},{1,3},{2,0},{3,1},{4,6},{5,7},{6,4},{7,5},{8,10},{9,11},{10,... | collective-permute-start | bytes 393224 | tf_op jit(solution)/shard_map/ppermute | solution.py:49
  38.3 2.7 %partial_scores.4 = (f32[256,128]{1,0:T(8,128)S(1)}, f32[256,128]{1,0:T(8,128)S(1)}) custom-call(bf16[256,8192]{1,0:T(8,128)(2,1)S(1)} %get-tuple-element.65.refs_0_.refs_4_, bf16[256,8192]{1,0:T(8,128)(2,1)S(1)} %get-tuple-element.59.refs_1_.refs_2_, bf16[32,4096]{1,0:T(8,128)(2,1)S(1)} %get-tuple-element.73.refs_2_, ...), custom_call_target="tpu_custom_call" | custom-call | tf_op jit(solution)/shard_map/partial_scores/pallas_call | solution.py:97
  42.4 1.5 %partial_scores.5.refs_0_ = f32[256,128]{1,0:T(8,128)S(1)} custom-call(bf16[256,8192]{1,0:T(8,128)(2,1)S(1)} %get-tuple-element.55.refs_0_.refs_1_, bf16[32,4096]{1,0:T(8,128)(2,1)S(1)} %get-tuple-element.76.refs_1_, bf16[16,8192]{1,0:T(8,128)(2,1)S(1)} %own_references.1.refs_2_.refs_4_, bf16[16,8192]{1,0:T(8,128)(2,1)S(1)} %collective-permute-done.3.refs_3_.refs_5_, ...), custom_call_target="tpu_custom_call" | custom-call | tf_op jit(solution)/shard_map/partial_scores/pallas_call | solution.py:97
  44.0 2.9 %collective-permute-done.11.refs_1_ = f32[256,128]{1,0:T(8,128)S(1)} collective-permute-done((f32[256,128]{1,0:T(8,128)S(1)}, f32[256,128]{1,0:T(8,128)S(1)}, u32[]{:S(2)}, u32[]{:S(2)}) %collective-permute-start.11) | collective-permute-done | bytes 131104 | tf_op jit(solution)/shard_map/ppermute | solution.py:49
  49.1 3.1 %collective-permute-done.14.refs_7_ = bf16[128,256]{1,0:T(8,128)(2,1)S(1)} collective-permute-done((bf16[128,256]{1,0:T(8,128)(2,1)S(1)}, bf16[128,256]{1,0:T(8,128)(2,1)S(1)}, u32[]{:S(2)}, u32[]{:S(2)}) %collective-permute-start.14) | collective-permute-done | bytes 65568 | tf_op jit(solution)/shard_map/ppermute | solution.py:49
  52.7 1.8 %weighted_sums.2 = (bf16[32,4096]{1,0:T(8,128)(2,1)S(1)}, bf16[32,4096]{1,0:T(8,128)(2,1)S(1)}, bf16[32,4096]{1,0:T(8,128)(2,1)S(1)}, bf16[32,4096]{1,0:T(8,128)(2,1)S(1)}) custom-call(s32[1]{0:T(128)} %bitcast.1.x_ref.refs_0_, bf16[256,8192]{1,0:T(8,128)(2,1)S(1)} %get-tuple-element.55.refs_0_.refs_1_, ...), custom_call_target="tpu_custom_call" | custom-call | tf_op jit(solution)/shard_map/weighted_sums/pallas_call | solution.py:97
  54.5 1.5 %collective-permute-start.16 = (bf16[32,4096]{1,0:T(8,128)(2,1)S(1)}, bf16[32,4096]{1,0:T(8,128)(2,1)S(1)}, u32[]{:S(2)}, u32[]{:S(2)}) collective-permute-start(bf16[32,4096]{1,0:T(8,128)(2,1)S(1)} %get-tuple-element.79), channel_id=1, source_target_pairs={{0,64},{1,65},{2,66},{3,67},{4,68},{5,69},{6,70},{7,71},{8,72},{9,... | collective-permute-start | bytes 786440 | tf_op jit(solution)/shard_map/ppermute | solution.py:49
  56.0 3.7 %collective-permute-start.17 = (bf16[32,4096]{1,0:T(8,128)(2,1)S(1)}, bf16[32,4096]{1,0:T(8,128)(2,1)S(1)}, u32[]{:S(2)}, u32[]{:S(2)}) collective-permute-start(bf16[32,4096]{1,0:T(8,128)(2,1)S(1)} %get-tuple-element.80), channel_id=1, source_target_pairs={{0,128},{1,129},{2,130},{3,131},{4,132},{5,133},{6,134},{7,135},{8... | collective-permute-start | bytes 786440 | tf_op jit(solution)/shard_map/ppermute | solution.py:49
  60.3 1.9 %weighted_sums.3 = (bf16[64,2048]{1,0:T(8,128)(2,1)S(1)}, bf16[64,2048]{1,0:T(8,128)(2,1)S(1)}, bf16[64,2048]{1,0:T(8,128)(2,1)S(1)}, bf16[64,2048]{1,0:T(8,128)(2,1)S(1)}) custom-call(s32[1]{0:T(128)} %bitcast.1.x_ref.refs_0_, bf16[256,8192]{1,0:T(8,128)(2,1)S(1)} %get-tuple-element.55.refs_0_.refs_1_, ...), custom_call_target="tpu_custom_call" | custom-call | tf_op jit(solution)/shard_map/weighted_sums/pallas_call | solution.py:97
  62.2 1.6 %collective-permute-start.22 = (bf16[64,2048]{1,0:T(8,128)(2,1)S(1)}, bf16[64,2048]{1,0:T(8,128)(2,1)S(1)}, u32[]{:S(2)}, u32[]{:S(2)}) collective-permute-start(bf16[64,2048]{1,0:T(8,128)(2,1)S(1)} %get-tuple-element.87), channel_id=1, source_target_pairs={{0,32},{1,33},{2,34},{3,35},{4,36},{5,37},{6,38},{7,39},{8,40},{9,... | collective-permute-start | bytes 786440 | tf_op jit(solution)/shard_map/ppermute | solution.py:49
  65.1 1.4 %collective-permute-start.23 = (bf16[64,2048]{1,0:T(8,128)(2,1)S(1)}, bf16[64,2048]{1,0:T(8,128)(2,1)S(1)}, u32[]{:S(2)}, u32[]{:S(2)}) collective-permute-start(bf16[64,2048]{1,0:T(8,128)(2,1)S(1)} %get-tuple-element.89), channel_id=1, source_target_pairs={{0,16},{1,17},{2,18},{3,19},{4,20},{5,21},{6,22},{7,23},{8,24},{9,... | collective-permute-start | bytes 786440 | tf_op jit(solution)/shard_map/ppermute | solution.py:49
  66.4 5.4 %collective-permute-done.17.refs_2_ = bf16[32,4096]{1,0:T(8,128)(2,1)S(1)} collective-permute-done((bf16[32,4096]{1,0:T(8,128)(2,1)S(1)}, bf16[32,4096]{1,0:T(8,128)(2,1)S(1)}, u32[]{:S(2)}, u32[]{:S(2)}) %collective-permute-start.17) | collective-permute-done | bytes 262176 | tf_op jit(solution)/shard_map/ppermute | solution.py:49
  72.8 2.2 %collective-permute-start.20 = (bf16[16,2048]{1,0:T(8,128)(2,1)S(1)}, bf16[16,2048]{1,0:T(8,128)(2,1)S(1)}, u32[]{:S(2)}, u32[]{:S(2)}) collective-permute-start(bf16[16,2048]{1,0:T(8,128)(2,1)S(1)} %get-tuple-element.84), channel_id=1, source_target_pairs={{0,16},{1,17},{2,18},{3,19},{4,20},{5,21},{6,22},{7,23},{8,24},{9,... | collective-permute-start | bytes 196616 | tf_op jit(solution)/shard_map/ppermute | solution.py:49
  76.0 2.6 %collective-permute-done.23.refs_2_ = bf16[64,2048]{1,0:T(8,128)(2,1)S(1)} collective-permute-done((bf16[64,2048]{1,0:T(8,128)(2,1)S(1)}, bf16[64,2048]{1,0:T(8,128)(2,1)S(1)}, u32[]{:S(2)}, u32[]{:S(2)}) %collective-permute-start.23) | collective-permute-done | bytes 262176 | tf_op jit(solution)/shard_map/ppermute | solution.py:49
  79.0 2.3 %collective-permute-start.26 = (bf16[16,2048]{1,0:T(8,128)(2,1)S(1)}, bf16[16,2048]{1,0:T(8,128)(2,1)S(1)}, u32[]{:S(2)}, u32[]{:S(2)}) collective-permute-start(bf16[16,2048]{1,0:T(8,128)(2,1)S(1)} %get-tuple-element.93), channel_id=1, source_target_pairs={{0,128},{1,129},{2,130},{3,131},{4,132},{5,133},{6,134},{7,135},{8... | collective-permute-start | bytes 196616 | tf_op jit(solution)/shard_map/ppermute | solution.py:49
  81.3 2.5 %collective-permute-start.27 = (bf16[16,2048]{1,0:T(8,128)(2,1)S(1)}, bf16[16,2048]{1,0:T(8,128)(2,1)S(1)}, u32[]{:S(2)}, u32[]{:S(2)}) collective-permute-start(bf16[16,2048]{1,0:T(8,128)(2,1)S(1)} %get-tuple-element.94), channel_id=1, source_target_pairs={{0,192},{1,193},{2,194},{3,195},{4,196},{5,197},{6,198},{7,199},{8... | collective-permute-start | bytes 196616 | tf_op jit(solution)/shard_map/ppermute | solution.py:49
  85.9 3.4 %collective-permute-start.28 = (bf16[16,1024]{1,0:T(8,128)(2,1)S(1)}, bf16[16,1024]{1,0:T(8,128)(2,1)S(1)}, u32[]{:S(2)}, u32[]{:S(2)}) collective-permute-start(bf16[16,1024]{1,0:T(8,128)(2,1)S(1)} %get-tuple-element.96), channel_id=1, source_target_pairs={{0,4},{1,5},{2,6},{3,7},{4,8},{5,9},{6,10},{7,11},{8,12},{9,13},{1... | collective-permute-start | bytes 98312 | tf_op jit(solution)/shard_map/ppermute | solution.py:49
  89.3 5.2 %collective-permute-start.29 = (bf16[16,1024]{1,0:T(8,128)(2,1)S(1)}, bf16[16,1024]{1,0:T(8,128)(2,1)S(1)}, u32[]{:S(2)}, u32[]{:S(2)}) collective-permute-start(bf16[16,1024]{1,0:T(8,128)(2,1)S(1)} %get-tuple-element.97), channel_id=1, source_target_pairs={{0,8},{1,9},{2,10},{3,11},{4,12},{5,13},{6,14},{7,15},{8,0},{9,1},... | collective-permute-start | bytes 98312 | tf_op jit(solution)/shard_map/ppermute | solution.py:49
  94.5 2.7 %collective-permute-start.30 = (bf16[16,1024]{1,0:T(8,128)(2,1)S(1)}, bf16[16,1024]{1,0:T(8,128)(2,1)S(1)}, u32[]{:S(2)}, u32[]{:S(2)}) collective-permute-start(bf16[16,1024]{1,0:T(8,128)(2,1)S(1)} %get-tuple-element.98), channel_id=1, source_target_pairs={{0,12},{1,13},{2,14},{3,15},{4,0},{5,1},{6,2},{7,3},{8,4},{9,5},{1... | collective-permute-start | bytes 98312 | tf_op jit(solution)/shard_map/ppermute | solution.py:49
  97.3 2.1 %collective-permute-done.30 = bf16[16,1024]{1,0:T(8,128)(2,1)S(1)} collective-permute-done((bf16[16,1024]{1,0:T(8,128)(2,1)S(1)}, bf16[16,1024]{1,0:T(8,128)(2,1)S(1)}, u32[]{:S(2)}, u32[]{:S(2)}) %collective-permute-start.30) | collective-permute-done | bytes 32800 | tf_op jit(solution)/shard_map/ppermute | solution.py:49
  (47 shorter events, 13.5 us)
Async XLA Ops:
  2.0 15.4 %collective-permute-start = (bf16[32,8576]{1,0:T(8,128)(2,1)S(1)}, bf16[32,8576]{1,0:T(8,128)(2,1)S(1)}, u32[]{:S(2)}, u32[]{:S(2)}) collective-permute-start(bf16[32,8576]{1,0:T(8,128)(2,1)S(1)} %get-tuple-element.56), channel_id=1, source_target_pairs={{0,1},{1,0},{2,3},{3,2},{4,5},{5,4},{6,7},{7,6},{8,9},{9,8},{10,11... | collective-permute-start | bytes 1646600 | tf_op jit(solution)/shard_map/ppermute | solution.py:49
  2.1 15.3 %collective-permute-start.4 = (bf16[32,8576]{1,0:T(8,128)(2,1)S(1)}, bf16[32,8576]{1,0:T(8,128)(2,1)S(1)}, u32[]{:S(2)}, u32[]{:S(2)}) collective-permute-start(bf16[32,8576]{1,0:T(8,128)(2,1)S(1)} %get-tuple-element.57.after), channel_id=1, source_target_pairs={{0,2},{1,3},{2,0},{3,1},{4,6},{5,7},{6,4},{7,5},{8,10},{9,11},{10,... | collective-permute-start | bytes 1646600 | tf_op jit(solution)/shard_map/ppermute | solution.py:49
  5.0 12.3 %collective-permute-start.1 = (bf16[16,8192]{1,0:T(8,128)(2,1)S(1)}, bf16[16,8192]{1,0:T(8,128)(2,1)S(1)}, u32[]{:S(2)}, u32[]{:S(2)}) collective-permute-start(bf16[16,8192]{1,0:T(8,128)(2,1)S(1)} %own_references.1.refs_2_.refs_4_), channel_id=1, source_target_pairs={{0,192},{1,193},{2,194},{3,195},{4,196},{5,197},{6,198},{7,199},{8... | collective-permute-start | bytes 786440 | tf_op jit(solution)/shard_map/ppermute | solution.py:49
  8.1 9.3 %collective-permute-start.2 = (bf16[16,8192]{1,0:T(8,128)(2,1)S(1)}, bf16[16,8192]{1,0:T(8,128)(2,1)S(1)}, u32[]{:S(2)}, u32[]{:S(2)}) collective-permute-start(bf16[16,8192]{1,0:T(8,128)(2,1)S(1)} %own_references.1.refs_2_.refs_4_), channel_id=1, source_target_pairs={{0,64},{1,65},{2,66},{3,67},{4,68},{5,69},{6,70},{7,71},{8,72},{9,... | collective-permute-start | bytes 786440 | tf_op jit(solution)/shard_map/ppermute | solution.py:49
  8.1 9.3 %collective-permute-start.3 = (bf16[16,8192]{1,0:T(8,128)(2,1)S(1)}, bf16[16,8192]{1,0:T(8,128)(2,1)S(1)}, u32[]{:S(2)}, u32[]{:S(2)}) collective-permute-start(bf16[16,8192]{1,0:T(8,128)(2,1)S(1)} %own_references.1.refs_2_.refs_4_), channel_id=1, source_target_pairs={{0,48},{1,49},{2,50},{3,51},{4,52},{5,53},{6,54},{7,55},{8,56},{9,... | collective-permute-start | bytes 786440 | tf_op jit(solution)/shard_map/ppermute | solution.py:49
  17.4 14.7 %collective-permute-start.5 = (bf16[32,8576]{1,0:T(8,128)(2,1)S(1)}, bf16[32,8576]{1,0:T(8,128)(2,1)S(1)}, u32[]{:S(2)}, u32[]{:S(2)}) collective-permute-start(bf16[32,8576]{1,0:T(8,128)(2,1)S(1)} %get-tuple-element.63), channel_id=1, source_target_pairs={{0,3},{1,2},{2,1},{3,0},{4,7},{5,6},{6,5},{7,4},{8,11},{9,10},{10,... | collective-permute-start | bytes 1646600 | tf_op jit(solution)/shard_map/ppermute | solution.py:49
  18.1 17.2 %collective-permute-start.6 = (bf16[16,8192]{1,0:T(8,128)(2,1)S(1)}, bf16[16,8192]{1,0:T(8,128)(2,1)S(1)}, u32[]{:S(2)}, u32[]{:S(2)}) collective-permute-start(bf16[16,8192]{1,0:T(8,128)(2,1)S(1)} %collective-permute-done.1.refs_4_.refs_6_), channel_id=1, source_target_pairs={{0,48},{1,49},{2,50},{3,51},{4,52},{5,53},{6,54},{7,55},{8,56},{9,... | collective-permute-start | bytes 786440 | tf_op jit(solution)/shard_map/ppermute | solution.py:49
  20.4 15.0 %collective-permute-start.7 = (bf16[16,8192]{1,0:T(8,128)(2,1)S(1)}, bf16[16,8192]{1,0:T(8,128)(2,1)S(1)}, u32[]{:S(2)}, u32[]{:S(2)}) collective-permute-start(bf16[16,8192]{1,0:T(8,128)(2,1)S(1)} %collective-permute-done.1.refs_4_.refs_6_), channel_id=1, source_target_pairs={{0,192},{1,193},{2,194},{3,195},{4,196},{5,197},{6,198},{7,199},{8... | collective-permute-start | bytes 786440 | tf_op jit(solution)/shard_map/ppermute | solution.py:49
  23.6 11.8 %collective-permute-start.8 = (bf16[16,8192]{1,0:T(8,128)(2,1)S(1)}, bf16[16,8192]{1,0:T(8,128)(2,1)S(1)}, u32[]{:S(2)}, u32[]{:S(2)}) collective-permute-start(bf16[16,8192]{1,0:T(8,128)(2,1)S(1)} %collective-permute-done.3.refs_3_.refs_5_), channel_id=1, source_target_pairs={{0,128},{1,129},{2,130},{3,131},{4,132},{5,133},{6,134},{7,135},{8... | collective-permute-start | bytes 786440 | tf_op jit(solution)/shard_map/ppermute | solution.py:49
  23.6 11.8 %collective-permute-start.9 = (bf16[16,8192]{1,0:T(8,128)(2,1)S(1)}, bf16[16,8192]{1,0:T(8,128)(2,1)S(1)}, u32[]{:S(2)}, u32[]{:S(2)}) collective-permute-start(bf16[16,8192]{1,0:T(8,128)(2,1)S(1)} %collective-permute-done.2.refs_8_.refs_10_), channel_id=1, source_target_pairs={{0,32},{1,33},{2,34},{3,35},{4,36},{5,37},{6,38},{7,39},{8,40},{9,... | collective-permute-start | bytes 786440 | tf_op jit(solution)/shard_map/ppermute | solution.py:49
  36.9 5.5 %collective-permute-start.10 = (f32[256,128]{1,0:T(8,128)S(1)}, f32[256,128]{1,0:T(8,128)S(1)}, u32[]{:S(2)}, u32[]{:S(2)}) collective-permute-start(f32[256,128]{1,0:T(8,128)S(1)} %partial_scores.3), channel_id=1, source_target_pairs={{0,2},{1,3},{2,0},{3,1},{4,6},{5,7},{6,4},{7,5},{8,10},{9,11},{10,... | collective-permute-start | bytes 393224 | tf_op jit(solution)/shard_map/ppermute | solution.py:49
  41.0 5.8 %collective-permute-start.11 = (f32[256,128]{1,0:T(8,128)S(1)}, f32[256,128]{1,0:T(8,128)S(1)}, u32[]{:S(2)}, u32[]{:S(2)}) collective-permute-start(f32[256,128]{1,0:T(8,128)S(1)} %get-tuple-element.75), channel_id=1, source_target_pairs={{0,3},{1,2},{2,1},{3,0},{4,7},{5,6},{6,5},{7,4},{8,11},{9,10},{10,... | collective-permute-start | bytes 393224 | tf_op jit(solution)/shard_map/ppermute | solution.py:49
  41.2 5.7 %collective-permute-start.12 = (f32[256,128]{1,0:T(8,128)S(1)}, f32[256,128]{1,0:T(8,128)S(1)}, u32[]{:S(2)}, u32[]{:S(2)}) collective-permute-start(f32[256,128]{1,0:T(8,128)S(1)} %get-tuple-element.77), channel_id=1, source_target_pairs={{0,1},{1,0},{2,3},{3,2},{4,5},{5,4},{6,7},{7,6},{8,9},{9,8},{10,11... | collective-permute-start | bytes 393224 | tf_op jit(solution)/shard_map/ppermute | solution.py:49
  47.2 2.0 %collective-permute-start.13 = (bf16[128,256]{1,0:T(8,128)(2,1)S(1)}, bf16[128,256]{1,0:T(8,128)(2,1)S(1)}, u32[]{:S(2)}, u32[]{:S(2)}) collective-permute-start(bf16[128,256]{1,0:T(8,128)(2,1)S(1)} %posterior.1.refs_5_), channel_id=1, source_target_pairs={{0,1},{1,0},{2,3},{3,2},{4,5},{5,4},{6,7},{7,6},{8,9},{9,8},{10,11... | collective-permute-start | bytes 196616 | tf_op jit(solution)/shard_map/ppermute | solution.py:49
  47.3 4.9 %collective-permute-start.14 = (bf16[128,256]{1,0:T(8,128)(2,1)S(1)}, bf16[128,256]{1,0:T(8,128)(2,1)S(1)}, u32[]{:S(2)}, u32[]{:S(2)}) collective-permute-start(bf16[128,256]{1,0:T(8,128)(2,1)S(1)} %posterior.1.refs_5_), channel_id=1, source_target_pairs={{0,2},{1,3},{2,0},{3,1},{4,6},{5,7},{6,4},{7,5},{8,10},{9,11},{10,... | collective-permute-start | bytes 196616 | tf_op jit(solution)/shard_map/ppermute | solution.py:49
  48.0 4.7 %collective-permute-start.15 = (bf16[128,256]{1,0:T(8,128)(2,1)S(1)}, bf16[128,256]{1,0:T(8,128)(2,1)S(1)}, u32[]{:S(2)}, u32[]{:S(2)}) collective-permute-start(bf16[128,256]{1,0:T(8,128)(2,1)S(1)} %posterior.1.refs_5_), channel_id=1, source_target_pairs={{0,3},{1,2},{2,1},{3,0},{4,7},{5,6},{6,5},{7,4},{8,11},{9,10},{10,... | collective-permute-start | bytes 196616 | tf_op jit(solution)/shard_map/ppermute | solution.py:49
  54.5 10.5 %collective-permute-start.16 = (bf16[32,4096]{1,0:T(8,128)(2,1)S(1)}, bf16[32,4096]{1,0:T(8,128)(2,1)S(1)}, u32[]{:S(2)}, u32[]{:S(2)}) collective-permute-start(bf16[32,4096]{1,0:T(8,128)(2,1)S(1)} %get-tuple-element.79), channel_id=1, source_target_pairs={{0,64},{1,65},{2,66},{3,67},{4,68},{5,69},{6,70},{7,71},{8,72},{9,... | collective-permute-start | bytes 786440 | tf_op jit(solution)/shard_map/ppermute | solution.py:49
  56.0 15.8 %collective-permute-start.17 = (bf16[32,4096]{1,0:T(8,128)(2,1)S(1)}, bf16[32,4096]{1,0:T(8,128)(2,1)S(1)}, u32[]{:S(2)}, u32[]{:S(2)}) collective-permute-start(bf16[32,4096]{1,0:T(8,128)(2,1)S(1)} %get-tuple-element.80), channel_id=1, source_target_pairs={{0,128},{1,129},{2,130},{3,131},{4,132},{5,133},{6,134},{7,135},{8... | collective-permute-start | bytes 786440 | tf_op jit(solution)/shard_map/ppermute | solution.py:49
  59.8 12.1 %collective-permute-start.18 = (bf16[32,4096]{1,0:T(8,128)(2,1)S(1)}, bf16[32,4096]{1,0:T(8,128)(2,1)S(1)}, u32[]{:S(2)}, u32[]{:S(2)}) collective-permute-start(bf16[32,4096]{1,0:T(8,128)(2,1)S(1)} %get-tuple-element.81), channel_id=1, source_target_pairs={{0,192},{1,193},{2,194},{3,195},{4,196},{5,197},{6,198},{7,199},{8... | collective-permute-start | bytes 786440 | tf_op jit(solution)/shard_map/ppermute | solution.py:49
  62.2 12.7 %collective-permute-start.22 = (bf16[64,2048]{1,0:T(8,128)(2,1)S(1)}, bf16[64,2048]{1,0:T(8,128)(2,1)S(1)}, u32[]{:S(2)}, u32[]{:S(2)}) collective-permute-start(bf16[64,2048]{1,0:T(8,128)(2,1)S(1)} %get-tuple-element.87), channel_id=1, source_target_pairs={{0,32},{1,33},{2,34},{3,35},{4,36},{5,37},{6,38},{7,39},{8,40},{9,... | collective-permute-start | bytes 786440 | tf_op jit(solution)/shard_map/ppermute | solution.py:49
  63.8 12.2 %collective-permute-start.24 = (bf16[64,2048]{1,0:T(8,128)(2,1)S(1)}, bf16[64,2048]{1,0:T(8,128)(2,1)S(1)}, u32[]{:S(2)}, u32[]{:S(2)}) collective-permute-start(bf16[64,2048]{1,0:T(8,128)(2,1)S(1)} %get-tuple-element.90), channel_id=1, source_target_pairs={{0,48},{1,49},{2,50},{3,51},{4,52},{5,53},{6,54},{7,55},{8,56},{9,... | collective-permute-start | bytes 786440 | tf_op jit(solution)/shard_map/ppermute | solution.py:49
  65.1 13.5 %collective-permute-start.23 = (bf16[64,2048]{1,0:T(8,128)(2,1)S(1)}, bf16[64,2048]{1,0:T(8,128)(2,1)S(1)}, u32[]{:S(2)}, u32[]{:S(2)}) collective-permute-start(bf16[64,2048]{1,0:T(8,128)(2,1)S(1)} %get-tuple-element.89), channel_id=1, source_target_pairs={{0,16},{1,17},{2,18},{3,19},{4,20},{5,21},{6,22},{7,23},{8,24},{9,... | collective-permute-start | bytes 786440 | tf_op jit(solution)/shard_map/ppermute | solution.py:49
  72.0 9.3 %collective-permute-start.19 = (bf16[16,2048]{1,0:T(8,128)(2,1)S(1)}, bf16[16,2048]{1,0:T(8,128)(2,1)S(1)}, u32[]{:S(2)}, u32[]{:S(2)}) collective-permute-start(bf16[16,2048]{1,0:T(8,128)(2,1)S(1)} %get-tuple-element.83), channel_id=1, source_target_pairs={{0,32},{1,33},{2,34},{3,35},{4,36},{5,37},{6,38},{7,39},{8,40},{9,... | collective-permute-start | bytes 196616 | tf_op jit(solution)/shard_map/ppermute | solution.py:49
  72.8 11.1 %collective-permute-start.20 = (bf16[16,2048]{1,0:T(8,128)(2,1)S(1)}, bf16[16,2048]{1,0:T(8,128)(2,1)S(1)}, u32[]{:S(2)}, u32[]{:S(2)}) collective-permute-start(bf16[16,2048]{1,0:T(8,128)(2,1)S(1)} %get-tuple-element.84), channel_id=1, source_target_pairs={{0,16},{1,17},{2,18},{3,19},{4,20},{5,21},{6,22},{7,23},{8,24},{9,... | collective-permute-start | bytes 196616 | tf_op jit(solution)/shard_map/ppermute | solution.py:49
  75.0 8.9 %collective-permute-start.21 = (bf16[16,2048]{1,0:T(8,128)(2,1)S(1)}, bf16[16,2048]{1,0:T(8,128)(2,1)S(1)}, u32[]{:S(2)}, u32[]{:S(2)}) collective-permute-start(bf16[16,2048]{1,0:T(8,128)(2,1)S(1)} %get-tuple-element.85), channel_id=1, source_target_pairs={{0,48},{1,49},{2,50},{3,51},{4,52},{5,53},{6,54},{7,55},{8,56},{9,... | collective-permute-start | bytes 196616 | tf_op jit(solution)/shard_map/ppermute | solution.py:49
  78.7 6.3 %collective-permute-start.25 = (bf16[16,2048]{1,0:T(8,128)(2,1)S(1)}, bf16[16,2048]{1,0:T(8,128)(2,1)S(1)}, u32[]{:S(2)}, u32[]{:S(2)}) collective-permute-start(bf16[16,2048]{1,0:T(8,128)(2,1)S(1)} %get-tuple-element.92), channel_id=1, source_target_pairs={{0,64},{1,65},{2,66},{3,67},{4,68},{5,69},{6,70},{7,71},{8,72},{9,... | collective-permute-start | bytes 196616 | tf_op jit(solution)/shard_map/ppermute | solution.py:49
  79.0 6.0 %collective-permute-start.26 = (bf16[16,2048]{1,0:T(8,128)(2,1)S(1)}, bf16[16,2048]{1,0:T(8,128)(2,1)S(1)}, u32[]{:S(2)}, u32[]{:S(2)}) collective-permute-start(bf16[16,2048]{1,0:T(8,128)(2,1)S(1)} %get-tuple-element.93), channel_id=1, source_target_pairs={{0,128},{1,129},{2,130},{3,131},{4,132},{5,133},{6,134},{7,135},{8... | collective-permute-start | bytes 196616 | tf_op jit(solution)/shard_map/ppermute | solution.py:49
  81.3 4.6 %collective-permute-start.27 = (bf16[16,2048]{1,0:T(8,128)(2,1)S(1)}, bf16[16,2048]{1,0:T(8,128)(2,1)S(1)}, u32[]{:S(2)}, u32[]{:S(2)}) collective-permute-start(bf16[16,2048]{1,0:T(8,128)(2,1)S(1)} %get-tuple-element.94), channel_id=1, source_target_pairs={{0,192},{1,193},{2,194},{3,195},{4,196},{5,197},{6,198},{7,199},{8... | collective-permute-start | bytes 196616 | tf_op jit(solution)/shard_map/ppermute | solution.py:49
  85.9 11.4 %collective-permute-start.28 = (bf16[16,1024]{1,0:T(8,128)(2,1)S(1)}, bf16[16,1024]{1,0:T(8,128)(2,1)S(1)}, u32[]{:S(2)}, u32[]{:S(2)}) collective-permute-start(bf16[16,1024]{1,0:T(8,128)(2,1)S(1)} %get-tuple-element.96), channel_id=1, source_target_pairs={{0,4},{1,5},{2,6},{3,7},{4,8},{5,9},{6,10},{7,11},{8,12},{9,13},{1... | collective-permute-start | bytes 98312 | tf_op jit(solution)/shard_map/ppermute | solution.py:49
  89.3 7.9 %collective-permute-start.29 = (bf16[16,1024]{1,0:T(8,128)(2,1)S(1)}, bf16[16,1024]{1,0:T(8,128)(2,1)S(1)}, u32[]{:S(2)}, u32[]{:S(2)}) collective-permute-start(bf16[16,1024]{1,0:T(8,128)(2,1)S(1)} %get-tuple-element.97), channel_id=1, source_target_pairs={{0,8},{1,9},{2,10},{3,11},{4,12},{5,13},{6,14},{7,15},{8,0},{9,1},... | collective-permute-start | bytes 98312 | tf_op jit(solution)/shard_map/ppermute | solution.py:49
  94.5 4.8 %collective-permute-start.30 = (bf16[16,1024]{1,0:T(8,128)(2,1)S(1)}, bf16[16,1024]{1,0:T(8,128)(2,1)S(1)}, u32[]{:S(2)}, u32[]{:S(2)}) collective-permute-start(bf16[16,1024]{1,0:T(8,128)(2,1)S(1)} %get-tuple-element.98), channel_id=1, source_target_pairs={{0,12},{1,13},{2,14},{3,15},{4,0},{5,1},{6,2},{7,3},{8,4},{9,5},{1... | collective-permute-start | bytes 98312 | tf_op jit(solution)/shard_map/ppermute | solution.py:49

commit v9 on v8

--- a/solution.py
+++ b/solution.py
@@ -31,10 +31,10 @@
     return (y * 2 + x % 2) * 32 + (x // 2) * 16 + z * 2 + core
 
 
-def moves(dy=0, dx=0, dz=0):
+def flips(y=0, x=0, z=0):
     return [
-        (linear(y, x, z, c), linear(y + dy, x + dx, z + dz, c))
-        for y in range(Y) for x in range(X) for z in range(Z) for c in range(2)
+        (linear(i, j, k, c), linear(i ^ y, j ^ x, k ^ z, c))
+        for i in range(Y) for j in range(X) for k in range(Z) for c in range(2)
     ]
 
 
@@ -359,7 +359,7 @@
         else:
             for n in range(X):
                 low = n & 1
-                upper = ((x_ref[0] + n) & (X - 1)) >= 2
+                upper = (x_ref[0] >> 1) ^ (n >> 1) == 1
                 spot = pl.multiple_of(block * HALF, HALF)
                 for k in range(Y):
                     mine = slice(k * 32 + low * 16, k * 32 + low * 16 + 16)
@@ -393,7 +393,7 @@
         imag = added([ref[:, start + HALF : start + COLS] for ref in refs[:4]])
         for n, out in enumerate(outs):
             mine = slice((n & 1) * 16, (n & 1) * 16 + 16)
-            chosen = jnp.where(((x_ref[0] + n) & (X - 1)) >= 2, imag[mine], real[mine])
+            chosen = jnp.where((x_ref[0] >> 1) ^ (n >> 1) == 1, imag[mine], real[mine])
             out[:, block * HALF : (block + 1) * HALF] = chosen.astype(out.dtype)
 
 
@@ -404,7 +404,7 @@
 
 def joined_kernel(block_ref, *refs):
     for n, out in enumerate(refs[8:]):
-        spot = pl.ds(pl.multiple_of(((block_ref[0] + n) % NB) * HALF, HALF), HALF)
+        spot = pl.ds(pl.multiple_of((block_ref[0] ^ n) * HALF, HALF), HALF)
         out[:, :HALF] = added([ref[:, spot] for ref in refs[:4]]).astype(out.dtype)
         out[:, HALF:] = added([ref[:, spot] for ref in refs[4:8]]).astype(out.dtype)
 
@@ -426,16 +426,16 @@
     got[1] = send(chunks[1], partners(1))
     own = own_columns(member, refs, chunks[2])
     gathered[0, 0] = own
-    gathered[1, 0] = send(own, moves(dy=-1))
-    gathered[3, 0] = send(own, moves(dy=1))
-    gathered[0, 1] = send(own, moves(dx=-1))
+    gathered[1, 0] = send(own, flips(y=1))
+    gathered[3, 0] = send(own, flips(y=3))
+    gathered[0, 1] = send(own, flips(x=1))
     table, geo = make_table(member, geo)
     rows[0], pens[0] = make_rows(member, chunks[0], geo, table)
     wave = [got[1], gathered[1, 0], gathered[3, 0], gathered[0, 1], rows[0]]
-    gathered[1, 1] = send(after(gathered[1, 0], *wave), moves(dx=-1))
-    gathered[3, 1] = send(after(gathered[3, 0], *wave), moves(dx=1))
-    gathered[2, 1] = send(after(gathered[0, 1], *wave), moves(dy=2))
-    gathered[2, 0] = send(after(gathered[1, 0], *wave), moves(dy=-1))
+    gathered[1, 1] = send(after(gathered[1, 0], *wave), flips(x=1))
+    gathered[3, 1] = send(after(gathered[3, 0], *wave), flips(x=3))
+    gathered[2, 1] = send(after(gathered[0, 1], *wave), flips(y=2))
+    gathered[2, 0] = send(after(gathered[1, 0], *wave), flips(y=3))
     got[3] = send(after(chunks[3], *wave, got[2]), partners(3))
     rows[1], pens[1] = make_rows(member, after(got[1], *wave, got[2]), geo, table)
     rows[2], pens[2] = make_rows(member, after(got[2], rows[1]), geo, table)
@@ -451,21 +451,21 @@
     rows = [rows[n] for n in range(G)]
 
     first = make_accum(0, x_at, rows, posts)
-    first = [first[0]] + [send(first[n], moves(dy=n)) for n in range(1, Y)]
+    first = [first[0]] + [send(first[n], flips(y=n)) for n in range(1, Y)]
     second = make_accum(1, x_at, rows, posts)
     second = [
         second[0],
-        send(second[1], moves(dx=1)),
-        send(after(second[2], first[1]), moves(dx=2)),
-        send(second[3], moves(dx=3)),
+        send(second[1], flips(x=1)),
+        send(after(second[2], first[1]), flips(x=2)),
+        send(second[3], flips(x=3)),
     ]
     first = local(first_kernel, "first_sums", PIECES, [x_at], first, 4)
-    first = [first[0]] + [send(first[n], moves(dx=n)) for n in range(1, X)]
+    first = [first[0]] + [send(first[n], flips(x=n)) for n in range(1, X)]
     second = local(second_kernel, "second_sums", PIECES, [], second, 4)
-    second = [second[0]] + [send(second[n], moves(dy=n)) for n in range(1, Y)]
+    second = [second[0]] + [send(second[n], flips(y=n)) for n in range(1, Y)]
     outs = [((16, COLS), F32)] + [((16, COLS), BF16)] * (NB - 1)
     ends = local(joined_kernel, "joined_sums", outs, [block], [*first, *second], 4)
-    return added([ends[0]] + [send(ends[n], moves(dz=n * (G // 2))) for n in range(1, NB)])
+    return added([ends[0]] + [send(ends[n], flips(z=n * (G // 2))) for n in range(1, NB)])
 
 
 def solution(mesh):

time: 101 us -> 103 us (1.020)
  waiting for transfers between devices: 21.9 us -> 27 us
  starting transfers between devices: 46 us -> 42.7 us
    ppermute x31, waiting for transfers between devices: 21.9 us -> 27 us  [send(): return lax.ppermute(value, AXES, pairs)]
    ppermute x31, starting transfers between devices: 46 us -> 42.7 us  [send(): return lax.ppermute(value, AXES, pairs)]
  transfers between devices with their start and end apart: 31 -> 31, of which waited for: 11 -> 11; matrix products, arithmetic and copies ran while one was open for 0% -> 0% of each run, Pallas kernels for 26% -> 25%
where the time goes in v9:
time: 103 us; the launch traced here: 102 us
  starting transfers between devices  42.7 us (41%)
  Pallas kernels  31.3 us (30%)
  waiting for transfers between devices  27 us (26%)
    ppermute x31, starting transfers between devices, send(): return lax.ppermute(value, AXES, pairs)  42.7 us
    pallas_call x16, Pallas kernels, local(): pl.pallas_call(kernel, in_specs=[SCALARS] * len(scalars) + [PLACED] * pla...  31.3 us
    ppermute x31, waiting for transfers between devices, send(): return lax.ppermute(value, AXES, pairs)  27 us
  transfers between devices with their start and end apart: 31, of which 11 were waited for; matrix products, arithmetic and copies ran while one was open for 0% of the time, Pallas kernels for 25%

profile of v9, /device:TPU:2, one launch (start us, length us, event | category | flops | bytes accessed | tf_op | source)
XLA Modules:
  0.0 101.9 jit_solution(3411730710798729718)
XLA Ops:
  0.0 2.0 %split_particles.1 = (bf16[32,8576]{1,0:T(8,128)(2,1)S(1)}, bf16[32,8576]{1,0:T(8,128)(2,1)S(1)}, bf16[32,8576]{1,0:T(8,128)(2,1)S(1)}, bf16[32,8576]{1,0:T(8,128)(2,1)S(1)}) custom-call(s32[1]{0:T(128)} %bitcast.2.member_ref, s32[1]{0:T(128)} %bitcast.block_ref, s32[1]{0:T(128)} %bitcast.1.x_ref.refs_0_, bf16[32,32768]{1,0:T(8,128)(2,1)} %source.2, ...), custom_call_target="tpu_custom_call" | custom-call | tf_op jit(solution)/shard_map/split_particles/pallas_call | solution.py:97
  2.1 2.0 %collective-permute-start.4 = (bf16[32,8576]{1,0:T(8,128)(2,1)S(1)}, bf16[32,8576]{1,0:T(8,128)(2,1)S(1)}, u32[]{:S(2)}, u32[]{:S(2)}) collective-permute-start(bf16[32,8576]{1,0:T(8,128)(2,1)S(1)} %get-tuple-element.57.after), channel_id=1, source_target_pairs={{0,2},{1,3},{2,0},{3,1},{4,6},{5,7},{6,4},{7,5},{8,10},{9,11},{10,... | collective-permute-start | bytes 1646600 | tf_op jit(solution)/shard_map/ppermute | solution.py:49
  5.0 1.7 %collective-permute-start.1 = (bf16[16,8192]{1,0:T(8,128)(2,1)S(1)}, bf16[16,8192]{1,0:T(8,128)(2,1)S(1)}, u32[]{:S(2)}, u32[]{:S(2)}) collective-permute-start(bf16[16,8192]{1,0:T(8,128)(2,1)S(1)} %own_references.1.refs_2_.refs_4_), channel_id=1, source_target_pairs={{0,64},{1,65},{2,66},{3,67},{4,68},{5,69},{6,70},{7,71},{8,72},{9,... | collective-permute-start | bytes 786440 | tf_op jit(solution)/shard_map/ppermute | solution.py:49
  6.7 2.2 %collective-permute-start.2 = (bf16[16,8192]{1,0:T(8,128)(2,1)S(1)}, bf16[16,8192]{1,0:T(8,128)(2,1)S(1)}, u32[]{:S(2)}, u32[]{:S(2)}) collective-permute-start(bf16[16,8192]{1,0:T(8,128)(2,1)S(1)} %own_references.1.refs_2_.refs_4_), channel_id=1, source_target_pairs={{0,192},{1,193},{2,194},{3,195},{4,196},{5,197},{6,198},{7,199},{8... | collective-permute-start | bytes 786440 | tf_op jit(solution)/shard_map/ppermute | solution.py:49
  9.4 5.5 %phase_table.1 = (bf16[256,8192]{1,0:T(8,128)(2,1)S(1)}, f32[4,8,1024]{2,1,0:T(8,128)S(1)}) custom-call(s32[1]{0:T(128)} %bitcast.2.member_ref, f32[16,8,1024]{2,1,0:T(8,128)} %constant.63.clone.geo_ref), custom_call_target="tpu_custom_call" | custom-call | tf_op jit(solution)/shard_map/phase_table/pallas_call | solution.py:97
  14.9 3.2 %shifted_rows.4 = (bf16[256,8192]{1,0:T(8,128)(2,1)S(1)}, bf16[32,4096]{1,0:T(8,128)(2,1)S(1)}) custom-call(s32[1]{0:T(128)} %bitcast.2.member_ref, bf16[32,8576]{1,0:T(8,128)(2,1)S(1)} %get-tuple-element.52.x_ref, f32[4,8,1024]{2,1,0:T(8,128)S(1)} %get-tuple-element.53.geo_ref, bf16[256,8192]{1,0:T(8,128)(2,1)S(1)} %get-tuple-element.54.table_ref), custom_call_target="tpu_custom_call" | custom-call | tf_op jit(solution)/shard_map/shifted_rows/pallas_call | solution.py:97
  18.3 1.6 %collective-permute-start.6 = (bf16[16,8192]{1,0:T(8,128)(2,1)S(1)}, bf16[16,8192]{1,0:T(8,128)(2,1)S(1)}, u32[]{:S(2)}, u32[]{:S(2)}) collective-permute-start(bf16[16,8192]{1,0:T(8,128)(2,1)S(1)} %collective-permute-done.1.refs_4_.refs_6_), channel_id=1, source_target_pairs={{0,32},{1,33},{2,34},{3,35},{4,36},{5,37},{6,38},{7,39},{8,40},{9,... | collective-permute-start | bytes 786440 | tf_op jit(solution)/shard_map/ppermute | solution.py:49
  19.8 1.8 %collective-permute-start.7 = (bf16[16,8192]{1,0:T(8,128)(2,1)S(1)}, bf16[16,8192]{1,0:T(8,128)(2,1)S(1)}, u32[]{:S(2)}, u32[]{:S(2)}) collective-permute-start(bf16[16,8192]{1,0:T(8,128)(2,1)S(1)} %collective-permute-done.1.refs_4_.refs_6_), channel_id=1, source_target_pairs={{0,192},{1,193},{2,194},{3,195},{4,196},{5,197},{6,198},{7,199},{8... | collective-permute-start | bytes 786440 | tf_op jit(solution)/shard_map/ppermute | solution.py:49
  22.6 1.9 %collective-permute-start.9 = (bf16[16,8192]{1,0:T(8,128)(2,1)S(1)}, bf16[16,8192]{1,0:T(8,128)(2,1)S(1)}, u32[]{:S(2)}, u32[]{:S(2)}) collective-permute-start(bf16[16,8192]{1,0:T(8,128)(2,1)S(1)} %collective-permute-done.2.refs_8_.refs_10_), channel_id=1, source_target_pairs={{0,48},{1,49},{2,50},{3,51},{4,52},{5,53},{6,54},{7,55},{8,56},{9,... | collective-permute-start | bytes 786440 | tf_op jit(solution)/shard_map/ppermute | solution.py:49
  24.4 3.2 %shifted_rows.5 = (bf16[256,8192]{1,0:T(8,128)(2,1)S(1)}, bf16[32,4096]{1,0:T(8,128)(2,1)S(1)}) custom-call(s32[1]{0:T(128)} %bitcast.2.member_ref, bf16[32,8576]{1,0:T(8,128)(2,1)S(1)} %collective-permute-done.x_ref, f32[4,8,1024]{2,1,0:T(8,128)S(1)} %get-tuple-element.53.geo_ref, bf16[256,8192]{1,0:T(8,128)(2,1)S(1)} %get-tuple-element.54.table_ref), custom_call_target="tpu_custom_call" | custom-call | tf_op jit(solution)/shard_map/shifted_rows/pallas_call | solution.py:97
  27.6 3.2 %shifted_rows.6 = (bf16[256,8192]{1,0:T(8,128)(2,1)S(1)}, bf16[32,4096]{1,0:T(8,128)(2,1)S(1)}) custom-call(s32[1]{0:T(128)} %bitcast.2.member_ref, bf16[32,8576]{1,0:T(8,128)(2,1)S(1)} %collective-permute-done.4.x_ref, f32[4,8,1024]{2,1,0:T(8,128)S(1)} %get-tuple-element.53.geo_ref, bf16[256,8192]{1,0:T(8,128)(2,1)S(1)} %get-tuple-element.54.table_ref), custom_call_target="tpu_custom_call" | custom-call | tf_op jit(solution)/shard_map/shifted_rows/pallas_call | solution.py:97
  30.8 1.7 %collective-permute-done.5.x_ref = bf16[32,8576]{1,0:T(8,128)(2,1)S(1)} collective-permute-done((bf16[32,8576]{1,0:T(8,128)(2,1)S(1)}, bf16[32,8576]{1,0:T(8,128)(2,1)S(1)}, u32[]{:S(2)}, u32[]{:S(2)}) %collective-permute-start.5) | collective-permute-done | bytes 548896 | tf_op jit(solution)/shard_map/ppermute | solution.py:49
  32.5 3.2 %shifted_rows.7 = (bf16[256,8192]{1,0:T(8,128)(2,1)S(1)}, bf16[32,4096]{1,0:T(8,128)(2,1)S(1)}) custom-call(s32[1]{0:T(128)} %bitcast.2.member_ref, bf16[32,8576]{1,0:T(8,128)(2,1)S(1)} %collective-permute-done.5.x_ref, f32[4,8,1024]{2,1,0:T(8,128)S(1)} %get-tuple-element.53.geo_ref, bf16[256,8192]{1,0:T(8,128)(2,1)S(1)} %get-tuple-element.54.table_ref), custom_call_target="tpu_custom_call" | custom-call | tf_op jit(solution)/shard_map/shifted_rows/pallas_call | solution.py:97
  38.6 2.7 %partial_scores.4 = (f32[256,128]{1,0:T(8,128)S(1)}, f32[256,128]{1,0:T(8,128)S(1)}) custom-call(bf16[256,8192]{1,0:T(8,128)(2,1)S(1)} %get-tuple-element.65.refs_0_.refs_4_, bf16[256,8192]{1,0:T(8,128)(2,1)S(1)} %get-tuple-element.59.refs_1_.refs_2_, bf16[32,4096]{1,0:T(8,128)(2,1)S(1)} %get-tuple-element.73.refs_2_, ...), custom_call_target="tpu_custom_call" | custom-call | tf_op jit(solution)/shard_map/partial_scores/pallas_call | solution.py:97
  42.6 1.5 %partial_scores.5.refs_0_ = f32[256,128]{1,0:T(8,128)S(1)} custom-call(bf16[256,8192]{1,0:T(8,128)(2,1)S(1)} %get-tuple-element.55.refs_0_.refs_1_, bf16[32,4096]{1,0:T(8,128)(2,1)S(1)} %get-tuple-element.76.refs_1_, bf16[16,8192]{1,0:T(8,128)(2,1)S(1)} %own_references.1.refs_2_.refs_4_, bf16[16,8192]{1,0:T(8,128)(2,1)S(1)} %collective-permute-done.3.refs_3_.refs_5_, ...), custom_call_target="tpu_custom_call" | custom-call | tf_op jit(solution)/shard_map/partial_scores/pallas_call | solution.py:97
  44.1 3.0 %collective-permute-done.11.refs_1_ = f32[256,128]{1,0:T(8,128)S(1)} collective-permute-done((f32[256,128]{1,0:T(8,128)S(1)}, f32[256,128]{1,0:T(8,128)S(1)}, u32[]{:S(2)}, u32[]{:S(2)}) %collective-permute-start.11) | collective-permute-done | bytes 131104 | tf_op jit(solution)/shard_map/ppermute | solution.py:49
  49.4 3.1 %collective-permute-done.14.refs_7_ = bf16[128,256]{1,0:T(8,128)(2,1)S(1)} collective-permute-done((bf16[128,256]{1,0:T(8,128)(2,1)S(1)}, bf16[128,256]{1,0:T(8,128)(2,1)S(1)}, u32[]{:S(2)}, u32[]{:S(2)}) %collective-permute-start.14) | collective-permute-done | bytes 65568 | tf_op jit(solution)/shard_map/ppermute | solution.py:49
  53.0 1.8 %weighted_sums.2 = (bf16[32,4096]{1,0:T(8,128)(2,1)S(1)}, bf16[32,4096]{1,0:T(8,128)(2,1)S(1)}, bf16[32,4096]{1,0:T(8,128)(2,1)S(1)}, bf16[32,4096]{1,0:T(8,128)(2,1)S(1)}) custom-call(s32[1]{0:T(128)} %bitcast.1.x_ref.refs_0_, bf16[256,8192]{1,0:T(8,128)(2,1)S(1)} %get-tuple-element.55.refs_0_.refs_1_, ...), custom_call_target="tpu_custom_call" | custom-call | tf_op jit(solution)/shard_map/weighted_sums/pallas_call | solution.py:97
  56.2 2.9 %collective-permute-start.17 = (bf16[32,4096]{1,0:T(8,128)(2,1)S(1)}, bf16[32,4096]{1,0:T(8,128)(2,1)S(1)}, u32[]{:S(2)}, u32[]{:S(2)}) collective-permute-start(bf16[32,4096]{1,0:T(8,128)(2,1)S(1)} %get-tuple-element.80), channel_id=1, source_target_pairs={{0,128},{1,129},{2,130},{3,131},{4,132},{5,133},{6,134},{7,135},{8... | collective-permute-start | bytes 786440 | tf_op jit(solution)/shard_map/ppermute | solution.py:49
  59.6 1.9 %weighted_sums.3 = (bf16[64,2048]{1,0:T(8,128)(2,1)S(1)}, bf16[64,2048]{1,0:T(8,128)(2,1)S(1)}, bf16[64,2048]{1,0:T(8,128)(2,1)S(1)}, bf16[64,2048]{1,0:T(8,128)(2,1)S(1)}) custom-call(s32[1]{0:T(128)} %bitcast.1.x_ref.refs_0_, bf16[256,8192]{1,0:T(8,128)(2,1)S(1)} %get-tuple-element.55.refs_0_.refs_1_, ...), custom_call_target="tpu_custom_call" | custom-call | tf_op jit(solution)/shard_map/weighted_sums/pallas_call | solution.py:97
  62.3 1.8 %collective-permute-start.24 = (bf16[64,2048]{1,0:T(8,128)(2,1)S(1)}, bf16[64,2048]{1,0:T(8,128)(2,1)S(1)}, u32[]{:S(2)}, u32[]{:S(2)}) collective-permute-start(bf16[64,2048]{1,0:T(8,128)(2,1)S(1)} %get-tuple-element.90), channel_id=1, source_target_pairs={{0,48},{1,49},{2,50},{3,51},{4,52},{5,53},{6,54},{7,55},{8,56},{9,... | collective-permute-start | bytes 786440 | tf_op jit(solution)/shard_map/ppermute | solution.py:49
  64.1 1.9 %collective-permute-start.23 = (bf16[64,2048]{1,0:T(8,128)(2,1)S(1)}, bf16[64,2048]{1,0:T(8,128)(2,1)S(1)}, u32[]{:S(2)}, u32[]{:S(2)}) collective-permute-start(bf16[64,2048]{1,0:T(8,128)(2,1)S(1)} %get-tuple-element.89), channel_id=1, source_target_pairs={{0,16},{1,17},{2,18},{3,19},{4,20},{5,21},{6,22},{7,23},{8,24},{9,... | collective-permute-start | bytes 786440 | tf_op jit(solution)/shard_map/ppermute | solution.py:49
  66.0 5.3 %collective-permute-done.17.refs_2_ = bf16[32,4096]{1,0:T(8,128)(2,1)S(1)} collective-permute-done((bf16[32,4096]{1,0:T(8,128)(2,1)S(1)}, bf16[32,4096]{1,0:T(8,128)(2,1)S(1)}, u32[]{:S(2)}, u32[]{:S(2)}) %collective-permute-start.17) | collective-permute-done | bytes 262176 | tf_op jit(solution)/shard_map/ppermute | solution.py:49
  71.3 2.6 %collective-permute-done.18.refs_3_ = bf16[32,4096]{1,0:T(8,128)(2,1)S(1)} collective-permute-done((bf16[32,4096]{1,0:T(8,128)(2,1)S(1)}, bf16[32,4096]{1,0:T(8,128)(2,1)S(1)}, u32[]{:S(2)}, u32[]{:S(2)}) %collective-permute-start.18) | collective-permute-done | bytes 262176 | tf_op jit(solution)/shard_map/ppermute | solution.py:49
  74.7 2.4 %collective-permute-start.20 = (bf16[16,2048]{1,0:T(8,128)(2,1)S(1)}, bf16[16,2048]{1,0:T(8,128)(2,1)S(1)}, u32[]{:S(2)}, u32[]{:S(2)}) collective-permute-start(bf16[16,2048]{1,0:T(8,128)(2,1)S(1)} %get-tuple-element.84), channel_id=1, source_target_pairs={{0,16},{1,17},{2,18},{3,19},{4,20},{5,21},{6,22},{7,23},{8,24},{9,... | collective-permute-start | bytes 196616 | tf_op jit(solution)/shard_map/ppermute | solution.py:49
  78.1 3.9 %collective-permute-start.26 = (bf16[16,2048]{1,0:T(8,128)(2,1)S(1)}, bf16[16,2048]{1,0:T(8,128)(2,1)S(1)}, u32[]{:S(2)}, u32[]{:S(2)}) collective-permute-start(bf16[16,2048]{1,0:T(8,128)(2,1)S(1)} %get-tuple-element.93), channel_id=1, source_target_pairs={{0,128},{1,129},{2,130},{3,131},{4,132},{5,133},{6,134},{7,135},{8... | collective-permute-start | bytes 196616 | tf_op jit(solution)/shard_map/ppermute | solution.py:49
  82.8 2.1 %collective-permute-done.26.refs_6_ = bf16[16,2048]{1,0:T(8,128)(2,1)S(1)} collective-permute-done((bf16[16,2048]{1,0:T(8,128)(2,1)S(1)}, bf16[16,2048]{1,0:T(8,128)(2,1)S(1)}, u32[]{:S(2)}, u32[]{:S(2)}) %collective-permute-start.26) | collective-permute-done | bytes 65568 | tf_op jit(solution)/shard_map/ppermute | solution.py:49
  84.9 2.5 %collective-permute-done.27.refs_7_ = bf16[16,2048]{1,0:T(8,128)(2,1)S(1)} collective-permute-done((bf16[16,2048]{1,0:T(8,128)(2,1)S(1)}, bf16[16,2048]{1,0:T(8,128)(2,1)S(1)}, u32[]{:S(2)}, u32[]{:S(2)}) %collective-permute-start.27) | collective-permute-done | bytes 65568 | tf_op jit(solution)/shard_map/ppermute | solution.py:49
  87.5 3.4 %collective-permute-start.28 = (bf16[16,1024]{1,0:T(8,128)(2,1)S(1)}, bf16[16,1024]{1,0:T(8,128)(2,1)S(1)}, u32[]{:S(2)}, u32[]{:S(2)}) collective-permute-start(bf16[16,1024]{1,0:T(8,128)(2,1)S(1)} %get-tuple-element.96), channel_id=1, source_target_pairs={{0,4},{1,5},{2,6},{3,7},{4,0},{5,1},{6,2},{7,3},{8,12},{9,13},{10,... | collective-permute-start | bytes 98312 | tf_op jit(solution)/shard_map/ppermute | solution.py:49
  90.9 4.3 %collective-permute-start.29 = (bf16[16,1024]{1,0:T(8,128)(2,1)S(1)}, bf16[16,1024]{1,0:T(8,128)(2,1)S(1)}, u32[]{:S(2)}, u32[]{:S(2)}) collective-permute-start(bf16[16,1024]{1,0:T(8,128)(2,1)S(1)} %get-tuple-element.97), channel_id=1, source_target_pairs={{0,8},{1,9},{2,10},{3,11},{4,12},{5,13},{6,14},{7,15},{8,0},{9,1},... | collective-permute-start | bytes 98312 | tf_op jit(solution)/shard_map/ppermute | solution.py:49
  95.2 3.5 %collective-permute-done.29 = bf16[16,1024]{1,0:T(8,128)(2,1)S(1)} collective-permute-done((bf16[16,1024]{1,0:T(8,128)(2,1)S(1)}, bf16[16,1024]{1,0:T(8,128)(2,1)S(1)}, u32[]{:S(2)}, u32[]{:S(2)}) %collective-permute-start.29) | collective-permute-done | bytes 32800 | tf_op jit(solution)/shard_map/ppermute | solution.py:49
  98.7 2.5 %collective-permute-done.30 = bf16[16,1024]{1,0:T(8,128)(2,1)S(1)} collective-permute-done((bf16[16,1024]{1,0:T(8,128)(2,1)S(1)}, bf16[16,1024]{1,0:T(8,128)(2,1)S(1)}, u32[]{:S(2)}, u32[]{:S(2)}) %collective-permute-start.30) | collective-permute-done | bytes 32800 | tf_op jit(solution)/shard_map/ppermute | solution.py:49
  (47 shorter events, 15.4 us)
Async XLA Ops:
  2.0 16.2 %collective-permute-start = (bf16[32,8576]{1,0:T(8,128)(2,1)S(1)}, bf16[32,8576]{1,0:T(8,128)(2,1)S(1)}, u32[]{:S(2)}, u32[]{:S(2)}) collective-permute-start(bf16[32,8576]{1,0:T(8,128)(2,1)S(1)} %get-tuple-element.56), channel_id=1, source_target_pairs={{0,1},{1,0},{2,3},{3,2},{4,5},{5,4},{6,7},{7,6},{8,9},{9,8},{10,11... | collective-permute-start | bytes 1646600 | tf_op jit(solution)/shard_map/ppermute | solution.py:49
  2.1 16.1 %collective-permute-start.4 = (bf16[32,8576]{1,0:T(8,128)(2,1)S(1)}, bf16[32,8576]{1,0:T(8,128)(2,1)S(1)}, u32[]{:S(2)}, u32[]{:S(2)}) collective-permute-start(bf16[32,8576]{1,0:T(8,128)(2,1)S(1)} %get-tuple-element.57.after), channel_id=1, source_target_pairs={{0,2},{1,3},{2,0},{3,1},{4,6},{5,7},{6,4},{7,5},{8,10},{9,11},{10,... | collective-permute-start | bytes 1646600 | tf_op jit(solution)/shard_map/ppermute | solution.py:49
  5.0 13.1 %collective-permute-start.1 = (bf16[16,8192]{1,0:T(8,128)(2,1)S(1)}, bf16[16,8192]{1,0:T(8,128)(2,1)S(1)}, u32[]{:S(2)}, u32[]{:S(2)}) collective-permute-start(bf16[16,8192]{1,0:T(8,128)(2,1)S(1)} %own_references.1.refs_2_.refs_4_), channel_id=1, source_target_pairs={{0,64},{1,65},{2,66},{3,67},{4,68},{5,69},{6,70},{7,71},{8,72},{9,... | collective-permute-start | bytes 786440 | tf_op jit(solution)/shard_map/ppermute | solution.py:49
  6.7 11.4 %collective-permute-start.2 = (bf16[16,8192]{1,0:T(8,128)(2,1)S(1)}, bf16[16,8192]{1,0:T(8,128)(2,1)S(1)}, u32[]{:S(2)}, u32[]{:S(2)}) collective-permute-start(bf16[16,8192]{1,0:T(8,128)(2,1)S(1)} %own_references.1.refs_2_.refs_4_), channel_id=1, source_target_pairs={{0,192},{1,193},{2,194},{3,195},{4,196},{5,197},{6,198},{7,199},{8... | collective-permute-start | bytes 786440 | tf_op jit(solution)/shard_map/ppermute | solution.py:49
  8.9 9.3 %collective-permute-start.3 = (bf16[16,8192]{1,0:T(8,128)(2,1)S(1)}, bf16[16,8192]{1,0:T(8,128)(2,1)S(1)}, u32[]{:S(2)}, u32[]{:S(2)}) collective-permute-start(bf16[16,8192]{1,0:T(8,128)(2,1)S(1)} %own_references.1.refs_2_.refs_4_), channel_id=1, source_target_pairs={{0,32},{1,33},{2,34},{3,35},{4,36},{5,37},{6,38},{7,39},{8,40},{9,... | collective-permute-start | bytes 786440 | tf_op jit(solution)/shard_map/ppermute | solution.py:49
  18.2 14.3 %collective-permute-start.5 = (bf16[32,8576]{1,0:T(8,128)(2,1)S(1)}, bf16[32,8576]{1,0:T(8,128)(2,1)S(1)}, u32[]{:S(2)}, u32[]{:S(2)}) collective-permute-start(bf16[32,8576]{1,0:T(8,128)(2,1)S(1)} %get-tuple-element.63), channel_id=1, source_target_pairs={{0,3},{1,2},{2,1},{3,0},{4,7},{5,6},{6,5},{7,4},{8,11},{9,10},{10,... | collective-permute-start | bytes 1646600 | tf_op jit(solution)/shard_map/ppermute | solution.py:49
  18.3 17.4 %collective-permute-start.6 = (bf16[16,8192]{1,0:T(8,128)(2,1)S(1)}, bf16[16,8192]{1,0:T(8,128)(2,1)S(1)}, u32[]{:S(2)}, u32[]{:S(2)}) collective-permute-start(bf16[16,8192]{1,0:T(8,128)(2,1)S(1)} %collective-permute-done.1.refs_4_.refs_6_), channel_id=1, source_target_pairs={{0,32},{1,33},{2,34},{3,35},{4,36},{5,37},{6,38},{7,39},{8,40},{9,... | collective-permute-start | bytes 786440 | tf_op jit(solution)/shard_map/ppermute | solution.py:49
  19.8 15.8 %collective-permute-start.7 = (bf16[16,8192]{1,0:T(8,128)(2,1)S(1)}, bf16[16,8192]{1,0:T(8,128)(2,1)S(1)}, u32[]{:S(2)}, u32[]{:S(2)}) collective-permute-start(bf16[16,8192]{1,0:T(8,128)(2,1)S(1)} %collective-permute-done.1.refs_4_.refs_6_), channel_id=1, source_target_pairs={{0,192},{1,193},{2,194},{3,195},{4,196},{5,197},{6,198},{7,199},{8... | collective-permute-start | bytes 786440 | tf_op jit(solution)/shard_map/ppermute | solution.py:49
  21.7 14.0 %collective-permute-start.8 = (bf16[16,8192]{1,0:T(8,128)(2,1)S(1)}, bf16[16,8192]{1,0:T(8,128)(2,1)S(1)}, u32[]{:S(2)}, u32[]{:S(2)}) collective-permute-start(bf16[16,8192]{1,0:T(8,128)(2,1)S(1)} %collective-permute-done.3.refs_3_.refs_5_), channel_id=1, source_target_pairs={{0,128},{1,129},{2,130},{3,131},{4,132},{5,133},{6,134},{7,135},{8... | collective-permute-start | bytes 786440 | tf_op jit(solution)/shard_map/ppermute | solution.py:49
  22.6 13.1 %collective-permute-start.9 = (bf16[16,8192]{1,0:T(8,128)(2,1)S(1)}, bf16[16,8192]{1,0:T(8,128)(2,1)S(1)}, u32[]{:S(2)}, u32[]{:S(2)}) collective-permute-start(bf16[16,8192]{1,0:T(8,128)(2,1)S(1)} %collective-permute-done.2.refs_8_.refs_10_), channel_id=1, source_target_pairs={{0,48},{1,49},{2,50},{3,51},{4,52},{5,53},{6,54},{7,55},{8,56},{9,... | collective-permute-start | bytes 786440 | tf_op jit(solution)/shard_map/ppermute | solution.py:49
  37.3 5.3 %collective-permute-start.10 = (f32[256,128]{1,0:T(8,128)S(1)}, f32[256,128]{1,0:T(8,128)S(1)}, u32[]{:S(2)}, u32[]{:S(2)}) collective-permute-start(f32[256,128]{1,0:T(8,128)S(1)} %partial_scores.3), channel_id=1, source_target_pairs={{0,2},{1,3},{2,0},{3,1},{4,6},{5,7},{6,4},{7,5},{8,10},{9,11},{10,... | collective-permute-start | bytes 393224 | tf_op jit(solution)/shard_map/ppermute | solution.py:49
  41.3 5.9 %collective-permute-start.11 = (f32[256,128]{1,0:T(8,128)S(1)}, f32[256,128]{1,0:T(8,128)S(1)}, u32[]{:S(2)}, u32[]{:S(2)}) collective-permute-start(f32[256,128]{1,0:T(8,128)S(1)} %get-tuple-element.75), channel_id=1, source_target_pairs={{0,3},{1,2},{2,1},{3,0},{4,7},{5,6},{6,5},{7,4},{8,11},{9,10},{10,... | collective-permute-start | bytes 393224 | tf_op jit(solution)/shard_map/ppermute | solution.py:49
  41.4 5.8 %collective-permute-start.12 = (f32[256,128]{1,0:T(8,128)S(1)}, f32[256,128]{1,0:T(8,128)S(1)}, u32[]{:S(2)}, u32[]{:S(2)}) collective-permute-start(f32[256,128]{1,0:T(8,128)S(1)} %get-tuple-element.77), channel_id=1, source_target_pairs={{0,1},{1,0},{2,3},{3,2},{4,5},{5,4},{6,7},{7,6},{8,9},{9,8},{10,11... | collective-permute-start | bytes 393224 | tf_op jit(solution)/shard_map/ppermute | solution.py:49
  47.5 2.0 %collective-permute-start.13 = (bf16[128,256]{1,0:T(8,128)(2,1)S(1)}, bf16[128,256]{1,0:T(8,128)(2,1)S(1)}, u32[]{:S(2)}, u32[]{:S(2)}) collective-permute-start(bf16[128,256]{1,0:T(8,128)(2,1)S(1)} %posterior.1.refs_5_), channel_id=1, source_target_pairs={{0,1},{1,0},{2,3},{3,2},{4,5},{5,4},{6,7},{7,6},{8,9},{9,8},{10,11... | collective-permute-start | bytes 196616 | tf_op jit(solution)/shard_map/ppermute | solution.py:49
  47.7 4.9 %collective-permute-start.14 = (bf16[128,256]{1,0:T(8,128)(2,1)S(1)}, bf16[128,256]{1,0:T(8,128)(2,1)S(1)}, u32[]{:S(2)}, u32[]{:S(2)}) collective-permute-start(bf16[128,256]{1,0:T(8,128)(2,1)S(1)} %posterior.1.refs_5_), channel_id=1, source_target_pairs={{0,2},{1,3},{2,0},{3,1},{4,6},{5,7},{6,4},{7,5},{8,10},{9,11},{10,... | collective-permute-start | bytes 196616 | tf_op jit(solution)/shard_map/ppermute | solution.py:49
  48.3 4.8 %collective-permute-start.15 = (bf16[128,256]{1,0:T(8,128)(2,1)S(1)}, bf16[128,256]{1,0:T(8,128)(2,1)S(1)}, u32[]{:S(2)}, u32[]{:S(2)}) collective-permute-start(bf16[128,256]{1,0:T(8,128)(2,1)S(1)} %posterior.1.refs_5_), channel_id=1, source_target_pairs={{0,3},{1,2},{2,1},{3,0},{4,7},{5,6},{6,5},{7,4},{8,11},{9,10},{10,... | collective-permute-start | bytes 196616 | tf_op jit(solution)/shard_map/ppermute | solution.py:49
  54.9 9.3 %collective-permute-start.16 = (bf16[32,4096]{1,0:T(8,128)(2,1)S(1)}, bf16[32,4096]{1,0:T(8,128)(2,1)S(1)}, u32[]{:S(2)}, u32[]{:S(2)}) collective-permute-start(bf16[32,4096]{1,0:T(8,128)(2,1)S(1)} %get-tuple-element.79), channel_id=1, source_target_pairs={{0,64},{1,65},{2,66},{3,67},{4,68},{5,69},{6,70},{7,71},{8,72},{9,... | collective-permute-start | bytes 786440 | tf_op jit(solution)/shard_map/ppermute | solution.py:49
  56.2 15.1 %collective-permute-start.17 = (bf16[32,4096]{1,0:T(8,128)(2,1)S(1)}, bf16[32,4096]{1,0:T(8,128)(2,1)S(1)}, u32[]{:S(2)}, u32[]{:S(2)}) collective-permute-start(bf16[32,4096]{1,0:T(8,128)(2,1)S(1)} %get-tuple-element.80), channel_id=1, source_target_pairs={{0,128},{1,129},{2,130},{3,131},{4,132},{5,133},{6,134},{7,135},{8... | collective-permute-start | bytes 786440 | tf_op jit(solution)/shard_map/ppermute | solution.py:49
  59.1 14.8 %collective-permute-start.18 = (bf16[32,4096]{1,0:T(8,128)(2,1)S(1)}, bf16[32,4096]{1,0:T(8,128)(2,1)S(1)}, u32[]{:S(2)}, u32[]{:S(2)}) collective-permute-start(bf16[32,4096]{1,0:T(8,128)(2,1)S(1)} %get-tuple-element.81), channel_id=1, source_target_pairs={{0,192},{1,193},{2,194},{3,195},{4,196},{5,197},{6,198},{7,199},{8... | collective-permute-start | bytes 786440 | tf_op jit(solution)/shard_map/ppermute | solution.py:49
  61.6 15.5 %collective-permute-start.22 = (bf16[64,2048]{1,0:T(8,128)(2,1)S(1)}, bf16[64,2048]{1,0:T(8,128)(2,1)S(1)}, u32[]{:S(2)}, u32[]{:S(2)}) collective-permute-start(bf16[64,2048]{1,0:T(8,128)(2,1)S(1)} %get-tuple-element.87), channel_id=1, source_target_pairs={{0,32},{1,33},{2,34},{3,35},{4,36},{5,37},{6,38},{7,39},{8,40},{9,... | collective-permute-start | bytes 786440 | tf_op jit(solution)/shard_map/ppermute | solution.py:49
  62.3 15.3 %collective-permute-start.24 = (bf16[64,2048]{1,0:T(8,128)(2,1)S(1)}, bf16[64,2048]{1,0:T(8,128)(2,1)S(1)}, u32[]{:S(2)}, u32[]{:S(2)}) collective-permute-start(bf16[64,2048]{1,0:T(8,128)(2,1)S(1)} %get-tuple-element.90), channel_id=1, source_target_pairs={{0,48},{1,49},{2,50},{3,51},{4,52},{5,53},{6,54},{7,55},{8,56},{9,... | collective-permute-start | bytes 786440 | tf_op jit(solution)/shard_map/ppermute | solution.py:49
  64.1 13.5 %collective-permute-start.23 = (bf16[64,2048]{1,0:T(8,128)(2,1)S(1)}, bf16[64,2048]{1,0:T(8,128)(2,1)S(1)}, u32[]{:S(2)}, u32[]{:S(2)}) collective-permute-start(bf16[64,2048]{1,0:T(8,128)(2,1)S(1)} %get-tuple-element.89), channel_id=1, source_target_pairs={{0,16},{1,17},{2,18},{3,19},{4,20},{5,21},{6,22},{7,23},{8,24},{9,... | collective-permute-start | bytes 786440 | tf_op jit(solution)/shard_map/ppermute | solution.py:49
  74.0 7.9 %collective-permute-start.19 = (bf16[16,2048]{1,0:T(8,128)(2,1)S(1)}, bf16[16,2048]{1,0:T(8,128)(2,1)S(1)}, u32[]{:S(2)}, u32[]{:S(2)}) collective-permute-start(bf16[16,2048]{1,0:T(8,128)(2,1)S(1)} %get-tuple-element.83), channel_id=1, source_target_pairs={{0,32},{1,33},{2,34},{3,35},{4,36},{5,37},{6,38},{7,39},{8,40},{9,... | collective-permute-start | bytes 196616 | tf_op jit(solution)/shard_map/ppermute | solution.py:49
  74.7 8.1 %collective-permute-start.20 = (bf16[16,2048]{1,0:T(8,128)(2,1)S(1)}, bf16[16,2048]{1,0:T(8,128)(2,1)S(1)}, u32[]{:S(2)}, u32[]{:S(2)}) collective-permute-start(bf16[16,2048]{1,0:T(8,128)(2,1)S(1)} %get-tuple-element.84), channel_id=1, source_target_pairs={{0,16},{1,17},{2,18},{3,19},{4,20},{5,21},{6,22},{7,23},{8,24},{9,... | collective-permute-start | bytes 196616 | tf_op jit(solution)/shard_map/ppermute | solution.py:49
  77.1 5.7 %collective-permute-start.21 = (bf16[16,2048]{1,0:T(8,128)(2,1)S(1)}, bf16[16,2048]{1,0:T(8,128)(2,1)S(1)}, u32[]{:S(2)}, u32[]{:S(2)}) collective-permute-start(bf16[16,2048]{1,0:T(8,128)(2,1)S(1)} %get-tuple-element.85), channel_id=1, source_target_pairs={{0,48},{1,49},{2,50},{3,51},{4,52},{5,53},{6,54},{7,55},{8,56},{9,... | collective-permute-start | bytes 196616 | tf_op jit(solution)/shard_map/ppermute | solution.py:49
  77.8 5.0 %collective-permute-start.25 = (bf16[16,2048]{1,0:T(8,128)(2,1)S(1)}, bf16[16,2048]{1,0:T(8,128)(2,1)S(1)}, u32[]{:S(2)}, u32[]{:S(2)}) collective-permute-start(bf16[16,2048]{1,0:T(8,128)(2,1)S(1)} %get-tuple-element.92), channel_id=1, source_target_pairs={{0,64},{1,65},{2,66},{3,67},{4,68},{5,69},{6,70},{7,71},{8,72},{9,... | collective-permute-start | bytes 196616 | tf_op jit(solution)/shard_map/ppermute | solution.py:49
  78.1 6.8 %collective-permute-start.26 = (bf16[16,2048]{1,0:T(8,128)(2,1)S(1)}, bf16[16,2048]{1,0:T(8,128)(2,1)S(1)}, u32[]{:S(2)}, u32[]{:S(2)}) collective-permute-start(bf16[16,2048]{1,0:T(8,128)(2,1)S(1)} %get-tuple-element.93), channel_id=1, source_target_pairs={{0,128},{1,129},{2,130},{3,131},{4,132},{5,133},{6,134},{7,135},{8... | collective-permute-start | bytes 196616 | tf_op jit(solution)/shard_map/ppermute | solution.py:49
  82.0 5.5 %collective-permute-start.27 = (bf16[16,2048]{1,0:T(8,128)(2,1)S(1)}, bf16[16,2048]{1,0:T(8,128)(2,1)S(1)}, u32[]{:S(2)}, u32[]{:S(2)}) collective-permute-start(bf16[16,2048]{1,0:T(8,128)(2,1)S(1)} %get-tuple-element.94), channel_id=1, source_target_pairs={{0,192},{1,193},{2,194},{3,195},{4,196},{5,197},{6,198},{7,199},{8... | collective-permute-start | bytes 196616 | tf_op jit(solution)/shard_map/ppermute | solution.py:49
  87.5 7.7 %collective-permute-start.28 = (bf16[16,1024]{1,0:T(8,128)(2,1)S(1)}, bf16[16,1024]{1,0:T(8,128)(2,1)S(1)}, u32[]{:S(2)}, u32[]{:S(2)}) collective-permute-start(bf16[16,1024]{1,0:T(8,128)(2,1)S(1)} %get-tuple-element.96), channel_id=1, source_target_pairs={{0,4},{1,5},{2,6},{3,7},{4,0},{5,1},{6,2},{7,3},{8,12},{9,13},{10,... | collective-permute-start | bytes 98312 | tf_op jit(solution)/shard_map/ppermute | solution.py:49
  90.9 7.8 %collective-permute-start.29 = (bf16[16,1024]{1,0:T(8,128)(2,1)S(1)}, bf16[16,1024]{1,0:T(8,128)(2,1)S(1)}, u32[]{:S(2)}, u32[]{:S(2)}) collective-permute-start(bf16[16,1024]{1,0:T(8,128)(2,1)S(1)} %get-tuple-element.97), channel_id=1, source_target_pairs={{0,8},{1,9},{2,10},{3,11},{4,12},{5,13},{6,14},{7,15},{8,0},{9,1},... | collective-permute-start | bytes 98312 | tf_op jit(solution)/shard_map/ppermute | solution.py:49
  95.2 6.0 %collective-permute-start.30 = (bf16[16,1024]{1,0:T(8,128)(2,1)S(1)}, bf16[16,1024]{1,0:T(8,128)(2,1)S(1)}, u32[]{:S(2)}, u32[]{:S(2)}) collective-permute-start(bf16[16,1024]{1,0:T(8,128)(2,1)S(1)} %get-tuple-element.98), channel_id=1, source_target_pairs={{0,12},{1,13},{2,14},{3,15},{4,8},{5,9},{6,10},{7,11},{8,4},{9,5},... | collective-permute-start | bytes 98312 | tf_op jit(solution)/shard_map/ppermute | solution.py:49

commit v10 on v9

--- a/solution.py
+++ b/solution.py
@@ -34,6 +34,13 @@
 def flips(y=0, x=0, z=0):
     return [
         (linear(i, j, k, c), linear(i ^ y, j ^ x, k ^ z, c))
+        for i in range(Y) for j in range(X) for k in range(Z) for c in range(2)
+    ]
+
+
+def crossed(n, core):
+    return [
+        (linear(i, j, k, c), linear(i ^ (n if c == core else 0), j ^ (0 if c == core else n), k, c))
         for i in range(Y) for j in range(X) for k in range(Z) for c in range(2)
     ]
 
@@ -287,10 +294,9 @@
     )
 
 
-def scores_kernel(count, more, *refs):
+def scores_kernel(count, *refs):
     blocks = refs[2 * count : 2 * count + 8]
-    added_in = refs[2 * count + 8 : 2 * count + 8 + more]
-    outs = refs[2 * count + 8 + more :]
+    outs = refs[2 * count + 8 :]
     stacked = jnp.concatenate([block[...] for block in blocks], axis=0)
     power = []
     for block in range(NB):
@@ -305,18 +311,19 @@
     total = lax.dot_general(rows, stacked, NT, preferred_element_type=F32)
     for n, out in enumerate(outs):
         mine = total[n * ROWS : (n + 1) * ROWS].reshape(SHIFTS, P_DEV, 128)
-        mine = (mine - energy[None, n * P_DEV : (n + 1) * P_DEV]).reshape(ROWS, 128)
-        for value in added_in:
-            mine = mine + value[...]
-        out[...] = mine
-
-
-def make_scores(rows, pens, blocks, plus=()):
-    count, more = len(rows), len(plus)
-    return local(
-        lambda *refs: scores_kernel(count, more, *refs), "partial_scores", [((ROWS, 128), F32)] * count,
-        [], [*rows, *pens, *blocks, *plus], 12,
-    )
+        out[...] = (mine - energy[None, n * P_DEV : (n + 1) * P_DEV]).reshape(ROWS, 128)
+
+
+def make_scores(rows, pens, blocks):
+    count = len(rows)
+    return local(
+        lambda *refs: scores_kernel(count, *refs), "partial_scores", [((ROWS, 128), F32)] * count,
+        [], [*rows, *pens, *blocks], 12,
+    )
+
+
+def sum_kernel(*refs):
+    refs[-1][...] = refs[0][...] + refs[1][...] + refs[2][...]
 
 
 def posterior_kernel(*refs):
@@ -337,8 +344,10 @@
     return out
 
 
-def accum_kernel(part, x_ref, *refs):
+def accum_kernel(part, member_ref, x_ref, *refs):
     rows, posts, outs = refs[:G], refs[G : 2 * G], refs[2 * G :]
+    along_y = (member_ref[0] & 1) == part
+    high = x_ref[0] >> 1
 
     @pl.loop(0, NB)
     def _(block):
@@ -351,27 +360,21 @@
                     posts[n][...], rows[n][:, pl.ds(start, HALF)], preferred_element_type=F32
                 )
             sums.append(total)
-        if part == 0:
-            for n in range(Y):
-                for half, total in enumerate(sums):
-                    spot = pl.multiple_of(block * COLS + half * HALF, HALF)
-                    outs[n][:, pl.ds(spot, HALF)] = total[n * 32 : (n + 1) * 32].astype(BF16)
-        else:
-            for n in range(X):
-                low = n & 1
-                upper = (x_ref[0] >> 1) ^ (n >> 1) == 1
-                spot = pl.multiple_of(block * HALF, HALF)
-                for k in range(Y):
-                    mine = slice(k * 32 + low * 16, k * 32 + low * 16 + 16)
-                    chosen = jnp.where(upper, sums[1][mine], sums[0][mine])
-                    outs[n][k * 16 : (k + 1) * 16, pl.ds(spot, HALF)] = chosen.astype(BF16)
-
-
-def make_accum(part, place, rows, posts):
-    shape = (32, NB * COLS) if part == 0 else (64, NB * HALF)
-    return local(
-        lambda *refs: accum_kernel(part, *refs), "weighted_sums", [(shape, BF16)] * 4, [place],
-        [*rows, *posts], 8,
+        spot = pl.ds(pl.multiple_of(block * HALF, HALF), HALF)
+        for n, out in enumerate(outs):
+            upper = high ^ (n >> 1) == 1
+            for group in range(4):
+                at = n * 32 + (group >> 1) * 16
+                for_y = sums[group & 1][at : at + 16]
+                at = group * 32 + (n & 1) * 16
+                for_x = jnp.where(upper, sums[1][at : at + 16], sums[0][at : at + 16])
+                out[group * 16 : (group + 1) * 16, spot] = jnp.where(along_y, for_y, for_x).astype(BF16)
+
+
+def make_accum(part, member, x_at, rows, posts):
+    return local(
+        lambda *refs: accum_kernel(part, *refs), "weighted_sums", [((64, NB * HALF), BF16)] * 4,
+        [member, x_at], [*rows, *posts], 8,
     )
 
 
@@ -385,21 +388,18 @@
 PIECES = [((16, NB * HALF), F32)] + [((16, NB * HALF), BF16)] * 3
 
 
-def first_kernel(x_ref, *refs):
-    outs = refs[4:]
-    for block in range(NB):
-        start = block * COLS
-        real = added([ref[:, start : start + HALF] for ref in refs[:4]])
-        imag = added([ref[:, start + HALF : start + COLS] for ref in refs[:4]])
-        for n, out in enumerate(outs):
-            mine = slice((n & 1) * 16, (n & 1) * 16 + 16)
-            chosen = jnp.where((x_ref[0] >> 1) ^ (n >> 1) == 1, imag[mine], real[mine])
-            out[:, block * HALF : (block + 1) * HALF] = chosen.astype(out.dtype)
-
-
-def second_kernel(*refs):
+def turn_kernel(part, member_ref, x_ref, *refs):
+    along_y = (member_ref[0] & 1) == part
     for n, out in enumerate(refs[4:]):
-        out[...] = added([ref[n * 16 : (n + 1) * 16] for ref in refs[:4]]).astype(out.dtype)
+        group = jnp.where(along_y, (n & 1) * 2 + ((x_ref[0] >> 1) ^ (n >> 1)), n)
+        mine = pl.ds(pl.multiple_of(group * 16, 16), 16)
+        out[...] = added([ref[mine, :] for ref in refs[:4]]).astype(out.dtype)
+
+
+def make_turn(part, member, x_at, values):
+    return local(
+        lambda *refs: turn_kernel(part, *refs), "turned_sums", PIECES, [member, x_at], values, 4
+    )
 
 
 def joined_kernel(block_ref, *refs):
@@ -443,26 +443,27 @@
     blocks = [gathered[ky, kx] for ky in range(Y) for kx in range(2)]
 
     (second,) = make_scores([rows[2]], [after(pens[2], rows[3])], blocks)
-    third, other = make_scores([rows[3], rows[1]], [after(pens[3], second), pens[1]], blocks)
-    (mine,) = make_scores([rows[0]], [after(pens[0], third)], blocks, [send(second, partners(2))])
-    arrived = [send(value, partners(n)) for value, n in ((third, 3), (other, 1))]
-    posterior = make_posterior([mine, *arrived])
+    (third,) = make_scores([rows[3]], [after(pens[3], second)], blocks)
+    mine, other = make_scores([rows[0], rows[1]], [after(pens[0], third), pens[1]], blocks)
+    near = [mine, send(second, partners(2)), send(third, partners(3))]
+    (near,) = local(sum_kernel, "score_sums", [((ROWS, 128), F32)], [], near, 4)
+    posterior = make_posterior([near, send(other, partners(1))])
     posts = [posterior] + [send(posterior, partners(n)) for n in range(1, G)]
     rows = [rows[n] for n in range(G)]
 
-    first = make_accum(0, x_at, rows, posts)
-    first = [first[0]] + [send(first[n], flips(y=n)) for n in range(1, Y)]
-    second = make_accum(1, x_at, rows, posts)
+    first = make_accum(0, member, x_at, rows, posts)
+    first = [first[0]] + [send(first[n], crossed(n, 0)) for n in range(1, 4)]
+    second = make_accum(1, member, x_at, rows, posts)
     second = [
         second[0],
-        send(second[1], flips(x=1)),
-        send(after(second[2], first[1]), flips(x=2)),
-        send(second[3], flips(x=3)),
-    ]
-    first = local(first_kernel, "first_sums", PIECES, [x_at], first, 4)
-    first = [first[0]] + [send(first[n], flips(x=n)) for n in range(1, X)]
-    second = local(second_kernel, "second_sums", PIECES, [], second, 4)
-    second = [second[0]] + [send(second[n], flips(y=n)) for n in range(1, Y)]
+        send(second[1], crossed(1, 1)),
+        send(after(second[2], first[1]), crossed(2, 1)),
+        send(second[3], crossed(3, 1)),
+    ]
+    first = make_turn(0, member, x_at, first)
+    first = [first[0]] + [send(first[n], crossed(n, 1)) for n in range(1, 4)]
+    second = make_turn(1, member, x_at, second)
+    second = [second[0]] + [send(second[n], crossed(n, 0)) for n in range(1, 4)]
     outs = [((16, COLS), F32)] + [((16, COLS), BF16)] * (NB - 1)
     ends = local(joined_kernel, "joined_sums", outs, [block], [*first, *second], 4)
     return added([ends[0]] + [send(ends[n], flips(z=n * (G // 2))) for n in range(1, NB)])

time: 103 us -> 101 us (0.981)
  waiting for transfers between devices: 27 us -> 25.1 us
    ppermute x31, waiting for transfers between devices: 27 us -> 25.1 us  [send(): return lax.ppermute(value, AXES, pairs)]
    pallas_call x16 -> x17, Pallas kernels: 31.3 us -> 31.4 us  [local(): pl.pallas_call(kernel, in_specs=[SCALARS] * len(scalars) + [PLACED] * pla...]
  transfers between devices with their start and end apart: 31 -> 31, of which waited for: 11 -> 10; matrix products, arithmetic and copies ran while one was open for 0% -> 0% of each run, Pallas kernels for 25% -> 26%
where the time goes in v10:
time: 101 us; the launch traced here: 100 us
  starting transfers between devices  42.7 us (42%)
  Pallas kernels  31.4 us (31%)
  waiting for transfers between devices  25.1 us (25%)
    ppermute x31, starting transfers between devices, send(): return lax.ppermute(value, AXES, pairs)  42.7 us
    pallas_call x17, Pallas kernels, local(): pl.pallas_call(kernel, in_specs=[SCALARS] * len(scalars) + [PLACED] * pla...  31.4 us
    ppermute x31, waiting for transfers between devices, send(): return lax.ppermute(value, AXES, pairs)  25.1 us
  transfers between devices with their start and end apart: 31, of which 10 were waited for; matrix products, arithmetic and copies ran while one was open for 0% of the time, Pallas kernels for 26%

profile of v10, /device:TPU:2, one launch (start us, length us, event | category | flops | bytes accessed | tf_op | source)
XLA Modules:
  0.0 100.0 jit_solution(12107180562508607716)
XLA Ops:
  0.0 2.0 %split_particles.1 = (bf16[32,8576]{1,0:T(8,128)(2,1)S(1)}, bf16[32,8576]{1,0:T(8,128)(2,1)S(1)}, bf16[32,8576]{1,0:T(8,128)(2,1)S(1)}, bf16[32,8576]{1,0:T(8,128)(2,1)S(1)}) custom-call(s32[1]{0:T(128)} %bitcast.1.member_ref.refs_0_, s32[1]{0:T(128)} %bitcast.block_ref, s32[1]{0:T(128)} %bitcast.2.x_ref.refs_1_, bf16[32,32768]{1,0:T(8,128)(2,1)} %source.2, ...), custom_call_target="tpu_custom_call" | custom-call | tf_op jit(solution)/shard_map/split_particles/pallas_call | solution.py:104
  2.1 2.0 %collective-permute-start.4 = (bf16[32,8576]{1,0:T(8,128)(2,1)S(1)}, bf16[32,8576]{1,0:T(8,128)(2,1)S(1)}, u32[]{:S(2)}, u32[]{:S(2)}) collective-permute-start(bf16[32,8576]{1,0:T(8,128)(2,1)S(1)} %get-tuple-element.57.after), channel_id=1, source_target_pairs={{0,2},{1,3},{2,0},{3,1},{4,6},{5,7},{6,4},{7,5},{8,10},{9,11},{10,... | collective-permute-start | bytes 1646600 | tf_op jit(solution)/shard_map/ppermute | solution.py:56
  5.0 1.7 %collective-permute-start.1 = (bf16[16,8192]{1,0:T(8,128)(2,1)S(1)}, bf16[16,8192]{1,0:T(8,128)(2,1)S(1)}, u32[]{:S(2)}, u32[]{:S(2)}) collective-permute-start(bf16[16,8192]{1,0:T(8,128)(2,1)S(1)} %own_references.1.refs_2_.refs_4_), channel_id=1, source_target_pairs={{0,64},{1,65},{2,66},{3,67},{4,68},{5,69},{6,70},{7,71},{8,72},{9,... | collective-permute-start | bytes 786440 | tf_op jit(solution)/shard_map/ppermute | solution.py:56
  6.7 2.2 %collective-permute-start.2 = (bf16[16,8192]{1,0:T(8,128)(2,1)S(1)}, bf16[16,8192]{1,0:T(8,128)(2,1)S(1)}, u32[]{:S(2)}, u32[]{:S(2)}) collective-permute-start(bf16[16,8192]{1,0:T(8,128)(2,1)S(1)} %own_references.1.refs_2_.refs_4_), channel_id=1, source_target_pairs={{0,192},{1,193},{2,194},{3,195},{4,196},{5,197},{6,198},{7,199},{8... | collective-permute-start | bytes 786440 | tf_op jit(solution)/shard_map/ppermute | solution.py:56
  9.4 5.5 %phase_table.1 = (bf16[256,8192]{1,0:T(8,128)(2,1)S(1)}, f32[4,8,1024]{2,1,0:T(8,128)S(1)}) custom-call(s32[1]{0:T(128)} %bitcast.1.member_ref.refs_0_, f32[16,8,1024]{2,1,0:T(8,128)} %constant.63.clone.geo_ref), custom_call_target="tpu_custom_call" | custom-call | tf_op jit(solution)/shard_map/phase_table/pallas_call | solution.py:104
  14.9 3.2 %shifted_rows.4 = (bf16[256,8192]{1,0:T(8,128)(2,1)S(1)}, bf16[32,4096]{1,0:T(8,128)(2,1)S(1)}) custom-call(s32[1]{0:T(128)} %bitcast.1.member_ref.refs_0_, bf16[32,8576]{1,0:T(8,128)(2,1)S(1)} %get-tuple-element.52.x_ref, f32[4,8,1024]{2,1,0:T(8,128)S(1)} %get-tuple-element.53.geo_ref, bf16[256,8192]{1,0:T(8,128)(2,1)S(1)} %get-tuple-element.54.table_ref), custom_call_target="tpu_custom_call" | custom-call | tf_op jit(solution)/shard_map/shifted_rows/pallas_call | solution.py:104
  18.3 1.6 %collective-permute-start.6 = (bf16[16,8192]{1,0:T(8,128)(2,1)S(1)}, bf16[16,8192]{1,0:T(8,128)(2,1)S(1)}, u32[]{:S(2)}, u32[]{:S(2)}) collective-permute-start(bf16[16,8192]{1,0:T(8,128)(2,1)S(1)} %collective-permute-done.1.refs_4_.refs_6_), channel_id=1, source_target_pairs={{0,32},{1,33},{2,34},{3,35},{4,36},{5,37},{6,38},{7,39},{8,40},{9,... | collective-permute-start | bytes 786440 | tf_op jit(solution)/shard_map/ppermute | solution.py:56
  19.8 1.8 %collective-permute-start.7 = (bf16[16,8192]{1,0:T(8,128)(2,1)S(1)}, bf16[16,8192]{1,0:T(8,128)(2,1)S(1)}, u32[]{:S(2)}, u32[]{:S(2)}) collective-permute-start(bf16[16,8192]{1,0:T(8,128)(2,1)S(1)} %collective-permute-done.1.refs_4_.refs_6_), channel_id=1, source_target_pairs={{0,192},{1,193},{2,194},{3,195},{4,196},{5,197},{6,198},{7,199},{8... | collective-permute-start | bytes 786440 | tf_op jit(solution)/shard_map/ppermute | solution.py:56
  22.6 1.9 %collective-permute-start.9 = (bf16[16,8192]{1,0:T(8,128)(2,1)S(1)}, bf16[16,8192]{1,0:T(8,128)(2,1)S(1)}, u32[]{:S(2)}, u32[]{:S(2)}) collective-permute-start(bf16[16,8192]{1,0:T(8,128)(2,1)S(1)} %collective-permute-done.2.refs_8_.refs_10_), channel_id=1, source_target_pairs={{0,48},{1,49},{2,50},{3,51},{4,52},{5,53},{6,54},{7,55},{8,56},{9,... | collective-permute-start | bytes 786440 | tf_op jit(solution)/shard_map/ppermute | solution.py:56
  24.4 3.2 %shifted_rows.5 = (bf16[256,8192]{1,0:T(8,128)(2,1)S(1)}, bf16[32,4096]{1,0:T(8,128)(2,1)S(1)}) custom-call(s32[1]{0:T(128)} %bitcast.1.member_ref.refs_0_, bf16[32,8576]{1,0:T(8,128)(2,1)S(1)} %collective-permute-done.x_ref, f32[4,8,1024]{2,1,0:T(8,128)S(1)} %get-tuple-element.53.geo_ref, bf16[256,8192]{1,0:T(8,128)(2,1)S(1)} %get-tuple-element.54.table_ref), custom_call_target="tpu_custom_call" | custom-call | tf_op jit(solution)/shard_map/shifted_rows/pallas_call | solution.py:104
  27.6 3.2 %shifted_rows.6 = (bf16[256,8192]{1,0:T(8,128)(2,1)S(1)}, bf16[32,4096]{1,0:T(8,128)(2,1)S(1)}) custom-call(s32[1]{0:T(128)} %bitcast.1.member_ref.refs_0_, bf16[32,8576]{1,0:T(8,128)(2,1)S(1)} %collective-permute-done.4.x_ref, f32[4,8,1024]{2,1,0:T(8,128)S(1)} %get-tuple-element.53.geo_ref, bf16[256,8192]{1,0:T(8,128)(2,1)S(1)} %get-tuple-element.54.table_ref), custom_call_target="tpu_custom_call" | custom-call | tf_op jit(solution)/shard_map/shifted_rows/pallas_call | solution.py:104
  30.8 1.7 %collective-permute-done.5.x_ref = bf16[32,8576]{1,0:T(8,128)(2,1)S(1)} collective-permute-done((bf16[32,8576]{1,0:T(8,128)(2,1)S(1)}, bf16[32,8576]{1,0:T(8,128)(2,1)S(1)}, u32[]{:S(2)}, u32[]{:S(2)}) %collective-permute-start.5) | collective-permute-done | bytes 548896 | tf_op jit(solution)/shard_map/ppermute | solution.py:56
  32.5 3.2 %shifted_rows.7 = (bf16[256,8192]{1,0:T(8,128)(2,1)S(1)}, bf16[32,4096]{1,0:T(8,128)(2,1)S(1)}) custom-call(s32[1]{0:T(128)} %bitcast.1.member_ref.refs_0_, bf16[32,8576]{1,0:T(8,128)(2,1)S(1)} %collective-permute-done.5.x_ref, f32[4,8,1024]{2,1,0:T(8,128)S(1)} %get-tuple-element.53.geo_ref, bf16[256,8192]{1,0:T(8,128)(2,1)S(1)} %get-tuple-element.54.table_ref), custom_call_target="tpu_custom_call" | custom-call | tf_op jit(solution)/shard_map/shifted_rows/pallas_call | solution.py:104
  35.7 1.5 %partial_scores.3 = f32[256,128]{1,0:T(8,128)S(1)} custom-call(bf16[256,8192]{1,0:T(8,128)(2,1)S(1)} %get-tuple-element.61.refs_0_.refs_4_, bf16[32,4096]{1,0:T(8,128)(2,1)S(1)} %get-tuple-element.69.refs_1_, bf16[16,8192]{1,0:T(8,128)(2,1)S(1)} %own_references.1.refs_2_.refs_4_, bf16[16,8192]{1,0:T(8,128)(2,1)S(1)} %collective-permute-done.3.refs_3_.refs_5_, ...), custom_call_target="tpu_custom_call" | custom-call | tf_op jit(solution)/shard_map/partial_scores/pallas_call | solution.py:104
  38.6 1.5 %partial_scores.4 = f32[256,128]{1,0:T(8,128)S(1)} custom-call(bf16[256,8192]{1,0:T(8,128)(2,1)S(1)} %get-tuple-element.65.refs_0_.refs_5_, bf16[32,4096]{1,0:T(8,128)(2,1)S(1)} %get-tuple-element.73.refs_1_, bf16[16,8192]{1,0:T(8,128)(2,1)S(1)} %own_references.1.refs_2_.refs_4_, bf16[16,8192]{1,0:T(8,128)(2,1)S(1)} %collective-permute-done.3.refs_3_.refs_5_, ...), custom_call_target="tpu_custom_call" | custom-call | tf_op jit(solution)/shard_map/partial_scores/pallas_call | solution.py:104
  40.3 2.7 %partial_scores.5 = (f32[256,128]{1,0:T(8,128)S(1)}, f32[256,128]{1,0:T(8,128)S(1)}) custom-call(bf16[256,8192]{1,0:T(8,128)(2,1)S(1)} %get-tuple-element.55.refs_0_.refs_2_, bf16[256,8192]{1,0:T(8,128)(2,1)S(1)} %get-tuple-element.59.refs_1_.refs_3_, bf16[32,4096]{1,0:T(8,128)(2,1)S(1)} %get-tuple-element.74.refs_2_, ...), custom_call_target="tpu_custom_call" | custom-call | tf_op jit(solution)/shard_map/partial_scores/pallas_call | solution.py:104
  44.1 2.0 %collective-permute-done.11.refs_2_ = f32[256,128]{1,0:T(8,128)S(1)} collective-permute-done((f32[256,128]{1,0:T(8,128)S(1)}, f32[256,128]{1,0:T(8,128)S(1)}, u32[]{:S(2)}, u32[]{:S(2)}) %collective-permute-start.11) | collective-permute-done | bytes 131104 | tf_op jit(solution)/shard_map/ppermute | solution.py:56
  48.3 3.1 %collective-permute-done.14.refs_8_ = bf16[128,256]{1,0:T(8,128)(2,1)S(1)} collective-permute-done((bf16[128,256]{1,0:T(8,128)(2,1)S(1)}, bf16[128,256]{1,0:T(8,128)(2,1)S(1)}, u32[]{:S(2)}, u32[]{:S(2)}) %collective-permute-start.14) | collective-permute-done | bytes 65568 | tf_op jit(solution)/shard_map/ppermute | solution.py:56
  51.9 1.9 %weighted_sums.2 = (bf16[64,2048]{1,0:T(8,128)(2,1)S(1)}, bf16[64,2048]{1,0:T(8,128)(2,1)S(1)}, bf16[64,2048]{1,0:T(8,128)(2,1)S(1)}, bf16[64,2048]{1,0:T(8,128)(2,1)S(1)}) custom-call(s32[1]{0:T(128)} %bitcast.1.member_ref.refs_0_, s32[1]{0:T(128)} %bitcast.2.x_ref.refs_1_, bf16[256,8192]{1,0:T(8,128)(2,1)S(1)} %get-tuple-element.55.refs_0_.refs_2_, ...), custom_call_target="tpu_custom_call" | custom-call | tf_op jit(solution)/shard_map/weighted_sums/pallas_call | solution.py:104
  53.8 1.4 %collective-permute-start.16 = (bf16[64,2048]{1,0:T(8,128)(2,1)S(1)}, bf16[64,2048]{1,0:T(8,128)(2,1)S(1)}, u32[]{:S(2)}, u32[]{:S(2)}) collective-permute-start(bf16[64,2048]{1,0:T(8,128)(2,1)S(1)} %get-tuple-element.79), channel_id=1, source_target_pairs={{0,64},{1,33},{2,66},{3,35},{4,68},{5,37},{6,70},{7,39},{8,72},{9,... | collective-permute-start | bytes 786440 | tf_op jit(solution)/shard_map/ppermute | solution.py:56
  55.2 2.9 %collective-permute-start.17 = (bf16[64,2048]{1,0:T(8,128)(2,1)S(1)}, bf16[64,2048]{1,0:T(8,128)(2,1)S(1)}, u32[]{:S(2)}, u32[]{:S(2)}) collective-permute-start(bf16[64,2048]{1,0:T(8,128)(2,1)S(1)} %get-tuple-element.80), channel_id=1, source_target_pairs={{0,128},{1,17},{2,130},{3,19},{4,132},{5,21},{6,134},{7,23},{8,136... | collective-permute-start | bytes 786440 | tf_op jit(solution)/shard_map/ppermute | solution.py:56
  58.6 1.9 %weighted_sums.3 = (bf16[64,2048]{1,0:T(8,128)(2,1)S(1)}, bf16[64,2048]{1,0:T(8,128)(2,1)S(1)}, bf16[64,2048]{1,0:T(8,128)(2,1)S(1)}, bf16[64,2048]{1,0:T(8,128)(2,1)S(1)}) custom-call(s32[1]{0:T(128)} %bitcast.1.member_ref.refs_0_, s32[1]{0:T(128)} %bitcast.2.x_ref.refs_1_, bf16[256,8192]{1,0:T(8,128)(2,1)S(1)} %get-tuple-element.55.refs_0_.refs_2_, ...), custom_call_target="tpu_custom_call" | custom-call | tf_op jit(solution)/shard_map/weighted_sums/pallas_call | solution.py:104
  61.5 1.8 %collective-permute-start.24 = (bf16[64,2048]{1,0:T(8,128)(2,1)S(1)}, bf16[64,2048]{1,0:T(8,128)(2,1)S(1)}, u32[]{:S(2)}, u32[]{:S(2)}) collective-permute-start(bf16[64,2048]{1,0:T(8,128)(2,1)S(1)} %get-tuple-element.90), channel_id=1, source_target_pairs={{0,48},{1,193},{2,50},{3,195},{4,52},{5,197},{6,54},{7,199},{8,56}... | collective-permute-start | bytes 786440 | tf_op jit(solution)/shard_map/ppermute | solution.py:56
  63.3 1.5 %collective-permute-start.23 = (bf16[64,2048]{1,0:T(8,128)(2,1)S(1)}, bf16[64,2048]{1,0:T(8,128)(2,1)S(1)}, u32[]{:S(2)}, u32[]{:S(2)}) collective-permute-start(bf16[64,2048]{1,0:T(8,128)(2,1)S(1)} %get-tuple-element.89), channel_id=1, source_target_pairs={{0,16},{1,129},{2,18},{3,131},{4,20},{5,133},{6,22},{7,135},{8,24}... | collective-permute-start | bytes 786440 | tf_op jit(solution)/shard_map/ppermute | solution.py:56
  64.7 2.0 %collective-permute-done.17.refs_4_ = bf16[64,2048]{1,0:T(8,128)(2,1)S(1)} collective-permute-done((bf16[64,2048]{1,0:T(8,128)(2,1)S(1)}, bf16[64,2048]{1,0:T(8,128)(2,1)S(1)}, u32[]{:S(2)}, u32[]{:S(2)}) %collective-permute-start.17) | collective-permute-done | bytes 262176 | tf_op jit(solution)/shard_map/ppermute | solution.py:56
  66.8 7.5 %collective-permute-done.18.refs_5_ = bf16[64,2048]{1,0:T(8,128)(2,1)S(1)} collective-permute-done((bf16[64,2048]{1,0:T(8,128)(2,1)S(1)}, bf16[64,2048]{1,0:T(8,128)(2,1)S(1)}, u32[]{:S(2)}, u32[]{:S(2)}) %collective-permute-start.18) | collective-permute-done | bytes 262176 | tf_op jit(solution)/shard_map/ppermute | solution.py:56
  74.5 2.9 %collective-permute-start.20 = (bf16[16,2048]{1,0:T(8,128)(2,1)S(1)}, bf16[16,2048]{1,0:T(8,128)(2,1)S(1)}, u32[]{:S(2)}, u32[]{:S(2)}) collective-permute-start(bf16[16,2048]{1,0:T(8,128)(2,1)S(1)} %get-tuple-element.84), channel_id=1, source_target_pairs={{0,16},{1,129},{2,18},{3,131},{4,20},{5,133},{6,22},{7,135},{8,24}... | collective-permute-start | bytes 196616 | tf_op jit(solution)/shard_map/ppermute | solution.py:56
  79.5 3.7 %collective-permute-start.27 = (bf16[16,2048]{1,0:T(8,128)(2,1)S(1)}, bf16[16,2048]{1,0:T(8,128)(2,1)S(1)}, u32[]{:S(2)}, u32[]{:S(2)}) collective-permute-start(bf16[16,2048]{1,0:T(8,128)(2,1)S(1)} %get-tuple-element.94), channel_id=1, source_target_pairs={{0,192},{1,49},{2,194},{3,51},{4,196},{5,53},{6,198},{7,55},{8,200... | collective-permute-start | bytes 196616 | tf_op jit(solution)/shard_map/ppermute | solution.py:56
  85.5 3.4 %collective-permute-start.28 = (bf16[16,1024]{1,0:T(8,128)(2,1)S(1)}, bf16[16,1024]{1,0:T(8,128)(2,1)S(1)}, u32[]{:S(2)}, u32[]{:S(2)}) collective-permute-start(bf16[16,1024]{1,0:T(8,128)(2,1)S(1)} %get-tuple-element.96), channel_id=1, source_target_pairs={{0,4},{1,5},{2,6},{3,7},{4,0},{5,1},{6,2},{7,3},{8,12},{9,13},{10,... | collective-permute-start | bytes 98312 | tf_op jit(solution)/shard_map/ppermute | solution.py:56
  88.8 4.6 %collective-permute-start.29 = (bf16[16,1024]{1,0:T(8,128)(2,1)S(1)}, bf16[16,1024]{1,0:T(8,128)(2,1)S(1)}, u32[]{:S(2)}, u32[]{:S(2)}) collective-permute-start(bf16[16,1024]{1,0:T(8,128)(2,1)S(1)} %get-tuple-element.97), channel_id=1, source_target_pairs={{0,8},{1,9},{2,10},{3,11},{4,12},{5,13},{6,14},{7,15},{8,0},{9,1},... | collective-permute-start | bytes 98312 | tf_op jit(solution)/shard_map/ppermute | solution.py:56
  93.4 3.3 %collective-permute-done.29 = bf16[16,1024]{1,0:T(8,128)(2,1)S(1)} collective-permute-done((bf16[16,1024]{1,0:T(8,128)(2,1)S(1)}, bf16[16,1024]{1,0:T(8,128)(2,1)S(1)}, u32[]{:S(2)}, u32[]{:S(2)}) %collective-permute-start.29) | collective-permute-done | bytes 32800 | tf_op jit(solution)/shard_map/ppermute | solution.py:56
  96.6 2.8 %collective-permute-done.30 = bf16[16,1024]{1,0:T(8,128)(2,1)S(1)} collective-permute-done((bf16[16,1024]{1,0:T(8,128)(2,1)S(1)}, bf16[16,1024]{1,0:T(8,128)(2,1)S(1)}, u32[]{:S(2)}, u32[]{:S(2)}) %collective-permute-start.30) | collective-permute-done | bytes 32800 | tf_op jit(solution)/shard_map/ppermute | solution.py:56
  (48 shorter events, 14.5 us)
Async XLA Ops:
  2.0 16.2 %collective-permute-start = (bf16[32,8576]{1,0:T(8,128)(2,1)S(1)}, bf16[32,8576]{1,0:T(8,128)(2,1)S(1)}, u32[]{:S(2)}, u32[]{:S(2)}) collective-permute-start(bf16[32,8576]{1,0:T(8,128)(2,1)S(1)} %get-tuple-element.56), channel_id=1, source_target_pairs={{0,1},{1,0},{2,3},{3,2},{4,5},{5,4},{6,7},{7,6},{8,9},{9,8},{10,11... | collective-permute-start | bytes 1646600 | tf_op jit(solution)/shard_map/ppermute | solution.py:56
  2.1 16.1 %collective-permute-start.4 = (bf16[32,8576]{1,0:T(8,128)(2,1)S(1)}, bf16[32,8576]{1,0:T(8,128)(2,1)S(1)}, u32[]{:S(2)}, u32[]{:S(2)}) collective-permute-start(bf16[32,8576]{1,0:T(8,128)(2,1)S(1)} %get-tuple-element.57.after), channel_id=1, source_target_pairs={{0,2},{1,3},{2,0},{3,1},{4,6},{5,7},{6,4},{7,5},{8,10},{9,11},{10,... | collective-permute-start | bytes 1646600 | tf_op jit(solution)/shard_map/ppermute | solution.py:56
  5.0 13.1 %collective-permute-start.1 = (bf16[16,8192]{1,0:T(8,128)(2,1)S(1)}, bf16[16,8192]{1,0:T(8,128)(2,1)S(1)}, u32[]{:S(2)}, u32[]{:S(2)}) collective-permute-start(bf16[16,8192]{1,0:T(8,128)(2,1)S(1)} %own_references.1.refs_2_.refs_4_), channel_id=1, source_target_pairs={{0,64},{1,65},{2,66},{3,67},{4,68},{5,69},{6,70},{7,71},{8,72},{9,... | collective-permute-start | bytes 786440 | tf_op jit(solution)/shard_map/ppermute | solution.py:56
  6.7 11.4 %collective-permute-start.2 = (bf16[16,8192]{1,0:T(8,128)(2,1)S(1)}, bf16[16,8192]{1,0:T(8,128)(2,1)S(1)}, u32[]{:S(2)}, u32[]{:S(2)}) collective-permute-start(bf16[16,8192]{1,0:T(8,128)(2,1)S(1)} %own_references.1.refs_2_.refs_4_), channel_id=1, source_target_pairs={{0,192},{1,193},{2,194},{3,195},{4,196},{5,197},{6,198},{7,199},{8... | collective-permute-start | bytes 786440 | tf_op jit(solution)/shard_map/ppermute | solution.py:56
  8.9 9.3 %collective-permute-start.3 = (bf16[16,8192]{1,0:T(8,128)(2,1)S(1)}, bf16[16,8192]{1,0:T(8,128)(2,1)S(1)}, u32[]{:S(2)}, u32[]{:S(2)}) collective-permute-start(bf16[16,8192]{1,0:T(8,128)(2,1)S(1)} %own_references.1.refs_2_.refs_4_), channel_id=1, source_target_pairs={{0,32},{1,33},{2,34},{3,35},{4,36},{5,37},{6,38},{7,39},{8,40},{9,... | collective-permute-start | bytes 786440 | tf_op jit(solution)/shard_map/ppermute | solution.py:56
  18.2 14.3 %collective-permute-start.5 = (bf16[32,8576]{1,0:T(8,128)(2,1)S(1)}, bf16[32,8576]{1,0:T(8,128)(2,1)S(1)}, u32[]{:S(2)}, u32[]{:S(2)}) collective-permute-start(bf16[32,8576]{1,0:T(8,128)(2,1)S(1)} %get-tuple-element.63), channel_id=1, source_target_pairs={{0,3},{1,2},{2,1},{3,0},{4,7},{5,6},{6,5},{7,4},{8,11},{9,10},{10,... | collective-permute-start | bytes 1646600 | tf_op jit(solution)/shard_map/ppermute | solution.py:56
  18.3 17.4 %collective-permute-start.6 = (bf16[16,8192]{1,0:T(8,128)(2,1)S(1)}, bf16[16,8192]{1,0:T(8,128)(2,1)S(1)}, u32[]{:S(2)}, u32[]{:S(2)}) collective-permute-start(bf16[16,8192]{1,0:T(8,128)(2,1)S(1)} %collective-permute-done.1.refs_4_.refs_6_), channel_id=1, source_target_pairs={{0,32},{1,33},{2,34},{3,35},{4,36},{5,37},{6,38},{7,39},{8,40},{9,... | collective-permute-start | bytes 786440 | tf_op jit(solution)/shard_map/ppermute | solution.py:56
  19.8 15.8 %collective-permute-start.7 = (bf16[16,8192]{1,0:T(8,128)(2,1)S(1)}, bf16[16,8192]{1,0:T(8,128)(2,1)S(1)}, u32[]{:S(2)}, u32[]{:S(2)}) collective-permute-start(bf16[16,8192]{1,0:T(8,128)(2,1)S(1)} %collective-permute-done.1.refs_4_.refs_6_), channel_id=1, source_target_pairs={{0,192},{1,193},{2,194},{3,195},{4,196},{5,197},{6,198},{7,199},{8... | collective-permute-start | bytes 786440 | tf_op jit(solution)/shard_map/ppermute | solution.py:56
  21.7 14.0 %collective-permute-start.8 = (bf16[16,8192]{1,0:T(8,128)(2,1)S(1)}, bf16[16,8192]{1,0:T(8,128)(2,1)S(1)}, u32[]{:S(2)}, u32[]{:S(2)}) collective-permute-start(bf16[16,8192]{1,0:T(8,128)(2,1)S(1)} %collective-permute-done.3.refs_3_.refs_5_), channel_id=1, source_target_pairs={{0,128},{1,129},{2,130},{3,131},{4,132},{5,133},{6,134},{7,135},{8... | collective-permute-start | bytes 786440 | tf_op jit(solution)/shard_map/ppermute | solution.py:56
  22.6 13.1 %collective-permute-start.9 = (bf16[16,8192]{1,0:T(8,128)(2,1)S(1)}, bf16[16,8192]{1,0:T(8,128)(2,1)S(1)}, u32[]{:S(2)}, u32[]{:S(2)}) collective-permute-start(bf16[16,8192]{1,0:T(8,128)(2,1)S(1)} %collective-permute-done.2.refs_8_.refs_10_), channel_id=1, source_target_pairs={{0,48},{1,49},{2,50},{3,51},{4,52},{5,53},{6,54},{7,55},{8,56},{9,... | collective-permute-start | bytes 786440 | tf_op jit(solution)/shard_map/ppermute | solution.py:56
  37.3 8.8 %collective-permute-start.10 = (f32[256,128]{1,0:T(8,128)S(1)}, f32[256,128]{1,0:T(8,128)S(1)}, u32[]{:S(2)}, u32[]{:S(2)}) collective-permute-start(f32[256,128]{1,0:T(8,128)S(1)} %partial_scores.3), channel_id=1, source_target_pairs={{0,2},{1,3},{2,0},{3,1},{4,6},{5,7},{6,4},{7,5},{8,10},{9,11},{10,... | collective-permute-start | bytes 393224 | tf_op jit(solution)/shard_map/ppermute | solution.py:56
  40.2 5.9 %collective-permute-start.11 = (f32[256,128]{1,0:T(8,128)S(1)}, f32[256,128]{1,0:T(8,128)S(1)}, u32[]{:S(2)}, u32[]{:S(2)}) collective-permute-start(f32[256,128]{1,0:T(8,128)S(1)} %partial_scores.4), channel_id=1, source_target_pairs={{0,3},{1,2},{2,1},{3,0},{4,7},{5,6},{6,5},{7,4},{8,11},{9,10},{10,... | collective-permute-start | bytes 393224 | tf_op jit(solution)/shard_map/ppermute | solution.py:56
  43.0 3.1 %collective-permute-start.12 = (f32[256,128]{1,0:T(8,128)S(1)}, f32[256,128]{1,0:T(8,128)S(1)}, u32[]{:S(2)}, u32[]{:S(2)}) collective-permute-start(f32[256,128]{1,0:T(8,128)S(1)} %get-tuple-element.77), channel_id=1, source_target_pairs={{0,1},{1,0},{2,3},{3,2},{4,5},{5,4},{6,7},{7,6},{8,9},{9,8},{10,11... | collective-permute-start | bytes 393224 | tf_op jit(solution)/shard_map/ppermute | solution.py:56
  46.4 2.0 %collective-permute-start.13 = (bf16[128,256]{1,0:T(8,128)(2,1)S(1)}, bf16[128,256]{1,0:T(8,128)(2,1)S(1)}, u32[]{:S(2)}, u32[]{:S(2)}) collective-permute-start(bf16[128,256]{1,0:T(8,128)(2,1)S(1)} %posterior.1.refs_6_), channel_id=1, source_target_pairs={{0,1},{1,0},{2,3},{3,2},{4,5},{5,4},{6,7},{7,6},{8,9},{9,8},{10,11... | collective-permute-start | bytes 196616 | tf_op jit(solution)/shard_map/ppermute | solution.py:56
  46.6 4.9 %collective-permute-start.14 = (bf16[128,256]{1,0:T(8,128)(2,1)S(1)}, bf16[128,256]{1,0:T(8,128)(2,1)S(1)}, u32[]{:S(2)}, u32[]{:S(2)}) collective-permute-start(bf16[128,256]{1,0:T(8,128)(2,1)S(1)} %posterior.1.refs_6_), channel_id=1, source_target_pairs={{0,2},{1,3},{2,0},{3,1},{4,6},{5,7},{6,4},{7,5},{8,10},{9,11},{10,... | collective-permute-start | bytes 196616 | tf_op jit(solution)/shard_map/ppermute | solution.py:56
  47.4 4.5 %collective-permute-start.15 = (bf16[128,256]{1,0:T(8,128)(2,1)S(1)}, bf16[128,256]{1,0:T(8,128)(2,1)S(1)}, u32[]{:S(2)}, u32[]{:S(2)}) collective-permute-start(bf16[128,256]{1,0:T(8,128)(2,1)S(1)} %posterior.1.refs_6_), channel_id=1, source_target_pairs={{0,3},{1,2},{2,1},{3,0},{4,7},{5,6},{6,5},{7,4},{8,11},{9,10},{10,... | collective-permute-start | bytes 196616 | tf_op jit(solution)/shard_map/ppermute | solution.py:56
  53.8 9.4 %collective-permute-start.16 = (bf16[64,2048]{1,0:T(8,128)(2,1)S(1)}, bf16[64,2048]{1,0:T(8,128)(2,1)S(1)}, u32[]{:S(2)}, u32[]{:S(2)}) collective-permute-start(bf16[64,2048]{1,0:T(8,128)(2,1)S(1)} %get-tuple-element.79), channel_id=1, source_target_pairs={{0,64},{1,33},{2,66},{3,35},{4,68},{5,37},{6,70},{7,39},{8,72},{9,... | collective-permute-start | bytes 786440 | tf_op jit(solution)/shard_map/ppermute | solution.py:56
  55.2 11.6 %collective-permute-start.17 = (bf16[64,2048]{1,0:T(8,128)(2,1)S(1)}, bf16[64,2048]{1,0:T(8,128)(2,1)S(1)}, u32[]{:S(2)}, u32[]{:S(2)}) collective-permute-start(bf16[64,2048]{1,0:T(8,128)(2,1)S(1)} %get-tuple-element.80), channel_id=1, source_target_pairs={{0,128},{1,17},{2,130},{3,19},{4,132},{5,21},{6,134},{7,23},{8,136... | collective-permute-start | bytes 786440 | tf_op jit(solution)/shard_map/ppermute | solution.py:56
  58.1 16.2 %collective-permute-start.18 = (bf16[64,2048]{1,0:T(8,128)(2,1)S(1)}, bf16[64,2048]{1,0:T(8,128)(2,1)S(1)}, u32[]{:S(2)}, u32[]{:S(2)}) collective-permute-start(bf16[64,2048]{1,0:T(8,128)(2,1)S(1)} %get-tuple-element.81), channel_id=1, source_target_pairs={{0,192},{1,49},{2,194},{3,51},{4,196},{5,53},{6,198},{7,55},{8,200... | collective-permute-start | bytes 786440 | tf_op jit(solution)/shard_map/ppermute | solution.py:56
  60.5 16.9 %collective-permute-start.22 = (bf16[64,2048]{1,0:T(8,128)(2,1)S(1)}, bf16[64,2048]{1,0:T(8,128)(2,1)S(1)}, u32[]{:S(2)}, u32[]{:S(2)}) collective-permute-start(bf16[64,2048]{1,0:T(8,128)(2,1)S(1)} %get-tuple-element.87), channel_id=1, source_target_pairs={{0,32},{1,65},{2,34},{3,67},{4,36},{5,69},{6,38},{7,71},{8,40},{9,... | collective-permute-start | bytes 786440 | tf_op jit(solution)/shard_map/ppermute | solution.py:56
  61.5 16.5 %collective-permute-start.24 = (bf16[64,2048]{1,0:T(8,128)(2,1)S(1)}, bf16[64,2048]{1,0:T(8,128)(2,1)S(1)}, u32[]{:S(2)}, u32[]{:S(2)}) collective-permute-start(bf16[64,2048]{1,0:T(8,128)(2,1)S(1)} %get-tuple-element.90), channel_id=1, source_target_pairs={{0,48},{1,193},{2,50},{3,195},{4,52},{5,197},{6,54},{7,199},{8,56}... | collective-permute-start | bytes 786440 | tf_op jit(solution)/shard_map/ppermute | solution.py:56
  63.3 14.7 %collective-permute-start.23 = (bf16[64,2048]{1,0:T(8,128)(2,1)S(1)}, bf16[64,2048]{1,0:T(8,128)(2,1)S(1)}, u32[]{:S(2)}, u32[]{:S(2)}) collective-permute-start(bf16[64,2048]{1,0:T(8,128)(2,1)S(1)} %get-tuple-element.89), channel_id=1, source_target_pairs={{0,16},{1,129},{2,18},{3,131},{4,20},{5,133},{6,22},{7,135},{8,24}... | collective-permute-start | bytes 786440 | tf_op jit(solution)/shard_map/ppermute | solution.py:56
  74.4 5.0 %collective-permute-start.19 = (bf16[16,2048]{1,0:T(8,128)(2,1)S(1)}, bf16[16,2048]{1,0:T(8,128)(2,1)S(1)}, u32[]{:S(2)}, u32[]{:S(2)}) collective-permute-start(bf16[16,2048]{1,0:T(8,128)(2,1)S(1)} %get-tuple-element.83), channel_id=1, source_target_pairs={{0,32},{1,65},{2,34},{3,67},{4,36},{5,69},{6,38},{7,71},{8,40},{9,... | collective-permute-start | bytes 196616 | tf_op jit(solution)/shard_map/ppermute | solution.py:56
  74.5 8.6 %collective-permute-start.20 = (bf16[16,2048]{1,0:T(8,128)(2,1)S(1)}, bf16[16,2048]{1,0:T(8,128)(2,1)S(1)}, u32[]{:S(2)}, u32[]{:S(2)}) collective-permute-start(bf16[16,2048]{1,0:T(8,128)(2,1)S(1)} %get-tuple-element.84), channel_id=1, source_target_pairs={{0,16},{1,129},{2,18},{3,131},{4,20},{5,133},{6,22},{7,135},{8,24}... | collective-permute-start | bytes 196616 | tf_op jit(solution)/shard_map/ppermute | solution.py:56
  77.5 5.7 %collective-permute-start.21 = (bf16[16,2048]{1,0:T(8,128)(2,1)S(1)}, bf16[16,2048]{1,0:T(8,128)(2,1)S(1)}, u32[]{:S(2)}, u32[]{:S(2)}) collective-permute-start(bf16[16,2048]{1,0:T(8,128)(2,1)S(1)} %get-tuple-element.85), channel_id=1, source_target_pairs={{0,48},{1,193},{2,50},{3,195},{4,52},{5,197},{6,54},{7,199},{8,56}... | collective-permute-start | bytes 196616 | tf_op jit(solution)/shard_map/ppermute | solution.py:56
  78.1 5.0 %collective-permute-start.25 = (bf16[16,2048]{1,0:T(8,128)(2,1)S(1)}, bf16[16,2048]{1,0:T(8,128)(2,1)S(1)}, u32[]{:S(2)}, u32[]{:S(2)}) collective-permute-start(bf16[16,2048]{1,0:T(8,128)(2,1)S(1)} %get-tuple-element.92), channel_id=1, source_target_pairs={{0,64},{1,33},{2,66},{3,35},{4,68},{5,37},{6,70},{7,39},{8,72},{9,... | collective-permute-start | bytes 196616 | tf_op jit(solution)/shard_map/ppermute | solution.py:56
  78.5 5.9 %collective-permute-start.26 = (bf16[16,2048]{1,0:T(8,128)(2,1)S(1)}, bf16[16,2048]{1,0:T(8,128)(2,1)S(1)}, u32[]{:S(2)}, u32[]{:S(2)}) collective-permute-start(bf16[16,2048]{1,0:T(8,128)(2,1)S(1)} %get-tuple-element.93), channel_id=1, source_target_pairs={{0,128},{1,17},{2,130},{3,19},{4,132},{5,21},{6,134},{7,23},{8,136... | collective-permute-start | bytes 196616 | tf_op jit(solution)/shard_map/ppermute | solution.py:56
  79.5 5.9 %collective-permute-start.27 = (bf16[16,2048]{1,0:T(8,128)(2,1)S(1)}, bf16[16,2048]{1,0:T(8,128)(2,1)S(1)}, u32[]{:S(2)}, u32[]{:S(2)}) collective-permute-start(bf16[16,2048]{1,0:T(8,128)(2,1)S(1)} %get-tuple-element.94), channel_id=1, source_target_pairs={{0,192},{1,49},{2,194},{3,51},{4,196},{5,53},{6,198},{7,55},{8,200... | collective-permute-start | bytes 196616 | tf_op jit(solution)/shard_map/ppermute | solution.py:56
  85.5 7.9 %collective-permute-start.28 = (bf16[16,1024]{1,0:T(8,128)(2,1)S(1)}, bf16[16,1024]{1,0:T(8,128)(2,1)S(1)}, u32[]{:S(2)}, u32[]{:S(2)}) collective-permute-start(bf16[16,1024]{1,0:T(8,128)(2,1)S(1)} %get-tuple-element.96), channel_id=1, source_target_pairs={{0,4},{1,5},{2,6},{3,7},{4,0},{5,1},{6,2},{7,3},{8,12},{9,13},{10,... | collective-permute-start | bytes 98312 | tf_op jit(solution)/shard_map/ppermute | solution.py:56
  88.8 7.8 %collective-permute-start.29 = (bf16[16,1024]{1,0:T(8,128)(2,1)S(1)}, bf16[16,1024]{1,0:T(8,128)(2,1)S(1)}, u32[]{:S(2)}, u32[]{:S(2)}) collective-permute-start(bf16[16,1024]{1,0:T(8,128)(2,1)S(1)} %get-tuple-element.97), channel_id=1, source_target_pairs={{0,8},{1,9},{2,10},{3,11},{4,12},{5,13},{6,14},{7,15},{8,0},{9,1},... | collective-permute-start | bytes 98312 | tf_op jit(solution)/shard_map/ppermute | solution.py:56
  93.4 6.0 %collective-permute-start.30 = (bf16[16,1024]{1,0:T(8,128)(2,1)S(1)}, bf16[16,1024]{1,0:T(8,128)(2,1)S(1)}, u32[]{:S(2)}, u32[]{:S(2)}) collective-permute-start(bf16[16,1024]{1,0:T(8,128)(2,1)S(1)} %get-tuple-element.98), channel_id=1, source_target_pairs={{0,12},{1,13},{2,14},{3,15},{4,8},{5,9},{6,10},{7,11},{8,4},{9,5},... | collective-permute-start | bytes 98312 | tf_op jit(solution)/shard_map/ppermute | solution.py:56

commit v11 on v10

--- a/solution.py
+++ b/solution.py
@@ -294,17 +294,19 @@
     )
 
 
-def scores_kernel(count, *refs):
+def scores_kernel(count, fresh, *refs):
     blocks = refs[2 * count : 2 * count + 8]
     outs = refs[2 * count + 8 :]
     stacked = jnp.concatenate([block[...] for block in blocks], axis=0)
-    power = []
-    for block in range(NB):
-        start = block * 2 * COLS
-        real = stacked[:, start : start + COLS].astype(F32)
-        imag = stacked[:, start + COLS : start + 2 * COLS].astype(F32)
-        power.append((real * real + imag * imag).astype(BF16))
-    power = jnp.concatenate(power, axis=1)
+    if fresh:
+        for block in range(NB):
+            start = block * 2 * COLS
+            real = stacked[:, start : start + COLS].astype(F32)
+            imag = stacked[:, start + COLS : start + 2 * COLS].astype(F32)
+            outs[-1][:, block * COLS : (block + 1) * COLS] = (real * real + imag * imag).astype(BF16)
+        power, outs = outs[-1][...], outs[:-1]
+    else:
+        power, outs = outs[0][...], outs[1:]
     pens = jnp.concatenate([pen[...] for pen in refs[count : 2 * count]], axis=0)
     rows = jnp.concatenate([row[...] for row in refs[:count]], axis=0)
     energy = lax.dot_general(pens, power, NT, preferred_element_type=F32)
@@ -314,11 +316,12 @@
         out[...] = (mine - energy[None, n * P_DEV : (n + 1) * P_DEV]).reshape(ROWS, 128)
 
 
-def make_scores(rows, pens, blocks):
-    count = len(rows)
-    return local(
-        lambda *refs: scores_kernel(count, *refs), "partial_scores", [((ROWS, 128), F32)] * count,
-        [], [*rows, *pens, *blocks], 12,
+def make_scores(rows, pens, blocks, power=None):
+    count, fresh = len(rows), power is None
+    outs = [((ROWS, 128), F32)] * count + [((128, NB * COLS), BF16)] * fresh
+    return local(
+        lambda *refs: scores_kernel(count, fresh, *refs), "partial_scores", outs, [],
+        [*rows, *pens, *blocks] + ([] if fresh else [power]), 12,
     )
 
 
@@ -442,31 +445,27 @@
     rows[3], pens[3] = make_rows(member, after(got[3], rows[2]), geo, table)
     blocks = [gathered[ky, kx] for ky in range(Y) for kx in range(2)]
 
-    (second,) = make_scores([rows[2]], [after(pens[2], rows[3])], blocks)
-    (third,) = make_scores([rows[3]], [after(pens[3], second)], blocks)
-    mine, other = make_scores([rows[0], rows[1]], [after(pens[0], third), pens[1]], blocks)
+    second, power = make_scores([rows[2]], [after(pens[2], rows[3])], blocks)
+    (third,) = make_scores([rows[3]], [after(pens[3], second)], blocks, power)
+    mine, other = make_scores([rows[0], rows[1]], [after(pens[0], third), pens[1]], blocks, power)
     near = [mine, send(second, partners(2)), send(third, partners(3))]
     (near,) = local(sum_kernel, "score_sums", [((ROWS, 128), F32)], [], near, 4)
     posterior = make_posterior([near, send(other, partners(1))])
-    posts = [posterior] + [send(posterior, partners(n)) for n in range(1, G)]
+    posts = {n: send(posterior, partners(n)) for n in (3, 2, 1)}
+    posts = [posterior] + [posts[n] for n in range(1, G)]
     rows = [rows[n] for n in range(G)]
 
     first = make_accum(0, member, x_at, rows, posts)
-    first = [first[0]] + [send(first[n], crossed(n, 0)) for n in range(1, 4)]
+    first = [first[0]] + [send(first[n], crossed(n, 0)) for n in (2, 1, 3)]
     second = make_accum(1, member, x_at, rows, posts)
-    second = [
-        second[0],
-        send(second[1], crossed(1, 1)),
-        send(after(second[2], first[1]), crossed(2, 1)),
-        send(second[3], crossed(3, 1)),
-    ]
+    second = [second[0]] + [send(second[n], crossed(n, 1)) for n in (2, 1, 3)]
     first = make_turn(0, member, x_at, first)
-    first = [first[0]] + [send(first[n], crossed(n, 1)) for n in range(1, 4)]
+    first = [first[0]] + [send(first[n], crossed(n, 1)) for n in (2, 1, 3)]
     second = make_turn(1, member, x_at, second)
-    second = [second[0]] + [send(second[n], crossed(n, 0)) for n in range(1, 4)]
+    second = [second[0]] + [send(second[n], crossed(n, 0)) for n in (2, 1, 3)]
     outs = [((16, COLS), F32)] + [((16, COLS), BF16)] * (NB - 1)
     ends = local(joined_kernel, "joined_sums", outs, [block], [*first, *second], 4)
-    return added([ends[0]] + [send(ends[n], flips(z=n * (G // 2))) for n in range(1, NB)])
+    return added([ends[0]] + [send(ends[n], flips(z=n * (G // 2))) for n in (2, 1, 3)])
 
 
 def solution(mesh):

time: 101 us -> 96 us (0.950)
  waiting for transfers between devices: 25.1 us -> 20 us
    ppermute x31, waiting for transfers between devices: 25.1 us -> 20 us  [send(): return lax.ppermute(value, AXES, pairs)]
  transfers between devices with their start and end apart: 31 -> 31, of which waited for: 10 -> 13; matrix products, arithmetic and copies ran while one was open for 0% -> 0% of each run, Pallas kernels for 26% -> 27%
where the time goes in v11:
time: 96 us; the launch traced here: 95.7 us
  starting transfers between devices  43.4 us (45%)
  Pallas kernels  31.4 us (33%)
  waiting for transfers between devices  20 us (21%)
    ppermute x31, starting transfers between devices, send(): return lax.ppermute(value, AXES, pairs)  43.4 us
    pallas_call x17, Pallas kernels, local(): pl.pallas_call(kernel, in_specs=[SCALARS] * len(scalars) + [PLACED] * pla...  31.4 us
    ppermute x31, waiting for transfers between devices, send(): return lax.ppermute(value, AXES, pairs)  20 us
  transfers between devices with their start and end apart: 31, of which 13 were waited for; matrix products, arithmetic and copies ran while one was open for 0% of the time, Pallas kernels for 27%

profile of v11, /device:TPU:2, one launch (start us, length us, event | category | flops | bytes accessed | tf_op | source)
XLA Modules:
  0.0 95.7 jit_solution(17688863911290415538)
XLA Ops:
  0.0 2.0 %split_particles.1 = (bf16[32,8576]{1,0:T(8,128)(2,1)S(1)}, bf16[32,8576]{1,0:T(8,128)(2,1)S(1)}, bf16[32,8576]{1,0:T(8,128)(2,1)S(1)}, bf16[32,8576]{1,0:T(8,128)(2,1)S(1)}) custom-call(s32[1]{0:T(128)} %bitcast.1.member_ref.refs_0_, s32[1]{0:T(128)} %bitcast.block_ref, s32[1]{0:T(128)} %bitcast.2.x_ref.refs_1_, bf16[32,32768]{1,0:T(8,128)(2,1)} %source.2, ...), custom_call_target="tpu_custom_call" | custom-call | tf_op jit(solution)/shard_map/split_particles/pallas_call | solution.py:104
  2.1 2.0 %collective-permute-start.4 = (bf16[32,8576]{1,0:T(8,128)(2,1)S(1)}, bf16[32,8576]{1,0:T(8,128)(2,1)S(1)}, u32[]{:S(2)}, u32[]{:S(2)}) collective-permute-start(bf16[32,8576]{1,0:T(8,128)(2,1)S(1)} %get-tuple-element.58.after), channel_id=1, source_target_pairs={{0,2},{1,3},{2,0},{3,1},{4,6},{5,7},{6,4},{7,5},{8,10},{9,11},{10,... | collective-permute-start | bytes 1646600 | tf_op jit(solution)/shard_map/ppermute | solution.py:56
  5.0 1.7 %collective-permute-start.1 = (bf16[16,8192]{1,0:T(8,128)(2,1)S(1)}, bf16[16,8192]{1,0:T(8,128)(2,1)S(1)}, u32[]{:S(2)}, u32[]{:S(2)}) collective-permute-start(bf16[16,8192]{1,0:T(8,128)(2,1)S(1)} %own_references.1.refs_2_.refs_4_), channel_id=1, source_target_pairs={{0,64},{1,65},{2,66},{3,67},{4,68},{5,69},{6,70},{7,71},{8,72},{9,... | collective-permute-start | bytes 786440 | tf_op jit(solution)/shard_map/ppermute | solution.py:56
  6.7 2.2 %collective-permute-start.2 = (bf16[16,8192]{1,0:T(8,128)(2,1)S(1)}, bf16[16,8192]{1,0:T(8,128)(2,1)S(1)}, u32[]{:S(2)}, u32[]{:S(2)}) collective-permute-start(bf16[16,8192]{1,0:T(8,128)(2,1)S(1)} %own_references.1.refs_2_.refs_4_), channel_id=1, source_target_pairs={{0,192},{1,193},{2,194},{3,195},{4,196},{5,197},{6,198},{7,199},{8... | collective-permute-start | bytes 786440 | tf_op jit(solution)/shard_map/ppermute | solution.py:56
  9.4 5.5 %phase_table.1 = (bf16[256,8192]{1,0:T(8,128)(2,1)S(1)}, f32[4,8,1024]{2,1,0:T(8,128)S(1)}) custom-call(s32[1]{0:T(128)} %bitcast.1.member_ref.refs_0_, f32[16,8,1024]{2,1,0:T(8,128)} %constant.63.clone.geo_ref), custom_call_target="tpu_custom_call" | custom-call | tf_op jit(solution)/shard_map/phase_table/pallas_call | solution.py:104
  14.9 3.2 %shifted_rows.4 = (bf16[256,8192]{1,0:T(8,128)(2,1)S(1)}, bf16[32,4096]{1,0:T(8,128)(2,1)S(1)}) custom-call(s32[1]{0:T(128)} %bitcast.1.member_ref.refs_0_, bf16[32,8576]{1,0:T(8,128)(2,1)S(1)} %get-tuple-element.53.x_ref, f32[4,8,1024]{2,1,0:T(8,128)S(1)} %get-tuple-element.54.geo_ref, bf16[256,8192]{1,0:T(8,128)(2,1)S(1)} %get-tuple-element.55.table_ref), custom_call_target="tpu_custom_call" | custom-call | tf_op jit(solution)/shard_map/shifted_rows/pallas_call | solution.py:104
  18.3 1.6 %collective-permute-start.6 = (bf16[16,8192]{1,0:T(8,128)(2,1)S(1)}, bf16[16,8192]{1,0:T(8,128)(2,1)S(1)}, u32[]{:S(2)}, u32[]{:S(2)}) collective-permute-start(bf16[16,8192]{1,0:T(8,128)(2,1)S(1)} %collective-permute-done.1.refs_4_.refs_6_), channel_id=1, source_target_pairs={{0,32},{1,33},{2,34},{3,35},{4,36},{5,37},{6,38},{7,39},{8,40},{9,... | collective-permute-start | bytes 786440 | tf_op jit(solution)/shard_map/ppermute | solution.py:56
  19.8 1.8 %collective-permute-start.7 = (bf16[16,8192]{1,0:T(8,128)(2,1)S(1)}, bf16[16,8192]{1,0:T(8,128)(2,1)S(1)}, u32[]{:S(2)}, u32[]{:S(2)}) collective-permute-start(bf16[16,8192]{1,0:T(8,128)(2,1)S(1)} %collective-permute-done.1.refs_4_.refs_6_), channel_id=1, source_target_pairs={{0,192},{1,193},{2,194},{3,195},{4,196},{5,197},{6,198},{7,199},{8... | collective-permute-start | bytes 786440 | tf_op jit(solution)/shard_map/ppermute | solution.py:56
  22.6 1.9 %collective-permute-start.9 = (bf16[16,8192]{1,0:T(8,128)(2,1)S(1)}, bf16[16,8192]{1,0:T(8,128)(2,1)S(1)}, u32[]{:S(2)}, u32[]{:S(2)}) collective-permute-start(bf16[16,8192]{1,0:T(8,128)(2,1)S(1)} %collective-permute-done.2.refs_8_.refs_10_), channel_id=1, source_target_pairs={{0,48},{1,49},{2,50},{3,51},{4,52},{5,53},{6,54},{7,55},{8,56},{9,... | collective-permute-start | bytes 786440 | tf_op jit(solution)/shard_map/ppermute | solution.py:56
  24.4 3.2 %shifted_rows.5 = (bf16[256,8192]{1,0:T(8,128)(2,1)S(1)}, bf16[32,4096]{1,0:T(8,128)(2,1)S(1)}) custom-call(s32[1]{0:T(128)} %bitcast.1.member_ref.refs_0_, bf16[32,8576]{1,0:T(8,128)(2,1)S(1)} %collective-permute-done.x_ref, f32[4,8,1024]{2,1,0:T(8,128)S(1)} %get-tuple-element.54.geo_ref, bf16[256,8192]{1,0:T(8,128)(2,1)S(1)} %get-tuple-element.55.table_ref), custom_call_target="tpu_custom_call" | custom-call | tf_op jit(solution)/shard_map/shifted_rows/pallas_call | solution.py:104
  27.6 3.2 %shifted_rows.6 = (bf16[256,8192]{1,0:T(8,128)(2,1)S(1)}, bf16[32,4096]{1,0:T(8,128)(2,1)S(1)}) custom-call(s32[1]{0:T(128)} %bitcast.1.member_ref.refs_0_, bf16[32,8576]{1,0:T(8,128)(2,1)S(1)} %collective-permute-done.4.x_ref, f32[4,8,1024]{2,1,0:T(8,128)S(1)} %get-tuple-element.54.geo_ref, bf16[256,8192]{1,0:T(8,128)(2,1)S(1)} %get-tuple-element.55.table_ref), custom_call_target="tpu_custom_call" | custom-call | tf_op jit(solution)/shard_map/shifted_rows/pallas_call | solution.py:104
  30.8 1.7 %collective-permute-done.5.x_ref = bf16[32,8576]{1,0:T(8,128)(2,1)S(1)} collective-permute-done((bf16[32,8576]{1,0:T(8,128)(2,1)S(1)}, bf16[32,8576]{1,0:T(8,128)(2,1)S(1)}, u32[]{:S(2)}, u32[]{:S(2)}) %collective-permute-start.5) | collective-permute-done | bytes 548896 | tf_op jit(solution)/shard_map/ppermute | solution.py:56
  32.5 3.2 %shifted_rows.7 = (bf16[256,8192]{1,0:T(8,128)(2,1)S(1)}, bf16[32,4096]{1,0:T(8,128)(2,1)S(1)}) custom-call(s32[1]{0:T(128)} %bitcast.1.member_ref.refs_0_, bf16[32,8576]{1,0:T(8,128)(2,1)S(1)} %collective-permute-done.5.x_ref, f32[4,8,1024]{2,1,0:T(8,128)S(1)} %get-tuple-element.54.geo_ref, bf16[256,8192]{1,0:T(8,128)(2,1)S(1)} %get-tuple-element.55.table_ref), custom_call_target="tpu_custom_call" | custom-call | tf_op jit(solution)/shard_map/shifted_rows/pallas_call | solution.py:104
  35.7 1.6 %partial_scores.3 = (f32[256,128]{1,0:T(8,128)S(1)}, bf16[128,4096]{1,0:T(8,128)(2,1)S(1)}) custom-call(bf16[256,8192]{1,0:T(8,128)(2,1)S(1)} %get-tuple-element.62.refs_0_.refs_4_, bf16[32,4096]{1,0:T(8,128)(2,1)S(1)} %get-tuple-element.70.refs_1_, bf16[16,8192]{1,0:T(8,128)(2,1)S(1)} %own_references.1.refs_2_.refs_4_, ...), custom_call_target="tpu_custom_call" | custom-call | tf_op jit(solution)/shard_map/partial_scores/pallas_call | solution.py:104
  37.3 1.4 %collective-permute-start.10 = (f32[256,128]{1,0:T(8,128)S(1)}, f32[256,128]{1,0:T(8,128)S(1)}, u32[]{:S(2)}, u32[]{:S(2)}) collective-permute-start(f32[256,128]{1,0:T(8,128)S(1)} %get-tuple-element.74), channel_id=1, source_target_pairs={{0,2},{1,3},{2,0},{3,1},{4,6},{5,7},{6,4},{7,5},{8,10},{9,11},{10,... | collective-permute-start | bytes 393224 | tf_op jit(solution)/shard_map/ppermute | solution.py:56
  38.7 1.5 %partial_scores.4 = f32[256,128]{1,0:T(8,128)S(1)} custom-call(bf16[256,8192]{1,0:T(8,128)(2,1)S(1)} %get-tuple-element.66.refs_0_.refs_5_, bf16[32,4096]{1,0:T(8,128)(2,1)S(1)} %get-tuple-element.75.refs_1_, bf16[16,8192]{1,0:T(8,128)(2,1)S(1)} %own_references.1.refs_2_.refs_4_, bf16[16,8192]{1,0:T(8,128)(2,1)S(1)} %collective-permute-done.3.refs_3_.refs_5_, ...), custom_call_target="tpu_custom_call" | custom-call | tf_op jit(solution)/shard_map/partial_scores/pallas_call | solution.py:104
  40.3 2.7 %partial_scores.5 = (f32[256,128]{1,0:T(8,128)S(1)}, f32[256,128]{1,0:T(8,128)S(1)}) custom-call(bf16[256,8192]{1,0:T(8,128)(2,1)S(1)} %get-tuple-element.56.refs_0_.refs_2_, bf16[256,8192]{1,0:T(8,128)(2,1)S(1)} %get-tuple-element.60.refs_1_.refs_3_, bf16[32,4096]{1,0:T(8,128)(2,1)S(1)} %get-tuple-element.77.refs_2_, ...), custom_call_target="tpu_custom_call" | custom-call | tf_op jit(solution)/shard_map/partial_scores/pallas_call | solution.py:104
  44.1 2.0 %collective-permute-done.11.refs_2_ = f32[256,128]{1,0:T(8,128)S(1)} collective-permute-done((f32[256,128]{1,0:T(8,128)S(1)}, f32[256,128]{1,0:T(8,128)S(1)}, u32[]{:S(2)}, u32[]{:S(2)}) %collective-permute-start.11) | collective-permute-done | bytes 131104 | tf_op jit(solution)/shard_map/ppermute | solution.py:56
  48.4 3.1 %collective-permute-done.14.refs_8_ = bf16[128,256]{1,0:T(8,128)(2,1)S(1)} collective-permute-done((bf16[128,256]{1,0:T(8,128)(2,1)S(1)}, bf16[128,256]{1,0:T(8,128)(2,1)S(1)}, u32[]{:S(2)}, u32[]{:S(2)}) %collective-permute-start.14) | collective-permute-done | bytes 65568 | tf_op jit(solution)/shard_map/ppermute | solution.py:56
  52.0 1.9 %weighted_sums.3 = (bf16[64,2048]{1,0:T(8,128)(2,1)S(1)}, bf16[64,2048]{1,0:T(8,128)(2,1)S(1)}, bf16[64,2048]{1,0:T(8,128)(2,1)S(1)}, bf16[64,2048]{1,0:T(8,128)(2,1)S(1)}) custom-call(s32[1]{0:T(128)} %bitcast.1.member_ref.refs_0_, s32[1]{0:T(128)} %bitcast.2.x_ref.refs_1_, bf16[256,8192]{1,0:T(8,128)(2,1)S(1)} %get-tuple-element.56.refs_0_.refs_2_, ...), custom_call_target="tpu_custom_call" | custom-call | tf_op jit(solution)/shard_map/weighted_sums/pallas_call | solution.py:104
  53.9 2.2 %collective-permute-start.22 = (bf16[64,2048]{1,0:T(8,128)(2,1)S(1)}, bf16[64,2048]{1,0:T(8,128)(2,1)S(1)}, u32[]{:S(2)}, u32[]{:S(2)}) collective-permute-start(bf16[64,2048]{1,0:T(8,128)(2,1)S(1)} %get-tuple-element.90), channel_id=1, source_target_pairs={{0,16},{1,129},{2,18},{3,131},{4,20},{5,133},{6,22},{7,135},{8,24}... | collective-permute-start | bytes 786440 | tf_op jit(solution)/shard_map/ppermute | solution.py:56
  56.1 1.6 %collective-permute-start.23 = (bf16[64,2048]{1,0:T(8,128)(2,1)S(1)}, bf16[64,2048]{1,0:T(8,128)(2,1)S(1)}, u32[]{:S(2)}, u32[]{:S(2)}) collective-permute-start(bf16[64,2048]{1,0:T(8,128)(2,1)S(1)} %get-tuple-element.91), channel_id=1, source_target_pairs={{0,32},{1,65},{2,34},{3,67},{4,36},{5,69},{6,38},{7,71},{8,40},{9,... | collective-permute-start | bytes 786440 | tf_op jit(solution)/shard_map/ppermute | solution.py:56
  58.1 1.9 %weighted_sums.2 = (bf16[64,2048]{1,0:T(8,128)(2,1)S(1)}, bf16[64,2048]{1,0:T(8,128)(2,1)S(1)}, bf16[64,2048]{1,0:T(8,128)(2,1)S(1)}, bf16[64,2048]{1,0:T(8,128)(2,1)S(1)}) custom-call(s32[1]{0:T(128)} %bitcast.1.member_ref.refs_0_, s32[1]{0:T(128)} %bitcast.2.x_ref.refs_1_, bf16[256,8192]{1,0:T(8,128)(2,1)S(1)} %get-tuple-element.56.refs_0_.refs_2_, ...), custom_call_target="tpu_custom_call" | custom-call | tf_op jit(solution)/shard_map/weighted_sums/pallas_call | solution.py:104
  60.0 3.0 %collective-permute-start.16 = (bf16[64,2048]{1,0:T(8,128)(2,1)S(1)}, bf16[64,2048]{1,0:T(8,128)(2,1)S(1)}, u32[]{:S(2)}, u32[]{:S(2)}) collective-permute-start(bf16[64,2048]{1,0:T(8,128)(2,1)S(1)} %get-tuple-element.82), channel_id=1, source_target_pairs={{0,128},{1,17},{2,130},{3,19},{4,132},{5,21},{6,134},{7,23},{8,136... | collective-permute-start | bytes 786440 | tf_op jit(solution)/shard_map/ppermute | solution.py:56
  67.3 3.5 %collective-permute-start.25 = (bf16[16,2048]{1,0:T(8,128)(2,1)S(1)}, bf16[16,2048]{1,0:T(8,128)(2,1)S(1)}, u32[]{:S(2)}, u32[]{:S(2)}) collective-permute-start(bf16[16,2048]{1,0:T(8,128)(2,1)S(1)} %get-tuple-element.94), channel_id=1, source_target_pairs={{0,128},{1,17},{2,130},{3,19},{4,132},{5,21},{6,134},{7,23},{8,136... | collective-permute-start | bytes 196616 | tf_op jit(solution)/shard_map/ppermute | solution.py:56
  72.0 2.3 %collective-permute-start.19 = (bf16[16,2048]{1,0:T(8,128)(2,1)S(1)}, bf16[16,2048]{1,0:T(8,128)(2,1)S(1)}, u32[]{:S(2)}, u32[]{:S(2)}) collective-permute-start(bf16[16,2048]{1,0:T(8,128)(2,1)S(1)} %get-tuple-element.86), channel_id=1, source_target_pairs={{0,16},{1,129},{2,18},{3,131},{4,20},{5,133},{6,22},{7,135},{8,24}... | collective-permute-start | bytes 196616 | tf_op jit(solution)/shard_map/ppermute | solution.py:56
  74.3 2.1 %collective-permute-start.20 = (bf16[16,2048]{1,0:T(8,128)(2,1)S(1)}, bf16[16,2048]{1,0:T(8,128)(2,1)S(1)}, u32[]{:S(2)}, u32[]{:S(2)}) collective-permute-start(bf16[16,2048]{1,0:T(8,128)(2,1)S(1)} %get-tuple-element.87), channel_id=1, source_target_pairs={{0,32},{1,65},{2,34},{3,67},{4,36},{5,69},{6,38},{7,71},{8,40},{9,... | collective-permute-start | bytes 196616 | tf_op jit(solution)/shard_map/ppermute | solution.py:56
  77.9 1.5 %collective-permute-done.20.refs_2_ = bf16[16,2048]{1,0:T(8,128)(2,1)S(1)} collective-permute-done((bf16[16,2048]{1,0:T(8,128)(2,1)S(1)}, bf16[16,2048]{1,0:T(8,128)(2,1)S(1)}, u32[]{:S(2)}, u32[]{:S(2)}) %collective-permute-start.20) | collective-permute-done | bytes 65568 | tf_op jit(solution)/shard_map/ppermute | solution.py:56
  80.7 6.9 %collective-permute-start.28 = (bf16[16,1024]{1,0:T(8,128)(2,1)S(1)}, bf16[16,1024]{1,0:T(8,128)(2,1)S(1)}, u32[]{:S(2)}, u32[]{:S(2)}) collective-permute-start(bf16[16,1024]{1,0:T(8,128)(2,1)S(1)} %get-tuple-element.98), channel_id=1, source_target_pairs={{0,8},{1,9},{2,10},{3,11},{4,12},{5,13},{6,14},{7,15},{8,0},{9,1},... | collective-permute-start | bytes 98312 | tf_op jit(solution)/shard_map/ppermute | solution.py:56
  87.6 1.4 %collective-permute-start.29 = (bf16[16,1024]{1,0:T(8,128)(2,1)S(1)}, bf16[16,1024]{1,0:T(8,128)(2,1)S(1)}, u32[]{:S(2)}, u32[]{:S(2)}) collective-permute-start(bf16[16,1024]{1,0:T(8,128)(2,1)S(1)} %get-tuple-element.99), channel_id=1, source_target_pairs={{0,4},{1,5},{2,6},{3,7},{4,0},{5,1},{6,2},{7,3},{8,12},{9,13},{10,... | collective-permute-start | bytes 98312 | tf_op jit(solution)/shard_map/ppermute | solution.py:56
  89.6 2.9 %collective-permute-done.29 = bf16[16,1024]{1,0:T(8,128)(2,1)S(1)} collective-permute-done((bf16[16,1024]{1,0:T(8,128)(2,1)S(1)}, bf16[16,1024]{1,0:T(8,128)(2,1)S(1)}, u32[]{:S(2)}, u32[]{:S(2)}) %collective-permute-start.29) | collective-permute-done | bytes 32800 | tf_op jit(solution)/shard_map/ppermute | solution.py:56
  92.4 2.6 %collective-permute-done.30 = bf16[16,1024]{1,0:T(8,128)(2,1)S(1)} collective-permute-done((bf16[16,1024]{1,0:T(8,128)(2,1)S(1)}, bf16[16,1024]{1,0:T(8,128)(2,1)S(1)}, u32[]{:S(2)}, u32[]{:S(2)}) %collective-permute-start.30) | collective-permute-done | bytes 32800 | tf_op jit(solution)/shard_map/ppermute | solution.py:56
  (48 shorter events, 16.4 us)
Async XLA Ops:
  2.0 16.2 %collective-permute-start = (bf16[32,8576]{1,0:T(8,128)(2,1)S(1)}, bf16[32,8576]{1,0:T(8,128)(2,1)S(1)}, u32[]{:S(2)}, u32[]{:S(2)}) collective-permute-start(bf16[32,8576]{1,0:T(8,128)(2,1)S(1)} %get-tuple-element.57), channel_id=1, source_target_pairs={{0,1},{1,0},{2,3},{3,2},{4,5},{5,4},{6,7},{7,6},{8,9},{9,8},{10,11... | collective-permute-start | bytes 1646600 | tf_op jit(solution)/shard_map/ppermute | solution.py:56
  2.1 16.1 %collective-permute-start.4 = (bf16[32,8576]{1,0:T(8,128)(2,1)S(1)}, bf16[32,8576]{1,0:T(8,128)(2,1)S(1)}, u32[]{:S(2)}, u32[]{:S(2)}) collective-permute-start(bf16[32,8576]{1,0:T(8,128)(2,1)S(1)} %get-tuple-element.58.after), channel_id=1, source_target_pairs={{0,2},{1,3},{2,0},{3,1},{4,6},{5,7},{6,4},{7,5},{8,10},{9,11},{10,... | collective-permute-start | bytes 1646600 | tf_op jit(solution)/shard_map/ppermute | solution.py:56
  5.0 13.1 %collective-permute-start.1 = (bf16[16,8192]{1,0:T(8,128)(2,1)S(1)}, bf16[16,8192]{1,0:T(8,128)(2,1)S(1)}, u32[]{:S(2)}, u32[]{:S(2)}) collective-permute-start(bf16[16,8192]{1,0:T(8,128)(2,1)S(1)} %own_references.1.refs_2_.refs_4_), channel_id=1, source_target_pairs={{0,64},{1,65},{2,66},{3,67},{4,68},{5,69},{6,70},{7,71},{8,72},{9,... | collective-permute-start | bytes 786440 | tf_op jit(solution)/shard_map/ppermute | solution.py:56
  6.7 11.4 %collective-permute-start.2 = (bf16[16,8192]{1,0:T(8,128)(2,1)S(1)}, bf16[16,8192]{1,0:T(8,128)(2,1)S(1)}, u32[]{:S(2)}, u32[]{:S(2)}) collective-permute-start(bf16[16,8192]{1,0:T(8,128)(2,1)S(1)} %own_references.1.refs_2_.refs_4_), channel_id=1, source_target_pairs={{0,192},{1,193},{2,194},{3,195},{4,196},{5,197},{6,198},{7,199},{8... | collective-permute-start | bytes 786440 | tf_op jit(solution)/shard_map/ppermute | solution.py:56
  8.9 9.3 %collective-permute-start.3 = (bf16[16,8192]{1,0:T(8,128)(2,1)S(1)}, bf16[16,8192]{1,0:T(8,128)(2,1)S(1)}, u32[]{:S(2)}, u32[]{:S(2)}) collective-permute-start(bf16[16,8192]{1,0:T(8,128)(2,1)S(1)} %own_references.1.refs_2_.refs_4_), channel_id=1, source_target_pairs={{0,32},{1,33},{2,34},{3,35},{4,36},{5,37},{6,38},{7,39},{8,40},{9,... | collective-permute-start | bytes 786440 | tf_op jit(solution)/shard_map/ppermute | solution.py:56
  18.2 14.3 %collective-permute-start.5 = (bf16[32,8576]{1,0:T(8,128)(2,1)S(1)}, bf16[32,8576]{1,0:T(8,128)(2,1)S(1)}, u32[]{:S(2)}, u32[]{:S(2)}) collective-permute-start(bf16[32,8576]{1,0:T(8,128)(2,1)S(1)} %get-tuple-element.64), channel_id=1, source_target_pairs={{0,3},{1,2},{2,1},{3,0},{4,7},{5,6},{6,5},{7,4},{8,11},{9,10},{10,... | collective-permute-start | bytes 1646600 | tf_op jit(solution)/shard_map/ppermute | solution.py:56
  18.3 17.4 %collective-permute-start.6 = (bf16[16,8192]{1,0:T(8,128)(2,1)S(1)}, bf16[16,8192]{1,0:T(8,128)(2,1)S(1)}, u32[]{:S(2)}, u32[]{:S(2)}) collective-permute-start(bf16[16,8192]{1,0:T(8,128)(2,1)S(1)} %collective-permute-done.1.refs_4_.refs_6_), channel_id=1, source_target_pairs={{0,32},{1,33},{2,34},{3,35},{4,36},{5,37},{6,38},{7,39},{8,40},{9,... | collective-permute-start | bytes 786440 | tf_op jit(solution)/shard_map/ppermute | solution.py:56
  19.8 15.8 %collective-permute-start.7 = (bf16[16,8192]{1,0:T(8,128)(2,1)S(1)}, bf16[16,8192]{1,0:T(8,128)(2,1)S(1)}, u32[]{:S(2)}, u32[]{:S(2)}) collective-permute-start(bf16[16,8192]{1,0:T(8,128)(2,1)S(1)} %collective-permute-done.1.refs_4_.refs_6_), channel_id=1, source_target_pairs={{0,192},{1,193},{2,194},{3,195},{4,196},{5,197},{6,198},{7,199},{8... | collective-permute-start | bytes 786440 | tf_op jit(solution)/shard_map/ppermute | solution.py:56
  21.7 14.0 %collective-permute-start.8 = (bf16[16,8192]{1,0:T(8,128)(2,1)S(1)}, bf16[16,8192]{1,0:T(8,128)(2,1)S(1)}, u32[]{:S(2)}, u32[]{:S(2)}) collective-permute-start(bf16[16,8192]{1,0:T(8,128)(2,1)S(1)} %collective-permute-done.3.refs_3_.refs_5_), channel_id=1, source_target_pairs={{0,128},{1,129},{2,130},{3,131},{4,132},{5,133},{6,134},{7,135},{8... | collective-permute-start | bytes 786440 | tf_op jit(solution)/shard_map/ppermute | solution.py:56
  22.6 13.1 %collective-permute-start.9 = (bf16[16,8192]{1,0:T(8,128)(2,1)S(1)}, bf16[16,8192]{1,0:T(8,128)(2,1)S(1)}, u32[]{:S(2)}, u32[]{:S(2)}) collective-permute-start(bf16[16,8192]{1,0:T(8,128)(2,1)S(1)} %collective-permute-done.2.refs_8_.refs_10_), channel_id=1, source_target_pairs={{0,48},{1,49},{2,50},{3,51},{4,52},{5,53},{6,54},{7,55},{8,56},{9,... | collective-permute-start | bytes 786440 | tf_op jit(solution)/shard_map/ppermute | solution.py:56
  37.3 8.8 %collective-permute-start.10 = (f32[256,128]{1,0:T(8,128)S(1)}, f32[256,128]{1,0:T(8,128)S(1)}, u32[]{:S(2)}, u32[]{:S(2)}) collective-permute-start(f32[256,128]{1,0:T(8,128)S(1)} %get-tuple-element.74), channel_id=1, source_target_pairs={{0,2},{1,3},{2,0},{3,1},{4,6},{5,7},{6,4},{7,5},{8,10},{9,11},{10,... | collective-permute-start | bytes 393224 | tf_op jit(solution)/shard_map/ppermute | solution.py:56
  40.2 5.9 %collective-permute-start.11 = (f32[256,128]{1,0:T(8,128)S(1)}, f32[256,128]{1,0:T(8,128)S(1)}, u32[]{:S(2)}, u32[]{:S(2)}) collective-permute-start(f32[256,128]{1,0:T(8,128)S(1)} %partial_scores.4), channel_id=1, source_target_pairs={{0,3},{1,2},{2,1},{3,0},{4,7},{5,6},{6,5},{7,4},{8,11},{9,10},{10,... | collective-permute-start | bytes 393224 | tf_op jit(solution)/shard_map/ppermute | solution.py:56
  43.0 3.1 %collective-permute-start.12 = (f32[256,128]{1,0:T(8,128)S(1)}, f32[256,128]{1,0:T(8,128)S(1)}, u32[]{:S(2)}, u32[]{:S(2)}) collective-permute-start(f32[256,128]{1,0:T(8,128)S(1)} %get-tuple-element.80), channel_id=1, source_target_pairs={{0,1},{1,0},{2,3},{3,2},{4,5},{5,4},{6,7},{7,6},{8,9},{9,8},{10,11... | collective-permute-start | bytes 393224 | tf_op jit(solution)/shard_map/ppermute | solution.py:56
  46.4 2.0 %collective-permute-start.13 = (bf16[128,256]{1,0:T(8,128)(2,1)S(1)}, bf16[128,256]{1,0:T(8,128)(2,1)S(1)}, u32[]{:S(2)}, u32[]{:S(2)}) collective-permute-start(bf16[128,256]{1,0:T(8,128)(2,1)S(1)} %posterior.1.refs_6_), channel_id=1, source_target_pairs={{0,1},{1,0},{2,3},{3,2},{4,5},{5,4},{6,7},{7,6},{8,9},{9,8},{10,11... | collective-permute-start | bytes 196616 | tf_op jit(solution)/shard_map/ppermute | solution.py:56
  46.6 4.9 %collective-permute-start.14 = (bf16[128,256]{1,0:T(8,128)(2,1)S(1)}, bf16[128,256]{1,0:T(8,128)(2,1)S(1)}, u32[]{:S(2)}, u32[]{:S(2)}) collective-permute-start(bf16[128,256]{1,0:T(8,128)(2,1)S(1)} %posterior.1.refs_6_), channel_id=1, source_target_pairs={{0,2},{1,3},{2,0},{3,1},{4,6},{5,7},{6,4},{7,5},{8,10},{9,11},{10,... | collective-permute-start | bytes 196616 | tf_op jit(solution)/shard_map/ppermute | solution.py:56
  47.5 4.4 %collective-permute-start.15 = (bf16[128,256]{1,0:T(8,128)(2,1)S(1)}, bf16[128,256]{1,0:T(8,128)(2,1)S(1)}, u32[]{:S(2)}, u32[]{:S(2)}) collective-permute-start(bf16[128,256]{1,0:T(8,128)(2,1)S(1)} %posterior.1.refs_6_), channel_id=1, source_target_pairs={{0,3},{1,2},{2,1},{3,0},{4,7},{5,6},{6,5},{7,4},{8,11},{9,10},{10,... | collective-permute-start | bytes 196616 | tf_op jit(solution)/shard_map/ppermute | solution.py:56
  53.9 9.8 %collective-permute-start.22 = (bf16[64,2048]{1,0:T(8,128)(2,1)S(1)}, bf16[64,2048]{1,0:T(8,128)(2,1)S(1)}, u32[]{:S(2)}, u32[]{:S(2)}) collective-permute-start(bf16[64,2048]{1,0:T(8,128)(2,1)S(1)} %get-tuple-element.90), channel_id=1, source_target_pairs={{0,16},{1,129},{2,18},{3,131},{4,20},{5,133},{6,22},{7,135},{8,24}... | collective-permute-start | bytes 786440 | tf_op jit(solution)/shard_map/ppermute | solution.py:56
  56.1 9.9 %collective-permute-start.23 = (bf16[64,2048]{1,0:T(8,128)(2,1)S(1)}, bf16[64,2048]{1,0:T(8,128)(2,1)S(1)}, u32[]{:S(2)}, u32[]{:S(2)}) collective-permute-start(bf16[64,2048]{1,0:T(8,128)(2,1)S(1)} %get-tuple-element.91), channel_id=1, source_target_pairs={{0,32},{1,65},{2,34},{3,67},{4,36},{5,69},{6,38},{7,71},{8,40},{9,... | collective-permute-start | bytes 786440 | tf_op jit(solution)/shard_map/ppermute | solution.py:56
  57.7 9.5 %collective-permute-start.24 = (bf16[64,2048]{1,0:T(8,128)(2,1)S(1)}, bf16[64,2048]{1,0:T(8,128)(2,1)S(1)}, u32[]{:S(2)}, u32[]{:S(2)}) collective-permute-start(bf16[64,2048]{1,0:T(8,128)(2,1)S(1)} %get-tuple-element.92), channel_id=1, source_target_pairs={{0,48},{1,193},{2,50},{3,195},{4,52},{5,197},{6,54},{7,199},{8,56}... | collective-permute-start | bytes 786440 | tf_op jit(solution)/shard_map/ppermute | solution.py:56
  60.0 11.5 %collective-permute-start.16 = (bf16[64,2048]{1,0:T(8,128)(2,1)S(1)}, bf16[64,2048]{1,0:T(8,128)(2,1)S(1)}, u32[]{:S(2)}, u32[]{:S(2)}) collective-permute-start(bf16[64,2048]{1,0:T(8,128)(2,1)S(1)} %get-tuple-element.82), channel_id=1, source_target_pairs={{0,128},{1,17},{2,130},{3,19},{4,132},{5,21},{6,134},{7,23},{8,136... | collective-permute-start | bytes 786440 | tf_op jit(solution)/shard_map/ppermute | solution.py:56
  63.0 8.9 %collective-permute-start.17 = (bf16[64,2048]{1,0:T(8,128)(2,1)S(1)}, bf16[64,2048]{1,0:T(8,128)(2,1)S(1)}, u32[]{:S(2)}, u32[]{:S(2)}) collective-permute-start(bf16[64,2048]{1,0:T(8,128)(2,1)S(1)} %get-tuple-element.83), channel_id=1, source_target_pairs={{0,64},{1,33},{2,66},{3,35},{4,68},{5,37},{6,70},{7,39},{8,72},{9,... | collective-permute-start | bytes 786440 | tf_op jit(solution)/shard_map/ppermute | solution.py:56
  63.7 8.2 %collective-permute-start.18 = (bf16[64,2048]{1,0:T(8,128)(2,1)S(1)}, bf16[64,2048]{1,0:T(8,128)(2,1)S(1)}, u32[]{:S(2)}, u32[]{:S(2)}) collective-permute-start(bf16[64,2048]{1,0:T(8,128)(2,1)S(1)} %get-tuple-element.84), channel_id=1, source_target_pairs={{0,192},{1,49},{2,194},{3,51},{4,196},{5,53},{6,198},{7,55},{8,200... | collective-permute-start | bytes 786440 | tf_op jit(solution)/shard_map/ppermute | solution.py:56
  67.3 9.1 %collective-permute-start.25 = (bf16[16,2048]{1,0:T(8,128)(2,1)S(1)}, bf16[16,2048]{1,0:T(8,128)(2,1)S(1)}, u32[]{:S(2)}, u32[]{:S(2)}) collective-permute-start(bf16[16,2048]{1,0:T(8,128)(2,1)S(1)} %get-tuple-element.94), channel_id=1, source_target_pairs={{0,128},{1,17},{2,130},{3,19},{4,132},{5,21},{6,134},{7,23},{8,136... | collective-permute-start | bytes 196616 | tf_op jit(solution)/shard_map/ppermute | solution.py:56
  70.8 5.6 %collective-permute-start.26 = (bf16[16,2048]{1,0:T(8,128)(2,1)S(1)}, bf16[16,2048]{1,0:T(8,128)(2,1)S(1)}, u32[]{:S(2)}, u32[]{:S(2)}) collective-permute-start(bf16[16,2048]{1,0:T(8,128)(2,1)S(1)} %get-tuple-element.95), channel_id=1, source_target_pairs={{0,64},{1,33},{2,66},{3,35},{4,68},{5,37},{6,70},{7,39},{8,72},{9,... | collective-permute-start | bytes 196616 | tf_op jit(solution)/shard_map/ppermute | solution.py:56
  71.5 5.5 %collective-permute-start.27 = (bf16[16,2048]{1,0:T(8,128)(2,1)S(1)}, bf16[16,2048]{1,0:T(8,128)(2,1)S(1)}, u32[]{:S(2)}, u32[]{:S(2)}) collective-permute-start(bf16[16,2048]{1,0:T(8,128)(2,1)S(1)} %get-tuple-element.96), channel_id=1, source_target_pairs={{0,192},{1,49},{2,194},{3,51},{4,196},{5,53},{6,198},{7,55},{8,200... | collective-permute-start | bytes 196616 | tf_op jit(solution)/shard_map/ppermute | solution.py:56
  72.0 5.9 %collective-permute-start.19 = (bf16[16,2048]{1,0:T(8,128)(2,1)S(1)}, bf16[16,2048]{1,0:T(8,128)(2,1)S(1)}, u32[]{:S(2)}, u32[]{:S(2)}) collective-permute-start(bf16[16,2048]{1,0:T(8,128)(2,1)S(1)} %get-tuple-element.86), channel_id=1, source_target_pairs={{0,16},{1,129},{2,18},{3,131},{4,20},{5,133},{6,22},{7,135},{8,24}... | collective-permute-start | bytes 196616 | tf_op jit(solution)/shard_map/ppermute | solution.py:56
  74.3 5.0 %collective-permute-start.20 = (bf16[16,2048]{1,0:T(8,128)(2,1)S(1)}, bf16[16,2048]{1,0:T(8,128)(2,1)S(1)}, u32[]{:S(2)}, u32[]{:S(2)}) collective-permute-start(bf16[16,2048]{1,0:T(8,128)(2,1)S(1)} %get-tuple-element.87), channel_id=1, source_target_pairs={{0,32},{1,65},{2,34},{3,67},{4,36},{5,69},{6,38},{7,71},{8,40},{9,... | collective-permute-start | bytes 196616 | tf_op jit(solution)/shard_map/ppermute | solution.py:56
  76.4 4.3 %collective-permute-start.21 = (bf16[16,2048]{1,0:T(8,128)(2,1)S(1)}, bf16[16,2048]{1,0:T(8,128)(2,1)S(1)}, u32[]{:S(2)}, u32[]{:S(2)}) collective-permute-start(bf16[16,2048]{1,0:T(8,128)(2,1)S(1)} %get-tuple-element.88), channel_id=1, source_target_pairs={{0,48},{1,193},{2,50},{3,195},{4,52},{5,197},{6,54},{7,199},{8,56}... | collective-permute-start | bytes 196616 | tf_op jit(solution)/shard_map/ppermute | solution.py:56
  80.7 8.8 %collective-permute-start.28 = (bf16[16,1024]{1,0:T(8,128)(2,1)S(1)}, bf16[16,1024]{1,0:T(8,128)(2,1)S(1)}, u32[]{:S(2)}, u32[]{:S(2)}) collective-permute-start(bf16[16,1024]{1,0:T(8,128)(2,1)S(1)} %get-tuple-element.98), channel_id=1, source_target_pairs={{0,8},{1,9},{2,10},{3,11},{4,12},{5,13},{6,14},{7,15},{8,0},{9,1},... | collective-permute-start | bytes 98312 | tf_op jit(solution)/shard_map/ppermute | solution.py:56
  87.6 4.8 %collective-permute-start.29 = (bf16[16,1024]{1,0:T(8,128)(2,1)S(1)}, bf16[16,1024]{1,0:T(8,128)(2,1)S(1)}, u32[]{:S(2)}, u32[]{:S(2)}) collective-permute-start(bf16[16,1024]{1,0:T(8,128)(2,1)S(1)} %get-tuple-element.99), channel_id=1, source_target_pairs={{0,4},{1,5},{2,6},{3,7},{4,0},{5,1},{6,2},{7,3},{8,12},{9,13},{10,... | collective-permute-start | bytes 98312 | tf_op jit(solution)/shard_map/ppermute | solution.py:56
  89.1 6.0 %collective-permute-start.30 = (bf16[16,1024]{1,0:T(8,128)(2,1)S(1)}, bf16[16,1024]{1,0:T(8,128)(2,1)S(1)}, u32[]{:S(2)}, u32[]{:S(2)}) collective-permute-start(bf16[16,1024]{1,0:T(8,128)(2,1)S(1)} %get-tuple-element.100), channel_id=1, source_target_pairs={{0,12},{1,13},{2,14},{3,15},{4,8},{5,9},{6,10},{7,11},{8,4},{9,5},... | collective-permute-start | bytes 98312 | tf_op jit(solution)/shard_map/ppermute | solution.py:56

commit v12 on v11

--- a/solution.py
+++ b/solution.py
@@ -294,10 +294,14 @@
     )
 
 
+ARRIVAL = [(2, 1), (2, 0), (1, 1), (3, 1), (0, 1), (1, 0), (3, 0), (0, 0)]
+
+
 def scores_kernel(count, fresh, *refs):
     blocks = refs[2 * count : 2 * count + 8]
     outs = refs[2 * count + 8 :]
-    stacked = jnp.concatenate([block[...] for block in blocks], axis=0)
+    stacked = dict(zip(ARRIVAL, blocks))
+    stacked = jnp.concatenate([stacked[at][...] for at in sorted(ARRIVAL)], axis=0)
     if fresh:
         for block in range(NB):
             start = block * 2 * COLS
@@ -435,17 +439,17 @@
     table, geo = make_table(member, geo)
     rows[0], pens[0] = make_rows(member, chunks[0], geo, table)
     wave = [got[1], gathered[1, 0], gathered[3, 0], gathered[0, 1], rows[0]]
+    gathered[2, 1] = send(after(gathered[0, 1], *wave), flips(y=2))
+    gathered[2, 0] = send(after(gathered[1, 0], *wave), flips(y=3))
     gathered[1, 1] = send(after(gathered[1, 0], *wave), flips(x=1))
     gathered[3, 1] = send(after(gathered[3, 0], *wave), flips(x=3))
-    gathered[2, 1] = send(after(gathered[0, 1], *wave), flips(y=2))
-    gathered[2, 0] = send(after(gathered[1, 0], *wave), flips(y=3))
-    got[3] = send(after(chunks[3], *wave, got[2]), partners(3))
-    rows[1], pens[1] = make_rows(member, after(got[1], *wave, got[2]), geo, table)
-    rows[2], pens[2] = make_rows(member, after(got[2], rows[1]), geo, table)
-    rows[3], pens[3] = make_rows(member, after(got[3], rows[2]), geo, table)
-    blocks = [gathered[ky, kx] for ky in range(Y) for kx in range(2)]
-
-    second, power = make_scores([rows[2]], [after(pens[2], rows[3])], blocks)
+    got[3] = send(after(chunks[3], got[2], *wave), partners(3))
+    rows[2], pens[2] = make_rows(member, after(got[2], *wave), geo, table)
+    rows[1], pens[1] = make_rows(member, after(got[1], rows[2]), geo, table)
+    blocks = [gathered[at] for at in ARRIVAL]
+
+    second, power = make_scores([rows[2]], [after(pens[2], rows[1])], blocks)
+    rows[3], pens[3] = make_rows(member, after(got[3], second), geo, table)
     (third,) = make_scores([rows[3]], [after(pens[3], second)], blocks, power)
     mine, other = make_scores([rows[0], rows[1]], [after(pens[0], third), pens[1]], blocks, power)
     near = [mine, send(second, partners(2)), send(third, partners(3))]

time: 96 us -> 99.1 us (1.032)
  waiting for transfers between devices: 20 us -> 23.6 us
  starting transfers between devices: 43.4 us -> 42.1 us
    ppermute x31, waiting for transfers between devices: 20 us -> 23.6 us  [send(): return lax.ppermute(value, AXES, pairs)]
    ppermute x31, starting transfers between devices: 43.4 us -> 42.1 us  [send(): return lax.ppermute(value, AXES, pairs)]
  transfers between devices with their start and end apart: 31 -> 31, of which waited for: 13 -> 14; matrix products, arithmetic and copies ran while one was open for 0% -> 0% of each run, Pallas kernels for 27% -> 28%
where the time goes in v12:
time: 99.1 us; the launch traced here: 98 us
  starting transfers between devices  42.1 us (42%)
  Pallas kernels  31.4 us (32%)
  waiting for transfers between devices  23.6 us (24%)
    ppermute x31, starting transfers between devices, send(): return lax.ppermute(value, AXES, pairs)  42.1 us
    pallas_call x17, Pallas kernels, local(): pl.pallas_call(kernel, in_specs=[SCALARS] * len(scalars) + [PLACED] * pla...  31.4 us
    ppermute x31, waiting for transfers between devices, send(): return lax.ppermute(value, AXES, pairs)  23.6 us
  transfers between devices with their start and end apart: 31, of which 14 were waited for; matrix products, arithmetic and copies ran while one was open for 0% of the time, Pallas kernels for 28%

profile of v12, /device:TPU:2, one launch (start us, length us, event | category | flops | bytes accessed | tf_op | source)
XLA Modules:
  0.0 98.0 jit_solution(4870825688711686100)
XLA Ops:
  0.0 2.0 %split_particles.1 = (bf16[32,8576]{1,0:T(8,128)(2,1)S(1)}, bf16[32,8576]{1,0:T(8,128)(2,1)S(1)}, bf16[32,8576]{1,0:T(8,128)(2,1)S(1)}, bf16[32,8576]{1,0:T(8,128)(2,1)S(1)}) custom-call(s32[1]{0:T(128)} %bitcast.1.member_ref.refs_0_, s32[1]{0:T(128)} %bitcast.block_ref, s32[1]{0:T(128)} %bitcast.2.x_ref.refs_1_, bf16[32,32768]{1,0:T(8,128)(2,1)} %source.2, ...), custom_call_target="tpu_custom_call" | custom-call | tf_op jit(solution)/shard_map/split_particles/pallas_call | solution.py:104
  2.1 2.0 %collective-permute-start.1 = (bf16[32,8576]{1,0:T(8,128)(2,1)S(1)}, bf16[32,8576]{1,0:T(8,128)(2,1)S(1)}, u32[]{:S(2)}, u32[]{:S(2)}) collective-permute-start(bf16[32,8576]{1,0:T(8,128)(2,1)S(1)} %get-tuple-element.58.after), channel_id=1, source_target_pairs={{0,2},{1,3},{2,0},{3,1},{4,6},{5,7},{6,4},{7,5},{8,10},{9,11},{10,... | collective-permute-start | bytes 1646600 | tf_op jit(solution)/shard_map/ppermute | solution.py:56
  5.7 3.0 %collective-permute-start.3 = (bf16[16,8192]{1,0:T(8,128)(2,1)S(1)}, bf16[16,8192]{1,0:T(8,128)(2,1)S(1)}, u32[]{:S(2)}, u32[]{:S(2)}) collective-permute-start(bf16[16,8192]{1,0:T(8,128)(2,1)S(1)} %own_references.1.refs_9_.refs_11_), channel_id=1, source_target_pairs={{0,192},{1,193},{2,194},{3,195},{4,196},{5,197},{6,198},{7,199},{8... | collective-permute-start | bytes 786440 | tf_op jit(solution)/shard_map/ppermute | solution.py:56
  8.8 5.5 %phase_table.1 = (bf16[256,8192]{1,0:T(8,128)(2,1)S(1)}, f32[4,8,1024]{2,1,0:T(8,128)S(1)}) custom-call(s32[1]{0:T(128)} %bitcast.1.member_ref.refs_0_, f32[16,8,1024]{2,1,0:T(8,128)} %constant.63.clone.geo_ref), custom_call_target="tpu_custom_call" | custom-call | tf_op jit(solution)/shard_map/phase_table/pallas_call | solution.py:104
  14.3 3.2 %shifted_rows.4 = (bf16[256,8192]{1,0:T(8,128)(2,1)S(1)}, bf16[32,4096]{1,0:T(8,128)(2,1)S(1)}) custom-call(s32[1]{0:T(128)} %bitcast.1.member_ref.refs_0_, bf16[32,8576]{1,0:T(8,128)(2,1)S(1)} %get-tuple-element.53.x_ref, f32[4,8,1024]{2,1,0:T(8,128)S(1)} %get-tuple-element.54.geo_ref, bf16[256,8192]{1,0:T(8,128)(2,1)S(1)} %get-tuple-element.55.table_ref), custom_call_target="tpu_custom_call" | custom-call | tf_op jit(solution)/shard_map/shifted_rows/pallas_call | solution.py:104
  19.2 2.4 %collective-permute-start.7 = (bf16[16,8192]{1,0:T(8,128)(2,1)S(1)}, bf16[16,8192]{1,0:T(8,128)(2,1)S(1)}, u32[]{:S(2)}, u32[]{:S(2)}) collective-permute-start(bf16[16,8192]{1,0:T(8,128)(2,1)S(1)} %collective-permute-done.2.refs_7_.refs_9_), channel_id=1, source_target_pairs={{0,192},{1,193},{2,194},{3,195},{4,196},{5,197},{6,198},{7,199},{8... | collective-permute-start | bytes 786440 | tf_op jit(solution)/shard_map/ppermute | solution.py:56
  21.7 1.5 %collective-permute-start.6 = (bf16[16,8192]{1,0:T(8,128)(2,1)S(1)}, bf16[16,8192]{1,0:T(8,128)(2,1)S(1)}, u32[]{:S(2)}, u32[]{:S(2)}) collective-permute-start(bf16[16,8192]{1,0:T(8,128)(2,1)S(1)} %collective-permute-done.4.refs_6_.refs_8_), channel_id=1, source_target_pairs={{0,128},{1,129},{2,130},{3,131},{4,132},{5,133},{6,134},{7,135},{8... | collective-permute-start | bytes 786440 | tf_op jit(solution)/shard_map/ppermute | solution.py:56
  23.2 1.5 %collective-permute-start.9 = (bf16[16,8192]{1,0:T(8,128)(2,1)S(1)}, bf16[16,8192]{1,0:T(8,128)(2,1)S(1)}, u32[]{:S(2)}, u32[]{:S(2)}) collective-permute-start(bf16[16,8192]{1,0:T(8,128)(2,1)S(1)} %collective-permute-done.3.refs_8_.refs_10_), channel_id=1, source_target_pairs={{0,48},{1,49},{2,50},{3,51},{4,52},{5,53},{6,54},{7,55},{8,56},{9,... | collective-permute-start | bytes 786440 | tf_op jit(solution)/shard_map/ppermute | solution.py:56
  24.7 3.2 %shifted_rows.5 = (bf16[256,8192]{1,0:T(8,128)(2,1)S(1)}, bf16[32,4096]{1,0:T(8,128)(2,1)S(1)}) custom-call(s32[1]{0:T(128)} %bitcast.1.member_ref.refs_0_, bf16[32,8576]{1,0:T(8,128)(2,1)S(1)} %collective-permute-done.1.x_ref, f32[4,8,1024]{2,1,0:T(8,128)S(1)} %get-tuple-element.54.geo_ref, bf16[256,8192]{1,0:T(8,128)(2,1)S(1)} %get-tuple-element.55.table_ref), custom_call_target="tpu_custom_call" | custom-call | tf_op jit(solution)/shard_map/shifted_rows/pallas_call | solution.py:104
  27.9 3.2 %shifted_rows.6 = (bf16[256,8192]{1,0:T(8,128)(2,1)S(1)}, bf16[32,4096]{1,0:T(8,128)(2,1)S(1)}) custom-call(s32[1]{0:T(128)} %bitcast.1.member_ref.refs_0_, bf16[32,8576]{1,0:T(8,128)(2,1)S(1)} %collective-permute-done.x_ref, f32[4,8,1024]{2,1,0:T(8,128)S(1)} %get-tuple-element.54.geo_ref, bf16[256,8192]{1,0:T(8,128)(2,1)S(1)} %get-tuple-element.55.table_ref), custom_call_target="tpu_custom_call" | custom-call | tf_op jit(solution)/shard_map/shifted_rows/pallas_call | solution.py:104
  31.8 2.6 %collective-permute-done.7.refs_3_.refs_5_ = bf16[16,8192]{1,0:T(8,128)(2,1)S(1)} collective-permute-done((bf16[16,8192]{1,0:T(8,128)(2,1)S(1)}, bf16[16,8192]{1,0:T(8,128)(2,1)S(1)}, u32[]{:S(2)}, u32[]{:S(2)}) %collective-permute-start.7) | collective-permute-done | bytes 262176 | tf_op jit(solution)/shard_map/ppermute | solution.py:56
  34.4 1.6 %partial_scores.3 = (f32[256,128]{1,0:T(8,128)S(1)}, bf16[128,4096]{1,0:T(8,128)(2,1)S(1)}) custom-call(bf16[256,8192]{1,0:T(8,128)(2,1)S(1)} %get-tuple-element.60.refs_0_.refs_4_, bf16[32,4096]{1,0:T(8,128)(2,1)S(1)} %get-tuple-element.66.refs_1_, bf16[16,8192]{1,0:T(8,128)(2,1)S(1)} %collective-permute-done.6.refs_2_.refs_4_, ...), custom_call_target="tpu_custom_call" | custom-call | tf_op jit(solution)/shard_map/partial_scores/pallas_call | solution.py:104
  36.0 2.0 %collective-permute-start.10 = (f32[256,128]{1,0:T(8,128)S(1)}, f32[256,128]{1,0:T(8,128)S(1)}, u32[]{:S(2)}, u32[]{:S(2)}) collective-permute-start(f32[256,128]{1,0:T(8,128)S(1)} %get-tuple-element.70), channel_id=1, source_target_pairs={{0,2},{1,3},{2,0},{3,1},{4,6},{5,7},{6,4},{7,5},{8,10},{9,11},{10,... | collective-permute-start | bytes 393224 | tf_op jit(solution)/shard_map/ppermute | solution.py:56
  38.0 3.2 %shifted_rows.7 = (bf16[256,8192]{1,0:T(8,128)(2,1)S(1)}, bf16[32,4096]{1,0:T(8,128)(2,1)S(1)}) custom-call(s32[1]{0:T(128)} %bitcast.1.member_ref.refs_0_, bf16[32,8576]{1,0:T(8,128)(2,1)S(1)} %collective-permute-done.5.x_ref, f32[4,8,1024]{2,1,0:T(8,128)S(1)} %get-tuple-element.54.geo_ref, bf16[256,8192]{1,0:T(8,128)(2,1)S(1)} %get-tuple-element.55.table_ref), custom_call_target="tpu_custom_call" | custom-call | tf_op jit(solution)/shard_map/shifted_rows/pallas_call | solution.py:104
  41.2 1.5 %partial_scores.4 = f32[256,128]{1,0:T(8,128)S(1)} custom-call(bf16[256,8192]{1,0:T(8,128)(2,1)S(1)} %get-tuple-element.72.refs_0_.refs_5_, bf16[32,4096]{1,0:T(8,128)(2,1)S(1)} %get-tuple-element.75.refs_1_, bf16[16,8192]{1,0:T(8,128)(2,1)S(1)} %collective-permute-done.6.refs_2_.refs_4_, bf16[16,8192]{1,0:T(8,128)(2,1)S(1)} %collective-permute-done.7.refs_3_.refs_5_, ...), custom_call_target="tpu_custom_call" | custom-call | tf_op jit(solution)/shard_map/partial_scores/pallas_call | solution.py:104
  42.8 2.7 %partial_scores.5 = (f32[256,128]{1,0:T(8,128)S(1)}, f32[256,128]{1,0:T(8,128)S(1)}) custom-call(bf16[256,8192]{1,0:T(8,128)(2,1)S(1)} %get-tuple-element.56.refs_0_.refs_2_, bf16[256,8192]{1,0:T(8,128)(2,1)S(1)} %get-tuple-element.62.refs_1_.refs_3_, bf16[32,4096]{1,0:T(8,128)(2,1)S(1)} %get-tuple-element.77.refs_2_, ...), custom_call_target="tpu_custom_call" | custom-call | tf_op jit(solution)/shard_map/partial_scores/pallas_call | solution.py:104
  46.0 2.4 %collective-permute-done.11.refs_2_ = f32[256,128]{1,0:T(8,128)S(1)} collective-permute-done((f32[256,128]{1,0:T(8,128)S(1)}, f32[256,128]{1,0:T(8,128)S(1)}, u32[]{:S(2)}, u32[]{:S(2)}) %collective-permute-start.11) | collective-permute-done | bytes 131104 | tf_op jit(solution)/shard_map/ppermute | solution.py:56
  50.6 2.5 %collective-permute-done.15.refs_9_ = bf16[128,256]{1,0:T(8,128)(2,1)S(1)} collective-permute-done((bf16[128,256]{1,0:T(8,128)(2,1)S(1)}, bf16[128,256]{1,0:T(8,128)(2,1)S(1)}, u32[]{:S(2)}, u32[]{:S(2)}) %collective-permute-start.15) | collective-permute-done | bytes 65568 | tf_op jit(solution)/shard_map/ppermute | solution.py:56
  54.6 1.9 %weighted_sums.3 = (bf16[64,2048]{1,0:T(8,128)(2,1)S(1)}, bf16[64,2048]{1,0:T(8,128)(2,1)S(1)}, bf16[64,2048]{1,0:T(8,128)(2,1)S(1)}, bf16[64,2048]{1,0:T(8,128)(2,1)S(1)}) custom-call(s32[1]{0:T(128)} %bitcast.1.member_ref.refs_0_, s32[1]{0:T(128)} %bitcast.2.x_ref.refs_1_, bf16[256,8192]{1,0:T(8,128)(2,1)S(1)} %get-tuple-element.56.refs_0_.refs_2_, ...), custom_call_target="tpu_custom_call" | custom-call | tf_op jit(solution)/shard_map/weighted_sums/pallas_call | solution.py:104
  56.5 2.2 %collective-permute-start.22 = (bf16[64,2048]{1,0:T(8,128)(2,1)S(1)}, bf16[64,2048]{1,0:T(8,128)(2,1)S(1)}, u32[]{:S(2)}, u32[]{:S(2)}) collective-permute-start(bf16[64,2048]{1,0:T(8,128)(2,1)S(1)} %get-tuple-element.90), channel_id=1, source_target_pairs={{0,16},{1,129},{2,18},{3,131},{4,20},{5,133},{6,22},{7,135},{8,24}... | collective-permute-start | bytes 786440 | tf_op jit(solution)/shard_map/ppermute | solution.py:56
  60.7 1.9 %weighted_sums.2 = (bf16[64,2048]{1,0:T(8,128)(2,1)S(1)}, bf16[64,2048]{1,0:T(8,128)(2,1)S(1)}, bf16[64,2048]{1,0:T(8,128)(2,1)S(1)}, bf16[64,2048]{1,0:T(8,128)(2,1)S(1)}) custom-call(s32[1]{0:T(128)} %bitcast.1.member_ref.refs_0_, s32[1]{0:T(128)} %bitcast.2.x_ref.refs_1_, bf16[256,8192]{1,0:T(8,128)(2,1)S(1)} %get-tuple-element.56.refs_0_.refs_2_, ...), custom_call_target="tpu_custom_call" | custom-call | tf_op jit(solution)/shard_map/weighted_sums/pallas_call | solution.py:104
  63.7 1.5 %collective-permute-start.17 = (bf16[64,2048]{1,0:T(8,128)(2,1)S(1)}, bf16[64,2048]{1,0:T(8,128)(2,1)S(1)}, u32[]{:S(2)}, u32[]{:S(2)}) collective-permute-start(bf16[64,2048]{1,0:T(8,128)(2,1)S(1)} %get-tuple-element.83), channel_id=1, source_target_pairs={{0,64},{1,33},{2,66},{3,35},{4,68},{5,37},{6,70},{7,39},{8,72},{9,... | collective-permute-start | bytes 786440 | tf_op jit(solution)/shard_map/ppermute | solution.py:56
  65.2 1.6 %collective-permute-start.18 = (bf16[64,2048]{1,0:T(8,128)(2,1)S(1)}, bf16[64,2048]{1,0:T(8,128)(2,1)S(1)}, u32[]{:S(2)}, u32[]{:S(2)}) collective-permute-start(bf16[64,2048]{1,0:T(8,128)(2,1)S(1)} %get-tuple-element.84), channel_id=1, source_target_pairs={{0,192},{1,49},{2,194},{3,51},{4,196},{5,53},{6,198},{7,55},{8,200... | collective-permute-start | bytes 786440 | tf_op jit(solution)/shard_map/ppermute | solution.py:56
  66.8 1.9 %collective-permute-done.23.refs_4_ = bf16[64,2048]{1,0:T(8,128)(2,1)S(1)} collective-permute-done((bf16[64,2048]{1,0:T(8,128)(2,1)S(1)}, bf16[64,2048]{1,0:T(8,128)(2,1)S(1)}, u32[]{:S(2)}, u32[]{:S(2)}) %collective-permute-start.23) | collective-permute-done | bytes 262176 | tf_op jit(solution)/shard_map/ppermute | solution.py:56
  68.7 1.9 %collective-permute-done.24.refs_5_ = bf16[64,2048]{1,0:T(8,128)(2,1)S(1)} collective-permute-done((bf16[64,2048]{1,0:T(8,128)(2,1)S(1)}, bf16[64,2048]{1,0:T(8,128)(2,1)S(1)}, u32[]{:S(2)}, u32[]{:S(2)}) %collective-permute-start.24) | collective-permute-done | bytes 262176 | tf_op jit(solution)/shard_map/ppermute | solution.py:56
  71.8 1.9 %collective-permute-start.26 = (bf16[16,2048]{1,0:T(8,128)(2,1)S(1)}, bf16[16,2048]{1,0:T(8,128)(2,1)S(1)}, u32[]{:S(2)}, u32[]{:S(2)}) collective-permute-start(bf16[16,2048]{1,0:T(8,128)(2,1)S(1)} %get-tuple-element.95), channel_id=1, source_target_pairs={{0,64},{1,33},{2,66},{3,35},{4,68},{5,37},{6,70},{7,39},{8,72},{9,... | collective-permute-start | bytes 196616 | tf_op jit(solution)/shard_map/ppermute | solution.py:56
  75.0 2.5 %collective-permute-start.19 = (bf16[16,2048]{1,0:T(8,128)(2,1)S(1)}, bf16[16,2048]{1,0:T(8,128)(2,1)S(1)}, u32[]{:S(2)}, u32[]{:S(2)}) collective-permute-start(bf16[16,2048]{1,0:T(8,128)(2,1)S(1)} %get-tuple-element.86), channel_id=1, source_target_pairs={{0,16},{1,129},{2,18},{3,131},{4,20},{5,133},{6,22},{7,135},{8,24}... | collective-permute-start | bytes 196616 | tf_op jit(solution)/shard_map/ppermute | solution.py:56
  77.5 1.8 %collective-permute-start.20 = (bf16[16,2048]{1,0:T(8,128)(2,1)S(1)}, bf16[16,2048]{1,0:T(8,128)(2,1)S(1)}, u32[]{:S(2)}, u32[]{:S(2)}) collective-permute-start(bf16[16,2048]{1,0:T(8,128)(2,1)S(1)} %get-tuple-element.87), channel_id=1, source_target_pairs={{0,32},{1,65},{2,34},{3,67},{4,36},{5,69},{6,38},{7,71},{8,40},{9,... | collective-permute-start | bytes 196616 | tf_op jit(solution)/shard_map/ppermute | solution.py:56
  79.5 1.6 %collective-permute-done.19.refs_1_ = bf16[16,2048]{1,0:T(8,128)(2,1)S(1)} collective-permute-done((bf16[16,2048]{1,0:T(8,128)(2,1)S(1)}, bf16[16,2048]{1,0:T(8,128)(2,1)S(1)}, u32[]{:S(2)}, u32[]{:S(2)}) %collective-permute-start.19) | collective-permute-done | bytes 65568 | tf_op jit(solution)/shard_map/ppermute | solution.py:56
  83.7 6.2 %collective-permute-start.28 = (bf16[16,1024]{1,0:T(8,128)(2,1)S(1)}, bf16[16,1024]{1,0:T(8,128)(2,1)S(1)}, u32[]{:S(2)}, u32[]{:S(2)}) collective-permute-start(bf16[16,1024]{1,0:T(8,128)(2,1)S(1)} %get-tuple-element.98), channel_id=1, source_target_pairs={{0,8},{1,9},{2,10},{3,11},{4,12},{5,13},{6,14},{7,15},{8,0},{9,1},... | collective-permute-start | bytes 98312 | tf_op jit(solution)/shard_map/ppermute | solution.py:56
  91.8 2.9 %collective-permute-done.29 = bf16[16,1024]{1,0:T(8,128)(2,1)S(1)} collective-permute-done((bf16[16,1024]{1,0:T(8,128)(2,1)S(1)}, bf16[16,1024]{1,0:T(8,128)(2,1)S(1)}, u32[]{:S(2)}, u32[]{:S(2)}) %collective-permute-start.29) | collective-permute-done | bytes 32800 | tf_op jit(solution)/shard_map/ppermute | solution.py:56
  94.7 2.7 %collective-permute-done.30 = bf16[16,1024]{1,0:T(8,128)(2,1)S(1)} collective-permute-done((bf16[16,1024]{1,0:T(8,128)(2,1)S(1)}, bf16[16,1024]{1,0:T(8,128)(2,1)S(1)}, u32[]{:S(2)}, u32[]{:S(2)}) %collective-permute-start.30) | collective-permute-done | bytes 32800 | tf_op jit(solution)/shard_map/ppermute | solution.py:56
  (48 shorter events, 19.3 us)
Async XLA Ops:
  2.0 15.6 %collective-permute-start = (bf16[32,8576]{1,0:T(8,128)(2,1)S(1)}, bf16[32,8576]{1,0:T(8,128)(2,1)S(1)}, u32[]{:S(2)}, u32[]{:S(2)}) collective-permute-start(bf16[32,8576]{1,0:T(8,128)(2,1)S(1)} %get-tuple-element.57), channel_id=1, source_target_pairs={{0,1},{1,0},{2,3},{3,2},{4,5},{5,4},{6,7},{7,6},{8,9},{9,8},{10,11... | collective-permute-start | bytes 1646600 | tf_op jit(solution)/shard_map/ppermute | solution.py:56
  2.1 15.5 %collective-permute-start.1 = (bf16[32,8576]{1,0:T(8,128)(2,1)S(1)}, bf16[32,8576]{1,0:T(8,128)(2,1)S(1)}, u32[]{:S(2)}, u32[]{:S(2)}) collective-permute-start(bf16[32,8576]{1,0:T(8,128)(2,1)S(1)} %get-tuple-element.58.after), channel_id=1, source_target_pairs={{0,2},{1,3},{2,0},{3,1},{4,6},{5,7},{6,4},{7,5},{8,10},{9,11},{10,... | collective-permute-start | bytes 1646600 | tf_op jit(solution)/shard_map/ppermute | solution.py:56
  5.0 12.5 %collective-permute-start.4 = (bf16[16,8192]{1,0:T(8,128)(2,1)S(1)}, bf16[16,8192]{1,0:T(8,128)(2,1)S(1)}, u32[]{:S(2)}, u32[]{:S(2)}) collective-permute-start(bf16[16,8192]{1,0:T(8,128)(2,1)S(1)} %own_references.1.refs_9_.refs_11_), channel_id=1, source_target_pairs={{0,32},{1,33},{2,34},{3,35},{4,36},{5,37},{6,38},{7,39},{8,40},{9,... | collective-permute-start | bytes 786440 | tf_op jit(solution)/shard_map/ppermute | solution.py:56
  5.7 11.9 %collective-permute-start.3 = (bf16[16,8192]{1,0:T(8,128)(2,1)S(1)}, bf16[16,8192]{1,0:T(8,128)(2,1)S(1)}, u32[]{:S(2)}, u32[]{:S(2)}) collective-permute-start(bf16[16,8192]{1,0:T(8,128)(2,1)S(1)} %own_references.1.refs_9_.refs_11_), channel_id=1, source_target_pairs={{0,192},{1,193},{2,194},{3,195},{4,196},{5,197},{6,198},{7,199},{8... | collective-permute-start | bytes 786440 | tf_op jit(solution)/shard_map/ppermute | solution.py:56
  8.7 8.9 %collective-permute-start.2 = (bf16[16,8192]{1,0:T(8,128)(2,1)S(1)}, bf16[16,8192]{1,0:T(8,128)(2,1)S(1)}, u32[]{:S(2)}, u32[]{:S(2)}) collective-permute-start(bf16[16,8192]{1,0:T(8,128)(2,1)S(1)} %own_references.1.refs_9_.refs_11_), channel_id=1, source_target_pairs={{0,64},{1,65},{2,66},{3,67},{4,68},{5,69},{6,70},{7,71},{8,72},{9,... | collective-permute-start | bytes 786440 | tf_op jit(solution)/shard_map/ppermute | solution.py:56
  17.6 20.5 %collective-permute-start.5 = (bf16[32,8576]{1,0:T(8,128)(2,1)S(1)}, bf16[32,8576]{1,0:T(8,128)(2,1)S(1)}, u32[]{:S(2)}, u32[]{:S(2)}) collective-permute-start(bf16[32,8576]{1,0:T(8,128)(2,1)S(1)} %get-tuple-element.64), channel_id=1, source_target_pairs={{0,3},{1,2},{2,1},{3,0},{4,7},{5,6},{6,5},{7,4},{8,11},{9,10},{10,... | collective-permute-start | bytes 1646600 | tf_op jit(solution)/shard_map/ppermute | solution.py:56
  18.1 13.7 %collective-permute-start.8 = (bf16[16,8192]{1,0:T(8,128)(2,1)S(1)}, bf16[16,8192]{1,0:T(8,128)(2,1)S(1)}, u32[]{:S(2)}, u32[]{:S(2)}) collective-permute-start(bf16[16,8192]{1,0:T(8,128)(2,1)S(1)} %collective-permute-done.2.refs_7_.refs_9_), channel_id=1, source_target_pairs={{0,32},{1,33},{2,34},{3,35},{4,36},{5,37},{6,38},{7,39},{8,40},{9,... | collective-permute-start | bytes 786440 | tf_op jit(solution)/shard_map/ppermute | solution.py:56
  19.2 15.1 %collective-permute-start.7 = (bf16[16,8192]{1,0:T(8,128)(2,1)S(1)}, bf16[16,8192]{1,0:T(8,128)(2,1)S(1)}, u32[]{:S(2)}, u32[]{:S(2)}) collective-permute-start(bf16[16,8192]{1,0:T(8,128)(2,1)S(1)} %collective-permute-done.2.refs_7_.refs_9_), channel_id=1, source_target_pairs={{0,192},{1,193},{2,194},{3,195},{4,196},{5,197},{6,198},{7,199},{8... | collective-permute-start | bytes 786440 | tf_op jit(solution)/shard_map/ppermute | solution.py:56
  21.7 10.1 %collective-permute-start.6 = (bf16[16,8192]{1,0:T(8,128)(2,1)S(1)}, bf16[16,8192]{1,0:T(8,128)(2,1)S(1)}, u32[]{:S(2)}, u32[]{:S(2)}) collective-permute-start(bf16[16,8192]{1,0:T(8,128)(2,1)S(1)} %collective-permute-done.4.refs_6_.refs_8_), channel_id=1, source_target_pairs={{0,128},{1,129},{2,130},{3,131},{4,132},{5,133},{6,134},{7,135},{8... | collective-permute-start | bytes 786440 | tf_op jit(solution)/shard_map/ppermute | solution.py:56
  23.2 11.2 %collective-permute-start.9 = (bf16[16,8192]{1,0:T(8,128)(2,1)S(1)}, bf16[16,8192]{1,0:T(8,128)(2,1)S(1)}, u32[]{:S(2)}, u32[]{:S(2)}) collective-permute-start(bf16[16,8192]{1,0:T(8,128)(2,1)S(1)} %collective-permute-done.3.refs_8_.refs_10_), channel_id=1, source_target_pairs={{0,48},{1,49},{2,50},{3,51},{4,52},{5,53},{6,54},{7,55},{8,56},{9,... | collective-permute-start | bytes 786440 | tf_op jit(solution)/shard_map/ppermute | solution.py:56
  36.0 10.0 %collective-permute-start.10 = (f32[256,128]{1,0:T(8,128)S(1)}, f32[256,128]{1,0:T(8,128)S(1)}, u32[]{:S(2)}, u32[]{:S(2)}) collective-permute-start(f32[256,128]{1,0:T(8,128)S(1)} %get-tuple-element.70), channel_id=1, source_target_pairs={{0,2},{1,3},{2,0},{3,1},{4,6},{5,7},{6,4},{7,5},{8,10},{9,11},{10,... | collective-permute-start | bytes 393224 | tf_op jit(solution)/shard_map/ppermute | solution.py:56
  42.7 5.6 %collective-permute-start.11 = (f32[256,128]{1,0:T(8,128)S(1)}, f32[256,128]{1,0:T(8,128)S(1)}, u32[]{:S(2)}, u32[]{:S(2)}) collective-permute-start(f32[256,128]{1,0:T(8,128)S(1)} %partial_scores.4), channel_id=1, source_target_pairs={{0,3},{1,2},{2,1},{3,0},{4,7},{5,6},{6,5},{7,4},{8,11},{9,10},{10,... | collective-permute-start | bytes 393224 | tf_op jit(solution)/shard_map/ppermute | solution.py:56
  45.5 2.9 %collective-permute-start.12 = (f32[256,128]{1,0:T(8,128)S(1)}, f32[256,128]{1,0:T(8,128)S(1)}, u32[]{:S(2)}, u32[]{:S(2)}) collective-permute-start(f32[256,128]{1,0:T(8,128)S(1)} %get-tuple-element.80), channel_id=1, source_target_pairs={{0,1},{1,0},{2,3},{3,2},{4,5},{5,4},{6,7},{7,6},{8,9},{9,8},{10,11... | collective-permute-start | bytes 393224 | tf_op jit(solution)/shard_map/ppermute | solution.py:56
  48.7 4.5 %collective-permute-start.15 = (bf16[128,256]{1,0:T(8,128)(2,1)S(1)}, bf16[128,256]{1,0:T(8,128)(2,1)S(1)}, u32[]{:S(2)}, u32[]{:S(2)}) collective-permute-start(bf16[128,256]{1,0:T(8,128)(2,1)S(1)} %posterior.1.refs_6_), channel_id=1, source_target_pairs={{0,3},{1,2},{2,1},{3,0},{4,7},{5,6},{6,5},{7,4},{8,11},{9,10},{10,... | collective-permute-start | bytes 196616 | tf_op jit(solution)/shard_map/ppermute | solution.py:56
  49.1 5.5 %collective-permute-start.14 = (bf16[128,256]{1,0:T(8,128)(2,1)S(1)}, bf16[128,256]{1,0:T(8,128)(2,1)S(1)}, u32[]{:S(2)}, u32[]{:S(2)}) collective-permute-start(bf16[128,256]{1,0:T(8,128)(2,1)S(1)} %posterior.1.refs_6_), channel_id=1, source_target_pairs={{0,2},{1,3},{2,0},{3,1},{4,6},{5,7},{6,4},{7,5},{8,10},{9,11},{10,... | collective-permute-start | bytes 196616 | tf_op jit(solution)/shard_map/ppermute | solution.py:56
  50.2 4.3 %collective-permute-start.13 = (bf16[128,256]{1,0:T(8,128)(2,1)S(1)}, bf16[128,256]{1,0:T(8,128)(2,1)S(1)}, u32[]{:S(2)}, u32[]{:S(2)}) collective-permute-start(bf16[128,256]{1,0:T(8,128)(2,1)S(1)} %posterior.1.refs_6_), channel_id=1, source_target_pairs={{0,1},{1,0},{2,3},{3,2},{4,5},{5,4},{6,7},{7,6},{8,9},{9,8},{10,11... | collective-permute-start | bytes 196616 | tf_op jit(solution)/shard_map/ppermute | solution.py:56
  56.5 8.7 %collective-permute-start.22 = (bf16[64,2048]{1,0:T(8,128)(2,1)S(1)}, bf16[64,2048]{1,0:T(8,128)(2,1)S(1)}, u32[]{:S(2)}, u32[]{:S(2)}) collective-permute-start(bf16[64,2048]{1,0:T(8,128)(2,1)S(1)} %get-tuple-element.90), channel_id=1, source_target_pairs={{0,16},{1,129},{2,18},{3,131},{4,20},{5,133},{6,22},{7,135},{8,24}... | collective-permute-start | bytes 786440 | tf_op jit(solution)/shard_map/ppermute | solution.py:56
  58.7 9.9 %collective-permute-start.23 = (bf16[64,2048]{1,0:T(8,128)(2,1)S(1)}, bf16[64,2048]{1,0:T(8,128)(2,1)S(1)}, u32[]{:S(2)}, u32[]{:S(2)}) collective-permute-start(bf16[64,2048]{1,0:T(8,128)(2,1)S(1)} %get-tuple-element.91), channel_id=1, source_target_pairs={{0,32},{1,65},{2,34},{3,67},{4,36},{5,69},{6,38},{7,71},{8,40},{9,... | collective-permute-start | bytes 786440 | tf_op jit(solution)/shard_map/ppermute | solution.py:56
  60.2 10.4 %collective-permute-start.24 = (bf16[64,2048]{1,0:T(8,128)(2,1)S(1)}, bf16[64,2048]{1,0:T(8,128)(2,1)S(1)}, u32[]{:S(2)}, u32[]{:S(2)}) collective-permute-start(bf16[64,2048]{1,0:T(8,128)(2,1)S(1)} %get-tuple-element.92), channel_id=1, source_target_pairs={{0,48},{1,193},{2,50},{3,195},{4,52},{5,197},{6,54},{7,199},{8,56}... | collective-permute-start | bytes 786440 | tf_op jit(solution)/shard_map/ppermute | solution.py:56
  62.6 11.1 %collective-permute-start.16 = (bf16[64,2048]{1,0:T(8,128)(2,1)S(1)}, bf16[64,2048]{1,0:T(8,128)(2,1)S(1)}, u32[]{:S(2)}, u32[]{:S(2)}) collective-permute-start(bf16[64,2048]{1,0:T(8,128)(2,1)S(1)} %get-tuple-element.82), channel_id=1, source_target_pairs={{0,128},{1,17},{2,130},{3,19},{4,132},{5,21},{6,134},{7,23},{8,136... | collective-permute-start | bytes 786440 | tf_op jit(solution)/shard_map/ppermute | solution.py:56
  63.7 11.2 %collective-permute-start.17 = (bf16[64,2048]{1,0:T(8,128)(2,1)S(1)}, bf16[64,2048]{1,0:T(8,128)(2,1)S(1)}, u32[]{:S(2)}, u32[]{:S(2)}) collective-permute-start(bf16[64,2048]{1,0:T(8,128)(2,1)S(1)} %get-tuple-element.83), channel_id=1, source_target_pairs={{0,64},{1,33},{2,66},{3,35},{4,68},{5,37},{6,70},{7,39},{8,72},{9,... | collective-permute-start | bytes 786440 | tf_op jit(solution)/shard_map/ppermute | solution.py:56
  65.2 9.7 %collective-permute-start.18 = (bf16[64,2048]{1,0:T(8,128)(2,1)S(1)}, bf16[64,2048]{1,0:T(8,128)(2,1)S(1)}, u32[]{:S(2)}, u32[]{:S(2)}) collective-permute-start(bf16[64,2048]{1,0:T(8,128)(2,1)S(1)} %get-tuple-element.84), channel_id=1, source_target_pairs={{0,192},{1,49},{2,194},{3,51},{4,196},{5,53},{6,198},{7,55},{8,200... | collective-permute-start | bytes 786440 | tf_op jit(solution)/shard_map/ppermute | solution.py:56
  70.7 8.7 %collective-permute-start.25 = (bf16[16,2048]{1,0:T(8,128)(2,1)S(1)}, bf16[16,2048]{1,0:T(8,128)(2,1)S(1)}, u32[]{:S(2)}, u32[]{:S(2)}) collective-permute-start(bf16[16,2048]{1,0:T(8,128)(2,1)S(1)} %get-tuple-element.94), channel_id=1, source_target_pairs={{0,128},{1,17},{2,130},{3,19},{4,132},{5,21},{6,134},{7,23},{8,136... | collective-permute-start | bytes 196616 | tf_op jit(solution)/shard_map/ppermute | solution.py:56
  71.8 7.6 %collective-permute-start.26 = (bf16[16,2048]{1,0:T(8,128)(2,1)S(1)}, bf16[16,2048]{1,0:T(8,128)(2,1)S(1)}, u32[]{:S(2)}, u32[]{:S(2)}) collective-permute-start(bf16[16,2048]{1,0:T(8,128)(2,1)S(1)} %get-tuple-element.95), channel_id=1, source_target_pairs={{0,64},{1,33},{2,66},{3,35},{4,68},{5,37},{6,70},{7,39},{8,72},{9,... | collective-permute-start | bytes 196616 | tf_op jit(solution)/shard_map/ppermute | solution.py:56
  73.7 5.8 %collective-permute-start.27 = (bf16[16,2048]{1,0:T(8,128)(2,1)S(1)}, bf16[16,2048]{1,0:T(8,128)(2,1)S(1)}, u32[]{:S(2)}, u32[]{:S(2)}) collective-permute-start(bf16[16,2048]{1,0:T(8,128)(2,1)S(1)} %get-tuple-element.96), channel_id=1, source_target_pairs={{0,192},{1,49},{2,194},{3,51},{4,196},{5,53},{6,198},{7,55},{8,200... | collective-permute-start | bytes 196616 | tf_op jit(solution)/shard_map/ppermute | solution.py:56
  75.0 6.1 %collective-permute-start.19 = (bf16[16,2048]{1,0:T(8,128)(2,1)S(1)}, bf16[16,2048]{1,0:T(8,128)(2,1)S(1)}, u32[]{:S(2)}, u32[]{:S(2)}) collective-permute-start(bf16[16,2048]{1,0:T(8,128)(2,1)S(1)} %get-tuple-element.86), channel_id=1, source_target_pairs={{0,16},{1,129},{2,18},{3,131},{4,20},{5,133},{6,22},{7,135},{8,24}... | collective-permute-start | bytes 196616 | tf_op jit(solution)/shard_map/ppermute | solution.py:56
  77.5 4.8 %collective-permute-start.20 = (bf16[16,2048]{1,0:T(8,128)(2,1)S(1)}, bf16[16,2048]{1,0:T(8,128)(2,1)S(1)}, u32[]{:S(2)}, u32[]{:S(2)}) collective-permute-start(bf16[16,2048]{1,0:T(8,128)(2,1)S(1)} %get-tuple-element.87), channel_id=1, source_target_pairs={{0,32},{1,65},{2,34},{3,67},{4,36},{5,69},{6,38},{7,71},{8,40},{9,... | collective-permute-start | bytes 196616 | tf_op jit(solution)/shard_map/ppermute | solution.py:56
  79.4 4.3 %collective-permute-start.21 = (bf16[16,2048]{1,0:T(8,128)(2,1)S(1)}, bf16[16,2048]{1,0:T(8,128)(2,1)S(1)}, u32[]{:S(2)}, u32[]{:S(2)}) collective-permute-start(bf16[16,2048]{1,0:T(8,128)(2,1)S(1)} %get-tuple-element.88), channel_id=1, source_target_pairs={{0,48},{1,193},{2,50},{3,195},{4,52},{5,197},{6,54},{7,199},{8,56}... | collective-permute-start | bytes 196616 | tf_op jit(solution)/shard_map/ppermute | solution.py:56
  83.7 8.1 %collective-permute-start.28 = (bf16[16,1024]{1,0:T(8,128)(2,1)S(1)}, bf16[16,1024]{1,0:T(8,128)(2,1)S(1)}, u32[]{:S(2)}, u32[]{:S(2)}) collective-permute-start(bf16[16,1024]{1,0:T(8,128)(2,1)S(1)} %get-tuple-element.98), channel_id=1, source_target_pairs={{0,8},{1,9},{2,10},{3,11},{4,12},{5,13},{6,14},{7,15},{8,0},{9,1},... | collective-permute-start | bytes 98312 | tf_op jit(solution)/shard_map/ppermute | solution.py:56
  89.9 4.8 %collective-permute-start.29 = (bf16[16,1024]{1,0:T(8,128)(2,1)S(1)}, bf16[16,1024]{1,0:T(8,128)(2,1)S(1)}, u32[]{:S(2)}, u32[]{:S(2)}) collective-permute-start(bf16[16,1024]{1,0:T(8,128)(2,1)S(1)} %get-tuple-element.99), channel_id=1, source_target_pairs={{0,4},{1,5},{2,6},{3,7},{4,0},{5,1},{6,2},{7,3},{8,12},{9,13},{10,... | collective-permute-start | bytes 98312 | tf_op jit(solution)/shard_map/ppermute | solution.py:56
  91.4 6.0 %collective-permute-start.30 = (bf16[16,1024]{1,0:T(8,128)(2,1)S(1)}, bf16[16,1024]{1,0:T(8,128)(2,1)S(1)}, u32[]{:S(2)}, u32[]{:S(2)}) collective-permute-start(bf16[16,1024]{1,0:T(8,128)(2,1)S(1)} %get-tuple-element.100), channel_id=1, source_target_pairs={{0,12},{1,13},{2,14},{3,15},{4,8},{5,9},{6,10},{7,11},{8,4},{9,5},... | collective-permute-start | bytes 98312 | tf_op jit(solution)/shard_map/ppermute | solution.py:56

commit v13 on v12

--- a/solution.py
+++ b/solution.py
@@ -41,6 +41,13 @@
 def crossed(n, core):
     return [
         (linear(i, j, k, c), linear(i ^ (n if c == core else 0), j ^ (0 if c == core else n), k, c))
+        for i in range(Y) for j in range(X) for k in range(Z) for c in range(2)
+    ]
+
+
+def second_hop():
+    return [
+        (linear(i, j, k, c), linear(i ^ (1 if c else 3), j, k, c))
         for i in range(Y) for j in range(X) for k in range(Z) for c in range(2)
     ]
 
@@ -187,6 +194,21 @@
         placed=1, scratch=[pltpu.SemaphoreType.DMA((2 * NB,))],
     )
     return own
+
+
+def relay_kernel(member_ref, one, other, out):
+    @pl.when(member_ref[0] & 1 == 0)
+    def _():
+        out[...] = one[...]
+
+    @pl.when(member_ref[0] & 1 == 1)
+    def _():
+        out[...] = other[...]
+
+
+def pair_kernel(one, other, out):
+    out[16:32] = one[...]
+    out[0:16] = other[...]
 
 
 def parts_of(values):
@@ -294,12 +316,12 @@
     )
 
 
-ARRIVAL = [(2, 1), (2, 0), (1, 1), (3, 1), (0, 1), (1, 0), (3, 0), (0, 0)]
+ARRIVAL = [(2, 0), (1, 1), (3, 1), (0, 1), (1, 0), (3, 0), (0, 0)]
 
 
 def scores_kernel(count, fresh, *refs):
-    blocks = refs[2 * count : 2 * count + 8]
-    outs = refs[2 * count + 8 :]
+    blocks = refs[2 * count : 2 * count + 7]
+    outs = refs[2 * count + 7 :]
     stacked = dict(zip(ARRIVAL, blocks))
     stacked = jnp.concatenate([stacked[at][...] for at in sorted(ARRIVAL)], axis=0)
     if fresh:
@@ -440,12 +462,16 @@
     rows[0], pens[0] = make_rows(member, chunks[0], geo, table)
     wave = [got[1], gathered[1, 0], gathered[3, 0], gathered[0, 1], rows[0]]
     gathered[2, 1] = send(after(gathered[0, 1], *wave), flips(y=2))
-    gathered[2, 0] = send(after(gathered[1, 0], *wave), flips(y=3))
-    gathered[1, 1] = send(after(gathered[1, 0], *wave), flips(x=1))
-    gathered[3, 1] = send(after(gathered[3, 0], *wave), flips(x=3))
+    relayed = [gathered[1, 0], after(gathered[3, 0], *wave)]
+    (relay,) = local(relay_kernel, "relay", [((16, WIDTH), BF16)], [member], relayed, 2)
+    gathered[2, 0] = send(relay, second_hop())
+    gathered[1, 1] = send(after(gathered[1, 0], relay), flips(x=1))
+    gathered[3, 1] = send(after(gathered[3, 0], relay), flips(x=3))
     got[3] = send(after(chunks[3], got[2], *wave), partners(3))
     rows[2], pens[2] = make_rows(member, after(got[2], *wave), geo, table)
     rows[1], pens[1] = make_rows(member, after(got[1], rows[2]), geo, table)
+    far = [gathered[2, 1], gathered[2, 0]]
+    (gathered[2, 0],) = local(pair_kernel, "pair", [((32, WIDTH), BF16)], [], far, 2)
     blocks = [gathered[at] for at in ARRIVAL]
 
     second, power = make_scores([rows[2]], [after(pens[2], rows[1])], blocks)

time: 99.1 us -> 96.1 us (0.970)
  waiting for transfers between devices: 23.6 us -> 20.5 us
    ppermute x31, waiting for transfers between devices: 23.6 us -> 20.5 us  [send(): return lax.ppermute(value, AXES, pairs)]
    pallas_call x17 -> x19, Pallas kernels: 31.4 us -> 31.5 us  [local(): pl.pallas_call(kernel, in_specs=[SCALARS] * len(scalars) + [PLACED] * pla...]
  transfers between devices with their start and end apart: 31 -> 31, of which waited for: 14 -> 12; matrix products, arithmetic and copies ran while one was open for 0% -> 0% of each run, Pallas kernels for 28% -> 28%
where the time goes in v13:
time: 96.1 us; the launch traced here: 95.6 us
  starting transfers between devices  42.7 us (44%)
  Pallas kernels  31.5 us (33%)
  waiting for transfers between devices  20.5 us (21%)
    ppermute x31, starting transfers between devices, send(): return lax.ppermute(value, AXES, pairs)  42.7 us
    pallas_call x19, Pallas kernels, local(): pl.pallas_call(kernel, in_specs=[SCALARS] * len(scalars) + [PLACED] * pla...  31.5 us
    ppermute x31, waiting for transfers between devices, send(): return lax.ppermute(value, AXES, pairs)  20.5 us
  transfers between devices with their start and end apart: 31, of which 12 were waited for; matrix products, arithmetic and copies ran while one was open for 0% of the time, Pallas kernels for 28%

profile of v13, /device:TPU:2, one launch (start us, length us, event | category | flops | bytes accessed | tf_op | source)
XLA Modules:
  0.0 95.6 jit_solution(16071235628309189847)
XLA Ops:
  0.0 2.0 %split_particles.1 = (bf16[32,8576]{1,0:T(8,128)(2,1)S(1)}, bf16[32,8576]{1,0:T(8,128)(2,1)S(1)}, bf16[32,8576]{1,0:T(8,128)(2,1)S(1)}, bf16[32,8576]{1,0:T(8,128)(2,1)S(1)}) custom-call(s32[1]{0:T(128)} %bitcast.1.member_ref.refs_0_, s32[1]{0:T(128)} %bitcast.block_ref, s32[1]{0:T(128)} %bitcast.2.x_ref.refs_1_, bf16[32,32768]{1,0:T(8,128)(2,1)} %source.2, ...), custom_call_target="tpu_custom_call" | custom-call | tf_op jit(solution)/shard_map/split_particles/pallas_call | solution.py:111
  2.1 2.0 %collective-permute-start.1 = (bf16[32,8576]{1,0:T(8,128)(2,1)S(1)}, bf16[32,8576]{1,0:T(8,128)(2,1)S(1)}, u32[]{:S(2)}, u32[]{:S(2)}) collective-permute-start(bf16[32,8576]{1,0:T(8,128)(2,1)S(1)} %get-tuple-element.59.after), channel_id=1, source_target_pairs={{0,2},{1,3},{2,0},{3,1},{4,6},{5,7},{6,4},{7,5},{8,10},{9,11},{10,... | collective-permute-start | bytes 1646600 | tf_op jit(solution)/shard_map/ppermute | solution.py:63
  5.7 3.0 %collective-permute-start.3 = (bf16[16,8192]{1,0:T(8,128)(2,1)S(1)}, bf16[16,8192]{1,0:T(8,128)(2,1)S(1)}, u32[]{:S(2)}, u32[]{:S(2)}) collective-permute-start(bf16[16,8192]{1,0:T(8,128)(2,1)S(1)} %own_references.1.refs_8_.refs_10_), channel_id=1, source_target_pairs={{0,192},{1,193},{2,194},{3,195},{4,196},{5,197},{6,198},{7,199},{8... | collective-permute-start | bytes 786440 | tf_op jit(solution)/shard_map/ppermute | solution.py:63
  8.8 5.5 %phase_table.1 = (bf16[256,8192]{1,0:T(8,128)(2,1)S(1)}, f32[4,8,1024]{2,1,0:T(8,128)S(1)}) custom-call(s32[1]{0:T(128)} %bitcast.1.member_ref.refs_0_, f32[16,8,1024]{2,1,0:T(8,128)} %constant.63.clone.geo_ref), custom_call_target="tpu_custom_call" | custom-call | tf_op jit(solution)/shard_map/phase_table/pallas_call | solution.py:111
  14.3 3.2 %shifted_rows.4 = (bf16[256,8192]{1,0:T(8,128)(2,1)S(1)}, bf16[32,4096]{1,0:T(8,128)(2,1)S(1)}) custom-call(s32[1]{0:T(128)} %bitcast.1.member_ref.refs_0_, bf16[32,8576]{1,0:T(8,128)(2,1)S(1)} %get-tuple-element.54.x_ref, f32[4,8,1024]{2,1,0:T(8,128)S(1)} %get-tuple-element.55.geo_ref, bf16[256,8192]{1,0:T(8,128)(2,1)S(1)} %get-tuple-element.56.table_ref), custom_call_target="tpu_custom_call" | custom-call | tf_op jit(solution)/shard_map/shifted_rows/pallas_call | solution.py:111
  18.1 3.1 %collective-permute-start.7 = (bf16[16,8192]{1,0:T(8,128)(2,1)S(1)}, bf16[16,8192]{1,0:T(8,128)(2,1)S(1)}, u32[]{:S(2)}, u32[]{:S(2)}) collective-permute-start(bf16[16,8192]{1,0:T(8,128)(2,1)S(1)} %relay.1), channel_id=1, source_target_pairs={{0,192},{1,65},{2,194},{3,67},{4,196},{5,69},{6,198},{7,71},{8,200... | collective-permute-start | bytes 786440 | tf_op jit(solution)/shard_map/ppermute | solution.py:63
  21.9 1.4 %collective-permute-start.8 = (bf16[16,8192]{1,0:T(8,128)(2,1)S(1)}, bf16[16,8192]{1,0:T(8,128)(2,1)S(1)}, u32[]{:S(2)}, u32[]{:S(2)}) collective-permute-start(bf16[16,8192]{1,0:T(8,128)(2,1)S(1)} %collective-permute-done.2.one.refs_6_.refs_8_), channel_id=1, source_target_pairs={{0,32},{1,33},{2,34},{3,35},{4,36},{5,37},{6,38},{7,39},{8,40},{9,... | collective-permute-start | bytes 786440 | tf_op jit(solution)/shard_map/ppermute | solution.py:63
  23.2 1.5 %collective-permute-start.9 = (bf16[16,8192]{1,0:T(8,128)(2,1)S(1)}, bf16[16,8192]{1,0:T(8,128)(2,1)S(1)}, u32[]{:S(2)}, u32[]{:S(2)}) collective-permute-start(bf16[16,8192]{1,0:T(8,128)(2,1)S(1)} %collective-permute-done.3.other.refs_7_.refs_9_), channel_id=1, source_target_pairs={{0,48},{1,49},{2,50},{3,51},{4,52},{5,53},{6,54},{7,55},{8,56},{9,... | collective-permute-start | bytes 786440 | tf_op jit(solution)/shard_map/ppermute | solution.py:63
  24.7 3.2 %shifted_rows.5 = (bf16[256,8192]{1,0:T(8,128)(2,1)S(1)}, bf16[32,4096]{1,0:T(8,128)(2,1)S(1)}) custom-call(s32[1]{0:T(128)} %bitcast.1.member_ref.refs_0_, bf16[32,8576]{1,0:T(8,128)(2,1)S(1)} %collective-permute-done.1.x_ref, f32[4,8,1024]{2,1,0:T(8,128)S(1)} %get-tuple-element.55.geo_ref, bf16[256,8192]{1,0:T(8,128)(2,1)S(1)} %get-tuple-element.56.table_ref), custom_call_target="tpu_custom_call" | custom-call | tf_op jit(solution)/shard_map/shifted_rows/pallas_call | solution.py:111
  27.9 3.2 %shifted_rows.6 = (bf16[256,8192]{1,0:T(8,128)(2,1)S(1)}, bf16[32,4096]{1,0:T(8,128)(2,1)S(1)}) custom-call(s32[1]{0:T(128)} %bitcast.1.member_ref.refs_0_, bf16[32,8576]{1,0:T(8,128)(2,1)S(1)} %collective-permute-done.x_ref, f32[4,8,1024]{2,1,0:T(8,128)S(1)} %get-tuple-element.55.geo_ref, bf16[256,8192]{1,0:T(8,128)(2,1)S(1)} %get-tuple-element.56.table_ref), custom_call_target="tpu_custom_call" | custom-call | tf_op jit(solution)/shard_map/shifted_rows/pallas_call | solution.py:111
  32.1 1.6 %partial_scores.3 = (f32[256,128]{1,0:T(8,128)S(1)}, bf16[128,4096]{1,0:T(8,128)(2,1)S(1)}) custom-call(bf16[256,8192]{1,0:T(8,128)(2,1)S(1)} %get-tuple-element.61.refs_0_.refs_4_, bf16[32,4096]{1,0:T(8,128)(2,1)S(1)} %get-tuple-element.67.refs_1_, bf16[32,8192]{1,0:T(8,128)(2,1)S(1)} %pair.1.refs_2_.refs_4_, ...), custom_call_target="tpu_custom_call" | custom-call | tf_op jit(solution)/shard_map/partial_scores/pallas_call | solution.py:111
  34.7 3.2 %shifted_rows.7 = (bf16[256,8192]{1,0:T(8,128)(2,1)S(1)}, bf16[32,4096]{1,0:T(8,128)(2,1)S(1)}) custom-call(s32[1]{0:T(128)} %bitcast.1.member_ref.refs_0_, bf16[32,8576]{1,0:T(8,128)(2,1)S(1)} %collective-permute-done.5.x_ref, f32[4,8,1024]{2,1,0:T(8,128)S(1)} %get-tuple-element.55.geo_ref, bf16[256,8192]{1,0:T(8,128)(2,1)S(1)} %get-tuple-element.56.table_ref), custom_call_target="tpu_custom_call" | custom-call | tf_op jit(solution)/shard_map/shifted_rows/pallas_call | solution.py:111
  37.9 1.5 %partial_scores.4 = f32[256,128]{1,0:T(8,128)S(1)} custom-call(bf16[256,8192]{1,0:T(8,128)(2,1)S(1)} %get-tuple-element.74.refs_0_.refs_5_, bf16[32,4096]{1,0:T(8,128)(2,1)S(1)} %get-tuple-element.77.refs_1_, bf16[32,8192]{1,0:T(8,128)(2,1)S(1)} %pair.1.refs_2_.refs_4_, bf16[16,8192]{1,0:T(8,128)(2,1)S(1)} %collective-permute-done.8.refs_3_.refs_5_, ...), custom_call_target="tpu_custom_call" | custom-call | tf_op jit(solution)/shard_map/partial_scores/pallas_call | solution.py:111
  40.5 2.7 %partial_scores.5 = (f32[256,128]{1,0:T(8,128)S(1)}, f32[256,128]{1,0:T(8,128)S(1)}) custom-call(bf16[256,8192]{1,0:T(8,128)(2,1)S(1)} %get-tuple-element.57.refs_0_.refs_2_, bf16[256,8192]{1,0:T(8,128)(2,1)S(1)} %get-tuple-element.63.refs_1_.refs_3_, bf16[32,4096]{1,0:T(8,128)(2,1)S(1)} %get-tuple-element.79.refs_2_, ...), custom_call_target="tpu_custom_call" | custom-call | tf_op jit(solution)/shard_map/partial_scores/pallas_call | solution.py:111
  43.7 1.6 %collective-permute-done.11.refs_2_ = f32[256,128]{1,0:T(8,128)S(1)} collective-permute-done((f32[256,128]{1,0:T(8,128)S(1)}, f32[256,128]{1,0:T(8,128)S(1)}, u32[]{:S(2)}, u32[]{:S(2)}) %collective-permute-start.11) | collective-permute-done | bytes 131104 | tf_op jit(solution)/shard_map/ppermute | solution.py:63
  47.6 2.2 %collective-permute-done.15.refs_9_ = bf16[128,256]{1,0:T(8,128)(2,1)S(1)} collective-permute-done((bf16[128,256]{1,0:T(8,128)(2,1)S(1)}, bf16[128,256]{1,0:T(8,128)(2,1)S(1)}, u32[]{:S(2)}, u32[]{:S(2)}) %collective-permute-start.15) | collective-permute-done | bytes 65568 | tf_op jit(solution)/shard_map/ppermute | solution.py:63
  49.8 1.7 %collective-permute-done.14.refs_8_ = bf16[128,256]{1,0:T(8,128)(2,1)S(1)} collective-permute-done((bf16[128,256]{1,0:T(8,128)(2,1)S(1)}, bf16[128,256]{1,0:T(8,128)(2,1)S(1)}, u32[]{:S(2)}, u32[]{:S(2)}) %collective-permute-start.14) | collective-permute-done | bytes 65568 | tf_op jit(solution)/shard_map/ppermute | solution.py:63
  51.5 2.0 %weighted_sums.3 = (bf16[64,2048]{1,0:T(8,128)(2,1)S(1)}, bf16[64,2048]{1,0:T(8,128)(2,1)S(1)}, bf16[64,2048]{1,0:T(8,128)(2,1)S(1)}, bf16[64,2048]{1,0:T(8,128)(2,1)S(1)}) custom-call(s32[1]{0:T(128)} %bitcast.1.member_ref.refs_0_, s32[1]{0:T(128)} %bitcast.2.x_ref.refs_1_, bf16[256,8192]{1,0:T(8,128)(2,1)S(1)} %get-tuple-element.57.refs_0_.refs_2_, ...), custom_call_target="tpu_custom_call" | custom-call | tf_op jit(solution)/shard_map/weighted_sums/pallas_call | solution.py:111
  53.5 2.4 %collective-permute-start.22 = (bf16[64,2048]{1,0:T(8,128)(2,1)S(1)}, bf16[64,2048]{1,0:T(8,128)(2,1)S(1)}, u32[]{:S(2)}, u32[]{:S(2)}) collective-permute-start(bf16[64,2048]{1,0:T(8,128)(2,1)S(1)} %get-tuple-element.92), channel_id=1, source_target_pairs={{0,16},{1,129},{2,18},{3,131},{4,20},{5,133},{6,22},{7,135},{8,24}... | collective-permute-start | bytes 786440 | tf_op jit(solution)/shard_map/ppermute | solution.py:63
  57.6 1.9 %weighted_sums.2 = (bf16[64,2048]{1,0:T(8,128)(2,1)S(1)}, bf16[64,2048]{1,0:T(8,128)(2,1)S(1)}, bf16[64,2048]{1,0:T(8,128)(2,1)S(1)}, bf16[64,2048]{1,0:T(8,128)(2,1)S(1)}) custom-call(s32[1]{0:T(128)} %bitcast.1.member_ref.refs_0_, s32[1]{0:T(128)} %bitcast.2.x_ref.refs_1_, bf16[256,8192]{1,0:T(8,128)(2,1)S(1)} %get-tuple-element.57.refs_0_.refs_2_, ...), custom_call_target="tpu_custom_call" | custom-call | tf_op jit(solution)/shard_map/weighted_sums/pallas_call | solution.py:111
  59.6 1.8 %collective-permute-start.16 = (bf16[64,2048]{1,0:T(8,128)(2,1)S(1)}, bf16[64,2048]{1,0:T(8,128)(2,1)S(1)}, u32[]{:S(2)}, u32[]{:S(2)}) collective-permute-start(bf16[64,2048]{1,0:T(8,128)(2,1)S(1)} %get-tuple-element.84), channel_id=1, source_target_pairs={{0,128},{1,17},{2,130},{3,19},{4,132},{5,21},{6,134},{7,23},{8,136... | collective-permute-start | bytes 786440 | tf_op jit(solution)/shard_map/ppermute | solution.py:63
  61.4 1.4 %collective-permute-start.17 = (bf16[64,2048]{1,0:T(8,128)(2,1)S(1)}, bf16[64,2048]{1,0:T(8,128)(2,1)S(1)}, u32[]{:S(2)}, u32[]{:S(2)}) collective-permute-start(bf16[64,2048]{1,0:T(8,128)(2,1)S(1)} %get-tuple-element.85), channel_id=1, source_target_pairs={{0,64},{1,33},{2,66},{3,35},{4,68},{5,37},{6,70},{7,39},{8,72},{9,... | collective-permute-start | bytes 786440 | tf_op jit(solution)/shard_map/ppermute | solution.py:63
  63.8 2.0 %collective-permute-done.23.refs_4_ = bf16[64,2048]{1,0:T(8,128)(2,1)S(1)} collective-permute-done((bf16[64,2048]{1,0:T(8,128)(2,1)S(1)}, bf16[64,2048]{1,0:T(8,128)(2,1)S(1)}, u32[]{:S(2)}, u32[]{:S(2)}) %collective-permute-start.23) | collective-permute-done | bytes 262176 | tf_op jit(solution)/shard_map/ppermute | solution.py:63
  65.8 1.9 %collective-permute-done.24.refs_5_ = bf16[64,2048]{1,0:T(8,128)(2,1)S(1)} collective-permute-done((bf16[64,2048]{1,0:T(8,128)(2,1)S(1)}, bf16[64,2048]{1,0:T(8,128)(2,1)S(1)}, u32[]{:S(2)}, u32[]{:S(2)}) %collective-permute-start.24) | collective-permute-done | bytes 262176 | tf_op jit(solution)/shard_map/ppermute | solution.py:63
  67.8 1.8 %collective-permute-start.25 = (bf16[16,2048]{1,0:T(8,128)(2,1)S(1)}, bf16[16,2048]{1,0:T(8,128)(2,1)S(1)}, u32[]{:S(2)}, u32[]{:S(2)}) collective-permute-start(bf16[16,2048]{1,0:T(8,128)(2,1)S(1)} %get-tuple-element.96), channel_id=1, source_target_pairs={{0,128},{1,17},{2,130},{3,19},{4,132},{5,21},{6,134},{7,23},{8,136... | collective-permute-start | bytes 196616 | tf_op jit(solution)/shard_map/ppermute | solution.py:63
  72.2 2.7 %collective-permute-start.19 = (bf16[16,2048]{1,0:T(8,128)(2,1)S(1)}, bf16[16,2048]{1,0:T(8,128)(2,1)S(1)}, u32[]{:S(2)}, u32[]{:S(2)}) collective-permute-start(bf16[16,2048]{1,0:T(8,128)(2,1)S(1)} %get-tuple-element.88), channel_id=1, source_target_pairs={{0,16},{1,129},{2,18},{3,131},{4,20},{5,133},{6,22},{7,135},{8,24}... | collective-permute-start | bytes 196616 | tf_op jit(solution)/shard_map/ppermute | solution.py:63
  74.9 1.6 %collective-permute-start.20 = (bf16[16,2048]{1,0:T(8,128)(2,1)S(1)}, bf16[16,2048]{1,0:T(8,128)(2,1)S(1)}, u32[]{:S(2)}, u32[]{:S(2)}) collective-permute-start(bf16[16,2048]{1,0:T(8,128)(2,1)S(1)} %get-tuple-element.89), channel_id=1, source_target_pairs={{0,32},{1,65},{2,34},{3,67},{4,36},{5,69},{6,38},{7,71},{8,40},{9,... | collective-permute-start | bytes 196616 | tf_op jit(solution)/shard_map/ppermute | solution.py:63
  76.6 1.7 %collective-permute-done.19.refs_1_ = bf16[16,2048]{1,0:T(8,128)(2,1)S(1)} collective-permute-done((bf16[16,2048]{1,0:T(8,128)(2,1)S(1)}, bf16[16,2048]{1,0:T(8,128)(2,1)S(1)}, u32[]{:S(2)}, u32[]{:S(2)}) %collective-permute-start.19) | collective-permute-done | bytes 65568 | tf_op jit(solution)/shard_map/ppermute | solution.py:63
  80.9 6.6 %collective-permute-start.28 = (bf16[16,1024]{1,0:T(8,128)(2,1)S(1)}, bf16[16,1024]{1,0:T(8,128)(2,1)S(1)}, u32[]{:S(2)}, u32[]{:S(2)}) collective-permute-start(bf16[16,1024]{1,0:T(8,128)(2,1)S(1)} %get-tuple-element.100), channel_id=1, source_target_pairs={{0,8},{1,9},{2,10},{3,11},{4,12},{5,13},{6,14},{7,15},{8,0},{9,1},... | collective-permute-start | bytes 98312 | tf_op jit(solution)/shard_map/ppermute | solution.py:63
  87.4 1.5 %collective-permute-start.29 = (bf16[16,1024]{1,0:T(8,128)(2,1)S(1)}, bf16[16,1024]{1,0:T(8,128)(2,1)S(1)}, u32[]{:S(2)}, u32[]{:S(2)}) collective-permute-start(bf16[16,1024]{1,0:T(8,128)(2,1)S(1)} %get-tuple-element.101), channel_id=1, source_target_pairs={{0,4},{1,5},{2,6},{3,7},{4,0},{5,1},{6,2},{7,3},{8,12},{9,13},{10,... | collective-permute-start | bytes 98312 | tf_op jit(solution)/shard_map/ppermute | solution.py:63
  89.7 2.5 %collective-permute-done.29 = bf16[16,1024]{1,0:T(8,128)(2,1)S(1)} collective-permute-done((bf16[16,1024]{1,0:T(8,128)(2,1)S(1)}, bf16[16,1024]{1,0:T(8,128)(2,1)S(1)}, u32[]{:S(2)}, u32[]{:S(2)}) %collective-permute-start.29) | collective-permute-done | bytes 32800 | tf_op jit(solution)/shard_map/ppermute | solution.py:63
  92.3 2.7 %collective-permute-done.30 = bf16[16,1024]{1,0:T(8,128)(2,1)S(1)} collective-permute-done((bf16[16,1024]{1,0:T(8,128)(2,1)S(1)}, bf16[16,1024]{1,0:T(8,128)(2,1)S(1)}, u32[]{:S(2)}, u32[]{:S(2)}) %collective-permute-start.30) | collective-permute-done | bytes 32800 | tf_op jit(solution)/shard_map/ppermute | solution.py:63
  (50 shorter events, 18.4 us)
Async XLA Ops:
  2.0 15.6 %collective-permute-start = (bf16[32,8576]{1,0:T(8,128)(2,1)S(1)}, bf16[32,8576]{1,0:T(8,128)(2,1)S(1)}, u32[]{:S(2)}, u32[]{:S(2)}) collective-permute-start(bf16[32,8576]{1,0:T(8,128)(2,1)S(1)} %get-tuple-element.58), channel_id=1, source_target_pairs={{0,1},{1,0},{2,3},{3,2},{4,5},{5,4},{6,7},{7,6},{8,9},{9,8},{10,11... | collective-permute-start | bytes 1646600 | tf_op jit(solution)/shard_map/ppermute | solution.py:63
  2.1 15.5 %collective-permute-start.1 = (bf16[32,8576]{1,0:T(8,128)(2,1)S(1)}, bf16[32,8576]{1,0:T(8,128)(2,1)S(1)}, u32[]{:S(2)}, u32[]{:S(2)}) collective-permute-start(bf16[32,8576]{1,0:T(8,128)(2,1)S(1)} %get-tuple-element.59.after), channel_id=1, source_target_pairs={{0,2},{1,3},{2,0},{3,1},{4,6},{5,7},{6,4},{7,5},{8,10},{9,11},{10,... | collective-permute-start | bytes 1646600 | tf_op jit(solution)/shard_map/ppermute | solution.py:63
  5.0 12.5 %collective-permute-start.4 = (bf16[16,8192]{1,0:T(8,128)(2,1)S(1)}, bf16[16,8192]{1,0:T(8,128)(2,1)S(1)}, u32[]{:S(2)}, u32[]{:S(2)}) collective-permute-start(bf16[16,8192]{1,0:T(8,128)(2,1)S(1)} %own_references.1.refs_8_.refs_10_), channel_id=1, source_target_pairs={{0,32},{1,33},{2,34},{3,35},{4,36},{5,37},{6,38},{7,39},{8,40},{9,... | collective-permute-start | bytes 786440 | tf_op jit(solution)/shard_map/ppermute | solution.py:63
  5.7 11.9 %collective-permute-start.3 = (bf16[16,8192]{1,0:T(8,128)(2,1)S(1)}, bf16[16,8192]{1,0:T(8,128)(2,1)S(1)}, u32[]{:S(2)}, u32[]{:S(2)}) collective-permute-start(bf16[16,8192]{1,0:T(8,128)(2,1)S(1)} %own_references.1.refs_8_.refs_10_), channel_id=1, source_target_pairs={{0,192},{1,193},{2,194},{3,195},{4,196},{5,197},{6,198},{7,199},{8... | collective-permute-start | bytes 786440 | tf_op jit(solution)/shard_map/ppermute | solution.py:63
  8.7 8.9 %collective-permute-start.2 = (bf16[16,8192]{1,0:T(8,128)(2,1)S(1)}, bf16[16,8192]{1,0:T(8,128)(2,1)S(1)}, u32[]{:S(2)}, u32[]{:S(2)}) collective-permute-start(bf16[16,8192]{1,0:T(8,128)(2,1)S(1)} %own_references.1.refs_8_.refs_10_), channel_id=1, source_target_pairs={{0,64},{1,65},{2,66},{3,67},{4,68},{5,69},{6,70},{7,71},{8,72},{9,... | collective-permute-start | bytes 786440 | tf_op jit(solution)/shard_map/ppermute | solution.py:63
  17.6 17.1 %collective-permute-start.5 = (bf16[32,8576]{1,0:T(8,128)(2,1)S(1)}, bf16[32,8576]{1,0:T(8,128)(2,1)S(1)}, u32[]{:S(2)}, u32[]{:S(2)}) collective-permute-start(bf16[32,8576]{1,0:T(8,128)(2,1)S(1)} %get-tuple-element.65), channel_id=1, source_target_pairs={{0,3},{1,2},{2,1},{3,0},{4,7},{5,6},{6,5},{7,4},{8,11},{9,10},{10,... | collective-permute-start | bytes 1646600 | tf_op jit(solution)/shard_map/ppermute | solution.py:63
  18.1 13.0 %collective-permute-start.7 = (bf16[16,8192]{1,0:T(8,128)(2,1)S(1)}, bf16[16,8192]{1,0:T(8,128)(2,1)S(1)}, u32[]{:S(2)}, u32[]{:S(2)}) collective-permute-start(bf16[16,8192]{1,0:T(8,128)(2,1)S(1)} %relay.1), channel_id=1, source_target_pairs={{0,192},{1,65},{2,194},{3,67},{4,196},{5,69},{6,198},{7,71},{8,200... | collective-permute-start | bytes 786440 | tf_op jit(solution)/shard_map/ppermute | solution.py:63
  21.2 10.7 %collective-permute-start.6 = (bf16[16,8192]{1,0:T(8,128)(2,1)S(1)}, bf16[16,8192]{1,0:T(8,128)(2,1)S(1)}, u32[]{:S(2)}, u32[]{:S(2)}) collective-permute-start(bf16[16,8192]{1,0:T(8,128)(2,1)S(1)} %collective-permute-done.4.refs_5_.refs_7_), channel_id=1, source_target_pairs={{0,128},{1,129},{2,130},{3,131},{4,132},{5,133},{6,134},{7,135},{8... | collective-permute-start | bytes 786440 | tf_op jit(solution)/shard_map/ppermute | solution.py:63
  21.9 10.2 %collective-permute-start.8 = (bf16[16,8192]{1,0:T(8,128)(2,1)S(1)}, bf16[16,8192]{1,0:T(8,128)(2,1)S(1)}, u32[]{:S(2)}, u32[]{:S(2)}) collective-permute-start(bf16[16,8192]{1,0:T(8,128)(2,1)S(1)} %collective-permute-done.2.one.refs_6_.refs_8_), channel_id=1, source_target_pairs={{0,32},{1,33},{2,34},{3,35},{4,36},{5,37},{6,38},{7,39},{8,40},{9,... | collective-permute-start | bytes 786440 | tf_op jit(solution)/shard_map/ppermute | solution.py:63
  23.2 8.8 %collective-permute-start.9 = (bf16[16,8192]{1,0:T(8,128)(2,1)S(1)}, bf16[16,8192]{1,0:T(8,128)(2,1)S(1)}, u32[]{:S(2)}, u32[]{:S(2)}) collective-permute-start(bf16[16,8192]{1,0:T(8,128)(2,1)S(1)} %collective-permute-done.3.other.refs_7_.refs_9_), channel_id=1, source_target_pairs={{0,48},{1,49},{2,50},{3,51},{4,52},{5,53},{6,54},{7,55},{8,56},{9,... | collective-permute-start | bytes 786440 | tf_op jit(solution)/shard_map/ppermute | solution.py:63
  33.7 10.0 %collective-permute-start.10 = (f32[256,128]{1,0:T(8,128)S(1)}, f32[256,128]{1,0:T(8,128)S(1)}, u32[]{:S(2)}, u32[]{:S(2)}) collective-permute-start(f32[256,128]{1,0:T(8,128)S(1)} %get-tuple-element.72), channel_id=1, source_target_pairs={{0,2},{1,3},{2,0},{3,1},{4,6},{5,7},{6,4},{7,5},{8,10},{9,11},{10,... | collective-permute-start | bytes 393224 | tf_op jit(solution)/shard_map/ppermute | solution.py:63
  39.4 5.9 %collective-permute-start.11 = (f32[256,128]{1,0:T(8,128)S(1)}, f32[256,128]{1,0:T(8,128)S(1)}, u32[]{:S(2)}, u32[]{:S(2)}) collective-permute-start(f32[256,128]{1,0:T(8,128)S(1)} %partial_scores.4), channel_id=1, source_target_pairs={{0,3},{1,2},{2,1},{3,0},{4,7},{5,6},{6,5},{7,4},{8,11},{9,10},{10,... | collective-permute-start | bytes 393224 | tf_op jit(solution)/shard_map/ppermute | solution.py:63
  43.2 2.1 %collective-permute-start.12 = (f32[256,128]{1,0:T(8,128)S(1)}, f32[256,128]{1,0:T(8,128)S(1)}, u32[]{:S(2)}, u32[]{:S(2)}) collective-permute-start(f32[256,128]{1,0:T(8,128)S(1)} %get-tuple-element.82), channel_id=1, source_target_pairs={{0,1},{1,0},{2,3},{3,2},{4,5},{5,4},{6,7},{7,6},{8,9},{9,8},{10,11... | collective-permute-start | bytes 393224 | tf_op jit(solution)/shard_map/ppermute | solution.py:63
  45.6 4.2 %collective-permute-start.15 = (bf16[128,256]{1,0:T(8,128)(2,1)S(1)}, bf16[128,256]{1,0:T(8,128)(2,1)S(1)}, u32[]{:S(2)}, u32[]{:S(2)}) collective-permute-start(bf16[128,256]{1,0:T(8,128)(2,1)S(1)} %posterior.1.refs_6_), channel_id=1, source_target_pairs={{0,3},{1,2},{2,1},{3,0},{4,7},{5,6},{6,5},{7,4},{8,11},{9,10},{10,... | collective-permute-start | bytes 196616 | tf_op jit(solution)/shard_map/ppermute | solution.py:63
  46.5 5.0 %collective-permute-start.14 = (bf16[128,256]{1,0:T(8,128)(2,1)S(1)}, bf16[128,256]{1,0:T(8,128)(2,1)S(1)}, u32[]{:S(2)}, u32[]{:S(2)}) collective-permute-start(bf16[128,256]{1,0:T(8,128)(2,1)S(1)} %posterior.1.refs_6_), channel_id=1, source_target_pairs={{0,2},{1,3},{2,0},{3,1},{4,6},{5,7},{6,4},{7,5},{8,10},{9,11},{10,... | collective-permute-start | bytes 196616 | tf_op jit(solution)/shard_map/ppermute | solution.py:63
  47.5 4.1 %collective-permute-start.13 = (bf16[128,256]{1,0:T(8,128)(2,1)S(1)}, bf16[128,256]{1,0:T(8,128)(2,1)S(1)}, u32[]{:S(2)}, u32[]{:S(2)}) collective-permute-start(bf16[128,256]{1,0:T(8,128)(2,1)S(1)} %posterior.1.refs_6_), channel_id=1, source_target_pairs={{0,1},{1,0},{2,3},{3,2},{4,5},{5,4},{6,7},{7,6},{8,9},{9,8},{10,11... | collective-permute-start | bytes 196616 | tf_op jit(solution)/shard_map/ppermute | solution.py:63
  53.5 9.3 %collective-permute-start.22 = (bf16[64,2048]{1,0:T(8,128)(2,1)S(1)}, bf16[64,2048]{1,0:T(8,128)(2,1)S(1)}, u32[]{:S(2)}, u32[]{:S(2)}) collective-permute-start(bf16[64,2048]{1,0:T(8,128)(2,1)S(1)} %get-tuple-element.92), channel_id=1, source_target_pairs={{0,16},{1,129},{2,18},{3,131},{4,20},{5,133},{6,22},{7,135},{8,24}... | collective-permute-start | bytes 786440 | tf_op jit(solution)/shard_map/ppermute | solution.py:63
  55.9 9.9 %collective-permute-start.23 = (bf16[64,2048]{1,0:T(8,128)(2,1)S(1)}, bf16[64,2048]{1,0:T(8,128)(2,1)S(1)}, u32[]{:S(2)}, u32[]{:S(2)}) collective-permute-start(bf16[64,2048]{1,0:T(8,128)(2,1)S(1)} %get-tuple-element.93), channel_id=1, source_target_pairs={{0,32},{1,65},{2,34},{3,67},{4,36},{5,69},{6,38},{7,71},{8,40},{9,... | collective-permute-start | bytes 786440 | tf_op jit(solution)/shard_map/ppermute | solution.py:63
  57.1 10.6 %collective-permute-start.24 = (bf16[64,2048]{1,0:T(8,128)(2,1)S(1)}, bf16[64,2048]{1,0:T(8,128)(2,1)S(1)}, u32[]{:S(2)}, u32[]{:S(2)}) collective-permute-start(bf16[64,2048]{1,0:T(8,128)(2,1)S(1)} %get-tuple-element.94), channel_id=1, source_target_pairs={{0,48},{1,193},{2,50},{3,195},{4,52},{5,197},{6,54},{7,199},{8,56}... | collective-permute-start | bytes 786440 | tf_op jit(solution)/shard_map/ppermute | solution.py:63
  59.6 11.4 %collective-permute-start.16 = (bf16[64,2048]{1,0:T(8,128)(2,1)S(1)}, bf16[64,2048]{1,0:T(8,128)(2,1)S(1)}, u32[]{:S(2)}, u32[]{:S(2)}) collective-permute-start(bf16[64,2048]{1,0:T(8,128)(2,1)S(1)} %get-tuple-element.84), channel_id=1, source_target_pairs={{0,128},{1,17},{2,130},{3,19},{4,132},{5,21},{6,134},{7,23},{8,136... | collective-permute-start | bytes 786440 | tf_op jit(solution)/shard_map/ppermute | solution.py:63
  61.4 10.7 %collective-permute-start.17 = (bf16[64,2048]{1,0:T(8,128)(2,1)S(1)}, bf16[64,2048]{1,0:T(8,128)(2,1)S(1)}, u32[]{:S(2)}, u32[]{:S(2)}) collective-permute-start(bf16[64,2048]{1,0:T(8,128)(2,1)S(1)} %get-tuple-element.85), channel_id=1, source_target_pairs={{0,64},{1,33},{2,66},{3,35},{4,68},{5,37},{6,70},{7,39},{8,72},{9,... | collective-permute-start | bytes 786440 | tf_op jit(solution)/shard_map/ppermute | solution.py:63
  62.8 9.2 %collective-permute-start.18 = (bf16[64,2048]{1,0:T(8,128)(2,1)S(1)}, bf16[64,2048]{1,0:T(8,128)(2,1)S(1)}, u32[]{:S(2)}, u32[]{:S(2)}) collective-permute-start(bf16[64,2048]{1,0:T(8,128)(2,1)S(1)} %get-tuple-element.86), channel_id=1, source_target_pairs={{0,192},{1,49},{2,194},{3,51},{4,196},{5,53},{6,198},{7,55},{8,200... | collective-permute-start | bytes 786440 | tf_op jit(solution)/shard_map/ppermute | solution.py:63
  67.8 8.7 %collective-permute-start.25 = (bf16[16,2048]{1,0:T(8,128)(2,1)S(1)}, bf16[16,2048]{1,0:T(8,128)(2,1)S(1)}, u32[]{:S(2)}, u32[]{:S(2)}) collective-permute-start(bf16[16,2048]{1,0:T(8,128)(2,1)S(1)} %get-tuple-element.96), channel_id=1, source_target_pairs={{0,128},{1,17},{2,130},{3,19},{4,132},{5,21},{6,134},{7,23},{8,136... | collective-permute-start | bytes 196616 | tf_op jit(solution)/shard_map/ppermute | solution.py:63
  69.6 7.0 %collective-permute-start.26 = (bf16[16,2048]{1,0:T(8,128)(2,1)S(1)}, bf16[16,2048]{1,0:T(8,128)(2,1)S(1)}, u32[]{:S(2)}, u32[]{:S(2)}) collective-permute-start(bf16[16,2048]{1,0:T(8,128)(2,1)S(1)} %get-tuple-element.97), channel_id=1, source_target_pairs={{0,64},{1,33},{2,66},{3,35},{4,68},{5,37},{6,70},{7,39},{8,72},{9,... | collective-permute-start | bytes 196616 | tf_op jit(solution)/shard_map/ppermute | solution.py:63
  70.9 5.7 %collective-permute-start.27 = (bf16[16,2048]{1,0:T(8,128)(2,1)S(1)}, bf16[16,2048]{1,0:T(8,128)(2,1)S(1)}, u32[]{:S(2)}, u32[]{:S(2)}) collective-permute-start(bf16[16,2048]{1,0:T(8,128)(2,1)S(1)} %get-tuple-element.98), channel_id=1, source_target_pairs={{0,192},{1,49},{2,194},{3,51},{4,196},{5,53},{6,198},{7,55},{8,200... | collective-permute-start | bytes 196616 | tf_op jit(solution)/shard_map/ppermute | solution.py:63
  72.2 6.1 %collective-permute-start.19 = (bf16[16,2048]{1,0:T(8,128)(2,1)S(1)}, bf16[16,2048]{1,0:T(8,128)(2,1)S(1)}, u32[]{:S(2)}, u32[]{:S(2)}) collective-permute-start(bf16[16,2048]{1,0:T(8,128)(2,1)S(1)} %get-tuple-element.88), channel_id=1, source_target_pairs={{0,16},{1,129},{2,18},{3,131},{4,20},{5,133},{6,22},{7,135},{8,24}... | collective-permute-start | bytes 196616 | tf_op jit(solution)/shard_map/ppermute | solution.py:63
  74.9 4.6 %collective-permute-start.20 = (bf16[16,2048]{1,0:T(8,128)(2,1)S(1)}, bf16[16,2048]{1,0:T(8,128)(2,1)S(1)}, u32[]{:S(2)}, u32[]{:S(2)}) collective-permute-start(bf16[16,2048]{1,0:T(8,128)(2,1)S(1)} %get-tuple-element.89), channel_id=1, source_target_pairs={{0,32},{1,65},{2,34},{3,67},{4,36},{5,69},{6,38},{7,71},{8,40},{9,... | collective-permute-start | bytes 196616 | tf_op jit(solution)/shard_map/ppermute | solution.py:63
  76.5 4.3 %collective-permute-start.21 = (bf16[16,2048]{1,0:T(8,128)(2,1)S(1)}, bf16[16,2048]{1,0:T(8,128)(2,1)S(1)}, u32[]{:S(2)}, u32[]{:S(2)}) collective-permute-start(bf16[16,2048]{1,0:T(8,128)(2,1)S(1)} %get-tuple-element.90), channel_id=1, source_target_pairs={{0,48},{1,193},{2,50},{3,195},{4,52},{5,197},{6,54},{7,199},{8,56}... | collective-permute-start | bytes 196616 | tf_op jit(solution)/shard_map/ppermute | solution.py:63
  80.9 8.9 %collective-permute-start.28 = (bf16[16,1024]{1,0:T(8,128)(2,1)S(1)}, bf16[16,1024]{1,0:T(8,128)(2,1)S(1)}, u32[]{:S(2)}, u32[]{:S(2)}) collective-permute-start(bf16[16,1024]{1,0:T(8,128)(2,1)S(1)} %get-tuple-element.100), channel_id=1, source_target_pairs={{0,8},{1,9},{2,10},{3,11},{4,12},{5,13},{6,14},{7,15},{8,0},{9,1},... | collective-permute-start | bytes 98312 | tf_op jit(solution)/shard_map/ppermute | solution.py:63
  87.4 4.8 %collective-permute-start.29 = (bf16[16,1024]{1,0:T(8,128)(2,1)S(1)}, bf16[16,1024]{1,0:T(8,128)(2,1)S(1)}, u32[]{:S(2)}, u32[]{:S(2)}) collective-permute-start(bf16[16,1024]{1,0:T(8,128)(2,1)S(1)} %get-tuple-element.101), channel_id=1, source_target_pairs={{0,4},{1,5},{2,6},{3,7},{4,0},{5,1},{6,2},{7,3},{8,12},{9,13},{10,... | collective-permute-start | bytes 98312 | tf_op jit(solution)/shard_map/ppermute | solution.py:63
  88.9 6.0 %collective-permute-start.30 = (bf16[16,1024]{1,0:T(8,128)(2,1)S(1)}, bf16[16,1024]{1,0:T(8,128)(2,1)S(1)}, u32[]{:S(2)}, u32[]{:S(2)}) collective-permute-start(bf16[16,1024]{1,0:T(8,128)(2,1)S(1)} %get-tuple-element.102), channel_id=1, source_target_pairs={{0,12},{1,13},{2,14},{3,15},{4,8},{5,9},{6,10},{7,11},{8,4},{9,5},... | collective-permute-start | bytes 98312 | tf_op jit(solution)/shard_map/ppermute | solution.py:63

commit v14 on v13

--- a/solution.py
+++ b/solution.py
@@ -19,7 +19,7 @@
 NB = 16 // G
 ROWS = P_DEV * SHIFTS
 WIDTH = NB * 2 * COLS
-EXTRA = 384
+EXTRA = 128
 AXES = ("blk", "dom")
 F32, BF16 = jnp.float32, jnp.bfloat16
 NT = (((1,), (1,)), ((), ()))
@@ -247,18 +247,12 @@
     first = jnp.concatenate(
         [ids_in[...].astype(F32), jnp.broadcast_to(sigma_in[...], (8, P_DEV))], axis=0
     )
-    info = jnp.concatenate(
-        [
-            turned_over(first),
-            wedge_in[...].astype(F32),
-            focus_in[...],
-            jnp.zeros((P_DEV, 128 - 16 - 2 * TILTS), F32),
-        ],
-        axis=1,
-    )
-    for spot, piece in enumerate(parts_of(info)):
-        for out in outs:
-            out[:, WIDTH + spot * 128 : WIDTH + (spot + 1) * 128] = piece
+    turned = turned_over(first)
+    pieces = [turned[:, :SHIFTS], *parts_of(turned[:, SHIFTS : SHIFTS + 1]), jnp.zeros((P_DEV, 5), F32)]
+    pieces += [*parts_of(wedge_in[...].astype(F32) * focus_in[...]), jnp.zeros((P_DEV, 16), F32)]
+    info = jnp.concatenate([piece.astype(F32) for piece in pieces], axis=1).astype(BF16)
+    for out in outs:
+        out[:, WIDTH:] = info
     for copy in copies:
         copy.wait()
 
@@ -279,20 +273,22 @@
 
 
 def rows_kernel(member_ref, x_ref, geo_ref, table_ref, rows_ref, pen_ref):
-    info = sum(x_ref[:, WIDTH + n * 128 : WIDTH + (n + 1) * 128].astype(F32) for n in range(3))
+    info = x_ref[:, WIDTH:].astype(F32)
     lane = lax.broadcasted_iota(jnp.int32, (ROWS, 256), 1) & 127
     ids = jnp.concatenate([info[:, s : s + 1] for s in range(SHIFTS)], axis=0)
     pick = (ids == lane.astype(F32)).astype(BF16)
-    sigma = info[:, SHIFTS : SHIFTS + 1]
+    sigma = sum(info[:, SHIFTS + n : SHIFTS + n + 1] for n in range(3))
     small = lax.broadcasted_iota(jnp.int32, (P_DEV, 128), 1)
 
-    @pl.loop(0, NB)
+    @pl.loop(0, NB, unroll=True)
     def _(block):
         first = 2 * (block * G + member_ref[0]) + 16
         start = pl.multiple_of(block * 2 * COLS, 2 * COLS)
         for tilt in range(2):
-            kept = jnp.sum(jnp.where(small == first + tilt, info, 0.0), axis=1, keepdims=True)
-            focus = jnp.sum(jnp.where(small == first + tilt + TILTS, info, 0.0), axis=1, keepdims=True)
+            at = first + tilt
+            mine = (small == at) | (small == at + TILTS) | (small == at + 2 * TILTS)
+            focus = jnp.sum(jnp.where(mine, info, 0.0), axis=1, keepdims=True)
+            kept = jnp.where(focus > 0.5, 1.0, 0.0)
             shell = geo_ref[block, 3:4, tilt * HALF : (tilt + 1) * HALF]
             transfer = -sine_turns((4.0 * focus * shell + 0.1) * (0.5 / math.pi))
             weight = kept * transfer * sigma
@@ -301,12 +297,18 @@
             lower, upper = pl.ds(start + tilt * HALF, HALF), pl.ds(start + COLS + tilt * HALF, HALF)
             real = (weight * x_ref[:, lower].astype(F32))[None]
             imag = (weight * x_ref[:, upper].astype(F32))[None]
-            turned = jnp.dot(
-                pick, table_ref[:, pl.ds(start + tilt * COLS, COLS)], preferred_element_type=F32
-            ).reshape(SHIFTS, P_DEV, COLS)
-            cosine, sine = turned[:, :, :HALF], turned[:, :, HALF:]
-            rows_ref[:, lower] = (real * cosine + imag * sine).reshape(ROWS, HALF).astype(BF16)
-            rows_ref[:, upper] = (imag * cosine - real * sine).reshape(ROWS, HALF).astype(BF16)
+            real, imag = real[0], imag[0]
+            for part in range(0, HALF, 256):
+                lanes = slice(part, part + 256)
+                at = start + tilt * COLS + part
+                cosine = jnp.dot(pick, table_ref[:, pl.ds(at, 256)], preferred_element_type=F32)
+                sine = jnp.dot(pick, table_ref[:, pl.ds(at + HALF, 256)], preferred_element_type=F32)
+                cosine, sine = cosine.reshape(SHIFTS, P_DEV, 256), sine.reshape(SHIFTS, P_DEV, 256)
+                one, two = real[None, :, lanes], imag[None, :, lanes]
+                low = pl.ds(start + tilt * HALF + part, 256)
+                high = pl.ds(start + COLS + tilt * HALF + part, 256)
+                rows_ref[:, low] = (one * cosine + two * sine).reshape(ROWS, 256).astype(BF16)
+                rows_ref[:, high] = (two * cosine - one * sine).reshape(ROWS, 256).astype(BF16)
 
 
 def make_rows(member, x, geo, table):
@@ -378,7 +380,7 @@
     along_y = (member_ref[0] & 1) == part
     high = x_ref[0] >> 1
 
-    @pl.loop(0, NB)
+    @pl.loop(0, NB, unroll=True)
     def _(block):
         sums = []
         for half in range(2):

time: 96.1 us -> 94.8 us (0.986)
  Pallas kernels: 31.5 us -> 27.1 us
  waiting for transfers between devices: 20.5 us -> 23 us
    pallas_call x19, Pallas kernels: 31.5 us -> 27.1 us  [local(): pl.pallas_call(kernel, in_specs=[SCALARS] * len(scalars) + [PLACED] * pla...]
    ppermute x31, waiting for transfers between devices: 20.5 us -> 23 us  [send(): return lax.ppermute(value, AXES, pairs)]
  transfers between devices with their start and end apart: 31 -> 31, of which waited for: 12 -> 15; matrix products, arithmetic and copies ran while one was open for 0% -> 0% of each run, Pallas kernels for 28% -> 25%
where the time goes in v14:
time: 94.8 us; the launch traced here: 94.2 us
  starting transfers between devices  43.2 us (46%)
  Pallas kernels  27.1 us (29%)
  waiting for transfers between devices  23 us (24%)
    ppermute x31, starting transfers between devices, send(): return lax.ppermute(value, AXES, pairs)  43.2 us
    pallas_call x19, Pallas kernels, local(): pl.pallas_call(kernel, in_specs=[SCALARS] * len(scalars) + [PLACED] * pla...  27.1 us
    ppermute x31, waiting for transfers between devices, send(): return lax.ppermute(value, AXES, pairs)  23 us
  transfers between devices with their start and end apart: 31, of which 15 were waited for; matrix products, arithmetic and copies ran while one was open for 0% of the time, Pallas kernels for 25%

profile of v14, /device:TPU:2, one launch (start us, length us, event | category | flops | bytes accessed | tf_op | source)
XLA Modules:
  0.0 94.2 jit_solution(9622228465365761375)
XLA Ops:
  0.0 2.0 %split_particles.1 = (bf16[32,8320]{1,0:T(8,128)(2,1)S(1)}, bf16[32,8320]{1,0:T(8,128)(2,1)S(1)}, bf16[32,8320]{1,0:T(8,128)(2,1)S(1)}, bf16[32,8320]{1,0:T(8,128)(2,1)S(1)}) custom-call(s32[1]{0:T(128)} %bitcast.1.member_ref.refs_0_, s32[1]{0:T(128)} %bitcast.block_ref, s32[1]{0:T(128)} %bitcast.2.x_ref.refs_1_, bf16[32,32768]{1,0:T(8,128)(2,1)} %source.2, ...), custom_call_target="tpu_custom_call" | custom-call | tf_op jit(solution)/shard_map/split_particles/pallas_call | solution.py:111
  2.1 2.0 %collective-permute-start.1 = (bf16[32,8320]{1,0:T(8,128)(2,1)S(1)}, bf16[32,8320]{1,0:T(8,128)(2,1)S(1)}, u32[]{:S(2)}, u32[]{:S(2)}) collective-permute-start(bf16[32,8320]{1,0:T(8,128)(2,1)S(1)} %get-tuple-element.59.after), channel_id=1, source_target_pairs={{0,2},{1,3},{2,0},{3,1},{4,6},{5,7},{6,4},{7,5},{8,10},{9,11},{10,... | collective-permute-start | bytes 1597448 | tf_op jit(solution)/shard_map/ppermute | solution.py:63
  5.7 3.0 %collective-permute-start.3 = (bf16[16,8192]{1,0:T(8,128)(2,1)S(1)}, bf16[16,8192]{1,0:T(8,128)(2,1)S(1)}, u32[]{:S(2)}, u32[]{:S(2)}) collective-permute-start(bf16[16,8192]{1,0:T(8,128)(2,1)S(1)} %own_references.1.refs_8_.refs_10_), channel_id=1, source_target_pairs={{0,192},{1,193},{2,194},{3,195},{4,196},{5,197},{6,198},{7,199},{8... | collective-permute-start | bytes 786440 | tf_op jit(solution)/shard_map/ppermute | solution.py:63
  8.9 5.5 %phase_table.1 = (bf16[256,8192]{1,0:T(8,128)(2,1)S(1)}, f32[4,8,1024]{2,1,0:T(8,128)S(1)}) custom-call(s32[1]{0:T(128)} %bitcast.1.member_ref.refs_0_, f32[16,8,1024]{2,1,0:T(8,128)} %constant.63.clone.geo_ref), custom_call_target="tpu_custom_call" | custom-call | tf_op jit(solution)/shard_map/phase_table/pallas_call | solution.py:111
  14.4 2.3 %shifted_rows.4 = (bf16[256,8192]{1,0:T(8,128)(2,1)S(1)}, bf16[32,4096]{1,0:T(8,128)(2,1)S(1)}) custom-call(s32[1]{0:T(128)} %bitcast.1.member_ref.refs_0_, bf16[32,8320]{1,0:T(8,128)(2,1)S(1)} %get-tuple-element.54.x_ref, f32[4,8,1024]{2,1,0:T(8,128)S(1)} %get-tuple-element.55.geo_ref, bf16[256,8192]{1,0:T(8,128)(2,1)S(1)} %get-tuple-element.56.table_ref), custom_call_target="tpu_custom_call" | custom-call | tf_op jit(solution)/shard_map/shifted_rows/pallas_call | solution.py:111
  17.8 3.1 %collective-permute-start.7 = (bf16[16,8192]{1,0:T(8,128)(2,1)S(1)}, bf16[16,8192]{1,0:T(8,128)(2,1)S(1)}, u32[]{:S(2)}, u32[]{:S(2)}) collective-permute-start(bf16[16,8192]{1,0:T(8,128)(2,1)S(1)} %relay.1), channel_id=1, source_target_pairs={{0,192},{1,65},{2,194},{3,67},{4,196},{5,69},{6,198},{7,71},{8,200... | collective-permute-start | bytes 786440 | tf_op jit(solution)/shard_map/ppermute | solution.py:63
  22.4 1.9 %collective-permute-start.9 = (bf16[16,8192]{1,0:T(8,128)(2,1)S(1)}, bf16[16,8192]{1,0:T(8,128)(2,1)S(1)}, u32[]{:S(2)}, u32[]{:S(2)}) collective-permute-start(bf16[16,8192]{1,0:T(8,128)(2,1)S(1)} %collective-permute-done.3.other.refs_7_.refs_9_), channel_id=1, source_target_pairs={{0,48},{1,49},{2,50},{3,51},{4,52},{5,53},{6,54},{7,55},{8,56},{9,... | collective-permute-start | bytes 786440 | tf_op jit(solution)/shard_map/ppermute | solution.py:63
  24.3 2.3 %shifted_rows.5 = (bf16[256,8192]{1,0:T(8,128)(2,1)S(1)}, bf16[32,4096]{1,0:T(8,128)(2,1)S(1)}) custom-call(s32[1]{0:T(128)} %bitcast.1.member_ref.refs_0_, bf16[32,8320]{1,0:T(8,128)(2,1)S(1)} %collective-permute-done.1.x_ref, f32[4,8,1024]{2,1,0:T(8,128)S(1)} %get-tuple-element.55.geo_ref, bf16[256,8192]{1,0:T(8,128)(2,1)S(1)} %get-tuple-element.56.table_ref), custom_call_target="tpu_custom_call" | custom-call | tf_op jit(solution)/shard_map/shifted_rows/pallas_call | solution.py:111
  26.6 2.3 %shifted_rows.6 = (bf16[256,8192]{1,0:T(8,128)(2,1)S(1)}, bf16[32,4096]{1,0:T(8,128)(2,1)S(1)}) custom-call(s32[1]{0:T(128)} %bitcast.1.member_ref.refs_0_, bf16[32,8320]{1,0:T(8,128)(2,1)S(1)} %collective-permute-done.x_ref, f32[4,8,1024]{2,1,0:T(8,128)S(1)} %get-tuple-element.55.geo_ref, bf16[256,8192]{1,0:T(8,128)(2,1)S(1)} %get-tuple-element.56.table_ref), custom_call_target="tpu_custom_call" | custom-call | tf_op jit(solution)/shard_map/shifted_rows/pallas_call | solution.py:111
  28.9 1.6 %collective-permute-done.7.other = bf16[16,8192]{1,0:T(8,128)(2,1)S(1)} collective-permute-done((bf16[16,8192]{1,0:T(8,128)(2,1)S(1)}, bf16[16,8192]{1,0:T(8,128)(2,1)S(1)}, u32[]{:S(2)}, u32[]{:S(2)}) %collective-permute-start.7) | collective-permute-done | bytes 262176 | tf_op jit(solution)/shard_map/ppermute | solution.py:63
  31.8 1.6 %partial_scores.3 = (f32[256,128]{1,0:T(8,128)S(1)}, bf16[128,4096]{1,0:T(8,128)(2,1)S(1)}) custom-call(bf16[256,8192]{1,0:T(8,128)(2,1)S(1)} %get-tuple-element.61.refs_0_.refs_4_, bf16[32,4096]{1,0:T(8,128)(2,1)S(1)} %get-tuple-element.67.refs_1_, bf16[32,8192]{1,0:T(8,128)(2,1)S(1)} %pair.1.refs_2_.refs_4_, ...), custom_call_target="tpu_custom_call" | custom-call | tf_op jit(solution)/shard_map/partial_scores/pallas_call | solution.py:111
  34.2 2.3 %shifted_rows.7 = (bf16[256,8192]{1,0:T(8,128)(2,1)S(1)}, bf16[32,4096]{1,0:T(8,128)(2,1)S(1)}) custom-call(s32[1]{0:T(128)} %bitcast.1.member_ref.refs_0_, bf16[32,8320]{1,0:T(8,128)(2,1)S(1)} %collective-permute-done.5.x_ref, f32[4,8,1024]{2,1,0:T(8,128)S(1)} %get-tuple-element.55.geo_ref, bf16[256,8192]{1,0:T(8,128)(2,1)S(1)} %get-tuple-element.56.table_ref), custom_call_target="tpu_custom_call" | custom-call | tf_op jit(solution)/shard_map/shifted_rows/pallas_call | solution.py:111
  36.6 1.5 %partial_scores.4 = f32[256,128]{1,0:T(8,128)S(1)} custom-call(bf16[256,8192]{1,0:T(8,128)(2,1)S(1)} %get-tuple-element.74.refs_0_.refs_5_, bf16[32,4096]{1,0:T(8,128)(2,1)S(1)} %get-tuple-element.77.refs_1_, bf16[32,8192]{1,0:T(8,128)(2,1)S(1)} %pair.1.refs_2_.refs_4_, bf16[16,8192]{1,0:T(8,128)(2,1)S(1)} %collective-permute-done.8.refs_3_.refs_5_, ...), custom_call_target="tpu_custom_call" | custom-call | tf_op jit(solution)/shard_map/partial_scores/pallas_call | solution.py:111
  39.1 2.7 %partial_scores.5 = (f32[256,128]{1,0:T(8,128)S(1)}, f32[256,128]{1,0:T(8,128)S(1)}) custom-call(bf16[256,8192]{1,0:T(8,128)(2,1)S(1)} %get-tuple-element.57.refs_0_.refs_2_, bf16[256,8192]{1,0:T(8,128)(2,1)S(1)} %get-tuple-element.63.refs_1_.refs_3_, bf16[32,4096]{1,0:T(8,128)(2,1)S(1)} %get-tuple-element.79.refs_2_, ...), custom_call_target="tpu_custom_call" | custom-call | tf_op jit(solution)/shard_map/partial_scores/pallas_call | solution.py:111
  42.3 1.6 %collective-permute-done.11.refs_2_ = f32[256,128]{1,0:T(8,128)S(1)} collective-permute-done((f32[256,128]{1,0:T(8,128)S(1)}, f32[256,128]{1,0:T(8,128)S(1)}, u32[]{:S(2)}, u32[]{:S(2)}) %collective-permute-start.11) | collective-permute-done | bytes 131104 | tf_op jit(solution)/shard_map/ppermute | solution.py:63
  46.5 2.2 %collective-permute-done.15.refs_9_ = bf16[128,256]{1,0:T(8,128)(2,1)S(1)} collective-permute-done((bf16[128,256]{1,0:T(8,128)(2,1)S(1)}, bf16[128,256]{1,0:T(8,128)(2,1)S(1)}, u32[]{:S(2)}, u32[]{:S(2)}) %collective-permute-start.15) | collective-permute-done | bytes 65568 | tf_op jit(solution)/shard_map/ppermute | solution.py:63
  48.7 1.7 %collective-permute-done.14.refs_8_ = bf16[128,256]{1,0:T(8,128)(2,1)S(1)} collective-permute-done((bf16[128,256]{1,0:T(8,128)(2,1)S(1)}, bf16[128,256]{1,0:T(8,128)(2,1)S(1)}, u32[]{:S(2)}, u32[]{:S(2)}) %collective-permute-start.14) | collective-permute-done | bytes 65568 | tf_op jit(solution)/shard_map/ppermute | solution.py:63
  50.4 1.4 %weighted_sums.3 = (bf16[64,2048]{1,0:T(8,128)(2,1)S(1)}, bf16[64,2048]{1,0:T(8,128)(2,1)S(1)}, bf16[64,2048]{1,0:T(8,128)(2,1)S(1)}, bf16[64,2048]{1,0:T(8,128)(2,1)S(1)}) custom-call(s32[1]{0:T(128)} %bitcast.1.member_ref.refs_0_, s32[1]{0:T(128)} %bitcast.2.x_ref.refs_1_, bf16[256,8192]{1,0:T(8,128)(2,1)S(1)} %get-tuple-element.57.refs_0_.refs_2_, ...), custom_call_target="tpu_custom_call" | custom-call | tf_op jit(solution)/shard_map/weighted_sums/pallas_call | solution.py:111
  51.8 2.6 %collective-permute-start.22 = (bf16[64,2048]{1,0:T(8,128)(2,1)S(1)}, bf16[64,2048]{1,0:T(8,128)(2,1)S(1)}, u32[]{:S(2)}, u32[]{:S(2)}) collective-permute-start(bf16[64,2048]{1,0:T(8,128)(2,1)S(1)} %get-tuple-element.92), channel_id=1, source_target_pairs={{0,16},{1,129},{2,18},{3,131},{4,20},{5,133},{6,22},{7,135},{8,24}... | collective-permute-start | bytes 786440 | tf_op jit(solution)/shard_map/ppermute | solution.py:63
  56.0 1.4 %weighted_sums.2 = (bf16[64,2048]{1,0:T(8,128)(2,1)S(1)}, bf16[64,2048]{1,0:T(8,128)(2,1)S(1)}, bf16[64,2048]{1,0:T(8,128)(2,1)S(1)}, bf16[64,2048]{1,0:T(8,128)(2,1)S(1)}) custom-call(s32[1]{0:T(128)} %bitcast.1.member_ref.refs_0_, s32[1]{0:T(128)} %bitcast.2.x_ref.refs_1_, bf16[256,8192]{1,0:T(8,128)(2,1)S(1)} %get-tuple-element.57.refs_0_.refs_2_, ...), custom_call_target="tpu_custom_call" | custom-call | tf_op jit(solution)/shard_map/weighted_sums/pallas_call | solution.py:111
  57.5 1.3 %collective-permute-start.16 = (bf16[64,2048]{1,0:T(8,128)(2,1)S(1)}, bf16[64,2048]{1,0:T(8,128)(2,1)S(1)}, u32[]{:S(2)}, u32[]{:S(2)}) collective-permute-start(bf16[64,2048]{1,0:T(8,128)(2,1)S(1)} %get-tuple-element.84), channel_id=1, source_target_pairs={{0,128},{1,17},{2,130},{3,19},{4,132},{5,21},{6,134},{7,23},{8,136... | collective-permute-start | bytes 786440 | tf_op jit(solution)/shard_map/ppermute | solution.py:63
  58.8 1.9 %collective-permute-start.17 = (bf16[64,2048]{1,0:T(8,128)(2,1)S(1)}, bf16[64,2048]{1,0:T(8,128)(2,1)S(1)}, u32[]{:S(2)}, u32[]{:S(2)}) collective-permute-start(bf16[64,2048]{1,0:T(8,128)(2,1)S(1)} %get-tuple-element.85), channel_id=1, source_target_pairs={{0,64},{1,33},{2,66},{3,35},{4,68},{5,37},{6,70},{7,39},{8,72},{9,... | collective-permute-start | bytes 786440 | tf_op jit(solution)/shard_map/ppermute | solution.py:63
  60.7 1.5 %collective-permute-start.18 = (bf16[64,2048]{1,0:T(8,128)(2,1)S(1)}, bf16[64,2048]{1,0:T(8,128)(2,1)S(1)}, u32[]{:S(2)}, u32[]{:S(2)}) collective-permute-start(bf16[64,2048]{1,0:T(8,128)(2,1)S(1)} %get-tuple-element.86), channel_id=1, source_target_pairs={{0,192},{1,49},{2,194},{3,51},{4,196},{5,53},{6,198},{7,55},{8,200... | collective-permute-start | bytes 786440 | tf_op jit(solution)/shard_map/ppermute | solution.py:63
  62.2 2.4 %collective-permute-done.23.refs_4_ = bf16[64,2048]{1,0:T(8,128)(2,1)S(1)} collective-permute-done((bf16[64,2048]{1,0:T(8,128)(2,1)S(1)}, bf16[64,2048]{1,0:T(8,128)(2,1)S(1)}, u32[]{:S(2)}, u32[]{:S(2)}) %collective-permute-start.23) | collective-permute-done | bytes 262176 | tf_op jit(solution)/shard_map/ppermute | solution.py:63
  64.6 2.0 %collective-permute-done.24.refs_5_ = bf16[64,2048]{1,0:T(8,128)(2,1)S(1)} collective-permute-done((bf16[64,2048]{1,0:T(8,128)(2,1)S(1)}, bf16[64,2048]{1,0:T(8,128)(2,1)S(1)}, u32[]{:S(2)}, u32[]{:S(2)}) %collective-permute-start.24) | collective-permute-done | bytes 262176 | tf_op jit(solution)/shard_map/ppermute | solution.py:63
  67.7 2.1 %collective-permute-start.26 = (bf16[16,2048]{1,0:T(8,128)(2,1)S(1)}, bf16[16,2048]{1,0:T(8,128)(2,1)S(1)}, u32[]{:S(2)}, u32[]{:S(2)}) collective-permute-start(bf16[16,2048]{1,0:T(8,128)(2,1)S(1)} %get-tuple-element.97), channel_id=1, source_target_pairs={{0,64},{1,33},{2,66},{3,35},{4,68},{5,37},{6,70},{7,39},{8,72},{9,... | collective-permute-start | bytes 196616 | tf_op jit(solution)/shard_map/ppermute | solution.py:63
  71.0 2.4 %collective-permute-start.19 = (bf16[16,2048]{1,0:T(8,128)(2,1)S(1)}, bf16[16,2048]{1,0:T(8,128)(2,1)S(1)}, u32[]{:S(2)}, u32[]{:S(2)}) collective-permute-start(bf16[16,2048]{1,0:T(8,128)(2,1)S(1)} %get-tuple-element.88), channel_id=1, source_target_pairs={{0,16},{1,129},{2,18},{3,131},{4,20},{5,133},{6,22},{7,135},{8,24}... | collective-permute-start | bytes 196616 | tf_op jit(solution)/shard_map/ppermute | solution.py:63
  73.5 1.6 %collective-permute-start.20 = (bf16[16,2048]{1,0:T(8,128)(2,1)S(1)}, bf16[16,2048]{1,0:T(8,128)(2,1)S(1)}, u32[]{:S(2)}, u32[]{:S(2)}) collective-permute-start(bf16[16,2048]{1,0:T(8,128)(2,1)S(1)} %get-tuple-element.89), channel_id=1, source_target_pairs={{0,32},{1,65},{2,34},{3,67},{4,36},{5,69},{6,38},{7,71},{8,40},{9,... | collective-permute-start | bytes 196616 | tf_op jit(solution)/shard_map/ppermute | solution.py:63
  79.4 6.6 %collective-permute-start.28 = (bf16[16,1024]{1,0:T(8,128)(2,1)S(1)}, bf16[16,1024]{1,0:T(8,128)(2,1)S(1)}, u32[]{:S(2)}, u32[]{:S(2)}) collective-permute-start(bf16[16,1024]{1,0:T(8,128)(2,1)S(1)} %get-tuple-element.100), channel_id=1, source_target_pairs={{0,8},{1,9},{2,10},{3,11},{4,12},{5,13},{6,14},{7,15},{8,0},{9,1},... | collective-permute-start | bytes 98312 | tf_op jit(solution)/shard_map/ppermute | solution.py:63
  86.0 1.4 %collective-permute-start.29 = (bf16[16,1024]{1,0:T(8,128)(2,1)S(1)}, bf16[16,1024]{1,0:T(8,128)(2,1)S(1)}, u32[]{:S(2)}, u32[]{:S(2)}) collective-permute-start(bf16[16,1024]{1,0:T(8,128)(2,1)S(1)} %get-tuple-element.101), channel_id=1, source_target_pairs={{0,4},{1,5},{2,6},{3,7},{4,0},{5,1},{6,2},{7,3},{8,12},{9,13},{10,... | collective-permute-start | bytes 98312 | tf_op jit(solution)/shard_map/ppermute | solution.py:63
  88.0 2.8 %collective-permute-done.29 = bf16[16,1024]{1,0:T(8,128)(2,1)S(1)} collective-permute-done((bf16[16,1024]{1,0:T(8,128)(2,1)S(1)}, bf16[16,1024]{1,0:T(8,128)(2,1)S(1)}, u32[]{:S(2)}, u32[]{:S(2)}) %collective-permute-start.29) | collective-permute-done | bytes 32800 | tf_op jit(solution)/shard_map/ppermute | solution.py:63
  90.8 2.7 %collective-permute-done.30 = bf16[16,1024]{1,0:T(8,128)(2,1)S(1)} collective-permute-done((bf16[16,1024]{1,0:T(8,128)(2,1)S(1)}, bf16[16,1024]{1,0:T(8,128)(2,1)S(1)}, u32[]{:S(2)}, u32[]{:S(2)}) %collective-permute-start.30) | collective-permute-done | bytes 32800 | tf_op jit(solution)/shard_map/ppermute | solution.py:63
  (50 shorter events, 20.0 us)
Async XLA Ops:
  2.0 14.7 %collective-permute-start = (bf16[32,8320]{1,0:T(8,128)(2,1)S(1)}, bf16[32,8320]{1,0:T(8,128)(2,1)S(1)}, u32[]{:S(2)}, u32[]{:S(2)}) collective-permute-start(bf16[32,8320]{1,0:T(8,128)(2,1)S(1)} %get-tuple-element.58), channel_id=1, source_target_pairs={{0,1},{1,0},{2,3},{3,2},{4,5},{5,4},{6,7},{7,6},{8,9},{9,8},{10,11... | collective-permute-start | bytes 1597448 | tf_op jit(solution)/shard_map/ppermute | solution.py:63
  2.1 14.7 %collective-permute-start.1 = (bf16[32,8320]{1,0:T(8,128)(2,1)S(1)}, bf16[32,8320]{1,0:T(8,128)(2,1)S(1)}, u32[]{:S(2)}, u32[]{:S(2)}) collective-permute-start(bf16[32,8320]{1,0:T(8,128)(2,1)S(1)} %get-tuple-element.59.after), channel_id=1, source_target_pairs={{0,2},{1,3},{2,0},{3,1},{4,6},{5,7},{6,4},{7,5},{8,10},{9,11},{10,... | collective-permute-start | bytes 1597448 | tf_op jit(solution)/shard_map/ppermute | solution.py:63
  5.1 11.6 %collective-permute-start.4 = (bf16[16,8192]{1,0:T(8,128)(2,1)S(1)}, bf16[16,8192]{1,0:T(8,128)(2,1)S(1)}, u32[]{:S(2)}, u32[]{:S(2)}) collective-permute-start(bf16[16,8192]{1,0:T(8,128)(2,1)S(1)} %own_references.1.refs_8_.refs_10_), channel_id=1, source_target_pairs={{0,32},{1,33},{2,34},{3,35},{4,36},{5,37},{6,38},{7,39},{8,40},{9,... | collective-permute-start | bytes 786440 | tf_op jit(solution)/shard_map/ppermute | solution.py:63
  5.7 11.0 %collective-permute-start.3 = (bf16[16,8192]{1,0:T(8,128)(2,1)S(1)}, bf16[16,8192]{1,0:T(8,128)(2,1)S(1)}, u32[]{:S(2)}, u32[]{:S(2)}) collective-permute-start(bf16[16,8192]{1,0:T(8,128)(2,1)S(1)} %own_references.1.refs_8_.refs_10_), channel_id=1, source_target_pairs={{0,192},{1,193},{2,194},{3,195},{4,196},{5,197},{6,198},{7,199},{8... | collective-permute-start | bytes 786440 | tf_op jit(solution)/shard_map/ppermute | solution.py:63
  8.7 8.0 %collective-permute-start.2 = (bf16[16,8192]{1,0:T(8,128)(2,1)S(1)}, bf16[16,8192]{1,0:T(8,128)(2,1)S(1)}, u32[]{:S(2)}, u32[]{:S(2)}) collective-permute-start(bf16[16,8192]{1,0:T(8,128)(2,1)S(1)} %own_references.1.refs_8_.refs_10_), channel_id=1, source_target_pairs={{0,64},{1,65},{2,66},{3,67},{4,68},{5,69},{6,70},{7,71},{8,72},{9,... | collective-permute-start | bytes 786440 | tf_op jit(solution)/shard_map/ppermute | solution.py:63
  16.8 17.4 %collective-permute-start.5 = (bf16[32,8320]{1,0:T(8,128)(2,1)S(1)}, bf16[32,8320]{1,0:T(8,128)(2,1)S(1)}, u32[]{:S(2)}, u32[]{:S(2)}) collective-permute-start(bf16[32,8320]{1,0:T(8,128)(2,1)S(1)} %get-tuple-element.65), channel_id=1, source_target_pairs={{0,3},{1,2},{2,1},{3,0},{4,7},{5,6},{6,5},{7,4},{8,11},{9,10},{10,... | collective-permute-start | bytes 1597448 | tf_op jit(solution)/shard_map/ppermute | solution.py:63
  17.8 12.6 %collective-permute-start.7 = (bf16[16,8192]{1,0:T(8,128)(2,1)S(1)}, bf16[16,8192]{1,0:T(8,128)(2,1)S(1)}, u32[]{:S(2)}, u32[]{:S(2)}) collective-permute-start(bf16[16,8192]{1,0:T(8,128)(2,1)S(1)} %relay.1), channel_id=1, source_target_pairs={{0,192},{1,65},{2,194},{3,67},{4,196},{5,69},{6,198},{7,71},{8,200... | collective-permute-start | bytes 786440 | tf_op jit(solution)/shard_map/ppermute | solution.py:63
  20.9 10.8 %collective-permute-start.6 = (bf16[16,8192]{1,0:T(8,128)(2,1)S(1)}, bf16[16,8192]{1,0:T(8,128)(2,1)S(1)}, u32[]{:S(2)}, u32[]{:S(2)}) collective-permute-start(bf16[16,8192]{1,0:T(8,128)(2,1)S(1)} %collective-permute-done.4.refs_5_.refs_7_), channel_id=1, source_target_pairs={{0,128},{1,129},{2,130},{3,131},{4,132},{5,133},{6,134},{7,135},{8... | collective-permute-start | bytes 786440 | tf_op jit(solution)/shard_map/ppermute | solution.py:63
  21.6 10.2 %collective-permute-start.8 = (bf16[16,8192]{1,0:T(8,128)(2,1)S(1)}, bf16[16,8192]{1,0:T(8,128)(2,1)S(1)}, u32[]{:S(2)}, u32[]{:S(2)}) collective-permute-start(bf16[16,8192]{1,0:T(8,128)(2,1)S(1)} %collective-permute-done.2.one.refs_6_.refs_8_), channel_id=1, source_target_pairs={{0,32},{1,33},{2,34},{3,35},{4,36},{5,37},{6,38},{7,39},{8,40},{9,... | collective-permute-start | bytes 786440 | tf_op jit(solution)/shard_map/ppermute | solution.py:63
  22.4 9.3 %collective-permute-start.9 = (bf16[16,8192]{1,0:T(8,128)(2,1)S(1)}, bf16[16,8192]{1,0:T(8,128)(2,1)S(1)}, u32[]{:S(2)}, u32[]{:S(2)}) collective-permute-start(bf16[16,8192]{1,0:T(8,128)(2,1)S(1)} %collective-permute-done.3.other.refs_7_.refs_9_), channel_id=1, source_target_pairs={{0,48},{1,49},{2,50},{3,51},{4,52},{5,53},{6,54},{7,55},{8,56},{9,... | collective-permute-start | bytes 786440 | tf_op jit(solution)/shard_map/ppermute | solution.py:63
  33.4 9.0 %collective-permute-start.10 = (f32[256,128]{1,0:T(8,128)S(1)}, f32[256,128]{1,0:T(8,128)S(1)}, u32[]{:S(2)}, u32[]{:S(2)}) collective-permute-start(f32[256,128]{1,0:T(8,128)S(1)} %get-tuple-element.72), channel_id=1, source_target_pairs={{0,2},{1,3},{2,0},{3,1},{4,6},{5,7},{6,4},{7,5},{8,10},{9,11},{10,... | collective-permute-start | bytes 393224 | tf_op jit(solution)/shard_map/ppermute | solution.py:63
  38.1 5.9 %collective-permute-start.11 = (f32[256,128]{1,0:T(8,128)S(1)}, f32[256,128]{1,0:T(8,128)S(1)}, u32[]{:S(2)}, u32[]{:S(2)}) collective-permute-start(f32[256,128]{1,0:T(8,128)S(1)} %partial_scores.4), channel_id=1, source_target_pairs={{0,3},{1,2},{2,1},{3,0},{4,7},{5,6},{6,5},{7,4},{8,11},{9,10},{10,... | collective-permute-start | bytes 393224 | tf_op jit(solution)/shard_map/ppermute | solution.py:63
  41.8 2.2 %collective-permute-start.12 = (f32[256,128]{1,0:T(8,128)S(1)}, f32[256,128]{1,0:T(8,128)S(1)}, u32[]{:S(2)}, u32[]{:S(2)}) collective-permute-start(f32[256,128]{1,0:T(8,128)S(1)} %get-tuple-element.82), channel_id=1, source_target_pairs={{0,1},{1,0},{2,3},{3,2},{4,5},{5,4},{6,7},{7,6},{8,9},{9,8},{10,11... | collective-permute-start | bytes 393224 | tf_op jit(solution)/shard_map/ppermute | solution.py:63
  44.3 4.4 %collective-permute-start.15 = (bf16[128,256]{1,0:T(8,128)(2,1)S(1)}, bf16[128,256]{1,0:T(8,128)(2,1)S(1)}, u32[]{:S(2)}, u32[]{:S(2)}) collective-permute-start(bf16[128,256]{1,0:T(8,128)(2,1)S(1)} %posterior.1.refs_6_), channel_id=1, source_target_pairs={{0,3},{1,2},{2,1},{3,0},{4,7},{5,6},{6,5},{7,4},{8,11},{9,10},{10,... | collective-permute-start | bytes 196616 | tf_op jit(solution)/shard_map/ppermute | solution.py:63
  45.3 5.1 %collective-permute-start.14 = (bf16[128,256]{1,0:T(8,128)(2,1)S(1)}, bf16[128,256]{1,0:T(8,128)(2,1)S(1)}, u32[]{:S(2)}, u32[]{:S(2)}) collective-permute-start(bf16[128,256]{1,0:T(8,128)(2,1)S(1)} %posterior.1.refs_6_), channel_id=1, source_target_pairs={{0,2},{1,3},{2,0},{3,1},{4,6},{5,7},{6,4},{7,5},{8,10},{9,11},{10,... | collective-permute-start | bytes 196616 | tf_op jit(solution)/shard_map/ppermute | solution.py:63
  46.3 4.1 %collective-permute-start.13 = (bf16[128,256]{1,0:T(8,128)(2,1)S(1)}, bf16[128,256]{1,0:T(8,128)(2,1)S(1)}, u32[]{:S(2)}, u32[]{:S(2)}) collective-permute-start(bf16[128,256]{1,0:T(8,128)(2,1)S(1)} %posterior.1.refs_6_), channel_id=1, source_target_pairs={{0,1},{1,0},{2,3},{3,2},{4,5},{5,4},{6,7},{7,6},{8,9},{9,8},{10,11... | collective-permute-start | bytes 196616 | tf_op jit(solution)/shard_map/ppermute | solution.py:63
  51.8 8.9 %collective-permute-start.22 = (bf16[64,2048]{1,0:T(8,128)(2,1)S(1)}, bf16[64,2048]{1,0:T(8,128)(2,1)S(1)}, u32[]{:S(2)}, u32[]{:S(2)}) collective-permute-start(bf16[64,2048]{1,0:T(8,128)(2,1)S(1)} %get-tuple-element.92), channel_id=1, source_target_pairs={{0,16},{1,129},{2,18},{3,131},{4,20},{5,133},{6,22},{7,135},{8,24}... | collective-permute-start | bytes 786440 | tf_op jit(solution)/shard_map/ppermute | solution.py:63
  54.4 10.1 %collective-permute-start.23 = (bf16[64,2048]{1,0:T(8,128)(2,1)S(1)}, bf16[64,2048]{1,0:T(8,128)(2,1)S(1)}, u32[]{:S(2)}, u32[]{:S(2)}) collective-permute-start(bf16[64,2048]{1,0:T(8,128)(2,1)S(1)} %get-tuple-element.93), channel_id=1, source_target_pairs={{0,32},{1,65},{2,34},{3,67},{4,36},{5,69},{6,38},{7,71},{8,40},{9,... | collective-permute-start | bytes 786440 | tf_op jit(solution)/shard_map/ppermute | solution.py:63
  55.5 11.1 %collective-permute-start.24 = (bf16[64,2048]{1,0:T(8,128)(2,1)S(1)}, bf16[64,2048]{1,0:T(8,128)(2,1)S(1)}, u32[]{:S(2)}, u32[]{:S(2)}) collective-permute-start(bf16[64,2048]{1,0:T(8,128)(2,1)S(1)} %get-tuple-element.94), channel_id=1, source_target_pairs={{0,48},{1,193},{2,50},{3,195},{4,52},{5,197},{6,54},{7,199},{8,56}... | collective-permute-start | bytes 786440 | tf_op jit(solution)/shard_map/ppermute | solution.py:63
  57.5 12.3 %collective-permute-start.16 = (bf16[64,2048]{1,0:T(8,128)(2,1)S(1)}, bf16[64,2048]{1,0:T(8,128)(2,1)S(1)}, u32[]{:S(2)}, u32[]{:S(2)}) collective-permute-start(bf16[64,2048]{1,0:T(8,128)(2,1)S(1)} %get-tuple-element.84), channel_id=1, source_target_pairs={{0,128},{1,17},{2,130},{3,19},{4,132},{5,21},{6,134},{7,23},{8,136... | collective-permute-start | bytes 786440 | tf_op jit(solution)/shard_map/ppermute | solution.py:63
  58.8 12.1 %collective-permute-start.17 = (bf16[64,2048]{1,0:T(8,128)(2,1)S(1)}, bf16[64,2048]{1,0:T(8,128)(2,1)S(1)}, u32[]{:S(2)}, u32[]{:S(2)}) collective-permute-start(bf16[64,2048]{1,0:T(8,128)(2,1)S(1)} %get-tuple-element.85), channel_id=1, source_target_pairs={{0,64},{1,33},{2,66},{3,35},{4,68},{5,37},{6,70},{7,39},{8,72},{9,... | collective-permute-start | bytes 786440 | tf_op jit(solution)/shard_map/ppermute | solution.py:63
  60.7 10.2 %collective-permute-start.18 = (bf16[64,2048]{1,0:T(8,128)(2,1)S(1)}, bf16[64,2048]{1,0:T(8,128)(2,1)S(1)}, u32[]{:S(2)}, u32[]{:S(2)}) collective-permute-start(bf16[64,2048]{1,0:T(8,128)(2,1)S(1)} %get-tuple-element.86), channel_id=1, source_target_pairs={{0,192},{1,49},{2,194},{3,51},{4,196},{5,53},{6,198},{7,55},{8,200... | collective-permute-start | bytes 786440 | tf_op jit(solution)/shard_map/ppermute | solution.py:63
  66.7 8.4 %collective-permute-start.25 = (bf16[16,2048]{1,0:T(8,128)(2,1)S(1)}, bf16[16,2048]{1,0:T(8,128)(2,1)S(1)}, u32[]{:S(2)}, u32[]{:S(2)}) collective-permute-start(bf16[16,2048]{1,0:T(8,128)(2,1)S(1)} %get-tuple-element.96), channel_id=1, source_target_pairs={{0,128},{1,17},{2,130},{3,19},{4,132},{5,21},{6,134},{7,23},{8,136... | collective-permute-start | bytes 196616 | tf_op jit(solution)/shard_map/ppermute | solution.py:63
  67.7 7.5 %collective-permute-start.26 = (bf16[16,2048]{1,0:T(8,128)(2,1)S(1)}, bf16[16,2048]{1,0:T(8,128)(2,1)S(1)}, u32[]{:S(2)}, u32[]{:S(2)}) collective-permute-start(bf16[16,2048]{1,0:T(8,128)(2,1)S(1)} %get-tuple-element.97), channel_id=1, source_target_pairs={{0,64},{1,33},{2,66},{3,35},{4,68},{5,37},{6,70},{7,39},{8,72},{9,... | collective-permute-start | bytes 196616 | tf_op jit(solution)/shard_map/ppermute | solution.py:63
  69.8 5.8 %collective-permute-start.27 = (bf16[16,2048]{1,0:T(8,128)(2,1)S(1)}, bf16[16,2048]{1,0:T(8,128)(2,1)S(1)}, u32[]{:S(2)}, u32[]{:S(2)}) collective-permute-start(bf16[16,2048]{1,0:T(8,128)(2,1)S(1)} %get-tuple-element.98), channel_id=1, source_target_pairs={{0,192},{1,49},{2,194},{3,51},{4,196},{5,53},{6,198},{7,55},{8,200... | collective-permute-start | bytes 196616 | tf_op jit(solution)/shard_map/ppermute | solution.py:63
  71.0 5.9 %collective-permute-start.19 = (bf16[16,2048]{1,0:T(8,128)(2,1)S(1)}, bf16[16,2048]{1,0:T(8,128)(2,1)S(1)}, u32[]{:S(2)}, u32[]{:S(2)}) collective-permute-start(bf16[16,2048]{1,0:T(8,128)(2,1)S(1)} %get-tuple-element.88), channel_id=1, source_target_pairs={{0,16},{1,129},{2,18},{3,131},{4,20},{5,133},{6,22},{7,135},{8,24}... | collective-permute-start | bytes 196616 | tf_op jit(solution)/shard_map/ppermute | solution.py:63
  73.5 4.6 %collective-permute-start.20 = (bf16[16,2048]{1,0:T(8,128)(2,1)S(1)}, bf16[16,2048]{1,0:T(8,128)(2,1)S(1)}, u32[]{:S(2)}, u32[]{:S(2)}) collective-permute-start(bf16[16,2048]{1,0:T(8,128)(2,1)S(1)} %get-tuple-element.89), channel_id=1, source_target_pairs={{0,32},{1,65},{2,34},{3,67},{4,36},{5,69},{6,38},{7,71},{8,40},{9,... | collective-permute-start | bytes 196616 | tf_op jit(solution)/shard_map/ppermute | solution.py:63
  75.1 4.3 %collective-permute-start.21 = (bf16[16,2048]{1,0:T(8,128)(2,1)S(1)}, bf16[16,2048]{1,0:T(8,128)(2,1)S(1)}, u32[]{:S(2)}, u32[]{:S(2)}) collective-permute-start(bf16[16,2048]{1,0:T(8,128)(2,1)S(1)} %get-tuple-element.90), channel_id=1, source_target_pairs={{0,48},{1,193},{2,50},{3,195},{4,52},{5,197},{6,54},{7,199},{8,56}... | collective-permute-start | bytes 196616 | tf_op jit(solution)/shard_map/ppermute | solution.py:63
  79.4 8.6 %collective-permute-start.28 = (bf16[16,1024]{1,0:T(8,128)(2,1)S(1)}, bf16[16,1024]{1,0:T(8,128)(2,1)S(1)}, u32[]{:S(2)}, u32[]{:S(2)}) collective-permute-start(bf16[16,1024]{1,0:T(8,128)(2,1)S(1)} %get-tuple-element.100), channel_id=1, source_target_pairs={{0,8},{1,9},{2,10},{3,11},{4,12},{5,13},{6,14},{7,15},{8,0},{9,1},... | collective-permute-start | bytes 98312 | tf_op jit(solution)/shard_map/ppermute | solution.py:63
  86.0 4.8 %collective-permute-start.29 = (bf16[16,1024]{1,0:T(8,128)(2,1)S(1)}, bf16[16,1024]{1,0:T(8,128)(2,1)S(1)}, u32[]{:S(2)}, u32[]{:S(2)}) collective-permute-start(bf16[16,1024]{1,0:T(8,128)(2,1)S(1)} %get-tuple-element.101), channel_id=1, source_target_pairs={{0,4},{1,5},{2,6},{3,7},{4,0},{5,1},{6,2},{7,3},{8,12},{9,13},{10,... | collective-permute-start | bytes 98312 | tf_op jit(solution)/shard_map/ppermute | solution.py:63
  87.5 6.0 %collective-permute-start.30 = (bf16[16,1024]{1,0:T(8,128)(2,1)S(1)}, bf16[16,1024]{1,0:T(8,128)(2,1)S(1)}, u32[]{:S(2)}, u32[]{:S(2)}) collective-permute-start(bf16[16,1024]{1,0:T(8,128)(2,1)S(1)} %get-tuple-element.102), channel_id=1, source_target_pairs={{0,12},{1,13},{2,14},{3,15},{4,8},{5,9},{6,10},{7,11},{8,4},{9,5},... | collective-permute-start | bytes 98312 | tf_op jit(solution)/shard_map/ppermute | solution.py:63

commit v15 on v14

--- a/solution.py
+++ b/solution.py
@@ -131,7 +131,7 @@
     ]
     for copy in copies:
         copy.start()
-    ids = lax.broadcasted_iota(jnp.int32, (128, 1), 0).astype(F32)
+    ids = lax.broadcasted_iota(jnp.int32, (64, 1), 0).astype(F32)
     high = jnp.floor((ids + 0.5) * (1 / 25))
     middle = jnp.floor((ids - 25 * high + 0.5) * (1 / 5))
     low = ids - 25 * high - 5 * middle
@@ -139,7 +139,7 @@
     for copy in copies:
         copy.wait()
 
-    @pl.loop(0, NB)
+    @pl.loop(0, NB, unroll=True)
     def _(block):
         geo = picked_ref[block]
         for tilt in range(2):
@@ -153,9 +153,11 @@
             for at, values in enumerate((cosine, sine)):
                 high = values.astype(BF16)
                 low = (values - high.astype(F32)).astype(BF16)
-                spot = pl.multiple_of(block * 2 * COLS + tilt * COLS + at * HALF, HALF)
-                out_ref[0:128, pl.ds(spot, HALF)] = high
-                out_ref[128:256, pl.ds(spot, HALF)] = low
+                spot = pl.ds(pl.multiple_of(block * 2 * COLS + tilt * COLS + at * HALF, HALF), HALF)
+                out_ref[0:64, spot] = high
+                out_ref[64:128, spot] = -high if at else high
+                out_ref[128:192, spot] = low
+                out_ref[192:256, spot] = -low if at else low
 
 
 def make_table(member, geo):
@@ -276,6 +278,7 @@
     info = x_ref[:, WIDTH:].astype(F32)
     lane = lax.broadcasted_iota(jnp.int32, (ROWS, 256), 1) & 127
     ids = jnp.concatenate([info[:, s : s + 1] for s in range(SHIFTS)], axis=0)
+    ids = jnp.where(ids > 62.5, 188.0 - ids, ids)
     pick = (ids == lane.astype(F32)).astype(BF16)
     sigma = sum(info[:, SHIFTS + n : SHIFTS + n + 1] for n in range(3))
     small = lax.broadcasted_iota(jnp.int32, (P_DEV, 128), 1)
@@ -462,7 +465,8 @@
     gathered[0, 1] = send(own, flips(x=1))
     table, geo = make_table(member, geo)
     rows[0], pens[0] = make_rows(member, chunks[0], geo, table)
-    wave = [got[1], gathered[1, 0], gathered[3, 0], gathered[0, 1], rows[0]]
+    rows[1], pens[1] = make_rows(member, after(got[1], rows[0]), geo, table)
+    wave = [gathered[1, 0], gathered[3, 0], gathered[0, 1], rows[1]]
     gathered[2, 1] = send(after(gathered[0, 1], *wave), flips(y=2))
     relayed = [gathered[1, 0], after(gathered[3, 0], *wave)]
     (relay,) = local(relay_kernel, "relay", [((16, WIDTH), BF16)], [member], relayed, 2)
@@ -471,12 +475,11 @@
     gathered[3, 1] = send(after(gathered[3, 0], relay), flips(x=3))
     got[3] = send(after(chunks[3], got[2], *wave), partners(3))
     rows[2], pens[2] = make_rows(member, after(got[2], *wave), geo, table)
-    rows[1], pens[1] = make_rows(member, after(got[1], rows[2]), geo, table)
     far = [gathered[2, 1], gathered[2, 0]]
     (gathered[2, 0],) = local(pair_kernel, "pair", [((32, WIDTH), BF16)], [], far, 2)
     blocks = [gathered[at] for at in ARRIVAL]
 
-    second, power = make_scores([rows[2]], [after(pens[2], rows[1])], blocks)
+    second, power = make_scores([rows[2]], [pens[2]], blocks)
     rows[3], pens[3] = make_rows(member, after(got[3], second), geo, table)
     (third,) = make_scores([rows[3]], [after(pens[3], second)], blocks, power)
     mine, other = make_scores([rows[0], rows[1]], [after(pens[0], third), pens[1]], blocks, power)

time: 94.8 us -> 94.7 us (level)
  waiting for transfers between devices: 23 us -> 25.9 us
  Pallas kernels: 27.1 us -> 24.3 us
    ppermute x31, waiting for transfers between devices: 23 us -> 25.9 us  [send(): return lax.ppermute(value, AXES, pairs)]
    pallas_call x19, Pallas kernels: 27.1 us -> 24.3 us  [local(): pl.pallas_call(kernel, in_specs=[SCALARS] * len(scalars) + [PLACED] * pla...]
  transfers between devices with their start and end apart: 31 -> 31, of which waited for: 15 -> 16; matrix products, arithmetic and copies ran while one was open for 0% -> 0% of each run, Pallas kernels for 25% -> 22%
where the time goes in v15:
time: 94.7 us; the launch traced here: 93.9 us
  starting transfers between devices  42.9 us (45%)
  waiting for transfers between devices  25.9 us (27%)
  Pallas kernels  24.3 us (26%)
    ppermute x31, starting transfers between devices, send(): return lax.ppermute(value, AXES, pairs)  42.9 us
    ppermute x31, waiting for transfers between devices, send(): return lax.ppermute(value, AXES, pairs)  25.9 us
    pallas_call x19, Pallas kernels, local(): pl.pallas_call(kernel, in_specs=[SCALARS] * len(scalars) + [PLACED] * pla...  24.3 us
  transfers between devices with their start and end apart: 31, of which 16 were waited for; matrix products, arithmetic and copies ran while one was open for 0% of the time, Pallas kernels for 22%

profile of v15, /device:TPU:2, one launch (start us, length us, event | category | flops | bytes accessed | tf_op | source)
XLA Modules:
  0.0 93.9 jit_solution(2564234745731097698)
XLA Ops:
  0.0 2.0 %split_particles.1 = (bf16[32,8320]{1,0:T(8,128)(2,1)S(1)}, bf16[32,8320]{1,0:T(8,128)(2,1)S(1)}, bf16[32,8320]{1,0:T(8,128)(2,1)S(1)}, bf16[32,8320]{1,0:T(8,128)(2,1)S(1)}) custom-call(s32[1]{0:T(128)} %bitcast.1.member_ref.refs_0_, s32[1]{0:T(128)} %bitcast.block_ref, s32[1]{0:T(128)} %bitcast.2.x_ref.refs_1_, bf16[32,32768]{1,0:T(8,128)(2,1)} %source.2, ...), custom_call_target="tpu_custom_call" | custom-call | tf_op jit(solution)/shard_map/split_particles/pallas_call | solution.py:111
  2.1 2.0 %collective-permute-start.1 = (bf16[32,8320]{1,0:T(8,128)(2,1)S(1)}, bf16[32,8320]{1,0:T(8,128)(2,1)S(1)}, u32[]{:S(2)}, u32[]{:S(2)}) collective-permute-start(bf16[32,8320]{1,0:T(8,128)(2,1)S(1)} %get-tuple-element.60.after), channel_id=1, source_target_pairs={{0,2},{1,3},{2,0},{3,1},{4,6},{5,7},{6,4},{7,5},{8,10},{9,11},{10,... | collective-permute-start | bytes 1597448 | tf_op jit(solution)/shard_map/ppermute | solution.py:63
  5.7 3.0 %collective-permute-start.3 = (bf16[16,8192]{1,0:T(8,128)(2,1)S(1)}, bf16[16,8192]{1,0:T(8,128)(2,1)S(1)}, u32[]{:S(2)}, u32[]{:S(2)}) collective-permute-start(bf16[16,8192]{1,0:T(8,128)(2,1)S(1)} %own_references.1.refs_8_.refs_10_), channel_id=1, source_target_pairs={{0,192},{1,193},{2,194},{3,195},{4,196},{5,197},{6,198},{7,199},{8... | collective-permute-start | bytes 786440 | tf_op jit(solution)/shard_map/ppermute | solution.py:63
  8.9 2.7 %phase_table.1 = (bf16[256,8192]{1,0:T(8,128)(2,1)S(1)}, f32[4,8,1024]{2,1,0:T(8,128)S(1)}) custom-call(s32[1]{0:T(128)} %bitcast.1.member_ref.refs_0_, f32[16,8,1024]{2,1,0:T(8,128)} %constant.63.clone.geo_ref), custom_call_target="tpu_custom_call" | custom-call | tf_op jit(solution)/shard_map/phase_table/pallas_call | solution.py:111
  11.6 2.3 %shifted_rows.4 = (bf16[256,8192]{1,0:T(8,128)(2,1)S(1)}, bf16[32,4096]{1,0:T(8,128)(2,1)S(1)}) custom-call(s32[1]{0:T(128)} %bitcast.1.member_ref.refs_0_, bf16[32,8320]{1,0:T(8,128)(2,1)S(1)} %get-tuple-element.53.x_ref, f32[4,8,1024]{2,1,0:T(8,128)S(1)} %get-tuple-element.54.geo_ref, bf16[256,8192]{1,0:T(8,128)(2,1)S(1)} %get-tuple-element.55.table_ref), custom_call_target="tpu_custom_call" | custom-call | tf_op jit(solution)/shard_map/shifted_rows/pallas_call | solution.py:111
  13.9 2.3 %shifted_rows.5 = (bf16[256,8192]{1,0:T(8,128)(2,1)S(1)}, bf16[32,4096]{1,0:T(8,128)(2,1)S(1)}) custom-call(s32[1]{0:T(128)} %bitcast.1.member_ref.refs_0_, bf16[32,8320]{1,0:T(8,128)(2,1)S(1)} %collective-permute-done.x_ref, f32[4,8,1024]{2,1,0:T(8,128)S(1)} %get-tuple-element.54.geo_ref, bf16[256,8192]{1,0:T(8,128)(2,1)S(1)} %get-tuple-element.55.table_ref), custom_call_target="tpu_custom_call" | custom-call | tf_op jit(solution)/shard_map/shifted_rows/pallas_call | solution.py:111
  17.8 3.1 %collective-permute-start.7 = (bf16[16,8192]{1,0:T(8,128)(2,1)S(1)}, bf16[16,8192]{1,0:T(8,128)(2,1)S(1)}, u32[]{:S(2)}, u32[]{:S(2)}) collective-permute-start(bf16[16,8192]{1,0:T(8,128)(2,1)S(1)} %relay.1), channel_id=1, source_target_pairs={{0,192},{1,65},{2,194},{3,67},{4,196},{5,69},{6,198},{7,71},{8,200... | collective-permute-start | bytes 786440 | tf_op jit(solution)/shard_map/ppermute | solution.py:63
  22.1 2.2 %collective-permute-start.9 = (bf16[16,8192]{1,0:T(8,128)(2,1)S(1)}, bf16[16,8192]{1,0:T(8,128)(2,1)S(1)}, u32[]{:S(2)}, u32[]{:S(2)}) collective-permute-start(bf16[16,8192]{1,0:T(8,128)(2,1)S(1)} %collective-permute-done.3.other.refs_7_.refs_9_), channel_id=1, source_target_pairs={{0,48},{1,49},{2,50},{3,51},{4,52},{5,53},{6,54},{7,55},{8,56},{9,... | collective-permute-start | bytes 786440 | tf_op jit(solution)/shard_map/ppermute | solution.py:63
  24.3 2.3 %shifted_rows.6 = (bf16[256,8192]{1,0:T(8,128)(2,1)S(1)}, bf16[32,4096]{1,0:T(8,128)(2,1)S(1)}) custom-call(s32[1]{0:T(128)} %bitcast.1.member_ref.refs_0_, bf16[32,8320]{1,0:T(8,128)(2,1)S(1)} %collective-permute-done.1.x_ref, f32[4,8,1024]{2,1,0:T(8,128)S(1)} %get-tuple-element.54.geo_ref, bf16[256,8192]{1,0:T(8,128)(2,1)S(1)} %get-tuple-element.55.table_ref), custom_call_target="tpu_custom_call" | custom-call | tf_op jit(solution)/shard_map/shifted_rows/pallas_call | solution.py:111
  26.6 3.9 %collective-permute-done.7.other = bf16[16,8192]{1,0:T(8,128)(2,1)S(1)} collective-permute-done((bf16[16,8192]{1,0:T(8,128)(2,1)S(1)}, bf16[16,8192]{1,0:T(8,128)(2,1)S(1)}, u32[]{:S(2)}, u32[]{:S(2)}) %collective-permute-start.7) | collective-permute-done | bytes 262176 | tf_op jit(solution)/shard_map/ppermute | solution.py:63
  31.8 1.6 %partial_scores.3 = (f32[256,128]{1,0:T(8,128)S(1)}, bf16[128,4096]{1,0:T(8,128)(2,1)S(1)}) custom-call(bf16[256,8192]{1,0:T(8,128)(2,1)S(1)} %get-tuple-element.62.refs_0_.refs_4_, bf16[32,4096]{1,0:T(8,128)(2,1)S(1)} %get-tuple-element.65.refs_1_, bf16[32,8192]{1,0:T(8,128)(2,1)S(1)} %pair.1.refs_2_.refs_4_, ...), custom_call_target="tpu_custom_call" | custom-call | tf_op jit(solution)/shard_map/partial_scores/pallas_call | solution.py:111
  34.2 2.3 %shifted_rows.7 = (bf16[256,8192]{1,0:T(8,128)(2,1)S(1)}, bf16[32,4096]{1,0:T(8,128)(2,1)S(1)}) custom-call(s32[1]{0:T(128)} %bitcast.1.member_ref.refs_0_, bf16[32,8320]{1,0:T(8,128)(2,1)S(1)} %collective-permute-done.5.x_ref, f32[4,8,1024]{2,1,0:T(8,128)S(1)} %get-tuple-element.54.geo_ref, bf16[256,8192]{1,0:T(8,128)(2,1)S(1)} %get-tuple-element.55.table_ref), custom_call_target="tpu_custom_call" | custom-call | tf_op jit(solution)/shard_map/shifted_rows/pallas_call | solution.py:111
  36.5 1.5 %partial_scores.4 = f32[256,128]{1,0:T(8,128)S(1)} custom-call(bf16[256,8192]{1,0:T(8,128)(2,1)S(1)} %get-tuple-element.72.refs_0_.refs_5_, bf16[32,4096]{1,0:T(8,128)(2,1)S(1)} %get-tuple-element.75.refs_1_, bf16[32,8192]{1,0:T(8,128)(2,1)S(1)} %pair.1.refs_2_.refs_4_, bf16[16,8192]{1,0:T(8,128)(2,1)S(1)} %collective-permute-done.8.refs_3_.refs_5_, ...), custom_call_target="tpu_custom_call" | custom-call | tf_op jit(solution)/shard_map/partial_scores/pallas_call | solution.py:111
  39.1 2.7 %partial_scores.5 = (f32[256,128]{1,0:T(8,128)S(1)}, f32[256,128]{1,0:T(8,128)S(1)}) custom-call(bf16[256,8192]{1,0:T(8,128)(2,1)S(1)} %get-tuple-element.56.refs_0_.refs_2_, bf16[256,8192]{1,0:T(8,128)(2,1)S(1)} %get-tuple-element.59.refs_1_.refs_3_, bf16[32,4096]{1,0:T(8,128)(2,1)S(1)} %get-tuple-element.77.refs_2_, ...), custom_call_target="tpu_custom_call" | custom-call | tf_op jit(solution)/shard_map/partial_scores/pallas_call | solution.py:111
  42.3 1.6 %collective-permute-done.11.refs_2_ = f32[256,128]{1,0:T(8,128)S(1)} collective-permute-done((f32[256,128]{1,0:T(8,128)S(1)}, f32[256,128]{1,0:T(8,128)S(1)}, u32[]{:S(2)}, u32[]{:S(2)}) %collective-permute-start.11) | collective-permute-done | bytes 131104 | tf_op jit(solution)/shard_map/ppermute | solution.py:63
  46.2 2.2 %collective-permute-done.15.refs_9_ = bf16[128,256]{1,0:T(8,128)(2,1)S(1)} collective-permute-done((bf16[128,256]{1,0:T(8,128)(2,1)S(1)}, bf16[128,256]{1,0:T(8,128)(2,1)S(1)}, u32[]{:S(2)}, u32[]{:S(2)}) %collective-permute-start.15) | collective-permute-done | bytes 65568 | tf_op jit(solution)/shard_map/ppermute | solution.py:63
  48.4 1.7 %collective-permute-done.14.refs_8_ = bf16[128,256]{1,0:T(8,128)(2,1)S(1)} collective-permute-done((bf16[128,256]{1,0:T(8,128)(2,1)S(1)}, bf16[128,256]{1,0:T(8,128)(2,1)S(1)}, u32[]{:S(2)}, u32[]{:S(2)}) %collective-permute-start.14) | collective-permute-done | bytes 65568 | tf_op jit(solution)/shard_map/ppermute | solution.py:63
  50.1 1.4 %weighted_sums.3 = (bf16[64,2048]{1,0:T(8,128)(2,1)S(1)}, bf16[64,2048]{1,0:T(8,128)(2,1)S(1)}, bf16[64,2048]{1,0:T(8,128)(2,1)S(1)}, bf16[64,2048]{1,0:T(8,128)(2,1)S(1)}) custom-call(s32[1]{0:T(128)} %bitcast.1.member_ref.refs_0_, s32[1]{0:T(128)} %bitcast.2.x_ref.refs_1_, bf16[256,8192]{1,0:T(8,128)(2,1)S(1)} %get-tuple-element.56.refs_0_.refs_2_, ...), custom_call_target="tpu_custom_call" | custom-call | tf_op jit(solution)/shard_map/weighted_sums/pallas_call | solution.py:111
  51.6 2.6 %collective-permute-start.22 = (bf16[64,2048]{1,0:T(8,128)(2,1)S(1)}, bf16[64,2048]{1,0:T(8,128)(2,1)S(1)}, u32[]{:S(2)}, u32[]{:S(2)}) collective-permute-start(bf16[64,2048]{1,0:T(8,128)(2,1)S(1)} %get-tuple-element.90), channel_id=1, source_target_pairs={{0,16},{1,129},{2,18},{3,131},{4,20},{5,133},{6,22},{7,135},{8,24}... | collective-permute-start | bytes 786440 | tf_op jit(solution)/shard_map/ppermute | solution.py:63
  55.8 1.4 %weighted_sums.2 = (bf16[64,2048]{1,0:T(8,128)(2,1)S(1)}, bf16[64,2048]{1,0:T(8,128)(2,1)S(1)}, bf16[64,2048]{1,0:T(8,128)(2,1)S(1)}, bf16[64,2048]{1,0:T(8,128)(2,1)S(1)}) custom-call(s32[1]{0:T(128)} %bitcast.1.member_ref.refs_0_, s32[1]{0:T(128)} %bitcast.2.x_ref.refs_1_, bf16[256,8192]{1,0:T(8,128)(2,1)S(1)} %get-tuple-element.56.refs_0_.refs_2_, ...), custom_call_target="tpu_custom_call" | custom-call | tf_op jit(solution)/shard_map/weighted_sums/pallas_call | solution.py:111
  57.2 1.3 %collective-permute-start.16 = (bf16[64,2048]{1,0:T(8,128)(2,1)S(1)}, bf16[64,2048]{1,0:T(8,128)(2,1)S(1)}, u32[]{:S(2)}, u32[]{:S(2)}) collective-permute-start(bf16[64,2048]{1,0:T(8,128)(2,1)S(1)} %get-tuple-element.82), channel_id=1, source_target_pairs={{0,128},{1,17},{2,130},{3,19},{4,132},{5,21},{6,134},{7,23},{8,136... | collective-permute-start | bytes 786440 | tf_op jit(solution)/shard_map/ppermute | solution.py:63
  58.6 1.9 %collective-permute-start.17 = (bf16[64,2048]{1,0:T(8,128)(2,1)S(1)}, bf16[64,2048]{1,0:T(8,128)(2,1)S(1)}, u32[]{:S(2)}, u32[]{:S(2)}) collective-permute-start(bf16[64,2048]{1,0:T(8,128)(2,1)S(1)} %get-tuple-element.83), channel_id=1, source_target_pairs={{0,64},{1,33},{2,66},{3,35},{4,68},{5,37},{6,70},{7,39},{8,72},{9,... | collective-permute-start | bytes 786440 | tf_op jit(solution)/shard_map/ppermute | solution.py:63
  60.5 1.5 %collective-permute-start.18 = (bf16[64,2048]{1,0:T(8,128)(2,1)S(1)}, bf16[64,2048]{1,0:T(8,128)(2,1)S(1)}, u32[]{:S(2)}, u32[]{:S(2)}) collective-permute-start(bf16[64,2048]{1,0:T(8,128)(2,1)S(1)} %get-tuple-element.84), channel_id=1, source_target_pairs={{0,192},{1,49},{2,194},{3,51},{4,196},{5,53},{6,198},{7,55},{8,200... | collective-permute-start | bytes 786440 | tf_op jit(solution)/shard_map/ppermute | solution.py:63
  61.9 2.5 %collective-permute-done.23.refs_4_ = bf16[64,2048]{1,0:T(8,128)(2,1)S(1)} collective-permute-done((bf16[64,2048]{1,0:T(8,128)(2,1)S(1)}, bf16[64,2048]{1,0:T(8,128)(2,1)S(1)}, u32[]{:S(2)}, u32[]{:S(2)}) %collective-permute-start.23) | collective-permute-done | bytes 262176 | tf_op jit(solution)/shard_map/ppermute | solution.py:63
  64.4 1.9 %collective-permute-done.24.refs_5_ = bf16[64,2048]{1,0:T(8,128)(2,1)S(1)} collective-permute-done((bf16[64,2048]{1,0:T(8,128)(2,1)S(1)}, bf16[64,2048]{1,0:T(8,128)(2,1)S(1)}, u32[]{:S(2)}, u32[]{:S(2)}) %collective-permute-start.24) | collective-permute-done | bytes 262176 | tf_op jit(solution)/shard_map/ppermute | solution.py:63
  67.5 2.0 %collective-permute-start.26 = (bf16[16,2048]{1,0:T(8,128)(2,1)S(1)}, bf16[16,2048]{1,0:T(8,128)(2,1)S(1)}, u32[]{:S(2)}, u32[]{:S(2)}) collective-permute-start(bf16[16,2048]{1,0:T(8,128)(2,1)S(1)} %get-tuple-element.95), channel_id=1, source_target_pairs={{0,64},{1,33},{2,66},{3,35},{4,68},{5,37},{6,70},{7,39},{8,72},{9,... | collective-permute-start | bytes 196616 | tf_op jit(solution)/shard_map/ppermute | solution.py:63
  70.8 2.5 %collective-permute-start.19 = (bf16[16,2048]{1,0:T(8,128)(2,1)S(1)}, bf16[16,2048]{1,0:T(8,128)(2,1)S(1)}, u32[]{:S(2)}, u32[]{:S(2)}) collective-permute-start(bf16[16,2048]{1,0:T(8,128)(2,1)S(1)} %get-tuple-element.86), channel_id=1, source_target_pairs={{0,16},{1,129},{2,18},{3,131},{4,20},{5,133},{6,22},{7,135},{8,24}... | collective-permute-start | bytes 196616 | tf_op jit(solution)/shard_map/ppermute | solution.py:63
  73.3 1.7 %collective-permute-start.20 = (bf16[16,2048]{1,0:T(8,128)(2,1)S(1)}, bf16[16,2048]{1,0:T(8,128)(2,1)S(1)}, u32[]{:S(2)}, u32[]{:S(2)}) collective-permute-start(bf16[16,2048]{1,0:T(8,128)(2,1)S(1)} %get-tuple-element.87), channel_id=1, source_target_pairs={{0,32},{1,65},{2,34},{3,67},{4,36},{5,69},{6,38},{7,71},{8,40},{9,... | collective-permute-start | bytes 196616 | tf_op jit(solution)/shard_map/ppermute | solution.py:63
  79.3 6.5 %collective-permute-start.28 = (bf16[16,1024]{1,0:T(8,128)(2,1)S(1)}, bf16[16,1024]{1,0:T(8,128)(2,1)S(1)}, u32[]{:S(2)}, u32[]{:S(2)}) collective-permute-start(bf16[16,1024]{1,0:T(8,128)(2,1)S(1)} %get-tuple-element.98), channel_id=1, source_target_pairs={{0,8},{1,9},{2,10},{3,11},{4,12},{5,13},{6,14},{7,15},{8,0},{9,1},... | collective-permute-start | bytes 98312 | tf_op jit(solution)/shard_map/ppermute | solution.py:63
  85.7 1.5 %collective-permute-start.29 = (bf16[16,1024]{1,0:T(8,128)(2,1)S(1)}, bf16[16,1024]{1,0:T(8,128)(2,1)S(1)}, u32[]{:S(2)}, u32[]{:S(2)}) collective-permute-start(bf16[16,1024]{1,0:T(8,128)(2,1)S(1)} %get-tuple-element.99), channel_id=1, source_target_pairs={{0,4},{1,5},{2,6},{3,7},{4,0},{5,1},{6,2},{7,3},{8,12},{9,13},{10,... | collective-permute-start | bytes 98312 | tf_op jit(solution)/shard_map/ppermute | solution.py:63
  87.7 2.8 %collective-permute-done.29 = bf16[16,1024]{1,0:T(8,128)(2,1)S(1)} collective-permute-done((bf16[16,1024]{1,0:T(8,128)(2,1)S(1)}, bf16[16,1024]{1,0:T(8,128)(2,1)S(1)}, u32[]{:S(2)}, u32[]{:S(2)}) %collective-permute-start.29) | collective-permute-done | bytes 32800 | tf_op jit(solution)/shard_map/ppermute | solution.py:63
  90.5 2.7 %collective-permute-done.30 = bf16[16,1024]{1,0:T(8,128)(2,1)S(1)} collective-permute-done((bf16[16,1024]{1,0:T(8,128)(2,1)S(1)}, bf16[16,1024]{1,0:T(8,128)(2,1)S(1)}, u32[]{:S(2)}, u32[]{:S(2)}) %collective-permute-start.30) | collective-permute-done | bytes 32800 | tf_op jit(solution)/shard_map/ppermute | solution.py:63
  (50 shorter events, 20.1 us)
Async XLA Ops:
  2.0 11.9 %collective-permute-start = (bf16[32,8320]{1,0:T(8,128)(2,1)S(1)}, bf16[32,8320]{1,0:T(8,128)(2,1)S(1)}, u32[]{:S(2)}, u32[]{:S(2)}) collective-permute-start(bf16[32,8320]{1,0:T(8,128)(2,1)S(1)} %get-tuple-element.57), channel_id=1, source_target_pairs={{0,1},{1,0},{2,3},{3,2},{4,5},{5,4},{6,7},{7,6},{8,9},{9,8},{10,11... | collective-permute-start | bytes 1597448 | tf_op jit(solution)/shard_map/ppermute | solution.py:63
  2.1 14.7 %collective-permute-start.1 = (bf16[32,8320]{1,0:T(8,128)(2,1)S(1)}, bf16[32,8320]{1,0:T(8,128)(2,1)S(1)}, u32[]{:S(2)}, u32[]{:S(2)}) collective-permute-start(bf16[32,8320]{1,0:T(8,128)(2,1)S(1)} %get-tuple-element.60.after), channel_id=1, source_target_pairs={{0,2},{1,3},{2,0},{3,1},{4,6},{5,7},{6,4},{7,5},{8,10},{9,11},{10,... | collective-permute-start | bytes 1597448 | tf_op jit(solution)/shard_map/ppermute | solution.py:63
  5.1 11.1 %collective-permute-start.4 = (bf16[16,8192]{1,0:T(8,128)(2,1)S(1)}, bf16[16,8192]{1,0:T(8,128)(2,1)S(1)}, u32[]{:S(2)}, u32[]{:S(2)}) collective-permute-start(bf16[16,8192]{1,0:T(8,128)(2,1)S(1)} %own_references.1.refs_8_.refs_10_), channel_id=1, source_target_pairs={{0,32},{1,33},{2,34},{3,35},{4,36},{5,37},{6,38},{7,39},{8,40},{9,... | collective-permute-start | bytes 786440 | tf_op jit(solution)/shard_map/ppermute | solution.py:63
  5.7 10.5 %collective-permute-start.3 = (bf16[16,8192]{1,0:T(8,128)(2,1)S(1)}, bf16[16,8192]{1,0:T(8,128)(2,1)S(1)}, u32[]{:S(2)}, u32[]{:S(2)}) collective-permute-start(bf16[16,8192]{1,0:T(8,128)(2,1)S(1)} %own_references.1.refs_8_.refs_10_), channel_id=1, source_target_pairs={{0,192},{1,193},{2,194},{3,195},{4,196},{5,197},{6,198},{7,199},{8... | collective-permute-start | bytes 786440 | tf_op jit(solution)/shard_map/ppermute | solution.py:63
  8.7 7.8 %collective-permute-start.2 = (bf16[16,8192]{1,0:T(8,128)(2,1)S(1)}, bf16[16,8192]{1,0:T(8,128)(2,1)S(1)}, u32[]{:S(2)}, u32[]{:S(2)}) collective-permute-start(bf16[16,8192]{1,0:T(8,128)(2,1)S(1)} %own_references.1.refs_8_.refs_10_), channel_id=1, source_target_pairs={{0,64},{1,65},{2,66},{3,67},{4,68},{5,69},{6,70},{7,71},{8,72},{9,... | collective-permute-start | bytes 786440 | tf_op jit(solution)/shard_map/ppermute | solution.py:63
  16.8 17.4 %collective-permute-start.5 = (bf16[32,8320]{1,0:T(8,128)(2,1)S(1)}, bf16[32,8320]{1,0:T(8,128)(2,1)S(1)}, u32[]{:S(2)}, u32[]{:S(2)}) collective-permute-start(bf16[32,8320]{1,0:T(8,128)(2,1)S(1)} %get-tuple-element.64), channel_id=1, source_target_pairs={{0,3},{1,2},{2,1},{3,0},{4,7},{5,6},{6,5},{7,4},{8,11},{9,10},{10,... | collective-permute-start | bytes 1597448 | tf_op jit(solution)/shard_map/ppermute | solution.py:63
  17.8 12.6 %collective-permute-start.7 = (bf16[16,8192]{1,0:T(8,128)(2,1)S(1)}, bf16[16,8192]{1,0:T(8,128)(2,1)S(1)}, u32[]{:S(2)}, u32[]{:S(2)}) collective-permute-start(bf16[16,8192]{1,0:T(8,128)(2,1)S(1)} %relay.1), channel_id=1, source_target_pairs={{0,192},{1,65},{2,194},{3,67},{4,196},{5,69},{6,198},{7,71},{8,200... | collective-permute-start | bytes 786440 | tf_op jit(solution)/shard_map/ppermute | solution.py:63
  20.9 10.8 %collective-permute-start.6 = (bf16[16,8192]{1,0:T(8,128)(2,1)S(1)}, bf16[16,8192]{1,0:T(8,128)(2,1)S(1)}, u32[]{:S(2)}, u32[]{:S(2)}) collective-permute-start(bf16[16,8192]{1,0:T(8,128)(2,1)S(1)} %collective-permute-done.4.refs_5_.refs_7_), channel_id=1, source_target_pairs={{0,128},{1,129},{2,130},{3,131},{4,132},{5,133},{6,134},{7,135},{8... | collective-permute-start | bytes 786440 | tf_op jit(solution)/shard_map/ppermute | solution.py:63
  21.6 10.2 %collective-permute-start.8 = (bf16[16,8192]{1,0:T(8,128)(2,1)S(1)}, bf16[16,8192]{1,0:T(8,128)(2,1)S(1)}, u32[]{:S(2)}, u32[]{:S(2)}) collective-permute-start(bf16[16,8192]{1,0:T(8,128)(2,1)S(1)} %collective-permute-done.2.one.refs_6_.refs_8_), channel_id=1, source_target_pairs={{0,32},{1,33},{2,34},{3,35},{4,36},{5,37},{6,38},{7,39},{8,40},{9,... | collective-permute-start | bytes 786440 | tf_op jit(solution)/shard_map/ppermute | solution.py:63
  22.1 9.6 %collective-permute-start.9 = (bf16[16,8192]{1,0:T(8,128)(2,1)S(1)}, bf16[16,8192]{1,0:T(8,128)(2,1)S(1)}, u32[]{:S(2)}, u32[]{:S(2)}) collective-permute-start(bf16[16,8192]{1,0:T(8,128)(2,1)S(1)} %collective-permute-done.3.other.refs_7_.refs_9_), channel_id=1, source_target_pairs={{0,48},{1,49},{2,50},{3,51},{4,52},{5,53},{6,54},{7,55},{8,56},{9,... | collective-permute-start | bytes 786440 | tf_op jit(solution)/shard_map/ppermute | solution.py:63
  33.4 9.0 %collective-permute-start.10 = (f32[256,128]{1,0:T(8,128)S(1)}, f32[256,128]{1,0:T(8,128)S(1)}, u32[]{:S(2)}, u32[]{:S(2)}) collective-permute-start(f32[256,128]{1,0:T(8,128)S(1)} %get-tuple-element.70), channel_id=1, source_target_pairs={{0,2},{1,3},{2,0},{3,1},{4,6},{5,7},{6,4},{7,5},{8,10},{9,11},{10,... | collective-permute-start | bytes 393224 | tf_op jit(solution)/shard_map/ppermute | solution.py:63
  38.1 5.9 %collective-permute-start.11 = (f32[256,128]{1,0:T(8,128)S(1)}, f32[256,128]{1,0:T(8,128)S(1)}, u32[]{:S(2)}, u32[]{:S(2)}) collective-permute-start(f32[256,128]{1,0:T(8,128)S(1)} %partial_scores.4), channel_id=1, source_target_pairs={{0,3},{1,2},{2,1},{3,0},{4,7},{5,6},{6,5},{7,4},{8,11},{9,10},{10,... | collective-permute-start | bytes 393224 | tf_op jit(solution)/shard_map/ppermute | solution.py:63
  41.8 2.1 %collective-permute-start.12 = (f32[256,128]{1,0:T(8,128)S(1)}, f32[256,128]{1,0:T(8,128)S(1)}, u32[]{:S(2)}, u32[]{:S(2)}) collective-permute-start(f32[256,128]{1,0:T(8,128)S(1)} %get-tuple-element.80), channel_id=1, source_target_pairs={{0,1},{1,0},{2,3},{3,2},{4,5},{5,4},{6,7},{7,6},{8,9},{9,8},{10,11... | collective-permute-start | bytes 393224 | tf_op jit(solution)/shard_map/ppermute | solution.py:63
  44.3 4.2 %collective-permute-start.15 = (bf16[128,256]{1,0:T(8,128)(2,1)S(1)}, bf16[128,256]{1,0:T(8,128)(2,1)S(1)}, u32[]{:S(2)}, u32[]{:S(2)}) collective-permute-start(bf16[128,256]{1,0:T(8,128)(2,1)S(1)} %posterior.1.refs_6_), channel_id=1, source_target_pairs={{0,3},{1,2},{2,1},{3,0},{4,7},{5,6},{6,5},{7,4},{8,11},{9,10},{10,... | collective-permute-start | bytes 196616 | tf_op jit(solution)/shard_map/ppermute | solution.py:63
  45.1 5.0 %collective-permute-start.14 = (bf16[128,256]{1,0:T(8,128)(2,1)S(1)}, bf16[128,256]{1,0:T(8,128)(2,1)S(1)}, u32[]{:S(2)}, u32[]{:S(2)}) collective-permute-start(bf16[128,256]{1,0:T(8,128)(2,1)S(1)} %posterior.1.refs_6_), channel_id=1, source_target_pairs={{0,2},{1,3},{2,0},{3,1},{4,6},{5,7},{6,4},{7,5},{8,10},{9,11},{10,... | collective-permute-start | bytes 196616 | tf_op jit(solution)/shard_map/ppermute | solution.py:63
  46.1 4.1 %collective-permute-start.13 = (bf16[128,256]{1,0:T(8,128)(2,1)S(1)}, bf16[128,256]{1,0:T(8,128)(2,1)S(1)}, u32[]{:S(2)}, u32[]{:S(2)}) collective-permute-start(bf16[128,256]{1,0:T(8,128)(2,1)S(1)} %posterior.1.refs_6_), channel_id=1, source_target_pairs={{0,1},{1,0},{2,3},{3,2},{4,5},{5,4},{6,7},{7,6},{8,9},{9,8},{10,11... | collective-permute-start | bytes 196616 | tf_op jit(solution)/shard_map/ppermute | solution.py:63
  51.6 8.9 %collective-permute-start.22 = (bf16[64,2048]{1,0:T(8,128)(2,1)S(1)}, bf16[64,2048]{1,0:T(8,128)(2,1)S(1)}, u32[]{:S(2)}, u32[]{:S(2)}) collective-permute-start(bf16[64,2048]{1,0:T(8,128)(2,1)S(1)} %get-tuple-element.90), channel_id=1, source_target_pairs={{0,16},{1,129},{2,18},{3,131},{4,20},{5,133},{6,22},{7,135},{8,24}... | collective-permute-start | bytes 786440 | tf_op jit(solution)/shard_map/ppermute | solution.py:63
  54.2 10.2 %collective-permute-start.23 = (bf16[64,2048]{1,0:T(8,128)(2,1)S(1)}, bf16[64,2048]{1,0:T(8,128)(2,1)S(1)}, u32[]{:S(2)}, u32[]{:S(2)}) collective-permute-start(bf16[64,2048]{1,0:T(8,128)(2,1)S(1)} %get-tuple-element.91), channel_id=1, source_target_pairs={{0,32},{1,65},{2,34},{3,67},{4,36},{5,69},{6,38},{7,71},{8,40},{9,... | collective-permute-start | bytes 786440 | tf_op jit(solution)/shard_map/ppermute | solution.py:63
  55.3 11.1 %collective-permute-start.24 = (bf16[64,2048]{1,0:T(8,128)(2,1)S(1)}, bf16[64,2048]{1,0:T(8,128)(2,1)S(1)}, u32[]{:S(2)}, u32[]{:S(2)}) collective-permute-start(bf16[64,2048]{1,0:T(8,128)(2,1)S(1)} %get-tuple-element.92), channel_id=1, source_target_pairs={{0,48},{1,193},{2,50},{3,195},{4,52},{5,197},{6,54},{7,199},{8,56}... | collective-permute-start | bytes 786440 | tf_op jit(solution)/shard_map/ppermute | solution.py:63
  57.2 12.3 %collective-permute-start.16 = (bf16[64,2048]{1,0:T(8,128)(2,1)S(1)}, bf16[64,2048]{1,0:T(8,128)(2,1)S(1)}, u32[]{:S(2)}, u32[]{:S(2)}) collective-permute-start(bf16[64,2048]{1,0:T(8,128)(2,1)S(1)} %get-tuple-element.82), channel_id=1, source_target_pairs={{0,128},{1,17},{2,130},{3,19},{4,132},{5,21},{6,134},{7,23},{8,136... | collective-permute-start | bytes 786440 | tf_op jit(solution)/shard_map/ppermute | solution.py:63
  58.6 12.1 %collective-permute-start.17 = (bf16[64,2048]{1,0:T(8,128)(2,1)S(1)}, bf16[64,2048]{1,0:T(8,128)(2,1)S(1)}, u32[]{:S(2)}, u32[]{:S(2)}) collective-permute-start(bf16[64,2048]{1,0:T(8,128)(2,1)S(1)} %get-tuple-element.83), channel_id=1, source_target_pairs={{0,64},{1,33},{2,66},{3,35},{4,68},{5,37},{6,70},{7,39},{8,72},{9,... | collective-permute-start | bytes 786440 | tf_op jit(solution)/shard_map/ppermute | solution.py:63
  60.5 10.2 %collective-permute-start.18 = (bf16[64,2048]{1,0:T(8,128)(2,1)S(1)}, bf16[64,2048]{1,0:T(8,128)(2,1)S(1)}, u32[]{:S(2)}, u32[]{:S(2)}) collective-permute-start(bf16[64,2048]{1,0:T(8,128)(2,1)S(1)} %get-tuple-element.84), channel_id=1, source_target_pairs={{0,192},{1,49},{2,194},{3,51},{4,196},{5,53},{6,198},{7,55},{8,200... | collective-permute-start | bytes 786440 | tf_op jit(solution)/shard_map/ppermute | solution.py:63
  66.5 8.5 %collective-permute-start.25 = (bf16[16,2048]{1,0:T(8,128)(2,1)S(1)}, bf16[16,2048]{1,0:T(8,128)(2,1)S(1)}, u32[]{:S(2)}, u32[]{:S(2)}) collective-permute-start(bf16[16,2048]{1,0:T(8,128)(2,1)S(1)} %get-tuple-element.94), channel_id=1, source_target_pairs={{0,128},{1,17},{2,130},{3,19},{4,132},{5,21},{6,134},{7,23},{8,136... | collective-permute-start | bytes 196616 | tf_op jit(solution)/shard_map/ppermute | solution.py:63
  67.5 7.5 %collective-permute-start.26 = (bf16[16,2048]{1,0:T(8,128)(2,1)S(1)}, bf16[16,2048]{1,0:T(8,128)(2,1)S(1)}, u32[]{:S(2)}, u32[]{:S(2)}) collective-permute-start(bf16[16,2048]{1,0:T(8,128)(2,1)S(1)} %get-tuple-element.95), channel_id=1, source_target_pairs={{0,64},{1,33},{2,66},{3,35},{4,68},{5,37},{6,70},{7,39},{8,72},{9,... | collective-permute-start | bytes 196616 | tf_op jit(solution)/shard_map/ppermute | solution.py:63
  69.5 5.8 %collective-permute-start.27 = (bf16[16,2048]{1,0:T(8,128)(2,1)S(1)}, bf16[16,2048]{1,0:T(8,128)(2,1)S(1)}, u32[]{:S(2)}, u32[]{:S(2)}) collective-permute-start(bf16[16,2048]{1,0:T(8,128)(2,1)S(1)} %get-tuple-element.96), channel_id=1, source_target_pairs={{0,192},{1,49},{2,194},{3,51},{4,196},{5,53},{6,198},{7,55},{8,200... | collective-permute-start | bytes 196616 | tf_op jit(solution)/shard_map/ppermute | solution.py:63
  70.8 5.9 %collective-permute-start.19 = (bf16[16,2048]{1,0:T(8,128)(2,1)S(1)}, bf16[16,2048]{1,0:T(8,128)(2,1)S(1)}, u32[]{:S(2)}, u32[]{:S(2)}) collective-permute-start(bf16[16,2048]{1,0:T(8,128)(2,1)S(1)} %get-tuple-element.86), channel_id=1, source_target_pairs={{0,16},{1,129},{2,18},{3,131},{4,20},{5,133},{6,22},{7,135},{8,24}... | collective-permute-start | bytes 196616 | tf_op jit(solution)/shard_map/ppermute | solution.py:63
  73.3 4.6 %collective-permute-start.20 = (bf16[16,2048]{1,0:T(8,128)(2,1)S(1)}, bf16[16,2048]{1,0:T(8,128)(2,1)S(1)}, u32[]{:S(2)}, u32[]{:S(2)}) collective-permute-start(bf16[16,2048]{1,0:T(8,128)(2,1)S(1)} %get-tuple-element.87), channel_id=1, source_target_pairs={{0,32},{1,65},{2,34},{3,67},{4,36},{5,69},{6,38},{7,71},{8,40},{9,... | collective-permute-start | bytes 196616 | tf_op jit(solution)/shard_map/ppermute | solution.py:63
  74.9 4.3 %collective-permute-start.21 = (bf16[16,2048]{1,0:T(8,128)(2,1)S(1)}, bf16[16,2048]{1,0:T(8,128)(2,1)S(1)}, u32[]{:S(2)}, u32[]{:S(2)}) collective-permute-start(bf16[16,2048]{1,0:T(8,128)(2,1)S(1)} %get-tuple-element.88), channel_id=1, source_target_pairs={{0,48},{1,193},{2,50},{3,195},{4,52},{5,197},{6,54},{7,199},{8,56}... | collective-permute-start | bytes 196616 | tf_op jit(solution)/shard_map/ppermute | solution.py:63
  79.3 8.5 %collective-permute-start.28 = (bf16[16,1024]{1,0:T(8,128)(2,1)S(1)}, bf16[16,1024]{1,0:T(8,128)(2,1)S(1)}, u32[]{:S(2)}, u32[]{:S(2)}) collective-permute-start(bf16[16,1024]{1,0:T(8,128)(2,1)S(1)} %get-tuple-element.98), channel_id=1, source_target_pairs={{0,8},{1,9},{2,10},{3,11},{4,12},{5,13},{6,14},{7,15},{8,0},{9,1},... | collective-permute-start | bytes 98312 | tf_op jit(solution)/shard_map/ppermute | solution.py:63
  85.7 4.8 %collective-permute-start.29 = (bf16[16,1024]{1,0:T(8,128)(2,1)S(1)}, bf16[16,1024]{1,0:T(8,128)(2,1)S(1)}, u32[]{:S(2)}, u32[]{:S(2)}) collective-permute-start(bf16[16,1024]{1,0:T(8,128)(2,1)S(1)} %get-tuple-element.99), channel_id=1, source_target_pairs={{0,4},{1,5},{2,6},{3,7},{4,0},{5,1},{6,2},{7,3},{8,12},{9,13},{10,... | collective-permute-start | bytes 98312 | tf_op jit(solution)/shard_map/ppermute | solution.py:63
  87.2 6.0 %collective-permute-start.30 = (bf16[16,1024]{1,0:T(8,128)(2,1)S(1)}, bf16[16,1024]{1,0:T(8,128)(2,1)S(1)}, u32[]{:S(2)}, u32[]{:S(2)}) collective-permute-start(bf16[16,1024]{1,0:T(8,128)(2,1)S(1)} %get-tuple-element.100), channel_id=1, source_target_pairs={{0,12},{1,13},{2,14},{3,15},{4,8},{5,9},{6,10},{7,11},{8,4},{9,5},... | collective-permute-start | bytes 98312 | tf_op jit(solution)/shard_map/ppermute | solution.py:63

commit v16 on v15

--- a/solution.py
+++ b/solution.py
@@ -467,7 +467,7 @@
     rows[0], pens[0] = make_rows(member, chunks[0], geo, table)
     rows[1], pens[1] = make_rows(member, after(got[1], rows[0]), geo, table)
     wave = [gathered[1, 0], gathered[3, 0], gathered[0, 1], rows[1]]
-    gathered[2, 1] = send(after(gathered[0, 1], *wave), flips(y=2))
+    gathered[2, 1] = send(gathered[0, 1], flips(y=2))
     relayed = [gathered[1, 0], after(gathered[3, 0], *wave)]
     (relay,) = local(relay_kernel, "relay", [((16, WIDTH), BF16)], [member], relayed, 2)
     gathered[2, 0] = send(relay, second_hop())

time: 94.7 us -> 94.2 us (level)
  waiting for transfers between devices: 25.9 us -> 23.2 us
  starting transfers between devices: 42.9 us -> 45.1 us
    ppermute x31, waiting for transfers between devices: 25.9 us -> 23.2 us  [send(): return lax.ppermute(value, AXES, pairs)]
    ppermute x31, starting transfers between devices: 42.9 us -> 45.1 us  [send(): return lax.ppermute(value, AXES, pairs)]
  transfers between devices with their start and end apart: 31 -> 31, of which waited for: 16 -> 17; matrix products, arithmetic and copies ran while one was open for 0% -> 0% of each run, Pallas kernels for 22% -> 22%
where the time goes in v16:
time: 94.2 us; the launch traced here: 93.4 us
  starting transfers between devices  45.1 us (48%)
  Pallas kernels  24.3 us (26%)
  waiting for transfers between devices  23.2 us (25%)
    ppermute x31, starting transfers between devices, send(): return lax.ppermute(value, AXES, pairs)  45.1 us
    pallas_call x19, Pallas kernels, local(): pl.pallas_call(kernel, in_specs=[SCALARS] * len(scalars) + [PLACED] * pla...  24.3 us
    ppermute x31, waiting for transfers between devices, send(): return lax.ppermute(value, AXES, pairs)  23.2 us
  transfers between devices with their start and end apart: 31, of which 17 were waited for; matrix products, arithmetic and copies ran while one was open for 0% of the time, Pallas kernels for 22%

profile of v16, /device:TPU:2, one launch (start us, length us, event | category | flops | bytes accessed | tf_op | source)
XLA Modules:
  0.0 93.4 jit_solution(13176268195933635648)
XLA Ops:
  0.0 2.0 %split_particles.1 = (bf16[32,8320]{1,0:T(8,128)(2,1)S(1)}, bf16[32,8320]{1,0:T(8,128)(2,1)S(1)}, bf16[32,8320]{1,0:T(8,128)(2,1)S(1)}, bf16[32,8320]{1,0:T(8,128)(2,1)S(1)}) custom-call(s32[1]{0:T(128)} %bitcast.1.member_ref.refs_0_, s32[1]{0:T(128)} %bitcast.block_ref, s32[1]{0:T(128)} %bitcast.2.x_ref.refs_1_, bf16[32,32768]{1,0:T(8,128)(2,1)} %source.2, ...), custom_call_target="tpu_custom_call" | custom-call | tf_op jit(solution)/shard_map/split_particles/pallas_call | solution.py:111
  2.1 2.0 %collective-permute-start.1 = (bf16[32,8320]{1,0:T(8,128)(2,1)S(1)}, bf16[32,8320]{1,0:T(8,128)(2,1)S(1)}, u32[]{:S(2)}, u32[]{:S(2)}) collective-permute-start(bf16[32,8320]{1,0:T(8,128)(2,1)S(1)} %get-tuple-element.59.after), channel_id=1, source_target_pairs={{0,2},{1,3},{2,0},{3,1},{4,6},{5,7},{6,4},{7,5},{8,10},{9,11},{10,... | collective-permute-start | bytes 1597448 | tf_op jit(solution)/shard_map/ppermute | solution.py:63
  5.7 3.0 %collective-permute-start.3 = (bf16[16,8192]{1,0:T(8,128)(2,1)S(1)}, bf16[16,8192]{1,0:T(8,128)(2,1)S(1)}, u32[]{:S(2)}, u32[]{:S(2)}) collective-permute-start(bf16[16,8192]{1,0:T(8,128)(2,1)S(1)} %own_references.1.refs_8_.refs_10_), channel_id=1, source_target_pairs={{0,192},{1,193},{2,194},{3,195},{4,196},{5,197},{6,198},{7,199},{8... | collective-permute-start | bytes 786440 | tf_op jit(solution)/shard_map/ppermute | solution.py:63
  8.9 2.7 %phase_table.1 = (bf16[256,8192]{1,0:T(8,128)(2,1)S(1)}, f32[4,8,1024]{2,1,0:T(8,128)S(1)}) custom-call(s32[1]{0:T(128)} %bitcast.1.member_ref.refs_0_, f32[16,8,1024]{2,1,0:T(8,128)} %constant.63.clone.geo_ref), custom_call_target="tpu_custom_call" | custom-call | tf_op jit(solution)/shard_map/phase_table/pallas_call | solution.py:111
  11.6 2.3 %shifted_rows.4 = (bf16[256,8192]{1,0:T(8,128)(2,1)S(1)}, bf16[32,4096]{1,0:T(8,128)(2,1)S(1)}) custom-call(s32[1]{0:T(128)} %bitcast.1.member_ref.refs_0_, bf16[32,8320]{1,0:T(8,128)(2,1)S(1)} %get-tuple-element.52.x_ref, f32[4,8,1024]{2,1,0:T(8,128)S(1)} %get-tuple-element.53.geo_ref, bf16[256,8192]{1,0:T(8,128)(2,1)S(1)} %get-tuple-element.54.table_ref), custom_call_target="tpu_custom_call" | custom-call | tf_op jit(solution)/shard_map/shifted_rows/pallas_call | solution.py:111
  13.9 2.3 %shifted_rows.5 = (bf16[256,8192]{1,0:T(8,128)(2,1)S(1)}, bf16[32,4096]{1,0:T(8,128)(2,1)S(1)}) custom-call(s32[1]{0:T(128)} %bitcast.1.member_ref.refs_0_, bf16[32,8320]{1,0:T(8,128)(2,1)S(1)} %collective-permute-done.x_ref, f32[4,8,1024]{2,1,0:T(8,128)S(1)} %get-tuple-element.53.geo_ref, bf16[256,8192]{1,0:T(8,128)(2,1)S(1)} %get-tuple-element.54.table_ref), custom_call_target="tpu_custom_call" | custom-call | tf_op jit(solution)/shard_map/shifted_rows/pallas_call | solution.py:111
  17.8 3.2 %collective-permute-start.6 = (bf16[16,8192]{1,0:T(8,128)(2,1)S(1)}, bf16[16,8192]{1,0:T(8,128)(2,1)S(1)}, u32[]{:S(2)}, u32[]{:S(2)}) collective-permute-start(bf16[16,8192]{1,0:T(8,128)(2,1)S(1)} %collective-permute-done.4.refs_5_.refs_7_), channel_id=1, source_target_pairs={{0,128},{1,129},{2,130},{3,131},{4,132},{5,133},{6,134},{7,135},{8... | collective-permute-start | bytes 786440 | tf_op jit(solution)/shard_map/ppermute | solution.py:63
  22.7 2.2 %collective-permute-start.9 = (bf16[16,8192]{1,0:T(8,128)(2,1)S(1)}, bf16[16,8192]{1,0:T(8,128)(2,1)S(1)}, u32[]{:S(2)}, u32[]{:S(2)}) collective-permute-start(bf16[16,8192]{1,0:T(8,128)(2,1)S(1)} %collective-permute-done.3.other.refs_7_.refs_9_), channel_id=1, source_target_pairs={{0,48},{1,49},{2,50},{3,51},{4,52},{5,53},{6,54},{7,55},{8,56},{9,... | collective-permute-start | bytes 786440 | tf_op jit(solution)/shard_map/ppermute | solution.py:63
  24.9 2.3 %shifted_rows.6 = (bf16[256,8192]{1,0:T(8,128)(2,1)S(1)}, bf16[32,4096]{1,0:T(8,128)(2,1)S(1)}) custom-call(s32[1]{0:T(128)} %bitcast.1.member_ref.refs_0_, bf16[32,8320]{1,0:T(8,128)(2,1)S(1)} %collective-permute-done.1.x_ref, f32[4,8,1024]{2,1,0:T(8,128)S(1)} %get-tuple-element.53.geo_ref, bf16[256,8192]{1,0:T(8,128)(2,1)S(1)} %get-tuple-element.54.table_ref), custom_call_target="tpu_custom_call" | custom-call | tf_op jit(solution)/shard_map/shifted_rows/pallas_call | solution.py:111
  28.5 2.7 %collective-permute-done.7.other = bf16[16,8192]{1,0:T(8,128)(2,1)S(1)} collective-permute-done((bf16[16,8192]{1,0:T(8,128)(2,1)S(1)}, bf16[16,8192]{1,0:T(8,128)(2,1)S(1)}, u32[]{:S(2)}, u32[]{:S(2)}) %collective-permute-start.7) | collective-permute-done | bytes 262176 | tf_op jit(solution)/shard_map/ppermute | solution.py:63
  31.3 1.6 %partial_scores.3 = (f32[256,128]{1,0:T(8,128)S(1)}, bf16[128,4096]{1,0:T(8,128)(2,1)S(1)}) custom-call(bf16[256,8192]{1,0:T(8,128)(2,1)S(1)} %get-tuple-element.61.refs_0_.refs_4_, bf16[32,4096]{1,0:T(8,128)(2,1)S(1)} %get-tuple-element.64.refs_1_, bf16[32,8192]{1,0:T(8,128)(2,1)S(1)} %pair.1.refs_2_.refs_4_, ...), custom_call_target="tpu_custom_call" | custom-call | tf_op jit(solution)/shard_map/partial_scores/pallas_call | solution.py:111
  33.3 2.3 %shifted_rows.7 = (bf16[256,8192]{1,0:T(8,128)(2,1)S(1)}, bf16[32,4096]{1,0:T(8,128)(2,1)S(1)}) custom-call(s32[1]{0:T(128)} %bitcast.1.member_ref.refs_0_, bf16[32,8320]{1,0:T(8,128)(2,1)S(1)} %collective-permute-done.5.x_ref, f32[4,8,1024]{2,1,0:T(8,128)S(1)} %get-tuple-element.53.geo_ref, bf16[256,8192]{1,0:T(8,128)(2,1)S(1)} %get-tuple-element.54.table_ref), custom_call_target="tpu_custom_call" | custom-call | tf_op jit(solution)/shard_map/shifted_rows/pallas_call | solution.py:111
  35.6 1.5 %partial_scores.4 = f32[256,128]{1,0:T(8,128)S(1)} custom-call(bf16[256,8192]{1,0:T(8,128)(2,1)S(1)} %get-tuple-element.70.refs_0_.refs_5_, bf16[32,4096]{1,0:T(8,128)(2,1)S(1)} %get-tuple-element.73.refs_1_, bf16[32,8192]{1,0:T(8,128)(2,1)S(1)} %pair.1.refs_2_.refs_4_, bf16[16,8192]{1,0:T(8,128)(2,1)S(1)} %collective-permute-done.8.refs_3_.refs_5_, ...), custom_call_target="tpu_custom_call" | custom-call | tf_op jit(solution)/shard_map/partial_scores/pallas_call | solution.py:111
  37.1 1.4 %collective-permute-start.11 = (f32[256,128]{1,0:T(8,128)S(1)}, f32[256,128]{1,0:T(8,128)S(1)}, u32[]{:S(2)}, u32[]{:S(2)}) collective-permute-start(f32[256,128]{1,0:T(8,128)S(1)} %partial_scores.4), channel_id=1, source_target_pairs={{0,3},{1,2},{2,1},{3,0},{4,7},{5,6},{6,5},{7,4},{8,11},{9,10},{10,... | collective-permute-start | bytes 393224 | tf_op jit(solution)/shard_map/ppermute | solution.py:63
  38.5 2.7 %partial_scores.5 = (f32[256,128]{1,0:T(8,128)S(1)}, f32[256,128]{1,0:T(8,128)S(1)}) custom-call(bf16[256,8192]{1,0:T(8,128)(2,1)S(1)} %get-tuple-element.55.refs_0_.refs_2_, bf16[256,8192]{1,0:T(8,128)(2,1)S(1)} %get-tuple-element.58.refs_1_.refs_3_, bf16[32,4096]{1,0:T(8,128)(2,1)S(1)} %get-tuple-element.75.refs_2_, ...), custom_call_target="tpu_custom_call" | custom-call | tf_op jit(solution)/shard_map/partial_scores/pallas_call | solution.py:111
  43.1 1.7 %collective-permute-start.15 = (bf16[128,256]{1,0:T(8,128)(2,1)S(1)}, bf16[128,256]{1,0:T(8,128)(2,1)S(1)}, u32[]{:S(2)}, u32[]{:S(2)}) collective-permute-start(bf16[128,256]{1,0:T(8,128)(2,1)S(1)} %posterior.1.refs_6_), channel_id=1, source_target_pairs={{0,3},{1,2},{2,1},{3,0},{4,7},{5,6},{6,5},{7,4},{8,11},{9,10},{10,... | collective-permute-start | bytes 196616 | tf_op jit(solution)/shard_map/ppermute | solution.py:63
  45.2 2.1 %collective-permute-done.15.refs_9_ = bf16[128,256]{1,0:T(8,128)(2,1)S(1)} collective-permute-done((bf16[128,256]{1,0:T(8,128)(2,1)S(1)}, bf16[128,256]{1,0:T(8,128)(2,1)S(1)}, u32[]{:S(2)}, u32[]{:S(2)}) %collective-permute-start.15) | collective-permute-done | bytes 65568 | tf_op jit(solution)/shard_map/ppermute | solution.py:63
  47.2 1.9 %collective-permute-done.14.refs_8_ = bf16[128,256]{1,0:T(8,128)(2,1)S(1)} collective-permute-done((bf16[128,256]{1,0:T(8,128)(2,1)S(1)}, bf16[128,256]{1,0:T(8,128)(2,1)S(1)}, u32[]{:S(2)}, u32[]{:S(2)}) %collective-permute-start.14) | collective-permute-done | bytes 65568 | tf_op jit(solution)/shard_map/ppermute | solution.py:63
  49.2 1.4 %weighted_sums.3 = (bf16[64,2048]{1,0:T(8,128)(2,1)S(1)}, bf16[64,2048]{1,0:T(8,128)(2,1)S(1)}, bf16[64,2048]{1,0:T(8,128)(2,1)S(1)}, bf16[64,2048]{1,0:T(8,128)(2,1)S(1)}) custom-call(s32[1]{0:T(128)} %bitcast.1.member_ref.refs_0_, s32[1]{0:T(128)} %bitcast.2.x_ref.refs_1_, bf16[256,8192]{1,0:T(8,128)(2,1)S(1)} %get-tuple-element.55.refs_0_.refs_2_, ...), custom_call_target="tpu_custom_call" | custom-call | tf_op jit(solution)/shard_map/weighted_sums/pallas_call | solution.py:111
  50.6 2.8 %collective-permute-start.22 = (bf16[64,2048]{1,0:T(8,128)(2,1)S(1)}, bf16[64,2048]{1,0:T(8,128)(2,1)S(1)}, u32[]{:S(2)}, u32[]{:S(2)}) collective-permute-start(bf16[64,2048]{1,0:T(8,128)(2,1)S(1)} %get-tuple-element.88), channel_id=1, source_target_pairs={{0,16},{1,129},{2,18},{3,131},{4,20},{5,133},{6,22},{7,135},{8,24}... | collective-permute-start | bytes 786440 | tf_op jit(solution)/shard_map/ppermute | solution.py:63
  54.8 1.4 %weighted_sums.2 = (bf16[64,2048]{1,0:T(8,128)(2,1)S(1)}, bf16[64,2048]{1,0:T(8,128)(2,1)S(1)}, bf16[64,2048]{1,0:T(8,128)(2,1)S(1)}, bf16[64,2048]{1,0:T(8,128)(2,1)S(1)}) custom-call(s32[1]{0:T(128)} %bitcast.1.member_ref.refs_0_, s32[1]{0:T(128)} %bitcast.2.x_ref.refs_1_, bf16[256,8192]{1,0:T(8,128)(2,1)S(1)} %get-tuple-element.55.refs_0_.refs_2_, ...), custom_call_target="tpu_custom_call" | custom-call | tf_op jit(solution)/shard_map/weighted_sums/pallas_call | solution.py:111
  56.3 3.0 %collective-permute-start.16 = (bf16[64,2048]{1,0:T(8,128)(2,1)S(1)}, bf16[64,2048]{1,0:T(8,128)(2,1)S(1)}, u32[]{:S(2)}, u32[]{:S(2)}) collective-permute-start(bf16[64,2048]{1,0:T(8,128)(2,1)S(1)} %get-tuple-element.80), channel_id=1, source_target_pairs={{0,128},{1,17},{2,130},{3,19},{4,132},{5,21},{6,134},{7,23},{8,136... | collective-permute-start | bytes 786440 | tf_op jit(solution)/shard_map/ppermute | solution.py:63
  60.0 1.5 %collective-permute-start.18 = (bf16[64,2048]{1,0:T(8,128)(2,1)S(1)}, bf16[64,2048]{1,0:T(8,128)(2,1)S(1)}, u32[]{:S(2)}, u32[]{:S(2)}) collective-permute-start(bf16[64,2048]{1,0:T(8,128)(2,1)S(1)} %get-tuple-element.82), channel_id=1, source_target_pairs={{0,192},{1,49},{2,194},{3,51},{4,196},{5,53},{6,198},{7,55},{8,200... | collective-permute-start | bytes 786440 | tf_op jit(solution)/shard_map/ppermute | solution.py:63
  61.5 1.8 %collective-permute-done.23.refs_4_ = bf16[64,2048]{1,0:T(8,128)(2,1)S(1)} collective-permute-done((bf16[64,2048]{1,0:T(8,128)(2,1)S(1)}, bf16[64,2048]{1,0:T(8,128)(2,1)S(1)}, u32[]{:S(2)}, u32[]{:S(2)}) %collective-permute-start.23) | collective-permute-done | bytes 262176 | tf_op jit(solution)/shard_map/ppermute | solution.py:63
  63.3 1.5 %collective-permute-done.24.refs_5_ = bf16[64,2048]{1,0:T(8,128)(2,1)S(1)} collective-permute-done((bf16[64,2048]{1,0:T(8,128)(2,1)S(1)}, bf16[64,2048]{1,0:T(8,128)(2,1)S(1)}, u32[]{:S(2)}, u32[]{:S(2)}) %collective-permute-start.24) | collective-permute-done | bytes 262176 | tf_op jit(solution)/shard_map/ppermute | solution.py:63
  65.0 3.4 %collective-permute-start.25 = (bf16[16,2048]{1,0:T(8,128)(2,1)S(1)}, bf16[16,2048]{1,0:T(8,128)(2,1)S(1)}, u32[]{:S(2)}, u32[]{:S(2)}) collective-permute-start(bf16[16,2048]{1,0:T(8,128)(2,1)S(1)} %get-tuple-element.92), channel_id=1, source_target_pairs={{0,128},{1,17},{2,130},{3,19},{4,132},{5,21},{6,134},{7,23},{8,136... | collective-permute-start | bytes 196616 | tf_op jit(solution)/shard_map/ppermute | solution.py:63
  70.0 2.3 %collective-permute-start.19 = (bf16[16,2048]{1,0:T(8,128)(2,1)S(1)}, bf16[16,2048]{1,0:T(8,128)(2,1)S(1)}, u32[]{:S(2)}, u32[]{:S(2)}) collective-permute-start(bf16[16,2048]{1,0:T(8,128)(2,1)S(1)} %get-tuple-element.84), channel_id=1, source_target_pairs={{0,16},{1,129},{2,18},{3,131},{4,20},{5,133},{6,22},{7,135},{8,24}... | collective-permute-start | bytes 196616 | tf_op jit(solution)/shard_map/ppermute | solution.py:63
  72.3 1.9 %collective-permute-start.20 = (bf16[16,2048]{1,0:T(8,128)(2,1)S(1)}, bf16[16,2048]{1,0:T(8,128)(2,1)S(1)}, u32[]{:S(2)}, u32[]{:S(2)}) collective-permute-start(bf16[16,2048]{1,0:T(8,128)(2,1)S(1)} %get-tuple-element.85), channel_id=1, source_target_pairs={{0,32},{1,65},{2,34},{3,67},{4,36},{5,69},{6,38},{7,71},{8,40},{9,... | collective-permute-start | bytes 196616 | tf_op jit(solution)/shard_map/ppermute | solution.py:63
  78.6 6.7 %collective-permute-start.28 = (bf16[16,1024]{1,0:T(8,128)(2,1)S(1)}, bf16[16,1024]{1,0:T(8,128)(2,1)S(1)}, u32[]{:S(2)}, u32[]{:S(2)}) collective-permute-start(bf16[16,1024]{1,0:T(8,128)(2,1)S(1)} %get-tuple-element.96), channel_id=1, source_target_pairs={{0,8},{1,9},{2,10},{3,11},{4,12},{5,13},{6,14},{7,15},{8,0},{9,1},... | collective-permute-start | bytes 98312 | tf_op jit(solution)/shard_map/ppermute | solution.py:63
  85.2 1.5 %collective-permute-start.29 = (bf16[16,1024]{1,0:T(8,128)(2,1)S(1)}, bf16[16,1024]{1,0:T(8,128)(2,1)S(1)}, u32[]{:S(2)}, u32[]{:S(2)}) collective-permute-start(bf16[16,1024]{1,0:T(8,128)(2,1)S(1)} %get-tuple-element.97), channel_id=1, source_target_pairs={{0,4},{1,5},{2,6},{3,7},{4,0},{5,1},{6,2},{7,3},{8,12},{9,13},{10,... | collective-permute-start | bytes 98312 | tf_op jit(solution)/shard_map/ppermute | solution.py:63
  87.5 2.5 %collective-permute-done.29 = bf16[16,1024]{1,0:T(8,128)(2,1)S(1)} collective-permute-done((bf16[16,1024]{1,0:T(8,128)(2,1)S(1)}, bf16[16,1024]{1,0:T(8,128)(2,1)S(1)}, u32[]{:S(2)}, u32[]{:S(2)}) %collective-permute-start.29) | collective-permute-done | bytes 32800 | tf_op jit(solution)/shard_map/ppermute | solution.py:63
  90.1 2.7 %collective-permute-done.30 = bf16[16,1024]{1,0:T(8,128)(2,1)S(1)} collective-permute-done((bf16[16,1024]{1,0:T(8,128)(2,1)S(1)}, bf16[16,1024]{1,0:T(8,128)(2,1)S(1)}, u32[]{:S(2)}, u32[]{:S(2)}) %collective-permute-start.30) | collective-permute-done | bytes 32800 | tf_op jit(solution)/shard_map/ppermute | solution.py:63
  (50 shorter events, 18.9 us)
Async XLA Ops:
  2.0 11.9 %collective-permute-start = (bf16[32,8320]{1,0:T(8,128)(2,1)S(1)}, bf16[32,8320]{1,0:T(8,128)(2,1)S(1)}, u32[]{:S(2)}, u32[]{:S(2)}) collective-permute-start(bf16[32,8320]{1,0:T(8,128)(2,1)S(1)} %get-tuple-element.56), channel_id=1, source_target_pairs={{0,1},{1,0},{2,3},{3,2},{4,5},{5,4},{6,7},{7,6},{8,9},{9,8},{10,11... | collective-permute-start | bytes 1597448 | tf_op jit(solution)/shard_map/ppermute | solution.py:63
  2.1 14.7 %collective-permute-start.1 = (bf16[32,8320]{1,0:T(8,128)(2,1)S(1)}, bf16[32,8320]{1,0:T(8,128)(2,1)S(1)}, u32[]{:S(2)}, u32[]{:S(2)}) collective-permute-start(bf16[32,8320]{1,0:T(8,128)(2,1)S(1)} %get-tuple-element.59.after), channel_id=1, source_target_pairs={{0,2},{1,3},{2,0},{3,1},{4,6},{5,7},{6,4},{7,5},{8,10},{9,11},{10,... | collective-permute-start | bytes 1597448 | tf_op jit(solution)/shard_map/ppermute | solution.py:63
  5.1 11.1 %collective-permute-start.4 = (bf16[16,8192]{1,0:T(8,128)(2,1)S(1)}, bf16[16,8192]{1,0:T(8,128)(2,1)S(1)}, u32[]{:S(2)}, u32[]{:S(2)}) collective-permute-start(bf16[16,8192]{1,0:T(8,128)(2,1)S(1)} %own_references.1.refs_8_.refs_10_), channel_id=1, source_target_pairs={{0,32},{1,33},{2,34},{3,35},{4,36},{5,37},{6,38},{7,39},{8,40},{9,... | collective-permute-start | bytes 786440 | tf_op jit(solution)/shard_map/ppermute | solution.py:63
  5.7 10.5 %collective-permute-start.3 = (bf16[16,8192]{1,0:T(8,128)(2,1)S(1)}, bf16[16,8192]{1,0:T(8,128)(2,1)S(1)}, u32[]{:S(2)}, u32[]{:S(2)}) collective-permute-start(bf16[16,8192]{1,0:T(8,128)(2,1)S(1)} %own_references.1.refs_8_.refs_10_), channel_id=1, source_target_pairs={{0,192},{1,193},{2,194},{3,195},{4,196},{5,197},{6,198},{7,199},{8... | collective-permute-start | bytes 786440 | tf_op jit(solution)/shard_map/ppermute | solution.py:63
  8.7 7.8 %collective-permute-start.2 = (bf16[16,8192]{1,0:T(8,128)(2,1)S(1)}, bf16[16,8192]{1,0:T(8,128)(2,1)S(1)}, u32[]{:S(2)}, u32[]{:S(2)}) collective-permute-start(bf16[16,8192]{1,0:T(8,128)(2,1)S(1)} %own_references.1.refs_8_.refs_10_), channel_id=1, source_target_pairs={{0,64},{1,65},{2,66},{3,67},{4,68},{5,69},{6,70},{7,71},{8,72},{9,... | collective-permute-start | bytes 786440 | tf_op jit(solution)/shard_map/ppermute | solution.py:63
  16.8 16.4 %collective-permute-start.5 = (bf16[32,8320]{1,0:T(8,128)(2,1)S(1)}, bf16[32,8320]{1,0:T(8,128)(2,1)S(1)}, u32[]{:S(2)}, u32[]{:S(2)}) collective-permute-start(bf16[32,8320]{1,0:T(8,128)(2,1)S(1)} %get-tuple-element.63), channel_id=1, source_target_pairs={{0,3},{1,2},{2,1},{3,0},{4,7},{5,6},{6,5},{7,4},{8,11},{9,10},{10,... | collective-permute-start | bytes 1597448 | tf_op jit(solution)/shard_map/ppermute | solution.py:63
  17.8 10.7 %collective-permute-start.6 = (bf16[16,8192]{1,0:T(8,128)(2,1)S(1)}, bf16[16,8192]{1,0:T(8,128)(2,1)S(1)}, u32[]{:S(2)}, u32[]{:S(2)}) collective-permute-start(bf16[16,8192]{1,0:T(8,128)(2,1)S(1)} %collective-permute-done.4.refs_5_.refs_7_), channel_id=1, source_target_pairs={{0,128},{1,129},{2,130},{3,131},{4,132},{5,133},{6,134},{7,135},{8... | collective-permute-start | bytes 786440 | tf_op jit(solution)/shard_map/ppermute | solution.py:63
  21.0 10.2 %collective-permute-start.7 = (bf16[16,8192]{1,0:T(8,128)(2,1)S(1)}, bf16[16,8192]{1,0:T(8,128)(2,1)S(1)}, u32[]{:S(2)}, u32[]{:S(2)}) collective-permute-start(bf16[16,8192]{1,0:T(8,128)(2,1)S(1)} %relay.1), channel_id=1, source_target_pairs={{0,192},{1,65},{2,194},{3,67},{4,196},{5,69},{6,198},{7,71},{8,200... | collective-permute-start | bytes 786440 | tf_op jit(solution)/shard_map/ppermute | solution.py:63
  22.2 9.1 %collective-permute-start.8 = (bf16[16,8192]{1,0:T(8,128)(2,1)S(1)}, bf16[16,8192]{1,0:T(8,128)(2,1)S(1)}, u32[]{:S(2)}, u32[]{:S(2)}) collective-permute-start(bf16[16,8192]{1,0:T(8,128)(2,1)S(1)} %collective-permute-done.2.one.refs_6_.refs_8_), channel_id=1, source_target_pairs={{0,32},{1,33},{2,34},{3,35},{4,36},{5,37},{6,38},{7,39},{8,40},{9,... | collective-permute-start | bytes 786440 | tf_op jit(solution)/shard_map/ppermute | solution.py:63
  22.7 8.5 %collective-permute-start.9 = (bf16[16,8192]{1,0:T(8,128)(2,1)S(1)}, bf16[16,8192]{1,0:T(8,128)(2,1)S(1)}, u32[]{:S(2)}, u32[]{:S(2)}) collective-permute-start(bf16[16,8192]{1,0:T(8,128)(2,1)S(1)} %collective-permute-done.3.other.refs_7_.refs_9_), channel_id=1, source_target_pairs={{0,48},{1,49},{2,50},{3,51},{4,52},{5,53},{6,54},{7,55},{8,56},{9,... | collective-permute-start | bytes 786440 | tf_op jit(solution)/shard_map/ppermute | solution.py:63
  32.9 8.9 %collective-permute-start.10 = (f32[256,128]{1,0:T(8,128)S(1)}, f32[256,128]{1,0:T(8,128)S(1)}, u32[]{:S(2)}, u32[]{:S(2)}) collective-permute-start(f32[256,128]{1,0:T(8,128)S(1)} %get-tuple-element.68), channel_id=1, source_target_pairs={{0,2},{1,3},{2,0},{3,1},{4,6},{5,7},{6,4},{7,5},{8,10},{9,11},{10,... | collective-permute-start | bytes 393224 | tf_op jit(solution)/shard_map/ppermute | solution.py:63
  37.1 5.6 %collective-permute-start.11 = (f32[256,128]{1,0:T(8,128)S(1)}, f32[256,128]{1,0:T(8,128)S(1)}, u32[]{:S(2)}, u32[]{:S(2)}) collective-permute-start(f32[256,128]{1,0:T(8,128)S(1)} %partial_scores.4), channel_id=1, source_target_pairs={{0,3},{1,2},{2,1},{3,0},{4,7},{5,6},{6,5},{7,4},{8,11},{9,10},{10,... | collective-permute-start | bytes 393224 | tf_op jit(solution)/shard_map/ppermute | solution.py:63
  41.2 1.6 %collective-permute-start.12 = (f32[256,128]{1,0:T(8,128)S(1)}, f32[256,128]{1,0:T(8,128)S(1)}, u32[]{:S(2)}, u32[]{:S(2)}) collective-permute-start(f32[256,128]{1,0:T(8,128)S(1)} %get-tuple-element.78), channel_id=1, source_target_pairs={{0,1},{1,0},{2,3},{3,2},{4,5},{5,4},{6,7},{7,6},{8,9},{9,8},{10,11... | collective-permute-start | bytes 393224 | tf_op jit(solution)/shard_map/ppermute | solution.py:63
  43.1 4.1 %collective-permute-start.15 = (bf16[128,256]{1,0:T(8,128)(2,1)S(1)}, bf16[128,256]{1,0:T(8,128)(2,1)S(1)}, u32[]{:S(2)}, u32[]{:S(2)}) collective-permute-start(bf16[128,256]{1,0:T(8,128)(2,1)S(1)} %posterior.1.refs_6_), channel_id=1, source_target_pairs={{0,3},{1,2},{2,1},{3,0},{4,7},{5,6},{6,5},{7,4},{8,11},{9,10},{10,... | collective-permute-start | bytes 196616 | tf_op jit(solution)/shard_map/ppermute | solution.py:63
  44.8 4.4 %collective-permute-start.14 = (bf16[128,256]{1,0:T(8,128)(2,1)S(1)}, bf16[128,256]{1,0:T(8,128)(2,1)S(1)}, u32[]{:S(2)}, u32[]{:S(2)}) collective-permute-start(bf16[128,256]{1,0:T(8,128)(2,1)S(1)} %posterior.1.refs_6_), channel_id=1, source_target_pairs={{0,2},{1,3},{2,0},{3,1},{4,6},{5,7},{6,4},{7,5},{8,10},{9,11},{10,... | collective-permute-start | bytes 196616 | tf_op jit(solution)/shard_map/ppermute | solution.py:63
  45.2 4.0 %collective-permute-start.13 = (bf16[128,256]{1,0:T(8,128)(2,1)S(1)}, bf16[128,256]{1,0:T(8,128)(2,1)S(1)}, u32[]{:S(2)}, u32[]{:S(2)}) collective-permute-start(bf16[128,256]{1,0:T(8,128)(2,1)S(1)} %posterior.1.refs_6_), channel_id=1, source_target_pairs={{0,1},{1,0},{2,3},{3,2},{4,5},{5,4},{6,7},{7,6},{8,9},{9,8},{10,11... | collective-permute-start | bytes 196616 | tf_op jit(solution)/shard_map/ppermute | solution.py:63
  50.6 9.4 %collective-permute-start.22 = (bf16[64,2048]{1,0:T(8,128)(2,1)S(1)}, bf16[64,2048]{1,0:T(8,128)(2,1)S(1)}, u32[]{:S(2)}, u32[]{:S(2)}) collective-permute-start(bf16[64,2048]{1,0:T(8,128)(2,1)S(1)} %get-tuple-element.88), channel_id=1, source_target_pairs={{0,16},{1,129},{2,18},{3,131},{4,20},{5,133},{6,22},{7,135},{8,24}... | collective-permute-start | bytes 786440 | tf_op jit(solution)/shard_map/ppermute | solution.py:63
  53.5 9.8 %collective-permute-start.23 = (bf16[64,2048]{1,0:T(8,128)(2,1)S(1)}, bf16[64,2048]{1,0:T(8,128)(2,1)S(1)}, u32[]{:S(2)}, u32[]{:S(2)}) collective-permute-start(bf16[64,2048]{1,0:T(8,128)(2,1)S(1)} %get-tuple-element.89), channel_id=1, source_target_pairs={{0,32},{1,65},{2,34},{3,67},{4,36},{5,69},{6,38},{7,71},{8,40},{9,... | collective-permute-start | bytes 786440 | tf_op jit(solution)/shard_map/ppermute | solution.py:63
  54.6 10.2 %collective-permute-start.24 = (bf16[64,2048]{1,0:T(8,128)(2,1)S(1)}, bf16[64,2048]{1,0:T(8,128)(2,1)S(1)}, u32[]{:S(2)}, u32[]{:S(2)}) collective-permute-start(bf16[64,2048]{1,0:T(8,128)(2,1)S(1)} %get-tuple-element.90), channel_id=1, source_target_pairs={{0,48},{1,193},{2,50},{3,195},{4,52},{5,197},{6,54},{7,199},{8,56}... | collective-permute-start | bytes 786440 | tf_op jit(solution)/shard_map/ppermute | solution.py:63
  56.3 13.2 %collective-permute-start.16 = (bf16[64,2048]{1,0:T(8,128)(2,1)S(1)}, bf16[64,2048]{1,0:T(8,128)(2,1)S(1)}, u32[]{:S(2)}, u32[]{:S(2)}) collective-permute-start(bf16[64,2048]{1,0:T(8,128)(2,1)S(1)} %get-tuple-element.80), channel_id=1, source_target_pairs={{0,128},{1,17},{2,130},{3,19},{4,132},{5,21},{6,134},{7,23},{8,136... | collective-permute-start | bytes 786440 | tf_op jit(solution)/shard_map/ppermute | solution.py:63
  59.3 10.6 %collective-permute-start.17 = (bf16[64,2048]{1,0:T(8,128)(2,1)S(1)}, bf16[64,2048]{1,0:T(8,128)(2,1)S(1)}, u32[]{:S(2)}, u32[]{:S(2)}) collective-permute-start(bf16[64,2048]{1,0:T(8,128)(2,1)S(1)} %get-tuple-element.81), channel_id=1, source_target_pairs={{0,64},{1,33},{2,66},{3,35},{4,68},{5,37},{6,70},{7,39},{8,72},{9,... | collective-permute-start | bytes 786440 | tf_op jit(solution)/shard_map/ppermute | solution.py:63
  60.0 9.8 %collective-permute-start.18 = (bf16[64,2048]{1,0:T(8,128)(2,1)S(1)}, bf16[64,2048]{1,0:T(8,128)(2,1)S(1)}, u32[]{:S(2)}, u32[]{:S(2)}) collective-permute-start(bf16[64,2048]{1,0:T(8,128)(2,1)S(1)} %get-tuple-element.82), channel_id=1, source_target_pairs={{0,192},{1,49},{2,194},{3,51},{4,196},{5,53},{6,198},{7,55},{8,200... | collective-permute-start | bytes 786440 | tf_op jit(solution)/shard_map/ppermute | solution.py:63
  65.0 9.3 %collective-permute-start.25 = (bf16[16,2048]{1,0:T(8,128)(2,1)S(1)}, bf16[16,2048]{1,0:T(8,128)(2,1)S(1)}, u32[]{:S(2)}, u32[]{:S(2)}) collective-permute-start(bf16[16,2048]{1,0:T(8,128)(2,1)S(1)} %get-tuple-element.92), channel_id=1, source_target_pairs={{0,128},{1,17},{2,130},{3,19},{4,132},{5,21},{6,134},{7,23},{8,136... | collective-permute-start | bytes 196616 | tf_op jit(solution)/shard_map/ppermute | solution.py:63
  68.3 5.9 %collective-permute-start.26 = (bf16[16,2048]{1,0:T(8,128)(2,1)S(1)}, bf16[16,2048]{1,0:T(8,128)(2,1)S(1)}, u32[]{:S(2)}, u32[]{:S(2)}) collective-permute-start(bf16[16,2048]{1,0:T(8,128)(2,1)S(1)} %get-tuple-element.93), channel_id=1, source_target_pairs={{0,64},{1,33},{2,66},{3,35},{4,68},{5,37},{6,70},{7,39},{8,72},{9,... | collective-permute-start | bytes 196616 | tf_op jit(solution)/shard_map/ppermute | solution.py:63
  69.5 6.1 %collective-permute-start.27 = (bf16[16,2048]{1,0:T(8,128)(2,1)S(1)}, bf16[16,2048]{1,0:T(8,128)(2,1)S(1)}, u32[]{:S(2)}, u32[]{:S(2)}) collective-permute-start(bf16[16,2048]{1,0:T(8,128)(2,1)S(1)} %get-tuple-element.94), channel_id=1, source_target_pairs={{0,192},{1,49},{2,194},{3,51},{4,196},{5,53},{6,198},{7,55},{8,200... | collective-permute-start | bytes 196616 | tf_op jit(solution)/shard_map/ppermute | solution.py:63
  70.0 5.9 %collective-permute-start.19 = (bf16[16,2048]{1,0:T(8,128)(2,1)S(1)}, bf16[16,2048]{1,0:T(8,128)(2,1)S(1)}, u32[]{:S(2)}, u32[]{:S(2)}) collective-permute-start(bf16[16,2048]{1,0:T(8,128)(2,1)S(1)} %get-tuple-element.84), channel_id=1, source_target_pairs={{0,16},{1,129},{2,18},{3,131},{4,20},{5,133},{6,22},{7,135},{8,24}... | collective-permute-start | bytes 196616 | tf_op jit(solution)/shard_map/ppermute | solution.py:63
  72.3 4.8 %collective-permute-start.20 = (bf16[16,2048]{1,0:T(8,128)(2,1)S(1)}, bf16[16,2048]{1,0:T(8,128)(2,1)S(1)}, u32[]{:S(2)}, u32[]{:S(2)}) collective-permute-start(bf16[16,2048]{1,0:T(8,128)(2,1)S(1)} %get-tuple-element.85), channel_id=1, source_target_pairs={{0,32},{1,65},{2,34},{3,67},{4,36},{5,69},{6,38},{7,71},{8,40},{9,... | collective-permute-start | bytes 196616 | tf_op jit(solution)/shard_map/ppermute | solution.py:63
  74.2 4.3 %collective-permute-start.21 = (bf16[16,2048]{1,0:T(8,128)(2,1)S(1)}, bf16[16,2048]{1,0:T(8,128)(2,1)S(1)}, u32[]{:S(2)}, u32[]{:S(2)}) collective-permute-start(bf16[16,2048]{1,0:T(8,128)(2,1)S(1)} %get-tuple-element.86), channel_id=1, source_target_pairs={{0,48},{1,193},{2,50},{3,195},{4,52},{5,197},{6,54},{7,199},{8,56}... | collective-permute-start | bytes 196616 | tf_op jit(solution)/shard_map/ppermute | solution.py:63
  78.6 9.0 %collective-permute-start.28 = (bf16[16,1024]{1,0:T(8,128)(2,1)S(1)}, bf16[16,1024]{1,0:T(8,128)(2,1)S(1)}, u32[]{:S(2)}, u32[]{:S(2)}) collective-permute-start(bf16[16,1024]{1,0:T(8,128)(2,1)S(1)} %get-tuple-element.96), channel_id=1, source_target_pairs={{0,8},{1,9},{2,10},{3,11},{4,12},{5,13},{6,14},{7,15},{8,0},{9,1},... | collective-permute-start | bytes 98312 | tf_op jit(solution)/shard_map/ppermute | solution.py:63
  85.2 4.8 %collective-permute-start.29 = (bf16[16,1024]{1,0:T(8,128)(2,1)S(1)}, bf16[16,1024]{1,0:T(8,128)(2,1)S(1)}, u32[]{:S(2)}, u32[]{:S(2)}) collective-permute-start(bf16[16,1024]{1,0:T(8,128)(2,1)S(1)} %get-tuple-element.97), channel_id=1, source_target_pairs={{0,4},{1,5},{2,6},{3,7},{4,0},{5,1},{6,2},{7,3},{8,12},{9,13},{10,... | collective-permute-start | bytes 98312 | tf_op jit(solution)/shard_map/ppermute | solution.py:63
  86.7 6.0 %collective-permute-start.30 = (bf16[16,1024]{1,0:T(8,128)(2,1)S(1)}, bf16[16,1024]{1,0:T(8,128)(2,1)S(1)}, u32[]{:S(2)}, u32[]{:S(2)}) collective-permute-start(bf16[16,1024]{1,0:T(8,128)(2,1)S(1)} %get-tuple-element.98), channel_id=1, source_target_pairs={{0,12},{1,13},{2,14},{3,15},{4,8},{5,9},{6,10},{7,11},{8,4},{9,5},... | collective-permute-start | bytes 98312 | tf_op jit(solution)/shard_map/ppermute | solution.py:63

commit v17 on v16

--- a/solution.py
+++ b/solution.py
@@ -34,13 +34,6 @@
 def flips(y=0, x=0, z=0):
     return [
         (linear(i, j, k, c), linear(i ^ y, j ^ x, k ^ z, c))
-        for i in range(Y) for j in range(X) for k in range(Z) for c in range(2)
-    ]
-
-
-def crossed(n, core):
-    return [
-        (linear(i, j, k, c), linear(i ^ (n if c == core else 0), j ^ (0 if c == core else n), k, c))
         for i in range(Y) for j in range(X) for k in range(Z) for c in range(2)
     ]
 
@@ -380,7 +373,7 @@
 
 def accum_kernel(part, member_ref, x_ref, *refs):
     rows, posts, outs = refs[:G], refs[G : 2 * G], refs[2 * G :]
-    along_y = (member_ref[0] & 1) == part
+    along_y = part == 0
     high = x_ref[0] >> 1
 
     @pl.loop(0, NB, unroll=True)
@@ -402,7 +395,7 @@
                 for_y = sums[group & 1][at : at + 16]
                 at = group * 32 + (n & 1) * 16
                 for_x = jnp.where(upper, sums[1][at : at + 16], sums[0][at : at + 16])
-                out[group * 16 : (group + 1) * 16, spot] = jnp.where(along_y, for_y, for_x).astype(BF16)
+                out[group * 16 : (group + 1) * 16, spot] = (for_y if along_y else for_x).astype(BF16)
 
 
 def make_accum(part, member, x_at, rows, posts):
@@ -423,9 +416,9 @@
 
 
 def turn_kernel(part, member_ref, x_ref, *refs):
-    along_y = (member_ref[0] & 1) == part
+    along_y = part == 0
     for n, out in enumerate(refs[4:]):
-        group = jnp.where(along_y, (n & 1) * 2 + ((x_ref[0] >> 1) ^ (n >> 1)), n)
+        group = (n & 1) * 2 + ((x_ref[0] >> 1) ^ (n >> 1)) if along_y else n
         mine = pl.ds(pl.multiple_of(group * 16, 16), 16)
         out[...] = added([ref[mine, :] for ref in refs[:4]]).astype(out.dtype)
 
@@ -491,13 +484,13 @@
     rows = [rows[n] for n in range(G)]
 
     first = make_accum(0, member, x_at, rows, posts)
-    first = [first[0]] + [send(first[n], crossed(n, 0)) for n in (2, 1, 3)]
+    first = [first[0]] + [send(first[n], flips(y=n)) for n in (2, 1, 3)]
     second = make_accum(1, member, x_at, rows, posts)
-    second = [second[0]] + [send(second[n], crossed(n, 1)) for n in (2, 1, 3)]
+    second = [second[0]] + [send(second[n], flips(x=n)) for n in (2, 1, 3)]
     first = make_turn(0, member, x_at, first)
-    first = [first[0]] + [send(first[n], crossed(n, 1)) for n in (2, 1, 3)]
+    first = [first[0]] + [send(first[n], flips(x=n)) for n in (2, 1, 3)]
     second = make_turn(1, member, x_at, second)
-    second = [second[0]] + [send(second[n], crossed(n, 0)) for n in (2, 1, 3)]
+    second = [second[0]] + [send(second[n], flips(y=n)) for n in (2, 1, 3)]
     outs = [((16, COLS), F32)] + [((16, COLS), BF16)] * (NB - 1)
     ends = local(joined_kernel, "joined_sums", outs, [block], [*first, *second], 4)
     return added([ends[0]] + [send(ends[n], flips(z=n * (G // 2))) for n in (2, 1, 3)])

time: 94.2 us -> 96.2 us (1.021)
  starting transfers between devices: 45.1 us -> 46.7 us
    ppermute x31, starting transfers between devices: 45.1 us -> 46.7 us  [send(): return lax.ppermute(value, AXES, pairs)]
  transfers between devices with their start and end apart: 31 -> 31, of which waited for: 17 -> 17; matrix products, arithmetic and copies ran while one was open for 0% -> 0% of each run, Pallas kernels for 22% -> 21%
where the time goes in v17:
time: 96.2 us; the launch traced here: 95.2 us
  starting transfers between devices  46.7 us (49%)
  Pallas kernels  24 us (25%)
  waiting for transfers between devices  23.7 us (25%)
    ppermute x31, starting transfers between devices, send(): return lax.ppermute(value, AXES, pairs)  46.7 us
    pallas_call x19, Pallas kernels, local(): pl.pallas_call(kernel, in_specs=[SCALARS] * len(scalars) + [PLACED] * pla...  24 us
    ppermute x31, waiting for transfers between devices, send(): return lax.ppermute(value, AXES, pairs)  23.7 us
  transfers between devices with their start and end apart: 31, of which 17 were waited for; matrix products, arithmetic and copies ran while one was open for 0% of the time, Pallas kernels for 21%

profile of v17, /device:TPU:2, one launch (start us, length us, event | category | flops | bytes accessed | tf_op | source)
XLA Modules:
  0.0 95.2 jit_solution(10668810289868146569)
XLA Ops:
  0.0 2.0 %split_particles.1 = (bf16[32,8320]{1,0:T(8,128)(2,1)S(1)}, bf16[32,8320]{1,0:T(8,128)(2,1)S(1)}, bf16[32,8320]{1,0:T(8,128)(2,1)S(1)}, bf16[32,8320]{1,0:T(8,128)(2,1)S(1)}) custom-call(s32[1]{0:T(128)} %bitcast.1.member_ref.refs_0_, s32[1]{0:T(128)} %bitcast.block_ref, s32[1]{0:T(128)} %bitcast.2.x_ref.refs_1_, bf16[32,32768]{1,0:T(8,128)(2,1)} %source.2, ...), custom_call_target="tpu_custom_call" | custom-call | tf_op jit(solution)/shard_map/split_particles/pallas_call | solution.py:104
  2.1 2.0 %collective-permute-start.1 = (bf16[32,8320]{1,0:T(8,128)(2,1)S(1)}, bf16[32,8320]{1,0:T(8,128)(2,1)S(1)}, u32[]{:S(2)}, u32[]{:S(2)}) collective-permute-start(bf16[32,8320]{1,0:T(8,128)(2,1)S(1)} %get-tuple-element.59.after), channel_id=1, source_target_pairs={{0,2},{1,3},{2,0},{3,1},{4,6},{5,7},{6,4},{7,5},{8,10},{9,11},{10,... | collective-permute-start | bytes 1597448 | tf_op jit(solution)/shard_map/ppermute | solution.py:56
  5.7 3.0 %collective-permute-start.3 = (bf16[16,8192]{1,0:T(8,128)(2,1)S(1)}, bf16[16,8192]{1,0:T(8,128)(2,1)S(1)}, u32[]{:S(2)}, u32[]{:S(2)}) collective-permute-start(bf16[16,8192]{1,0:T(8,128)(2,1)S(1)} %own_references.1.refs_8_.refs_10_), channel_id=1, source_target_pairs={{0,192},{1,193},{2,194},{3,195},{4,196},{5,197},{6,198},{7,199},{8... | collective-permute-start | bytes 786440 | tf_op jit(solution)/shard_map/ppermute | solution.py:56
  8.9 2.7 %phase_table.1 = (bf16[256,8192]{1,0:T(8,128)(2,1)S(1)}, f32[4,8,1024]{2,1,0:T(8,128)S(1)}) custom-call(s32[1]{0:T(128)} %bitcast.1.member_ref.refs_0_, f32[16,8,1024]{2,1,0:T(8,128)} %constant.63.clone.geo_ref), custom_call_target="tpu_custom_call" | custom-call | tf_op jit(solution)/shard_map/phase_table/pallas_call | solution.py:104
  11.6 2.3 %shifted_rows.4 = (bf16[256,8192]{1,0:T(8,128)(2,1)S(1)}, bf16[32,4096]{1,0:T(8,128)(2,1)S(1)}) custom-call(s32[1]{0:T(128)} %bitcast.1.member_ref.refs_0_, bf16[32,8320]{1,0:T(8,128)(2,1)S(1)} %get-tuple-element.52.x_ref, f32[4,8,1024]{2,1,0:T(8,128)S(1)} %get-tuple-element.53.geo_ref, bf16[256,8192]{1,0:T(8,128)(2,1)S(1)} %get-tuple-element.54.table_ref), custom_call_target="tpu_custom_call" | custom-call | tf_op jit(solution)/shard_map/shifted_rows/pallas_call | solution.py:104
  13.9 2.3 %shifted_rows.5 = (bf16[256,8192]{1,0:T(8,128)(2,1)S(1)}, bf16[32,4096]{1,0:T(8,128)(2,1)S(1)}) custom-call(s32[1]{0:T(128)} %bitcast.1.member_ref.refs_0_, bf16[32,8320]{1,0:T(8,128)(2,1)S(1)} %collective-permute-done.x_ref, f32[4,8,1024]{2,1,0:T(8,128)S(1)} %get-tuple-element.53.geo_ref, bf16[256,8192]{1,0:T(8,128)(2,1)S(1)} %get-tuple-element.54.table_ref), custom_call_target="tpu_custom_call" | custom-call | tf_op jit(solution)/shard_map/shifted_rows/pallas_call | solution.py:104
  17.8 3.2 %collective-permute-start.6 = (bf16[16,8192]{1,0:T(8,128)(2,1)S(1)}, bf16[16,8192]{1,0:T(8,128)(2,1)S(1)}, u32[]{:S(2)}, u32[]{:S(2)}) collective-permute-start(bf16[16,8192]{1,0:T(8,128)(2,1)S(1)} %collective-permute-done.4.refs_5_.refs_7_), channel_id=1, source_target_pairs={{0,128},{1,129},{2,130},{3,131},{4,132},{5,133},{6,134},{7,135},{8... | collective-permute-start | bytes 786440 | tf_op jit(solution)/shard_map/ppermute | solution.py:56
  22.7 2.2 %collective-permute-start.9 = (bf16[16,8192]{1,0:T(8,128)(2,1)S(1)}, bf16[16,8192]{1,0:T(8,128)(2,1)S(1)}, u32[]{:S(2)}, u32[]{:S(2)}) collective-permute-start(bf16[16,8192]{1,0:T(8,128)(2,1)S(1)} %collective-permute-done.3.other.refs_7_.refs_9_), channel_id=1, source_target_pairs={{0,48},{1,49},{2,50},{3,51},{4,52},{5,53},{6,54},{7,55},{8,56},{9,... | collective-permute-start | bytes 786440 | tf_op jit(solution)/shard_map/ppermute | solution.py:56
  24.9 2.3 %shifted_rows.6 = (bf16[256,8192]{1,0:T(8,128)(2,1)S(1)}, bf16[32,4096]{1,0:T(8,128)(2,1)S(1)}) custom-call(s32[1]{0:T(128)} %bitcast.1.member_ref.refs_0_, bf16[32,8320]{1,0:T(8,128)(2,1)S(1)} %collective-permute-done.1.x_ref, f32[4,8,1024]{2,1,0:T(8,128)S(1)} %get-tuple-element.53.geo_ref, bf16[256,8192]{1,0:T(8,128)(2,1)S(1)} %get-tuple-element.54.table_ref), custom_call_target="tpu_custom_call" | custom-call | tf_op jit(solution)/shard_map/shifted_rows/pallas_call | solution.py:104
  27.2 1.4 %collective-permute-done.6.one = bf16[16,8192]{1,0:T(8,128)(2,1)S(1)} collective-permute-done((bf16[16,8192]{1,0:T(8,128)(2,1)S(1)}, bf16[16,8192]{1,0:T(8,128)(2,1)S(1)}, u32[]{:S(2)}, u32[]{:S(2)}) %collective-permute-start.6) | collective-permute-done | bytes 262176 | tf_op jit(solution)/shard_map/ppermute | solution.py:56
  28.5 2.7 %collective-permute-done.7.other = bf16[16,8192]{1,0:T(8,128)(2,1)S(1)} collective-permute-done((bf16[16,8192]{1,0:T(8,128)(2,1)S(1)}, bf16[16,8192]{1,0:T(8,128)(2,1)S(1)}, u32[]{:S(2)}, u32[]{:S(2)}) %collective-permute-start.7) | collective-permute-done | bytes 262176 | tf_op jit(solution)/shard_map/ppermute | solution.py:56
  31.3 1.6 %partial_scores.3 = (f32[256,128]{1,0:T(8,128)S(1)}, bf16[128,4096]{1,0:T(8,128)(2,1)S(1)}) custom-call(bf16[256,8192]{1,0:T(8,128)(2,1)S(1)} %get-tuple-element.61.refs_0_.refs_4_, bf16[32,4096]{1,0:T(8,128)(2,1)S(1)} %get-tuple-element.64.refs_1_, bf16[32,8192]{1,0:T(8,128)(2,1)S(1)} %pair.1.refs_2_.refs_4_, ...), custom_call_target="tpu_custom_call" | custom-call | tf_op jit(solution)/shard_map/partial_scores/pallas_call | solution.py:104
  33.3 2.3 %shifted_rows.7 = (bf16[256,8192]{1,0:T(8,128)(2,1)S(1)}, bf16[32,4096]{1,0:T(8,128)(2,1)S(1)}) custom-call(s32[1]{0:T(128)} %bitcast.1.member_ref.refs_0_, bf16[32,8320]{1,0:T(8,128)(2,1)S(1)} %collective-permute-done.5.x_ref, f32[4,8,1024]{2,1,0:T(8,128)S(1)} %get-tuple-element.53.geo_ref, bf16[256,8192]{1,0:T(8,128)(2,1)S(1)} %get-tuple-element.54.table_ref), custom_call_target="tpu_custom_call" | custom-call | tf_op jit(solution)/shard_map/shifted_rows/pallas_call | solution.py:104
  35.6 1.5 %partial_scores.4 = f32[256,128]{1,0:T(8,128)S(1)} custom-call(bf16[256,8192]{1,0:T(8,128)(2,1)S(1)} %get-tuple-element.70.refs_0_.refs_5_, bf16[32,4096]{1,0:T(8,128)(2,1)S(1)} %get-tuple-element.73.refs_1_, bf16[32,8192]{1,0:T(8,128)(2,1)S(1)} %pair.1.refs_2_.refs_4_, bf16[16,8192]{1,0:T(8,128)(2,1)S(1)} %collective-permute-done.8.refs_3_.refs_5_, ...), custom_call_target="tpu_custom_call" | custom-call | tf_op jit(solution)/shard_map/partial_scores/pallas_call | solution.py:104
  37.1 1.4 %collective-permute-start.11 = (f32[256,128]{1,0:T(8,128)S(1)}, f32[256,128]{1,0:T(8,128)S(1)}, u32[]{:S(2)}, u32[]{:S(2)}) collective-permute-start(f32[256,128]{1,0:T(8,128)S(1)} %partial_scores.4), channel_id=1, source_target_pairs={{0,3},{1,2},{2,1},{3,0},{4,7},{5,6},{6,5},{7,4},{8,11},{9,10},{10,... | collective-permute-start | bytes 393224 | tf_op jit(solution)/shard_map/ppermute | solution.py:56
  38.5 2.7 %partial_scores.5 = (f32[256,128]{1,0:T(8,128)S(1)}, f32[256,128]{1,0:T(8,128)S(1)}) custom-call(bf16[256,8192]{1,0:T(8,128)(2,1)S(1)} %get-tuple-element.55.refs_0_.refs_2_, bf16[256,8192]{1,0:T(8,128)(2,1)S(1)} %get-tuple-element.58.refs_1_.refs_3_, bf16[32,4096]{1,0:T(8,128)(2,1)S(1)} %get-tuple-element.75.refs_2_, ...), custom_call_target="tpu_custom_call" | custom-call | tf_op jit(solution)/shard_map/partial_scores/pallas_call | solution.py:104
  43.1 1.7 %collective-permute-start.15 = (bf16[128,256]{1,0:T(8,128)(2,1)S(1)}, bf16[128,256]{1,0:T(8,128)(2,1)S(1)}, u32[]{:S(2)}, u32[]{:S(2)}) collective-permute-start(bf16[128,256]{1,0:T(8,128)(2,1)S(1)} %posterior.1.refs_6_), channel_id=1, source_target_pairs={{0,3},{1,2},{2,1},{3,0},{4,7},{5,6},{6,5},{7,4},{8,11},{9,10},{10,... | collective-permute-start | bytes 196616 | tf_op jit(solution)/shard_map/ppermute | solution.py:56
  45.2 2.1 %collective-permute-done.15.refs_9_ = bf16[128,256]{1,0:T(8,128)(2,1)S(1)} collective-permute-done((bf16[128,256]{1,0:T(8,128)(2,1)S(1)}, bf16[128,256]{1,0:T(8,128)(2,1)S(1)}, u32[]{:S(2)}, u32[]{:S(2)}) %collective-permute-start.15) | collective-permute-done | bytes 65568 | tf_op jit(solution)/shard_map/ppermute | solution.py:56
  47.2 1.9 %collective-permute-done.14.refs_8_ = bf16[128,256]{1,0:T(8,128)(2,1)S(1)} collective-permute-done((bf16[128,256]{1,0:T(8,128)(2,1)S(1)}, bf16[128,256]{1,0:T(8,128)(2,1)S(1)}, u32[]{:S(2)}, u32[]{:S(2)}) %collective-permute-start.14) | collective-permute-done | bytes 65568 | tf_op jit(solution)/shard_map/ppermute | solution.py:56
  49.2 1.3 %weighted_sums.3 = (bf16[64,2048]{1,0:T(8,128)(2,1)S(1)}, bf16[64,2048]{1,0:T(8,128)(2,1)S(1)}, bf16[64,2048]{1,0:T(8,128)(2,1)S(1)}, bf16[64,2048]{1,0:T(8,128)(2,1)S(1)}) custom-call(s32[1]{0:T(128)} %bitcast.1.member_ref.refs_0_, s32[1]{0:T(128)} %bitcast.2.x_ref.refs_1_, bf16[256,8192]{1,0:T(8,128)(2,1)S(1)} %get-tuple-element.55.refs_0_.refs_2_, ...), custom_call_target="tpu_custom_call" | custom-call | tf_op jit(solution)/shard_map/weighted_sums/pallas_call | solution.py:104
  50.5 2.8 %collective-permute-start.22 = (bf16[64,2048]{1,0:T(8,128)(2,1)S(1)}, bf16[64,2048]{1,0:T(8,128)(2,1)S(1)}, u32[]{:S(2)}, u32[]{:S(2)}) collective-permute-start(bf16[64,2048]{1,0:T(8,128)(2,1)S(1)} %get-tuple-element.88), channel_id=1, source_target_pairs={{0,16},{1,17},{2,18},{3,19},{4,20},{5,21},{6,22},{7,23},{8,24},{9,... | collective-permute-start | bytes 786440 | tf_op jit(solution)/shard_map/ppermute | solution.py:56
  56.0 3.0 %collective-permute-start.16 = (bf16[64,2048]{1,0:T(8,128)(2,1)S(1)}, bf16[64,2048]{1,0:T(8,128)(2,1)S(1)}, u32[]{:S(2)}, u32[]{:S(2)}) collective-permute-start(bf16[64,2048]{1,0:T(8,128)(2,1)S(1)} %get-tuple-element.80), channel_id=1, source_target_pairs={{0,128},{1,129},{2,130},{3,131},{4,132},{5,133},{6,134},{7,135},{8... | collective-permute-start | bytes 786440 | tf_op jit(solution)/shard_map/ppermute | solution.py:56
  59.8 1.6 %collective-permute-done.22.refs_3_ = bf16[64,2048]{1,0:T(8,128)(2,1)S(1)} collective-permute-done((bf16[64,2048]{1,0:T(8,128)(2,1)S(1)}, bf16[64,2048]{1,0:T(8,128)(2,1)S(1)}, u32[]{:S(2)}, u32[]{:S(2)}) %collective-permute-start.22) | collective-permute-done | bytes 262176 | tf_op jit(solution)/shard_map/ppermute | solution.py:56
  61.4 2.8 %collective-permute-start.18 = (bf16[64,2048]{1,0:T(8,128)(2,1)S(1)}, bf16[64,2048]{1,0:T(8,128)(2,1)S(1)}, u32[]{:S(2)}, u32[]{:S(2)}) collective-permute-start(bf16[64,2048]{1,0:T(8,128)(2,1)S(1)} %get-tuple-element.82), channel_id=1, source_target_pairs={{0,192},{1,193},{2,194},{3,195},{4,196},{5,197},{6,198},{7,199},{8... | collective-permute-start | bytes 786440 | tf_op jit(solution)/shard_map/ppermute | solution.py:56
  64.2 2.0 %collective-permute-done.23.refs_4_ = bf16[64,2048]{1,0:T(8,128)(2,1)S(1)} collective-permute-done((bf16[64,2048]{1,0:T(8,128)(2,1)S(1)}, bf16[64,2048]{1,0:T(8,128)(2,1)S(1)}, u32[]{:S(2)}, u32[]{:S(2)}) %collective-permute-start.23) | collective-permute-done | bytes 262176 | tf_op jit(solution)/shard_map/ppermute | solution.py:56
  66.3 2.9 %collective-permute-start.25 = (bf16[16,2048]{1,0:T(8,128)(2,1)S(1)}, bf16[16,2048]{1,0:T(8,128)(2,1)S(1)}, u32[]{:S(2)}, u32[]{:S(2)}) collective-permute-start(bf16[16,2048]{1,0:T(8,128)(2,1)S(1)} %get-tuple-element.92), channel_id=1, source_target_pairs={{0,128},{1,129},{2,130},{3,131},{4,132},{5,133},{6,134},{7,135},{8... | collective-permute-start | bytes 196616 | tf_op jit(solution)/shard_map/ppermute | solution.py:56
  71.0 3.8 %collective-permute-start.19 = (bf16[16,2048]{1,0:T(8,128)(2,1)S(1)}, bf16[16,2048]{1,0:T(8,128)(2,1)S(1)}, u32[]{:S(2)}, u32[]{:S(2)}) collective-permute-start(bf16[16,2048]{1,0:T(8,128)(2,1)S(1)} %get-tuple-element.84), channel_id=1, source_target_pairs={{0,16},{1,17},{2,18},{3,19},{4,20},{5,21},{6,22},{7,23},{8,24},{9,... | collective-permute-start | bytes 196616 | tf_op jit(solution)/shard_map/ppermute | solution.py:56
  77.1 1.9 %collective-permute-done.20.refs_2_ = bf16[16,2048]{1,0:T(8,128)(2,1)S(1)} collective-permute-done((bf16[16,2048]{1,0:T(8,128)(2,1)S(1)}, bf16[16,2048]{1,0:T(8,128)(2,1)S(1)}, u32[]{:S(2)}, u32[]{:S(2)}) %collective-permute-start.20) | collective-permute-done | bytes 65568 | tf_op jit(solution)/shard_map/ppermute | solution.py:56
  80.4 6.7 %collective-permute-start.28 = (bf16[16,1024]{1,0:T(8,128)(2,1)S(1)}, bf16[16,1024]{1,0:T(8,128)(2,1)S(1)}, u32[]{:S(2)}, u32[]{:S(2)}) collective-permute-start(bf16[16,1024]{1,0:T(8,128)(2,1)S(1)} %get-tuple-element.96), channel_id=1, source_target_pairs={{0,8},{1,9},{2,10},{3,11},{4,12},{5,13},{6,14},{7,15},{8,0},{9,1},... | collective-permute-start | bytes 98312 | tf_op jit(solution)/shard_map/ppermute | solution.py:56
  87.1 1.5 %collective-permute-start.29 = (bf16[16,1024]{1,0:T(8,128)(2,1)S(1)}, bf16[16,1024]{1,0:T(8,128)(2,1)S(1)}, u32[]{:S(2)}, u32[]{:S(2)}) collective-permute-start(bf16[16,1024]{1,0:T(8,128)(2,1)S(1)} %get-tuple-element.97), channel_id=1, source_target_pairs={{0,4},{1,5},{2,6},{3,7},{4,0},{5,1},{6,2},{7,3},{8,12},{9,13},{10,... | collective-permute-start | bytes 98312 | tf_op jit(solution)/shard_map/ppermute | solution.py:56
  89.0 2.9 %collective-permute-done.29 = bf16[16,1024]{1,0:T(8,128)(2,1)S(1)} collective-permute-done((bf16[16,1024]{1,0:T(8,128)(2,1)S(1)}, bf16[16,1024]{1,0:T(8,128)(2,1)S(1)}, u32[]{:S(2)}, u32[]{:S(2)}) %collective-permute-start.29) | collective-permute-done | bytes 32800 | tf_op jit(solution)/shard_map/ppermute | solution.py:56
  91.9 2.7 %collective-permute-done.30 = bf16[16,1024]{1,0:T(8,128)(2,1)S(1)} collective-permute-done((bf16[16,1024]{1,0:T(8,128)(2,1)S(1)}, bf16[16,1024]{1,0:T(8,128)(2,1)S(1)}, u32[]{:S(2)}, u32[]{:S(2)}) %collective-permute-start.30) | collective-permute-done | bytes 32800 | tf_op jit(solution)/shard_map/ppermute | solution.py:56
  (50 shorter events, 17.9 us)
Async XLA Ops:
  2.0 11.9 %collective-permute-start = (bf16[32,8320]{1,0:T(8,128)(2,1)S(1)}, bf16[32,8320]{1,0:T(8,128)(2,1)S(1)}, u32[]{:S(2)}, u32[]{:S(2)}) collective-permute-start(bf16[32,8320]{1,0:T(8,128)(2,1)S(1)} %get-tuple-element.56), channel_id=1, source_target_pairs={{0,1},{1,0},{2,3},{3,2},{4,5},{5,4},{6,7},{7,6},{8,9},{9,8},{10,11... | collective-permute-start | bytes 1597448 | tf_op jit(solution)/shard_map/ppermute | solution.py:56
  2.1 14.7 %collective-permute-start.1 = (bf16[32,8320]{1,0:T(8,128)(2,1)S(1)}, bf16[32,8320]{1,0:T(8,128)(2,1)S(1)}, u32[]{:S(2)}, u32[]{:S(2)}) collective-permute-start(bf16[32,8320]{1,0:T(8,128)(2,1)S(1)} %get-tuple-element.59.after), channel_id=1, source_target_pairs={{0,2},{1,3},{2,0},{3,1},{4,6},{5,7},{6,4},{7,5},{8,10},{9,11},{10,... | collective-permute-start | bytes 1597448 | tf_op jit(solution)/shard_map/ppermute | solution.py:56
  5.1 11.1 %collective-permute-start.4 = (bf16[16,8192]{1,0:T(8,128)(2,1)S(1)}, bf16[16,8192]{1,0:T(8,128)(2,1)S(1)}, u32[]{:S(2)}, u32[]{:S(2)}) collective-permute-start(bf16[16,8192]{1,0:T(8,128)(2,1)S(1)} %own_references.1.refs_8_.refs_10_), channel_id=1, source_target_pairs={{0,32},{1,33},{2,34},{3,35},{4,36},{5,37},{6,38},{7,39},{8,40},{9,... | collective-permute-start | bytes 786440 | tf_op jit(solution)/shard_map/ppermute | solution.py:56
  5.7 10.5 %collective-permute-start.3 = (bf16[16,8192]{1,0:T(8,128)(2,1)S(1)}, bf16[16,8192]{1,0:T(8,128)(2,1)S(1)}, u32[]{:S(2)}, u32[]{:S(2)}) collective-permute-start(bf16[16,8192]{1,0:T(8,128)(2,1)S(1)} %own_references.1.refs_8_.refs_10_), channel_id=1, source_target_pairs={{0,192},{1,193},{2,194},{3,195},{4,196},{5,197},{6,198},{7,199},{8... | collective-permute-start | bytes 786440 | tf_op jit(solution)/shard_map/ppermute | solution.py:56
  8.7 7.8 %collective-permute-start.2 = (bf16[16,8192]{1,0:T(8,128)(2,1)S(1)}, bf16[16,8192]{1,0:T(8,128)(2,1)S(1)}, u32[]{:S(2)}, u32[]{:S(2)}) collective-permute-start(bf16[16,8192]{1,0:T(8,128)(2,1)S(1)} %own_references.1.refs_8_.refs_10_), channel_id=1, source_target_pairs={{0,64},{1,65},{2,66},{3,67},{4,68},{5,69},{6,70},{7,71},{8,72},{9,... | collective-permute-start | bytes 786440 | tf_op jit(solution)/shard_map/ppermute | solution.py:56
  16.8 16.4 %collective-permute-start.5 = (bf16[32,8320]{1,0:T(8,128)(2,1)S(1)}, bf16[32,8320]{1,0:T(8,128)(2,1)S(1)}, u32[]{:S(2)}, u32[]{:S(2)}) collective-permute-start(bf16[32,8320]{1,0:T(8,128)(2,1)S(1)} %get-tuple-element.63), channel_id=1, source_target_pairs={{0,3},{1,2},{2,1},{3,0},{4,7},{5,6},{6,5},{7,4},{8,11},{9,10},{10,... | collective-permute-start | bytes 1597448 | tf_op jit(solution)/shard_map/ppermute | solution.py:56
  17.8 10.7 %collective-permute-start.6 = (bf16[16,8192]{1,0:T(8,128)(2,1)S(1)}, bf16[16,8192]{1,0:T(8,128)(2,1)S(1)}, u32[]{:S(2)}, u32[]{:S(2)}) collective-permute-start(bf16[16,8192]{1,0:T(8,128)(2,1)S(1)} %collective-permute-done.4.refs_5_.refs_7_), channel_id=1, source_target_pairs={{0,128},{1,129},{2,130},{3,131},{4,132},{5,133},{6,134},{7,135},{8... | collective-permute-start | bytes 786440 | tf_op jit(solution)/shard_map/ppermute | solution.py:56
  21.0 10.2 %collective-permute-start.7 = (bf16[16,8192]{1,0:T(8,128)(2,1)S(1)}, bf16[16,8192]{1,0:T(8,128)(2,1)S(1)}, u32[]{:S(2)}, u32[]{:S(2)}) collective-permute-start(bf16[16,8192]{1,0:T(8,128)(2,1)S(1)} %relay.1), channel_id=1, source_target_pairs={{0,192},{1,65},{2,194},{3,67},{4,196},{5,69},{6,198},{7,71},{8,200... | collective-permute-start | bytes 786440 | tf_op jit(solution)/shard_map/ppermute | solution.py:56
  22.2 9.1 %collective-permute-start.8 = (bf16[16,8192]{1,0:T(8,128)(2,1)S(1)}, bf16[16,8192]{1,0:T(8,128)(2,1)S(1)}, u32[]{:S(2)}, u32[]{:S(2)}) collective-permute-start(bf16[16,8192]{1,0:T(8,128)(2,1)S(1)} %collective-permute-done.2.one.refs_6_.refs_8_), channel_id=1, source_target_pairs={{0,32},{1,33},{2,34},{3,35},{4,36},{5,37},{6,38},{7,39},{8,40},{9,... | collective-permute-start | bytes 786440 | tf_op jit(solution)/shard_map/ppermute | solution.py:56
  22.7 8.5 %collective-permute-start.9 = (bf16[16,8192]{1,0:T(8,128)(2,1)S(1)}, bf16[16,8192]{1,0:T(8,128)(2,1)S(1)}, u32[]{:S(2)}, u32[]{:S(2)}) collective-permute-start(bf16[16,8192]{1,0:T(8,128)(2,1)S(1)} %collective-permute-done.3.other.refs_7_.refs_9_), channel_id=1, source_target_pairs={{0,48},{1,49},{2,50},{3,51},{4,52},{5,53},{6,54},{7,55},{8,56},{9,... | collective-permute-start | bytes 786440 | tf_op jit(solution)/shard_map/ppermute | solution.py:56
  32.9 8.9 %collective-permute-start.10 = (f32[256,128]{1,0:T(8,128)S(1)}, f32[256,128]{1,0:T(8,128)S(1)}, u32[]{:S(2)}, u32[]{:S(2)}) collective-permute-start(f32[256,128]{1,0:T(8,128)S(1)} %get-tuple-element.68), channel_id=1, source_target_pairs={{0,2},{1,3},{2,0},{3,1},{4,6},{5,7},{6,4},{7,5},{8,10},{9,11},{10,... | collective-permute-start | bytes 393224 | tf_op jit(solution)/shard_map/ppermute | solution.py:56
  37.1 5.6 %collective-permute-start.11 = (f32[256,128]{1,0:T(8,128)S(1)}, f32[256,128]{1,0:T(8,128)S(1)}, u32[]{:S(2)}, u32[]{:S(2)}) collective-permute-start(f32[256,128]{1,0:T(8,128)S(1)} %partial_scores.4), channel_id=1, source_target_pairs={{0,3},{1,2},{2,1},{3,0},{4,7},{5,6},{6,5},{7,4},{8,11},{9,10},{10,... | collective-permute-start | bytes 393224 | tf_op jit(solution)/shard_map/ppermute | solution.py:56
  41.2 1.6 %collective-permute-start.12 = (f32[256,128]{1,0:T(8,128)S(1)}, f32[256,128]{1,0:T(8,128)S(1)}, u32[]{:S(2)}, u32[]{:S(2)}) collective-permute-start(f32[256,128]{1,0:T(8,128)S(1)} %get-tuple-element.78), channel_id=1, source_target_pairs={{0,1},{1,0},{2,3},{3,2},{4,5},{5,4},{6,7},{7,6},{8,9},{9,8},{10,11... | collective-permute-start | bytes 393224 | tf_op jit(solution)/shard_map/ppermute | solution.py:56
  43.1 4.1 %collective-permute-start.15 = (bf16[128,256]{1,0:T(8,128)(2,1)S(1)}, bf16[128,256]{1,0:T(8,128)(2,1)S(1)}, u32[]{:S(2)}, u32[]{:S(2)}) collective-permute-start(bf16[128,256]{1,0:T(8,128)(2,1)S(1)} %posterior.1.refs_6_), channel_id=1, source_target_pairs={{0,3},{1,2},{2,1},{3,0},{4,7},{5,6},{6,5},{7,4},{8,11},{9,10},{10,... | collective-permute-start | bytes 196616 | tf_op jit(solution)/shard_map/ppermute | solution.py:56
  44.8 4.4 %collective-permute-start.14 = (bf16[128,256]{1,0:T(8,128)(2,1)S(1)}, bf16[128,256]{1,0:T(8,128)(2,1)S(1)}, u32[]{:S(2)}, u32[]{:S(2)}) collective-permute-start(bf16[128,256]{1,0:T(8,128)(2,1)S(1)} %posterior.1.refs_6_), channel_id=1, source_target_pairs={{0,2},{1,3},{2,0},{3,1},{4,6},{5,7},{6,4},{7,5},{8,10},{9,11},{10,... | collective-permute-start | bytes 196616 | tf_op jit(solution)/shard_map/ppermute | solution.py:56
  45.2 4.0 %collective-permute-start.13 = (bf16[128,256]{1,0:T(8,128)(2,1)S(1)}, bf16[128,256]{1,0:T(8,128)(2,1)S(1)}, u32[]{:S(2)}, u32[]{:S(2)}) collective-permute-start(bf16[128,256]{1,0:T(8,128)(2,1)S(1)} %posterior.1.refs_6_), channel_id=1, source_target_pairs={{0,1},{1,0},{2,3},{3,2},{4,5},{5,4},{6,7},{7,6},{8,9},{9,8},{10,11... | collective-permute-start | bytes 196616 | tf_op jit(solution)/shard_map/ppermute | solution.py:56
  50.5 10.9 %collective-permute-start.22 = (bf16[64,2048]{1,0:T(8,128)(2,1)S(1)}, bf16[64,2048]{1,0:T(8,128)(2,1)S(1)}, u32[]{:S(2)}, u32[]{:S(2)}) collective-permute-start(bf16[64,2048]{1,0:T(8,128)(2,1)S(1)} %get-tuple-element.88), channel_id=1, source_target_pairs={{0,16},{1,17},{2,18},{3,19},{4,20},{5,21},{6,22},{7,23},{8,24},{9,... | collective-permute-start | bytes 786440 | tf_op jit(solution)/shard_map/ppermute | solution.py:56
  53.3 12.8 %collective-permute-start.23 = (bf16[64,2048]{1,0:T(8,128)(2,1)S(1)}, bf16[64,2048]{1,0:T(8,128)(2,1)S(1)}, u32[]{:S(2)}, u32[]{:S(2)}) collective-permute-start(bf16[64,2048]{1,0:T(8,128)(2,1)S(1)} %get-tuple-element.89), channel_id=1, source_target_pairs={{0,32},{1,33},{2,34},{3,35},{4,36},{5,37},{6,38},{7,39},{8,40},{9,... | collective-permute-start | bytes 786440 | tf_op jit(solution)/shard_map/ppermute | solution.py:56
  54.5 11.7 %collective-permute-start.24 = (bf16[64,2048]{1,0:T(8,128)(2,1)S(1)}, bf16[64,2048]{1,0:T(8,128)(2,1)S(1)}, u32[]{:S(2)}, u32[]{:S(2)}) collective-permute-start(bf16[64,2048]{1,0:T(8,128)(2,1)S(1)} %get-tuple-element.90), channel_id=1, source_target_pairs={{0,48},{1,49},{2,50},{3,51},{4,52},{5,53},{6,54},{7,55},{8,56},{9,... | collective-permute-start | bytes 786440 | tf_op jit(solution)/shard_map/ppermute | solution.py:56
  56.0 13.6 %collective-permute-start.16 = (bf16[64,2048]{1,0:T(8,128)(2,1)S(1)}, bf16[64,2048]{1,0:T(8,128)(2,1)S(1)}, u32[]{:S(2)}, u32[]{:S(2)}) collective-permute-start(bf16[64,2048]{1,0:T(8,128)(2,1)S(1)} %get-tuple-element.80), channel_id=1, source_target_pairs={{0,128},{1,129},{2,130},{3,131},{4,132},{5,133},{6,134},{7,135},{8... | collective-permute-start | bytes 786440 | tf_op jit(solution)/shard_map/ppermute | solution.py:56
  59.0 11.7 %collective-permute-start.17 = (bf16[64,2048]{1,0:T(8,128)(2,1)S(1)}, bf16[64,2048]{1,0:T(8,128)(2,1)S(1)}, u32[]{:S(2)}, u32[]{:S(2)}) collective-permute-start(bf16[64,2048]{1,0:T(8,128)(2,1)S(1)} %get-tuple-element.81), channel_id=1, source_target_pairs={{0,64},{1,65},{2,66},{3,67},{4,68},{5,69},{6,70},{7,71},{8,72},{9,... | collective-permute-start | bytes 786440 | tf_op jit(solution)/shard_map/ppermute | solution.py:56
  61.4 9.5 %collective-permute-start.18 = (bf16[64,2048]{1,0:T(8,128)(2,1)S(1)}, bf16[64,2048]{1,0:T(8,128)(2,1)S(1)}, u32[]{:S(2)}, u32[]{:S(2)}) collective-permute-start(bf16[64,2048]{1,0:T(8,128)(2,1)S(1)} %get-tuple-element.82), channel_id=1, source_target_pairs={{0,192},{1,193},{2,194},{3,195},{4,196},{5,197},{6,198},{7,199},{8... | collective-permute-start | bytes 786440 | tf_op jit(solution)/shard_map/ppermute | solution.py:56
  66.3 9.7 %collective-permute-start.25 = (bf16[16,2048]{1,0:T(8,128)(2,1)S(1)}, bf16[16,2048]{1,0:T(8,128)(2,1)S(1)}, u32[]{:S(2)}, u32[]{:S(2)}) collective-permute-start(bf16[16,2048]{1,0:T(8,128)(2,1)S(1)} %get-tuple-element.92), channel_id=1, source_target_pairs={{0,128},{1,129},{2,130},{3,131},{4,132},{5,133},{6,134},{7,135},{8... | collective-permute-start | bytes 196616 | tf_op jit(solution)/shard_map/ppermute | solution.py:56
  69.2 6.8 %collective-permute-start.26 = (bf16[16,2048]{1,0:T(8,128)(2,1)S(1)}, bf16[16,2048]{1,0:T(8,128)(2,1)S(1)}, u32[]{:S(2)}, u32[]{:S(2)}) collective-permute-start(bf16[16,2048]{1,0:T(8,128)(2,1)S(1)} %get-tuple-element.93), channel_id=1, source_target_pairs={{0,64},{1,65},{2,66},{3,67},{4,68},{5,69},{6,70},{7,71},{8,72},{9,... | collective-permute-start | bytes 196616 | tf_op jit(solution)/shard_map/ppermute | solution.py:56
  69.6 6.5 %collective-permute-start.27 = (bf16[16,2048]{1,0:T(8,128)(2,1)S(1)}, bf16[16,2048]{1,0:T(8,128)(2,1)S(1)}, u32[]{:S(2)}, u32[]{:S(2)}) collective-permute-start(bf16[16,2048]{1,0:T(8,128)(2,1)S(1)} %get-tuple-element.94), channel_id=1, source_target_pairs={{0,192},{1,193},{2,194},{3,195},{4,196},{5,197},{6,198},{7,199},{8... | collective-permute-start | bytes 196616 | tf_op jit(solution)/shard_map/ppermute | solution.py:56
  71.0 6.1 %collective-permute-start.19 = (bf16[16,2048]{1,0:T(8,128)(2,1)S(1)}, bf16[16,2048]{1,0:T(8,128)(2,1)S(1)}, u32[]{:S(2)}, u32[]{:S(2)}) collective-permute-start(bf16[16,2048]{1,0:T(8,128)(2,1)S(1)} %get-tuple-element.84), channel_id=1, source_target_pairs={{0,16},{1,17},{2,18},{3,19},{4,20},{5,21},{6,22},{7,23},{8,24},{9,... | collective-permute-start | bytes 196616 | tf_op jit(solution)/shard_map/ppermute | solution.py:56
  74.8 4.3 %collective-permute-start.20 = (bf16[16,2048]{1,0:T(8,128)(2,1)S(1)}, bf16[16,2048]{1,0:T(8,128)(2,1)S(1)}, u32[]{:S(2)}, u32[]{:S(2)}) collective-permute-start(bf16[16,2048]{1,0:T(8,128)(2,1)S(1)} %get-tuple-element.85), channel_id=1, source_target_pairs={{0,32},{1,33},{2,34},{3,35},{4,36},{5,37},{6,38},{7,39},{8,40},{9,... | collective-permute-start | bytes 196616 | tf_op jit(solution)/shard_map/ppermute | solution.py:56
  76.0 4.3 %collective-permute-start.21 = (bf16[16,2048]{1,0:T(8,128)(2,1)S(1)}, bf16[16,2048]{1,0:T(8,128)(2,1)S(1)}, u32[]{:S(2)}, u32[]{:S(2)}) collective-permute-start(bf16[16,2048]{1,0:T(8,128)(2,1)S(1)} %get-tuple-element.86), channel_id=1, source_target_pairs={{0,48},{1,49},{2,50},{3,51},{4,52},{5,53},{6,54},{7,55},{8,56},{9,... | collective-permute-start | bytes 196616 | tf_op jit(solution)/shard_map/ppermute | solution.py:56
  80.4 8.6 %collective-permute-start.28 = (bf16[16,1024]{1,0:T(8,128)(2,1)S(1)}, bf16[16,1024]{1,0:T(8,128)(2,1)S(1)}, u32[]{:S(2)}, u32[]{:S(2)}) collective-permute-start(bf16[16,1024]{1,0:T(8,128)(2,1)S(1)} %get-tuple-element.96), channel_id=1, source_target_pairs={{0,8},{1,9},{2,10},{3,11},{4,12},{5,13},{6,14},{7,15},{8,0},{9,1},... | collective-permute-start | bytes 98312 | tf_op jit(solution)/shard_map/ppermute | solution.py:56
  87.1 4.8 %collective-permute-start.29 = (bf16[16,1024]{1,0:T(8,128)(2,1)S(1)}, bf16[16,1024]{1,0:T(8,128)(2,1)S(1)}, u32[]{:S(2)}, u32[]{:S(2)}) collective-permute-start(bf16[16,1024]{1,0:T(8,128)(2,1)S(1)} %get-tuple-element.97), channel_id=1, source_target_pairs={{0,4},{1,5},{2,6},{3,7},{4,0},{5,1},{6,2},{7,3},{8,12},{9,13},{10,... | collective-permute-start | bytes 98312 | tf_op jit(solution)/shard_map/ppermute | solution.py:56
  88.5 6.0 %collective-permute-start.30 = (bf16[16,1024]{1,0:T(8,128)(2,1)S(1)}, bf16[16,1024]{1,0:T(8,128)(2,1)S(1)}, u32[]{:S(2)}, u32[]{:S(2)}) collective-permute-start(bf16[16,1024]{1,0:T(8,128)(2,1)S(1)} %get-tuple-element.98), channel_id=1, source_target_pairs={{0,12},{1,13},{2,14},{3,15},{4,8},{5,9},{6,10},{7,11},{8,4},{9,5},... | collective-permute-start | bytes 98312 | tf_op jit(solution)/shard_map/ppermute | solution.py:56

commit v18 on v16

--- a/solution.py
+++ b/solution.py
@@ -436,11 +436,16 @@
     )
 
 
-def joined_kernel(block_ref, *refs):
-    for n, out in enumerate(refs[8:]):
+def joined_kernel(picks, block_ref, *refs):
+    for n, out in zip(picks, refs[8:]):
         spot = pl.ds(pl.multiple_of((block_ref[0] ^ n) * HALF, HALF), HALF)
         out[:, :HALF] = added([ref[:, spot] for ref in refs[:4]]).astype(out.dtype)
         out[:, HALF:] = added([ref[:, spot] for ref in refs[4:8]]).astype(out.dtype)
+
+
+def make_joined(picks, block, values):
+    outs = [((16, COLS), BF16 if n else F32) for n in picks]
+    return local(lambda *refs: joined_kernel(picks, *refs), "joined_sums", outs, [block], values, 4)
 
 
 def after(value, *others):
@@ -498,9 +503,13 @@
     first = [first[0]] + [send(first[n], crossed(n, 1)) for n in (2, 1, 3)]
     second = make_turn(1, member, x_at, second)
     second = [second[0]] + [send(second[n], crossed(n, 0)) for n in (2, 1, 3)]
-    outs = [((16, COLS), F32)] + [((16, COLS), BF16)] * (NB - 1)
-    ends = local(joined_kernel, "joined_sums", outs, [block], [*first, *second], 4)
-    return added([ends[0]] + [send(ends[n], flips(z=n * (G // 2))) for n in (2, 1, 3)])
+    values = [*first, *second]
+    (far,) = make_joined([2], block, values)
+    values[0] = after(values[0], far)
+    far = send(far, flips(z=2 * (G // 2)))
+    mine, one, three = make_joined([0, 1, 3], block, values)
+    near = [send(one, flips(z=G // 2)), send(three, flips(z=3 * (G // 2)))]
+    return added([mine, far, *near])
 
 
 def solution(mesh):

time: 94.2 us -> 95.3 us (1.012)
    pallas_call x19 -> x20, Pallas kernels: 24.3 us -> 24.3 us  [local(): pl.pallas_call(kernel, in_specs=[SCALARS] * len(scalars) + [PLACED] * pla...]
  transfers between devices with their start and end apart: 31 -> 31, of which waited for: 17 -> 16; matrix products, arithmetic and copies ran while one was open for 0% -> 0% of each run, Pallas kernels for 22% -> 22%
where the time goes in v18:
time: 95.3 us; the launch traced here: 94.3 us
  starting transfers between devices  45.1 us (47%)
  Pallas kernels  24.3 us (25%)
  waiting for transfers between devices  24.1 us (25%)
    ppermute x31, starting transfers between devices, send(): return lax.ppermute(value, AXES, pairs)  45.1 us
    pallas_call x20, Pallas kernels, local(): pl.pallas_call(kernel, in_specs=[SCALARS] * len(scalars) + [PLACED] * pla...  24.3 us
    ppermute x31, waiting for transfers between devices, send(): return lax.ppermute(value, AXES, pairs)  24.1 us
  transfers between devices with their start and end apart: 31, of which 16 were waited for; matrix products, arithmetic and copies ran while one was open for 0% of the time, Pallas kernels for 22%

profile of v18, /device:TPU:2, one launch (start us, length us, event | category | flops | bytes accessed | tf_op | source)
XLA Modules:
  0.0 94.3 jit_solution(6083727809107926573)
XLA Ops:
  0.0 2.0 %split_particles.1 = (bf16[32,8320]{1,0:T(8,128)(2,1)S(1)}, bf16[32,8320]{1,0:T(8,128)(2,1)S(1)}, bf16[32,8320]{1,0:T(8,128)(2,1)S(1)}, bf16[32,8320]{1,0:T(8,128)(2,1)S(1)}) custom-call(s32[1]{0:T(128)} %bitcast.1.member_ref.refs_0_, s32[1]{0:T(128)} %bitcast.block_ref.refs_0_, s32[1]{0:T(128)} %bitcast.2.x_ref.refs_1_, bf16[32,32768]{1,0:T(8,128)(2,1)} %source.2, ...), custom_call_target="tpu_custom_call" | custom-call | tf_op jit(solution)/shard_map/split_particles/pallas_call | solution.py:111
  2.1 2.0 %collective-permute-start.1 = (bf16[32,8320]{1,0:T(8,128)(2,1)S(1)}, bf16[32,8320]{1,0:T(8,128)(2,1)S(1)}, u32[]{:S(2)}, u32[]{:S(2)}) collective-permute-start(bf16[32,8320]{1,0:T(8,128)(2,1)S(1)} %get-tuple-element.59.after), channel_id=1, source_target_pairs={{0,2},{1,3},{2,0},{3,1},{4,6},{5,7},{6,4},{7,5},{8,10},{9,11},{10,... | collective-permute-start | bytes 1597448 | tf_op jit(solution)/shard_map/ppermute | solution.py:63
  5.7 3.0 %collective-permute-start.3 = (bf16[16,8192]{1,0:T(8,128)(2,1)S(1)}, bf16[16,8192]{1,0:T(8,128)(2,1)S(1)}, u32[]{:S(2)}, u32[]{:S(2)}) collective-permute-start(bf16[16,8192]{1,0:T(8,128)(2,1)S(1)} %own_references.1.refs_8_.refs_10_), channel_id=1, source_target_pairs={{0,192},{1,193},{2,194},{3,195},{4,196},{5,197},{6,198},{7,199},{8... | collective-permute-start | bytes 786440 | tf_op jit(solution)/shard_map/ppermute | solution.py:63
  8.9 2.7 %phase_table.1 = (bf16[256,8192]{1,0:T(8,128)(2,1)S(1)}, f32[4,8,1024]{2,1,0:T(8,128)S(1)}) custom-call(s32[1]{0:T(128)} %bitcast.1.member_ref.refs_0_, f32[16,8,1024]{2,1,0:T(8,128)} %constant.63.clone.geo_ref), custom_call_target="tpu_custom_call" | custom-call | tf_op jit(solution)/shard_map/phase_table/pallas_call | solution.py:111
  11.6 2.3 %shifted_rows.4 = (bf16[256,8192]{1,0:T(8,128)(2,1)S(1)}, bf16[32,4096]{1,0:T(8,128)(2,1)S(1)}) custom-call(s32[1]{0:T(128)} %bitcast.1.member_ref.refs_0_, bf16[32,8320]{1,0:T(8,128)(2,1)S(1)} %get-tuple-element.52.x_ref, f32[4,8,1024]{2,1,0:T(8,128)S(1)} %get-tuple-element.53.geo_ref, bf16[256,8192]{1,0:T(8,128)(2,1)S(1)} %get-tuple-element.54.table_ref), custom_call_target="tpu_custom_call" | custom-call | tf_op jit(solution)/shard_map/shifted_rows/pallas_call | solution.py:111
  13.9 2.3 %shifted_rows.5 = (bf16[256,8192]{1,0:T(8,128)(2,1)S(1)}, bf16[32,4096]{1,0:T(8,128)(2,1)S(1)}) custom-call(s32[1]{0:T(128)} %bitcast.1.member_ref.refs_0_, bf16[32,8320]{1,0:T(8,128)(2,1)S(1)} %collective-permute-done.x_ref, f32[4,8,1024]{2,1,0:T(8,128)S(1)} %get-tuple-element.53.geo_ref, bf16[256,8192]{1,0:T(8,128)(2,1)S(1)} %get-tuple-element.54.table_ref), custom_call_target="tpu_custom_call" | custom-call | tf_op jit(solution)/shard_map/shifted_rows/pallas_call | solution.py:111
  17.8 3.2 %collective-permute-start.6 = (bf16[16,8192]{1,0:T(8,128)(2,1)S(1)}, bf16[16,8192]{1,0:T(8,128)(2,1)S(1)}, u32[]{:S(2)}, u32[]{:S(2)}) collective-permute-start(bf16[16,8192]{1,0:T(8,128)(2,1)S(1)} %collective-permute-done.4.refs_5_.refs_7_), channel_id=1, source_target_pairs={{0,128},{1,129},{2,130},{3,131},{4,132},{5,133},{6,134},{7,135},{8... | collective-permute-start | bytes 786440 | tf_op jit(solution)/shard_map/ppermute | solution.py:63
  22.7 2.2 %collective-permute-start.9 = (bf16[16,8192]{1,0:T(8,128)(2,1)S(1)}, bf16[16,8192]{1,0:T(8,128)(2,1)S(1)}, u32[]{:S(2)}, u32[]{:S(2)}) collective-permute-start(bf16[16,8192]{1,0:T(8,128)(2,1)S(1)} %collective-permute-done.3.other.refs_7_.refs_9_), channel_id=1, source_target_pairs={{0,48},{1,49},{2,50},{3,51},{4,52},{5,53},{6,54},{7,55},{8,56},{9,... | collective-permute-start | bytes 786440 | tf_op jit(solution)/shard_map/ppermute | solution.py:63
  24.9 2.3 %shifted_rows.6 = (bf16[256,8192]{1,0:T(8,128)(2,1)S(1)}, bf16[32,4096]{1,0:T(8,128)(2,1)S(1)}) custom-call(s32[1]{0:T(128)} %bitcast.1.member_ref.refs_0_, bf16[32,8320]{1,0:T(8,128)(2,1)S(1)} %collective-permute-done.1.x_ref, f32[4,8,1024]{2,1,0:T(8,128)S(1)} %get-tuple-element.53.geo_ref, bf16[256,8192]{1,0:T(8,128)(2,1)S(1)} %get-tuple-element.54.table_ref), custom_call_target="tpu_custom_call" | custom-call | tf_op jit(solution)/shard_map/shifted_rows/pallas_call | solution.py:111
  28.5 2.7 %collective-permute-done.7.other = bf16[16,8192]{1,0:T(8,128)(2,1)S(1)} collective-permute-done((bf16[16,8192]{1,0:T(8,128)(2,1)S(1)}, bf16[16,8192]{1,0:T(8,128)(2,1)S(1)}, u32[]{:S(2)}, u32[]{:S(2)}) %collective-permute-start.7) | collective-permute-done | bytes 262176 | tf_op jit(solution)/shard_map/ppermute | solution.py:63
  31.3 1.6 %partial_scores.3 = (f32[256,128]{1,0:T(8,128)S(1)}, bf16[128,4096]{1,0:T(8,128)(2,1)S(1)}) custom-call(bf16[256,8192]{1,0:T(8,128)(2,1)S(1)} %get-tuple-element.61.refs_0_.refs_4_, bf16[32,4096]{1,0:T(8,128)(2,1)S(1)} %get-tuple-element.64.refs_1_, bf16[32,8192]{1,0:T(8,128)(2,1)S(1)} %pair.1.refs_2_.refs_4_, ...), custom_call_target="tpu_custom_call" | custom-call | tf_op jit(solution)/shard_map/partial_scores/pallas_call | solution.py:111
  33.3 2.3 %shifted_rows.7 = (bf16[256,8192]{1,0:T(8,128)(2,1)S(1)}, bf16[32,4096]{1,0:T(8,128)(2,1)S(1)}) custom-call(s32[1]{0:T(128)} %bitcast.1.member_ref.refs_0_, bf16[32,8320]{1,0:T(8,128)(2,1)S(1)} %collective-permute-done.5.x_ref, f32[4,8,1024]{2,1,0:T(8,128)S(1)} %get-tuple-element.53.geo_ref, bf16[256,8192]{1,0:T(8,128)(2,1)S(1)} %get-tuple-element.54.table_ref), custom_call_target="tpu_custom_call" | custom-call | tf_op jit(solution)/shard_map/shifted_rows/pallas_call | solution.py:111
  35.6 1.5 %partial_scores.4 = f32[256,128]{1,0:T(8,128)S(1)} custom-call(bf16[256,8192]{1,0:T(8,128)(2,1)S(1)} %get-tuple-element.70.refs_0_.refs_5_, bf16[32,4096]{1,0:T(8,128)(2,1)S(1)} %get-tuple-element.73.refs_1_, bf16[32,8192]{1,0:T(8,128)(2,1)S(1)} %pair.1.refs_2_.refs_4_, bf16[16,8192]{1,0:T(8,128)(2,1)S(1)} %collective-permute-done.8.refs_3_.refs_5_, ...), custom_call_target="tpu_custom_call" | custom-call | tf_op jit(solution)/shard_map/partial_scores/pallas_call | solution.py:111
  37.1 1.4 %collective-permute-start.11 = (f32[256,128]{1,0:T(8,128)S(1)}, f32[256,128]{1,0:T(8,128)S(1)}, u32[]{:S(2)}, u32[]{:S(2)}) collective-permute-start(f32[256,128]{1,0:T(8,128)S(1)} %partial_scores.4), channel_id=1, source_target_pairs={{0,3},{1,2},{2,1},{3,0},{4,7},{5,6},{6,5},{7,4},{8,11},{9,10},{10,... | collective-permute-start | bytes 393224 | tf_op jit(solution)/shard_map/ppermute | solution.py:63
  38.5 2.7 %partial_scores.5 = (f32[256,128]{1,0:T(8,128)S(1)}, f32[256,128]{1,0:T(8,128)S(1)}) custom-call(bf16[256,8192]{1,0:T(8,128)(2,1)S(1)} %get-tuple-element.55.refs_0_.refs_2_, bf16[256,8192]{1,0:T(8,128)(2,1)S(1)} %get-tuple-element.58.refs_1_.refs_3_, bf16[32,4096]{1,0:T(8,128)(2,1)S(1)} %get-tuple-element.75.refs_2_, ...), custom_call_target="tpu_custom_call" | custom-call | tf_op jit(solution)/shard_map/partial_scores/pallas_call | solution.py:111
  43.1 1.7 %collective-permute-start.15 = (bf16[128,256]{1,0:T(8,128)(2,1)S(1)}, bf16[128,256]{1,0:T(8,128)(2,1)S(1)}, u32[]{:S(2)}, u32[]{:S(2)}) collective-permute-start(bf16[128,256]{1,0:T(8,128)(2,1)S(1)} %posterior.1.refs_6_), channel_id=1, source_target_pairs={{0,3},{1,2},{2,1},{3,0},{4,7},{5,6},{6,5},{7,4},{8,11},{9,10},{10,... | collective-permute-start | bytes 196616 | tf_op jit(solution)/shard_map/ppermute | solution.py:63
  45.2 2.1 %collective-permute-done.15.refs_9_ = bf16[128,256]{1,0:T(8,128)(2,1)S(1)} collective-permute-done((bf16[128,256]{1,0:T(8,128)(2,1)S(1)}, bf16[128,256]{1,0:T(8,128)(2,1)S(1)}, u32[]{:S(2)}, u32[]{:S(2)}) %collective-permute-start.15) | collective-permute-done | bytes 65568 | tf_op jit(solution)/shard_map/ppermute | solution.py:63
  47.2 1.9 %collective-permute-done.14.refs_8_ = bf16[128,256]{1,0:T(8,128)(2,1)S(1)} collective-permute-done((bf16[128,256]{1,0:T(8,128)(2,1)S(1)}, bf16[128,256]{1,0:T(8,128)(2,1)S(1)}, u32[]{:S(2)}, u32[]{:S(2)}) %collective-permute-start.14) | collective-permute-done | bytes 65568 | tf_op jit(solution)/shard_map/ppermute | solution.py:63
  49.2 1.4 %weighted_sums.3 = (bf16[64,2048]{1,0:T(8,128)(2,1)S(1)}, bf16[64,2048]{1,0:T(8,128)(2,1)S(1)}, bf16[64,2048]{1,0:T(8,128)(2,1)S(1)}, bf16[64,2048]{1,0:T(8,128)(2,1)S(1)}) custom-call(s32[1]{0:T(128)} %bitcast.1.member_ref.refs_0_, s32[1]{0:T(128)} %bitcast.2.x_ref.refs_1_, bf16[256,8192]{1,0:T(8,128)(2,1)S(1)} %get-tuple-element.55.refs_0_.refs_2_, ...), custom_call_target="tpu_custom_call" | custom-call | tf_op jit(solution)/shard_map/weighted_sums/pallas_call | solution.py:111
  50.6 2.8 %collective-permute-start.22 = (bf16[64,2048]{1,0:T(8,128)(2,1)S(1)}, bf16[64,2048]{1,0:T(8,128)(2,1)S(1)}, u32[]{:S(2)}, u32[]{:S(2)}) collective-permute-start(bf16[64,2048]{1,0:T(8,128)(2,1)S(1)} %get-tuple-element.88), channel_id=1, source_target_pairs={{0,16},{1,129},{2,18},{3,131},{4,20},{5,133},{6,22},{7,135},{8,24}... | collective-permute-start | bytes 786440 | tf_op jit(solution)/shard_map/ppermute | solution.py:63
  54.8 1.4 %weighted_sums.2 = (bf16[64,2048]{1,0:T(8,128)(2,1)S(1)}, bf16[64,2048]{1,0:T(8,128)(2,1)S(1)}, bf16[64,2048]{1,0:T(8,128)(2,1)S(1)}, bf16[64,2048]{1,0:T(8,128)(2,1)S(1)}) custom-call(s32[1]{0:T(128)} %bitcast.1.member_ref.refs_0_, s32[1]{0:T(128)} %bitcast.2.x_ref.refs_1_, bf16[256,8192]{1,0:T(8,128)(2,1)S(1)} %get-tuple-element.55.refs_0_.refs_2_, ...), custom_call_target="tpu_custom_call" | custom-call | tf_op jit(solution)/shard_map/weighted_sums/pallas_call | solution.py:111
  56.3 3.0 %collective-permute-start.16 = (bf16[64,2048]{1,0:T(8,128)(2,1)S(1)}, bf16[64,2048]{1,0:T(8,128)(2,1)S(1)}, u32[]{:S(2)}, u32[]{:S(2)}) collective-permute-start(bf16[64,2048]{1,0:T(8,128)(2,1)S(1)} %get-tuple-element.80), channel_id=1, source_target_pairs={{0,128},{1,17},{2,130},{3,19},{4,132},{5,21},{6,134},{7,23},{8,136... | collective-permute-start | bytes 786440 | tf_op jit(solution)/shard_map/ppermute | solution.py:63
  60.0 1.5 %collective-permute-start.18 = (bf16[64,2048]{1,0:T(8,128)(2,1)S(1)}, bf16[64,2048]{1,0:T(8,128)(2,1)S(1)}, u32[]{:S(2)}, u32[]{:S(2)}) collective-permute-start(bf16[64,2048]{1,0:T(8,128)(2,1)S(1)} %get-tuple-element.82), channel_id=1, source_target_pairs={{0,192},{1,49},{2,194},{3,51},{4,196},{5,53},{6,198},{7,55},{8,200... | collective-permute-start | bytes 786440 | tf_op jit(solution)/shard_map/ppermute | solution.py:63
  61.5 1.8 %collective-permute-done.23.refs_4_ = bf16[64,2048]{1,0:T(8,128)(2,1)S(1)} collective-permute-done((bf16[64,2048]{1,0:T(8,128)(2,1)S(1)}, bf16[64,2048]{1,0:T(8,128)(2,1)S(1)}, u32[]{:S(2)}, u32[]{:S(2)}) %collective-permute-start.23) | collective-permute-done | bytes 262176 | tf_op jit(solution)/shard_map/ppermute | solution.py:63
  63.3 1.5 %collective-permute-done.24.refs_5_ = bf16[64,2048]{1,0:T(8,128)(2,1)S(1)} collective-permute-done((bf16[64,2048]{1,0:T(8,128)(2,1)S(1)}, bf16[64,2048]{1,0:T(8,128)(2,1)S(1)}, u32[]{:S(2)}, u32[]{:S(2)}) %collective-permute-start.24) | collective-permute-done | bytes 262176 | tf_op jit(solution)/shard_map/ppermute | solution.py:63
  65.0 3.4 %collective-permute-start.25 = (bf16[16,2048]{1,0:T(8,128)(2,1)S(1)}, bf16[16,2048]{1,0:T(8,128)(2,1)S(1)}, u32[]{:S(2)}, u32[]{:S(2)}) collective-permute-start(bf16[16,2048]{1,0:T(8,128)(2,1)S(1)} %get-tuple-element.92), channel_id=1, source_target_pairs={{0,128},{1,17},{2,130},{3,19},{4,132},{5,21},{6,134},{7,23},{8,136... | collective-permute-start | bytes 196616 | tf_op jit(solution)/shard_map/ppermute | solution.py:63
  70.0 2.3 %collective-permute-start.19 = (bf16[16,2048]{1,0:T(8,128)(2,1)S(1)}, bf16[16,2048]{1,0:T(8,128)(2,1)S(1)}, u32[]{:S(2)}, u32[]{:S(2)}) collective-permute-start(bf16[16,2048]{1,0:T(8,128)(2,1)S(1)} %get-tuple-element.84), channel_id=1, source_target_pairs={{0,16},{1,129},{2,18},{3,131},{4,20},{5,133},{6,22},{7,135},{8,24}... | collective-permute-start | bytes 196616 | tf_op jit(solution)/shard_map/ppermute | solution.py:63
  72.3 1.9 %collective-permute-start.20 = (bf16[16,2048]{1,0:T(8,128)(2,1)S(1)}, bf16[16,2048]{1,0:T(8,128)(2,1)S(1)}, u32[]{:S(2)}, u32[]{:S(2)}) collective-permute-start(bf16[16,2048]{1,0:T(8,128)(2,1)S(1)} %get-tuple-element.85), channel_id=1, source_target_pairs={{0,32},{1,65},{2,34},{3,67},{4,36},{5,69},{6,38},{7,71},{8,40},{9,... | collective-permute-start | bytes 196616 | tf_op jit(solution)/shard_map/ppermute | solution.py:63
  78.6 3.4 %collective-permute-start.29 = (bf16[16,1024]{1,0:T(8,128)(2,1)S(1)}, bf16[16,1024]{1,0:T(8,128)(2,1)S(1)}, u32[]{:S(2)}, u32[]{:S(2)}) collective-permute-start(bf16[16,1024]{1,0:T(8,128)(2,1)S(1)} %get-tuple-element.97), channel_id=1, source_target_pairs={{0,4},{1,5},{2,6},{3,7},{4,0},{5,1},{6,2},{7,3},{8,12},{9,13},{10,... | collective-permute-start | bytes 98312 | tf_op jit(solution)/shard_map/ppermute | solution.py:63
  82.0 3.9 %collective-permute-start.30 = (bf16[16,1024]{1,0:T(8,128)(2,1)S(1)}, bf16[16,1024]{1,0:T(8,128)(2,1)S(1)}, u32[]{:S(2)}, u32[]{:S(2)}) collective-permute-start(bf16[16,1024]{1,0:T(8,128)(2,1)S(1)} %get-tuple-element.98), channel_id=1, source_target_pairs={{0,12},{1,13},{2,14},{3,15},{4,8},{5,9},{6,10},{7,11},{8,4},{9,5},... | collective-permute-start | bytes 98312 | tf_op jit(solution)/shard_map/ppermute | solution.py:63
  86.8 2.0 %collective-permute-done.30 = bf16[16,1024]{1,0:T(8,128)(2,1)S(1)} collective-permute-done((bf16[16,1024]{1,0:T(8,128)(2,1)S(1)}, bf16[16,1024]{1,0:T(8,128)(2,1)S(1)}, u32[]{:S(2)}, u32[]{:S(2)}) %collective-permute-start.30) | collective-permute-done | bytes 32800 | tf_op jit(solution)/shard_map/ppermute | solution.py:63
  88.7 5.0 %collective-permute-done.28 = bf16[16,1024]{1,0:T(8,128)(2,1)S(1)} collective-permute-done((bf16[16,1024]{1,0:T(8,128)(2,1)S(1)}, bf16[16,1024]{1,0:T(8,128)(2,1)S(1)}, u32[]{:S(2)}, u32[]{:S(2)}) %collective-permute-start.28) | collective-permute-done | bytes 32800 | tf_op jit(solution)/shard_map/ppermute | solution.py:63
  (51 shorter events, 19.0 us)
Async XLA Ops:
  2.0 11.9 %collective-permute-start = (bf16[32,8320]{1,0:T(8,128)(2,1)S(1)}, bf16[32,8320]{1,0:T(8,128)(2,1)S(1)}, u32[]{:S(2)}, u32[]{:S(2)}) collective-permute-start(bf16[32,8320]{1,0:T(8,128)(2,1)S(1)} %get-tuple-element.56), channel_id=1, source_target_pairs={{0,1},{1,0},{2,3},{3,2},{4,5},{5,4},{6,7},{7,6},{8,9},{9,8},{10,11... | collective-permute-start | bytes 1597448 | tf_op jit(solution)/shard_map/ppermute | solution.py:63
  2.1 14.7 %collective-permute-start.1 = (bf16[32,8320]{1,0:T(8,128)(2,1)S(1)}, bf16[32,8320]{1,0:T(8,128)(2,1)S(1)}, u32[]{:S(2)}, u32[]{:S(2)}) collective-permute-start(bf16[32,8320]{1,0:T(8,128)(2,1)S(1)} %get-tuple-element.59.after), channel_id=1, source_target_pairs={{0,2},{1,3},{2,0},{3,1},{4,6},{5,7},{6,4},{7,5},{8,10},{9,11},{10,... | collective-permute-start | bytes 1597448 | tf_op jit(solution)/shard_map/ppermute | solution.py:63
  5.1 11.1 %collective-permute-start.4 = (bf16[16,8192]{1,0:T(8,128)(2,1)S(1)}, bf16[16,8192]{1,0:T(8,128)(2,1)S(1)}, u32[]{:S(2)}, u32[]{:S(2)}) collective-permute-start(bf16[16,8192]{1,0:T(8,128)(2,1)S(1)} %own_references.1.refs_8_.refs_10_), channel_id=1, source_target_pairs={{0,32},{1,33},{2,34},{3,35},{4,36},{5,37},{6,38},{7,39},{8,40},{9,... | collective-permute-start | bytes 786440 | tf_op jit(solution)/shard_map/ppermute | solution.py:63
  5.7 10.5 %collective-permute-start.3 = (bf16[16,8192]{1,0:T(8,128)(2,1)S(1)}, bf16[16,8192]{1,0:T(8,128)(2,1)S(1)}, u32[]{:S(2)}, u32[]{:S(2)}) collective-permute-start(bf16[16,8192]{1,0:T(8,128)(2,1)S(1)} %own_references.1.refs_8_.refs_10_), channel_id=1, source_target_pairs={{0,192},{1,193},{2,194},{3,195},{4,196},{5,197},{6,198},{7,199},{8... | collective-permute-start | bytes 786440 | tf_op jit(solution)/shard_map/ppermute | solution.py:63
  8.7 7.8 %collective-permute-start.2 = (bf16[16,8192]{1,0:T(8,128)(2,1)S(1)}, bf16[16,8192]{1,0:T(8,128)(2,1)S(1)}, u32[]{:S(2)}, u32[]{:S(2)}) collective-permute-start(bf16[16,8192]{1,0:T(8,128)(2,1)S(1)} %own_references.1.refs_8_.refs_10_), channel_id=1, source_target_pairs={{0,64},{1,65},{2,66},{3,67},{4,68},{5,69},{6,70},{7,71},{8,72},{9,... | collective-permute-start | bytes 786440 | tf_op jit(solution)/shard_map/ppermute | solution.py:63
  16.8 16.4 %collective-permute-start.5 = (bf16[32,8320]{1,0:T(8,128)(2,1)S(1)}, bf16[32,8320]{1,0:T(8,128)(2,1)S(1)}, u32[]{:S(2)}, u32[]{:S(2)}) collective-permute-start(bf16[32,8320]{1,0:T(8,128)(2,1)S(1)} %get-tuple-element.63), channel_id=1, source_target_pairs={{0,3},{1,2},{2,1},{3,0},{4,7},{5,6},{6,5},{7,4},{8,11},{9,10},{10,... | collective-permute-start | bytes 1597448 | tf_op jit(solution)/shard_map/ppermute | solution.py:63
  17.8 10.7 %collective-permute-start.6 = (bf16[16,8192]{1,0:T(8,128)(2,1)S(1)}, bf16[16,8192]{1,0:T(8,128)(2,1)S(1)}, u32[]{:S(2)}, u32[]{:S(2)}) collective-permute-start(bf16[16,8192]{1,0:T(8,128)(2,1)S(1)} %collective-permute-done.4.refs_5_.refs_7_), channel_id=1, source_target_pairs={{0,128},{1,129},{2,130},{3,131},{4,132},{5,133},{6,134},{7,135},{8... | collective-permute-start | bytes 786440 | tf_op jit(solution)/shard_map/ppermute | solution.py:63
  21.0 10.2 %collective-permute-start.7 = (bf16[16,8192]{1,0:T(8,128)(2,1)S(1)}, bf16[16,8192]{1,0:T(8,128)(2,1)S(1)}, u32[]{:S(2)}, u32[]{:S(2)}) collective-permute-start(bf16[16,8192]{1,0:T(8,128)(2,1)S(1)} %relay.1), channel_id=1, source_target_pairs={{0,192},{1,65},{2,194},{3,67},{4,196},{5,69},{6,198},{7,71},{8,200... | collective-permute-start | bytes 786440 | tf_op jit(solution)/shard_map/ppermute | solution.py:63
  22.2 9.1 %collective-permute-start.8 = (bf16[16,8192]{1,0:T(8,128)(2,1)S(1)}, bf16[16,8192]{1,0:T(8,128)(2,1)S(1)}, u32[]{:S(2)}, u32[]{:S(2)}) collective-permute-start(bf16[16,8192]{1,0:T(8,128)(2,1)S(1)} %collective-permute-done.2.one.refs_6_.refs_8_), channel_id=1, source_target_pairs={{0,32},{1,33},{2,34},{3,35},{4,36},{5,37},{6,38},{7,39},{8,40},{9,... | collective-permute-start | bytes 786440 | tf_op jit(solution)/shard_map/ppermute | solution.py:63
  22.7 8.5 %collective-permute-start.9 = (bf16[16,8192]{1,0:T(8,128)(2,1)S(1)}, bf16[16,8192]{1,0:T(8,128)(2,1)S(1)}, u32[]{:S(2)}, u32[]{:S(2)}) collective-permute-start(bf16[16,8192]{1,0:T(8,128)(2,1)S(1)} %collective-permute-done.3.other.refs_7_.refs_9_), channel_id=1, source_target_pairs={{0,48},{1,49},{2,50},{3,51},{4,52},{5,53},{6,54},{7,55},{8,56},{9,... | collective-permute-start | bytes 786440 | tf_op jit(solution)/shard_map/ppermute | solution.py:63
  32.9 8.9 %collective-permute-start.10 = (f32[256,128]{1,0:T(8,128)S(1)}, f32[256,128]{1,0:T(8,128)S(1)}, u32[]{:S(2)}, u32[]{:S(2)}) collective-permute-start(f32[256,128]{1,0:T(8,128)S(1)} %get-tuple-element.68), channel_id=1, source_target_pairs={{0,2},{1,3},{2,0},{3,1},{4,6},{5,7},{6,4},{7,5},{8,10},{9,11},{10,... | collective-permute-start | bytes 393224 | tf_op jit(solution)/shard_map/ppermute | solution.py:63
  37.1 5.6 %collective-permute-start.11 = (f32[256,128]{1,0:T(8,128)S(1)}, f32[256,128]{1,0:T(8,128)S(1)}, u32[]{:S(2)}, u32[]{:S(2)}) collective-permute-start(f32[256,128]{1,0:T(8,128)S(1)} %partial_scores.4), channel_id=1, source_target_pairs={{0,3},{1,2},{2,1},{3,0},{4,7},{5,6},{6,5},{7,4},{8,11},{9,10},{10,... | collective-permute-start | bytes 393224 | tf_op jit(solution)/shard_map/ppermute | solution.py:63
  41.2 1.6 %collective-permute-start.12 = (f32[256,128]{1,0:T(8,128)S(1)}, f32[256,128]{1,0:T(8,128)S(1)}, u32[]{:S(2)}, u32[]{:S(2)}) collective-permute-start(f32[256,128]{1,0:T(8,128)S(1)} %get-tuple-element.78), channel_id=1, source_target_pairs={{0,1},{1,0},{2,3},{3,2},{4,5},{5,4},{6,7},{7,6},{8,9},{9,8},{10,11... | collective-permute-start | bytes 393224 | tf_op jit(solution)/shard_map/ppermute | solution.py:63
  43.1 4.1 %collective-permute-start.15 = (bf16[128,256]{1,0:T(8,128)(2,1)S(1)}, bf16[128,256]{1,0:T(8,128)(2,1)S(1)}, u32[]{:S(2)}, u32[]{:S(2)}) collective-permute-start(bf16[128,256]{1,0:T(8,128)(2,1)S(1)} %posterior.1.refs_6_), channel_id=1, source_target_pairs={{0,3},{1,2},{2,1},{3,0},{4,7},{5,6},{6,5},{7,4},{8,11},{9,10},{10,... | collective-permute-start | bytes 196616 | tf_op jit(solution)/shard_map/ppermute | solution.py:63
  44.8 4.4 %collective-permute-start.14 = (bf16[128,256]{1,0:T(8,128)(2,1)S(1)}, bf16[128,256]{1,0:T(8,128)(2,1)S(1)}, u32[]{:S(2)}, u32[]{:S(2)}) collective-permute-start(bf16[128,256]{1,0:T(8,128)(2,1)S(1)} %posterior.1.refs_6_), channel_id=1, source_target_pairs={{0,2},{1,3},{2,0},{3,1},{4,6},{5,7},{6,4},{7,5},{8,10},{9,11},{10,... | collective-permute-start | bytes 196616 | tf_op jit(solution)/shard_map/ppermute | solution.py:63
  45.2 4.0 %collective-permute-start.13 = (bf16[128,256]{1,0:T(8,128)(2,1)S(1)}, bf16[128,256]{1,0:T(8,128)(2,1)S(1)}, u32[]{:S(2)}, u32[]{:S(2)}) collective-permute-start(bf16[128,256]{1,0:T(8,128)(2,1)S(1)} %posterior.1.refs_6_), channel_id=1, source_target_pairs={{0,1},{1,0},{2,3},{3,2},{4,5},{5,4},{6,7},{7,6},{8,9},{9,8},{10,11... | collective-permute-start | bytes 196616 | tf_op jit(solution)/shard_map/ppermute | solution.py:63
  50.6 9.4 %collective-permute-start.22 = (bf16[64,2048]{1,0:T(8,128)(2,1)S(1)}, bf16[64,2048]{1,0:T(8,128)(2,1)S(1)}, u32[]{:S(2)}, u32[]{:S(2)}) collective-permute-start(bf16[64,2048]{1,0:T(8,128)(2,1)S(1)} %get-tuple-element.88), channel_id=1, source_target_pairs={{0,16},{1,129},{2,18},{3,131},{4,20},{5,133},{6,22},{7,135},{8,24}... | collective-permute-start | bytes 786440 | tf_op jit(solution)/shard_map/ppermute | solution.py:63
  53.5 9.8 %collective-permute-start.23 = (bf16[64,2048]{1,0:T(8,128)(2,1)S(1)}, bf16[64,2048]{1,0:T(8,128)(2,1)S(1)}, u32[]{:S(2)}, u32[]{:S(2)}) collective-permute-start(bf16[64,2048]{1,0:T(8,128)(2,1)S(1)} %get-tuple-element.89), channel_id=1, source_target_pairs={{0,32},{1,65},{2,34},{3,67},{4,36},{5,69},{6,38},{7,71},{8,40},{9,... | collective-permute-start | bytes 786440 | tf_op jit(solution)/shard_map/ppermute | solution.py:63
  54.6 10.2 %collective-permute-start.24 = (bf16[64,2048]{1,0:T(8,128)(2,1)S(1)}, bf16[64,2048]{1,0:T(8,128)(2,1)S(1)}, u32[]{:S(2)}, u32[]{:S(2)}) collective-permute-start(bf16[64,2048]{1,0:T(8,128)(2,1)S(1)} %get-tuple-element.90), channel_id=1, source_target_pairs={{0,48},{1,193},{2,50},{3,195},{4,52},{5,197},{6,54},{7,199},{8,56}... | collective-permute-start | bytes 786440 | tf_op jit(solution)/shard_map/ppermute | solution.py:63
  56.3 13.2 %collective-permute-start.16 = (bf16[64,2048]{1,0:T(8,128)(2,1)S(1)}, bf16[64,2048]{1,0:T(8,128)(2,1)S(1)}, u32[]{:S(2)}, u32[]{:S(2)}) collective-permute-start(bf16[64,2048]{1,0:T(8,128)(2,1)S(1)} %get-tuple-element.80), channel_id=1, source_target_pairs={{0,128},{1,17},{2,130},{3,19},{4,132},{5,21},{6,134},{7,23},{8,136... | collective-permute-start | bytes 786440 | tf_op jit(solution)/shard_map/ppermute | solution.py:63
  59.3 10.6 %collective-permute-start.17 = (bf16[64,2048]{1,0:T(8,128)(2,1)S(1)}, bf16[64,2048]{1,0:T(8,128)(2,1)S(1)}, u32[]{:S(2)}, u32[]{:S(2)}) collective-permute-start(bf16[64,2048]{1,0:T(8,128)(2,1)S(1)} %get-tuple-element.81), channel_id=1, source_target_pairs={{0,64},{1,33},{2,66},{3,35},{4,68},{5,37},{6,70},{7,39},{8,72},{9,... | collective-permute-start | bytes 786440 | tf_op jit(solution)/shard_map/ppermute | solution.py:63
  60.0 9.8 %collective-permute-start.18 = (bf16[64,2048]{1,0:T(8,128)(2,1)S(1)}, bf16[64,2048]{1,0:T(8,128)(2,1)S(1)}, u32[]{:S(2)}, u32[]{:S(2)}) collective-permute-start(bf16[64,2048]{1,0:T(8,128)(2,1)S(1)} %get-tuple-element.82), channel_id=1, source_target_pairs={{0,192},{1,49},{2,194},{3,51},{4,196},{5,53},{6,198},{7,55},{8,200... | collective-permute-start | bytes 786440 | tf_op jit(solution)/shard_map/ppermute | solution.py:63
  65.0 9.3 %collective-permute-start.25 = (bf16[16,2048]{1,0:T(8,128)(2,1)S(1)}, bf16[16,2048]{1,0:T(8,128)(2,1)S(1)}, u32[]{:S(2)}, u32[]{:S(2)}) collective-permute-start(bf16[16,2048]{1,0:T(8,128)(2,1)S(1)} %get-tuple-element.92), channel_id=1, source_target_pairs={{0,128},{1,17},{2,130},{3,19},{4,132},{5,21},{6,134},{7,23},{8,136... | collective-permute-start | bytes 196616 | tf_op jit(solution)/shard_map/ppermute | solution.py:63
  68.3 5.9 %collective-permute-start.26 = (bf16[16,2048]{1,0:T(8,128)(2,1)S(1)}, bf16[16,2048]{1,0:T(8,128)(2,1)S(1)}, u32[]{:S(2)}, u32[]{:S(2)}) collective-permute-start(bf16[16,2048]{1,0:T(8,128)(2,1)S(1)} %get-tuple-element.93), channel_id=1, source_target_pairs={{0,64},{1,33},{2,66},{3,35},{4,68},{5,37},{6,70},{7,39},{8,72},{9,... | collective-permute-start | bytes 196616 | tf_op jit(solution)/shard_map/ppermute | solution.py:63
  69.5 6.1 %collective-permute-start.27 = (bf16[16,2048]{1,0:T(8,128)(2,1)S(1)}, bf16[16,2048]{1,0:T(8,128)(2,1)S(1)}, u32[]{:S(2)}, u32[]{:S(2)}) collective-permute-start(bf16[16,2048]{1,0:T(8,128)(2,1)S(1)} %get-tuple-element.94), channel_id=1, source_target_pairs={{0,192},{1,49},{2,194},{3,51},{4,196},{5,53},{6,198},{7,55},{8,200... | collective-permute-start | bytes 196616 | tf_op jit(solution)/shard_map/ppermute | solution.py:63
  70.0 5.9 %collective-permute-start.19 = (bf16[16,2048]{1,0:T(8,128)(2,1)S(1)}, bf16[16,2048]{1,0:T(8,128)(2,1)S(1)}, u32[]{:S(2)}, u32[]{:S(2)}) collective-permute-start(bf16[16,2048]{1,0:T(8,128)(2,1)S(1)} %get-tuple-element.84), channel_id=1, source_target_pairs={{0,16},{1,129},{2,18},{3,131},{4,20},{5,133},{6,22},{7,135},{8,24}... | collective-permute-start | bytes 196616 | tf_op jit(solution)/shard_map/ppermute | solution.py:63
  72.3 4.8 %collective-permute-start.20 = (bf16[16,2048]{1,0:T(8,128)(2,1)S(1)}, bf16[16,2048]{1,0:T(8,128)(2,1)S(1)}, u32[]{:S(2)}, u32[]{:S(2)}) collective-permute-start(bf16[16,2048]{1,0:T(8,128)(2,1)S(1)} %get-tuple-element.85), channel_id=1, source_target_pairs={{0,32},{1,65},{2,34},{3,67},{4,36},{5,69},{6,38},{7,71},{8,40},{9,... | collective-permute-start | bytes 196616 | tf_op jit(solution)/shard_map/ppermute | solution.py:63
  74.2 4.3 %collective-permute-start.21 = (bf16[16,2048]{1,0:T(8,128)(2,1)S(1)}, bf16[16,2048]{1,0:T(8,128)(2,1)S(1)}, u32[]{:S(2)}, u32[]{:S(2)}) collective-permute-start(bf16[16,2048]{1,0:T(8,128)(2,1)S(1)} %get-tuple-element.86), channel_id=1, source_target_pairs={{0,48},{1,193},{2,50},{3,195},{4,52},{5,197},{6,54},{7,199},{8,56}... | collective-permute-start | bytes 196616 | tf_op jit(solution)/shard_map/ppermute | solution.py:63
  78.6 8.2 %collective-permute-start.29 = (bf16[16,1024]{1,0:T(8,128)(2,1)S(1)}, bf16[16,1024]{1,0:T(8,128)(2,1)S(1)}, u32[]{:S(2)}, u32[]{:S(2)}) collective-permute-start(bf16[16,1024]{1,0:T(8,128)(2,1)S(1)} %get-tuple-element.97), channel_id=1, source_target_pairs={{0,4},{1,5},{2,6},{3,7},{4,0},{5,1},{6,2},{7,3},{8,12},{9,13},{10,... | collective-permute-start | bytes 98312 | tf_op jit(solution)/shard_map/ppermute | solution.py:63
  82.0 6.8 %collective-permute-start.30 = (bf16[16,1024]{1,0:T(8,128)(2,1)S(1)}, bf16[16,1024]{1,0:T(8,128)(2,1)S(1)}, u32[]{:S(2)}, u32[]{:S(2)}) collective-permute-start(bf16[16,1024]{1,0:T(8,128)(2,1)S(1)} %get-tuple-element.98), channel_id=1, source_target_pairs={{0,12},{1,13},{2,14},{3,15},{4,8},{5,9},{6,10},{7,11},{8,4},{9,5},... | collective-permute-start | bytes 98312 | tf_op jit(solution)/shard_map/ppermute | solution.py:63
  85.8 7.9 %collective-permute-start.28 = (bf16[16,1024]{1,0:T(8,128)(2,1)S(1)}, bf16[16,1024]{1,0:T(8,128)(2,1)S(1)}, u32[]{:S(2)}, u32[]{:S(2)}) collective-permute-start(bf16[16,1024]{1,0:T(8,128)(2,1)S(1)} %joined_sums.2), channel_id=1, source_target_pairs={{0,8},{1,9},{2,10},{3,11},{4,12},{5,13},{6,14},{7,15},{8,0},{9,1},... | collective-permute-start | bytes 98312 | tf_op jit(solution)/shard_map/ppermute | solution.py:63
